TPU v7x, 32 devices: a whole 2x2x4 slice. The times are simulated.
32 devices in a mesh: groups: 2 (over y), blk: 4 (over x, core), sub: 4 (over z).
Axes of the slice: x: 2, y: 2, z: 4, core: 2. Of those that a mesh axis runs over, the one named last changes fastest.
Arguments:
- embeds: bfloat16 [32768, 1024], P(('groups', 'blk', 'sub')), parts along dimension 0, may hold values from -6 to 6
- pick_blk: int32 [32, 4], P(('groups', 'blk', 'sub')), parts along dimension 0, may hold values from 0 to 3
- mask_blk: int32 [32, 16], P(('groups', 'blk', 'sub')), parts along dimension 0, may hold values from 0 to 1, as said below
- pick_sub: int32 [32, 4], P(('groups', 'blk')), parts along dimension 0, may hold values from 0 to 3
- mask_sub: int32 [32, 16], P(('groups', 'blk', 'sub')), parts along dimension 0, may hold values from 0 to 1, as said below
Outputs:
- dup_frac: float32 [32768], P(('groups', 'blk', 'sub')), parts along dimension 0
There are 2 independent parts, one for each index of `groups`. A program takes and returns all parts, laid end to end along the dimension named above; each array names one. Nothing has to cross between parts.
Inputs may be any that keep to these rules, and one draw needn't show every extreme that they name: mask_blk[e, p * 4 + i] is 0 where p is device e's own blk index. mask_sub[e, p * 4 + i] is 0 where p is device e's own sub index.
All inputs are finite; a program needn't handle non-finite values.
Results may differ from a plain program's by a relative error of at most 0.00086.
Values may be sent and summed in bfloat16 or wider, within the bound.
No kernel may reach another device: no remote copies, remote signals or barrier semaphores. Data moves between devices by JAX's collectives and lax.ppermute only.
A program may use at most 64 MiB of HBM per device.

v0:
```python
import jax
import jax.numpy as jnp
from jax import lax
from jax.sharding import PartitionSpec as P

BLOCK = 256
BPD = 4


cutoff = 0.05
sharpness = 100.0


def normalize(embeds):
    wide = embeds.astype(jnp.float32)
    scale = lax.rsqrt(jnp.sum(wide * wide, axis=1, keepdims=True) + 1e-06)
    return (wide * scale).astype(jnp.bfloat16)


def sweep_slots(arrived, unit_rows, slot_masks):
    per_device = slot_masks.shape[1]
    block_rows = arrived.shape[1]

    def compute(arrived_block, live_mask):
        cosines = lax.dot_general(
            arrived_block, unit_rows, (((1,), (1,)), ((), ())), preferred_element_type=jnp.float32
        )
        weight = jax.nn.sigmoid((cosines - cutoff) * sharpness).reshape(
            block_rows, per_device, block_rows
        )
        weight = weight * live_mask.astype(jnp.float32)[None, :, None]
        return (jnp.sum(weight, axis=0), jnp.sum(weight, axis=(1, 2)))

    def visit(totals, slot_item):
        arrived_block, live_mask = slot_item
        local_part, back_sums = compute(arrived_block, live_mask)
        return (totals + local_part, back_sums)

    return lax.scan(visit, jnp.zeros((per_device, block_rows), jnp.float32), (arrived, slot_masks))


def credit(picked, returned, per_device):
    onehot = (picked[:, None] == jnp.arange(per_device, dtype=jnp.int32)[None, :]).astype(
        jnp.float32
    )
    return jnp.einsum("sc,sr->cr", onehot, returned, precision=lax.Precision.HIGHEST)


def body(embeds, pick_blk, mask_blk, pick_sub, mask_sub):
    unit_rows = normalize(embeds)
    features = unit_rows.shape[1]
    blocks = unit_rows.reshape(BPD, BLOCK, features)
    blk_picks = pick_blk[0]
    outgoing = blocks[blk_picks]
    arrived = lax.all_to_all(outgoing, "blk", split_axis=0, concat_axis=0, tiled=True)
    blk_masks = mask_blk[0].reshape(-1, BPD)
    local_blk, backs_blk = sweep_slots(arrived, unit_rows, blk_masks)
    returned_blk = lax.all_to_all(backs_blk, "blk", split_axis=0, concat_axis=0, tiled=True)
    sub_masks = mask_sub[0].reshape(-1, BPD)
    own_index = lax.axis_index("sub")
    sub_picks = lax.dynamic_index_in_dim(pick_sub, own_index, 0, keepdims=False)
    arrived_sub = lax.all_to_all(blocks[sub_picks], "sub", split_axis=0, concat_axis=0, tiled=True)
    local_sub, backs_sub = sweep_slots(arrived_sub, unit_rows, sub_masks)
    returned_sub = lax.all_to_all(backs_sub, "sub", split_axis=0, concat_axis=0, tiled=True)
    totals = (
        local_blk
        + local_sub
        + credit(blk_picks, returned_blk, BPD)
        + credit(sub_picks, returned_sub, BPD)
    )
    return totals.reshape(-1) / BLOCK


def solution(mesh):
    return jax.shard_map(
        body,
        mesh=mesh,
        in_specs=(
            P(("groups", "blk", "sub"), None),
            P(("groups", "blk", "sub"), None),
            P(("groups", "blk", "sub"), None),
            P(("groups", "blk"), None),
            P(("groups", "blk", "sub"), None),
        ),
        out_specs=P(("groups", "blk", "sub")),
        check_vma=False,
    )
```

profile of v0, /device:TPU:0, one launch (start us, length us, event | category | flops | bytes accessed | tf_op | source)
XLA Modules:
  0.0 112.2 jit_solution(17018003070514671519)
XLA Ops:
  0.0 2.2 %fusion.18 = f32[1024]{0:T(1024)S(1)} fusion(bf16[1024,1024]{1,0:T(8,128)(2,1)} %param.9), kind=kLoop, calls=%fused_computation.30 | loop fusion | flops 3144704 | bytes 2101248 | tf_op jit(solution)/shard_map/reduce_sum | solution.py:16
  2.2 0.0 copy-done
  2.2 0.0 copy-start.4
  2.3 0.4 fusion.19
  2.7 0.2 copy-done.4
  2.9 2.0 %gather_fusion = bf16[4,256,1024]{2,1,0:T(8,128)(2,1)} fusion(bf16[4,256,1024]{2,1,0:T(8,128)(2,1)S(1)} %bitcast.69, s32[1024]{0:T(1024)S(1)} %pad_clamp_fusion.1), kind=kCustom, calls=%fused_computation | custom fusion | bytes 4194320 | tf_op jit(solution)/shard_map/gather | solution.py:54
  4.9 4.6 %all-to-all-start = ((bf16[4,256,1024]{2,1,0:T(8,128)(2,1)}), bf16[4,256,1024]{2,1,0:T(8,128)(2,1)}, u32[]{:S(2)}, u32[]{:S(2)}) async-start(bf16[4,256,1024]{2,1,0:T(8,128)(2,1)} %gather_fusion), calls=%async_computation | async-start | bytes 4194304 | tf_op jit(solution)/shard_map/all_to_all | solution.py:55
  9.6 0.0 copy-done.1
  9.6 0.0 copy-start.2
  9.6 0.0 copy-start.3
  9.6 2.0 %gather_fusion.1 = bf16[4,256,1024]{2,1,0:T(8,128)(2,1)} fusion(bf16[4,256,1024]{2,1,0:T(8,128)(2,1)S(1)} %bitcast.70, s32[1024]{0:T(1024)S(1)} %pad_clamp_fusion), kind=kCustom, calls=%fused_computation.1 | custom fusion | bytes 4194320 | tf_op jit(solution)/shard_map/gather | solution.py:62
  11.6 0.5 broadcast.152
  12.2 0.0 copy-done.2
  12.2 0.7 reduce.17
  12.8 0.1 reshape_squeeze.7
  12.9 0.0 copy-done.3
  12.9 0.7 reduce.16
  13.6 0.1 reshape_squeeze.6
  13.7 22.3 %all-to-all-done = bf16[4,256,1024]{2,1,0:T(8,128)(2,1)} async-done(((bf16[4,256,1024]{2,1,0:T(8,128)(2,1)}), bf16[4,256,1024]{2,1,0:T(8,128)(2,1)}, u32[]{:S(2)}, u32[]{:S(2)}) %all-to-all-start) | async-done | bytes 2097184 | tf_op jit(solution)/shard_map/all_to_all | solution.py:55
  35.9 5.7 %all-to-all-start.1 = ((bf16[4,256,1024]{2,1,0:T(8,128)(2,1)}), bf16[4,256,1024]{2,1,0:T(8,128)(2,1)}, u32[]{:S(2)}, u32[]{:S(2)}) async-start(bf16[4,256,1024]{2,1,0:T(8,128)(2,1)} %gather_fusion.1), calls=%async_computation.1 | async-start | bytes 4194304 | tf_op jit(solution)/shard_map/all_to_all | solution.py:62
  41.6 9.0 %while.30 = (s32[]{:T(128)}, f32[4,256]{1,0:T(4,128)S(1)}, f32[4,256]{1,0:T(4,128)S(1)}, bf16[4,256,1024]{2,1,0:T(8,128)(2,1)}, bf16[1024,1024]{1,0:T(8,128)(2,1...) while((s32[]{:T(128)}, f32[4,256]{1,0:T(4,128)S(1)}, f32[4,256]{1,0:T(4,128)S(1)}, ...), condition=%wide.region_4.5_spmd.clone, body=%wide.region_1.4_spmd.clone.sunk | while | flops 538968832 | bytes 2666135 | solution.py:39
  41.6 0.1 broadcast_bitcast_fusion.4
  41.7 2.1 %fusion.40 = (f32[256]{0:T(256)S(1)}, f32[1024]{0:T(1024)S(1)}) fusion(f32[1024]{0:T(1024)S(1)} %bitcast.71, bf16[1024,1024]{1,0:T(8,128)(2,1)S(1)} %get-tuple-element.337, bf16[4,256,1024]{2,1,0:T(8,128)(2,1)} %get-tuple-element.336, s32[]{:T(128)} %get-tuple-element.325), kind=kOutput, calls=%fused_computation.53.clone.1 | convolution fusion | flops 538966784 | bytes 2631168 | tf_op jit(solution)/shard_map/while/body/eval_jaxpr/dot_general | solution.py:25
  43.9 0.1 broadcast_bitcast_fusion.4
  44.0 2.1 %fusion.40 = (f32[256]{0:T(256)S(1)}, f32[1024]{0:T(1024)S(1)}) fusion(f32[1024]{0:T(1024)S(1)} %bitcast.71, bf16[1024,1024]{1,0:T(8,128)(2,1)S(1)} %get-tuple-element.337, bf16[4,256,1024]{2,1,0:T(8,128)(2,1)} %get-tuple-element.336, s32[]{:T(128)} %get-tuple-element.325), kind=kOutput, calls=%fused_computation.53.clone.1 | convolution fusion | flops 538966784 | bytes 2631168 | tf_op jit(solution)/shard_map/while/body/eval_jaxpr/dot_general | solution.py:25
  46.1 0.1 broadcast_bitcast_fusion.4
  46.2 2.1 %fusion.40 = (f32[256]{0:T(256)S(1)}, f32[1024]{0:T(1024)S(1)}) fusion(f32[1024]{0:T(1024)S(1)} %bitcast.71, bf16[1024,1024]{1,0:T(8,128)(2,1)S(1)} %get-tuple-element.337, bf16[4,256,1024]{2,1,0:T(8,128)(2,1)} %get-tuple-element.336, s32[]{:T(128)} %get-tuple-element.325), kind=kOutput, calls=%fused_computation.53.clone.1 | convolution fusion | flops 538966784 | bytes 2631168 | tf_op jit(solution)/shard_map/while/body/eval_jaxpr/dot_general | solution.py:25
  48.4 0.1 broadcast_bitcast_fusion.4
  48.4 2.1 %fusion.40 = (f32[256]{0:T(256)S(1)}, f32[1024]{0:T(1024)S(1)}) fusion(f32[1024]{0:T(1024)S(1)} %bitcast.71, bf16[1024,1024]{1,0:T(8,128)(2,1)S(1)} %get-tuple-element.337, bf16[4,256,1024]{2,1,0:T(8,128)(2,1)} %get-tuple-element.336, s32[]{:T(128)} %get-tuple-element.325), kind=kOutput, calls=%fused_computation.53.clone.1 | convolution fusion | flops 538966784 | bytes 2631168 | tf_op jit(solution)/shard_map/while/body/eval_jaxpr/dot_general | solution.py:25
  50.6 0.6 all_to_all.24
  51.2 38.5 %all-to-all-done.1 = bf16[4,256,1024]{2,1,0:T(8,128)(2,1)} async-done(((bf16[4,256,1024]{2,1,0:T(8,128)(2,1)}), bf16[4,256,1024]{2,1,0:T(8,128)(2,1)}, u32[]{:S(2)}, u32[]{:S(2)}) %all-to-all-start.1) | async-done | bytes 2097184 | tf_op jit(solution)/shard_map/all_to_all | solution.py:62
  89.7 3.2 %all-to-all-start.2 = ((f32[4,1,256]{2,1,0:T(1,128)}), f32[4,1,256]{2,1,0:T(1,128)S(1)}, u32[]{:S(2)}, u32[]{:S(2)}) async-start(f32[4,1,256]{2,1,0:T(1,128)} %all_to_all.24), calls=%async_computation.2 | async-start | bytes 8192 | tf_op jit(solution)/shard_map/all_to_all | solution.py:58
  93.0 9.0 %while.31 = (s32[]{:T(128)}, f32[4,256]{1,0:T(4,128)S(1)}, f32[4,256]{1,0:T(4,128)S(1)}, bf16[4,256,1024]{2,1,0:T(8,128)(2,1)}, bf16[1024,1024]{1,0:T(8,128)(2,1...) while((s32[]{:T(128)}, f32[4,256]{1,0:T(4,128)S(1)}, f32[4,256]{1,0:T(4,128)S(1)}, ...), condition=%wide.region_8.9_spmd.clone, body=%wide.region_5.8_spmd.clone.sunk | while | flops 538968832 | bytes 2666135 | solution.py:39
  93.0 0.1 broadcast_bitcast_fusion.5
  93.1 2.1 %fusion.42 = (f32[256]{0:T(256)S(1)}, f32[1024]{0:T(1024)S(1)}) fusion(f32[1024]{0:T(1024)S(1)} %bitcast.72, bf16[1024,1024]{1,0:T(8,128)(2,1)S(1)} %get-tuple-element.361, bf16[4,256,1024]{2,1,0:T(8,128)(2,1)} %get-tuple-element.360, s32[]{:T(128)} %get-tuple-element.349), kind=kOutput, calls=%fused_computation.54.clone.1 | convolution fusion | flops 538966784 | bytes 2631168 | tf_op jit(solution)/shard_map/while/body/eval_jaxpr/dot_general | solution.py:25
  95.3 0.1 broadcast_bitcast_fusion.5
  95.3 2.1 %fusion.42 = (f32[256]{0:T(256)S(1)}, f32[1024]{0:T(1024)S(1)}) fusion(f32[1024]{0:T(1024)S(1)} %bitcast.72, bf16[1024,1024]{1,0:T(8,128)(2,1)S(1)} %get-tuple-element.361, bf16[4,256,1024]{2,1,0:T(8,128)(2,1)} %get-tuple-element.360, s32[]{:T(128)} %get-tuple-element.349), kind=kOutput, calls=%fused_computation.54.clone.1 | convolution fusion | flops 538966784 | bytes 2631168 | tf_op jit(solution)/shard_map/while/body/eval_jaxpr/dot_general | solution.py:25
  97.5 0.1 broadcast_bitcast_fusion.5
  97.6 2.1 %fusion.42 = (f32[256]{0:T(256)S(1)}, f32[1024]{0:T(1024)S(1)}) fusion(f32[1024]{0:T(1024)S(1)} %bitcast.72, bf16[1024,1024]{1,0:T(8,128)(2,1)S(1)} %get-tuple-element.361, bf16[4,256,1024]{2,1,0:T(8,128)(2,1)} %get-tuple-element.360, s32[]{:T(128)} %get-tuple-element.349), kind=kOutput, calls=%fused_computation.54.clone.1 | convolution fusion | flops 538966784 | bytes 2631168 | tf_op jit(solution)/shard_map/while/body/eval_jaxpr/dot_general | solution.py:25
  99.7 0.1 broadcast_bitcast_fusion.5
  99.8 2.1 %fusion.42 = (f32[256]{0:T(256)S(1)}, f32[1024]{0:T(1024)S(1)}) fusion(f32[1024]{0:T(1024)S(1)} %bitcast.72, bf16[1024,1024]{1,0:T(8,128)(2,1)S(1)} %get-tuple-element.361, bf16[4,256,1024]{2,1,0:T(8,128)(2,1)} %get-tuple-element.360, s32[]{:T(128)} %get-tuple-element.349), kind=kOutput, calls=%fused_computation.54.clone.1 | convolution fusion | flops 538966784 | bytes 2631168 | tf_op jit(solution)/shard_map/while/body/eval_jaxpr/dot_general | solution.py:25
  102.0 0.6 all_to_all.27
  102.6 0.0 all-to-all-done.2
  102.6 3.2 %all-to-all-start.3 = ((f32[4,1,256]{2,1,0:T(1,128)}), f32[4,1,256]{2,1,0:T(1,128)S(1)}, u32[]{:S(2)}, u32[]{:S(2)}) async-start(f32[4,1,256]{2,1,0:T(1,128)} %all_to_all.27), calls=%async_computation.3 | async-start | bytes 8192 | tf_op jit(solution)/shard_map/all_to_all | solution.py:64
  105.8 0.3 convolution_add_fusion.3
  106.1 5.3 %all-to-all-done.3 = f32[4,1,256]{2,1,0:T(1,128)S(1)} async-done(((f32[4,1,256]{2,1,0:T(1,128)}), f32[4,1,256]{2,1,0:T(1,128)S(1)}, u32[]{:S(2)}, u32[]{:S(2)}) %all-to-all-start.3) | async-done | bytes 4128 | tf_op jit(solution)/shard_map/all_to_all | solution.py:64
  111.3 0.3 fusion.21
  111.6 0.6 copy.10
  (52 shorter events, 0.7 us)
Async XLA Ops:
  0.0 2.2 %copy-start = (bf16[1024,1024]{1,0:T(8,128)(2,1)S(1)}, bf16[1024,1024]{1,0:T(8,128)(2,1)}, u32[]{:S(2)}) copy-start(bf16[1024,1024]{1,0:T(8,128)(2,1)} %param.9) | copy-start | bytes 6291460
  2.2 0.7 copy-start.4
  4.9 4.6 %copy-start.1 = (s32[4,4]{1,0:T(4,128)S(1)}, s32[4,4]{1,0:T(4,128)}, u32[]{:S(2)}) copy-start(s32[4,4]{1,0:T(4,128)} %param.12) | copy-start | bytes 196
  4.9 31.0 %all-to-all-start = ((bf16[4,256,1024]{2,1,0:T(8,128)(2,1)}), bf16[4,256,1024]{2,1,0:T(8,128)(2,1)}, u32[]{:S(2)}, u32[]{:S(2)}) async-start(bf16[4,256,1024]{2,1,0:T(8,128)(2,1)} %gather_fusion), calls=%async_computation | async-start | bytes 4194304 | tf_op jit(solution)/shard_map/all_to_all | solution.py:55
  9.6 2.6 %copy-start.2 = (s32[1,16]{1,0:T(1,128)S(1)}, s32[1,16]{1,0:T(1,128)}, u32[]{:S(2)}) copy-start(s32[1,16]{1,0:T(1,128)} %param.13) | copy-start | bytes 196
  9.6 3.3 %copy-start.3 = (s32[1,16]{1,0:T(1,128)S(1)}, s32[1,16]{1,0:T(1,128)}, u32[]{:S(2)}) copy-start(s32[1,16]{1,0:T(1,128)} %param.11) | copy-start | bytes 196
  35.9 53.8 %all-to-all-start.1 = ((bf16[4,256,1024]{2,1,0:T(8,128)(2,1)}), bf16[4,256,1024]{2,1,0:T(8,128)(2,1)}, u32[]{:S(2)}, u32[]{:S(2)}) async-start(bf16[4,256,1024]{2,1,0:T(8,128)(2,1)} %gather_fusion.1), calls=%async_computation.1 | async-start | bytes 4194304 | tf_op jit(solution)/shard_map/all_to_all | solution.py:62
  89.7 12.8 %all-to-all-start.2 = ((f32[4,1,256]{2,1,0:T(1,128)}), f32[4,1,256]{2,1,0:T(1,128)S(1)}, u32[]{:S(2)}, u32[]{:S(2)}) async-start(f32[4,1,256]{2,1,0:T(1,128)} %all_to_all.24), calls=%async_computation.2 | async-start | bytes 8192 | tf_op jit(solution)/shard_map/all_to_all | solution.py:58
  102.6 8.8 %all-to-all-start.3 = ((f32[4,1,256]{2,1,0:T(1,128)}), f32[4,1,256]{2,1,0:T(1,128)S(1)}, u32[]{:S(2)}, u32[]{:S(2)}) async-start(f32[4,1,256]{2,1,0:T(1,128)} %all_to_all.27), calls=%async_computation.3 | async-start | bytes 8192 | tf_op jit(solution)/shard_map/all_to_all | solution.py:64
where the time goes:
time: 113 us; the launch traced here: 112 us
  waiting for transfers between devices  66.1 us (58%)
  matrix products  17 us (15%)
  starting transfers between devices  16.8 us (15%)
  local copies, waits for them, and re-layouts  7.83 us (7%)
  other arithmetic  4.12 us (4%)
    all_to_all x1, waiting for transfers between devices, body(): lax.all_to_all(blocks[sub_picks], 'sub', split_axis=0, concat_axis=0, til...  38.5 us
    all_to_all x1, waiting for transfers between devices, body(): lax.all_to_all(outgoing, 'blk', split_axis=0, concat_axis=0, tiled=True)  22.3 us
    dot_general x8, matrix products, compute(): lax.dot_general(arrived_block, unit_rows, (((1,), (1,)), ((), ())), prefe...  16.5 us
    all_to_all x1, starting transfers between devices, body(): lax.all_to_all(blocks[sub_picks], 'sub', split_axis=0, concat_axis=0, til...  5.7 us
    all_to_all x1, waiting for transfers between devices, body(): lax.all_to_all(backs_sub, 'sub', split_axis=0, concat_axis=0, tiled=True)  5.28 us
    all_to_all x1, starting transfers between devices, body(): lax.all_to_all(outgoing, 'blk', split_axis=0, concat_axis=0, tiled=True)  4.58 us
    all_to_all x1, starting transfers between devices, body(): lax.all_to_all(backs_blk, 'blk', split_axis=0, concat_axis=0, tiled=True)  3.25 us
    all_to_all x1, starting transfers between devices, body(): lax.all_to_all(backs_sub, 'sub', split_axis=0, concat_axis=0, tiled=True)  3.25 us
  transfers between devices with their start and end apart: 4, of which 3 were waited for; matrix products, arithmetic and copies ran while one was open for 20% of the time, Pallas kernels for 0%

commit v1 on v0

v1 whole, which is shorter than its diff:
```python
import jax
import jax.numpy as jnp
from jax import lax
from jax.sharding import PartitionSpec as P

BLOCK = 256

cutoff = 0.05
sharpness = 100.0


def normalize(embeds):
    wide = embeds.astype(jnp.float32)
    scale = lax.rsqrt(jnp.sum(wide * wide, axis=1, keepdims=True) + 1e-06)
    return (wide * scale).astype(jnp.bfloat16)


def partner(index, step, size):
    if size & (size - 1) == 0:
        return index ^ step, index ^ step
    return (index + step) % size, (index - step) % size


def pairs(step, size):
    return [(i, partner(i, step, size)[0]) for i in range(size)]


def sweep(arrived, unit_rows, live_mask):
    count = live_mask.shape[0]
    rows = arrived.shape[0]
    cosines = lax.dot_general(
        normalize(arrived), unit_rows, (((1,), (1,)), ((), ())), preferred_element_type=jnp.float32
    )
    weight = jax.nn.sigmoid((cosines - cutoff) * sharpness).reshape(rows, count, -1)
    weight = weight * live_mask.astype(jnp.float32)[None, :, None]
    return jnp.sum(weight, axis=0), jnp.sum(weight, axis=(1, 2))


def body(embeds, pick_blk, mask_blk, pick_sub, mask_sub):
    features = embeds.shape[1]
    blocks = embeds.reshape(-1, BLOCK, features)
    count = blocks.shape[0]
    sub_size, blk_size = lax.axis_size("sub"), lax.axis_size("blk")
    own_sub, own_blk = lax.axis_index("sub"), lax.axis_index("blk")
    picks = {"sub": lax.dynamic_index_in_dim(pick_sub, own_sub, 0, keepdims=False), "blk": pick_blk[0]}
    masks = {"sub": mask_sub[0].reshape(-1, count), "blk": mask_blk[0].reshape(-1, count)}
    own = {"sub": own_sub, "blk": own_blk}
    size = {"sub": sub_size, "blk": blk_size}

    slots = []
    rounds = [("sub", k) for k in range(sub_size - 1, 0, -1)] + [("blk", k) for k in range(blk_size - 1, 0, -1)]
    for axis, step in rounds:
        target, source = partner(own[axis], step, size[axis])
        pick = lax.dynamic_index_in_dim(picks[axis], target, 0, keepdims=False)
        outgoing = lax.dynamic_index_in_dim(blocks, pick, 0, keepdims=False)
        arrived = lax.ppermute(outgoing, axis, pairs(step, size[axis]))
        mask = lax.dynamic_index_in_dim(masks[axis], source, 0, keepdims=False)
        slots.append((axis, step, pick, arrived, mask))

    unit_rows = normalize(embeds)
    totals = jnp.zeros((count, BLOCK), jnp.float32)
    for axis, step, pick, arrived, mask in reversed(slots):
        local, back = sweep(arrived, unit_rows, mask)
        back_pairs = [(b, a) for a, b in pairs(step, size[axis])]
        returned = lax.ppermute(back, axis, back_pairs)
        mine = (jnp.arange(count, dtype=jnp.int32) == pick)[:, None]
        totals = totals + local + jnp.where(mine, returned[None, :], 0.0)
    return totals.reshape(-1) / BLOCK


def solution(mesh):
    return jax.shard_map(
        body,
        mesh=mesh,
        in_specs=(
            P(("groups", "blk", "sub"), None),
            P(("groups", "blk", "sub"), None),
            P(("groups", "blk", "sub"), None),
            P(("groups", "blk"), None),
            P(("groups", "blk", "sub"), None),
        ),
        out_specs=P(("groups", "blk", "sub")),
        check_vma=False,
    )
```

time: 113 us -> 80.7 us (0.71)
  waiting for transfers between devices: 66.1 us -> 17.4 us
  between operations: 0.15 us -> 11.3 us
  other arithmetic: 4.12 us -> 12.9 us
  matrix products: 17 us -> 11.7 us
  starting transfers between devices: 16.8 us -> 19.1 us
    all_to_all x4 -> x0, waiting for transfers between devices: 66.1 us -> none  [the longest x1 38.5 us: body(): lax.all_to_all(blocks[sub_picks], 'sub', split_axis=0, concat_axis=0, til...]
    ppermute x0 -> x12, starting transfers between devices: none -> 19.1 us  [the longest x6 11.6 us: body(): returned = lax.ppermute(back, axis, back_pairs)]
    ppermute x0 -> x12, waiting for transfers between devices: none -> 17.4 us  [the longest x6 13.8 us: body(): arrived = lax.ppermute(outgoing, axis, pairs(step, size[axis]))]
    all_to_all x4 -> x0, starting transfers between devices: 16.8 us -> none  [the longest x1 5.7 us: body(): lax.all_to_all(blocks[sub_picks], 'sub', split_axis=0, concat_axis=0, til...]
    dot_general x10 -> x6, matrix products: 17 us -> 11.7 us  [sweep(): lax.dot_general(normalize(arrived), unit_rows, (((1,), (1,)), ((), ())),...]
    reduce_sum x1 -> x7, other arithmetic: 2.22 us -> 6.78 us  [normalize(): scale = lax.rsqrt(jnp.sum(wide * wide, axis=1, keepdims=True) + 1e-06)]
    gather x2 -> x0, local copies, waits for them, and re-layouts: 4.04 us -> none  [the longest x1 2.03 us: body(): outgoing = blocks[blk_picks]]
    eq x0 -> x6, other arithmetic: none -> 3.71 us  [body(): mine = (jnp.arange(count, dtype=jnp.int32) == pick)[:, None]]
  transfers between devices with their start and end apart: 4 -> 12, of which waited for: 3 -> 3; matrix products, arithmetic and copies ran while one was open for 20% -> 31% of each run, Pallas kernels for 0% -> 0%
where the time goes in v1:
time: 80.7 us; the launch traced here: 79.8 us
  starting transfers between devices  19.1 us (24%)
  waiting for transfers between devices  17.4 us (22%)
  other arithmetic  12.9 us (16%)
  matrix products  11.7 us (14%)
  between operations  11.3 us (14%)
  local copies, waits for them, and re-layouts  7.4 us (9%)
    ppermute x6, waiting for transfers between devices, body(): arrived = lax.ppermute(outgoing, axis, pairs(step, size[axis]))  13.8 us
    dot_general x6, matrix products, sweep(): lax.dot_general(normalize(arrived), unit_rows, (((1,), (1,)), ((), ())),...  11.7 us
    ppermute x6, starting transfers between devices, body(): returned = lax.ppermute(back, axis, back_pairs)  11.6 us
    ppermute x6, starting transfers between devices, body(): arrived = lax.ppermute(outgoing, axis, pairs(step, size[axis]))  7.54 us
    reduce_sum x7, other arithmetic, normalize(): scale = lax.rsqrt(jnp.sum(wide * wide, axis=1, keepdims=True) + 1e-06)  6.78 us
    eq x6, other arithmetic, body(): mine = (jnp.arange(count, dtype=jnp.int32) == pick)[:, None]  3.71 us
    ppermute x6, waiting for transfers between devices, body(): returned = lax.ppermute(back, axis, back_pairs)  3.62 us
    squeeze x1, local copies, waits for them, and re-layouts, body(): outgoing = lax.dynamic_index_in_dim(blocks, pick, 0, keepdims=False)  3.51 us
  transfers between devices with their start and end apart: 12, of which 3 were waited for; matrix products, arithmetic and copies ran while one was open for 31% of the time, Pallas kernels for 0%

profile of v1, /device:TPU:0, one launch (start us, length us, event | category | flops | bytes accessed | tf_op | source)
XLA Modules:
  0.0 79.8 jit_solution(2080457885010791737)
XLA Ops:
  0.0 1.4 %fusion.86 = (s32[1,1]{1,0:T(1,128)}, s32[1,1]{1,0:T(1,128)}, s32[1,1]{1,0:T(1,128)}) fusion(s32[4,4]{1,0:T(4,128)} %param.8, s32[]{:T(128)S(6)} %select_n.112, s32[]{:T(128)S(6)} %select_n.114, s32[]{:T(128)S(6)} %select_n.124, s32[]{:T(128)S(6)} %select_n.119), kind=kLoop, calls=%fused_computation.135 | loop fusion | bytes 40 | tf_op jit(solution)/shard_map/jit(dynamic_index_in_dim)/dynamic_slice | solution.py:54
  5.2 1.4 %constant_dynamic-slice_fusion.8 = (s32[1,1]{1,0:T(1,128)}, s32[1,1]{1,0:T(1,128)}, s32[1,1]{1,0:T(1,128)}) fusion(s32[1,4]{1,0:T(1,128)} %param.6, s32[]{:T(128)S(6)} %select_n.99, s32[]{:T(128)S(6)} %select_n.107, s32[]{:T(128)S(6)} %select_n.103), kind=kLoop, calls=%fused_computation.98 | loop fusion | bytes 36 | tf_op jit(solution)/shard_map/jit(dynamic_index_in_dim)/dynamic_slice | solution.py:54
  14.0 3.5 %dynamic-slice_bitcast_fusion.5 = (bf16[256,1024]{1,0:T(8,128)(2,1)}, bf16[256,1024]{1,0:T(8,128)(2,1)S(1)}, bf16[256,1024]{1,0:T(8,128)(2,1)S(1)}, bf16[256,102...) fusion(bf16[4,256,1024]{2,1,0:T(8,128)(2,1)} %bitcast.67, s32[]{:T(128)S(6)} %select_n.100, ...), kind=kLoop, calls=%fused_computation.81 | loop fusion | bytes 6291480 | tf_op jit(solution)/shard_map/jit(dynamic_index_in_dim)/squeeze | solution.py:55
  17.5 0.4 collective-permute-start
  17.9 2.5 %collective-permute-start.2 = (bf16[256,1024]{1,0:T(8,128)(2,1)}, bf16[256,1024]{1,0:T(8,128)(2,1)}, u32[]{:S(2)}, u32[]{:S(2)}) collective-permute-start(bf16[256,1024]{1,0:T(8,128)(2,1)} %get-tuple-element.22), channel_id=1, source_target_pairs={{0,8},{4,12},{8,0},{12,4},{1,9},{5,13},{9,1},{13,5},{2,10},{6,14},... | collective-permute-start | bytes 1572872 | tf_op jit(solution)/shard_map/ppermute | solution.py:56
  20.4 0.1 collective-permute-start.4
  20.6 1.8 %collective-permute-start.6 = (bf16[256,1024]{1,0:T(8,128)(2,1)}, bf16[256,1024]{1,0:T(8,128)(2,1)}, u32[]{:S(2)}, u32[]{:S(2)}) collective-permute-start(bf16[256,1024]{1,0:T(8,128)(2,1)} %get-tuple-element.20), channel_id=1, source_target_pairs={{0,1},{1,0},{2,3},{3,2},{4,5},{5,4},{6,7},{7,6},{8,9},{9,8},{10,11... | collective-permute-start | bytes 1572872 | tf_op jit(solution)/shard_map/ppermute | solution.py:56
  22.4 2.6 %collective-permute-start.8 = (bf16[256,1024]{1,0:T(8,128)(2,1)S(1)}, bf16[256,1024]{1,0:T(8,128)(2,1)}, u32[]{:S(2)}, u32[]{:S(2)}) collective-permute-start(bf16[256,1024]{1,0:T(8,128)(2,1)S(1)} %get-tuple-element.19), channel_id=1, source_target_pairs={{0,2},{1,3},{2,0},{3,1},{4,6},{5,7},{6,4},{7,5},{8,10},{9,11},{10,... | collective-permute-start | bytes 1572872 | tf_op jit(solution)/shard_map/ppermute | solution.py:56
  25.0 0.6 iota_compare_fusion.5
  25.6 0.6 iota_compare_fusion.4
  26.3 0.6 iota_compare_fusion.3
  26.8 0.6 iota_compare_fusion.2
  27.4 0.7 iota_compare_fusion.1
  28.1 0.5 broadcast.167
  28.6 0.7 reduce.19
  29.2 0.1 reshape_squeeze.6
  29.5 0.7 reduce.18
  30.2 0.1 reshape_squeeze.7
  30.4 0.6 iota_compare_fusion
  31.1 0.5 fusion
  31.6 0.1 collective-permute-start.10
  31.7 1.2 %fusion.38 = f32[256]{0:T(256)S(1)} fusion(bf16[256,1024]{1,0:T(8,128)(2,1)} %collective-permute-done), kind=kLoop, calls=%fused_computation.58 | loop fusion | flops 786176 | bytes 525312 | tf_op jit(solution)/shard_map/reduce_sum | solution.py:14
  32.9 2.1 %fusion.80 = (f32[256]{0:T(256)S(1)}, f32[1024]{0:T(1024)S(1)}) fusion(f32[1024]{0:T(1024)S(1)} %bitcast.79, bf16[1024,1024]{1,0:T(8,128)(2,1)S(1)} %copy-done, f32[1024]{0:T(1024)S(1)} %add_rsqrt_fusion, bf16[256,1024]{1,0:T(8,128)(2,1)} %collective-permute-done, f32[256]{0:T(256)S(1)} %add_rsqrt_fusion.6), kind=kOutput, calls=%fused_computation.129 | convolution fusion | flops 542898944 | bytes 2635776 | tf_op jit(solution)/shard_map/dot_general | solution.py:31
  35.0 0.1 collective-permute-start.1
  35.1 1.2 %fusion.40 = f32[256]{0:T(256)S(1)} fusion(bf16[256,1024]{1,0:T(8,128)(2,1)} %collective-permute-done.2), kind=kLoop, calls=%fused_computation.60 | loop fusion | flops 786176 | bytes 525312 | tf_op jit(solution)/shard_map/reduce_sum | solution.py:14
  36.3 2.1 %fusion.81 = (f32[1024]{0:T(1024)S(1)}, f32[256]{0:T(256)S(1)}) fusion(f32[1024]{0:T(1024)S(1)} %bitcast.78, bf16[1024,1024]{1,0:T(8,128)(2,1)S(1)} %copy-done, f32[1024]{0:T(1024)S(1)} %add_rsqrt_fusion, bf16[256,1024]{1,0:T(8,128)(2,1)} %collective-permute-done.2, f32[256]{0:T(256)S(1)} %add_rsqrt_fusion.5), kind=kOutput, calls=%fused_computation.130 | convolution fusion | flops 542898944 | bytes 2635776 | tf_op jit(solution)/shard_map/dot_general | solution.py:31
  38.5 5.9 %collective-permute-done.4 = bf16[256,1024]{1,0:T(8,128)(2,1)} collective-permute-done((bf16[256,1024]{1,0:T(8,128)(2,1)}, bf16[256,1024]{1,0:T(8,128)(2,1)}, u32[]{:S(2)}, u32[]{:S(2)}) %collective-permute-start.4) | collective-permute-done | bytes 524320 | tf_op jit(solution)/shard_map/ppermute | solution.py:56
  44.4 1.6 %collective-permute-start.3 = (f32[256]{0:T(256)S(1)}, f32[256]{0:T(256)S(1)}, u32[]{:S(2)}, u32[]{:S(2)}) collective-permute-start(f32[256]{0:T(256)S(1)} %get-tuple-element.8), channel_id=1, source_target_pairs={{8,0},{12,4},{0,8},{4,12},{9,1},{13,5},{1,9},{5,13},{10,2},{14,6},... | collective-permute-start | bytes 3080 | tf_op jit(solution)/shard_map/ppermute | solution.py:65
  46.0 1.2 %fusion.42 = f32[256]{0:T(256)S(1)} fusion(bf16[256,1024]{1,0:T(8,128)(2,1)} %collective-permute-done.4), kind=kLoop, calls=%fused_computation.62 | loop fusion | flops 786176 | bytes 525312 | tf_op jit(solution)/shard_map/reduce_sum | solution.py:14
  47.2 2.1 %fusion.82 = (f32[1024]{0:T(1024)S(1)}, f32[256]{0:T(256)S(1)}) fusion(f32[1024]{0:T(1024)S(1)} %bitcast.77, bf16[1024,1024]{1,0:T(8,128)(2,1)S(1)} %copy-done, f32[1024]{0:T(1024)S(1)} %add_rsqrt_fusion, bf16[256,1024]{1,0:T(8,128)(2,1)} %collective-permute-done.4, f32[256]{0:T(256)S(1)} %add_rsqrt_fusion.4), kind=kOutput, calls=%fused_computation.131 | convolution fusion | flops 542898944 | bytes 2635776 | tf_op jit(solution)/shard_map/dot_general | solution.py:31
  49.3 0.2 collective-permute-start.5
  49.5 1.2 %fusion.44 = f32[256]{0:T(256)S(1)} fusion(bf16[256,1024]{1,0:T(8,128)(2,1)} %collective-permute-done.6), kind=kLoop, calls=%fused_computation.64 | loop fusion | flops 786176 | bytes 525312 | tf_op jit(solution)/shard_map/reduce_sum | solution.py:14
  50.7 2.1 %fusion.83 = (f32[1024]{0:T(1024)S(1)}, f32[256]{0:T(256)S(1)}) fusion(f32[1024]{0:T(1024)S(1)} %bitcast.76, bf16[1024,1024]{1,0:T(8,128)(2,1)S(1)} %copy-done, f32[1024]{0:T(1024)S(1)} %add_rsqrt_fusion, bf16[256,1024]{1,0:T(8,128)(2,1)} %collective-permute-done.6, f32[256]{0:T(256)S(1)} %add_rsqrt_fusion.3), kind=kOutput, calls=%fused_computation.132 | convolution fusion | flops 542898944 | bytes 2635776 | tf_op jit(solution)/shard_map/dot_general | solution.py:31
  52.8 7.9 %collective-permute-done.8 = bf16[256,1024]{1,0:T(8,128)(2,1)} collective-permute-done((bf16[256,1024]{1,0:T(8,128)(2,1)S(1)}, bf16[256,1024]{1,0:T(8,128)(2,1)}, u32[]{:S(2)}, u32[]{:S(2)}) %collective-permute-start.8) | collective-permute-done | bytes 524320 | tf_op jit(solution)/shard_map/ppermute | solution.py:56
  60.7 1.2 %fusion.46 = f32[256]{0:T(256)S(1)} fusion(bf16[256,1024]{1,0:T(8,128)(2,1)} %collective-permute-done.8), kind=kLoop, calls=%fused_computation.66 | loop fusion | flops 786176 | bytes 525312 | tf_op jit(solution)/shard_map/reduce_sum | solution.py:14
  61.9 2.1 %fusion.84 = (f32[1024]{0:T(1024)S(1)}, f32[256]{0:T(256)S(1)}) fusion(f32[1024]{0:T(1024)S(1)} %bitcast.75, bf16[1024,1024]{1,0:T(8,128)(2,1)S(1)} %copy-done, f32[1024]{0:T(1024)S(1)} %add_rsqrt_fusion, bf16[256,1024]{1,0:T(8,128)(2,1)} %collective-permute-done.8, f32[256]{0:T(256)S(1)} %add_rsqrt_fusion.2), kind=kOutput, calls=%fused_computation.133 | convolution fusion | flops 542898944 | bytes 2635776 | tf_op jit(solution)/shard_map/dot_general | solution.py:31
  64.0 8.4 %collective-permute-start.9 = (f32[256]{0:T(256)S(1)}, f32[256]{0:T(256)S(1)}, u32[]{:S(2)}, u32[]{:S(2)}) collective-permute-start(f32[256]{0:T(256)S(1)} %get-tuple-element.14), channel_id=1, source_target_pairs={{2,0},{3,1},{0,2},{1,3},{6,4},{7,5},{4,6},{5,7},{10,8},{11,9},{8,1... | collective-permute-start | bytes 3080 | tf_op jit(solution)/shard_map/ppermute | solution.py:65
  72.4 0.2 fusion.48
  72.6 1.1 %fusion.85 = (f32[1024]{0:T(1024)S(1)}, f32[256]{0:T(256)S(1)}) fusion(f32[1024]{0:T(1024)S(1)} %bitcast.74, bf16[1024,1024]{1,0:T(8,128)(2,1)S(1)} %copy-done, f32[1024]{0:T(1024)S(1)} %add_rsqrt_fusion, bf16[256,1024]{1,0:T(8,128)(2,1)S(1)} %collective-permute-done.10, f32[256]{0:T(256)S(1)} %add_rsqrt_fusion.1), kind=kOutput, calls=%fused_computation.134 | convolution fusion | flops 542898944 | bytes 2635776 | tf_op jit(solution)/shard_map/dot_general | solution.py:31
  73.7 1.4 %collective-permute-start.11 = (f32[256]{0:T(256)S(1)}, f32[256]{0:T(256)S(1)}, u32[]{:S(2)}, u32[]{:S(2)}) collective-permute-start(f32[256]{0:T(256)S(1)} %get-tuple-element.16), channel_id=1, source_target_pairs={{3,0},{2,1},{1,2},{0,3},{7,4},{6,5},{5,6},{4,7},{11,8},{10,9},{9,1... | collective-permute-start | bytes 3080 | tf_op jit(solution)/shard_map/ppermute | solution.py:65
  75.1 0.1 select_bitcast_fusion.5
  75.2 0.1 select_bitcast_fusion.4
  75.3 0.1 select_bitcast_fusion.3
  75.4 0.1 select_bitcast_fusion.2
  75.4 0.1 select_bitcast_fusion.1
  75.5 3.6 %collective-permute-done.11 = f32[256]{0:T(256)S(1)} collective-permute-done((f32[256]{0:T(256)S(1)}, f32[256]{0:T(256)S(1)}, u32[]{:S(2)}, u32[]{:S(2)}) %collective-permute-start.11) | collective-permute-done | bytes 1056 | tf_op jit(solution)/shard_map/ppermute | solution.py:65
  79.1 0.1 select_bitcast_fusion
  79.2 0.6 add_multiply_fusion
  (41 shorter events, 0.5 us)
Async XLA Ops:
  13.9 14.6 %copy-start.1 = (s32[1,16]{1,0:T(1,128)S(1)}, s32[1,16]{1,0:T(1,128)}, u32[]{:S(2)}) copy-start(s32[1,16]{1,0:T(1,128)} %param.7) | copy-start | bytes 196
  14.0 15.5 %copy-start.2 = (s32[1,16]{1,0:T(1,128)S(1)}, s32[1,16]{1,0:T(1,128)}, u32[]{:S(2)}) copy-start(s32[1,16]{1,0:T(1,128)} %param.9) | copy-start | bytes 196
  14.0 17.1 %copy-start = (bf16[1024,1024]{1,0:T(8,128)(2,1)S(1)}, bf16[1024,1024]{1,0:T(8,128)(2,1)}, u32[]{:S(2)}) copy-start(bf16[1024,1024]{1,0:T(8,128)(2,1)} %param.5) | copy-start | bytes 6291460
  17.5 14.1 %collective-permute-start = (bf16[256,1024]{1,0:T(8,128)(2,1)}, bf16[256,1024]{1,0:T(8,128)(2,1)}, u32[]{:S(2)}, u32[]{:S(2)}) collective-permute-start(bf16[256,1024]{1,0:T(8,128)(2,1)} %get-tuple-element.17), channel_id=1, source_target_pairs={{0,4},{4,0},{8,12},{12,8},{1,5},{5,1},{9,13},{13,9},{2,6},{6,2},{1... | collective-permute-start | bytes 1572872 | tf_op jit(solution)/shard_map/ppermute | solution.py:56
  17.9 17.1 %collective-permute-start.2 = (bf16[256,1024]{1,0:T(8,128)(2,1)}, bf16[256,1024]{1,0:T(8,128)(2,1)}, u32[]{:S(2)}, u32[]{:S(2)}) collective-permute-start(bf16[256,1024]{1,0:T(8,128)(2,1)} %get-tuple-element.22), channel_id=1, source_target_pairs={{0,8},{4,12},{8,0},{12,4},{1,9},{5,13},{9,1},{13,5},{2,10},{6,14},... | collective-permute-start | bytes 1572872 | tf_op jit(solution)/shard_map/ppermute | solution.py:56
  20.4 24.0 %collective-permute-start.4 = (bf16[256,1024]{1,0:T(8,128)(2,1)}, bf16[256,1024]{1,0:T(8,128)(2,1)}, u32[]{:S(2)}, u32[]{:S(2)}) collective-permute-start(bf16[256,1024]{1,0:T(8,128)(2,1)} %get-tuple-element.21), channel_id=1, source_target_pairs={{0,12},{4,8},{8,4},{12,0},{1,13},{5,9},{9,5},{13,1},{2,14},{6,10},... | collective-permute-start | bytes 1572872 | tf_op jit(solution)/shard_map/ppermute | solution.py:56
  20.6 28.7 %collective-permute-start.6 = (bf16[256,1024]{1,0:T(8,128)(2,1)}, bf16[256,1024]{1,0:T(8,128)(2,1)}, u32[]{:S(2)}, u32[]{:S(2)}) collective-permute-start(bf16[256,1024]{1,0:T(8,128)(2,1)} %get-tuple-element.20), channel_id=1, source_target_pairs={{0,1},{1,0},{2,3},{3,2},{4,5},{5,4},{6,7},{7,6},{8,9},{9,8},{10,11... | collective-permute-start | bytes 1572872 | tf_op jit(solution)/shard_map/ppermute | solution.py:56
  22.4 38.3 %collective-permute-start.8 = (bf16[256,1024]{1,0:T(8,128)(2,1)S(1)}, bf16[256,1024]{1,0:T(8,128)(2,1)}, u32[]{:S(2)}, u32[]{:S(2)}) collective-permute-start(bf16[256,1024]{1,0:T(8,128)(2,1)S(1)} %get-tuple-element.19), channel_id=1, source_target_pairs={{0,2},{1,3},{2,0},{3,1},{4,6},{5,7},{6,4},{7,5},{8,10},{9,11},{10,... | collective-permute-start | bytes 1572872 | tf_op jit(solution)/shard_map/ppermute | solution.py:56
  31.6 32.4 %collective-permute-start.10 = (bf16[256,1024]{1,0:T(8,128)(2,1)S(1)}, bf16[256,1024]{1,0:T(8,128)(2,1)S(1)}, u32[]{:S(2)}, u32[]{:S(2)}) collective-permute-start(bf16[256,1024]{1,0:T(8,128)(2,1)S(1)} %get-tuple-element.18), channel_id=1, source_target_pairs={{0,3},{1,2},{2,1},{3,0},{4,7},{5,6},{6,5},{7,4},{8,11},{9,10},{10,... | collective-permute-start | bytes 1572872 | tf_op jit(solution)/shard_map/ppermute | solution.py:56
  35.0 38.7 %collective-permute-start.1 = (f32[256]{0:T(256)S(1)}, f32[256]{0:T(256)S(1)}, u32[]{:S(2)}, u32[]{:S(2)}) collective-permute-start(f32[256]{0:T(256)S(1)} %get-tuple-element.5), channel_id=1, source_target_pairs={{4,0},{0,4},{12,8},{8,12},{5,1},{1,5},{13,9},{9,13},{6,2},{2,6},{1... | collective-permute-start | bytes 3080 | tf_op jit(solution)/shard_map/ppermute | solution.py:65
  44.4 30.8 %collective-permute-start.3 = (f32[256]{0:T(256)S(1)}, f32[256]{0:T(256)S(1)}, u32[]{:S(2)}, u32[]{:S(2)}) collective-permute-start(f32[256]{0:T(256)S(1)} %get-tuple-element.8), channel_id=1, source_target_pairs={{8,0},{12,4},{0,8},{4,12},{9,1},{13,5},{1,9},{5,13},{10,2},{14,6},... | collective-permute-start | bytes 3080 | tf_op jit(solution)/shard_map/ppermute | solution.py:65
  49.3 26.0 %collective-permute-start.5 = (f32[256]{0:T(256)S(1)}, f32[256]{0:T(256)S(1)}, u32[]{:S(2)}, u32[]{:S(2)}) collective-permute-start(f32[256]{0:T(256)S(1)} %get-tuple-element.10), channel_id=1, source_target_pairs={{12,0},{8,4},{4,8},{0,12},{13,1},{9,5},{5,9},{1,13},{14,2},{10,6},... | collective-permute-start | bytes 3080 | tf_op jit(solution)/shard_map/ppermute | solution.py:65
  60.7 14.7 %collective-permute-start.7 = (f32[256]{0:T(256)S(1)}, f32[256]{0:T(256)S(1)}, u32[]{:S(2)}, u32[]{:S(2)}) collective-permute-start(f32[256]{0:T(256)S(1)} %get-tuple-element.12), channel_id=1, source_target_pairs={{1,0},{0,1},{3,2},{2,3},{5,4},{4,5},{7,6},{6,7},{9,8},{8,9},{11,10... | collective-permute-start | bytes 3080 | tf_op jit(solution)/shard_map/ppermute | solution.py:65
  64.0 11.4 %collective-permute-start.9 = (f32[256]{0:T(256)S(1)}, f32[256]{0:T(256)S(1)}, u32[]{:S(2)}, u32[]{:S(2)}) collective-permute-start(f32[256]{0:T(256)S(1)} %get-tuple-element.14), channel_id=1, source_target_pairs={{2,0},{3,1},{0,2},{1,3},{6,4},{7,5},{4,6},{5,7},{10,8},{11,9},{8,1... | collective-permute-start | bytes 3080 | tf_op jit(solution)/shard_map/ppermute | solution.py:65
  73.7 5.4 %collective-permute-start.11 = (f32[256]{0:T(256)S(1)}, f32[256]{0:T(256)S(1)}, u32[]{:S(2)}, u32[]{:S(2)}) collective-permute-start(f32[256]{0:T(256)S(1)} %get-tuple-element.16), channel_id=1, source_target_pairs={{3,0},{2,1},{1,2},{0,3},{7,4},{6,5},{5,6},{4,7},{11,8},{10,9},{9,1... | collective-permute-start | bytes 3080 | tf_op jit(solution)/shard_map/ppermute | solution.py:65

commit v2 on v1

v2 whole, which is shorter than its diff:
```python
import functools

import jax
import jax.numpy as jnp
from jax import lax
from jax.experimental import pallas as pl
from jax.experimental.pallas import tpu as pltpu
from jax.sharding import PartitionSpec as P

BLOCK = 256

cutoff = 0.05
sharpness = 100.0


def partner(index, step, size):
    if size & (size - 1) == 0:
        return index ^ step, index ^ step
    return lax.rem(index + step, size), lax.rem(index + size - step, size)


def pairs(step, size):
    if size & (size - 1) == 0:
        return [(i, i ^ step) for i in range(size)]
    return [(i, (i + step) % size) for i in range(size)]


def rounded_units(rows):
    wide = rows.astype(jnp.float32)
    scale = lax.rsqrt(jnp.sum(wide * wide, axis=1, keepdims=True) + 1e-06)
    return (wide * scale).astype(jnp.bfloat16)


def take_pick(rounds, sizes, pick_blk, pick_sub, place):
    axis, step = rounds[place]
    target, _ = partner(lax.axis_index(axis), step, sizes[axis])
    return pick_blk[0, target] if axis == "blk" else pick_sub[lax.axis_index("sub"), target]


def pick_kernel(rounds, sizes, pick_blk, pick_sub, embeds, *rest):
    outs, sems = rest[:-1], rest[-1]
    copies = []
    for place, out in enumerate(outs):
        pick = take_pick(rounds, sizes, pick_blk, pick_sub, place)
        rows = pl.ds(pl.multiple_of(pick * BLOCK, BLOCK), BLOCK)
        copies.append(pltpu.make_async_copy(embeds.at[rows], out, sems.at[place]))
    for copy in copies:
        copy.start()
    for copy in copies:
        copy.wait()


def pick_blocks(rounds, sizes, pick_blk, pick_sub, embeds):
    smem, any_space = pl.BlockSpec(memory_space=pltpu.SMEM), pl.BlockSpec(memory_space=pl.ANY)
    shape = jax.ShapeDtypeStruct((BLOCK, embeds.shape[1]), embeds.dtype)
    return pl.pallas_call(
        functools.partial(pick_kernel, rounds, sizes),
        out_shape=[shape] * len(rounds),
        in_specs=[smem, smem, any_space],
        out_specs=[any_space] * len(rounds),
        scratch_shapes=[pltpu.SemaphoreType.DMA((len(rounds),))],
    )(pick_blk, pick_sub, embeds)


def unit_kernel(embeds, units):
    for start in range(0, embeds.shape[0], BLOCK):
        units[start : start + BLOCK] = rounded_units(embeds[start : start + BLOCK])


def unit_rows(embeds):
    vmem = pl.BlockSpec(memory_space=pltpu.VMEM)
    return pl.pallas_call(
        unit_kernel,
        out_shape=jax.ShapeDtypeStruct(embeds.shape, embeds.dtype),
        in_specs=[vmem],
        out_specs=vmem,
        compiler_params=pltpu.CompilerParams(vmem_limit_bytes=32 * 2**20),
    )(embeds)


def add_returned(totals, pick, sums):
    totals[pl.ds(pick, 1)] = totals[pl.ds(pick, 1)] + sums[...]


def slot_kernel(rounds, sizes, place, back_place, mask, pick_blk, pick_sub, arrived, units, totals, *rest):
    axis, step = rounds[place]
    _, source = partner(lax.axis_index(axis), step, sizes[axis])
    count = units.shape[0] // BLOCK
    new_totals, back = rest[-2:]
    x = rounded_units(arrived[...])
    along_rows = jnp.zeros((BLOCK, 128), jnp.float32)
    for i in range(count):
        y = units[i * BLOCK : (i + 1) * BLOCK]
        cosines = lax.dot_general(x, y, (((1,), (1,)), ((), ())), preferred_element_type=jnp.float32)
        weights = jax.nn.sigmoid((cosines - cutoff) * sharpness)
        live = mask[0, source * count + i].astype(jnp.float32)
        new_totals[i : i + 1] = totals[i : i + 1] + live * jnp.sum(weights, axis=0, keepdims=True)
        for lane in range(0, BLOCK, 128):
            along_rows = along_rows + live * weights[:, lane : lane + 128]
    back[...] = jnp.sum(along_rows.T, axis=0, keepdims=True)
    if back_place is not None:
        add_returned(new_totals, take_pick(rounds, sizes, pick_blk, pick_sub, back_place), rest[0])


def slot(rounds, sizes, place, masks, pick_blk, pick_sub, arrived, units, totals, back_place, returned):
    smem, vmem = pl.BlockSpec(memory_space=pltpu.SMEM), pl.BlockSpec(memory_space=pltpu.VMEM)
    operands = [masks[rounds[place][0]], pick_blk, pick_sub, arrived, units, totals]
    if back_place is not None:
        operands.append(returned)
    return pl.pallas_call(
        functools.partial(slot_kernel, rounds, sizes, place, back_place),
        out_shape=[
            jax.ShapeDtypeStruct(totals.shape, jnp.float32),
            jax.ShapeDtypeStruct((1, BLOCK), jnp.float32),
        ],
        in_specs=[smem] * 3 + [vmem] * (len(operands) - 3),
        out_specs=[vmem, vmem],
        compiler_params=pltpu.CompilerParams(vmem_limit_bytes=32 * 2**20),
    )(*operands)


def credit_kernel(rounds, sizes, places, pick_blk, pick_sub, totals, *rest):
    returned, out = rest[:-1], rest[-1]
    out[...] = totals[...]
    for place, sums in zip(places, returned):
        add_returned(out, take_pick(rounds, sizes, pick_blk, pick_sub, place), sums)
    out[...] = out[...] / BLOCK


def credit(rounds, sizes, places, pick_blk, pick_sub, totals, returned):
    smem, vmem = pl.BlockSpec(memory_space=pltpu.SMEM), pl.BlockSpec(memory_space=pltpu.VMEM)
    return pl.pallas_call(
        functools.partial(credit_kernel, rounds, sizes, places),
        out_shape=jax.ShapeDtypeStruct(totals.shape, jnp.float32),
        in_specs=[smem, smem, vmem] + [vmem] * len(returned),
        out_specs=vmem,
    )(pick_blk, pick_sub, totals, *returned)


def interleave(sub_size, blk_size):
    sub = [("sub", k) for k in ([2, 3, 1] if sub_size == 4 else range(1, sub_size))]
    blk = [("blk", k) for k in range(2, blk_size)]
    order = [("blk", 1)]
    for place in range(max(len(sub), len(blk))):
        order += sub[place : place + 1] + blk[place : place + 1]
    return order


BEHIND = 2


def body(embeds, pick_blk, mask_blk, pick_sub, mask_sub):
    count = embeds.shape[0] // BLOCK
    sizes = {"sub": lax.axis_size("sub"), "blk": lax.axis_size("blk")}
    masks = {"sub": mask_sub, "blk": mask_blk}
    rounds = interleave(sizes["sub"], sizes["blk"])

    outgoing = pick_blocks(rounds, sizes, pick_blk, pick_sub, embeds)
    arrived = [lax.ppermute(sent, axis, pairs(step, sizes[axis])) for (axis, step), sent in zip(rounds, outgoing)]

    units = unit_rows(embeds)
    totals = jnp.zeros((count, BLOCK), jnp.float32)
    returned = []
    for place, (axis, step) in enumerate(rounds):
        back_place = place - BEHIND if place >= BEHIND else None
        came_back = None if back_place is None else returned[back_place]
        totals, back = slot(
            rounds, sizes, place, masks, pick_blk, pick_sub, arrived[place], units, totals, back_place, came_back
        )
        returned.append(lax.ppermute(back, axis, [(b, a) for a, b in pairs(step, sizes[axis])]))
    last = list(range(len(rounds) - BEHIND, len(rounds)))
    out = credit(rounds, sizes, last, pick_blk, pick_sub, totals, [returned[place] for place in last])
    return out.reshape(-1)


def solution(mesh):
    return jax.shard_map(
        body,
        mesh=mesh,
        in_specs=(
            P(("groups", "blk", "sub"), None),
            P(("groups", "blk", "sub"), None),
            P(("groups", "blk", "sub"), None),
            P(("groups", "blk"), None),
            P(("groups", "blk", "sub"), None),
        ),
        out_specs=P(("groups", "blk", "sub")),
        check_vma=False,
    )
```

time: 80.7 us -> 164 us (2.03)
  Pallas kernels: 0 us -> 109 us
  waiting for transfers between devices: 17.4 us -> 39.2 us
  other arithmetic: 12.9 us -> 0 us
  matrix products: 11.7 us -> 0 us
  between operations: 11.3 us -> 0.14 us
  starting transfers between devices: 19.1 us -> 13.3 us
  local copies, waits for them, and re-layouts: 7.4 us -> 2.48 us
    pallas_call x0 -> x9, Pallas kernels: none -> 109 us  [the longest x1 97.3 us: pick_blocks(): pl.pallas_call(functools.partial(pick_kernel, rounds, sizes), out_shape=[...]
    ppermute x12, waiting for transfers between devices: 17.4 us -> 39.2 us  [the longest x6 30 us: body(): lax.ppermute(sent, axis, pairs(step, sizes[axis]))]
    dot_general x6 -> x0, matrix products: 11.7 us -> none  [sweep(): lax.dot_general(normalize(arrived), unit_rows, (((1,), (1,)), ((), ())),...]
    reduce_sum x7 -> x0, other arithmetic: 6.78 us -> none  [normalize(): scale = lax.rsqrt(jnp.sum(wide * wide, axis=1, keepdims=True) + 1e-06)]
    ppermute x12, starting transfers between devices: 19.1 us -> 13.3 us  [the longest x6 7.34 us: body(): lax.ppermute(sent, axis, pairs(step, sizes[axis]))]
    eq x6 -> x0, other arithmetic: 3.71 us -> none  [body(): mine = (jnp.arange(count, dtype=jnp.int32) == pick)[:, None]]
    squeeze x1 -> x0, local copies, waits for them, and re-layouts: 3.51 us -> none  [body(): outgoing = lax.dynamic_index_in_dim(blocks, pick, 0, keepdims=False)]
    dynamic_slice x2 -> x0, local copies, waits for them, and re-layouts: 2.85 us -> none  [body(): pick = lax.dynamic_index_in_dim(picks[axis], target, 0, keepdims=False)]
  transfers between devices with their start and end apart: 12 -> 12, of which waited for: 3 -> 4; matrix products, arithmetic and copies ran while one was open for 31% -> 0% of each run, Pallas kernels for 0% -> 5%
where the time goes in v2:
time: 164 us
  Pallas kernels  109 us (66%)
  waiting for transfers between devices  39.2 us (24%)
  starting transfers between devices  13.3 us (8%)
  local copies, waits for them, and re-layouts  2.48 us (2%)
    pallas_call x1, Pallas kernels, pick_blocks(): pl.pallas_call(functools.partial(pick_kernel, rounds, sizes), out_shape=[...  97.3 us
    ppermute x6, waiting for transfers between devices, body(): lax.ppermute(sent, axis, pairs(step, sizes[axis]))  30 us
    pallas_call x6, Pallas kernels, slot(): pl.pallas_call(functools.partial(slot_kernel, rounds, sizes, place, back_...  9.71 us
    ppermute x6, waiting for transfers between devices, body(): lax.ppermute(back, axis, [(b, a) for a, b in pairs(step, sizes[axis])])  9.16 us
    ppermute x6, starting transfers between devices, body(): lax.ppermute(sent, axis, pairs(step, sizes[axis]))  7.34 us
    ppermute x6, starting transfers between devices, body(): lax.ppermute(back, axis, [(b, a) for a, b in pairs(step, sizes[axis])])  5.95 us
  transfers between devices with their start and end apart: 12, of which 4 were waited for; matrix products, arithmetic and copies ran while one was open for 0% of the time, Pallas kernels for 5%

profile of v2, /device:TPU:0, one launch (start us, length us, event | category | flops | bytes accessed | tf_op | source)
XLA Modules:
  0.0 164.2 jit_solution(15416154517215658211)
XLA Ops:
  0.0 0.0 copy-start
  0.0 97.3 %shard_map.55 = (bf16[256,1024]{1,0:T(8,128)(2,1)}, bf16[256,1024]{1,0:T(8,128)(2,1)}, bf16[256,1024]{1,0:T(8,128)(2,1)}, bf16[256,1024]{1,0:T(8,128)(2,1)}, bf1...) custom-call(s32[1,4]{1,0:T(1,128)} %pick_blk.15, s32[4,4]{1,0:T(4,128)} %pick_sub.15, bf16[1024,1024]{1,0:T(8,128)(2,1)} %embeds.3), custom_call_target="tpu_custom_call" | custom-call | tf_op jit(solution)/shard_map/pallas_call | solution.py:56
  97.3 0.5 collective-permute-start.5
  97.8 3.7 %collective-permute-start.4 = (bf16[256,1024]{1,0:T(8,128)(2,1)}, bf16[256,1024]{1,0:T(8,128)(2,1)S(1)}, u32[]{:S(2)}, u32[]{:S(2)}) collective-permute-start(bf16[256,1024]{1,0:T(8,128)(2,1)} %get-tuple-element.27), channel_id=1, source_target_pairs={{0,2},{1,3},{2,0},{3,1},{4,6},{5,7},{6,4},{7,5},{8,10},{9,11},{10,... | collective-permute-start | bytes 1572872 | tf_op jit(solution)/shard_map/ppermute | solution.py:159
  101.5 1.5 collective-permute-start.3
  103.0 1.3 collective-permute-start.2
  104.3 0.0 collective-permute-start.1
  104.3 0.0 collective-permute-done.5.arrived
  104.3 0.0 copy-start.1
  104.3 0.0 copy-start.2
  104.3 0.0 copy-start.3
  104.4 0.3 collective-permute-start
  104.7 0.0 copy-done
  104.7 0.6 shard_map.56.units
  105.3 0.0 copy-start.4
  105.3 0.0 copy-done.1
  105.4 0.0 copy-done.2
  105.4 0.0 copy-done.3
  105.4 1.6 shard_map.57
  107.0 30.0 %collective-permute-done.4.arrived = bf16[256,1024]{1,0:T(8,128)(2,1)S(1)} collective-permute-done((bf16[256,1024]{1,0:T(8,128)(2,1)}, bf16[256,1024]{1,0:T(8,128)(2,1)S(1)}, u32[]{:S(2)}, u32[]{:S(2)}) %collective-permute-start.4) | collective-permute-done | bytes 524320 | tf_op jit(solution)/shard_map/ppermute | solution.py:159
  137.0 0.0 collective-permute-start.6
  137.0 0.0 copy-done.4
  137.0 1.6 shard_map.58
  138.6 0.0 collective-permute-done.3.arrived
  138.6 0.1 collective-permute-start.7
  138.7 0.0 collective-permute-done.6.rest_0_
  138.7 1.6 shard_map.59
  140.3 1.8 %collective-permute-start.8 = (f32[1,256]{1,0:T(1,128)S(1)}, f32[1,256]{1,0:T(1,128)S(1)}, u32[]{:S(2)}, u32[]{:S(2)}) collective-permute-start(f32[1,256]{1,0:T(1,128)S(1)} %get-tuple-element.35), channel_id=1, source_target_pairs={{8,0},{12,4},{0,8},{4,12},{9,1},{13,5},{1,9},{5,13},{10,2},{14,6},... | collective-permute-start | bytes 3080 | tf_op jit(solution)/shard_map/ppermute | solution.py:170
  142.2 0.0 collective-permute-done.2.arrived
  142.2 5.8 %collective-permute-done.7.rest_0_ = f32[1,256]{1,0:T(1,128)S(1)} collective-permute-done((f32[1,256]{1,0:T(1,128)S(1)}, f32[1,256]{1,0:T(1,128)S(1)}, u32[]{:S(2)}, u32[]{:S(2)}) %collective-permute-start.7) | collective-permute-done | bytes 1056 | tf_op jit(solution)/shard_map/ppermute | solution.py:170
  148.0 1.6 shard_map.60
  149.6 3.6 %collective-permute-start.9 = (f32[1,256]{1,0:T(1,128)S(1)}, f32[1,256]{1,0:T(1,128)S(1)}, u32[]{:S(2)}, u32[]{:S(2)}) collective-permute-start(f32[1,256]{1,0:T(1,128)S(1)} %get-tuple-element.37), channel_id=1, source_target_pairs={{3,0},{2,1},{1,2},{0,3},{7,4},{6,5},{5,6},{4,7},{11,8},{10,9},{9,1... | collective-permute-start | bytes 3080 | tf_op jit(solution)/shard_map/ppermute | solution.py:170
  153.2 0.0 collective-permute-done.1.arrived
  153.2 0.0 collective-permute-done.8.rest_0_
  153.2 1.6 shard_map.61
  154.9 0.0 collective-permute-done.arrived
  154.9 0.2 collective-permute-done.9.rest_0_
  155.1 1.6 shard_map.62
  156.7 0.0 copy-start.5
  156.7 0.6 copy-done.5
  157.3 0.0 collective-permute-start.11
  157.3 0.4 collective-permute-start.10
  157.7 3.1 %collective-permute-done.11.rest_1_ = f32[1,256]{1,0:T(1,128)S(1)} collective-permute-done((f32[1,256]{1,0:T(1,128)S(1)}, f32[1,256]{1,0:T(1,128)S(1)}, u32[]{:S(2)}, u32[]{:S(2)}) %collective-permute-start.11) | collective-permute-done | bytes 1056 | tf_op jit(solution)/shard_map/ppermute | solution.py:170
  160.8 0.0 collective-permute-done.10.rest_0_
  160.8 0.6 copy-done.6
  161.4 0.0 copy-done.7
  161.4 1.5 shard_map.63
  162.9 1.3 copy.6
  (3 shorter events, 0.0 us)
Async XLA Ops:
  0.0 104.7 %copy-start = (bf16[1024,1024]{1,0:T(8,128)(2,1)S(1)}, bf16[1024,1024]{1,0:T(8,128)(2,1)}, u32[]{:S(2)}) copy-start(bf16[1024,1024]{1,0:T(8,128)(2,1)} %embeds.3) | copy-start | bytes 6291460
  97.3 7.0 %collective-permute-start.5 = (bf16[256,1024]{1,0:T(8,128)(2,1)}, bf16[256,1024]{1,0:T(8,128)(2,1)S(1)}, u32[]{:S(2)}, u32[]{:S(2)}) collective-permute-start(bf16[256,1024]{1,0:T(8,128)(2,1)} %get-tuple-element.28), channel_id=1, source_target_pairs={{0,4},{4,0},{8,12},{12,8},{1,5},{5,1},{9,13},{13,9},{2,6},{6,2},{1... | collective-permute-start | bytes 1572872 | tf_op jit(solution)/shard_map/ppermute | solution.py:159
  97.8 39.2 %collective-permute-start.4 = (bf16[256,1024]{1,0:T(8,128)(2,1)}, bf16[256,1024]{1,0:T(8,128)(2,1)S(1)}, u32[]{:S(2)}, u32[]{:S(2)}) collective-permute-start(bf16[256,1024]{1,0:T(8,128)(2,1)} %get-tuple-element.27), channel_id=1, source_target_pairs={{0,2},{1,3},{2,0},{3,1},{4,6},{5,7},{6,4},{7,5},{8,10},{9,11},{10,... | collective-permute-start | bytes 1572872 | tf_op jit(solution)/shard_map/ppermute | solution.py:159
  101.5 37.1 %collective-permute-start.3 = (bf16[256,1024]{1,0:T(8,128)(2,1)}, bf16[256,1024]{1,0:T(8,128)(2,1)S(1)}, u32[]{:S(2)}, u32[]{:S(2)}) collective-permute-start(bf16[256,1024]{1,0:T(8,128)(2,1)} %get-tuple-element.26), channel_id=1, source_target_pairs={{0,8},{4,12},{8,0},{12,4},{1,9},{5,13},{9,1},{13,5},{2,10},{6,14},... | collective-permute-start | bytes 1572872 | tf_op jit(solution)/shard_map/ppermute | solution.py:159
  103.0 39.2 %collective-permute-start.2 = (bf16[256,1024]{1,0:T(8,128)(2,1)}, bf16[256,1024]{1,0:T(8,128)(2,1)S(1)}, u32[]{:S(2)}, u32[]{:S(2)}) collective-permute-start(bf16[256,1024]{1,0:T(8,128)(2,1)} %get-tuple-element.25), channel_id=1, source_target_pairs={{0,3},{1,2},{2,1},{3,0},{4,7},{5,6},{6,5},{7,4},{8,11},{9,10},{10,... | collective-permute-start | bytes 1572872 | tf_op jit(solution)/shard_map/ppermute | solution.py:159
  104.3 48.9 %collective-permute-start.1 = (bf16[256,1024]{1,0:T(8,128)(2,1)}, bf16[256,1024]{1,0:T(8,128)(2,1)S(1)}, u32[]{:S(2)}, u32[]{:S(2)}) collective-permute-start(bf16[256,1024]{1,0:T(8,128)(2,1)} %get-tuple-element.24), channel_id=1, source_target_pairs={{0,12},{4,8},{8,4},{12,0},{1,13},{5,9},{9,5},{13,1},{2,14},{6,10},... | collective-permute-start | bytes 1572872 | tf_op jit(solution)/shard_map/ppermute | solution.py:159
  104.3 1.0 copy-start.1
  104.3 1.0 copy-start.2
  104.3 1.0 copy-start.3
  104.4 50.5 %collective-permute-start = (bf16[256,1024]{1,0:T(8,128)(2,1)}, bf16[256,1024]{1,0:T(8,128)(2,1)S(1)}, u32[]{:S(2)}, u32[]{:S(2)}) collective-permute-start(bf16[256,1024]{1,0:T(8,128)(2,1)} %get-tuple-element.23), channel_id=1, source_target_pairs={{0,1},{1,0},{2,3},{3,2},{4,5},{5,4},{6,7},{7,6},{8,9},{9,8},{10,11... | collective-permute-start | bytes 1572872 | tf_op jit(solution)/shard_map/ppermute | solution.py:159
  105.3 31.7 %copy-start.4 = (s32[1,16]{1,0:T(1,128)S(1)}, s32[1,16]{1,0:T(1,128)}, u32[]{:S(2)}) copy-start(s32[1,16]{1,0:T(1,128)} %mask.11) | copy-start | bytes 196
  137.0 1.7 %collective-permute-start.6 = (f32[1,256]{1,0:T(1,128)S(1)}, f32[1,256]{1,0:T(1,128)S(1)}, u32[]{:S(2)}, u32[]{:S(2)}) collective-permute-start(f32[1,256]{1,0:T(1,128)S(1)} %get-tuple-element.31), channel_id=1, source_target_pairs={{4,0},{0,4},{12,8},{8,12},{5,1},{1,5},{13,9},{9,13},{6,2},{2,6},{1... | collective-permute-start | bytes 3080 | tf_op jit(solution)/shard_map/ppermute | solution.py:170
  138.6 9.4 %collective-permute-start.7 = (f32[1,256]{1,0:T(1,128)S(1)}, f32[1,256]{1,0:T(1,128)S(1)}, u32[]{:S(2)}, u32[]{:S(2)}) collective-permute-start(f32[1,256]{1,0:T(1,128)S(1)} %get-tuple-element.33), channel_id=1, source_target_pairs={{2,0},{3,1},{0,2},{1,3},{6,4},{7,5},{4,6},{5,7},{10,8},{11,9},{8,1... | collective-permute-start | bytes 3080 | tf_op jit(solution)/shard_map/ppermute | solution.py:170
  140.3 12.9 %collective-permute-start.8 = (f32[1,256]{1,0:T(1,128)S(1)}, f32[1,256]{1,0:T(1,128)S(1)}, u32[]{:S(2)}, u32[]{:S(2)}) collective-permute-start(f32[1,256]{1,0:T(1,128)S(1)} %get-tuple-element.35), channel_id=1, source_target_pairs={{8,0},{12,4},{0,8},{4,12},{9,1},{13,5},{1,9},{5,13},{10,2},{14,6},... | collective-permute-start | bytes 3080 | tf_op jit(solution)/shard_map/ppermute | solution.py:170
  149.6 5.4 %collective-permute-start.9 = (f32[1,256]{1,0:T(1,128)S(1)}, f32[1,256]{1,0:T(1,128)S(1)}, u32[]{:S(2)}, u32[]{:S(2)}) collective-permute-start(f32[1,256]{1,0:T(1,128)S(1)} %get-tuple-element.37), channel_id=1, source_target_pairs={{3,0},{2,1},{1,2},{0,3},{7,4},{6,5},{5,6},{4,7},{11,8},{10,9},{9,1... | collective-permute-start | bytes 3080 | tf_op jit(solution)/shard_map/ppermute | solution.py:170
  156.7 0.6 copy-start.5
  157.3 3.6 %collective-permute-start.11 = (f32[1,256]{1,0:T(1,128)S(1)}, f32[1,256]{1,0:T(1,128)S(1)}, u32[]{:S(2)}, u32[]{:S(2)}) collective-permute-start(f32[1,256]{1,0:T(1,128)S(1)} %get-tuple-element.40), channel_id=1, source_target_pairs={{1,0},{0,1},{3,2},{2,3},{5,4},{4,5},{7,6},{6,7},{9,8},{8,9},{11,10... | collective-permute-start | bytes 3080 | tf_op jit(solution)/shard_map/ppermute | solution.py:170
  157.3 3.6 %collective-permute-start.10 = (f32[1,256]{1,0:T(1,128)S(1)}, f32[1,256]{1,0:T(1,128)S(1)}, u32[]{:S(2)}, u32[]{:S(2)}) collective-permute-start(f32[1,256]{1,0:T(1,128)S(1)} %get-tuple-element.39), channel_id=1, source_target_pairs={{12,0},{8,4},{4,8},{0,12},{13,1},{9,5},{5,9},{1,13},{14,2},{10,6},... | collective-permute-start | bytes 3080 | tf_op jit(solution)/shard_map/ppermute | solution.py:170
  160.8 0.6 copy-start.6
  160.8 0.6 copy-start.7

commit v3 on v2

--- a/solution.py
+++ b/solution.py
@@ -37,28 +37,21 @@
     return pick_blk[0, target] if axis == "blk" else pick_sub[lax.axis_index("sub"), target]
 
 
-def pick_kernel(rounds, sizes, pick_blk, pick_sub, embeds, *rest):
-    outs, sems = rest[:-1], rest[-1]
-    copies = []
+def pick_kernel(rounds, sizes, pick_blk, pick_sub, embeds, *outs):
     for place, out in enumerate(outs):
         pick = take_pick(rounds, sizes, pick_blk, pick_sub, place)
-        rows = pl.ds(pl.multiple_of(pick * BLOCK, BLOCK), BLOCK)
-        copies.append(pltpu.make_async_copy(embeds.at[rows], out, sems.at[place]))
-    for copy in copies:
-        copy.start()
-    for copy in copies:
-        copy.wait()
+        out[...] = embeds[pl.ds(pl.multiple_of(pick * BLOCK, BLOCK), BLOCK)]
 
 
 def pick_blocks(rounds, sizes, pick_blk, pick_sub, embeds):
-    smem, any_space = pl.BlockSpec(memory_space=pltpu.SMEM), pl.BlockSpec(memory_space=pl.ANY)
+    smem, vmem = pl.BlockSpec(memory_space=pltpu.SMEM), pl.BlockSpec(memory_space=pltpu.VMEM)
     shape = jax.ShapeDtypeStruct((BLOCK, embeds.shape[1]), embeds.dtype)
     return pl.pallas_call(
         functools.partial(pick_kernel, rounds, sizes),
         out_shape=[shape] * len(rounds),
-        in_specs=[smem, smem, any_space],
-        out_specs=[any_space] * len(rounds),
-        scratch_shapes=[pltpu.SemaphoreType.DMA((len(rounds),))],
+        in_specs=[smem, smem, vmem],
+        out_specs=[vmem] * len(rounds),
+        compiler_params=pltpu.CompilerParams(vmem_limit_bytes=32 * 2**20),
     )(pick_blk, pick_sub, embeds)
 
 
@@ -120,20 +113,24 @@
 
 
 def credit_kernel(rounds, sizes, places, pick_blk, pick_sub, totals, *rest):
-    returned, out = rest[:-1], rest[-1]
-    out[...] = totals[...]
+    returned, out, sum_all = rest[:-2], rest[-2], rest[-1]
+    sum_all[...] = totals[...]
     for place, sums in zip(places, returned):
-        add_returned(out, take_pick(rounds, sizes, pick_blk, pick_sub, place), sums)
-    out[...] = out[...] / BLOCK
+        add_returned(sum_all, take_pick(rounds, sizes, pick_blk, pick_sub, place), sums)
+    for i in range(totals.shape[0]):
+        for lane in range(0, BLOCK, 128):
+            row = (i * BLOCK + lane) // 128
+            out[row : row + 1] = sum_all[i : i + 1, lane : lane + 128] / BLOCK
 
 
 def credit(rounds, sizes, places, pick_blk, pick_sub, totals, returned):
     smem, vmem = pl.BlockSpec(memory_space=pltpu.SMEM), pl.BlockSpec(memory_space=pltpu.VMEM)
     return pl.pallas_call(
         functools.partial(credit_kernel, rounds, sizes, places),
-        out_shape=jax.ShapeDtypeStruct(totals.shape, jnp.float32),
+        out_shape=jax.ShapeDtypeStruct((totals.size // 128, 128), jnp.float32),
         in_specs=[smem, smem, vmem] + [vmem] * len(returned),
         out_specs=vmem,
+        scratch_shapes=[pltpu.VMEM(totals.shape, jnp.float32)],
     )(pick_blk, pick_sub, totals, *returned)
 
 

time: 164 us -> 69.3 us (0.42)
  Pallas kernels: 109 us -> 12.6 us
  local copies, waits for them, and re-layouts: 2.48 us -> 4.12 us
    pallas_call x1, Pallas kernels: 97.3 us -> 0.78 us  [pick_blocks(): pl.pallas_call(functools.partial(pick_kernel, rounds, sizes), out_shape=[...]
    unnamed x17 -> x16, local copies, waits for them, and re-layouts: 2.48 us -> 4.12 us
  transfers between devices with their start and end apart: 12 -> 12, of which waited for: 4 -> 4; matrix products, arithmetic and copies ran while one was open for 0% -> 0% of each run, Pallas kernels for 5% -> 13%
where the time goes in v3:
time: 69.3 us; the launch traced here: 69.1 us
  waiting for transfers between devices  39 us (56%)
  starting transfers between devices  13.3 us (19%)
  Pallas kernels  12.6 us (18%)
  local copies, waits for them, and re-layouts  4.12 us (6%)
    ppermute x6, waiting for transfers between devices, body(): lax.ppermute(sent, axis, pairs(step, sizes[axis]))  29.9 us
    pallas_call x6, Pallas kernels, slot(): pl.pallas_call(functools.partial(slot_kernel, rounds, sizes, place, back_...  9.68 us
    ppermute x6, waiting for transfers between devices, body(): lax.ppermute(back, axis, [(b, a) for a, b in pairs(step, sizes[axis])])  9.19 us
    ppermute x6, starting transfers between devices, body(): lax.ppermute(sent, axis, pairs(step, sizes[axis]))  7.33 us
    ppermute x6, starting transfers between devices, body(): lax.ppermute(back, axis, [(b, a) for a, b in pairs(step, sizes[axis])])  5.93 us
    unnamed x16, local copies, waits for them, and re-layouts  4.12 us
    pallas_call x1, Pallas kernels, credit(): pl.pallas_call(functools.partial(credit_kernel, rounds, sizes, places), o...  1.46 us
  transfers between devices with their start and end apart: 12, of which 4 were waited for; matrix products, arithmetic and copies ran while one was open for 0% of the time, Pallas kernels for 13%

profile of v3, /device:TPU:0, one launch (start us, length us, event | category | flops | bytes accessed | tf_op | source)
XLA Modules:
  0.0 69.1 jit_solution(15600662645679838038)
XLA Ops:
  0.0 0.0 copy-start
  0.0 1.6 %copy-done = bf16[1024,1024]{1,0:T(8,128)(2,1)S(1)} copy-done((bf16[1024,1024]{1,0:T(8,128)(2,1)S(1)}, bf16[1024,1024]{1,0:T(8,128)(2,1)}, u32[]{:S(2)}) %copy-start) | copy-done | bytes 2097176
  1.6 0.0 copy-start.1
  1.6 0.7 copy-done.1
  2.3 0.0 copy-start.2
  2.3 0.7 copy-done.2
  2.9 0.8 %shard_map.55 = (bf16[256,1024]{1,0:T(8,128)(2,1)S(1)}, bf16[256,1024]{1,0:T(8,128)(2,1)S(1)}, bf16[256,1024]{1,0:T(8,128)(2,1)S(1)}, bf16[256,1024]{1,0:T(8,128...) custom-call(s32[1,4]{1,0:T(1,128)S(1)} %copy-done.2, s32[4,4]{1,0:T(4,128)S(1)} %copy-done.1, ...), custom_call_target="tpu_custom_call" | custom-call | tf_op jit(solution)/shard_map/pallas_call | solution.py:49
  3.7 0.5 collective-permute-start.5
  4.2 3.7 %collective-permute-start.4 = (bf16[256,1024]{1,0:T(8,128)(2,1)S(1)}, bf16[256,1024]{1,0:T(8,128)(2,1)S(1)}, u32[]{:S(2)}, u32[]{:S(2)}) collective-permute-start(bf16[256,1024]{1,0:T(8,128)(2,1)S(1)} %get-tuple-element.27), channel_id=1, source_target_pairs={{0,2},{1,3},{2,0},{3,1},{4,6},{5,7},{6,4},{7,5},{8,10},{9,11},{10,... | collective-permute-start | bytes 1572872 | tf_op jit(solution)/shard_map/ppermute | solution.py:156
  7.9 1.5 %collective-permute-start.3 = (bf16[256,1024]{1,0:T(8,128)(2,1)S(1)}, bf16[256,1024]{1,0:T(8,128)(2,1)S(1)}, u32[]{:S(2)}, u32[]{:S(2)}) collective-permute-start(bf16[256,1024]{1,0:T(8,128)(2,1)S(1)} %get-tuple-element.26), channel_id=1, source_target_pairs={{0,8},{4,12},{8,0},{12,4},{1,9},{5,13},{9,1},{13,5},{2,10},{6,14},... | collective-permute-start | bytes 1572872 | tf_op jit(solution)/shard_map/ppermute | solution.py:156
  9.4 1.3 %collective-permute-start.2 = (bf16[256,1024]{1,0:T(8,128)(2,1)S(1)}, bf16[256,1024]{1,0:T(8,128)(2,1)S(1)}, u32[]{:S(2)}, u32[]{:S(2)}) collective-permute-start(bf16[256,1024]{1,0:T(8,128)(2,1)S(1)} %get-tuple-element.25), channel_id=1, source_target_pairs={{0,3},{1,2},{2,1},{3,0},{4,7},{5,6},{6,5},{7,4},{8,11},{9,10},{10,... | collective-permute-start | bytes 1572872 | tf_op jit(solution)/shard_map/ppermute | solution.py:156
  10.7 0.0 collective-permute-start.1
  10.7 0.0 collective-permute-done.5.arrived
  10.8 0.0 copy-start.3
  10.8 0.3 collective-permute-start
  11.1 0.6 shard_map.56.units
  11.7 0.0 copy-start.4
  11.7 0.0 copy-done.3
  11.7 1.6 %shard_map.57 = (f32[4,256]{1,0:T(4,128)S(1)}, f32[1,256]{1,0:T(1,128)S(1)}) custom-call(s32[1,16]{1,0:T(1,128)S(1)} %copy-done.3, s32[1,4]{1,0:T(1,128)S(1)} %copy-done.2, s32[4,4]{1,0:T(4,128)S(1)} %copy-done.1, bf16[256,1024]{1,0:T(8,128)(2,1)S(1)} %collective-permute-done.5.arrived, bf16[1024,1024]{1,0:T(8,128)(2,1)S(1)} %shard_map.56.units, ...), custom_call_target="tpu_custom_call" | custom-call | tf_op jit(solution)/shard_map/pallas_call | solution.py:103
  13.4 29.8 %collective-permute-done.4.arrived = bf16[256,1024]{1,0:T(8,128)(2,1)S(1)} collective-permute-done((bf16[256,1024]{1,0:T(8,128)(2,1)S(1)}, bf16[256,1024]{1,0:T(8,128)(2,1)S(1)}, u32[]{:S(2)}, u32[]{:S(2)}) %collective-permute-start.4) | collective-permute-done | bytes 524320 | tf_op jit(solution)/shard_map/ppermute | solution.py:156
  43.2 0.0 collective-permute-start.6
  43.2 0.0 copy-done.4
  43.2 1.6 %shard_map.58 = (f32[4,256]{1,0:T(4,128)S(1)}, f32[1,256]{1,0:T(1,128)S(1)}) custom-call(s32[1,16]{1,0:T(1,128)S(1)} %copy-done.4, s32[1,4]{1,0:T(1,128)S(1)} %copy-done.2, s32[4,4]{1,0:T(4,128)S(1)} %copy-done.1, bf16[256,1024]{1,0:T(8,128)(2,1)S(1)} %collective-permute-done.4.arrived, bf16[1024,1024]{1,0:T(8,128)(2,1)S(1)} %shard_map.56.units, ...), custom_call_target="tpu_custom_call" | custom-call | tf_op jit(solution)/shard_map/pallas_call | solution.py:103
  44.8 0.0 collective-permute-done.3.arrived
  44.8 0.1 collective-permute-start.7
  44.9 0.0 collective-permute-done.6.rest_0_
  44.9 1.6 %shard_map.59 = (f32[4,256]{1,0:T(4,128)S(1)}, f32[1,256]{1,0:T(1,128)S(1)}) custom-call(s32[1,16]{1,0:T(1,128)S(1)} %copy-done.3, s32[1,4]{1,0:T(1,128)S(1)} %copy-done.2, s32[4,4]{1,0:T(4,128)S(1)} %copy-done.1, bf16[256,1024]{1,0:T(8,128)(2,1)S(1)} %collective-permute-done.3.arrived, bf16[1024,1024]{1,0:T(8,128)(2,1)S(1)} %shard_map.56.units, ...), custom_call_target="tpu_custom_call" | custom-call | tf_op jit(solution)/shard_map/pallas_call | solution.py:103
  46.5 1.8 %collective-permute-start.8 = (f32[1,256]{1,0:T(1,128)S(1)}, f32[1,256]{1,0:T(1,128)S(1)}, u32[]{:S(2)}, u32[]{:S(2)}) collective-permute-start(f32[1,256]{1,0:T(1,128)S(1)} %get-tuple-element.35), channel_id=1, source_target_pairs={{8,0},{12,4},{0,8},{4,12},{9,1},{13,5},{1,9},{5,13},{10,2},{14,6},... | collective-permute-start | bytes 3080 | tf_op jit(solution)/shard_map/ppermute | solution.py:167
  48.4 0.0 collective-permute-done.2.arrived
  48.4 5.9 %collective-permute-done.7.rest_0_ = f32[1,256]{1,0:T(1,128)S(1)} collective-permute-done((f32[1,256]{1,0:T(1,128)S(1)}, f32[1,256]{1,0:T(1,128)S(1)}, u32[]{:S(2)}, u32[]{:S(2)}) %collective-permute-start.7) | collective-permute-done | bytes 1056 | tf_op jit(solution)/shard_map/ppermute | solution.py:167
  54.2 1.6 %shard_map.60 = (f32[4,256]{1,0:T(4,128)S(1)}, f32[1,256]{1,0:T(1,128)S(1)}) custom-call(s32[1,16]{1,0:T(1,128)S(1)} %copy-done.4, s32[1,4]{1,0:T(1,128)S(1)} %copy-done.2, s32[4,4]{1,0:T(4,128)S(1)} %copy-done.1, bf16[256,1024]{1,0:T(8,128)(2,1)S(1)} %collective-permute-done.2.arrived, bf16[1024,1024]{1,0:T(8,128)(2,1)S(1)} %shard_map.56.units, ...), custom_call_target="tpu_custom_call" | custom-call | tf_op jit(solution)/shard_map/pallas_call | solution.py:103
  55.8 3.6 %collective-permute-start.9 = (f32[1,256]{1,0:T(1,128)S(1)}, f32[1,256]{1,0:T(1,128)S(1)}, u32[]{:S(2)}, u32[]{:S(2)}) collective-permute-start(f32[1,256]{1,0:T(1,128)S(1)} %get-tuple-element.37), channel_id=1, source_target_pairs={{3,0},{2,1},{1,2},{0,3},{7,4},{6,5},{5,6},{4,7},{11,8},{10,9},{9,1... | collective-permute-start | bytes 3080 | tf_op jit(solution)/shard_map/ppermute | solution.py:167
  59.5 0.0 collective-permute-done.1.arrived
  59.5 0.0 collective-permute-done.8.rest_0_
  59.5 1.6 %shard_map.61 = (f32[4,256]{1,0:T(4,128)S(1)}, f32[1,256]{1,0:T(1,128)S(1)}) custom-call(s32[1,16]{1,0:T(1,128)S(1)} %copy-done.3, s32[1,4]{1,0:T(1,128)S(1)} %copy-done.2, s32[4,4]{1,0:T(4,128)S(1)} %copy-done.1, bf16[256,1024]{1,0:T(8,128)(2,1)S(1)} %collective-permute-done.1.arrived, bf16[1024,1024]{1,0:T(8,128)(2,1)S(1)} %shard_map.56.units, ...), custom_call_target="tpu_custom_call" | custom-call | tf_op jit(solution)/shard_map/pallas_call | solution.py:103
  61.1 0.0 collective-permute-done.arrived
  61.1 0.2 collective-permute-done.9.rest_0_
  61.3 1.6 %shard_map.62 = (f32[4,256]{1,0:T(4,128)S(1)}, f32[1,256]{1,0:T(1,128)S(1)}) custom-call(s32[1,16]{1,0:T(1,128)S(1)} %copy-done.4, s32[1,4]{1,0:T(1,128)S(1)} %copy-done.2, s32[4,4]{1,0:T(4,128)S(1)} %copy-done.1, bf16[256,1024]{1,0:T(8,128)(2,1)S(1)} %collective-permute-done.arrived, bf16[1024,1024]{1,0:T(8,128)(2,1)S(1)} %shard_map.56.units, ...), custom_call_target="tpu_custom_call" | custom-call | tf_op jit(solution)/shard_map/pallas_call | solution.py:103
  62.9 0.0 copy-start.5
  62.9 0.6 copy-done.5
  63.5 0.0 collective-permute-start.11
  63.5 0.4 collective-permute-start.10
  63.9 3.2 %collective-permute-done.11.rest_1_ = f32[1,256]{1,0:T(1,128)S(1)} collective-permute-done((f32[1,256]{1,0:T(1,128)S(1)}, f32[1,256]{1,0:T(1,128)S(1)}, u32[]{:S(2)}, u32[]{:S(2)}) %collective-permute-start.11) | collective-permute-done | bytes 1056 | tf_op jit(solution)/shard_map/ppermute | solution.py:167
  67.0 0.0 copy-start.6
  67.0 0.0 collective-permute-done.10.rest_0_
  67.1 0.6 copy-done.6
  67.6 0.0 copy-done.7
  67.6 1.5 %shard_map.63 = f32[8,128]{1,0:T(8,128)} custom-call(s32[1,4]{1,0:T(1,128)} %pick_blk.15, s32[4,4]{1,0:T(4,128)} %pick_sub.15, f32[4,256]{1,0:T(4,128)} %copy-done.5, f32[1,256]{1,0:T(1,128)} %copy-done.7, f32[1,256]{1,0:T(1,128)} %copy-done.6), custom_call_target="tpu_custom_call" | custom-call | tf_op jit(solution)/shard_map/pallas_call | solution.py:128
  (2 shorter events, 0.0 us)
Async XLA Ops:
  0.0 1.6 %copy-start = (bf16[1024,1024]{1,0:T(8,128)(2,1)S(1)}, bf16[1024,1024]{1,0:T(8,128)(2,1)}, u32[]{:S(2)}) copy-start(bf16[1024,1024]{1,0:T(8,128)(2,1)} %embeds.3) | copy-start | bytes 6291460
  1.6 0.7 copy-start.1
  2.3 0.7 copy-start.2
  3.7 7.0 %collective-permute-start.5 = (bf16[256,1024]{1,0:T(8,128)(2,1)S(1)}, bf16[256,1024]{1,0:T(8,128)(2,1)S(1)}, u32[]{:S(2)}, u32[]{:S(2)}) collective-permute-start(bf16[256,1024]{1,0:T(8,128)(2,1)S(1)} %get-tuple-element.28), channel_id=1, source_target_pairs={{0,4},{4,0},{8,12},{12,8},{1,5},{5,1},{9,13},{13,9},{2,6},{6,2},{1... | collective-permute-start | bytes 1572872 | tf_op jit(solution)/shard_map/ppermute | solution.py:156
  4.2 39.0 %collective-permute-start.4 = (bf16[256,1024]{1,0:T(8,128)(2,1)S(1)}, bf16[256,1024]{1,0:T(8,128)(2,1)S(1)}, u32[]{:S(2)}, u32[]{:S(2)}) collective-permute-start(bf16[256,1024]{1,0:T(8,128)(2,1)S(1)} %get-tuple-element.27), channel_id=1, source_target_pairs={{0,2},{1,3},{2,0},{3,1},{4,6},{5,7},{6,4},{7,5},{8,10},{9,11},{10,... | collective-permute-start | bytes 1572872 | tf_op jit(solution)/shard_map/ppermute | solution.py:156
  7.9 36.9 %collective-permute-start.3 = (bf16[256,1024]{1,0:T(8,128)(2,1)S(1)}, bf16[256,1024]{1,0:T(8,128)(2,1)S(1)}, u32[]{:S(2)}, u32[]{:S(2)}) collective-permute-start(bf16[256,1024]{1,0:T(8,128)(2,1)S(1)} %get-tuple-element.26), channel_id=1, source_target_pairs={{0,8},{4,12},{8,0},{12,4},{1,9},{5,13},{9,1},{13,5},{2,10},{6,14},... | collective-permute-start | bytes 1572872 | tf_op jit(solution)/shard_map/ppermute | solution.py:156
  9.4 39.0 %collective-permute-start.2 = (bf16[256,1024]{1,0:T(8,128)(2,1)S(1)}, bf16[256,1024]{1,0:T(8,128)(2,1)S(1)}, u32[]{:S(2)}, u32[]{:S(2)}) collective-permute-start(bf16[256,1024]{1,0:T(8,128)(2,1)S(1)} %get-tuple-element.25), channel_id=1, source_target_pairs={{0,3},{1,2},{2,1},{3,0},{4,7},{5,6},{6,5},{7,4},{8,11},{9,10},{10,... | collective-permute-start | bytes 1572872 | tf_op jit(solution)/shard_map/ppermute | solution.py:156
  10.7 48.7 %collective-permute-start.1 = (bf16[256,1024]{1,0:T(8,128)(2,1)S(1)}, bf16[256,1024]{1,0:T(8,128)(2,1)S(1)}, u32[]{:S(2)}, u32[]{:S(2)}) collective-permute-start(bf16[256,1024]{1,0:T(8,128)(2,1)S(1)} %get-tuple-element.24), channel_id=1, source_target_pairs={{0,12},{4,8},{8,4},{12,0},{1,13},{5,9},{9,5},{13,1},{2,14},{6,10},... | collective-permute-start | bytes 1572872 | tf_op jit(solution)/shard_map/ppermute | solution.py:156
  10.8 1.0 %copy-start.3 = (s32[1,16]{1,0:T(1,128)S(1)}, s32[1,16]{1,0:T(1,128)}, u32[]{:S(2)}) copy-start(s32[1,16]{1,0:T(1,128)} %mask.10) | copy-start | bytes 196
  10.8 50.3 %collective-permute-start = (bf16[256,1024]{1,0:T(8,128)(2,1)S(1)}, bf16[256,1024]{1,0:T(8,128)(2,1)S(1)}, u32[]{:S(2)}, u32[]{:S(2)}) collective-permute-start(bf16[256,1024]{1,0:T(8,128)(2,1)S(1)} %get-tuple-element.23), channel_id=1, source_target_pairs={{0,1},{1,0},{2,3},{3,2},{4,5},{5,4},{6,7},{7,6},{8,9},{9,8},{10,11... | collective-permute-start | bytes 1572872 | tf_op jit(solution)/shard_map/ppermute | solution.py:156
  11.7 31.5 %copy-start.4 = (s32[1,16]{1,0:T(1,128)S(1)}, s32[1,16]{1,0:T(1,128)}, u32[]{:S(2)}) copy-start(s32[1,16]{1,0:T(1,128)} %mask.11) | copy-start | bytes 196
  43.2 1.7 %collective-permute-start.6 = (f32[1,256]{1,0:T(1,128)S(1)}, f32[1,256]{1,0:T(1,128)S(1)}, u32[]{:S(2)}, u32[]{:S(2)}) collective-permute-start(f32[1,256]{1,0:T(1,128)S(1)} %get-tuple-element.31), channel_id=1, source_target_pairs={{4,0},{0,4},{12,8},{8,12},{5,1},{1,5},{13,9},{9,13},{6,2},{2,6},{1... | collective-permute-start | bytes 3080 | tf_op jit(solution)/shard_map/ppermute | solution.py:167
  44.8 9.4 %collective-permute-start.7 = (f32[1,256]{1,0:T(1,128)S(1)}, f32[1,256]{1,0:T(1,128)S(1)}, u32[]{:S(2)}, u32[]{:S(2)}) collective-permute-start(f32[1,256]{1,0:T(1,128)S(1)} %get-tuple-element.33), channel_id=1, source_target_pairs={{2,0},{3,1},{0,2},{1,3},{6,4},{7,5},{4,6},{5,7},{10,8},{11,9},{8,1... | collective-permute-start | bytes 3080 | tf_op jit(solution)/shard_map/ppermute | solution.py:167
  46.5 12.9 %collective-permute-start.8 = (f32[1,256]{1,0:T(1,128)S(1)}, f32[1,256]{1,0:T(1,128)S(1)}, u32[]{:S(2)}, u32[]{:S(2)}) collective-permute-start(f32[1,256]{1,0:T(1,128)S(1)} %get-tuple-element.35), channel_id=1, source_target_pairs={{8,0},{12,4},{0,8},{4,12},{9,1},{13,5},{1,9},{5,13},{10,2},{14,6},... | collective-permute-start | bytes 3080 | tf_op jit(solution)/shard_map/ppermute | solution.py:167
  55.8 5.4 %collective-permute-start.9 = (f32[1,256]{1,0:T(1,128)S(1)}, f32[1,256]{1,0:T(1,128)S(1)}, u32[]{:S(2)}, u32[]{:S(2)}) collective-permute-start(f32[1,256]{1,0:T(1,128)S(1)} %get-tuple-element.37), channel_id=1, source_target_pairs={{3,0},{2,1},{1,2},{0,3},{7,4},{6,5},{5,6},{4,7},{11,8},{10,9},{9,1... | collective-permute-start | bytes 3080 | tf_op jit(solution)/shard_map/ppermute | solution.py:167
  62.9 0.6 copy-start.5
  63.5 3.6 %collective-permute-start.11 = (f32[1,256]{1,0:T(1,128)S(1)}, f32[1,256]{1,0:T(1,128)S(1)}, u32[]{:S(2)}, u32[]{:S(2)}) collective-permute-start(f32[1,256]{1,0:T(1,128)S(1)} %get-tuple-element.40), channel_id=1, source_target_pairs={{1,0},{0,1},{3,2},{2,3},{5,4},{4,5},{7,6},{6,7},{9,8},{8,9},{11,10... | collective-permute-start | bytes 3080 | tf_op jit(solution)/shard_map/ppermute | solution.py:167
  63.5 3.6 %collective-permute-start.10 = (f32[1,256]{1,0:T(1,128)S(1)}, f32[1,256]{1,0:T(1,128)S(1)}, u32[]{:S(2)}, u32[]{:S(2)}) collective-permute-start(f32[1,256]{1,0:T(1,128)S(1)} %get-tuple-element.39), channel_id=1, source_target_pairs={{12,0},{8,4},{4,8},{0,12},{13,1},{9,5},{5,9},{1,13},{14,2},{10,6},... | collective-permute-start | bytes 3080 | tf_op jit(solution)/shard_map/ppermute | solution.py:167
  67.0 0.6 copy-start.6
  67.0 0.6 copy-start.7

commit v4 on v1

v4 whole, which is shorter than its diff:
```python
import functools
import math

import jax
import jax.numpy as jnp
from jax import lax
from jax.experimental import pallas as pl
from jax.experimental.pallas import tpu as pltpu
from jax.sharding import PartitionSpec as P

BLOCK = 256
LANES = 128
ROWS = BLOCK // LANES

cutoff = 0.05
sharpness = 100.0

SMEM = pl.BlockSpec(memory_space=pltpu.SMEM)
VMEM = pl.BlockSpec(memory_space=pltpu.VMEM)
HBM = pl.BlockSpec(memory_space=pltpu.HBM)
PARAMS = pltpu.CompilerParams(vmem_limit_bytes=32 * 2**20)


def pairs(step, size):
    return [(i, i ^ step) for i in range(size)]


def rounded_units(rows):
    wide = rows.astype(jnp.float32)
    scale = lax.rsqrt(jnp.sum(wide * wide, axis=1, keepdims=True) + 1e-06)
    return (wide * scale).astype(jnp.bfloat16)


def soft_weights(cosines):
    rate = sharpness * math.log2(math.e)
    below = 1.0 + jnp.exp2(jnp.minimum(cutoff * rate - cosines * rate, 125.0))
    guess = pl.reciprocal(below, approx=True)
    return guess * (2.0 - below * guess)


def take_pick(axis, step, pick_blk, pick_sub):
    target = lax.axis_index(axis) ^ step
    return pick_blk[0, target] if axis == "blk" else pick_sub[lax.axis_index("sub"), target]


def pick_kernel(pieces, pick_blk, pick_sub, embeds, *rest):
    outs, (blk_scalars, sub_scalars, scalar_sems, block_sems) = rest[: len(pieces)], rest[-4:]
    scalars = [
        pltpu.make_async_copy(pick_blk, blk_scalars, scalar_sems.at[0]),
        pltpu.make_async_copy(pick_sub, sub_scalars, scalar_sems.at[1]),
    ]
    for copy in scalars:
        copy.start()
    for copy in scalars:
        copy.wait()
    copies = []
    for place, (out, (axis, step, first, rows)) in enumerate(zip(outs, pieces)):
        pick = take_pick(axis, step, blk_scalars, sub_scalars)
        start = pl.multiple_of(pick * BLOCK + first, math.gcd(BLOCK, first))
        copies.append(pltpu.make_async_copy(embeds.at[pl.ds(start, rows)], out, block_sems.at[place]))
    for copy in copies:
        copy.start()
    for copy in copies:
        copy.wait()


def pick_rows(pieces, pick_blk, pick_sub, embeds):
    return pl.pallas_call(
        functools.partial(pick_kernel, pieces),
        out_shape=[jax.ShapeDtypeStruct((rows, embeds.shape[1]), embeds.dtype) for _, _, _, rows in pieces],
        in_specs=[HBM] * 3,
        out_specs=[VMEM] * len(pieces),
        scratch_shapes=[
            pltpu.SMEM(pick_blk.shape, jnp.int32),
            pltpu.SMEM(pick_sub.shape, jnp.int32),
            pltpu.SemaphoreType.DMA((2,)),
            pltpu.SemaphoreType.DMA((len(pieces),)),
        ],
        compiler_params=PARAMS,
    )(pick_blk, pick_sub, embeds)


def prepare_kernel(slots, pick_blk, pick_sub, mask_blk, mask_sub, embeds, units, live, mine):
    for start in range(0, embeds.shape[0], BLOCK):
        units[start : start + BLOCK] = rounded_units(embeds[start : start + BLOCK])
    count = live.shape[1]
    block_of = lax.broadcasted_iota(jnp.int32, mine.shape[1:], 0) // ROWS
    for place, (axis, step, _, _) in enumerate(slots):
        source = lax.axis_index(axis) ^ step
        mask = mask_blk if axis == "blk" else mask_sub
        for i in range(count):
            value = mask[0, source * count + i].astype(jnp.float32)
            live[place, i : i + 1] = jnp.full((1, LANES), value, jnp.float32)
        pick = take_pick(axis, step, pick_blk, pick_sub)
        mine[place] = (block_of == pick).astype(jnp.float32)


def prepare(slots, pick_blk, pick_sub, mask_blk, mask_sub, embeds):
    count = embeds.shape[0] // BLOCK
    return pl.pallas_call(
        functools.partial(prepare_kernel, slots),
        out_shape=[
            jax.ShapeDtypeStruct(embeds.shape, embeds.dtype),
            jax.ShapeDtypeStruct((len(slots), count, LANES), jnp.float32),
            jax.ShapeDtypeStruct((len(slots), count * ROWS, LANES), jnp.float32),
        ],
        in_specs=[SMEM] * 4 + [VMEM],
        out_specs=[VMEM] * 3,
        compiler_params=PARAMS,
    )(pick_blk, pick_sub, mask_blk, mask_sub, embeds)


def slot_kernel(place, first, rows, back_place, arrived, units, live, mine, totals, *rest):
    new_totals, back = rest[-2:]
    count = live.shape[1]
    before = totals[...]
    if back_place is not None:
        before = before + mine[back_place] * rest[0][...]
    new_totals[...] = before
    x = rounded_units(arrived[...])
    along_rows = jnp.zeros((rows, LANES), jnp.float32)
    for i in range(count):
        y = units[i * BLOCK : (i + 1) * BLOCK]
        cosines = lax.dot_general(x, y, (((1,), (1,)), ((), ())), preferred_element_type=jnp.float32)
        weights = soft_weights(cosines)
        alive = live[place, i : i + 1]
        for part in range(ROWS):
            piece = alive * weights[:, part * LANES : (part + 1) * LANES]
            along_rows = along_rows + piece
            row = i * ROWS + part
            new_totals[row : row + 1] = new_totals[row : row + 1] + jnp.sum(piece, axis=0, keepdims=True)
    empty = [jnp.zeros((gap, LANES), jnp.float32) for gap in (first, BLOCK - first - rows)]
    along_rows = jnp.concatenate([part for part in (empty[0], along_rows, empty[1]) if part.shape[0]], axis=0)
    for part in range(ROWS):
        sums = jnp.sum(along_rows[part * LANES : (part + 1) * LANES].T, axis=0, keepdims=True)
        for i in range(count):
            row = i * ROWS + part
            back[row : row + 1] = sums


def work(place, slot, arrived, units, live, mine, totals, back_place, returned):
    operands = [arrived, units, live, mine, totals] + ([] if back_place is None else [returned])
    return pl.pallas_call(
        functools.partial(slot_kernel, place, *slot[2:], back_place),
        out_shape=[jax.ShapeDtypeStruct(totals.shape, jnp.float32)] * 2,
        in_specs=[VMEM] * len(operands),
        out_specs=[VMEM] * 2,
        compiler_params=PARAMS,
    )(*operands)


BEHIND = 2
EARLY_ROWS = 128


def plan_slots(sizes):
    slots = [("blk", 1, 0, BLOCK), ("blk", 2, 0, BLOCK), ("sub", 2, 0, EARLY_ROWS)]
    slots += [("blk", k, 0, BLOCK) for k in range(3, sizes["blk"])]
    slots += [("sub", 1, 0, BLOCK), ("sub", 2, EARLY_ROWS, BLOCK - EARLY_ROWS)]
    return slots + [("sub", k, 0, BLOCK) for k in range(3, sizes["sub"])]


AT_ONCE = 3


def body(embeds, pick_blk, mask_blk, pick_sub, mask_sub):
    count = embeds.shape[0] // BLOCK
    sizes = {"sub": lax.axis_size("sub"), "blk": lax.axis_size("blk")}
    slots = plan_slots(sizes)

    def send(array, slot):
        return lax.ppermute(array, slot[0], pairs(slot[1], sizes[slot[0]]))

    arrived = []
    for group in (slots[:AT_ONCE], slots[AT_ONCE:]):
        for rows, slot in zip(pick_rows(group, pick_blk, pick_sub, embeds), group):
            arrived.append(send(rows, slot))

    units, live, mine = prepare(slots, pick_blk, pick_sub, mask_blk, mask_sub, embeds)
    totals = jnp.zeros((count * ROWS, LANES), jnp.float32)
    returned = []
    for place, slot in enumerate(slots):
        back_place = place - BEHIND if place >= BEHIND else None
        came_back = None if back_place is None else returned[back_place]
        totals, back = work(place, slot, arrived[place], units, live, mine, totals, back_place, came_back)
        returned.append(send(back, slot))
    for place in range(len(slots) - BEHIND, len(slots)):
        totals = totals + mine[place] * returned[place]
    return (totals * (1.0 / BLOCK)).reshape(-1)


def solution(mesh):
    return jax.shard_map(
        body,
        mesh=mesh,
        in_specs=(
            P(("groups", "blk", "sub"), None),
            P(("groups", "blk", "sub"), None),
            P(("groups", "blk", "sub"), None),
            P(("groups", "blk"), None),
            P(("groups", "blk", "sub"), None),
        ),
        out_specs=P(("groups", "blk", "sub")),
        check_vma=False,
    )
```

time: 80.7 us -> 69.5 us (0.86)
  waiting for transfers between devices: 17.4 us -> 36.2 us
  other arithmetic: 12.9 us -> 0.6 us
  matrix products: 11.7 us -> 0 us
  between operations: 11.3 us -> 0.11 us
  Pallas kernels: 0 us -> 10.9 us
  local copies, waits for them, and re-layouts: 7.4 us -> 2.94 us
    ppermute x12 -> x14, waiting for transfers between devices: 17.4 us -> 36.2 us  [send(): return lax.ppermute(array, slot[0], pairs(slot[1], sizes[slot[0]]))]
    dot_general x6 -> x0, matrix products: 11.7 us -> none  [sweep(): lax.dot_general(normalize(arrived), unit_rows, (((1,), (1,)), ((), ())),...]
    pallas_call x0 -> x10, Pallas kernels: none -> 10.9 us  [the longest x7 8.17 us: work(): pl.pallas_call(functools.partial(slot_kernel, place, *slot[2:], back_plac...]
    reduce_sum x7 -> x0, other arithmetic: 6.78 us -> none  [normalize(): scale = lax.rsqrt(jnp.sum(wide * wide, axis=1, keepdims=True) + 1e-06)]
    eq x6 -> x0, other arithmetic: 3.71 us -> none  [body(): mine = (jnp.arange(count, dtype=jnp.int32) == pick)[:, None]]
    squeeze x1 -> x0, local copies, waits for them, and re-layouts: 3.51 us -> none  [body(): outgoing = lax.dynamic_index_in_dim(blocks, pick, 0, keepdims=False)]
    dynamic_slice x2 -> x0, local copies, waits for them, and re-layouts: 2.85 us -> none  [body(): pick = lax.dynamic_index_in_dim(picks[axis], target, 0, keepdims=False)]
    unnamed x23 -> x10, local copies, waits for them, and re-layouts: 0.86 us -> 2.93 us
  transfers between devices with their start and end apart: 12 -> 14, of which waited for: 3 -> 6; matrix products, arithmetic and copies ran while one was open for 31% -> 0% of each run, Pallas kernels for 0% -> 15%
where the time goes in v4:
time: 69.5 us; the launch traced here: 69.3 us
  waiting for transfers between devices  36.2 us (52%)
  starting transfers between devices  18.5 us (27%)
  Pallas kernels  10.9 us (16%)
  local copies, waits for them, and re-layouts  2.94 us (4%)
    ppermute x14, waiting for transfers between devices, send(): return lax.ppermute(array, slot[0], pairs(slot[1], sizes[slot[0]]))  36.2 us
    ppermute x14, starting transfers between devices, send(): return lax.ppermute(array, slot[0], pairs(slot[1], sizes[slot[0]]))  18.5 us
    pallas_call x7, Pallas kernels, work(): pl.pallas_call(functools.partial(slot_kernel, place, *slot[2:], back_plac...  8.17 us
    unnamed x10, local copies, waits for them, and re-layouts  2.93 us
    pallas_call x2, Pallas kernels, pick_rows(): pl.pallas_call(functools.partial(pick_kernel, pieces), out_shape=[jax.Sha...  1.49 us
  transfers between devices with their start and end apart: 14, of which 6 were waited for; matrix products, arithmetic and copies ran while one was open for 0% of the time, Pallas kernels for 15%

profile of v4, /device:TPU:0, one launch (start us, length us, event | category | flops | bytes accessed | tf_op | source)
XLA Modules:
  0.0 69.3 jit_solution(7450450705739792076)
XLA Ops:
  0.0 0.0 copy-start
  0.0 1.6 %copy-done = bf16[1024,1024]{1,0:T(8,128)(2,1)S(1)} copy-done((bf16[1024,1024]{1,0:T(8,128)(2,1)S(1)}, bf16[1024,1024]{1,0:T(8,128)(2,1)}, u32[]{:S(2)}) %copy-start) | copy-done | bytes 2097176
  1.6 0.0 copy-start.1
  1.6 0.7 copy-done.1
  2.3 0.0 copy-start.2
  2.3 0.7 copy-done.2
  2.9 0.0 copy-start.4
  2.9 0.7 %shard_map.57 = (bf16[256,1024]{1,0:T(8,128)(2,1)S(1)}, bf16[256,1024]{1,0:T(8,128)(2,1)S(1)}, bf16[128,1024]{1,0:T(8,128)(2,1)S(1)}) custom-call(s32[1,4]{1,0:T(1,128)S(1)} %copy-done.2, s32[4,4]{1,0:T(4,128)S(1)} %copy-done.1, bf16[1024,1024]{1,0:T(8,128)(2,1)S(1)} %copy-done), custom_call_target="tpu_custom_call" | custom-call | tf_op jit(solution)/shard_map/pallas_call | solution.py:68
  3.7 0.5 collective-permute-start.6
  4.2 3.7 %collective-permute-start.4 = (bf16[128,1024]{1,0:T(8,128)(2,1)S(1)}, bf16[128,1024]{1,0:T(8,128)(2,1)S(1)}, u32[]{:S(2)}, u32[]{:S(2)}) collective-permute-start(bf16[128,1024]{1,0:T(8,128)(2,1)S(1)} %get-tuple-element.36), channel_id=1, source_target_pairs={{0,2},{1,3},{2,0},{3,1},{4,6},{5,7},{6,4},{7,5},{8,10},{9,11},{10,... | collective-permute-start | bytes 786440 | tf_op jit(solution)/shard_map/ppermute | solution.py:172
  7.8 1.5 %collective-permute-start.5 = (bf16[256,1024]{1,0:T(8,128)(2,1)S(1)}, bf16[256,1024]{1,0:T(8,128)(2,1)S(1)}, u32[]{:S(2)}, u32[]{:S(2)}) collective-permute-start(bf16[256,1024]{1,0:T(8,128)(2,1)S(1)} %get-tuple-element.37), channel_id=1, source_target_pairs={{0,8},{4,12},{8,0},{12,4},{1,9},{5,13},{9,1},{13,5},{2,10},{6,14},... | collective-permute-start | bytes 1572872 | tf_op jit(solution)/shard_map/ppermute | solution.py:172
  9.3 0.8 %shard_map.55 = (bf16[256,1024]{1,0:T(8,128)(2,1)S(1)}, bf16[256,1024]{1,0:T(8,128)(2,1)S(1)}, bf16[128,1024]{1,0:T(8,128)(2,1)S(1)}, bf16[256,1024]{1,0:T(8,128)(2,1)S(1)}) custom-call(s32[1,4]{1,0:T(1,128)S(1)} %copy-done.2, s32[4,4]{1,0:T(4,128)S(1)} %copy-done.1, bf16[1024,1024]{1,0:T(8,128)(2,1)S(1)} %copy-done), custom_call_target="tpu_custom_call" | custom-call | tf_op jit(solution)/shard_map/pallas_call | solution.py:68
  10.1 0.1 collective-permute-start.3
  10.2 1.6 %collective-permute-start.2 = (bf16[256,1024]{1,0:T(8,128)(2,1)S(1)}, bf16[256,1024]{1,0:T(8,128)(2,1)S(1)}, u32[]{:S(2)}, u32[]{:S(2)}) collective-permute-start(bf16[256,1024]{1,0:T(8,128)(2,1)S(1)} %get-tuple-element.34), channel_id=1, source_target_pairs={{0,1},{1,0},{2,3},{3,2},{4,5},{5,4},{6,7},{7,6},{8,9},{9,8},{10,11... | collective-permute-start | bytes 1572872 | tf_op jit(solution)/shard_map/ppermute | solution.py:172
  11.8 8.6 %collective-permute-done.4.arrived = bf16[128,1024]{1,0:T(8,128)(2,1)S(1)} collective-permute-done((bf16[128,1024]{1,0:T(8,128)(2,1)S(1)}, bf16[128,1024]{1,0:T(8,128)(2,1)S(1)}, u32[]{:S(2)}, u32[]{:S(2)}) %collective-permute-start.4) | collective-permute-done | bytes 262176 | tf_op jit(solution)/shard_map/ppermute | solution.py:172
  20.5 3.6 %collective-permute-start = (bf16[256,1024]{1,0:T(8,128)(2,1)S(1)}, bf16[256,1024]{1,0:T(8,128)(2,1)S(1)}, u32[]{:S(2)}, u32[]{:S(2)}) collective-permute-start(bf16[256,1024]{1,0:T(8,128)(2,1)S(1)} %get-tuple-element.29), channel_id=1, source_target_pairs={{0,3},{1,2},{2,1},{3,0},{4,7},{5,6},{6,5},{7,4},{8,11},{9,10},{10,... | collective-permute-start | bytes 1572872 | tf_op jit(solution)/shard_map/ppermute | solution.py:172
  24.0 0.0 collective-permute-done.6.arrived
  24.0 0.0 collective-permute-start.1
  24.0 0.0 copy-done.3
  24.0 0.0 copy-done.4
  24.0 1.2 %shard_map.56 = (bf16[1024,1024]{1,0:T(8,128)(2,1)S(1)}, f32[7,4,128]{2,1,0:T(4,128)S(1)}, f32[7,8,128]{2,1,0:T(8,128)S(1)}) custom-call(s32[1,4]{1,0:T(1,128)S(1)} %copy-done.2, s32[4,4]{1,0:T(4,128)S(1)} %copy-done.1, s32[1,16]{1,0:T(1,128)S(1)} %copy-done.3, s32[1,16]{1,0:T(1,128)S(1)} %copy-done.4, bf16[1024,1024]{1,0:T(8,128)(2,1)S(1)} %copy-done), custom_call_target="tpu_custom_call" | custom-call | tf_op jit(solution)/shard_map/pallas_call | solution.py:100
  25.3 1.2 %shard_map.58 = (f32[8,128]{1,0:T(8,128)S(1)}, f32[8,128]{1,0:T(8,128)S(1)}) custom-call(bf16[256,1024]{1,0:T(8,128)(2,1)S(1)} %collective-permute-done.6.arrived, bf16[1024,1024]{1,0:T(8,128)(2,1)S(1)} %get-tuple-element.30.units, f32[7,4,128]{2,1,0:T(4,128)S(1)} %get-tuple-element.31.live, f32[7,8,128]{2,1,0:T(8,128)S(1)} %get-tuple-element.32.mine, ...), custom_call_target="tpu_custom_call" | custom-call | tf_op jit(solution)/shard_map/pallas_call | solution.py:143
  26.5 0.0 collective-permute-done.5.arrived
  26.5 0.1 collective-permute-start.7
  26.6 1.2 %shard_map.59 = (f32[8,128]{1,0:T(8,128)S(1)}, f32[8,128]{1,0:T(8,128)S(1)}) custom-call(bf16[256,1024]{1,0:T(8,128)(2,1)S(1)} %collective-permute-done.5.arrived, bf16[1024,1024]{1,0:T(8,128)(2,1)S(1)} %get-tuple-element.30.units, f32[7,4,128]{2,1,0:T(4,128)S(1)} %get-tuple-element.31.live, f32[7,8,128]{2,1,0:T(8,128)S(1)} %get-tuple-element.32.mine, ...), custom_call_target="tpu_custom_call" | custom-call | tf_op jit(solution)/shard_map/pallas_call | solution.py:143
  27.8 0.0 collective-permute-done.7.rest_0_
  27.8 1.5 %collective-permute-start.8 = (f32[8,128]{1,0:T(8,128)S(1)}, f32[8,128]{1,0:T(8,128)S(1)}, u32[]{:S(2)}, u32[]{:S(2)}) collective-permute-start(f32[8,128]{1,0:T(8,128)S(1)} %get-tuple-element.43), channel_id=1, source_target_pairs={{0,8},{4,12},{8,0},{12,4},{1,9},{5,13},{9,1},{13,5},{2,10},{6,14},... | collective-permute-start | bytes 12296 | tf_op jit(solution)/shard_map/ppermute | solution.py:172
  29.4 1.1 %shard_map.60 = (f32[8,128]{1,0:T(8,128)S(1)}, f32[8,128]{1,0:T(8,128)S(1)}) custom-call(bf16[128,1024]{1,0:T(8,128)(2,1)S(1)} %collective-permute-done.4.arrived, bf16[1024,1024]{1,0:T(8,128)(2,1)S(1)} %get-tuple-element.30.units, f32[7,4,128]{2,1,0:T(4,128)S(1)} %get-tuple-element.31.live, f32[7,8,128]{2,1,0:T(8,128)S(1)} %get-tuple-element.32.mine, ...), custom_call_target="tpu_custom_call" | custom-call | tf_op jit(solution)/shard_map/pallas_call | solution.py:143
  30.4 1.9 %collective-permute-done.3.arrived = bf16[256,1024]{1,0:T(8,128)(2,1)S(1)} collective-permute-done((bf16[256,1024]{1,0:T(8,128)(2,1)S(1)}, bf16[256,1024]{1,0:T(8,128)(2,1)S(1)}, u32[]{:S(2)}, u32[]{:S(2)}) %collective-permute-start.3) | collective-permute-done | bytes 524320 | tf_op jit(solution)/shard_map/ppermute | solution.py:172
  32.3 1.1 %collective-permute-start.9 = (f32[8,128]{1,0:T(8,128)S(1)}, f32[8,128]{1,0:T(8,128)S(1)}, u32[]{:S(2)}, u32[]{:S(2)}) collective-permute-start(f32[8,128]{1,0:T(8,128)S(1)} %get-tuple-element.45), channel_id=1, source_target_pairs={{0,2},{1,3},{2,0},{3,1},{4,6},{5,7},{6,4},{7,5},{8,10},{9,11},{10,... | collective-permute-start | bytes 12296 | tf_op jit(solution)/shard_map/ppermute | solution.py:172
  33.4 0.0 collective-permute-done.8.rest_0_
  33.4 1.2 %shard_map.61 = (f32[8,128]{1,0:T(8,128)S(1)}, f32[8,128]{1,0:T(8,128)S(1)}) custom-call(bf16[256,1024]{1,0:T(8,128)(2,1)S(1)} %collective-permute-done.3.arrived, bf16[1024,1024]{1,0:T(8,128)(2,1)S(1)} %get-tuple-element.30.units, f32[7,4,128]{2,1,0:T(4,128)S(1)} %get-tuple-element.31.live, f32[7,8,128]{2,1,0:T(8,128)S(1)} %get-tuple-element.32.mine, ...), custom_call_target="tpu_custom_call" | custom-call | tf_op jit(solution)/shard_map/pallas_call | solution.py:143
  34.6 1.0 %collective-permute-start.10 = (f32[8,128]{1,0:T(8,128)S(1)}, f32[8,128]{1,0:T(8,128)S(1)}, u32[]{:S(2)}, u32[]{:S(2)}) collective-permute-start(f32[8,128]{1,0:T(8,128)S(1)} %get-tuple-element.47), channel_id=1, source_target_pairs={{0,12},{4,8},{8,4},{12,0},{1,13},{5,9},{9,5},{13,1},{2,14},{6,10},... | collective-permute-start | bytes 12296 | tf_op jit(solution)/shard_map/ppermute | solution.py:172
  35.6 4.7 %collective-permute-done.2.arrived = bf16[256,1024]{1,0:T(8,128)(2,1)S(1)} collective-permute-done((bf16[256,1024]{1,0:T(8,128)(2,1)S(1)}, bf16[256,1024]{1,0:T(8,128)(2,1)S(1)}, u32[]{:S(2)}, u32[]{:S(2)}) %collective-permute-start.2) | collective-permute-done | bytes 524320 | tf_op jit(solution)/shard_map/ppermute | solution.py:172
  40.3 16.8 %collective-permute-done.9.rest_0_ = f32[8,128]{1,0:T(8,128)S(1)} collective-permute-done((f32[8,128]{1,0:T(8,128)S(1)}, f32[8,128]{1,0:T(8,128)S(1)}, u32[]{:S(2)}, u32[]{:S(2)}) %collective-permute-start.9) | collective-permute-done | bytes 4128 | tf_op jit(solution)/shard_map/ppermute | solution.py:172
  57.1 1.2 %shard_map.62 = (f32[8,128]{1,0:T(8,128)S(1)}, f32[8,128]{1,0:T(8,128)S(1)}) custom-call(bf16[256,1024]{1,0:T(8,128)(2,1)S(1)} %collective-permute-done.2.arrived, bf16[1024,1024]{1,0:T(8,128)(2,1)S(1)} %get-tuple-element.30.units, f32[7,4,128]{2,1,0:T(4,128)S(1)} %get-tuple-element.31.live, f32[7,8,128]{2,1,0:T(8,128)S(1)} %get-tuple-element.32.mine, ...), custom_call_target="tpu_custom_call" | custom-call | tf_op jit(solution)/shard_map/pallas_call | solution.py:143
  58.3 0.1 collective-permute-start.11
  58.4 0.0 collective-permute-done.1.arrived
  58.4 0.0 collective-permute-done.10.rest_0_
  58.4 1.1 %shard_map.63 = (f32[8,128]{1,0:T(8,128)S(1)}, f32[8,128]{1,0:T(8,128)S(1)}) custom-call(bf16[128,1024]{1,0:T(8,128)(2,1)S(1)} %collective-permute-done.1.arrived, bf16[1024,1024]{1,0:T(8,128)(2,1)S(1)} %get-tuple-element.30.units, f32[7,4,128]{2,1,0:T(4,128)S(1)} %get-tuple-element.31.live, f32[7,8,128]{2,1,0:T(8,128)S(1)} %get-tuple-element.32.mine, ...), custom_call_target="tpu_custom_call" | custom-call | tf_op jit(solution)/shard_map/pallas_call | solution.py:143
  59.5 1.8 %collective-permute-start.12 = (f32[8,128]{1,0:T(8,128)S(1)}, f32[8,128]{1,0:T(8,128)S(1)}, u32[]{:S(2)}, u32[]{:S(2)}) collective-permute-start(f32[8,128]{1,0:T(8,128)S(1)} %get-tuple-element.51), channel_id=1, source_target_pairs={{0,2},{1,3},{2,0},{3,1},{4,6},{5,7},{6,4},{7,5},{8,10},{9,11},{10,... | collective-permute-start | bytes 12296 | tf_op jit(solution)/shard_map/ppermute | solution.py:172
  61.3 0.0 collective-permute-done.arrived
  61.3 0.7 %collective-permute-done.11.rest_0_ = f32[8,128]{1,0:T(8,128)S(1)} collective-permute-done((f32[8,128]{1,0:T(8,128)S(1)}, f32[8,128]{1,0:T(8,128)S(1)}, u32[]{:S(2)}, u32[]{:S(2)}) %collective-permute-start.11) | collective-permute-done | bytes 4128 | tf_op jit(solution)/shard_map/ppermute | solution.py:172
  62.0 1.2 %shard_map.64 = (f32[8,128]{1,0:T(8,128)S(1)}, f32[8,128]{1,0:T(8,128)S(1)}) custom-call(bf16[256,1024]{1,0:T(8,128)(2,1)S(1)} %collective-permute-done.arrived, bf16[1024,1024]{1,0:T(8,128)(2,1)S(1)} %get-tuple-element.30.units, f32[7,4,128]{2,1,0:T(4,128)S(1)} %get-tuple-element.31.live, f32[7,8,128]{2,1,0:T(8,128)S(1)} %get-tuple-element.32.mine, ...), custom_call_target="tpu_custom_call" | custom-call | tf_op jit(solution)/shard_map/pallas_call | solution.py:143
  63.2 2.0 %collective-permute-start.13 = (f32[8,128]{1,0:T(8,128)S(1)}, f32[8,128]{1,0:T(8,128)S(1)}, u32[]{:S(2)}, u32[]{:S(2)}) collective-permute-start(f32[8,128]{1,0:T(8,128)S(1)} %get-tuple-element.52), channel_id=1, source_target_pairs={{0,3},{1,2},{2,1},{3,0},{4,7},{5,6},{6,5},{7,4},{8,11},{9,10},{10,... | collective-permute-start | bytes 12296 | tf_op jit(solution)/shard_map/ppermute | solution.py:172
  65.2 0.0 collective-permute-done.12
  65.2 3.5 %collective-permute-done.13 = f32[8,128]{1,0:T(8,128)S(1)} collective-permute-done((f32[8,128]{1,0:T(8,128)S(1)}, f32[8,128]{1,0:T(8,128)S(1)}, u32[]{:S(2)}, u32[]{:S(2)}) %collective-permute-start.13) | collective-permute-done | bytes 4128 | tf_op jit(solution)/shard_map/ppermute | solution.py:172
  68.7 0.6 fusion.2
  (2 shorter events, 0.0 us)
Async XLA Ops:
  0.0 1.6 %copy-start = (bf16[1024,1024]{1,0:T(8,128)(2,1)S(1)}, bf16[1024,1024]{1,0:T(8,128)(2,1)}, u32[]{:S(2)}) copy-start(bf16[1024,1024]{1,0:T(8,128)(2,1)} %embeds.5) | copy-start | bytes 6291460
  1.6 0.7 copy-start.1
  2.3 0.7 copy-start.2
  2.9 21.1 %copy-start.3 = (s32[1,16]{1,0:T(1,128)S(1)}, s32[1,16]{1,0:T(1,128)}, u32[]{:S(2)}) copy-start(s32[1,16]{1,0:T(1,128)} %mask_blk.1) | copy-start | bytes 196
  2.9 21.1 %copy-start.4 = (s32[1,16]{1,0:T(1,128)S(1)}, s32[1,16]{1,0:T(1,128)}, u32[]{:S(2)}) copy-start(s32[1,16]{1,0:T(1,128)} %mask_sub.1) | copy-start | bytes 196
  3.7 20.4 %collective-permute-start.6 = (bf16[256,1024]{1,0:T(8,128)(2,1)S(1)}, bf16[256,1024]{1,0:T(8,128)(2,1)S(1)}, u32[]{:S(2)}, u32[]{:S(2)}) collective-permute-start(bf16[256,1024]{1,0:T(8,128)(2,1)S(1)} %get-tuple-element.38), channel_id=1, source_target_pairs={{0,4},{4,0},{8,12},{12,8},{1,5},{5,1},{9,13},{13,9},{2,6},{6,2},{1... | collective-permute-start | bytes 1572872 | tf_op jit(solution)/shard_map/ppermute | solution.py:172
  4.2 16.3 %collective-permute-start.4 = (bf16[128,1024]{1,0:T(8,128)(2,1)S(1)}, bf16[128,1024]{1,0:T(8,128)(2,1)S(1)}, u32[]{:S(2)}, u32[]{:S(2)}) collective-permute-start(bf16[128,1024]{1,0:T(8,128)(2,1)S(1)} %get-tuple-element.36), channel_id=1, source_target_pairs={{0,2},{1,3},{2,0},{3,1},{4,6},{5,7},{6,4},{7,5},{8,10},{9,11},{10,... | collective-permute-start | bytes 786440 | tf_op jit(solution)/shard_map/ppermute | solution.py:172
  7.8 18.7 %collective-permute-start.5 = (bf16[256,1024]{1,0:T(8,128)(2,1)S(1)}, bf16[256,1024]{1,0:T(8,128)(2,1)S(1)}, u32[]{:S(2)}, u32[]{:S(2)}) collective-permute-start(bf16[256,1024]{1,0:T(8,128)(2,1)S(1)} %get-tuple-element.37), channel_id=1, source_target_pairs={{0,8},{4,12},{8,0},{12,4},{1,9},{5,13},{9,1},{13,5},{2,10},{6,14},... | collective-permute-start | bytes 1572872 | tf_op jit(solution)/shard_map/ppermute | solution.py:172
  10.1 22.2 %collective-permute-start.3 = (bf16[256,1024]{1,0:T(8,128)(2,1)S(1)}, bf16[256,1024]{1,0:T(8,128)(2,1)S(1)}, u32[]{:S(2)}, u32[]{:S(2)}) collective-permute-start(bf16[256,1024]{1,0:T(8,128)(2,1)S(1)} %get-tuple-element.35), channel_id=1, source_target_pairs={{0,12},{4,8},{8,4},{12,0},{1,13},{5,9},{9,5},{13,1},{2,14},{6,10},... | collective-permute-start | bytes 1572872 | tf_op jit(solution)/shard_map/ppermute | solution.py:172
  10.2 30.1 %collective-permute-start.2 = (bf16[256,1024]{1,0:T(8,128)(2,1)S(1)}, bf16[256,1024]{1,0:T(8,128)(2,1)S(1)}, u32[]{:S(2)}, u32[]{:S(2)}) collective-permute-start(bf16[256,1024]{1,0:T(8,128)(2,1)S(1)} %get-tuple-element.34), channel_id=1, source_target_pairs={{0,1},{1,0},{2,3},{3,2},{4,5},{5,4},{6,7},{7,6},{8,9},{9,8},{10,11... | collective-permute-start | bytes 1572872 | tf_op jit(solution)/shard_map/ppermute | solution.py:172
  20.5 40.8 %collective-permute-start = (bf16[256,1024]{1,0:T(8,128)(2,1)S(1)}, bf16[256,1024]{1,0:T(8,128)(2,1)S(1)}, u32[]{:S(2)}, u32[]{:S(2)}) collective-permute-start(bf16[256,1024]{1,0:T(8,128)(2,1)S(1)} %get-tuple-element.29), channel_id=1, source_target_pairs={{0,3},{1,2},{2,1},{3,0},{4,7},{5,6},{6,5},{7,4},{8,11},{9,10},{10,... | collective-permute-start | bytes 1572872 | tf_op jit(solution)/shard_map/ppermute | solution.py:172
  24.0 34.4 %collective-permute-start.1 = (bf16[128,1024]{1,0:T(8,128)(2,1)S(1)}, bf16[128,1024]{1,0:T(8,128)(2,1)S(1)}, u32[]{:S(2)}, u32[]{:S(2)}) collective-permute-start(bf16[128,1024]{1,0:T(8,128)(2,1)S(1)} %get-tuple-element.33), channel_id=1, source_target_pairs={{0,2},{1,3},{2,0},{3,1},{4,6},{5,7},{6,4},{7,5},{8,10},{9,11},{10,... | collective-permute-start | bytes 786440 | tf_op jit(solution)/shard_map/ppermute | solution.py:172
  26.5 1.3 %collective-permute-start.7 = (f32[8,128]{1,0:T(8,128)S(1)}, f32[8,128]{1,0:T(8,128)S(1)}, u32[]{:S(2)}, u32[]{:S(2)}) collective-permute-start(f32[8,128]{1,0:T(8,128)S(1)} %get-tuple-element.41), channel_id=1, source_target_pairs={{0,4},{4,0},{8,12},{12,8},{1,5},{5,1},{9,13},{13,9},{2,6},{6,2},{1... | collective-permute-start | bytes 12296 | tf_op jit(solution)/shard_map/ppermute | solution.py:172
  27.8 5.6 %collective-permute-start.8 = (f32[8,128]{1,0:T(8,128)S(1)}, f32[8,128]{1,0:T(8,128)S(1)}, u32[]{:S(2)}, u32[]{:S(2)}) collective-permute-start(f32[8,128]{1,0:T(8,128)S(1)} %get-tuple-element.43), channel_id=1, source_target_pairs={{0,8},{4,12},{8,0},{12,4},{1,9},{5,13},{9,1},{13,5},{2,10},{6,14},... | collective-permute-start | bytes 12296 | tf_op jit(solution)/shard_map/ppermute | solution.py:172
  32.3 24.8 %collective-permute-start.9 = (f32[8,128]{1,0:T(8,128)S(1)}, f32[8,128]{1,0:T(8,128)S(1)}, u32[]{:S(2)}, u32[]{:S(2)}) collective-permute-start(f32[8,128]{1,0:T(8,128)S(1)} %get-tuple-element.45), channel_id=1, source_target_pairs={{0,2},{1,3},{2,0},{3,1},{4,6},{5,7},{6,4},{7,5},{8,10},{9,11},{10,... | collective-permute-start | bytes 12296 | tf_op jit(solution)/shard_map/ppermute | solution.py:172
  34.6 23.8 %collective-permute-start.10 = (f32[8,128]{1,0:T(8,128)S(1)}, f32[8,128]{1,0:T(8,128)S(1)}, u32[]{:S(2)}, u32[]{:S(2)}) collective-permute-start(f32[8,128]{1,0:T(8,128)S(1)} %get-tuple-element.47), channel_id=1, source_target_pairs={{0,12},{4,8},{8,4},{12,0},{1,13},{5,9},{9,5},{13,1},{2,14},{6,10},... | collective-permute-start | bytes 12296 | tf_op jit(solution)/shard_map/ppermute | solution.py:172
  58.3 3.7 %collective-permute-start.11 = (f32[8,128]{1,0:T(8,128)S(1)}, f32[8,128]{1,0:T(8,128)S(1)}, u32[]{:S(2)}, u32[]{:S(2)}) collective-permute-start(f32[8,128]{1,0:T(8,128)S(1)} %get-tuple-element.49), channel_id=1, source_target_pairs={{0,1},{1,0},{2,3},{3,2},{4,5},{5,4},{6,7},{7,6},{8,9},{9,8},{10,11... | collective-permute-start | bytes 12296 | tf_op jit(solution)/shard_map/ppermute | solution.py:172
  59.5 5.7 %collective-permute-start.12 = (f32[8,128]{1,0:T(8,128)S(1)}, f32[8,128]{1,0:T(8,128)S(1)}, u32[]{:S(2)}, u32[]{:S(2)}) collective-permute-start(f32[8,128]{1,0:T(8,128)S(1)} %get-tuple-element.51), channel_id=1, source_target_pairs={{0,2},{1,3},{2,0},{3,1},{4,6},{5,7},{6,4},{7,5},{8,10},{9,11},{10,... | collective-permute-start | bytes 12296 | tf_op jit(solution)/shard_map/ppermute | solution.py:172
  63.2 5.5 %collective-permute-start.13 = (f32[8,128]{1,0:T(8,128)S(1)}, f32[8,128]{1,0:T(8,128)S(1)}, u32[]{:S(2)}, u32[]{:S(2)}) collective-permute-start(f32[8,128]{1,0:T(8,128)S(1)} %get-tuple-element.52), channel_id=1, source_target_pairs={{0,3},{1,2},{2,1},{3,0},{4,7},{5,6},{6,5},{7,4},{8,11},{9,10},{10,... | collective-permute-start | bytes 12296 | tf_op jit(solution)/shard_map/ppermute | solution.py:172

commit v5 on v4

--- a/solution.py
+++ b/solution.py
@@ -110,7 +110,7 @@
     )(pick_blk, pick_sub, mask_blk, mask_sub, embeds)
 
 
-def slot_kernel(place, first, rows, back_place, arrived, units, live, mine, totals, *rest):
+def slot_kernel(place, first, rows, back_place, carries, arrived, units, live, mine, totals, *rest):
     new_totals, back = rest[-2:]
     count = live.shape[1]
     before = totals[...]
@@ -135,13 +135,14 @@
         sums = jnp.sum(along_rows[part * LANES : (part + 1) * LANES].T, axis=0, keepdims=True)
         for i in range(count):
             row = i * ROWS + part
-            back[row : row + 1] = sums
-
-
-def work(place, slot, arrived, units, live, mine, totals, back_place, returned):
-    operands = [arrived, units, live, mine, totals] + ([] if back_place is None else [returned])
+            back[row : row + 1] = sums + rest[-3][row : row + 1] if carries else sums
+
+
+def work(place, slot, arrived, units, live, mine, totals, returned, carried):
+    back_place, came_back = returned or (None, None)
+    operands = [arrived, units, live, mine, totals] + [one for one in (came_back, carried) if one is not None]
     return pl.pallas_call(
-        functools.partial(slot_kernel, place, *slot[2:], back_place),
+        functools.partial(slot_kernel, place, *slot[2:], back_place, carried is not None),
         out_shape=[jax.ShapeDtypeStruct(totals.shape, jnp.float32)] * 2,
         in_specs=[VMEM] * len(operands),
         out_specs=[VMEM] * 2,
@@ -178,14 +179,20 @@
 
     units, live, mine = prepare(slots, pick_blk, pick_sub, mask_blk, mask_sub, embeds)
     totals = jnp.zeros((count * ROWS, LANES), jnp.float32)
-    returned = []
+    carried = {}
+    soon, late = [], []
     for place, slot in enumerate(slots):
-        back_place = place - BEHIND if place >= BEHIND else None
-        came_back = None if back_place is None else returned[back_place]
-        totals, back = work(place, slot, arrived[place], units, live, mine, totals, back_place, came_back)
-        returned.append(send(back, slot))
-    for place in range(len(slots) - BEHIND, len(slots)):
-        totals = totals + mine[place] * returned[place]
+        axis, step, first, rows = slot
+        ready = soon.pop(0) if soon and soon[0][0] <= place - BEHIND else None
+        totals, back = work(
+            place, slot, arrived[place], units, live, mine, totals, ready, carried.pop((axis, step), None)
+        )
+        if first + rows < BLOCK:
+            carried[axis, step] = back
+        else:
+            (soon if axis == "blk" else late).append((place, send(back, slot)))
+    for place, sums in soon + late:
+        totals = totals + mine[place] * sums
     return (totals * (1.0 / BLOCK)).reshape(-1)
 
 

time: 69.5 us -> 65.8 us (0.947)
  starting transfers between devices: 18.5 us -> 15.1 us
    ppermute x14 -> x13, starting transfers between devices: 18.5 us -> 15.1 us  [send(): return lax.ppermute(array, slot[0], pairs(slot[1], sizes[slot[0]]))]
    ppermute x14 -> x13, waiting for transfers between devices: 36.2 us -> 35.9 us  [send(): return lax.ppermute(array, slot[0], pairs(slot[1], sizes[slot[0]]))]
  transfers between devices with their start and end apart: 14 -> 13, of which waited for: 6 -> 7; matrix products, arithmetic and copies ran while one was open for 0% -> 0% of each run, Pallas kernels for 15% -> 16%
where the time goes in v5:
time: 65.8 us; the launch traced here: 65.6 us
  waiting for transfers between devices  35.9 us (55%)
  starting transfers between devices  15.1 us (23%)
  Pallas kernels  10.9 us (17%)
  local copies, waits for them, and re-layouts  2.94 us (4%)
    ppermute x13, waiting for transfers between devices, send(): return lax.ppermute(array, slot[0], pairs(slot[1], sizes[slot[0]]))  35.9 us
    ppermute x13, starting transfers between devices, send(): return lax.ppermute(array, slot[0], pairs(slot[1], sizes[slot[0]]))  15.1 us
    pallas_call x7, Pallas kernels, work(): pl.pallas_call(functools.partial(slot_kernel, place, *slot[2:], back_plac...  8.17 us
    unnamed x10, local copies, waits for them, and re-layouts  2.93 us
    pallas_call x2, Pallas kernels, pick_rows(): pl.pallas_call(functools.partial(pick_kernel, pieces), out_shape=[jax.Sha...  1.49 us
  transfers between devices with their start and end apart: 13, of which 7 were waited for; matrix products, arithmetic and copies ran while one was open for 0% of the time, Pallas kernels for 16%

profile of v5, /device:TPU:0, one launch (start us, length us, event | category | flops | bytes accessed | tf_op | source)
XLA Modules:
  0.0 65.6 jit_solution(3956200403925540535)
XLA Ops:
  0.0 0.0 copy-start
  0.0 1.6 %copy-done = bf16[1024,1024]{1,0:T(8,128)(2,1)S(1)} copy-done((bf16[1024,1024]{1,0:T(8,128)(2,1)S(1)}, bf16[1024,1024]{1,0:T(8,128)(2,1)}, u32[]{:S(2)}) %copy-start) | copy-done | bytes 2097176
  1.6 0.0 copy-start.1
  1.6 0.7 %copy-done.1 = s32[4,4]{1,0:T(4,128)S(1)} copy-done((s32[4,4]{1,0:T(4,128)S(1)}, s32[4,4]{1,0:T(4,128)}, u32[]{:S(2)}) %copy-start.1) | copy-done | bytes 88
  2.3 0.0 copy-start.2
  2.3 0.7 copy-done.2
  2.9 0.0 copy-start.3
  2.9 0.0 copy-start.4
  2.9 0.7 %shard_map.57 = (bf16[256,1024]{1,0:T(8,128)(2,1)S(1)}, bf16[256,1024]{1,0:T(8,128)(2,1)S(1)}, bf16[128,1024]{1,0:T(8,128)(2,1)S(1)}) custom-call(s32[1,4]{1,0:T(1,128)S(1)} %copy-done.2, s32[4,4]{1,0:T(4,128)S(1)} %copy-done.1, bf16[1024,1024]{1,0:T(8,128)(2,1)S(1)} %copy-done), custom_call_target="tpu_custom_call" | custom-call | tf_op jit(solution)/shard_map/pallas_call | solution.py:68
  3.7 0.5 collective-permute-start.6
  4.2 3.7 %collective-permute-start.4 = (bf16[128,1024]{1,0:T(8,128)(2,1)S(1)}, bf16[128,1024]{1,0:T(8,128)(2,1)S(1)}, u32[]{:S(2)}, u32[]{:S(2)}) collective-permute-start(bf16[128,1024]{1,0:T(8,128)(2,1)S(1)} %get-tuple-element.36), channel_id=1, source_target_pairs={{0,2},{1,3},{2,0},{3,1},{4,6},{5,7},{6,4},{7,5},{8,10},{9,11},{10,... | collective-permute-start | bytes 786440 | tf_op jit(solution)/shard_map/ppermute | solution.py:173
  7.8 1.5 %collective-permute-start.5 = (bf16[256,1024]{1,0:T(8,128)(2,1)S(1)}, bf16[256,1024]{1,0:T(8,128)(2,1)S(1)}, u32[]{:S(2)}, u32[]{:S(2)}) collective-permute-start(bf16[256,1024]{1,0:T(8,128)(2,1)S(1)} %get-tuple-element.37), channel_id=1, source_target_pairs={{0,8},{4,12},{8,0},{12,4},{1,9},{5,13},{9,1},{13,5},{2,10},{6,14},... | collective-permute-start | bytes 1572872 | tf_op jit(solution)/shard_map/ppermute | solution.py:173
  9.3 0.8 %shard_map.55 = (bf16[256,1024]{1,0:T(8,128)(2,1)S(1)}, bf16[256,1024]{1,0:T(8,128)(2,1)S(1)}, bf16[128,1024]{1,0:T(8,128)(2,1)S(1)}, bf16[256,1024]{1,0:T(8,128)(2,1)S(1)}) custom-call(s32[1,4]{1,0:T(1,128)S(1)} %copy-done.2, s32[4,4]{1,0:T(4,128)S(1)} %copy-done.1, bf16[1024,1024]{1,0:T(8,128)(2,1)S(1)} %copy-done), custom_call_target="tpu_custom_call" | custom-call | tf_op jit(solution)/shard_map/pallas_call | solution.py:68
  10.1 0.1 collective-permute-start.3
  10.2 1.6 %collective-permute-start.2 = (bf16[256,1024]{1,0:T(8,128)(2,1)S(1)}, bf16[256,1024]{1,0:T(8,128)(2,1)S(1)}, u32[]{:S(2)}, u32[]{:S(2)}) collective-permute-start(bf16[256,1024]{1,0:T(8,128)(2,1)S(1)} %get-tuple-element.34), channel_id=1, source_target_pairs={{0,1},{1,0},{2,3},{3,2},{4,5},{5,4},{6,7},{7,6},{8,9},{9,8},{10,11... | collective-permute-start | bytes 1572872 | tf_op jit(solution)/shard_map/ppermute | solution.py:173
  11.8 8.6 %collective-permute-done.4.arrived = bf16[128,1024]{1,0:T(8,128)(2,1)S(1)} collective-permute-done((bf16[128,1024]{1,0:T(8,128)(2,1)S(1)}, bf16[128,1024]{1,0:T(8,128)(2,1)S(1)}, u32[]{:S(2)}, u32[]{:S(2)}) %collective-permute-start.4) | collective-permute-done | bytes 262176 | tf_op jit(solution)/shard_map/ppermute | solution.py:173
  20.5 3.6 %collective-permute-start = (bf16[256,1024]{1,0:T(8,128)(2,1)S(1)}, bf16[256,1024]{1,0:T(8,128)(2,1)S(1)}, u32[]{:S(2)}, u32[]{:S(2)}) collective-permute-start(bf16[256,1024]{1,0:T(8,128)(2,1)S(1)} %get-tuple-element.29), channel_id=1, source_target_pairs={{0,3},{1,2},{2,1},{3,0},{4,7},{5,6},{6,5},{7,4},{8,11},{9,10},{10,... | collective-permute-start | bytes 1572872 | tf_op jit(solution)/shard_map/ppermute | solution.py:173
  24.0 0.0 collective-permute-done.6.arrived
  24.0 0.0 collective-permute-start.1
  24.0 0.0 copy-done.3
  24.0 0.0 copy-done.4
  24.0 1.2 %shard_map.56 = (bf16[1024,1024]{1,0:T(8,128)(2,1)S(1)}, f32[7,4,128]{2,1,0:T(4,128)S(1)}, f32[7,8,128]{2,1,0:T(8,128)S(1)}) custom-call(s32[1,4]{1,0:T(1,128)S(1)} %copy-done.2, s32[4,4]{1,0:T(4,128)S(1)} %copy-done.1, s32[1,16]{1,0:T(1,128)S(1)} %copy-done.3, s32[1,16]{1,0:T(1,128)S(1)} %copy-done.4, bf16[1024,1024]{1,0:T(8,128)(2,1)S(1)} %copy-done), custom_call_target="tpu_custom_call" | custom-call | tf_op jit(solution)/shard_map/pallas_call | solution.py:100
  25.3 1.2 %shard_map.58 = (f32[8,128]{1,0:T(8,128)S(1)}, f32[8,128]{1,0:T(8,128)S(1)}) custom-call(bf16[256,1024]{1,0:T(8,128)(2,1)S(1)} %collective-permute-done.6.arrived, bf16[1024,1024]{1,0:T(8,128)(2,1)S(1)} %get-tuple-element.30.units, f32[7,4,128]{2,1,0:T(4,128)S(1)} %get-tuple-element.31.live, f32[7,8,128]{2,1,0:T(8,128)S(1)} %get-tuple-element.32.mine, ...), custom_call_target="tpu_custom_call" | custom-call | tf_op jit(solution)/shard_map/pallas_call | solution.py:144
  26.5 0.0 collective-permute-done.5.arrived
  26.5 0.1 collective-permute-start.7
  26.6 1.2 %shard_map.59 = (f32[8,128]{1,0:T(8,128)S(1)}, f32[8,128]{1,0:T(8,128)S(1)}) custom-call(bf16[256,1024]{1,0:T(8,128)(2,1)S(1)} %collective-permute-done.5.arrived, bf16[1024,1024]{1,0:T(8,128)(2,1)S(1)} %get-tuple-element.30.units, f32[7,4,128]{2,1,0:T(4,128)S(1)} %get-tuple-element.31.live, f32[7,8,128]{2,1,0:T(8,128)S(1)} %get-tuple-element.32.mine, ...), custom_call_target="tpu_custom_call" | custom-call | tf_op jit(solution)/shard_map/pallas_call | solution.py:144
  27.8 0.0 collective-permute-done.7.rest_0_
  27.8 1.5 %collective-permute-start.8 = (f32[8,128]{1,0:T(8,128)S(1)}, f32[8,128]{1,0:T(8,128)S(1)}, u32[]{:S(2)}, u32[]{:S(2)}) collective-permute-start(f32[8,128]{1,0:T(8,128)S(1)} %get-tuple-element.43), channel_id=1, source_target_pairs={{0,8},{4,12},{8,0},{12,4},{1,9},{5,13},{9,1},{13,5},{2,10},{6,14},... | collective-permute-start | bytes 12296 | tf_op jit(solution)/shard_map/ppermute | solution.py:173
  29.4 1.1 %shard_map.60 = (f32[8,128]{1,0:T(8,128)S(1)}, f32[8,128]{1,0:T(8,128)S(1)}) custom-call(bf16[128,1024]{1,0:T(8,128)(2,1)S(1)} %collective-permute-done.4.arrived, bf16[1024,1024]{1,0:T(8,128)(2,1)S(1)} %get-tuple-element.30.units, f32[7,4,128]{2,1,0:T(4,128)S(1)} %get-tuple-element.31.live, f32[7,8,128]{2,1,0:T(8,128)S(1)} %get-tuple-element.32.mine, ...), custom_call_target="tpu_custom_call" | custom-call | tf_op jit(solution)/shard_map/pallas_call | solution.py:144
  30.4 1.9 %collective-permute-done.3.arrived = bf16[256,1024]{1,0:T(8,128)(2,1)S(1)} collective-permute-done((bf16[256,1024]{1,0:T(8,128)(2,1)S(1)}, bf16[256,1024]{1,0:T(8,128)(2,1)S(1)}, u32[]{:S(2)}, u32[]{:S(2)}) %collective-permute-start.3) | collective-permute-done | bytes 524320 | tf_op jit(solution)/shard_map/ppermute | solution.py:173
  32.3 0.9 %collective-permute-done.8.rest_0_ = f32[8,128]{1,0:T(8,128)S(1)} collective-permute-done((f32[8,128]{1,0:T(8,128)S(1)}, f32[8,128]{1,0:T(8,128)S(1)}, u32[]{:S(2)}, u32[]{:S(2)}) %collective-permute-start.8) | collective-permute-done | bytes 4128 | tf_op jit(solution)/shard_map/ppermute | solution.py:173
  33.2 1.2 %shard_map.61 = (f32[8,128]{1,0:T(8,128)S(1)}, f32[8,128]{1,0:T(8,128)S(1)}) custom-call(bf16[256,1024]{1,0:T(8,128)(2,1)S(1)} %collective-permute-done.3.arrived, bf16[1024,1024]{1,0:T(8,128)(2,1)S(1)} %get-tuple-element.30.units, f32[7,4,128]{2,1,0:T(4,128)S(1)} %get-tuple-element.31.live, f32[7,8,128]{2,1,0:T(8,128)S(1)} %get-tuple-element.32.mine, ...), custom_call_target="tpu_custom_call" | custom-call | tf_op jit(solution)/shard_map/pallas_call | solution.py:144
  34.4 1.2 %collective-permute-start.9 = (f32[8,128]{1,0:T(8,128)S(1)}, f32[8,128]{1,0:T(8,128)S(1)}, u32[]{:S(2)}, u32[]{:S(2)}) collective-permute-start(f32[8,128]{1,0:T(8,128)S(1)} %get-tuple-element.46), channel_id=1, source_target_pairs={{0,12},{4,8},{8,4},{12,0},{1,13},{5,9},{9,5},{13,1},{2,14},{6,10},... | collective-permute-start | bytes 12296 | tf_op jit(solution)/shard_map/ppermute | solution.py:173
  35.6 4.7 %collective-permute-done.2.arrived = bf16[256,1024]{1,0:T(8,128)(2,1)S(1)} collective-permute-done((bf16[256,1024]{1,0:T(8,128)(2,1)S(1)}, bf16[256,1024]{1,0:T(8,128)(2,1)S(1)}, u32[]{:S(2)}, u32[]{:S(2)}) %collective-permute-start.2) | collective-permute-done | bytes 524320 | tf_op jit(solution)/shard_map/ppermute | solution.py:173
  40.3 1.2 %shard_map.62 = (f32[8,128]{1,0:T(8,128)S(1)}, f32[8,128]{1,0:T(8,128)S(1)}) custom-call(bf16[256,1024]{1,0:T(8,128)(2,1)S(1)} %collective-permute-done.2.arrived, bf16[1024,1024]{1,0:T(8,128)(2,1)S(1)} %get-tuple-element.30.units, f32[7,4,128]{2,1,0:T(4,128)S(1)} %get-tuple-element.31.live, f32[7,8,128]{2,1,0:T(8,128)S(1)} %get-tuple-element.32.mine, ...), custom_call_target="tpu_custom_call" | custom-call | tf_op jit(solution)/shard_map/pallas_call | solution.py:144
  41.5 0.1 collective-permute-start.10
  41.6 15.3 %collective-permute-done.1.arrived = bf16[128,1024]{1,0:T(8,128)(2,1)S(1)} collective-permute-done((bf16[128,1024]{1,0:T(8,128)(2,1)S(1)}, bf16[128,1024]{1,0:T(8,128)(2,1)S(1)}, u32[]{:S(2)}, u32[]{:S(2)}) %collective-permute-start.1) | collective-permute-done | bytes 262176 | tf_op jit(solution)/shard_map/ppermute | solution.py:173
  57.0 0.0 collective-permute-done.9.rest_0_
  57.0 1.1 %shard_map.63 = (f32[8,128]{1,0:T(8,128)S(1)}, f32[8,128]{1,0:T(8,128)S(1)}) custom-call(bf16[128,1024]{1,0:T(8,128)(2,1)S(1)} %collective-permute-done.1.arrived, bf16[1024,1024]{1,0:T(8,128)(2,1)S(1)} %get-tuple-element.30.units, f32[7,4,128]{2,1,0:T(4,128)S(1)} %get-tuple-element.31.live, f32[7,8,128]{2,1,0:T(8,128)S(1)} %get-tuple-element.32.mine, ...), custom_call_target="tpu_custom_call" | custom-call | tf_op jit(solution)/shard_map/pallas_call | solution.py:144
  58.0 0.0 collective-permute-done.arrived
  58.0 1.2 %shard_map.64 = (f32[8,128]{1,0:T(8,128)S(1)}, f32[8,128]{1,0:T(8,128)S(1)}) custom-call(bf16[256,1024]{1,0:T(8,128)(2,1)S(1)} %collective-permute-done.arrived, bf16[1024,1024]{1,0:T(8,128)(2,1)S(1)} %get-tuple-element.30.units, f32[7,4,128]{2,1,0:T(4,128)S(1)} %get-tuple-element.31.live, f32[7,8,128]{2,1,0:T(8,128)S(1)} %get-tuple-element.32.mine, ...), custom_call_target="tpu_custom_call" | custom-call | tf_op jit(solution)/shard_map/pallas_call | solution.py:144
  59.2 1.2 %collective-permute-start.12 = (f32[8,128]{1,0:T(8,128)S(1)}, f32[8,128]{1,0:T(8,128)S(1)}, u32[]{:S(2)}, u32[]{:S(2)}) collective-permute-start(f32[8,128]{1,0:T(8,128)S(1)} %get-tuple-element.52), channel_id=1, source_target_pairs={{0,3},{1,2},{2,1},{3,0},{4,7},{5,6},{6,5},{7,4},{8,11},{9,10},{10,... | collective-permute-start | bytes 12296 | tf_op jit(solution)/shard_map/ppermute | solution.py:173
  60.5 0.0 collective-permute-start.11
  60.5 0.0 collective-permute-done.10
  60.5 4.2 %collective-permute-done.12 = f32[8,128]{1,0:T(8,128)S(1)} collective-permute-done((f32[8,128]{1,0:T(8,128)S(1)}, f32[8,128]{1,0:T(8,128)S(1)}, u32[]{:S(2)}, u32[]{:S(2)}) %collective-permute-start.12) | collective-permute-done | bytes 4128 | tf_op jit(solution)/shard_map/ppermute | solution.py:173
  64.7 0.3 collective-permute-done.11
  65.0 0.6 fusion.2
  (1 shorter events, 0.0 us)
Async XLA Ops:
  0.0 1.6 %copy-start = (bf16[1024,1024]{1,0:T(8,128)(2,1)S(1)}, bf16[1024,1024]{1,0:T(8,128)(2,1)}, u32[]{:S(2)}) copy-start(bf16[1024,1024]{1,0:T(8,128)(2,1)} %embeds.5) | copy-start | bytes 6291460
  1.6 0.7 %copy-start.1 = (s32[4,4]{1,0:T(4,128)S(1)}, s32[4,4]{1,0:T(4,128)}, u32[]{:S(2)}) copy-start(s32[4,4]{1,0:T(4,128)} %pick_sub.5) | copy-start | bytes 196
  2.3 0.7 copy-start.2
  2.9 21.1 %copy-start.3 = (s32[1,16]{1,0:T(1,128)S(1)}, s32[1,16]{1,0:T(1,128)}, u32[]{:S(2)}) copy-start(s32[1,16]{1,0:T(1,128)} %mask_blk.1) | copy-start | bytes 196
  2.9 21.1 %copy-start.4 = (s32[1,16]{1,0:T(1,128)S(1)}, s32[1,16]{1,0:T(1,128)}, u32[]{:S(2)}) copy-start(s32[1,16]{1,0:T(1,128)} %mask_sub.1) | copy-start | bytes 196
  3.7 20.4 %collective-permute-start.6 = (bf16[256,1024]{1,0:T(8,128)(2,1)S(1)}, bf16[256,1024]{1,0:T(8,128)(2,1)S(1)}, u32[]{:S(2)}, u32[]{:S(2)}) collective-permute-start(bf16[256,1024]{1,0:T(8,128)(2,1)S(1)} %get-tuple-element.38), channel_id=1, source_target_pairs={{0,4},{4,0},{8,12},{12,8},{1,5},{5,1},{9,13},{13,9},{2,6},{6,2},{1... | collective-permute-start | bytes 1572872 | tf_op jit(solution)/shard_map/ppermute | solution.py:173
  4.2 16.3 %collective-permute-start.4 = (bf16[128,1024]{1,0:T(8,128)(2,1)S(1)}, bf16[128,1024]{1,0:T(8,128)(2,1)S(1)}, u32[]{:S(2)}, u32[]{:S(2)}) collective-permute-start(bf16[128,1024]{1,0:T(8,128)(2,1)S(1)} %get-tuple-element.36), channel_id=1, source_target_pairs={{0,2},{1,3},{2,0},{3,1},{4,6},{5,7},{6,4},{7,5},{8,10},{9,11},{10,... | collective-permute-start | bytes 786440 | tf_op jit(solution)/shard_map/ppermute | solution.py:173
  7.8 18.7 %collective-permute-start.5 = (bf16[256,1024]{1,0:T(8,128)(2,1)S(1)}, bf16[256,1024]{1,0:T(8,128)(2,1)S(1)}, u32[]{:S(2)}, u32[]{:S(2)}) collective-permute-start(bf16[256,1024]{1,0:T(8,128)(2,1)S(1)} %get-tuple-element.37), channel_id=1, source_target_pairs={{0,8},{4,12},{8,0},{12,4},{1,9},{5,13},{9,1},{13,5},{2,10},{6,14},... | collective-permute-start | bytes 1572872 | tf_op jit(solution)/shard_map/ppermute | solution.py:173
  10.1 22.2 %collective-permute-start.3 = (bf16[256,1024]{1,0:T(8,128)(2,1)S(1)}, bf16[256,1024]{1,0:T(8,128)(2,1)S(1)}, u32[]{:S(2)}, u32[]{:S(2)}) collective-permute-start(bf16[256,1024]{1,0:T(8,128)(2,1)S(1)} %get-tuple-element.35), channel_id=1, source_target_pairs={{0,12},{4,8},{8,4},{12,0},{1,13},{5,9},{9,5},{13,1},{2,14},{6,10},... | collective-permute-start | bytes 1572872 | tf_op jit(solution)/shard_map/ppermute | solution.py:173
  10.2 30.1 %collective-permute-start.2 = (bf16[256,1024]{1,0:T(8,128)(2,1)S(1)}, bf16[256,1024]{1,0:T(8,128)(2,1)S(1)}, u32[]{:S(2)}, u32[]{:S(2)}) collective-permute-start(bf16[256,1024]{1,0:T(8,128)(2,1)S(1)} %get-tuple-element.34), channel_id=1, source_target_pairs={{0,1},{1,0},{2,3},{3,2},{4,5},{5,4},{6,7},{7,6},{8,9},{9,8},{10,11... | collective-permute-start | bytes 1572872 | tf_op jit(solution)/shard_map/ppermute | solution.py:173
  20.5 37.5 %collective-permute-start = (bf16[256,1024]{1,0:T(8,128)(2,1)S(1)}, bf16[256,1024]{1,0:T(8,128)(2,1)S(1)}, u32[]{:S(2)}, u32[]{:S(2)}) collective-permute-start(bf16[256,1024]{1,0:T(8,128)(2,1)S(1)} %get-tuple-element.29), channel_id=1, source_target_pairs={{0,3},{1,2},{2,1},{3,0},{4,7},{5,6},{6,5},{7,4},{8,11},{9,10},{10,... | collective-permute-start | bytes 1572872 | tf_op jit(solution)/shard_map/ppermute | solution.py:173
  24.0 32.9 %collective-permute-start.1 = (bf16[128,1024]{1,0:T(8,128)(2,1)S(1)}, bf16[128,1024]{1,0:T(8,128)(2,1)S(1)}, u32[]{:S(2)}, u32[]{:S(2)}) collective-permute-start(bf16[128,1024]{1,0:T(8,128)(2,1)S(1)} %get-tuple-element.33), channel_id=1, source_target_pairs={{0,2},{1,3},{2,0},{3,1},{4,6},{5,7},{6,4},{7,5},{8,10},{9,11},{10,... | collective-permute-start | bytes 786440 | tf_op jit(solution)/shard_map/ppermute | solution.py:173
  26.5 1.3 %collective-permute-start.7 = (f32[8,128]{1,0:T(8,128)S(1)}, f32[8,128]{1,0:T(8,128)S(1)}, u32[]{:S(2)}, u32[]{:S(2)}) collective-permute-start(f32[8,128]{1,0:T(8,128)S(1)} %get-tuple-element.41), channel_id=1, source_target_pairs={{0,4},{4,0},{8,12},{12,8},{1,5},{5,1},{9,13},{13,9},{2,6},{6,2},{1... | collective-permute-start | bytes 12296 | tf_op jit(solution)/shard_map/ppermute | solution.py:173
  27.8 5.3 %collective-permute-start.8 = (f32[8,128]{1,0:T(8,128)S(1)}, f32[8,128]{1,0:T(8,128)S(1)}, u32[]{:S(2)}, u32[]{:S(2)}) collective-permute-start(f32[8,128]{1,0:T(8,128)S(1)} %get-tuple-element.43), channel_id=1, source_target_pairs={{0,8},{4,12},{8,0},{12,4},{1,9},{5,13},{9,1},{13,5},{2,10},{6,14},... | collective-permute-start | bytes 12296 | tf_op jit(solution)/shard_map/ppermute | solution.py:173
  34.4 22.6 %collective-permute-start.9 = (f32[8,128]{1,0:T(8,128)S(1)}, f32[8,128]{1,0:T(8,128)S(1)}, u32[]{:S(2)}, u32[]{:S(2)}) collective-permute-start(f32[8,128]{1,0:T(8,128)S(1)} %get-tuple-element.46), channel_id=1, source_target_pairs={{0,12},{4,8},{8,4},{12,0},{1,13},{5,9},{9,5},{13,1},{2,14},{6,10},... | collective-permute-start | bytes 12296 | tf_op jit(solution)/shard_map/ppermute | solution.py:173
  41.5 19.0 %collective-permute-start.10 = (f32[8,128]{1,0:T(8,128)S(1)}, f32[8,128]{1,0:T(8,128)S(1)}, u32[]{:S(2)}, u32[]{:S(2)}) collective-permute-start(f32[8,128]{1,0:T(8,128)S(1)} %get-tuple-element.50), channel_id=1, source_target_pairs={{0,1},{1,0},{2,3},{3,2},{4,5},{5,4},{6,7},{7,6},{8,9},{9,8},{10,11... | collective-permute-start | bytes 12296 | tf_op jit(solution)/shard_map/ppermute | solution.py:173
  59.2 5.5 %collective-permute-start.12 = (f32[8,128]{1,0:T(8,128)S(1)}, f32[8,128]{1,0:T(8,128)S(1)}, u32[]{:S(2)}, u32[]{:S(2)}) collective-permute-start(f32[8,128]{1,0:T(8,128)S(1)} %get-tuple-element.52), channel_id=1, source_target_pairs={{0,3},{1,2},{2,1},{3,0},{4,7},{5,6},{6,5},{7,4},{8,11},{9,10},{10,... | collective-permute-start | bytes 12296 | tf_op jit(solution)/shard_map/ppermute | solution.py:173
  60.5 4.5 %collective-permute-start.11 = (f32[8,128]{1,0:T(8,128)S(1)}, f32[8,128]{1,0:T(8,128)S(1)}, u32[]{:S(2)}, u32[]{:S(2)}) collective-permute-start(f32[8,128]{1,0:T(8,128)S(1)} %get-tuple-element.51), channel_id=1, source_target_pairs={{0,2},{1,3},{2,0},{3,1},{4,6},{5,7},{6,4},{7,5},{8,10},{9,11},{10,... | collective-permute-start | bytes 12296 | tf_op jit(solution)/shard_map/ppermute | solution.py:173

commit v6 on v5

--- a/solution.py
+++ b/solution.py
@@ -18,6 +18,7 @@
 SMEM = pl.BlockSpec(memory_space=pltpu.SMEM)
 VMEM = pl.BlockSpec(memory_space=pltpu.VMEM)
 HBM = pl.BlockSpec(memory_space=pltpu.HBM)
+ANY = pl.BlockSpec(memory_space=pl.ANY)
 PARAMS = pltpu.CompilerParams(vmem_limit_bytes=32 * 2**20)
 
 
@@ -44,7 +45,7 @@
 
 
 def pick_kernel(pieces, pick_blk, pick_sub, embeds, *rest):
-    outs, (blk_scalars, sub_scalars, scalar_sems, block_sems) = rest[: len(pieces)], rest[-4:]
+    outs, (blk_scalars, sub_scalars, scalar_sems, in_sems, out_sems, *staged) = rest[: len(pieces)], rest[len(pieces) :]
     scalars = [
         pltpu.make_async_copy(pick_blk, blk_scalars, scalar_sems.at[0]),
         pltpu.make_async_copy(pick_sub, sub_scalars, scalar_sems.at[1]),
@@ -54,29 +55,38 @@
     for copy in scalars:
         copy.wait()
     copies = []
-    for place, (out, (axis, step, first, rows)) in enumerate(zip(outs, pieces)):
+    for place, (axis, step, first, rows) in enumerate(pieces):
         pick = take_pick(axis, step, blk_scalars, sub_scalars)
         start = pl.multiple_of(pick * BLOCK + first, math.gcd(BLOCK, first))
-        copies.append(pltpu.make_async_copy(embeds.at[pl.ds(start, rows)], out, block_sems.at[place]))
-    for copy in copies:
-        copy.start()
-    for copy in copies:
+        target = staged[place] if staged else outs[place]
+        copies.append(pltpu.make_async_copy(embeds.at[pl.ds(start, rows)], target, in_sems.at[place]))
+        copies[-1].start()
+    leaving = []
+    for place, copy in enumerate(copies):
         copy.wait()
-
-
-def pick_rows(pieces, pick_blk, pick_sub, embeds):
+        if staged:
+            leaving.append(pltpu.make_async_copy(staged[place], outs[place], out_sems.at[place]))
+            leaving[-1].start()
+    for copy in leaving:
+        copy.wait()
+
+
+def pick_rows(pieces, pick_blk, pick_sub, embeds, staged):
+    shapes = [(rows, embeds.shape[1]) for _, _, _, rows in pieces]
     return pl.pallas_call(
         functools.partial(pick_kernel, pieces),
-        out_shape=[jax.ShapeDtypeStruct((rows, embeds.shape[1]), embeds.dtype) for _, _, _, rows in pieces],
-        in_specs=[HBM] * 3,
-        out_specs=[VMEM] * len(pieces),
+        out_shape=[jax.ShapeDtypeStruct(shape, embeds.dtype) for shape in shapes],
+        in_specs=[ANY if staged else HBM] * 3,
+        out_specs=[ANY if staged else VMEM] * len(pieces),
         scratch_shapes=[
             pltpu.SMEM(pick_blk.shape, jnp.int32),
             pltpu.SMEM(pick_sub.shape, jnp.int32),
             pltpu.SemaphoreType.DMA((2,)),
             pltpu.SemaphoreType.DMA((len(pieces),)),
-        ],
-        compiler_params=PARAMS,
+            pltpu.SemaphoreType.DMA((len(pieces),)),
+        ]
+        + [pltpu.VMEM(shape, embeds.dtype) for shape in shapes if staged],
+        compiler_params=None if staged else PARAMS,
     )(pick_blk, pick_sub, embeds)
 
 
@@ -151,13 +161,14 @@
 
 
 BEHIND = 2
-EARLY_ROWS = 128
+EARLY_ROWS = 192
+HALF = BLOCK // 2
 
 
 def plan_slots(sizes):
-    slots = [("blk", 1, 0, BLOCK), ("blk", 2, 0, BLOCK), ("sub", 2, 0, EARLY_ROWS)]
-    slots += [("blk", k, 0, BLOCK) for k in range(3, sizes["blk"])]
-    slots += [("sub", 1, 0, BLOCK), ("sub", 2, EARLY_ROWS, BLOCK - EARLY_ROWS)]
+    slots = [("sub", 2, 0, EARLY_ROWS), ("blk", 1, 0, BLOCK), ("blk", 2, 0, BLOCK), ("sub", 1, 0, BLOCK)]
+    slots += [("blk", k, first, HALF) for k in range(3, sizes["blk"]) for first in (0, HALF)]
+    slots += [("sub", 2, EARLY_ROWS, BLOCK - EARLY_ROWS)]
     return slots + [("sub", k, 0, BLOCK) for k in range(3, sizes["sub"])]
 
 
@@ -173,8 +184,8 @@
         return lax.ppermute(array, slot[0], pairs(slot[1], sizes[slot[0]]))
 
     arrived = []
-    for group in (slots[:AT_ONCE], slots[AT_ONCE:]):
-        for rows, slot in zip(pick_rows(group, pick_blk, pick_sub, embeds), group):
+    for group, staged in ((slots[:AT_ONCE], True), (slots[AT_ONCE:], False)):
+        for rows, slot in zip(pick_rows(group, pick_blk, pick_sub, embeds, staged), group):
             arrived.append(send(rows, slot))
 
     units, live, mine = prepare(slots, pick_blk, pick_sub, mask_blk, mask_sub, embeds)

time: 65.8 us -> 66.4 us (level)
  Pallas kernels: 10.9 us -> 14.3 us
  local copies, waits for them, and re-layouts: 2.94 us -> 0.02 us
  waiting for transfers between devices: 35.9 us -> 36.7 us
  starting transfers between devices: 15.1 us -> 14.4 us
    unnamed x10, local copies, waits for them, and re-layouts: 2.93 us -> 0.02 us
    pallas_call x2, Pallas kernels: 1.49 us -> 4.07 us  [pick_rows(): pl.pallas_call(functools.partial(pick_kernel, pieces), out_shape=[jax.Sha...]
    pallas_call x7 -> x8, Pallas kernels: 8.17 us -> 9 us  [work(): pl.pallas_call(functools.partial(slot_kernel, place, *slot[2:], back_plac...]
    ppermute x13 -> x14, waiting for transfers between devices: 35.9 us -> 36.7 us  [send(): return lax.ppermute(array, slot[0], pairs(slot[1], sizes[slot[0]]))]
    ppermute x13 -> x14, starting transfers between devices: 15.1 us -> 14.4 us  [send(): return lax.ppermute(array, slot[0], pairs(slot[1], sizes[slot[0]]))]
  transfers between devices with their start and end apart: 13 -> 14, of which waited for: 7 -> 6; matrix products, arithmetic and copies ran while one was open for 0% -> 0% of each run, Pallas kernels for 16% -> 17%
where the time goes in v6:
time: 66.4 us; the launch traced here: 66.1 us
  waiting for transfers between devices  36.7 us (55%)
  starting transfers between devices  14.4 us (22%)
  Pallas kernels  14.3 us (22%)
    ppermute x14, waiting for transfers between devices, send(): return lax.ppermute(array, slot[0], pairs(slot[1], sizes[slot[0]]))  36.7 us
    ppermute x14, starting transfers between devices, send(): return lax.ppermute(array, slot[0], pairs(slot[1], sizes[slot[0]]))  14.4 us
    pallas_call x8, Pallas kernels, work(): pl.pallas_call(functools.partial(slot_kernel, place, *slot[2:], back_plac...  9 us
    pallas_call x2, Pallas kernels, pick_rows(): pl.pallas_call(functools.partial(pick_kernel, pieces), out_shape=[jax.Sha...  4.07 us
  transfers between devices with their start and end apart: 14, of which 6 were waited for; matrix products, arithmetic and copies ran while one was open for 0% of the time, Pallas kernels for 17%

profile of v6, /device:TPU:0, one launch (start us, length us, event | category | flops | bytes accessed | tf_op | source)
XLA Modules:
  0.0 66.1 jit_solution(11710365274099068440)
XLA Ops:
  0.0 0.0 copy-start.2
  0.0 0.0 copy-start.1
  0.0 0.0 copy-start.3
  0.0 3.1 %shard_map.57 = (bf16[192,1024]{1,0:T(8,128)(2,1)}, bf16[256,1024]{1,0:T(8,128)(2,1)}, bf16[256,1024]{1,0:T(8,128)(2,1)}) custom-call(s32[1,4]{1,0:T(1,128)} %pick_blk.5, s32[4,4]{1,0:T(4,128)} %pick_sub.5, bf16[1024,1024]{1,0:T(8,128)(2,1)} %embeds.5), custom_call_target="tpu_custom_call" | custom-call | tf_op jit(solution)/shard_map/pallas_call | solution.py:76
  3.1 0.8 %collective-permute-start.6 = (bf16[256,1024]{1,0:T(8,128)(2,1)}, bf16[256,1024]{1,0:T(8,128)(2,1)S(1)}, u32[]{:S(2)}, u32[]{:S(2)}) collective-permute-start(bf16[256,1024]{1,0:T(8,128)(2,1)} %get-tuple-element.41), channel_id=1, source_target_pairs={{0,4},{4,0},{8,12},{12,8},{1,5},{5,1},{9,13},{13,9},{2,6},{6,2},{1... | collective-permute-start | bytes 1572872 | tf_op jit(solution)/shard_map/ppermute | solution.py:184
  3.9 3.4 %collective-permute-start.7 = (bf16[192,1024]{1,0:T(8,128)(2,1)}, bf16[192,1024]{1,0:T(8,128)(2,1)S(1)}, u32[]{:S(2)}, u32[]{:S(2)}) collective-permute-start(bf16[192,1024]{1,0:T(8,128)(2,1)} %get-tuple-element.42), channel_id=1, source_target_pairs={{0,2},{1,3},{2,0},{3,1},{4,6},{5,7},{6,4},{7,5},{8,10},{9,11},{10,... | collective-permute-start | bytes 1179656 | tf_op jit(solution)/shard_map/ppermute | solution.py:184
  7.3 1.5 %collective-permute-start.5 = (bf16[256,1024]{1,0:T(8,128)(2,1)}, bf16[256,1024]{1,0:T(8,128)(2,1)S(1)}, u32[]{:S(2)}, u32[]{:S(2)}) collective-permute-start(bf16[256,1024]{1,0:T(8,128)(2,1)} %get-tuple-element.40), channel_id=1, source_target_pairs={{0,8},{4,12},{8,0},{12,4},{1,9},{5,13},{9,1},{13,5},{2,10},{6,14},... | collective-permute-start | bytes 1572872 | tf_op jit(solution)/shard_map/ppermute | solution.py:184
  8.8 0.0 copy-done
  8.8 0.0 copy-done.2
  8.8 0.0 copy-done.1
  8.8 1.0 %shard_map.55 = (bf16[256,1024]{1,0:T(8,128)(2,1)S(1)}, bf16[128,1024]{1,0:T(8,128)(2,1)S(1)}, bf16[128,1024]{1,0:T(8,128)(2,1)S(1)}, bf16[64,1024]{1,0:T(8,128)(2,1)S(1)}, bf16[256,1024]{1,0:T(8,128)(2,1)S(1)}) custom-call(s32[1,4]{1,0:T(1,128)S(1)} %copy-done.2, s32[4,4]{1,0:T(4,128)S(1)} %copy-done.1, bf16[1024,1024]{1,0:T(8,128)(2,1)S(1)} %copy-done), custom_call_target="tpu_custom_call" | custom-call | tf_op jit(solution)/shard_map/pallas_call | solution.py:76
  9.8 1.6 %collective-permute-start.4 = (bf16[256,1024]{1,0:T(8,128)(2,1)S(1)}, bf16[256,1024]{1,0:T(8,128)(2,1)S(1)}, u32[]{:S(2)}, u32[]{:S(2)}) collective-permute-start(bf16[256,1024]{1,0:T(8,128)(2,1)S(1)} %get-tuple-element.39), channel_id=1, source_target_pairs={{0,1},{1,0},{2,3},{3,2},{4,5},{5,4},{6,7},{7,6},{8,9},{9,8},{10,11... | collective-permute-start | bytes 1572872 | tf_op jit(solution)/shard_map/ppermute | solution.py:184
  11.4 0.2 collective-permute-start
  11.7 14.3 %collective-permute-done.7.arrived = bf16[192,1024]{1,0:T(8,128)(2,1)S(1)} collective-permute-done((bf16[192,1024]{1,0:T(8,128)(2,1)}, bf16[192,1024]{1,0:T(8,128)(2,1)S(1)}, u32[]{:S(2)}, u32[]{:S(2)}) %collective-permute-start.7) | collective-permute-done | bytes 393248 | tf_op jit(solution)/shard_map/ppermute | solution.py:184
  26.0 0.5 collective-permute-start.3
  26.5 0.0 collective-permute-done.6.arrived
  26.5 1.2 %collective-permute-start.2 = (bf16[128,1024]{1,0:T(8,128)(2,1)S(1)}, bf16[128,1024]{1,0:T(8,128)(2,1)S(1)}, u32[]{:S(2)}, u32[]{:S(2)}) collective-permute-start(bf16[128,1024]{1,0:T(8,128)(2,1)S(1)} %get-tuple-element.37), channel_id=1, source_target_pairs={{0,12},{4,8},{8,4},{12,0},{1,13},{5,9},{9,5},{13,1},{2,14},{6,10},... | collective-permute-start | bytes 786440 | tf_op jit(solution)/shard_map/ppermute | solution.py:184
  27.7 0.0 collective-permute-done.5.arrived
  27.7 0.0 collective-permute-start.1
  27.7 0.0 copy-done.3
  27.7 0.0 copy-done.4
  27.8 1.2 %shard_map.56 = (bf16[1024,1024]{1,0:T(8,128)(2,1)S(1)}, f32[8,4,128]{2,1,0:T(4,128)S(1)}, f32[8,8,128]{2,1,0:T(8,128)S(1)}) custom-call(s32[1,4]{1,0:T(1,128)S(1)} %copy-done.2, s32[4,4]{1,0:T(4,128)S(1)} %copy-done.1, s32[1,16]{1,0:T(1,128)S(1)} %copy-done.3, s32[1,16]{1,0:T(1,128)S(1)} %copy-done.4, bf16[1024,1024]{1,0:T(8,128)(2,1)S(1)} %copy-done), custom_call_target="tpu_custom_call" | custom-call | tf_op jit(solution)/shard_map/pallas_call | solution.py:110
  29.0 1.2 %shard_map.58 = (f32[8,128]{1,0:T(8,128)S(1)}, f32[8,128]{1,0:T(8,128)S(1)}) custom-call(bf16[192,1024]{1,0:T(8,128)(2,1)S(1)} %collective-permute-done.7.arrived, bf16[1024,1024]{1,0:T(8,128)(2,1)S(1)} %get-tuple-element.33.units, f32[8,4,128]{2,1,0:T(4,128)S(1)} %get-tuple-element.34.live, f32[8,8,128]{2,1,0:T(8,128)S(1)} %get-tuple-element.35.mine, ...), custom_call_target="tpu_custom_call" | custom-call | tf_op jit(solution)/shard_map/pallas_call | solution.py:154
  30.2 1.2 %shard_map.59 = (f32[8,128]{1,0:T(8,128)S(1)}, f32[8,128]{1,0:T(8,128)S(1)}) custom-call(bf16[256,1024]{1,0:T(8,128)(2,1)S(1)} %collective-permute-done.6.arrived, bf16[1024,1024]{1,0:T(8,128)(2,1)S(1)} %get-tuple-element.33.units, f32[8,4,128]{2,1,0:T(4,128)S(1)} %get-tuple-element.34.live, f32[8,8,128]{2,1,0:T(8,128)S(1)} %get-tuple-element.35.mine, ...), custom_call_target="tpu_custom_call" | custom-call | tf_op jit(solution)/shard_map/pallas_call | solution.py:154
  31.4 10.7 %collective-permute-done.4.arrived = bf16[256,1024]{1,0:T(8,128)(2,1)S(1)} collective-permute-done((bf16[256,1024]{1,0:T(8,128)(2,1)S(1)}, bf16[256,1024]{1,0:T(8,128)(2,1)S(1)}, u32[]{:S(2)}, u32[]{:S(2)}) %collective-permute-start.4) | collective-permute-done | bytes 524320 | tf_op jit(solution)/shard_map/ppermute | solution.py:184
  42.1 0.0 collective-permute-start.8
  42.1 1.2 %shard_map.60 = (f32[8,128]{1,0:T(8,128)S(1)}, f32[8,128]{1,0:T(8,128)S(1)}) custom-call(bf16[256,1024]{1,0:T(8,128)(2,1)S(1)} %collective-permute-done.5.arrived, bf16[1024,1024]{1,0:T(8,128)(2,1)S(1)} %get-tuple-element.33.units, f32[8,4,128]{2,1,0:T(4,128)S(1)} %get-tuple-element.34.live, f32[8,8,128]{2,1,0:T(8,128)S(1)} %get-tuple-element.35.mine, ...), custom_call_target="tpu_custom_call" | custom-call | tf_op jit(solution)/shard_map/pallas_call | solution.py:154
  43.2 0.0 collective-permute-done.8.rest_0_
  43.3 0.5 collective-permute-start.9
  43.7 1.2 %shard_map.61 = (f32[8,128]{1,0:T(8,128)S(1)}, f32[8,128]{1,0:T(8,128)S(1)}) custom-call(bf16[256,1024]{1,0:T(8,128)(2,1)S(1)} %collective-permute-done.4.arrived, bf16[1024,1024]{1,0:T(8,128)(2,1)S(1)} %get-tuple-element.33.units, f32[8,4,128]{2,1,0:T(4,128)S(1)} %get-tuple-element.34.live, f32[8,8,128]{2,1,0:T(8,128)S(1)} %get-tuple-element.35.mine, ...), custom_call_target="tpu_custom_call" | custom-call | tf_op jit(solution)/shard_map/pallas_call | solution.py:154
  44.9 0.0 collective-permute-done.3.arrived
  44.9 2.0 %collective-permute-done.9.rest_0_ = f32[8,128]{1,0:T(8,128)S(1)} collective-permute-done((f32[8,128]{1,0:T(8,128)S(1)}, f32[8,128]{1,0:T(8,128)S(1)}, u32[]{:S(2)}, u32[]{:S(2)}) %collective-permute-start.9) | collective-permute-done | bytes 4128 | tf_op jit(solution)/shard_map/ppermute | solution.py:184
  46.9 1.1 %shard_map.62 = (f32[8,128]{1,0:T(8,128)S(1)}, f32[8,128]{1,0:T(8,128)S(1)}) custom-call(bf16[128,1024]{1,0:T(8,128)(2,1)S(1)} %collective-permute-done.3.arrived, bf16[1024,1024]{1,0:T(8,128)(2,1)S(1)} %get-tuple-element.33.units, f32[8,4,128]{2,1,0:T(4,128)S(1)} %get-tuple-element.34.live, f32[8,8,128]{2,1,0:T(8,128)S(1)} %get-tuple-element.35.mine, ...), custom_call_target="tpu_custom_call" | custom-call | tf_op jit(solution)/shard_map/pallas_call | solution.py:154
  48.0 0.0 collective-permute-done.2.arrived
  48.0 1.1 %shard_map.63 = (f32[8,128]{1,0:T(8,128)S(1)}, f32[8,128]{1,0:T(8,128)S(1)}) custom-call(bf16[128,1024]{1,0:T(8,128)(2,1)S(1)} %collective-permute-done.2.arrived, bf16[1024,1024]{1,0:T(8,128)(2,1)S(1)} %get-tuple-element.33.units, f32[8,4,128]{2,1,0:T(4,128)S(1)} %get-tuple-element.34.live, f32[8,8,128]{2,1,0:T(8,128)S(1)} %get-tuple-element.35.mine, ...), custom_call_target="tpu_custom_call" | custom-call | tf_op jit(solution)/shard_map/pallas_call | solution.py:154
  49.1 0.1 collective-permute-start.10
  49.2 4.6 %collective-permute-done.1.arrived = bf16[64,1024]{1,0:T(8,128)(2,1)S(1)} collective-permute-done((bf16[64,1024]{1,0:T(8,128)(2,1)S(1)}, bf16[64,1024]{1,0:T(8,128)(2,1)S(1)}, u32[]{:S(2)}, u32[]{:S(2)}) %collective-permute-start.1) | collective-permute-done | bytes 131104 | tf_op jit(solution)/shard_map/ppermute | solution.py:184
  53.8 0.9 %shard_map.64 = (f32[8,128]{1,0:T(8,128)S(1)}, f32[8,128]{1,0:T(8,128)S(1)}) custom-call(bf16[64,1024]{1,0:T(8,128)(2,1)S(1)} %collective-permute-done.1.arrived, bf16[1024,1024]{1,0:T(8,128)(2,1)S(1)} %get-tuple-element.33.units, f32[8,4,128]{2,1,0:T(4,128)S(1)} %get-tuple-element.34.live, f32[8,8,128]{2,1,0:T(8,128)S(1)} %get-tuple-element.35.mine, ...), custom_call_target="tpu_custom_call" | custom-call | tf_op jit(solution)/shard_map/pallas_call | solution.py:154
  54.7 0.1 collective-permute-start.12
  54.8 4.1 %collective-permute-start.11 = (f32[8,128]{1,0:T(8,128)S(1)}, f32[8,128]{1,0:T(8,128)S(1)}, u32[]{:S(2)}, u32[]{:S(2)}) collective-permute-start(f32[8,128]{1,0:T(8,128)S(1)} %get-tuple-element.56), channel_id=1, source_target_pairs={{0,1},{1,0},{2,3},{3,2},{4,5},{5,4},{6,7},{7,6},{8,9},{9,8},{10,11... | collective-permute-start | bytes 12296 | tf_op jit(solution)/shard_map/ppermute | solution.py:184
  58.9 0.0 collective-permute-done.arrived
  58.9 0.0 collective-permute-done.10.rest_0_
  58.9 1.2 %shard_map.65 = (f32[8,128]{1,0:T(8,128)S(1)}, f32[8,128]{1,0:T(8,128)S(1)}) custom-call(bf16[256,1024]{1,0:T(8,128)(2,1)S(1)} %collective-permute-done.arrived, bf16[1024,1024]{1,0:T(8,128)(2,1)S(1)} %get-tuple-element.33.units, f32[8,4,128]{2,1,0:T(4,128)S(1)} %get-tuple-element.34.live, f32[8,8,128]{2,1,0:T(8,128)S(1)} %get-tuple-element.35.mine, ...), custom_call_target="tpu_custom_call" | custom-call | tf_op jit(solution)/shard_map/pallas_call | solution.py:154
  60.1 0.3 collective-permute-start.13
  60.4 0.0 collective-permute-done.12
  60.4 0.1 collective-permute-done.11
  60.4 5.1 %collective-permute-done.13 = f32[8,128]{1,0:T(8,128)S(1)} collective-permute-done((f32[8,128]{1,0:T(8,128)S(1)}, f32[8,128]{1,0:T(8,128)S(1)}, u32[]{:S(2)}, u32[]{:S(2)}) %collective-permute-start.13) | collective-permute-done | bytes 4128 | tf_op jit(solution)/shard_map/ppermute | solution.py:184
  65.5 0.6 fusion.2
  (3 shorter events, 0.0 us)
Async XLA Ops:
  0.0 8.8 %copy-start = (bf16[1024,1024]{1,0:T(8,128)(2,1)S(1)}, bf16[1024,1024]{1,0:T(8,128)(2,1)}, u32[]{:S(2)}) copy-start(bf16[1024,1024]{1,0:T(8,128)(2,1)} %embeds.5) | copy-start | bytes 6291460
  0.0 8.8 %copy-start.2 = (s32[1,4]{1,0:T(1,128)S(1)}, s32[1,4]{1,0:T(1,128)}, u32[]{:S(2)}) copy-start(s32[1,4]{1,0:T(1,128)} %pick_blk.5) | copy-start | bytes 52
  0.0 8.8 %copy-start.1 = (s32[4,4]{1,0:T(4,128)S(1)}, s32[4,4]{1,0:T(4,128)}, u32[]{:S(2)}) copy-start(s32[4,4]{1,0:T(4,128)} %pick_sub.5) | copy-start | bytes 196
  0.0 27.7 %copy-start.3 = (s32[1,16]{1,0:T(1,128)S(1)}, s32[1,16]{1,0:T(1,128)}, u32[]{:S(2)}) copy-start(s32[1,16]{1,0:T(1,128)} %mask_blk.1) | copy-start | bytes 196
  0.0 27.7 %copy-start.4 = (s32[1,16]{1,0:T(1,128)S(1)}, s32[1,16]{1,0:T(1,128)}, u32[]{:S(2)}) copy-start(s32[1,16]{1,0:T(1,128)} %mask_sub.1) | copy-start | bytes 196
  3.1 23.4 %collective-permute-start.6 = (bf16[256,1024]{1,0:T(8,128)(2,1)}, bf16[256,1024]{1,0:T(8,128)(2,1)S(1)}, u32[]{:S(2)}, u32[]{:S(2)}) collective-permute-start(bf16[256,1024]{1,0:T(8,128)(2,1)} %get-tuple-element.41), channel_id=1, source_target_pairs={{0,4},{4,0},{8,12},{12,8},{1,5},{5,1},{9,13},{13,9},{2,6},{6,2},{1... | collective-permute-start | bytes 1572872 | tf_op jit(solution)/shard_map/ppermute | solution.py:184
  3.9 22.1 %collective-permute-start.7 = (bf16[192,1024]{1,0:T(8,128)(2,1)}, bf16[192,1024]{1,0:T(8,128)(2,1)S(1)}, u32[]{:S(2)}, u32[]{:S(2)}) collective-permute-start(bf16[192,1024]{1,0:T(8,128)(2,1)} %get-tuple-element.42), channel_id=1, source_target_pairs={{0,2},{1,3},{2,0},{3,1},{4,6},{5,7},{6,4},{7,5},{8,10},{9,11},{10,... | collective-permute-start | bytes 1179656 | tf_op jit(solution)/shard_map/ppermute | solution.py:184
  7.3 20.4 %collective-permute-start.5 = (bf16[256,1024]{1,0:T(8,128)(2,1)}, bf16[256,1024]{1,0:T(8,128)(2,1)S(1)}, u32[]{:S(2)}, u32[]{:S(2)}) collective-permute-start(bf16[256,1024]{1,0:T(8,128)(2,1)} %get-tuple-element.40), channel_id=1, source_target_pairs={{0,8},{4,12},{8,0},{12,4},{1,9},{5,13},{9,1},{13,5},{2,10},{6,14},... | collective-permute-start | bytes 1572872 | tf_op jit(solution)/shard_map/ppermute | solution.py:184
  9.8 32.3 %collective-permute-start.4 = (bf16[256,1024]{1,0:T(8,128)(2,1)S(1)}, bf16[256,1024]{1,0:T(8,128)(2,1)S(1)}, u32[]{:S(2)}, u32[]{:S(2)}) collective-permute-start(bf16[256,1024]{1,0:T(8,128)(2,1)S(1)} %get-tuple-element.39), channel_id=1, source_target_pairs={{0,1},{1,0},{2,3},{3,2},{4,5},{5,4},{6,7},{7,6},{8,9},{9,8},{10,11... | collective-permute-start | bytes 1572872 | tf_op jit(solution)/shard_map/ppermute | solution.py:184
  11.4 47.4 %collective-permute-start = (bf16[256,1024]{1,0:T(8,128)(2,1)S(1)}, bf16[256,1024]{1,0:T(8,128)(2,1)S(1)}, u32[]{:S(2)}, u32[]{:S(2)}) collective-permute-start(bf16[256,1024]{1,0:T(8,128)(2,1)S(1)} %get-tuple-element.32), channel_id=1, source_target_pairs={{0,3},{1,2},{2,1},{3,0},{4,7},{5,6},{6,5},{7,4},{8,11},{9,10},{10,... | collective-permute-start | bytes 1572872 | tf_op jit(solution)/shard_map/ppermute | solution.py:184
  26.0 19.0 %collective-permute-start.3 = (bf16[128,1024]{1,0:T(8,128)(2,1)S(1)}, bf16[128,1024]{1,0:T(8,128)(2,1)S(1)}, u32[]{:S(2)}, u32[]{:S(2)}) collective-permute-start(bf16[128,1024]{1,0:T(8,128)(2,1)S(1)} %get-tuple-element.38), channel_id=1, source_target_pairs={{0,12},{4,8},{8,4},{12,0},{1,13},{5,9},{9,5},{13,1},{2,14},{6,10},... | collective-permute-start | bytes 786440 | tf_op jit(solution)/shard_map/ppermute | solution.py:184
  26.5 21.5 %collective-permute-start.2 = (bf16[128,1024]{1,0:T(8,128)(2,1)S(1)}, bf16[128,1024]{1,0:T(8,128)(2,1)S(1)}, u32[]{:S(2)}, u32[]{:S(2)}) collective-permute-start(bf16[128,1024]{1,0:T(8,128)(2,1)S(1)} %get-tuple-element.37), channel_id=1, source_target_pairs={{0,12},{4,8},{8,4},{12,0},{1,13},{5,9},{9,5},{13,1},{2,14},{6,10},... | collective-permute-start | bytes 786440 | tf_op jit(solution)/shard_map/ppermute | solution.py:184
  27.7 26.0 %collective-permute-start.1 = (bf16[64,1024]{1,0:T(8,128)(2,1)S(1)}, bf16[64,1024]{1,0:T(8,128)(2,1)S(1)}, u32[]{:S(2)}, u32[]{:S(2)}) collective-permute-start(bf16[64,1024]{1,0:T(8,128)(2,1)S(1)} %get-tuple-element.36), channel_id=1, source_target_pairs={{0,2},{1,3},{2,0},{3,1},{4,6},{5,7},{6,4},{7,5},{8,10},{9,11},{10,... | collective-permute-start | bytes 393224 | tf_op jit(solution)/shard_map/ppermute | solution.py:184
  42.1 1.2 %collective-permute-start.8 = (f32[8,128]{1,0:T(8,128)S(1)}, f32[8,128]{1,0:T(8,128)S(1)}, u32[]{:S(2)}, u32[]{:S(2)}) collective-permute-start(f32[8,128]{1,0:T(8,128)S(1)} %get-tuple-element.46), channel_id=1, source_target_pairs={{0,4},{4,0},{8,12},{12,8},{1,5},{5,1},{9,13},{13,9},{2,6},{6,2},{1... | collective-permute-start | bytes 12296 | tf_op jit(solution)/shard_map/ppermute | solution.py:184
  43.3 3.7 %collective-permute-start.9 = (f32[8,128]{1,0:T(8,128)S(1)}, f32[8,128]{1,0:T(8,128)S(1)}, u32[]{:S(2)}, u32[]{:S(2)}) collective-permute-start(f32[8,128]{1,0:T(8,128)S(1)} %get-tuple-element.48), channel_id=1, source_target_pairs={{0,8},{4,12},{8,0},{12,4},{1,9},{5,13},{9,1},{13,5},{2,10},{6,14},... | collective-permute-start | bytes 12296 | tf_op jit(solution)/shard_map/ppermute | solution.py:184
  49.1 9.8 %collective-permute-start.10 = (f32[8,128]{1,0:T(8,128)S(1)}, f32[8,128]{1,0:T(8,128)S(1)}, u32[]{:S(2)}, u32[]{:S(2)}) collective-permute-start(f32[8,128]{1,0:T(8,128)S(1)} %get-tuple-element.54), channel_id=1, source_target_pairs={{0,12},{4,8},{8,4},{12,0},{1,13},{5,9},{9,5},{13,1},{2,14},{6,10},... | collective-permute-start | bytes 12296 | tf_op jit(solution)/shard_map/ppermute | solution.py:184
  54.7 5.7 %collective-permute-start.12 = (f32[8,128]{1,0:T(8,128)S(1)}, f32[8,128]{1,0:T(8,128)S(1)}, u32[]{:S(2)}, u32[]{:S(2)}) collective-permute-start(f32[8,128]{1,0:T(8,128)S(1)} %get-tuple-element.57), channel_id=1, source_target_pairs={{0,2},{1,3},{2,0},{3,1},{4,6},{5,7},{6,4},{7,5},{8,10},{9,11},{10,... | collective-permute-start | bytes 12296 | tf_op jit(solution)/shard_map/ppermute | solution.py:184
  54.8 5.7 %collective-permute-start.11 = (f32[8,128]{1,0:T(8,128)S(1)}, f32[8,128]{1,0:T(8,128)S(1)}, u32[]{:S(2)}, u32[]{:S(2)}) collective-permute-start(f32[8,128]{1,0:T(8,128)S(1)} %get-tuple-element.56), channel_id=1, source_target_pairs={{0,1},{1,0},{2,3},{3,2},{4,5},{5,4},{6,7},{7,6},{8,9},{9,8},{10,11... | collective-permute-start | bytes 12296 | tf_op jit(solution)/shard_map/ppermute | solution.py:184
  60.1 5.5 %collective-permute-start.13 = (f32[8,128]{1,0:T(8,128)S(1)}, f32[8,128]{1,0:T(8,128)S(1)}, u32[]{:S(2)}, u32[]{:S(2)}) collective-permute-start(f32[8,128]{1,0:T(8,128)S(1)} %get-tuple-element.58), channel_id=1, source_target_pairs={{0,3},{1,2},{2,1},{3,0},{4,7},{5,6},{6,5},{7,4},{8,11},{9,10},{10,... | collective-permute-start | bytes 12296 | tf_op jit(solution)/shard_map/ppermute | solution.py:184

commit v7 on v6

--- a/solution.py
+++ b/solution.py
@@ -120,12 +120,12 @@
     )(pick_blk, pick_sub, mask_blk, mask_sub, embeds)
 
 
-def slot_kernel(place, first, rows, back_place, carries, arrived, units, live, mine, totals, *rest):
+def slot_kernel(place, first, rows, back_places, carries, arrived, units, live, mine, totals, *rest):
     new_totals, back = rest[-2:]
     count = live.shape[1]
     before = totals[...]
-    if back_place is not None:
-        before = before + mine[back_place] * rest[0][...]
+    for back_place, sums in zip(back_places, rest):
+        before = before + mine[back_place] * sums[...]
     new_totals[...] = before
     x = rounded_units(arrived[...])
     along_rows = jnp.zeros((rows, LANES), jnp.float32)
@@ -149,10 +149,10 @@
 
 
 def work(place, slot, arrived, units, live, mine, totals, returned, carried):
-    back_place, came_back = returned or (None, None)
-    operands = [arrived, units, live, mine, totals] + [one for one in (came_back, carried) if one is not None]
+    operands = [arrived, units, live, mine, totals] + [sums for _, sums in returned]
+    operands += [] if carried is None else [carried]
     return pl.pallas_call(
-        functools.partial(slot_kernel, place, *slot[2:], back_place, carried is not None),
+        functools.partial(slot_kernel, place, *slot[2:], [one for one, _ in returned], carried is not None),
         out_shape=[jax.ShapeDtypeStruct(totals.shape, jnp.float32)] * 2,
         in_specs=[VMEM] * len(operands),
         out_specs=[VMEM] * 2,
@@ -166,12 +166,14 @@
 
 
 def plan_slots(sizes):
-    slots = [("sub", 2, 0, EARLY_ROWS), ("blk", 1, 0, BLOCK), ("blk", 2, 0, BLOCK), ("sub", 1, 0, BLOCK)]
+    slots = [("sub", 2, 0, EARLY_ROWS), ("sub", 2, EARLY_ROWS, BLOCK - EARLY_ROWS)]
+    slots += [("blk", 1, 0, BLOCK), ("blk", 2, 0, BLOCK), ("sub", 1, 0, BLOCK)]
     slots += [("blk", k, first, HALF) for k in range(3, sizes["blk"]) for first in (0, HALF)]
-    slots += [("sub", 2, EARLY_ROWS, BLOCK - EARLY_ROWS)]
     return slots + [("sub", k, 0, BLOCK) for k in range(3, sizes["sub"])]
 
 
+EARLY_ROWS = 160
+HALF = BLOCK // 2
 AT_ONCE = 3
 
 
@@ -194,7 +196,11 @@
     soon, late = [], []
     for place, slot in enumerate(slots):
         axis, step, first, rows = slot
-        ready = soon.pop(0) if soon and soon[0][0] <= place - BEHIND else None
+        if place == len(slots) - 1:
+            ready, soon, late = soon + late, [], []
+        else:
+            done = sum(sent <= place - BEHIND for sent, _ in soon)
+            ready, soon = soon[:done], soon[done:]
         totals, back = work(
             place, slot, arrived[place], units, live, mine, totals, ready, carried.pop((axis, step), None)
         )
@@ -202,7 +208,7 @@
             carried[axis, step] = back
         else:
             (soon if axis == "blk" else late).append((place, send(back, slot)))
-    for place, sums in soon + late:
+    for place, sums in late:
         totals = totals + mine[place] * sums
     return (totals * (1.0 / BLOCK)).reshape(-1)
 

time: 66.4 us -> 63 us (0.949)
  waiting for transfers between devices: 36.7 us -> 25.8 us
  starting transfers between devices: 14.4 us -> 22.3 us
    ppermute x14, waiting for transfers between devices: 36.7 us -> 25.8 us  [send(): return lax.ppermute(array, slot[0], pairs(slot[1], sizes[slot[0]]))]
    ppermute x14, starting transfers between devices: 14.4 us -> 22.3 us  [send(): return lax.ppermute(array, slot[0], pairs(slot[1], sizes[slot[0]]))]
  transfers between devices with their start and end apart: 14 -> 14, of which waited for: 6 -> 6; matrix products, arithmetic and copies ran while one was open for 0% -> 0% of each run, Pallas kernels for 17% -> 16%
where the time goes in v7:
time: 63 us; the launch traced here: 62.8 us
  waiting for transfers between devices  25.8 us (41%)
  starting transfers between devices  22.3 us (35%)
  Pallas kernels  14.1 us (22%)
    ppermute x14, waiting for transfers between devices, send(): return lax.ppermute(array, slot[0], pairs(slot[1], sizes[slot[0]]))  25.8 us
    ppermute x14, starting transfers between devices, send(): return lax.ppermute(array, slot[0], pairs(slot[1], sizes[slot[0]]))  22.3 us
    pallas_call x8, Pallas kernels, work(): pl.pallas_call(functools.partial(slot_kernel, place, *slot[2:], [one for...  9.03 us
    pallas_call x2, Pallas kernels, pick_rows(): pl.pallas_call(functools.partial(pick_kernel, pieces), out_shape=[jax.Sha...  3.82 us
  transfers between devices with their start and end apart: 14, of which 6 were waited for; matrix products, arithmetic and copies ran while one was open for 0% of the time, Pallas kernels for 16%

profile of v7, /device:TPU:0, one launch (start us, length us, event | category | flops | bytes accessed | tf_op | source)
XLA Modules:
  0.0 62.8 jit_solution(17727635459899756750)
XLA Ops:
  0.0 0.0 copy-start
  0.0 0.0 copy-start.2
  0.0 0.0 copy-start.1
  0.0 3.0 %shard_map.57 = (bf16[160,1024]{1,0:T(8,128)(2,1)}, bf16[96,1024]{1,0:T(8,128)(2,1)}, bf16[256,1024]{1,0:T(8,128)(2,1)}) custom-call(s32[1,4]{1,0:T(1,128)} %pick_blk.5, s32[4,4]{1,0:T(4,128)} %pick_sub.5, bf16[1024,1024]{1,0:T(8,128)(2,1)} %embeds.5), custom_call_target="tpu_custom_call" | custom-call | tf_op jit(solution)/shard_map/pallas_call | solution.py:76
  3.0 0.5 collective-permute-start.5
  3.5 3.7 %collective-permute-start.6 = (bf16[96,1024]{1,0:T(8,128)(2,1)}, bf16[96,1024]{1,0:T(8,128)(2,1)S(1)}, u32[]{:S(2)}, u32[]{:S(2)}) collective-permute-start(bf16[96,1024]{1,0:T(8,128)(2,1)} %get-tuple-element.41), channel_id=1, source_target_pairs={{0,2},{1,3},{2,0},{3,1},{4,6},{5,7},{6,4},{7,5},{8,10},{9,11},{10,... | collective-permute-start | bytes 589832 | tf_op jit(solution)/shard_map/ppermute | solution.py:186
  7.2 0.1 collective-permute-start.7
  7.3 0.0 copy-done
  7.3 0.0 copy-done.2
  7.3 0.0 copy-done.1
  7.3 0.9 %shard_map.55 = (bf16[256,1024]{1,0:T(8,128)(2,1)S(1)}, bf16[256,1024]{1,0:T(8,128)(2,1)S(1)}, bf16[128,1024]{1,0:T(8,128)(2,1)S(1)}, bf16[128,1024]{1,0:T(8,128)(2,1)S(1)}, bf16[256,1024]{1,0:T(8,128)(2,1)S(1)}) custom-call(s32[1,4]{1,0:T(1,128)S(1)} %copy-done.2, s32[4,4]{1,0:T(4,128)S(1)} %copy-done.1, bf16[1024,1024]{1,0:T(8,128)(2,1)S(1)} %copy-done), custom_call_target="tpu_custom_call" | custom-call | tf_op jit(solution)/shard_map/pallas_call | solution.py:76
  8.2 1.8 %collective-permute-start.4 = (bf16[256,1024]{1,0:T(8,128)(2,1)S(1)}, bf16[256,1024]{1,0:T(8,128)(2,1)S(1)}, u32[]{:S(2)}, u32[]{:S(2)}) collective-permute-start(bf16[256,1024]{1,0:T(8,128)(2,1)S(1)} %get-tuple-element.39), channel_id=1, source_target_pairs={{0,8},{4,12},{8,0},{12,4},{1,9},{5,13},{9,1},{13,5},{2,10},{6,14},... | collective-permute-start | bytes 1572872 | tf_op jit(solution)/shard_map/ppermute | solution.py:186
  10.0 1.6 %collective-permute-start.3 = (bf16[256,1024]{1,0:T(8,128)(2,1)S(1)}, bf16[256,1024]{1,0:T(8,128)(2,1)S(1)}, u32[]{:S(2)}, u32[]{:S(2)}) collective-permute-start(bf16[256,1024]{1,0:T(8,128)(2,1)S(1)} %get-tuple-element.38), channel_id=1, source_target_pairs={{0,1},{1,0},{2,3},{3,2},{4,5},{5,4},{6,7},{7,6},{8,9},{9,8},{10,11... | collective-permute-start | bytes 1572872 | tf_op jit(solution)/shard_map/ppermute | solution.py:186
  11.5 12.9 %collective-permute-done.6.arrived = bf16[96,1024]{1,0:T(8,128)(2,1)S(1)} collective-permute-done((bf16[96,1024]{1,0:T(8,128)(2,1)}, bf16[96,1024]{1,0:T(8,128)(2,1)S(1)}, u32[]{:S(2)}, u32[]{:S(2)}) %collective-permute-start.6) | collective-permute-done | bytes 196640 | tf_op jit(solution)/shard_map/ppermute | solution.py:186
  24.5 3.3 %collective-permute-start = (bf16[256,1024]{1,0:T(8,128)(2,1)S(1)}, bf16[256,1024]{1,0:T(8,128)(2,1)S(1)}, u32[]{:S(2)}, u32[]{:S(2)}) collective-permute-start(bf16[256,1024]{1,0:T(8,128)(2,1)S(1)} %get-tuple-element.32), channel_id=1, source_target_pairs={{0,3},{1,2},{2,1},{3,0},{4,7},{5,6},{6,5},{7,4},{8,11},{9,10},{10,... | collective-permute-start | bytes 1572872 | tf_op jit(solution)/shard_map/ppermute | solution.py:186
  27.8 3.6 %collective-permute-done.7.arrived = bf16[160,1024]{1,0:T(8,128)(2,1)S(1)} collective-permute-done((bf16[160,1024]{1,0:T(8,128)(2,1)}, bf16[160,1024]{1,0:T(8,128)(2,1)S(1)}, u32[]{:S(2)}, u32[]{:S(2)}) %collective-permute-start.7) | collective-permute-done | bytes 327712 | tf_op jit(solution)/shard_map/ppermute | solution.py:186
  31.4 0.6 collective-permute-start.2
  32.0 0.0 collective-permute-done.5.arrived
  32.0 1.2 %collective-permute-start.1 = (bf16[128,1024]{1,0:T(8,128)(2,1)S(1)}, bf16[128,1024]{1,0:T(8,128)(2,1)S(1)}, u32[]{:S(2)}, u32[]{:S(2)}) collective-permute-start(bf16[128,1024]{1,0:T(8,128)(2,1)S(1)} %get-tuple-element.36), channel_id=1, source_target_pairs={{0,12},{4,8},{8,4},{12,0},{1,13},{5,9},{9,5},{13,1},{2,14},{6,10},... | collective-permute-start | bytes 786440 | tf_op jit(solution)/shard_map/ppermute | solution.py:186
  33.2 0.0 copy-done.3
  33.2 0.0 copy-done.4
  33.2 1.2 %shard_map.56 = (bf16[1024,1024]{1,0:T(8,128)(2,1)S(1)}, f32[8,4,128]{2,1,0:T(4,128)S(1)}, f32[8,8,128]{2,1,0:T(8,128)S(1)}) custom-call(s32[1,4]{1,0:T(1,128)S(1)} %copy-done.2, s32[4,4]{1,0:T(4,128)S(1)} %copy-done.1, s32[1,16]{1,0:T(1,128)S(1)} %copy-done.3, s32[1,16]{1,0:T(1,128)S(1)} %copy-done.4, bf16[1024,1024]{1,0:T(8,128)(2,1)S(1)} %copy-done), custom_call_target="tpu_custom_call" | custom-call | tf_op jit(solution)/shard_map/pallas_call | solution.py:110
  34.4 1.1 %shard_map.58 = (f32[8,128]{1,0:T(8,128)S(1)}, f32[8,128]{1,0:T(8,128)S(1)}) custom-call(bf16[160,1024]{1,0:T(8,128)(2,1)S(1)} %collective-permute-done.7.arrived, bf16[1024,1024]{1,0:T(8,128)(2,1)S(1)} %get-tuple-element.33.units, f32[8,4,128]{2,1,0:T(4,128)S(1)} %get-tuple-element.34.live, f32[8,8,128]{2,1,0:T(8,128)S(1)} %get-tuple-element.35.mine, ...), custom_call_target="tpu_custom_call" | custom-call | tf_op jit(solution)/shard_map/pallas_call | solution.py:154
  35.6 1.0 %shard_map.59 = (f32[8,128]{1,0:T(8,128)S(1)}, f32[8,128]{1,0:T(8,128)S(1)}) custom-call(bf16[96,1024]{1,0:T(8,128)(2,1)S(1)} %collective-permute-done.6.arrived, bf16[1024,1024]{1,0:T(8,128)(2,1)S(1)} %get-tuple-element.33.units, f32[8,4,128]{2,1,0:T(4,128)S(1)} %get-tuple-element.34.live, f32[8,8,128]{2,1,0:T(8,128)S(1)} %get-tuple-element.35.mine, ...), custom_call_target="tpu_custom_call" | custom-call | tf_op jit(solution)/shard_map/pallas_call | solution.py:154
  36.6 1.2 %shard_map.60 = (f32[8,128]{1,0:T(8,128)S(1)}, f32[8,128]{1,0:T(8,128)S(1)}) custom-call(bf16[256,1024]{1,0:T(8,128)(2,1)S(1)} %collective-permute-done.5.arrived, bf16[1024,1024]{1,0:T(8,128)(2,1)S(1)} %get-tuple-element.33.units, f32[8,4,128]{2,1,0:T(4,128)S(1)} %get-tuple-element.34.live, f32[8,8,128]{2,1,0:T(8,128)S(1)} %get-tuple-element.35.mine, ...), custom_call_target="tpu_custom_call" | custom-call | tf_op jit(solution)/shard_map/pallas_call | solution.py:154
  37.8 0.0 collective-permute-done.4.arrived
  37.8 0.2 collective-permute-start.8
  38.0 1.2 %shard_map.61 = (f32[8,128]{1,0:T(8,128)S(1)}, f32[8,128]{1,0:T(8,128)S(1)}) custom-call(bf16[256,1024]{1,0:T(8,128)(2,1)S(1)} %collective-permute-done.4.arrived, bf16[1024,1024]{1,0:T(8,128)(2,1)S(1)} %get-tuple-element.33.units, f32[8,4,128]{2,1,0:T(4,128)S(1)} %get-tuple-element.34.live, f32[8,8,128]{2,1,0:T(8,128)S(1)} %get-tuple-element.35.mine, ...), custom_call_target="tpu_custom_call" | custom-call | tf_op jit(solution)/shard_map/pallas_call | solution.py:154
  39.2 5.5 %collective-permute-done.3.arrived = bf16[256,1024]{1,0:T(8,128)(2,1)S(1)} collective-permute-done((bf16[256,1024]{1,0:T(8,128)(2,1)S(1)}, bf16[256,1024]{1,0:T(8,128)(2,1)S(1)}, u32[]{:S(2)}, u32[]{:S(2)}) %collective-permute-start.3) | collective-permute-done | bytes 524320 | tf_op jit(solution)/shard_map/ppermute | solution.py:186
  44.7 0.6 collective-permute-start.9
  45.2 0.0 collective-permute-done.8.rest_0_
  45.2 2.7 %collective-permute-start.11 = (f32[8,128]{1,0:T(8,128)S(1)}, f32[8,128]{1,0:T(8,128)S(1)}, u32[]{:S(2)}, u32[]{:S(2)}) collective-permute-start(f32[8,128]{1,0:T(8,128)S(1)} %get-tuple-element.55), channel_id=1, source_target_pairs={{0,2},{1,3},{2,0},{3,1},{4,6},{5,7},{6,4},{7,5},{8,10},{9,11},{10,... | collective-permute-start | bytes 12296 | tf_op jit(solution)/shard_map/ppermute | solution.py:186
  48.0 1.2 %shard_map.62 = (f32[8,128]{1,0:T(8,128)S(1)}, f32[8,128]{1,0:T(8,128)S(1)}) custom-call(bf16[256,1024]{1,0:T(8,128)(2,1)S(1)} %collective-permute-done.3.arrived, bf16[1024,1024]{1,0:T(8,128)(2,1)S(1)} %get-tuple-element.33.units, f32[8,4,128]{2,1,0:T(4,128)S(1)} %get-tuple-element.34.live, f32[8,8,128]{2,1,0:T(8,128)S(1)} %get-tuple-element.35.mine, ...), custom_call_target="tpu_custom_call" | custom-call | tf_op jit(solution)/shard_map/pallas_call | solution.py:154
  49.2 0.0 collective-permute-done.2.arrived
  49.2 0.0 collective-permute-done.9.rest_0_
  49.2 1.1 %shard_map.63 = (f32[8,128]{1,0:T(8,128)S(1)}, f32[8,128]{1,0:T(8,128)S(1)}) custom-call(bf16[128,1024]{1,0:T(8,128)(2,1)S(1)} %collective-permute-done.2.arrived, bf16[1024,1024]{1,0:T(8,128)(2,1)S(1)} %get-tuple-element.33.units, f32[8,4,128]{2,1,0:T(4,128)S(1)} %get-tuple-element.34.live, f32[8,8,128]{2,1,0:T(8,128)S(1)} %get-tuple-element.35.mine, ...), custom_call_target="tpu_custom_call" | custom-call | tf_op jit(solution)/shard_map/pallas_call | solution.py:154
  50.3 0.0 collective-permute-done.1.arrived
  50.3 1.1 %shard_map.64 = (f32[8,128]{1,0:T(8,128)S(1)}, f32[8,128]{1,0:T(8,128)S(1)}) custom-call(bf16[128,1024]{1,0:T(8,128)(2,1)S(1)} %collective-permute-done.1.arrived, bf16[1024,1024]{1,0:T(8,128)(2,1)S(1)} %get-tuple-element.33.units, f32[8,4,128]{2,1,0:T(4,128)S(1)} %get-tuple-element.34.live, f32[8,8,128]{2,1,0:T(8,128)S(1)} %get-tuple-element.35.mine, ...), custom_call_target="tpu_custom_call" | custom-call | tf_op jit(solution)/shard_map/pallas_call | solution.py:154
  51.4 0.1 collective-permute-start.10
  51.4 2.5 %collective-permute-start.12 = (f32[8,128]{1,0:T(8,128)S(1)}, f32[8,128]{1,0:T(8,128)S(1)}, u32[]{:S(2)}, u32[]{:S(2)}) collective-permute-start(f32[8,128]{1,0:T(8,128)S(1)} %get-tuple-element.56), channel_id=1, source_target_pairs={{0,1},{1,0},{2,3},{3,2},{4,5},{5,4},{6,7},{7,6},{8,9},{9,8},{10,11... | collective-permute-start | bytes 12296 | tf_op jit(solution)/shard_map/ppermute | solution.py:186
  54.0 0.0 collective-permute-done.11.rest_1_
  54.0 0.0 collective-permute-done.arrived
  54.0 0.5 collective-permute-done.10.rest_0_
  54.5 1.1 %collective-permute-done.12.rest_2_ = f32[8,128]{1,0:T(8,128)S(1)} collective-permute-done((f32[8,128]{1,0:T(8,128)S(1)}, f32[8,128]{1,0:T(8,128)S(1)}, u32[]{:S(2)}, u32[]{:S(2)}) %collective-permute-start.12) | collective-permute-done | bytes 4128 | tf_op jit(solution)/shard_map/ppermute | solution.py:186
  55.6 1.2 %shard_map.65 = (f32[8,128]{1,0:T(8,128)S(1)}, f32[8,128]{1,0:T(8,128)S(1)}) custom-call(bf16[256,1024]{1,0:T(8,128)(2,1)S(1)} %collective-permute-done.arrived, bf16[1024,1024]{1,0:T(8,128)(2,1)S(1)} %get-tuple-element.33.units, f32[8,4,128]{2,1,0:T(4,128)S(1)} %get-tuple-element.34.live, f32[8,8,128]{2,1,0:T(8,128)S(1)} %get-tuple-element.35.mine, ...), custom_call_target="tpu_custom_call" | custom-call | tf_op jit(solution)/shard_map/pallas_call | solution.py:154
  56.7 3.4 %collective-permute-start.13 = (f32[8,128]{1,0:T(8,128)S(1)}, f32[8,128]{1,0:T(8,128)S(1)}, u32[]{:S(2)}, u32[]{:S(2)}) collective-permute-start(f32[8,128]{1,0:T(8,128)S(1)} %get-tuple-element.58), channel_id=1, source_target_pairs={{0,3},{1,2},{2,1},{3,0},{4,7},{5,6},{6,5},{7,4},{8,11},{9,10},{10,... | collective-permute-start | bytes 12296 | tf_op jit(solution)/shard_map/ppermute | solution.py:186
  60.1 2.1 %collective-permute-done.13 = f32[8,128]{1,0:T(8,128)S(1)} collective-permute-done((f32[8,128]{1,0:T(8,128)S(1)}, f32[8,128]{1,0:T(8,128)S(1)}, u32[]{:S(2)}, u32[]{:S(2)}) %collective-permute-start.13) | collective-permute-done | bytes 4128 | tf_op jit(solution)/shard_map/ppermute | solution.py:186
  62.2 0.6 fusion.2
  (3 shorter events, 0.0 us)
Async XLA Ops:
  0.0 7.3 %copy-start = (bf16[1024,1024]{1,0:T(8,128)(2,1)S(1)}, bf16[1024,1024]{1,0:T(8,128)(2,1)}, u32[]{:S(2)}) copy-start(bf16[1024,1024]{1,0:T(8,128)(2,1)} %embeds.5) | copy-start | bytes 6291460
  0.0 7.3 %copy-start.2 = (s32[1,4]{1,0:T(1,128)S(1)}, s32[1,4]{1,0:T(1,128)}, u32[]{:S(2)}) copy-start(s32[1,4]{1,0:T(1,128)} %pick_blk.5) | copy-start | bytes 52
  0.0 7.3 %copy-start.1 = (s32[4,4]{1,0:T(4,128)S(1)}, s32[4,4]{1,0:T(4,128)}, u32[]{:S(2)}) copy-start(s32[4,4]{1,0:T(4,128)} %pick_sub.5) | copy-start | bytes 196
  0.0 33.2 %copy-start.3 = (s32[1,16]{1,0:T(1,128)S(1)}, s32[1,16]{1,0:T(1,128)}, u32[]{:S(2)}) copy-start(s32[1,16]{1,0:T(1,128)} %mask_blk.1) | copy-start | bytes 196
  0.0 33.2 %copy-start.4 = (s32[1,16]{1,0:T(1,128)S(1)}, s32[1,16]{1,0:T(1,128)}, u32[]{:S(2)}) copy-start(s32[1,16]{1,0:T(1,128)} %mask_sub.1) | copy-start | bytes 196
  3.0 29.0 %collective-permute-start.5 = (bf16[256,1024]{1,0:T(8,128)(2,1)}, bf16[256,1024]{1,0:T(8,128)(2,1)S(1)}, u32[]{:S(2)}, u32[]{:S(2)}) collective-permute-start(bf16[256,1024]{1,0:T(8,128)(2,1)} %get-tuple-element.40), channel_id=1, source_target_pairs={{0,4},{4,0},{8,12},{12,8},{1,5},{5,1},{9,13},{13,9},{2,6},{6,2},{1... | collective-permute-start | bytes 1572872 | tf_op jit(solution)/shard_map/ppermute | solution.py:186
  3.5 21.0 %collective-permute-start.6 = (bf16[96,1024]{1,0:T(8,128)(2,1)}, bf16[96,1024]{1,0:T(8,128)(2,1)S(1)}, u32[]{:S(2)}, u32[]{:S(2)}) collective-permute-start(bf16[96,1024]{1,0:T(8,128)(2,1)} %get-tuple-element.41), channel_id=1, source_target_pairs={{0,2},{1,3},{2,0},{3,1},{4,6},{5,7},{6,4},{7,5},{8,10},{9,11},{10,... | collective-permute-start | bytes 589832 | tf_op jit(solution)/shard_map/ppermute | solution.py:186
  7.2 24.3 %collective-permute-start.7 = (bf16[160,1024]{1,0:T(8,128)(2,1)}, bf16[160,1024]{1,0:T(8,128)(2,1)S(1)}, u32[]{:S(2)}, u32[]{:S(2)}) collective-permute-start(bf16[160,1024]{1,0:T(8,128)(2,1)} %get-tuple-element.42), channel_id=1, source_target_pairs={{0,2},{1,3},{2,0},{3,1},{4,6},{5,7},{6,4},{7,5},{8,10},{9,11},{10,... | collective-permute-start | bytes 983048 | tf_op jit(solution)/shard_map/ppermute | solution.py:186
  8.2 29.6 %collective-permute-start.4 = (bf16[256,1024]{1,0:T(8,128)(2,1)S(1)}, bf16[256,1024]{1,0:T(8,128)(2,1)S(1)}, u32[]{:S(2)}, u32[]{:S(2)}) collective-permute-start(bf16[256,1024]{1,0:T(8,128)(2,1)S(1)} %get-tuple-element.39), channel_id=1, source_target_pairs={{0,8},{4,12},{8,0},{12,4},{1,9},{5,13},{9,1},{13,5},{2,10},{6,14},... | collective-permute-start | bytes 1572872 | tf_op jit(solution)/shard_map/ppermute | solution.py:186
  10.0 34.7 %collective-permute-start.3 = (bf16[256,1024]{1,0:T(8,128)(2,1)S(1)}, bf16[256,1024]{1,0:T(8,128)(2,1)S(1)}, u32[]{:S(2)}, u32[]{:S(2)}) collective-permute-start(bf16[256,1024]{1,0:T(8,128)(2,1)S(1)} %get-tuple-element.38), channel_id=1, source_target_pairs={{0,1},{1,0},{2,3},{3,2},{4,5},{5,4},{6,7},{7,6},{8,9},{9,8},{10,11... | collective-permute-start | bytes 1572872 | tf_op jit(solution)/shard_map/ppermute | solution.py:186
  24.5 29.5 %collective-permute-start = (bf16[256,1024]{1,0:T(8,128)(2,1)S(1)}, bf16[256,1024]{1,0:T(8,128)(2,1)S(1)}, u32[]{:S(2)}, u32[]{:S(2)}) collective-permute-start(bf16[256,1024]{1,0:T(8,128)(2,1)S(1)} %get-tuple-element.32), channel_id=1, source_target_pairs={{0,3},{1,2},{2,1},{3,0},{4,7},{5,6},{6,5},{7,4},{8,11},{9,10},{10,... | collective-permute-start | bytes 1572872 | tf_op jit(solution)/shard_map/ppermute | solution.py:186
  31.4 17.7 %collective-permute-start.2 = (bf16[128,1024]{1,0:T(8,128)(2,1)S(1)}, bf16[128,1024]{1,0:T(8,128)(2,1)S(1)}, u32[]{:S(2)}, u32[]{:S(2)}) collective-permute-start(bf16[128,1024]{1,0:T(8,128)(2,1)S(1)} %get-tuple-element.37), channel_id=1, source_target_pairs={{0,12},{4,8},{8,4},{12,0},{1,13},{5,9},{9,5},{13,1},{2,14},{6,10},... | collective-permute-start | bytes 786440 | tf_op jit(solution)/shard_map/ppermute | solution.py:186
  32.0 18.3 %collective-permute-start.1 = (bf16[128,1024]{1,0:T(8,128)(2,1)S(1)}, bf16[128,1024]{1,0:T(8,128)(2,1)S(1)}, u32[]{:S(2)}, u32[]{:S(2)}) collective-permute-start(bf16[128,1024]{1,0:T(8,128)(2,1)S(1)} %get-tuple-element.36), channel_id=1, source_target_pairs={{0,12},{4,8},{8,4},{12,0},{1,13},{5,9},{9,5},{13,1},{2,14},{6,10},... | collective-permute-start | bytes 786440 | tf_op jit(solution)/shard_map/ppermute | solution.py:186
  37.8 7.5 %collective-permute-start.8 = (f32[8,128]{1,0:T(8,128)S(1)}, f32[8,128]{1,0:T(8,128)S(1)}, u32[]{:S(2)}, u32[]{:S(2)}) collective-permute-start(f32[8,128]{1,0:T(8,128)S(1)} %get-tuple-element.48), channel_id=1, source_target_pairs={{0,4},{4,0},{8,12},{12,8},{1,5},{5,1},{9,13},{13,9},{2,6},{6,2},{1... | collective-permute-start | bytes 12296 | tf_op jit(solution)/shard_map/ppermute | solution.py:186
  44.7 4.5 %collective-permute-start.9 = (f32[8,128]{1,0:T(8,128)S(1)}, f32[8,128]{1,0:T(8,128)S(1)}, u32[]{:S(2)}, u32[]{:S(2)}) collective-permute-start(f32[8,128]{1,0:T(8,128)S(1)} %get-tuple-element.50), channel_id=1, source_target_pairs={{0,8},{4,12},{8,0},{12,4},{1,9},{5,13},{9,1},{13,5},{2,10},{6,14},... | collective-permute-start | bytes 12296 | tf_op jit(solution)/shard_map/ppermute | solution.py:186
  45.2 8.7 %collective-permute-start.11 = (f32[8,128]{1,0:T(8,128)S(1)}, f32[8,128]{1,0:T(8,128)S(1)}, u32[]{:S(2)}, u32[]{:S(2)}) collective-permute-start(f32[8,128]{1,0:T(8,128)S(1)} %get-tuple-element.55), channel_id=1, source_target_pairs={{0,2},{1,3},{2,0},{3,1},{4,6},{5,7},{6,4},{7,5},{8,10},{9,11},{10,... | collective-permute-start | bytes 12296 | tf_op jit(solution)/shard_map/ppermute | solution.py:186
  51.4 3.1 %collective-permute-start.10 = (f32[8,128]{1,0:T(8,128)S(1)}, f32[8,128]{1,0:T(8,128)S(1)}, u32[]{:S(2)}, u32[]{:S(2)}) collective-permute-start(f32[8,128]{1,0:T(8,128)S(1)} %get-tuple-element.54), channel_id=1, source_target_pairs={{0,12},{4,8},{8,4},{12,0},{1,13},{5,9},{9,5},{13,1},{2,14},{6,10},... | collective-permute-start | bytes 12296 | tf_op jit(solution)/shard_map/ppermute | solution.py:186
  51.4 4.1 %collective-permute-start.12 = (f32[8,128]{1,0:T(8,128)S(1)}, f32[8,128]{1,0:T(8,128)S(1)}, u32[]{:S(2)}, u32[]{:S(2)}) collective-permute-start(f32[8,128]{1,0:T(8,128)S(1)} %get-tuple-element.56), channel_id=1, source_target_pairs={{0,1},{1,0},{2,3},{3,2},{4,5},{5,4},{6,7},{7,6},{8,9},{9,8},{10,11... | collective-permute-start | bytes 12296 | tf_op jit(solution)/shard_map/ppermute | solution.py:186
  56.7 5.5 %collective-permute-start.13 = (f32[8,128]{1,0:T(8,128)S(1)}, f32[8,128]{1,0:T(8,128)S(1)}, u32[]{:S(2)}, u32[]{:S(2)}) collective-permute-start(f32[8,128]{1,0:T(8,128)S(1)} %get-tuple-element.58), channel_id=1, source_target_pairs={{0,3},{1,2},{2,1},{3,0},{4,7},{5,6},{6,5},{7,4},{8,11},{9,10},{10,... | collective-permute-start | bytes 12296 | tf_op jit(solution)/shard_map/ppermute | solution.py:186

commit v8 on v7

--- a/solution.py
+++ b/solution.py
@@ -34,9 +34,7 @@
 
 def soft_weights(cosines):
     rate = sharpness * math.log2(math.e)
-    below = 1.0 + jnp.exp2(jnp.minimum(cutoff * rate - cosines * rate, 125.0))
-    guess = pl.reciprocal(below, approx=True)
-    return guess * (2.0 - below * guess)
+    return pltpu.reciprocal(1.0 + jnp.exp2(cutoff * rate - cosines * rate), approx=True)
 
 
 def take_pick(axis, step, pick_blk, pick_sub):
@@ -90,10 +88,14 @@
     )(pick_blk, pick_sub, embeds)
 
 
-def prepare_kernel(slots, pick_blk, pick_sub, mask_blk, mask_sub, embeds, units, live, mine):
-    for start in range(0, embeds.shape[0], BLOCK):
-        units[start : start + BLOCK] = rounded_units(embeds[start : start + BLOCK])
+def prepare_kernel(slots, pick_blk, pick_sub, mask_blk, mask_sub, embeds, units, live, mine, rows, sems):
     count = live.shape[1]
+    copies = [
+        pltpu.make_async_copy(embeds.at[pl.ds(i * BLOCK, BLOCK)], rows.at[pl.ds(i * BLOCK, BLOCK)], sems.at[i])
+        for i in range(count)
+    ]
+    for copy in copies:
+        copy.start()
     block_of = lax.broadcasted_iota(jnp.int32, mine.shape[1:], 0) // ROWS
     for place, (axis, step, _, _) in enumerate(slots):
         source = lax.axis_index(axis) ^ step
@@ -103,6 +105,9 @@
             live[place, i : i + 1] = jnp.full((1, LANES), value, jnp.float32)
         pick = take_pick(axis, step, pick_blk, pick_sub)
         mine[place] = (block_of == pick).astype(jnp.float32)
+    for i, copy in enumerate(copies):
+        copy.wait()
+        units[i * BLOCK : (i + 1) * BLOCK] = rounded_units(rows[i * BLOCK : (i + 1) * BLOCK])
 
 
 def prepare(slots, pick_blk, pick_sub, mask_blk, mask_sub, embeds):
@@ -114,9 +119,9 @@
             jax.ShapeDtypeStruct((len(slots), count, LANES), jnp.float32),
             jax.ShapeDtypeStruct((len(slots), count * ROWS, LANES), jnp.float32),
         ],
-        in_specs=[SMEM] * 4 + [VMEM],
+        in_specs=[SMEM] * 4 + [ANY],
         out_specs=[VMEM] * 3,
-        compiler_params=PARAMS,
+        scratch_shapes=[pltpu.VMEM(embeds.shape, embeds.dtype), pltpu.SemaphoreType.DMA((count,))],
     )(pick_blk, pick_sub, mask_blk, mask_sub, embeds)
 
 
@@ -134,11 +139,11 @@
         cosines = lax.dot_general(x, y, (((1,), (1,)), ((), ())), preferred_element_type=jnp.float32)
         weights = soft_weights(cosines)
         alive = live[place, i : i + 1]
-        for part in range(ROWS):
-            piece = alive * weights[:, part * LANES : (part + 1) * LANES]
-            along_rows = along_rows + piece
+        parts = [weights[:, part * LANES : (part + 1) * LANES] for part in range(ROWS)]
+        along_rows = along_rows + alive * sum(parts)
+        for part, piece in enumerate(parts):
             row = i * ROWS + part
-            new_totals[row : row + 1] = new_totals[row : row + 1] + jnp.sum(piece, axis=0, keepdims=True)
+            new_totals[row : row + 1] = new_totals[row : row + 1] + alive * jnp.sum(piece, axis=0, keepdims=True)
     empty = [jnp.zeros((gap, LANES), jnp.float32) for gap in (first, BLOCK - first - rows)]
     along_rows = jnp.concatenate([part for part in (empty[0], along_rows, empty[1]) if part.shape[0]], axis=0)
     for part in range(ROWS):
@@ -161,6 +166,17 @@
 
 
 BEHIND = 2
+EARLY_ROWS = 192
+HALF = BLOCK // 2
+
+
+def plan_slots(sizes):
+    slots = [("sub", 2, 0, EARLY_ROWS), ("sub", 2, EARLY_ROWS, BLOCK - EARLY_ROWS)]
+    slots += [("blk", 1, 0, BLOCK), ("blk", 2, 0, BLOCK)]
+    slots += [("blk", k, first, HALF) for k in range(3, sizes["blk"]) for first in (0, HALF)]
+    return slots + [("sub", k, 0, BLOCK) for k in (1, *range(3, sizes["sub"]))]
+
+
 EARLY_ROWS = 192
 HALF = BLOCK // 2
 

time: 63 us -> 64 us (1.016)
  waiting for transfers between devices: 25.8 us -> 20.4 us
  local copies, waits for them, and re-layouts: 0.02 us -> 3.07 us
  Pallas kernels: 14.1 us -> 16.8 us
    ppermute x14, waiting for transfers between devices: 25.8 us -> 20.4 us  [send(): return lax.ppermute(array, slot[0], pairs(slot[1], sizes[slot[0]]))]
    unnamed x10 -> x12, local copies, waits for them, and re-layouts: 0.02 us -> 3.07 us
    pallas_call x1, Pallas kernels: 1.23 us -> 3.9 us  [prepare(): pl.pallas_call(functools.partial(prepare_kernel, slots), out_shape=[jax.S...]
    pallas_call x2, Pallas kernels: 3.82 us -> 5.06 us  [pick_rows(): pl.pallas_call(functools.partial(pick_kernel, pieces), out_shape=[jax.Sha...]
    pallas_call x8, Pallas kernels: 9.03 us -> 7.84 us  [work(): pl.pallas_call(functools.partial(slot_kernel, place, *slot[2:], [one for...]
  transfers between devices with their start and end apart: 14 -> 14, of which waited for: 6 -> 6; matrix products, arithmetic and copies ran while one was open for 0% -> 0% of each run, Pallas kernels for 16% -> 20%
where the time goes in v8:
time: 64 us; the launch traced here: 63.7 us
  starting transfers between devices  22.6 us (35%)
  waiting for transfers between devices  20.4 us (32%)
  Pallas kernels  16.8 us (26%)
  local copies, waits for them, and re-layouts  3.07 us (5%)
    ppermute x14, starting transfers between devices, send(): return lax.ppermute(array, slot[0], pairs(slot[1], sizes[slot[0]]))  22.6 us
    ppermute x14, waiting for transfers between devices, send(): return lax.ppermute(array, slot[0], pairs(slot[1], sizes[slot[0]]))  20.4 us
    pallas_call x8, Pallas kernels, work(): pl.pallas_call(functools.partial(slot_kernel, place, *slot[2:], [one for...  7.84 us
    pallas_call x2, Pallas kernels, pick_rows(): pl.pallas_call(functools.partial(pick_kernel, pieces), out_shape=[jax.Sha...  5.06 us
    pallas_call x1, Pallas kernels, prepare(): pl.pallas_call(functools.partial(prepare_kernel, slots), out_shape=[jax.S...  3.9 us
    unnamed x12, local copies, waits for them, and re-layouts  3.07 us
  transfers between devices with their start and end apart: 14, of which 6 were waited for; matrix products, arithmetic and copies ran while one was open for 0% of the time, Pallas kernels for 20%

profile of v8, /device:TPU:0, one launch (start us, length us, event | category | flops | bytes accessed | tf_op | source)
XLA Modules:
  0.0 63.7 jit_solution(1497353817104397530)
XLA Ops:
  0.0 0.0 copy-start.1
  0.0 3.0 %shard_map.57 = (bf16[160,1024]{1,0:T(8,128)(2,1)}, bf16[96,1024]{1,0:T(8,128)(2,1)}, bf16[256,1024]{1,0:T(8,128)(2,1)}) custom-call(s32[1,4]{1,0:T(1,128)} %pick_blk.5, s32[4,4]{1,0:T(4,128)} %pick_sub.5, bf16[1024,1024]{1,0:T(8,128)(2,1)} %embeds.5), custom_call_target="tpu_custom_call" | custom-call | tf_op jit(solution)/shard_map/pallas_call | solution.py:74
  3.0 0.5 collective-permute-start.5
  3.5 3.7 %collective-permute-start.6 = (bf16[96,1024]{1,0:T(8,128)(2,1)}, bf16[96,1024]{1,0:T(8,128)(2,1)S(1)}, u32[]{:S(2)}, u32[]{:S(2)}) collective-permute-start(bf16[96,1024]{1,0:T(8,128)(2,1)} %get-tuple-element.41), channel_id=1, source_target_pairs={{0,2},{1,3},{2,0},{3,1},{4,6},{5,7},{6,4},{7,5},{8,10},{9,11},{10,... | collective-permute-start | bytes 589832 | tf_op jit(solution)/shard_map/ppermute | solution.py:202
  7.2 0.1 collective-permute-start.7
  7.3 0.0 copy-done.1
  7.3 0.0 copy-done.5
  7.3 0.0 copy-done.4
  7.3 2.1 %shard_map.55 = (bf16[256,1024]{1,0:T(8,128)(2,1)}, bf16[256,1024]{1,0:T(8,128)(2,1)}, bf16[128,1024]{1,0:T(8,128)(2,1)}, bf16[128,1024]{1,0:T(8,128)(2,1)S(1)}, bf16[256,1024]{1,0:T(8,128)(2,1)}) custom-call(s32[1,4]{1,0:T(1,128)S(1)} %copy-done.5, s32[4,4]{1,0:T(4,128)S(1)} %copy-done.4, bf16[1024,1024]{1,0:T(8,128)(2,1)S(1)} %copy-done.1), custom_call_target="tpu_custom_call" | custom-call | tf_op jit(solution)/shard_map/pallas_call | solution.py:74
  9.4 1.8 %collective-permute-start.4 = (bf16[256,1024]{1,0:T(8,128)(2,1)}, bf16[256,1024]{1,0:T(8,128)(2,1)S(1)}, u32[]{:S(2)}, u32[]{:S(2)}) collective-permute-start(bf16[256,1024]{1,0:T(8,128)(2,1)} %get-tuple-element.39), channel_id=1, source_target_pairs={{0,8},{4,12},{8,0},{12,4},{1,9},{5,13},{9,1},{13,5},{2,10},{6,14},... | collective-permute-start | bytes 1572872 | tf_op jit(solution)/shard_map/ppermute | solution.py:202
  11.2 1.8 %collective-permute-start.3 = (bf16[256,1024]{1,0:T(8,128)(2,1)}, bf16[256,1024]{1,0:T(8,128)(2,1)S(1)}, u32[]{:S(2)}, u32[]{:S(2)}) collective-permute-start(bf16[256,1024]{1,0:T(8,128)(2,1)} %get-tuple-element.38), channel_id=1, source_target_pairs={{0,1},{1,0},{2,3},{3,2},{4,5},{5,4},{6,7},{7,6},{8,9},{9,8},{10,11... | collective-permute-start | bytes 1572872 | tf_op jit(solution)/shard_map/ppermute | solution.py:202
  13.0 11.5 %collective-permute-done.6.arrived = bf16[96,1024]{1,0:T(8,128)(2,1)S(1)} collective-permute-done((bf16[96,1024]{1,0:T(8,128)(2,1)}, bf16[96,1024]{1,0:T(8,128)(2,1)S(1)}, u32[]{:S(2)}, u32[]{:S(2)}) %collective-permute-start.6) | collective-permute-done | bytes 196640 | tf_op jit(solution)/shard_map/ppermute | solution.py:202
  24.5 3.3 %collective-permute-start = (bf16[256,1024]{1,0:T(8,128)(2,1)}, bf16[256,1024]{1,0:T(8,128)(2,1)S(1)}, u32[]{:S(2)}, u32[]{:S(2)}) collective-permute-start(bf16[256,1024]{1,0:T(8,128)(2,1)} %get-tuple-element.32), channel_id=1, source_target_pairs={{0,3},{1,2},{2,1},{3,0},{4,7},{5,6},{6,5},{7,4},{8,11},{9,10},{10,... | collective-permute-start | bytes 1572872 | tf_op jit(solution)/shard_map/ppermute | solution.py:202
  27.8 3.6 %collective-permute-done.7.arrived = bf16[160,1024]{1,0:T(8,128)(2,1)S(1)} collective-permute-done((bf16[160,1024]{1,0:T(8,128)(2,1)}, bf16[160,1024]{1,0:T(8,128)(2,1)S(1)}, u32[]{:S(2)}, u32[]{:S(2)}) %collective-permute-start.7) | collective-permute-done | bytes 327712 | tf_op jit(solution)/shard_map/ppermute | solution.py:202
  31.4 0.6 collective-permute-start.2
  32.0 0.0 collective-permute-done.5.arrived
  32.0 1.2 %collective-permute-start.1 = (bf16[128,1024]{1,0:T(8,128)(2,1)S(1)}, bf16[128,1024]{1,0:T(8,128)(2,1)S(1)}, u32[]{:S(2)}, u32[]{:S(2)}) collective-permute-start(bf16[128,1024]{1,0:T(8,128)(2,1)S(1)} %get-tuple-element.36), channel_id=1, source_target_pairs={{0,12},{4,8},{8,4},{12,0},{1,13},{5,9},{9,5},{13,1},{2,14},{6,10},... | collective-permute-start | bytes 786440 | tf_op jit(solution)/shard_map/ppermute | solution.py:202
  33.2 3.9 %shard_map.56 = (bf16[1024,1024]{1,0:T(8,128)(2,1)}, f32[8,4,128]{2,1,0:T(4,128)}, f32[8,8,128]{2,1,0:T(8,128)}) custom-call(s32[1,4]{1,0:T(1,128)} %pick_blk.5, s32[4,4]{1,0:T(4,128)} %pick_sub.5, s32[1,16]{1,0:T(1,128)} %mask_blk.1, s32[1,16]{1,0:T(1,128)} %mask_sub.1, bf16[1024,1024]{1,0:T(8,128)(2,1)} %embeds.5), custom_call_target="tpu_custom_call" | custom-call | tf_op jit(solution)/shard_map/pallas_call | solution.py:115
  37.1 0.0 copy-start
  37.1 1.6 %copy-done = bf16[1024,1024]{1,0:T(8,128)(2,1)S(1)} copy-done((bf16[1024,1024]{1,0:T(8,128)(2,1)S(1)}, bf16[1024,1024]{1,0:T(8,128)(2,1)}, u32[]{:S(2)}) %copy-start) | copy-done | bytes 2097176
  38.7 0.8 %copy-done.2 = f32[8,8,128]{2,1,0:T(8,128)S(1)} copy-done((f32[8,8,128]{2,1,0:T(8,128)S(1)}, f32[8,8,128]{2,1,0:T(8,128)}, u32[]{:S(2)}) %copy-start.2) | copy-done | bytes 32792
  39.5 0.7 %copy-done.3 = f32[8,4,128]{2,1,0:T(4,128)S(1)} copy-done((f32[8,4,128]{2,1,0:T(4,128)S(1)}, f32[8,4,128]{2,1,0:T(4,128)}, u32[]{:S(2)}) %copy-start.3) | copy-done | bytes 16408
  40.2 1.0 %shard_map.58 = (f32[8,128]{1,0:T(8,128)S(1)}, f32[8,128]{1,0:T(8,128)S(1)}) custom-call(bf16[160,1024]{1,0:T(8,128)(2,1)S(1)} %collective-permute-done.7.arrived, bf16[1024,1024]{1,0:T(8,128)(2,1)S(1)} %copy-done, f32[8,4,128]{2,1,0:T(4,128)S(1)} %copy-done.3, f32[8,8,128]{2,1,0:T(8,128)S(1)} %copy-done.2, f32[8,128]{1,0:T(8,128)S(1)} %broadcast_in_dim.3.totals), custom_call_target="tpu_custom_call" | custom-call | tf_op jit(solution)/shard_map/pallas_call | solution.py:159
  41.2 0.9 %shard_map.59 = (f32[8,128]{1,0:T(8,128)S(1)}, f32[8,128]{1,0:T(8,128)S(1)}) custom-call(bf16[96,1024]{1,0:T(8,128)(2,1)S(1)} %collective-permute-done.6.arrived, bf16[1024,1024]{1,0:T(8,128)(2,1)S(1)} %copy-done, f32[8,4,128]{2,1,0:T(4,128)S(1)} %copy-done.3, f32[8,8,128]{2,1,0:T(8,128)S(1)} %copy-done.2, f32[8,128]{1,0:T(8,128)S(1)} %get-tuple-element.43.totals, ...), custom_call_target="tpu_custom_call" | custom-call | tf_op jit(solution)/shard_map/pallas_call | solution.py:159
  42.1 1.0 %shard_map.60 = (f32[8,128]{1,0:T(8,128)S(1)}, f32[8,128]{1,0:T(8,128)S(1)}) custom-call(bf16[256,1024]{1,0:T(8,128)(2,1)S(1)} %collective-permute-done.5.arrived, bf16[1024,1024]{1,0:T(8,128)(2,1)S(1)} %copy-done, f32[8,4,128]{2,1,0:T(4,128)S(1)} %copy-done.3, f32[8,8,128]{2,1,0:T(8,128)S(1)} %copy-done.2, f32[8,128]{1,0:T(8,128)S(1)} %get-tuple-element.45.totals), custom_call_target="tpu_custom_call" | custom-call | tf_op jit(solution)/shard_map/pallas_call | solution.py:159
  43.1 0.0 collective-permute-done.4.arrived
  43.1 0.2 collective-permute-start.8
  43.4 1.0 %shard_map.61 = (f32[8,128]{1,0:T(8,128)S(1)}, f32[8,128]{1,0:T(8,128)S(1)}) custom-call(bf16[256,1024]{1,0:T(8,128)(2,1)S(1)} %collective-permute-done.4.arrived, bf16[1024,1024]{1,0:T(8,128)(2,1)S(1)} %copy-done, f32[8,4,128]{2,1,0:T(4,128)S(1)} %copy-done.3, f32[8,8,128]{2,1,0:T(8,128)S(1)} %copy-done.2, f32[8,128]{1,0:T(8,128)S(1)} %get-tuple-element.46.totals), custom_call_target="tpu_custom_call" | custom-call | tf_op jit(solution)/shard_map/pallas_call | solution.py:159
  44.4 1.8 %collective-permute-done.3.arrived = bf16[256,1024]{1,0:T(8,128)(2,1)S(1)} collective-permute-done((bf16[256,1024]{1,0:T(8,128)(2,1)}, bf16[256,1024]{1,0:T(8,128)(2,1)S(1)}, u32[]{:S(2)}, u32[]{:S(2)}) %collective-permute-start.3) | collective-permute-done | bytes 524320 | tf_op jit(solution)/shard_map/ppermute | solution.py:202
  46.2 0.3 collective-permute-start.9
  46.5 0.0 collective-permute-done.8.rest_0_
  46.5 3.1 %collective-permute-start.11 = (f32[8,128]{1,0:T(8,128)S(1)}, f32[8,128]{1,0:T(8,128)S(1)}, u32[]{:S(2)}, u32[]{:S(2)}) collective-permute-start(f32[8,128]{1,0:T(8,128)S(1)} %get-tuple-element.55), channel_id=1, source_target_pairs={{0,2},{1,3},{2,0},{3,1},{4,6},{5,7},{6,4},{7,5},{8,10},{9,11},{10,... | collective-permute-start | bytes 12296 | tf_op jit(solution)/shard_map/ppermute | solution.py:202
  49.5 1.0 %shard_map.62 = (f32[8,128]{1,0:T(8,128)S(1)}, f32[8,128]{1,0:T(8,128)S(1)}) custom-call(bf16[256,1024]{1,0:T(8,128)(2,1)S(1)} %collective-permute-done.3.arrived, bf16[1024,1024]{1,0:T(8,128)(2,1)S(1)} %copy-done, f32[8,4,128]{2,1,0:T(4,128)S(1)} %copy-done.3, f32[8,8,128]{2,1,0:T(8,128)S(1)} %copy-done.2, f32[8,128]{1,0:T(8,128)S(1)} %get-tuple-element.47.totals, ...), custom_call_target="tpu_custom_call" | custom-call | tf_op jit(solution)/shard_map/pallas_call | solution.py:159
  50.5 0.0 collective-permute-done.2.arrived
  50.5 0.0 collective-permute-done.9.rest_0_
  50.5 1.0 %shard_map.63 = (f32[8,128]{1,0:T(8,128)S(1)}, f32[8,128]{1,0:T(8,128)S(1)}) custom-call(bf16[128,1024]{1,0:T(8,128)(2,1)S(1)} %collective-permute-done.2.arrived, bf16[1024,1024]{1,0:T(8,128)(2,1)S(1)} %copy-done, f32[8,4,128]{2,1,0:T(4,128)S(1)} %copy-done.3, f32[8,8,128]{2,1,0:T(8,128)S(1)} %copy-done.2, f32[8,128]{1,0:T(8,128)S(1)} %get-tuple-element.49.totals, ...), custom_call_target="tpu_custom_call" | custom-call | tf_op jit(solution)/shard_map/pallas_call | solution.py:159
  51.5 0.0 collective-permute-done.1.arrived
  51.5 1.0 %shard_map.64 = (f32[8,128]{1,0:T(8,128)S(1)}, f32[8,128]{1,0:T(8,128)S(1)}) custom-call(bf16[128,1024]{1,0:T(8,128)(2,1)S(1)} %collective-permute-done.1.arrived, bf16[1024,1024]{1,0:T(8,128)(2,1)S(1)} %copy-done, f32[8,4,128]{2,1,0:T(4,128)S(1)} %copy-done.3, f32[8,8,128]{2,1,0:T(8,128)S(1)} %copy-done.2, f32[8,128]{1,0:T(8,128)S(1)} %get-tuple-element.51.totals, ...), custom_call_target="tpu_custom_call" | custom-call | tf_op jit(solution)/shard_map/pallas_call | solution.py:159
  52.5 0.1 collective-permute-start.10
  52.6 2.4 %collective-permute-start.12 = (f32[8,128]{1,0:T(8,128)S(1)}, f32[8,128]{1,0:T(8,128)S(1)}, u32[]{:S(2)}, u32[]{:S(2)}) collective-permute-start(f32[8,128]{1,0:T(8,128)S(1)} %get-tuple-element.56), channel_id=1, source_target_pairs={{0,1},{1,0},{2,3},{3,2},{4,5},{5,4},{6,7},{7,6},{8,9},{9,8},{10,11... | collective-permute-start | bytes 12296 | tf_op jit(solution)/shard_map/ppermute | solution.py:202
  55.0 0.0 collective-permute-done.11.rest_1_
  55.0 0.0 collective-permute-done.arrived
  55.0 0.6 collective-permute-done.10.rest_0_
  55.6 1.0 %collective-permute-done.12.rest_2_ = f32[8,128]{1,0:T(8,128)S(1)} collective-permute-done((f32[8,128]{1,0:T(8,128)S(1)}, f32[8,128]{1,0:T(8,128)S(1)}, u32[]{:S(2)}, u32[]{:S(2)}) %collective-permute-start.12) | collective-permute-done | bytes 4128 | tf_op jit(solution)/shard_map/ppermute | solution.py:202
  56.6 1.0 %shard_map.65 = (f32[8,128]{1,0:T(8,128)S(1)}, f32[8,128]{1,0:T(8,128)S(1)}) custom-call(bf16[256,1024]{1,0:T(8,128)(2,1)S(1)} %collective-permute-done.arrived, bf16[1024,1024]{1,0:T(8,128)(2,1)S(1)} %copy-done, f32[8,4,128]{2,1,0:T(4,128)S(1)} %copy-done.3, f32[8,8,128]{2,1,0:T(8,128)S(1)} %copy-done.2, f32[8,128]{1,0:T(8,128)S(1)} %get-tuple-element.53.totals, ...), custom_call_target="tpu_custom_call" | custom-call | tf_op jit(solution)/shard_map/pallas_call | solution.py:159
  57.6 3.6 %collective-permute-start.13 = (f32[8,128]{1,0:T(8,128)S(1)}, f32[8,128]{1,0:T(8,128)S(1)}, u32[]{:S(2)}, u32[]{:S(2)}) collective-permute-start(f32[8,128]{1,0:T(8,128)S(1)} %get-tuple-element.58), channel_id=1, source_target_pairs={{0,3},{1,2},{2,1},{3,0},{4,7},{5,6},{6,5},{7,4},{8,11},{9,10},{10,... | collective-permute-start | bytes 12296 | tf_op jit(solution)/shard_map/ppermute | solution.py:202
  61.2 1.9 %collective-permute-done.13 = f32[8,128]{1,0:T(8,128)S(1)} collective-permute-done((f32[8,128]{1,0:T(8,128)S(1)}, f32[8,128]{1,0:T(8,128)S(1)}, u32[]{:S(2)}, u32[]{:S(2)}) %collective-permute-start.13) | collective-permute-done | bytes 4128 | tf_op jit(solution)/shard_map/ppermute | solution.py:202
  63.1 0.6 fusion.2
  (5 shorter events, 0.0 us)
Async XLA Ops:
  0.0 7.3 %copy-start.1 = (bf16[1024,1024]{1,0:T(8,128)(2,1)S(1)}, bf16[1024,1024]{1,0:T(8,128)(2,1)}, u32[]{:S(2)}) copy-start(bf16[1024,1024]{1,0:T(8,128)(2,1)} %embeds.5) | copy-start | bytes 6291460
  0.0 7.3 %copy-start.5 = (s32[1,4]{1,0:T(1,128)S(1)}, s32[1,4]{1,0:T(1,128)}, u32[]{:S(2)}) copy-start(s32[1,4]{1,0:T(1,128)} %pick_blk.5) | copy-start | bytes 52
  0.0 7.3 %copy-start.4 = (s32[4,4]{1,0:T(4,128)S(1)}, s32[4,4]{1,0:T(4,128)}, u32[]{:S(2)}) copy-start(s32[4,4]{1,0:T(4,128)} %pick_sub.5) | copy-start | bytes 196
  3.0 29.0 %collective-permute-start.5 = (bf16[256,1024]{1,0:T(8,128)(2,1)}, bf16[256,1024]{1,0:T(8,128)(2,1)S(1)}, u32[]{:S(2)}, u32[]{:S(2)}) collective-permute-start(bf16[256,1024]{1,0:T(8,128)(2,1)} %get-tuple-element.40), channel_id=1, source_target_pairs={{0,4},{4,0},{8,12},{12,8},{1,5},{5,1},{9,13},{13,9},{2,6},{6,2},{1... | collective-permute-start | bytes 1572872 | tf_op jit(solution)/shard_map/ppermute | solution.py:202
  3.5 21.0 %collective-permute-start.6 = (bf16[96,1024]{1,0:T(8,128)(2,1)}, bf16[96,1024]{1,0:T(8,128)(2,1)S(1)}, u32[]{:S(2)}, u32[]{:S(2)}) collective-permute-start(bf16[96,1024]{1,0:T(8,128)(2,1)} %get-tuple-element.41), channel_id=1, source_target_pairs={{0,2},{1,3},{2,0},{3,1},{4,6},{5,7},{6,4},{7,5},{8,10},{9,11},{10,... | collective-permute-start | bytes 589832 | tf_op jit(solution)/shard_map/ppermute | solution.py:202
  7.2 24.3 %collective-permute-start.7 = (bf16[160,1024]{1,0:T(8,128)(2,1)}, bf16[160,1024]{1,0:T(8,128)(2,1)S(1)}, u32[]{:S(2)}, u32[]{:S(2)}) collective-permute-start(bf16[160,1024]{1,0:T(8,128)(2,1)} %get-tuple-element.42), channel_id=1, source_target_pairs={{0,2},{1,3},{2,0},{3,1},{4,6},{5,7},{6,4},{7,5},{8,10},{9,11},{10,... | collective-permute-start | bytes 983048 | tf_op jit(solution)/shard_map/ppermute | solution.py:202
  9.4 33.8 %collective-permute-start.4 = (bf16[256,1024]{1,0:T(8,128)(2,1)}, bf16[256,1024]{1,0:T(8,128)(2,1)S(1)}, u32[]{:S(2)}, u32[]{:S(2)}) collective-permute-start(bf16[256,1024]{1,0:T(8,128)(2,1)} %get-tuple-element.39), channel_id=1, source_target_pairs={{0,8},{4,12},{8,0},{12,4},{1,9},{5,13},{9,1},{13,5},{2,10},{6,14},... | collective-permute-start | bytes 1572872 | tf_op jit(solution)/shard_map/ppermute | solution.py:202
  11.2 35.0 %collective-permute-start.3 = (bf16[256,1024]{1,0:T(8,128)(2,1)}, bf16[256,1024]{1,0:T(8,128)(2,1)S(1)}, u32[]{:S(2)}, u32[]{:S(2)}) collective-permute-start(bf16[256,1024]{1,0:T(8,128)(2,1)} %get-tuple-element.38), channel_id=1, source_target_pairs={{0,1},{1,0},{2,3},{3,2},{4,5},{5,4},{6,7},{7,6},{8,9},{9,8},{10,11... | collective-permute-start | bytes 1572872 | tf_op jit(solution)/shard_map/ppermute | solution.py:202
  24.5 30.5 %collective-permute-start = (bf16[256,1024]{1,0:T(8,128)(2,1)}, bf16[256,1024]{1,0:T(8,128)(2,1)S(1)}, u32[]{:S(2)}, u32[]{:S(2)}) collective-permute-start(bf16[256,1024]{1,0:T(8,128)(2,1)} %get-tuple-element.32), channel_id=1, source_target_pairs={{0,3},{1,2},{2,1},{3,0},{4,7},{5,6},{6,5},{7,4},{8,11},{9,10},{10,... | collective-permute-start | bytes 1572872 | tf_op jit(solution)/shard_map/ppermute | solution.py:202
  31.4 19.1 %collective-permute-start.2 = (bf16[128,1024]{1,0:T(8,128)(2,1)}, bf16[128,1024]{1,0:T(8,128)(2,1)S(1)}, u32[]{:S(2)}, u32[]{:S(2)}) collective-permute-start(bf16[128,1024]{1,0:T(8,128)(2,1)} %get-tuple-element.37), channel_id=1, source_target_pairs={{0,12},{4,8},{8,4},{12,0},{1,13},{5,9},{9,5},{13,1},{2,14},{6,10},... | collective-permute-start | bytes 786440 | tf_op jit(solution)/shard_map/ppermute | solution.py:202
  32.0 19.5 %collective-permute-start.1 = (bf16[128,1024]{1,0:T(8,128)(2,1)S(1)}, bf16[128,1024]{1,0:T(8,128)(2,1)S(1)}, u32[]{:S(2)}, u32[]{:S(2)}) collective-permute-start(bf16[128,1024]{1,0:T(8,128)(2,1)S(1)} %get-tuple-element.36), channel_id=1, source_target_pairs={{0,12},{4,8},{8,4},{12,0},{1,13},{5,9},{9,5},{13,1},{2,14},{6,10},... | collective-permute-start | bytes 786440 | tf_op jit(solution)/shard_map/ppermute | solution.py:202
  37.1 1.6 %copy-start = (bf16[1024,1024]{1,0:T(8,128)(2,1)S(1)}, bf16[1024,1024]{1,0:T(8,128)(2,1)}, u32[]{:S(2)}) copy-start(bf16[1024,1024]{1,0:T(8,128)(2,1)} %get-tuple-element.33.units) | copy-start | bytes 6291460
  38.7 0.8 %copy-start.2 = (f32[8,8,128]{2,1,0:T(8,128)S(1)}, f32[8,8,128]{2,1,0:T(8,128)}, u32[]{:S(2)}) copy-start(f32[8,8,128]{2,1,0:T(8,128)} %get-tuple-element.35.mine) | copy-start | bytes 98308
  39.5 0.7 %copy-start.3 = (f32[8,4,128]{2,1,0:T(4,128)S(1)}, f32[8,4,128]{2,1,0:T(4,128)}, u32[]{:S(2)}) copy-start(f32[8,4,128]{2,1,0:T(4,128)} %get-tuple-element.34.live) | copy-start | bytes 49156
  43.1 3.3 %collective-permute-start.8 = (f32[8,128]{1,0:T(8,128)S(1)}, f32[8,128]{1,0:T(8,128)S(1)}, u32[]{:S(2)}, u32[]{:S(2)}) collective-permute-start(f32[8,128]{1,0:T(8,128)S(1)} %get-tuple-element.48), channel_id=1, source_target_pairs={{0,4},{4,0},{8,12},{12,8},{1,5},{5,1},{9,13},{13,9},{2,6},{6,2},{1... | collective-permute-start | bytes 12296 | tf_op jit(solution)/shard_map/ppermute | solution.py:202
  46.2 4.4 %collective-permute-start.9 = (f32[8,128]{1,0:T(8,128)S(1)}, f32[8,128]{1,0:T(8,128)S(1)}, u32[]{:S(2)}, u32[]{:S(2)}) collective-permute-start(f32[8,128]{1,0:T(8,128)S(1)} %get-tuple-element.50), channel_id=1, source_target_pairs={{0,8},{4,12},{8,0},{12,4},{1,9},{5,13},{9,1},{13,5},{2,10},{6,14},... | collective-permute-start | bytes 12296 | tf_op jit(solution)/shard_map/ppermute | solution.py:202
  46.5 8.6 %collective-permute-start.11 = (f32[8,128]{1,0:T(8,128)S(1)}, f32[8,128]{1,0:T(8,128)S(1)}, u32[]{:S(2)}, u32[]{:S(2)}) collective-permute-start(f32[8,128]{1,0:T(8,128)S(1)} %get-tuple-element.55), channel_id=1, source_target_pairs={{0,2},{1,3},{2,0},{3,1},{4,6},{5,7},{6,4},{7,5},{8,10},{9,11},{10,... | collective-permute-start | bytes 12296 | tf_op jit(solution)/shard_map/ppermute | solution.py:202
  52.5 3.1 %collective-permute-start.10 = (f32[8,128]{1,0:T(8,128)S(1)}, f32[8,128]{1,0:T(8,128)S(1)}, u32[]{:S(2)}, u32[]{:S(2)}) collective-permute-start(f32[8,128]{1,0:T(8,128)S(1)} %get-tuple-element.54), channel_id=1, source_target_pairs={{0,12},{4,8},{8,4},{12,0},{1,13},{5,9},{9,5},{13,1},{2,14},{6,10},... | collective-permute-start | bytes 12296 | tf_op jit(solution)/shard_map/ppermute | solution.py:202
  52.6 4.0 %collective-permute-start.12 = (f32[8,128]{1,0:T(8,128)S(1)}, f32[8,128]{1,0:T(8,128)S(1)}, u32[]{:S(2)}, u32[]{:S(2)}) collective-permute-start(f32[8,128]{1,0:T(8,128)S(1)} %get-tuple-element.56), channel_id=1, source_target_pairs={{0,1},{1,0},{2,3},{3,2},{4,5},{5,4},{6,7},{7,6},{8,9},{9,8},{10,11... | collective-permute-start | bytes 12296 | tf_op jit(solution)/shard_map/ppermute | solution.py:202
  57.6 5.5 %collective-permute-start.13 = (f32[8,128]{1,0:T(8,128)S(1)}, f32[8,128]{1,0:T(8,128)S(1)}, u32[]{:S(2)}, u32[]{:S(2)}) collective-permute-start(f32[8,128]{1,0:T(8,128)S(1)} %get-tuple-element.58), channel_id=1, source_target_pairs={{0,3},{1,2},{2,1},{3,0},{4,7},{5,6},{6,5},{7,4},{8,11},{9,10},{10,... | collective-permute-start | bytes 12296 | tf_op jit(solution)/shard_map/ppermute | solution.py:202

commit v9 on v7

--- a/solution.py
+++ b/solution.py
@@ -34,9 +34,7 @@
 
 def soft_weights(cosines):
     rate = sharpness * math.log2(math.e)
-    below = 1.0 + jnp.exp2(jnp.minimum(cutoff * rate - cosines * rate, 125.0))
-    guess = pl.reciprocal(below, approx=True)
-    return guess * (2.0 - below * guess)
+    return pltpu.reciprocal(1.0 + jnp.exp2(cutoff * rate - cosines * rate), approx=True)
 
 
 def take_pick(axis, step, pick_blk, pick_sub):
@@ -134,11 +132,11 @@
         cosines = lax.dot_general(x, y, (((1,), (1,)), ((), ())), preferred_element_type=jnp.float32)
         weights = soft_weights(cosines)
         alive = live[place, i : i + 1]
-        for part in range(ROWS):
-            piece = alive * weights[:, part * LANES : (part + 1) * LANES]
-            along_rows = along_rows + piece
+        parts = [weights[:, part * LANES : (part + 1) * LANES] for part in range(ROWS)]
+        along_rows = along_rows + alive * sum(parts)
+        for part, piece in enumerate(parts):
             row = i * ROWS + part
-            new_totals[row : row + 1] = new_totals[row : row + 1] + jnp.sum(piece, axis=0, keepdims=True)
+            new_totals[row : row + 1] = new_totals[row : row + 1] + alive * jnp.sum(piece, axis=0, keepdims=True)
     empty = [jnp.zeros((gap, LANES), jnp.float32) for gap in (first, BLOCK - first - rows)]
     along_rows = jnp.concatenate([part for part in (empty[0], along_rows, empty[1]) if part.shape[0]], axis=0)
     for part in range(ROWS):
@@ -165,16 +163,17 @@
 HALF = BLOCK // 2
 
 
+FIRST_CUT = 240
+
+
 def plan_slots(sizes):
-    slots = [("sub", 2, 0, EARLY_ROWS), ("sub", 2, EARLY_ROWS, BLOCK - EARLY_ROWS)]
-    slots += [("blk", 1, 0, BLOCK), ("blk", 2, 0, BLOCK), ("sub", 1, 0, BLOCK)]
-    slots += [("blk", k, first, HALF) for k in range(3, sizes["blk"]) for first in (0, HALF)]
-    return slots + [("sub", k, 0, BLOCK) for k in range(3, sizes["sub"])]
-
-
-EARLY_ROWS = 160
-HALF = BLOCK // 2
-AT_ONCE = 3
+    slots = [("blk", 1, 0, BLOCK), ("sub", 2, 0, BLOCK), ("blk", 2, 0, BLOCK)]
+    for k in range(3, sizes["blk"]):
+        slots += [("blk", k, 0, FIRST_CUT), ("blk", k, FIRST_CUT, BLOCK - FIRST_CUT)]
+    return slots + [("sub", k, 0, BLOCK) for k in (1, *range(3, sizes["sub"]))]
+
+
+AT_ONCE = 2
 
 
 def body(embeds, pick_blk, mask_blk, pick_sub, mask_sub):

time: 63 us -> 61.1 us (0.970)
  starting transfers between devices: 22.3 us -> 13.6 us
  waiting for transfers between devices: 25.8 us -> 34.4 us
  Pallas kernels: 14.1 us -> 12.2 us
    ppermute x14 -> x13, starting transfers between devices: 22.3 us -> 13.6 us  [send(): return lax.ppermute(array, slot[0], pairs(slot[1], sizes[slot[0]]))]
    ppermute x14 -> x13, waiting for transfers between devices: 25.8 us -> 34.4 us  [send(): return lax.ppermute(array, slot[0], pairs(slot[1], sizes[slot[0]]))]
    pallas_call x8 -> x7, Pallas kernels: 9.03 us -> 6.86 us  [work(): pl.pallas_call(functools.partial(slot_kernel, place, *slot[2:], [one for...]
  transfers between devices with their start and end apart: 14 -> 13, of which waited for: 6 -> 5; matrix products, arithmetic and copies ran while one was open for 0% -> 0% of each run, Pallas kernels for 16% -> 14%
where the time goes in v9:
time: 61.1 us; the launch traced here: 60.9 us
  waiting for transfers between devices  34.4 us (56%)
  starting transfers between devices  13.6 us (22%)
  Pallas kernels  12.2 us (20%)
    ppermute x13, waiting for transfers between devices, send(): return lax.ppermute(array, slot[0], pairs(slot[1], sizes[slot[0]]))  34.4 us
    ppermute x13, starting transfers between devices, send(): return lax.ppermute(array, slot[0], pairs(slot[1], sizes[slot[0]]))  13.6 us
    pallas_call x7, Pallas kernels, work(): pl.pallas_call(functools.partial(slot_kernel, place, *slot[2:], [one for...  6.86 us
    pallas_call x2, Pallas kernels, pick_rows(): pl.pallas_call(functools.partial(pick_kernel, pieces), out_shape=[jax.Sha...  4.13 us
    pallas_call x1, Pallas kernels, prepare(): pl.pallas_call(functools.partial(prepare_kernel, slots), out_shape=[jax.S...  1.23 us
  transfers between devices with their start and end apart: 13, of which 5 were waited for; matrix products, arithmetic and copies ran while one was open for 0% of the time, Pallas kernels for 14%

profile of v9, /device:TPU:0, one launch (start us, length us, event | category | flops | bytes accessed | tf_op | source)
XLA Modules:
  0.0 60.9 jit_solution(16172082746810616597)
XLA Ops:
  0.0 0.0 copy-start
  0.0 0.0 copy-start.2
  0.0 0.0 copy-start.1
  0.0 0.0 copy-start.3
  0.0 0.0 copy-start.4
  0.0 2.9 %shard_map.57 = (bf16[256,1024]{1,0:T(8,128)(2,1)}, bf16[256,1024]{1,0:T(8,128)(2,1)}) custom-call(s32[1,4]{1,0:T(1,128)} %pick_blk.5, s32[4,4]{1,0:T(4,128)} %pick_sub.5, bf16[1024,1024]{1,0:T(8,128)(2,1)} %embeds.5), custom_call_target="tpu_custom_call" | custom-call | tf_op jit(solution)/shard_map/pallas_call | solution.py:74
  3.0 0.5 collective-permute-start.6
  3.5 3.7 %collective-permute-start.5 = (bf16[256,1024]{1,0:T(8,128)(2,1)}, bf16[256,1024]{1,0:T(8,128)(2,1)S(1)}, u32[]{:S(2)}, u32[]{:S(2)}) collective-permute-start(bf16[256,1024]{1,0:T(8,128)(2,1)} %get-tuple-element.37), channel_id=1, source_target_pairs={{0,2},{1,3},{2,0},{3,1},{4,6},{5,7},{6,4},{7,5},{8,10},{9,11},{10,... | collective-permute-start | bytes 1572872 | tf_op jit(solution)/shard_map/ppermute | solution.py:185
  7.2 0.0 copy-done
  7.2 0.0 copy-done.2
  7.2 0.0 copy-done.1
  7.2 1.2 %shard_map.55 = (bf16[256,1024]{1,0:T(8,128)(2,1)S(1)}, bf16[240,1024]{1,0:T(8,128)(2,1)S(1)}, bf16[16,1024]{1,0:T(8,128)(2,1)S(1)}, bf16[256,1024]{1,0:T(8,128)(2,1)S(1)}, bf16[256,1024]{1,0:T(8,128)(2,1)S(1)}) custom-call(s32[1,4]{1,0:T(1,128)S(1)} %copy-done.2, s32[4,4]{1,0:T(4,128)S(1)} %copy-done.1, bf16[1024,1024]{1,0:T(8,128)(2,1)S(1)} %copy-done), custom_call_target="tpu_custom_call" | custom-call | tf_op jit(solution)/shard_map/pallas_call | solution.py:74
  8.4 1.6 %collective-permute-start.4 = (bf16[256,1024]{1,0:T(8,128)(2,1)S(1)}, bf16[256,1024]{1,0:T(8,128)(2,1)S(1)}, u32[]{:S(2)}, u32[]{:S(2)}) collective-permute-start(bf16[256,1024]{1,0:T(8,128)(2,1)S(1)} %get-tuple-element.36), channel_id=1, source_target_pairs={{0,8},{4,12},{8,0},{12,4},{1,9},{5,13},{9,1},{13,5},{2,10},{6,14},... | collective-permute-start | bytes 1572872 | tf_op jit(solution)/shard_map/ppermute | solution.py:185
  9.9 1.6 %collective-permute-start.1 = (bf16[256,1024]{1,0:T(8,128)(2,1)S(1)}, bf16[256,1024]{1,0:T(8,128)(2,1)S(1)}, u32[]{:S(2)}, u32[]{:S(2)}) collective-permute-start(bf16[256,1024]{1,0:T(8,128)(2,1)S(1)} %get-tuple-element.33), channel_id=1, source_target_pairs={{0,1},{1,0},{2,3},{3,2},{4,5},{5,4},{6,7},{7,6},{8,9},{9,8},{10,11... | collective-permute-start | bytes 1572872 | tf_op jit(solution)/shard_map/ppermute | solution.py:185
  11.5 0.2 collective-permute-start
  11.7 0.0 collective-permute-done.6.arrived
  11.7 0.0 collective-permute-start.3
  11.7 19.7 %collective-permute-done.5.arrived = bf16[256,1024]{1,0:T(8,128)(2,1)S(1)} collective-permute-done((bf16[256,1024]{1,0:T(8,128)(2,1)}, bf16[256,1024]{1,0:T(8,128)(2,1)S(1)}, u32[]{:S(2)}, u32[]{:S(2)}) %collective-permute-start.5) | collective-permute-done | bytes 524320 | tf_op jit(solution)/shard_map/ppermute | solution.py:185
  31.4 0.6 collective-permute-start.2
  32.0 0.0 copy-done.3
  32.0 0.0 copy-done.4
  32.0 1.2 %shard_map.56 = (bf16[1024,1024]{1,0:T(8,128)(2,1)S(1)}, f32[7,4,128]{2,1,0:T(4,128)S(1)}, f32[7,8,128]{2,1,0:T(8,128)S(1)}) custom-call(s32[1,4]{1,0:T(1,128)S(1)} %copy-done.2, s32[4,4]{1,0:T(4,128)S(1)} %copy-done.1, s32[1,16]{1,0:T(1,128)S(1)} %copy-done.3, s32[1,16]{1,0:T(1,128)S(1)} %copy-done.4, bf16[1024,1024]{1,0:T(8,128)(2,1)S(1)} %copy-done), custom_call_target="tpu_custom_call" | custom-call | tf_op jit(solution)/shard_map/pallas_call | solution.py:108
  33.2 1.0 %shard_map.58 = (f32[8,128]{1,0:T(8,128)S(1)}, f32[8,128]{1,0:T(8,128)S(1)}) custom-call(bf16[256,1024]{1,0:T(8,128)(2,1)S(1)} %collective-permute-done.6.arrived, bf16[1024,1024]{1,0:T(8,128)(2,1)S(1)} %get-tuple-element.30.units, f32[7,4,128]{2,1,0:T(4,128)S(1)} %get-tuple-element.31.live, f32[7,8,128]{2,1,0:T(8,128)S(1)} %get-tuple-element.32.mine, ...), custom_call_target="tpu_custom_call" | custom-call | tf_op jit(solution)/shard_map/pallas_call | solution.py:152
  34.3 0.0 collective-permute-done.4.arrived
  34.3 1.4 %collective-permute-start.7 = (f32[8,128]{1,0:T(8,128)S(1)}, f32[8,128]{1,0:T(8,128)S(1)}, u32[]{:S(2)}, u32[]{:S(2)}) collective-permute-start(f32[8,128]{1,0:T(8,128)S(1)} %get-tuple-element.41), channel_id=1, source_target_pairs={{0,4},{4,0},{8,12},{12,8},{1,5},{5,1},{9,13},{13,9},{2,6},{6,2},{1... | collective-permute-start | bytes 12296 | tf_op jit(solution)/shard_map/ppermute | solution.py:185
  35.6 1.0 %shard_map.59 = (f32[8,128]{1,0:T(8,128)S(1)}, f32[8,128]{1,0:T(8,128)S(1)}) custom-call(bf16[256,1024]{1,0:T(8,128)(2,1)S(1)} %collective-permute-done.5.arrived, bf16[1024,1024]{1,0:T(8,128)(2,1)S(1)} %get-tuple-element.30.units, f32[7,4,128]{2,1,0:T(4,128)S(1)} %get-tuple-element.31.live, f32[7,8,128]{2,1,0:T(8,128)S(1)} %get-tuple-element.32.mine, ...), custom_call_target="tpu_custom_call" | custom-call | tf_op jit(solution)/shard_map/pallas_call | solution.py:152
  36.7 0.0 collective-permute-done.7.rest_0_
  36.7 1.0 %shard_map.60 = (f32[8,128]{1,0:T(8,128)S(1)}, f32[8,128]{1,0:T(8,128)S(1)}) custom-call(bf16[256,1024]{1,0:T(8,128)(2,1)S(1)} %collective-permute-done.4.arrived, bf16[1024,1024]{1,0:T(8,128)(2,1)S(1)} %get-tuple-element.30.units, f32[7,4,128]{2,1,0:T(4,128)S(1)} %get-tuple-element.31.live, f32[7,8,128]{2,1,0:T(8,128)S(1)} %get-tuple-element.32.mine, ...), custom_call_target="tpu_custom_call" | custom-call | tf_op jit(solution)/shard_map/pallas_call | solution.py:152
  37.7 0.3 collective-permute-start.8
  38.0 0.0 collective-permute-done.3.arrived
  38.0 0.0 collective-permute-start.10
  38.0 1.0 %shard_map.61 = (f32[8,128]{1,0:T(8,128)S(1)}, f32[8,128]{1,0:T(8,128)S(1)}) custom-call(bf16[240,1024]{1,0:T(8,128)(2,1)S(1)} %collective-permute-done.3.arrived, bf16[1024,1024]{1,0:T(8,128)(2,1)S(1)} %get-tuple-element.30.units, f32[7,4,128]{2,1,0:T(4,128)S(1)} %get-tuple-element.31.live, f32[7,8,128]{2,1,0:T(8,128)S(1)} %get-tuple-element.32.mine, ...), custom_call_target="tpu_custom_call" | custom-call | tf_op jit(solution)/shard_map/pallas_call | solution.py:152
  39.0 0.0 collective-permute-done.2.arrived
  39.1 2.3 %collective-permute-done.8.rest_0_ = f32[8,128]{1,0:T(8,128)S(1)} collective-permute-done((f32[8,128]{1,0:T(8,128)S(1)}, f32[8,128]{1,0:T(8,128)S(1)}, u32[]{:S(2)}, u32[]{:S(2)}) %collective-permute-start.8) | collective-permute-done | bytes 4128 | tf_op jit(solution)/shard_map/ppermute | solution.py:185
  41.4 0.8 %shard_map.62 = (f32[8,128]{1,0:T(8,128)S(1)}, f32[8,128]{1,0:T(8,128)S(1)}) custom-call(bf16[16,1024]{1,0:T(8,128)(2,1)S(1)} %collective-permute-done.2.arrived, bf16[1024,1024]{1,0:T(8,128)(2,1)S(1)} %get-tuple-element.30.units, f32[7,4,128]{2,1,0:T(4,128)S(1)} %get-tuple-element.31.live, f32[7,8,128]{2,1,0:T(8,128)S(1)} %get-tuple-element.32.mine, ...), custom_call_target="tpu_custom_call" | custom-call | tf_op jit(solution)/shard_map/pallas_call | solution.py:152
  42.1 2.8 %collective-permute-done.1.arrived = bf16[256,1024]{1,0:T(8,128)(2,1)S(1)} collective-permute-done((bf16[256,1024]{1,0:T(8,128)(2,1)S(1)}, bf16[256,1024]{1,0:T(8,128)(2,1)S(1)}, u32[]{:S(2)}, u32[]{:S(2)}) %collective-permute-start.1) | collective-permute-done | bytes 524320 | tf_op jit(solution)/shard_map/ppermute | solution.py:185
  44.9 1.0 %shard_map.63 = (f32[8,128]{1,0:T(8,128)S(1)}, f32[8,128]{1,0:T(8,128)S(1)}) custom-call(bf16[256,1024]{1,0:T(8,128)(2,1)S(1)} %collective-permute-done.1.arrived, bf16[1024,1024]{1,0:T(8,128)(2,1)S(1)} %get-tuple-element.30.units, f32[7,4,128]{2,1,0:T(4,128)S(1)} %get-tuple-element.31.live, f32[7,8,128]{2,1,0:T(8,128)S(1)} %get-tuple-element.32.mine, ...), custom_call_target="tpu_custom_call" | custom-call | tf_op jit(solution)/shard_map/pallas_call | solution.py:152
  45.9 0.1 collective-permute-start.11
  46.0 0.1 collective-permute-start.9
  46.1 0.0 collective-permute-done.arrived
  46.1 7.7 %collective-permute-done.10.rest_1_ = f32[8,128]{1,0:T(8,128)S(1)} collective-permute-done((f32[8,128]{1,0:T(8,128)S(1)}, f32[8,128]{1,0:T(8,128)S(1)}, u32[]{:S(2)}, u32[]{:S(2)}) %collective-permute-start.10) | collective-permute-done | bytes 4128 | tf_op jit(solution)/shard_map/ppermute | solution.py:185
  53.8 0.0 collective-permute-done.11.rest_2_
  53.8 0.0 collective-permute-done.9.rest_0_
  53.8 1.0 %shard_map.64 = (f32[8,128]{1,0:T(8,128)S(1)}, f32[8,128]{1,0:T(8,128)S(1)}) custom-call(bf16[256,1024]{1,0:T(8,128)(2,1)S(1)} %collective-permute-done.arrived, bf16[1024,1024]{1,0:T(8,128)(2,1)S(1)} %get-tuple-element.30.units, f32[7,4,128]{2,1,0:T(4,128)S(1)} %get-tuple-element.31.live, f32[7,8,128]{2,1,0:T(8,128)S(1)} %get-tuple-element.32.mine, ...), custom_call_target="tpu_custom_call" | custom-call | tf_op jit(solution)/shard_map/pallas_call | solution.py:152
  54.8 3.6 %collective-permute-start.12 = (f32[8,128]{1,0:T(8,128)S(1)}, f32[8,128]{1,0:T(8,128)S(1)}, u32[]{:S(2)}, u32[]{:S(2)}) collective-permute-start(f32[8,128]{1,0:T(8,128)S(1)} %get-tuple-element.52), channel_id=1, source_target_pairs={{0,3},{1,2},{2,1},{3,0},{4,7},{5,6},{6,5},{7,4},{8,11},{9,10},{10,... | collective-permute-start | bytes 12296 | tf_op jit(solution)/shard_map/ppermute | solution.py:185
  58.5 1.9 %collective-permute-done.12 = f32[8,128]{1,0:T(8,128)S(1)} collective-permute-done((f32[8,128]{1,0:T(8,128)S(1)}, f32[8,128]{1,0:T(8,128)S(1)}, u32[]{:S(2)}, u32[]{:S(2)}) %collective-permute-start.12) | collective-permute-done | bytes 4128 | tf_op jit(solution)/shard_map/ppermute | solution.py:185
  60.3 0.6 fusion.2
  (1 shorter events, 0.0 us)
Async XLA Ops:
  0.0 7.2 %copy-start = (bf16[1024,1024]{1,0:T(8,128)(2,1)S(1)}, bf16[1024,1024]{1,0:T(8,128)(2,1)}, u32[]{:S(2)}) copy-start(bf16[1024,1024]{1,0:T(8,128)(2,1)} %embeds.5) | copy-start | bytes 6291460
  0.0 7.2 %copy-start.2 = (s32[1,4]{1,0:T(1,128)S(1)}, s32[1,4]{1,0:T(1,128)}, u32[]{:S(2)}) copy-start(s32[1,4]{1,0:T(1,128)} %pick_blk.5) | copy-start | bytes 52
  0.0 7.2 %copy-start.1 = (s32[4,4]{1,0:T(4,128)S(1)}, s32[4,4]{1,0:T(4,128)}, u32[]{:S(2)}) copy-start(s32[4,4]{1,0:T(4,128)} %pick_sub.5) | copy-start | bytes 196
  0.0 32.0 %copy-start.3 = (s32[1,16]{1,0:T(1,128)S(1)}, s32[1,16]{1,0:T(1,128)}, u32[]{:S(2)}) copy-start(s32[1,16]{1,0:T(1,128)} %mask_blk.1) | copy-start | bytes 196
  0.0 32.0 %copy-start.4 = (s32[1,16]{1,0:T(1,128)S(1)}, s32[1,16]{1,0:T(1,128)}, u32[]{:S(2)}) copy-start(s32[1,16]{1,0:T(1,128)} %mask_sub.1) | copy-start | bytes 196
  3.0 8.8 %collective-permute-start.6 = (bf16[256,1024]{1,0:T(8,128)(2,1)}, bf16[256,1024]{1,0:T(8,128)(2,1)S(1)}, u32[]{:S(2)}, u32[]{:S(2)}) collective-permute-start(bf16[256,1024]{1,0:T(8,128)(2,1)} %get-tuple-element.38), channel_id=1, source_target_pairs={{0,4},{4,0},{8,12},{12,8},{1,5},{5,1},{9,13},{13,9},{2,6},{6,2},{1... | collective-permute-start | bytes 1572872 | tf_op jit(solution)/shard_map/ppermute | solution.py:185
  3.5 27.9 %collective-permute-start.5 = (bf16[256,1024]{1,0:T(8,128)(2,1)}, bf16[256,1024]{1,0:T(8,128)(2,1)S(1)}, u32[]{:S(2)}, u32[]{:S(2)}) collective-permute-start(bf16[256,1024]{1,0:T(8,128)(2,1)} %get-tuple-element.37), channel_id=1, source_target_pairs={{0,2},{1,3},{2,0},{3,1},{4,6},{5,7},{6,4},{7,5},{8,10},{9,11},{10,... | collective-permute-start | bytes 1572872 | tf_op jit(solution)/shard_map/ppermute | solution.py:185
  8.4 25.9 %collective-permute-start.4 = (bf16[256,1024]{1,0:T(8,128)(2,1)S(1)}, bf16[256,1024]{1,0:T(8,128)(2,1)S(1)}, u32[]{:S(2)}, u32[]{:S(2)}) collective-permute-start(bf16[256,1024]{1,0:T(8,128)(2,1)S(1)} %get-tuple-element.36), channel_id=1, source_target_pairs={{0,8},{4,12},{8,0},{12,4},{1,9},{5,13},{9,1},{13,5},{2,10},{6,14},... | collective-permute-start | bytes 1572872 | tf_op jit(solution)/shard_map/ppermute | solution.py:185
  9.9 35.0 %collective-permute-start.1 = (bf16[256,1024]{1,0:T(8,128)(2,1)S(1)}, bf16[256,1024]{1,0:T(8,128)(2,1)S(1)}, u32[]{:S(2)}, u32[]{:S(2)}) collective-permute-start(bf16[256,1024]{1,0:T(8,128)(2,1)S(1)} %get-tuple-element.33), channel_id=1, source_target_pairs={{0,1},{1,0},{2,3},{3,2},{4,5},{5,4},{6,7},{7,6},{8,9},{9,8},{10,11... | collective-permute-start | bytes 1572872 | tf_op jit(solution)/shard_map/ppermute | solution.py:185
  11.5 34.6 %collective-permute-start = (bf16[256,1024]{1,0:T(8,128)(2,1)S(1)}, bf16[256,1024]{1,0:T(8,128)(2,1)S(1)}, u32[]{:S(2)}, u32[]{:S(2)}) collective-permute-start(bf16[256,1024]{1,0:T(8,128)(2,1)S(1)} %get-tuple-element.29), channel_id=1, source_target_pairs={{0,3},{1,2},{2,1},{3,0},{4,7},{5,6},{6,5},{7,4},{8,11},{9,10},{10,... | collective-permute-start | bytes 1572872 | tf_op jit(solution)/shard_map/ppermute | solution.py:185
  11.7 26.3 %collective-permute-start.3 = (bf16[240,1024]{1,0:T(8,128)(2,1)S(1)}, bf16[240,1024]{1,0:T(8,128)(2,1)S(1)}, u32[]{:S(2)}, u32[]{:S(2)}) collective-permute-start(bf16[240,1024]{1,0:T(8,128)(2,1)S(1)} %get-tuple-element.35), channel_id=1, source_target_pairs={{0,12},{4,8},{8,4},{12,0},{1,13},{5,9},{9,5},{13,1},{2,14},{6,10},... | collective-permute-start | bytes 1474568 | tf_op jit(solution)/shard_map/ppermute | solution.py:185
  31.4 7.6 %collective-permute-start.2 = (bf16[16,1024]{1,0:T(8,128)(2,1)S(1)}, bf16[16,1024]{1,0:T(8,128)(2,1)S(1)}, u32[]{:S(2)}, u32[]{:S(2)}) collective-permute-start(bf16[16,1024]{1,0:T(8,128)(2,1)S(1)} %get-tuple-element.34), channel_id=1, source_target_pairs={{0,12},{4,8},{8,4},{12,0},{1,13},{5,9},{9,5},{13,1},{2,14},{6,10},... | collective-permute-start | bytes 98312 | tf_op jit(solution)/shard_map/ppermute | solution.py:185
  34.3 2.4 %collective-permute-start.7 = (f32[8,128]{1,0:T(8,128)S(1)}, f32[8,128]{1,0:T(8,128)S(1)}, u32[]{:S(2)}, u32[]{:S(2)}) collective-permute-start(f32[8,128]{1,0:T(8,128)S(1)} %get-tuple-element.41), channel_id=1, source_target_pairs={{0,4},{4,0},{8,12},{12,8},{1,5},{5,1},{9,13},{13,9},{2,6},{6,2},{1... | collective-permute-start | bytes 12296 | tf_op jit(solution)/shard_map/ppermute | solution.py:185
  37.7 3.7 %collective-permute-start.8 = (f32[8,128]{1,0:T(8,128)S(1)}, f32[8,128]{1,0:T(8,128)S(1)}, u32[]{:S(2)}, u32[]{:S(2)}) collective-permute-start(f32[8,128]{1,0:T(8,128)S(1)} %get-tuple-element.44), channel_id=1, source_target_pairs={{0,8},{4,12},{8,0},{12,4},{1,9},{5,13},{9,1},{13,5},{2,10},{6,14},... | collective-permute-start | bytes 12296 | tf_op jit(solution)/shard_map/ppermute | solution.py:185
  38.0 15.8 %collective-permute-start.10 = (f32[8,128]{1,0:T(8,128)S(1)}, f32[8,128]{1,0:T(8,128)S(1)}, u32[]{:S(2)}, u32[]{:S(2)}) collective-permute-start(f32[8,128]{1,0:T(8,128)S(1)} %get-tuple-element.49), channel_id=1, source_target_pairs={{0,2},{1,3},{2,0},{3,1},{4,6},{5,7},{6,4},{7,5},{8,10},{9,11},{10,... | collective-permute-start | bytes 12296 | tf_op jit(solution)/shard_map/ppermute | solution.py:185
  45.9 7.9 %collective-permute-start.11 = (f32[8,128]{1,0:T(8,128)S(1)}, f32[8,128]{1,0:T(8,128)S(1)}, u32[]{:S(2)}, u32[]{:S(2)}) collective-permute-start(f32[8,128]{1,0:T(8,128)S(1)} %get-tuple-element.50), channel_id=1, source_target_pairs={{0,1},{1,0},{2,3},{3,2},{4,5},{5,4},{6,7},{7,6},{8,9},{9,8},{10,11... | collective-permute-start | bytes 12296 | tf_op jit(solution)/shard_map/ppermute | solution.py:185
  46.0 7.8 %collective-permute-start.9 = (f32[8,128]{1,0:T(8,128)S(1)}, f32[8,128]{1,0:T(8,128)S(1)}, u32[]{:S(2)}, u32[]{:S(2)}) collective-permute-start(f32[8,128]{1,0:T(8,128)S(1)} %get-tuple-element.48), channel_id=1, source_target_pairs={{0,12},{4,8},{8,4},{12,0},{1,13},{5,9},{9,5},{13,1},{2,14},{6,10},... | collective-permute-start | bytes 12296 | tf_op jit(solution)/shard_map/ppermute | solution.py:185
  54.8 5.5 %collective-permute-start.12 = (f32[8,128]{1,0:T(8,128)S(1)}, f32[8,128]{1,0:T(8,128)S(1)}, u32[]{:S(2)}, u32[]{:S(2)}) collective-permute-start(f32[8,128]{1,0:T(8,128)S(1)} %get-tuple-element.52), channel_id=1, source_target_pairs={{0,3},{1,2},{2,1},{3,0},{4,7},{5,6},{6,5},{7,4},{8,11},{9,10},{10,... | collective-permute-start | bytes 12296 | tf_op jit(solution)/shard_map/ppermute | solution.py:185

commit v10 on v9

--- a/solution.py
+++ b/solution.py
@@ -42,8 +42,49 @@
     return pick_blk[0, target] if axis == "blk" else pick_sub[lax.axis_index("sub"), target]
 
 
-def pick_kernel(pieces, pick_blk, pick_sub, embeds, *rest):
-    outs, (blk_scalars, sub_scalars, scalar_sems, in_sems, out_sems, *staged) = rest[: len(pieces)], rest[len(pieces) :]
+def first_kernel(slot, pick_sub, embeds, out, scalars, staged, scalar_sem, in_sems, out_sems):
+    axis, step, first, rows = slot
+    copy = pltpu.make_async_copy(pick_sub, scalars, scalar_sem)
+    copy.start()
+    copy.wait()
+    pick = take_pick(axis, step, None, scalars)
+    part = rows // PARTS
+    entering, leaving = [], []
+    for i in range(PARTS):
+        start = pl.multiple_of(pick * BLOCK + (first + i * part), part)
+        here = staged.at[pl.ds(i * part, part)]
+        entering.append(pltpu.make_async_copy(embeds.at[pl.ds(start, part)], here, in_sems.at[i]))
+        leaving.append(pltpu.make_async_copy(here, out.at[pl.ds(i * part, part)], out_sems.at[i]))
+        entering[i].start()
+    for i in range(PARTS):
+        entering[i].wait()
+        leaving[i].start()
+    for copy in leaving:
+        copy.wait()
+
+
+PARTS = 4
+
+
+def first_rows(slot, pick_sub, embeds):
+    shape = (slot[3], embeds.shape[1])
+    return pl.pallas_call(
+        functools.partial(first_kernel, slot),
+        out_shape=jax.ShapeDtypeStruct(shape, embeds.dtype),
+        in_specs=[ANY, ANY],
+        out_specs=ANY,
+        scratch_shapes=[
+            pltpu.SMEM(pick_sub.shape, jnp.int32),
+            pltpu.VMEM(shape, embeds.dtype),
+            pltpu.SemaphoreType.DMA,
+            pltpu.SemaphoreType.DMA((PARTS,)),
+            pltpu.SemaphoreType.DMA((PARTS,)),
+        ],
+    )(pick_sub, embeds)
+
+
+def pick_kernel(slots, pick_blk, pick_sub, embeds, *rest):
+    outs, (blk_scalars, sub_scalars, scalar_sems, row_sems) = rest[: len(slots)], rest[len(slots) :]
     scalars = [
         pltpu.make_async_copy(pick_blk, blk_scalars, scalar_sems.at[0]),
         pltpu.make_async_copy(pick_sub, sub_scalars, scalar_sems.at[1]),
@@ -53,38 +94,28 @@
     for copy in scalars:
         copy.wait()
     copies = []
-    for place, (axis, step, first, rows) in enumerate(pieces):
+    for place, (axis, step, first, rows) in enumerate(slots):
         pick = take_pick(axis, step, blk_scalars, sub_scalars)
         start = pl.multiple_of(pick * BLOCK + first, math.gcd(BLOCK, first))
-        target = staged[place] if staged else outs[place]
-        copies.append(pltpu.make_async_copy(embeds.at[pl.ds(start, rows)], target, in_sems.at[place]))
+        copies.append(pltpu.make_async_copy(embeds.at[pl.ds(start, rows)], outs[place], row_sems.at[place]))
         copies[-1].start()
-    leaving = []
-    for place, copy in enumerate(copies):
+    for copy in copies:
         copy.wait()
-        if staged:
-            leaving.append(pltpu.make_async_copy(staged[place], outs[place], out_sems.at[place]))
-            leaving[-1].start()
-    for copy in leaving:
-        copy.wait()
-
-
-def pick_rows(pieces, pick_blk, pick_sub, embeds, staged):
-    shapes = [(rows, embeds.shape[1]) for _, _, _, rows in pieces]
-    return pl.pallas_call(
-        functools.partial(pick_kernel, pieces),
-        out_shape=[jax.ShapeDtypeStruct(shape, embeds.dtype) for shape in shapes],
-        in_specs=[ANY if staged else HBM] * 3,
-        out_specs=[ANY if staged else VMEM] * len(pieces),
+
+
+def pick_rows(slots, pick_blk, pick_sub, embeds):
+    return pl.pallas_call(
+        functools.partial(pick_kernel, slots),
+        out_shape=[jax.ShapeDtypeStruct((rows, embeds.shape[1]), embeds.dtype) for _, _, _, rows in slots],
+        in_specs=[HBM] * 3,
+        out_specs=[VMEM] * len(slots),
         scratch_shapes=[
             pltpu.SMEM(pick_blk.shape, jnp.int32),
             pltpu.SMEM(pick_sub.shape, jnp.int32),
             pltpu.SemaphoreType.DMA((2,)),
-            pltpu.SemaphoreType.DMA((len(pieces),)),
-            pltpu.SemaphoreType.DMA((len(pieces),)),
-        ]
-        + [pltpu.VMEM(shape, embeds.dtype) for shape in shapes if staged],
-        compiler_params=None if staged else PARAMS,
+            pltpu.SemaphoreType.DMA((len(slots),)),
+        ],
+        compiler_params=PARAMS,
     )(pick_blk, pick_sub, embeds)
 
 
@@ -167,13 +198,10 @@
 
 
 def plan_slots(sizes):
-    slots = [("blk", 1, 0, BLOCK), ("sub", 2, 0, BLOCK), ("blk", 2, 0, BLOCK)]
+    slots = [("sub", 2, 0, BLOCK), ("blk", 1, 0, BLOCK), ("blk", 2, 0, BLOCK)]
     for k in range(3, sizes["blk"]):
         slots += [("blk", k, 0, FIRST_CUT), ("blk", k, FIRST_CUT, BLOCK - FIRST_CUT)]
     return slots + [("sub", k, 0, BLOCK) for k in (1, *range(3, sizes["sub"]))]
-
-
-AT_ONCE = 2
 
 
 def body(embeds, pick_blk, mask_blk, pick_sub, mask_sub):
@@ -184,10 +212,8 @@
     def send(array, slot):
         return lax.ppermute(array, slot[0], pairs(slot[1], sizes[slot[0]]))
 
-    arrived = []
-    for group, staged in ((slots[:AT_ONCE], True), (slots[AT_ONCE:], False)):
-        for rows, slot in zip(pick_rows(group, pick_blk, pick_sub, embeds, staged), group):
-            arrived.append(send(rows, slot))
+    outgoing = [first_rows(slots[0], pick_sub, embeds), *pick_rows(slots[1:], pick_blk, pick_sub, embeds)]
+    arrived = [send(rows, slot) for rows, slot in zip(outgoing, slots)]
 
     units, live, mine = prepare(slots, pick_blk, pick_sub, mask_blk, mask_sub, embeds)
     totals = jnp.zeros((count * ROWS, LANES), jnp.float32)
@@ -195,11 +221,8 @@
     soon, late = [], []
     for place, slot in enumerate(slots):
         axis, step, first, rows = slot
-        if place == len(slots) - 1:
-            ready, soon, late = soon + late, [], []
-        else:
-            done = sum(sent <= place - BEHIND for sent, _ in soon)
-            ready, soon = soon[:done], soon[done:]
+        done = len(soon) if place == len(slots) - 1 else sum(sent <= place - BEHIND for sent, _ in soon)
+        ready, soon = soon[:done], soon[done:]
         totals, back = work(
             place, slot, arrived[place], units, live, mine, totals, ready, carried.pop((axis, step), None)
         )

time: 61.1 us -> 69.4 us (1.14)
  the two profiles are of different devices: /device:TPU:0 before, /device:TPU:4 now
where the time goes in v10:
time: 69.4 us; the launch traced here: 69.3 us
  waiting for transfers between devices  44.9 us (65%)
  Pallas kernels  11.9 us (17%)
  starting transfers between devices  11.7 us (17%)
    ppermute x13, waiting for transfers between devices, send(): return lax.ppermute(array, slot[0], pairs(slot[1], sizes[slot[0]]))  44.9 us
    ppermute x13, starting transfers between devices, send(): return lax.ppermute(array, slot[0], pairs(slot[1], sizes[slot[0]]))  11.7 us
    pallas_call x7, Pallas kernels, work(): pl.pallas_call(functools.partial(slot_kernel, place, *slot[2:], [one for...  6.86 us
    pallas_call x1, Pallas kernels, first_rows(): pl.pallas_call(functools.partial(first_kernel, slot), out_shape=jax.Shape...  2.65 us
  transfers between devices with their start and end apart: 13, of which 5 were waited for; matrix products, arithmetic and copies ran while one was open for 0% of the time, Pallas kernels for 13%

profile of v10, /device:TPU:4, one launch (start us, length us, event | category | flops | bytes accessed | tf_op | source)
XLA Modules:
  0.0 69.3 jit_solution(9986231775735921748)
XLA Ops:
  0.0 0.0 copy-start.1
  0.0 0.0 copy-start
  0.0 0.0 copy-start.2
  0.0 0.0 copy-start.4
  0.0 0.0 copy-start.3
  0.0 2.7 %shard_map.57 = bf16[256,1024]{1,0:T(8,128)(2,1)} custom-call(s32[4,4]{1,0:T(4,128)} %pick_sub.5, bf16[1024,1024]{1,0:T(8,128)(2,1)} %embeds.5), custom_call_target="tpu_custom_call" | custom-call | tf_op jit(solution)/shard_map/pallas_call | solution.py:71
  2.7 2.7 %collective-permute-start.6 = (bf16[256,1024]{1,0:T(8,128)(2,1)}, bf16[256,1024]{1,0:T(8,128)(2,1)S(1)}, u32[]{:S(2)}, u32[]{:S(2)}) collective-permute-start(bf16[256,1024]{1,0:T(8,128)(2,1)} %shard_map.57), channel_id=1, source_target_pairs={{0,2},{1,3},{2,0},{3,1},{4,6},{5,7},{6,4},{7,5},{8,10},{9,11},{10,... | collective-permute-start | bytes 1572872 | tf_op jit(solution)/shard_map/ppermute | solution.py:213
  5.3 0.0 copy-done.1
  5.3 0.0 copy-done
  5.3 0.0 copy-done.2
  5.4 1.2 %shard_map.55 = (bf16[256,1024]{1,0:T(8,128)(2,1)S(1)}, bf16[256,1024]{1,0:T(8,128)(2,1)S(1)}, bf16[240,1024]{1,0:T(8,128)(2,1)S(1)}, bf16[16,1024]{1,0:T(8,128)...) custom-call(s32[1,4]{1,0:T(1,128)S(1)} %copy-done.2, s32[4,4]{1,0:T(4,128)S(1)} %copy-done.1, ...), custom_call_target="tpu_custom_call" | custom-call | tf_op jit(solution)/shard_map/pallas_call | solution.py:107
  6.6 0.1 collective-permute-start.5
  6.6 1.6 %collective-permute-start.4 = (bf16[256,1024]{1,0:T(8,128)(2,1)S(1)}, bf16[256,1024]{1,0:T(8,128)(2,1)S(1)}, u32[]{:S(2)}, u32[]{:S(2)}) collective-permute-start(bf16[256,1024]{1,0:T(8,128)(2,1)S(1)} %get-tuple-element.35), channel_id=1, source_target_pairs={{0,8},{4,12},{8,0},{12,4},{1,9},{5,13},{9,1},{13,5},{2,10},{6,14},... | collective-permute-start | bytes 1572872 | tf_op jit(solution)/shard_map/ppermute | solution.py:213
  8.2 1.6 %collective-permute-start.1 = (bf16[256,1024]{1,0:T(8,128)(2,1)S(1)}, bf16[256,1024]{1,0:T(8,128)(2,1)S(1)}, u32[]{:S(2)}, u32[]{:S(2)}) collective-permute-start(bf16[256,1024]{1,0:T(8,128)(2,1)S(1)} %get-tuple-element.32), channel_id=1, source_target_pairs={{0,1},{1,0},{2,3},{3,2},{4,5},{5,4},{6,7},{7,6},{8,9},{9,8},{10,11... | collective-permute-start | bytes 1572872 | tf_op jit(solution)/shard_map/ppermute | solution.py:213
  9.8 0.2 collective-permute-start
  10.0 31.2 %collective-permute-done.6.arrived = bf16[256,1024]{1,0:T(8,128)(2,1)S(1)} collective-permute-done((bf16[256,1024]{1,0:T(8,128)(2,1)}, bf16[256,1024]{1,0:T(8,128)(2,1)S(1)}, u32[]{:S(2)}, u32[]{:S(2)}) %collective-permute-start.6) | collective-permute-done | bytes 524320 | tf_op jit(solution)/shard_map/ppermute | solution.py:213
  41.2 0.0 collective-permute-start.3
  41.2 0.0 collective-permute-done.5.arrived
  41.2 1.7 %collective-permute-start.2 = (bf16[16,1024]{1,0:T(8,128)(2,1)S(1)}, bf16[16,1024]{1,0:T(8,128)(2,1)S(1)}, u32[]{:S(2)}, u32[]{:S(2)}) collective-permute-start(bf16[16,1024]{1,0:T(8,128)(2,1)S(1)} %get-tuple-element.33), channel_id=1, source_target_pairs={{0,12},{4,8},{8,4},{12,0},{1,13},{5,9},{9,5},{13,1},{2,14},{6,10},... | collective-permute-start | bytes 98312 | tf_op jit(solution)/shard_map/ppermute | solution.py:213
  43.0 0.0 copy-done.4
  43.0 0.0 copy-done.3
  43.0 1.2 %shard_map.56 = (bf16[1024,1024]{1,0:T(8,128)(2,1)S(1)}, f32[7,4,128]{2,1,0:T(4,128)S(1)}, f32[7,8,128]{2,1,0:T(8,128)S(1)}) custom-call(s32[1,4]{1,0:T(1,128)S(1)} %copy-done.2, s32[4,4]{1,0:T(4,128)S(1)} %copy-done.1, s32[1,16]{1,0:T(1,128)S(1)} %copy-done.3, s32[1,16]{1,0:T(1,128)S(1)} %copy-done.4, bf16[1024,1024]{1,0:T(8,128)(2,1)S(1)} %copy-done), custom_call_target="tpu_custom_call" | custom-call | tf_op jit(solution)/shard_map/pallas_call | solution.py:139
  44.2 1.0 %shard_map.58 = (f32[8,128]{1,0:T(8,128)S(1)}, f32[8,128]{1,0:T(8,128)S(1)}) custom-call(bf16[256,1024]{1,0:T(8,128)(2,1)S(1)} %collective-permute-done.6.arrived, bf16[1024,1024]{1,0:T(8,128)(2,1)S(1)} %get-tuple-element.29.units, f32[7,4,128]{2,1,0:T(4,128)S(1)} %get-tuple-element.30.live, f32[7,8,128]{2,1,0:T(8,128)S(1)} %get-tuple-element.31.mine, ...), custom_call_target="tpu_custom_call" | custom-call | tf_op jit(solution)/shard_map/pallas_call | solution.py:183
  45.2 1.0 %shard_map.59 = (f32[8,128]{1,0:T(8,128)S(1)}, f32[8,128]{1,0:T(8,128)S(1)}) custom-call(bf16[256,1024]{1,0:T(8,128)(2,1)S(1)} %collective-permute-done.5.arrived, bf16[1024,1024]{1,0:T(8,128)(2,1)S(1)} %get-tuple-element.29.units, f32[7,4,128]{2,1,0:T(4,128)S(1)} %get-tuple-element.30.live, f32[7,8,128]{2,1,0:T(8,128)S(1)} %get-tuple-element.31.mine, ...), custom_call_target="tpu_custom_call" | custom-call | tf_op jit(solution)/shard_map/pallas_call | solution.py:183
  46.3 0.0 collective-permute-done.4.arrived
  46.3 0.1 collective-permute-start.7
  46.4 1.0 %shard_map.60 = (f32[8,128]{1,0:T(8,128)S(1)}, f32[8,128]{1,0:T(8,128)S(1)}) custom-call(bf16[256,1024]{1,0:T(8,128)(2,1)S(1)} %collective-permute-done.4.arrived, bf16[1024,1024]{1,0:T(8,128)(2,1)S(1)} %get-tuple-element.29.units, f32[7,4,128]{2,1,0:T(4,128)S(1)} %get-tuple-element.30.live, f32[7,8,128]{2,1,0:T(8,128)S(1)} %get-tuple-element.31.mine, ...), custom_call_target="tpu_custom_call" | custom-call | tf_op jit(solution)/shard_map/pallas_call | solution.py:183
  47.4 7.3 %collective-permute-done.3.arrived = bf16[240,1024]{1,0:T(8,128)(2,1)S(1)} collective-permute-done((bf16[240,1024]{1,0:T(8,128)(2,1)S(1)}, bf16[240,1024]{1,0:T(8,128)(2,1)S(1)}, u32[]{:S(2)}, u32[]{:S(2)}) %collective-permute-start.3) | collective-permute-done | bytes 491552 | tf_op jit(solution)/shard_map/ppermute | solution.py:213
  54.7 1.0 %collective-permute-start.8 = (f32[8,128]{1,0:T(8,128)S(1)}, f32[8,128]{1,0:T(8,128)S(1)}, u32[]{:S(2)}, u32[]{:S(2)}) collective-permute-start(f32[8,128]{1,0:T(8,128)S(1)} %get-tuple-element.42), channel_id=1, source_target_pairs={{0,8},{4,12},{8,0},{12,4},{1,9},{5,13},{9,1},{13,5},{2,10},{6,14},... | collective-permute-start | bytes 12296 | tf_op jit(solution)/shard_map/ppermute | solution.py:213
  55.7 0.0 collective-permute-done.7.rest_0_
  55.7 1.0 %shard_map.61 = (f32[8,128]{1,0:T(8,128)S(1)}, f32[8,128]{1,0:T(8,128)S(1)}) custom-call(bf16[240,1024]{1,0:T(8,128)(2,1)S(1)} %collective-permute-done.3.arrived, bf16[1024,1024]{1,0:T(8,128)(2,1)S(1)} %get-tuple-element.29.units, f32[7,4,128]{2,1,0:T(4,128)S(1)} %get-tuple-element.30.live, f32[7,8,128]{2,1,0:T(8,128)S(1)} %get-tuple-element.31.mine, ...), custom_call_target="tpu_custom_call" | custom-call | tf_op jit(solution)/shard_map/pallas_call | solution.py:183
  56.7 0.0 collective-permute-done.2.arrived
  56.7 1.6 %collective-permute-done.8.rest_0_ = f32[8,128]{1,0:T(8,128)S(1)} collective-permute-done((f32[8,128]{1,0:T(8,128)S(1)}, f32[8,128]{1,0:T(8,128)S(1)}, u32[]{:S(2)}, u32[]{:S(2)}) %collective-permute-start.8) | collective-permute-done | bytes 4128 | tf_op jit(solution)/shard_map/ppermute | solution.py:213
  58.3 0.8 %shard_map.62 = (f32[8,128]{1,0:T(8,128)S(1)}, f32[8,128]{1,0:T(8,128)S(1)}) custom-call(bf16[16,1024]{1,0:T(8,128)(2,1)S(1)} %collective-permute-done.2.arrived, bf16[1024,1024]{1,0:T(8,128)(2,1)S(1)} %get-tuple-element.29.units, f32[7,4,128]{2,1,0:T(4,128)S(1)} %get-tuple-element.30.live, f32[7,8,128]{2,1,0:T(8,128)S(1)} %get-tuple-element.31.mine, ...), custom_call_target="tpu_custom_call" | custom-call | tf_op jit(solution)/shard_map/pallas_call | solution.py:183
  59.1 0.1 collective-permute-start.9
  59.2 0.1 collective-permute-start.10
  59.2 0.0 collective-permute-done.1.arrived
  59.2 1.0 %shard_map.63 = (f32[8,128]{1,0:T(8,128)S(1)}, f32[8,128]{1,0:T(8,128)S(1)}) custom-call(bf16[256,1024]{1,0:T(8,128)(2,1)S(1)} %collective-permute-done.1.arrived, bf16[1024,1024]{1,0:T(8,128)(2,1)S(1)} %get-tuple-element.29.units, f32[7,4,128]{2,1,0:T(4,128)S(1)} %get-tuple-element.30.live, f32[7,8,128]{2,1,0:T(8,128)S(1)} %get-tuple-element.31.mine, ...), custom_call_target="tpu_custom_call" | custom-call | tf_op jit(solution)/shard_map/pallas_call | solution.py:183
  60.3 0.1 collective-permute-start.11
  60.3 0.0 collective-permute-done.arrived
  60.4 1.8 %collective-permute-done.9.rest_0_ = f32[8,128]{1,0:T(8,128)S(1)} collective-permute-done((f32[8,128]{1,0:T(8,128)S(1)}, f32[8,128]{1,0:T(8,128)S(1)}, u32[]{:S(2)}, u32[]{:S(2)}) %collective-permute-start.9) | collective-permute-done | bytes 4128 | tf_op jit(solution)/shard_map/ppermute | solution.py:213
  62.2 1.0 %shard_map.64 = (f32[8,128]{1,0:T(8,128)S(1)}, f32[8,128]{1,0:T(8,128)S(1)}) custom-call(bf16[256,1024]{1,0:T(8,128)(2,1)S(1)} %collective-permute-done.arrived, bf16[1024,1024]{1,0:T(8,128)(2,1)S(1)} %get-tuple-element.29.units, f32[7,4,128]{2,1,0:T(4,128)S(1)} %get-tuple-element.30.live, f32[7,8,128]{2,1,0:T(8,128)S(1)} %get-tuple-element.31.mine, ...), custom_call_target="tpu_custom_call" | custom-call | tf_op jit(solution)/shard_map/pallas_call | solution.py:183
  63.2 2.6 %collective-permute-start.12 = (f32[8,128]{1,0:T(8,128)S(1)}, f32[8,128]{1,0:T(8,128)S(1)}, u32[]{:S(2)}, u32[]{:S(2)}) collective-permute-start(f32[8,128]{1,0:T(8,128)S(1)} %get-tuple-element.50), channel_id=1, source_target_pairs={{0,3},{1,2},{2,1},{3,0},{4,7},{5,6},{6,5},{7,4},{8,11},{9,10},{10,... | collective-permute-start | bytes 12296 | tf_op jit(solution)/shard_map/ppermute | solution.py:213
  65.8 0.0 collective-permute-done.10
  65.8 0.0 collective-permute-done.11
  65.8 2.9 %collective-permute-done.12 = f32[8,128]{1,0:T(8,128)S(1)} collective-permute-done((f32[8,128]{1,0:T(8,128)S(1)}, f32[8,128]{1,0:T(8,128)S(1)}, u32[]{:S(2)}, u32[]{:S(2)}) %collective-permute-start.12) | collective-permute-done | bytes 4128 | tf_op jit(solution)/shard_map/ppermute | solution.py:213
  68.7 0.6 fusion.2
  (1 shorter events, 0.0 us)
Async XLA Ops:
  0.0 5.3 %copy-start.1 = (s32[4,4]{1,0:T(4,128)S(1)}, s32[4,4]{1,0:T(4,128)}, u32[]{:S(2)}) copy-start(s32[4,4]{1,0:T(4,128)} %pick_sub.5) | copy-start | bytes 196
  0.0 5.3 %copy-start = (bf16[1024,1024]{1,0:T(8,128)(2,1)S(1)}, bf16[1024,1024]{1,0:T(8,128)(2,1)}, u32[]{:S(2)}) copy-start(bf16[1024,1024]{1,0:T(8,128)(2,1)} %embeds.5) | copy-start | bytes 6291460
  0.0 5.3 %copy-start.2 = (s32[1,4]{1,0:T(1,128)S(1)}, s32[1,4]{1,0:T(1,128)}, u32[]{:S(2)}) copy-start(s32[1,4]{1,0:T(1,128)} %pick_blk.3) | copy-start | bytes 52
  0.0 43.0 %copy-start.4 = (s32[1,16]{1,0:T(1,128)S(1)}, s32[1,16]{1,0:T(1,128)}, u32[]{:S(2)}) copy-start(s32[1,16]{1,0:T(1,128)} %mask_sub.1) | copy-start | bytes 196
  0.0 43.0 %copy-start.3 = (s32[1,16]{1,0:T(1,128)S(1)}, s32[1,16]{1,0:T(1,128)}, u32[]{:S(2)}) copy-start(s32[1,16]{1,0:T(1,128)} %mask_blk.1) | copy-start | bytes 196
  2.7 38.5 %collective-permute-start.6 = (bf16[256,1024]{1,0:T(8,128)(2,1)}, bf16[256,1024]{1,0:T(8,128)(2,1)S(1)}, u32[]{:S(2)}, u32[]{:S(2)}) collective-permute-start(bf16[256,1024]{1,0:T(8,128)(2,1)} %shard_map.57), channel_id=1, source_target_pairs={{0,2},{1,3},{2,0},{3,1},{4,6},{5,7},{6,4},{7,5},{8,10},{9,11},{10,... | collective-permute-start | bytes 1572872 | tf_op jit(solution)/shard_map/ppermute | solution.py:213
  6.6 34.7 %collective-permute-start.5 = (bf16[256,1024]{1,0:T(8,128)(2,1)S(1)}, bf16[256,1024]{1,0:T(8,128)(2,1)S(1)}, u32[]{:S(2)}, u32[]{:S(2)}) collective-permute-start(bf16[256,1024]{1,0:T(8,128)(2,1)S(1)} %get-tuple-element.36), channel_id=1, source_target_pairs={{0,4},{4,0},{8,12},{12,8},{1,5},{5,1},{9,13},{13,9},{2,6},{6,2},{1... | collective-permute-start | bytes 1572872 | tf_op jit(solution)/shard_map/ppermute | solution.py:213
  6.6 39.6 %collective-permute-start.4 = (bf16[256,1024]{1,0:T(8,128)(2,1)S(1)}, bf16[256,1024]{1,0:T(8,128)(2,1)S(1)}, u32[]{:S(2)}, u32[]{:S(2)}) collective-permute-start(bf16[256,1024]{1,0:T(8,128)(2,1)S(1)} %get-tuple-element.35), channel_id=1, source_target_pairs={{0,8},{4,12},{8,0},{12,4},{1,9},{5,13},{9,1},{13,5},{2,10},{6,14},... | collective-permute-start | bytes 1572872 | tf_op jit(solution)/shard_map/ppermute | solution.py:213
  8.2 51.1 %collective-permute-start.1 = (bf16[256,1024]{1,0:T(8,128)(2,1)S(1)}, bf16[256,1024]{1,0:T(8,128)(2,1)S(1)}, u32[]{:S(2)}, u32[]{:S(2)}) collective-permute-start(bf16[256,1024]{1,0:T(8,128)(2,1)S(1)} %get-tuple-element.32), channel_id=1, source_target_pairs={{0,1},{1,0},{2,3},{3,2},{4,5},{5,4},{6,7},{7,6},{8,9},{9,8},{10,11... | collective-permute-start | bytes 1572872 | tf_op jit(solution)/shard_map/ppermute | solution.py:213
  9.8 50.6 %collective-permute-start = (bf16[256,1024]{1,0:T(8,128)(2,1)S(1)}, bf16[256,1024]{1,0:T(8,128)(2,1)S(1)}, u32[]{:S(2)}, u32[]{:S(2)}) collective-permute-start(bf16[256,1024]{1,0:T(8,128)(2,1)S(1)} %get-tuple-element.28), channel_id=1, source_target_pairs={{0,3},{1,2},{2,1},{3,0},{4,7},{5,6},{6,5},{7,4},{8,11},{9,10},{10,... | collective-permute-start | bytes 1572872 | tf_op jit(solution)/shard_map/ppermute | solution.py:213
  41.2 13.5 %collective-permute-start.3 = (bf16[240,1024]{1,0:T(8,128)(2,1)S(1)}, bf16[240,1024]{1,0:T(8,128)(2,1)S(1)}, u32[]{:S(2)}, u32[]{:S(2)}) collective-permute-start(bf16[240,1024]{1,0:T(8,128)(2,1)S(1)} %get-tuple-element.34), channel_id=1, source_target_pairs={{0,12},{4,8},{8,4},{12,0},{1,13},{5,9},{9,5},{13,1},{2,14},{6,10},... | collective-permute-start | bytes 1474568 | tf_op jit(solution)/shard_map/ppermute | solution.py:213
  41.2 15.5 %collective-permute-start.2 = (bf16[16,1024]{1,0:T(8,128)(2,1)S(1)}, bf16[16,1024]{1,0:T(8,128)(2,1)S(1)}, u32[]{:S(2)}, u32[]{:S(2)}) collective-permute-start(bf16[16,1024]{1,0:T(8,128)(2,1)S(1)} %get-tuple-element.33), channel_id=1, source_target_pairs={{0,12},{4,8},{8,4},{12,0},{1,13},{5,9},{9,5},{13,1},{2,14},{6,10},... | collective-permute-start | bytes 98312 | tf_op jit(solution)/shard_map/ppermute | solution.py:213
  46.3 9.4 %collective-permute-start.7 = (f32[8,128]{1,0:T(8,128)S(1)}, f32[8,128]{1,0:T(8,128)S(1)}, u32[]{:S(2)}, u32[]{:S(2)}) collective-permute-start(f32[8,128]{1,0:T(8,128)S(1)} %get-tuple-element.40), channel_id=1, source_target_pairs={{0,4},{4,0},{8,12},{12,8},{1,5},{5,1},{9,13},{13,9},{2,6},{6,2},{1... | collective-permute-start | bytes 12296 | tf_op jit(solution)/shard_map/ppermute | solution.py:213
  54.7 3.6 %collective-permute-start.8 = (f32[8,128]{1,0:T(8,128)S(1)}, f32[8,128]{1,0:T(8,128)S(1)}, u32[]{:S(2)}, u32[]{:S(2)}) collective-permute-start(f32[8,128]{1,0:T(8,128)S(1)} %get-tuple-element.42), channel_id=1, source_target_pairs={{0,8},{4,12},{8,0},{12,4},{1,9},{5,13},{9,1},{13,5},{2,10},{6,14},... | collective-permute-start | bytes 12296 | tf_op jit(solution)/shard_map/ppermute | solution.py:213
  59.1 3.1 %collective-permute-start.9 = (f32[8,128]{1,0:T(8,128)S(1)}, f32[8,128]{1,0:T(8,128)S(1)}, u32[]{:S(2)}, u32[]{:S(2)}) collective-permute-start(f32[8,128]{1,0:T(8,128)S(1)} %get-tuple-element.46), channel_id=1, source_target_pairs={{0,12},{4,8},{8,4},{12,0},{1,13},{5,9},{9,5},{13,1},{2,14},{6,10},... | collective-permute-start | bytes 12296 | tf_op jit(solution)/shard_map/ppermute | solution.py:213
  59.2 6.6 %collective-permute-start.10 = (f32[8,128]{1,0:T(8,128)S(1)}, f32[8,128]{1,0:T(8,128)S(1)}, u32[]{:S(2)}, u32[]{:S(2)}) collective-permute-start(f32[8,128]{1,0:T(8,128)S(1)} %get-tuple-element.48), channel_id=1, source_target_pairs={{0,2},{1,3},{2,0},{3,1},{4,6},{5,7},{6,4},{7,5},{8,10},{9,11},{10,... | collective-permute-start | bytes 12296 | tf_op jit(solution)/shard_map/ppermute | solution.py:213
  60.3 5.5 %collective-permute-start.11 = (f32[8,128]{1,0:T(8,128)S(1)}, f32[8,128]{1,0:T(8,128)S(1)}, u32[]{:S(2)}, u32[]{:S(2)}) collective-permute-start(f32[8,128]{1,0:T(8,128)S(1)} %get-tuple-element.49), channel_id=1, source_target_pairs={{0,1},{1,0},{2,3},{3,2},{4,5},{5,4},{6,7},{7,6},{8,9},{9,8},{10,11... | collective-permute-start | bytes 12296 | tf_op jit(solution)/shard_map/ppermute | solution.py:213
  63.2 5.5 %collective-permute-start.12 = (f32[8,128]{1,0:T(8,128)S(1)}, f32[8,128]{1,0:T(8,128)S(1)}, u32[]{:S(2)}, u32[]{:S(2)}) collective-permute-start(f32[8,128]{1,0:T(8,128)S(1)} %get-tuple-element.50), channel_id=1, source_target_pairs={{0,3},{1,2},{2,1},{3,0},{4,7},{5,6},{6,5},{7,4},{8,11},{9,10},{10,... | collective-permute-start | bytes 12296 | tf_op jit(solution)/shard_map/ppermute | solution.py:213

commit v11 on v10

--- a/solution.py
+++ b/solution.py
@@ -42,45 +42,53 @@
     return pick_blk[0, target] if axis == "blk" else pick_sub[lax.axis_index("sub"), target]
 
 
-def first_kernel(slot, pick_sub, embeds, out, scalars, staged, scalar_sem, in_sems, out_sems):
-    axis, step, first, rows = slot
-    copy = pltpu.make_async_copy(pick_sub, scalars, scalar_sem)
-    copy.start()
-    copy.wait()
-    pick = take_pick(axis, step, None, scalars)
-    part = rows // PARTS
+def first_kernel(slots, pick_blk, pick_sub, embeds, *rest):
+    outs, (blk_scalars, sub_scalars, staged, scalar_sems, in_sems, out_sems) = rest[: len(slots)], rest[len(slots) :]
+    scalars = [
+        pltpu.make_async_copy(pick_blk, blk_scalars, scalar_sems.at[0]),
+        pltpu.make_async_copy(pick_sub, sub_scalars, scalar_sems.at[1]),
+    ]
+    for copy in scalars:
+        copy.start()
+    for copy in scalars:
+        copy.wait()
     entering, leaving = [], []
-    for i in range(PARTS):
-        start = pl.multiple_of(pick * BLOCK + (first + i * part), part)
-        here = staged.at[pl.ds(i * part, part)]
-        entering.append(pltpu.make_async_copy(embeds.at[pl.ds(start, part)], here, in_sems.at[i]))
-        leaving.append(pltpu.make_async_copy(here, out.at[pl.ds(i * part, part)], out_sems.at[i]))
-        entering[i].start()
-    for i in range(PARTS):
-        entering[i].wait()
-        leaving[i].start()
-    for copy in leaving:
-        copy.wait()
-
-
-PARTS = 4
-
-
-def first_rows(slot, pick_sub, embeds):
-    shape = (slot[3], embeds.shape[1])
-    return pl.pallas_call(
-        functools.partial(first_kernel, slot),
-        out_shape=jax.ShapeDtypeStruct(shape, embeds.dtype),
-        in_specs=[ANY, ANY],
-        out_specs=ANY,
+    for place, (axis, step, first, rows) in enumerate(slots):
+        pick = take_pick(axis, step, blk_scalars, sub_scalars)
+        for start in range(0, rows, PART):
+            source = pl.multiple_of(pick * BLOCK + (first + start), PART)
+            here = staged.at[place, pl.ds(start, PART)]
+            number = len(entering)
+            entering.append(pltpu.make_async_copy(embeds.at[pl.ds(source, PART)], here, in_sems.at[number]))
+            leaving.append(pltpu.make_async_copy(here, outs[place].at[pl.ds(start, PART)], out_sems.at[number]))
+            entering[-1].start()
+    for copy, onward in zip(entering, leaving):
+        copy.wait()
+        onward.start()
+    for onward in leaving:
+        onward.wait()
+
+
+PART = 64
+
+
+def first_rows(slots, pick_blk, pick_sub, embeds):
+    shape = (BLOCK, embeds.shape[1])
+    parts = len(slots) * (BLOCK // PART)
+    return pl.pallas_call(
+        functools.partial(first_kernel, slots),
+        out_shape=[jax.ShapeDtypeStruct(shape, embeds.dtype)] * len(slots),
+        in_specs=[ANY] * 3,
+        out_specs=[ANY] * len(slots),
         scratch_shapes=[
+            pltpu.SMEM(pick_blk.shape, jnp.int32),
             pltpu.SMEM(pick_sub.shape, jnp.int32),
-            pltpu.VMEM(shape, embeds.dtype),
-            pltpu.SemaphoreType.DMA,
-            pltpu.SemaphoreType.DMA((PARTS,)),
-            pltpu.SemaphoreType.DMA((PARTS,)),
+            pltpu.VMEM((len(slots), *shape), embeds.dtype),
+            pltpu.SemaphoreType.DMA((2,)),
+            pltpu.SemaphoreType.DMA((parts,)),
+            pltpu.SemaphoreType.DMA((parts,)),
         ],
-    )(pick_sub, embeds)
+    )(pick_blk, pick_sub, embeds)
 
 
 def pick_kernel(slots, pick_blk, pick_sub, embeds, *rest):
@@ -198,10 +206,13 @@
 
 
 def plan_slots(sizes):
-    slots = [("sub", 2, 0, BLOCK), ("blk", 1, 0, BLOCK), ("blk", 2, 0, BLOCK)]
+    slots = [("blk", 1, 0, BLOCK), ("sub", 2, 0, BLOCK), ("blk", 2, 0, BLOCK)]
     for k in range(3, sizes["blk"]):
         slots += [("blk", k, 0, FIRST_CUT), ("blk", k, FIRST_CUT, BLOCK - FIRST_CUT)]
     return slots + [("sub", k, 0, BLOCK) for k in (1, *range(3, sizes["sub"]))]
+
+
+AT_ONCE = 2
 
 
 def body(embeds, pick_blk, mask_blk, pick_sub, mask_sub):
@@ -212,7 +223,8 @@
     def send(array, slot):
         return lax.ppermute(array, slot[0], pairs(slot[1], sizes[slot[0]]))
 
-    outgoing = [first_rows(slots[0], pick_sub, embeds), *pick_rows(slots[1:], pick_blk, pick_sub, embeds)]
+    outgoing = first_rows(slots[:AT_ONCE], pick_blk, pick_sub, embeds)
+    outgoing += pick_rows(slots[AT_ONCE:], pick_blk, pick_sub, embeds)
     arrived = [send(rows, slot) for rows, slot in zip(outgoing, slots)]
 
     units, live, mine = prepare(slots, pick_blk, pick_sub, mask_blk, mask_sub, embeds)

time: 69.4 us -> 58 us (0.84)
  the two profiles are of different devices: /device:TPU:4 before, /device:TPU:18 now
where the time goes in v11:
time: 58 us; the launch traced here: 57.8 us
  waiting for transfers between devices  31.4 us (54%)
  starting transfers between devices  13.5 us (23%)
  Pallas kernels  12.2 us (21%)
  other arithmetic  0.6 us (1%)
    ppermute x13, waiting for transfers between devices, send(): return lax.ppermute(array, slot[0], pairs(slot[1], sizes[slot[0]]))  31.4 us
    ppermute x13, starting transfers between devices, send(): return lax.ppermute(array, slot[0], pairs(slot[1], sizes[slot[0]]))  13.5 us
    pallas_call x7, Pallas kernels, work(): pl.pallas_call(functools.partial(slot_kernel, place, *slot[2:], [one for...  6.83 us
    pallas_call x1, Pallas kernels, first_rows(): pl.pallas_call(functools.partial(first_kernel, slots), out_shape=[jax.Sha...  2.97 us
    pallas_call x1, Pallas kernels, prepare(): pl.pallas_call(functools.partial(prepare_kernel, slots), out_shape=[jax.S...  1.23 us
  transfers between devices with their start and end apart: 13, of which 4 were waited for; matrix products, arithmetic and copies ran while one was open for 0% of the time, Pallas kernels for 16%

profile of v11, /device:TPU:18, one launch (start us, length us, event | category | flops | bytes accessed | tf_op | source)
XLA Modules:
  0.0 57.8 jit_solution(12824076572210728829)
XLA Ops:
  0.0 0.0 copy-start
  0.0 0.0 copy-start.2
  0.0 0.0 copy-start.1
  0.0 0.0 copy-start.3
  0.0 0.0 copy-start.4
  0.0 3.0 %shard_map.57 = (bf16[256,1024]{1,0:T(8,128)(2,1)}, bf16[256,1024]{1,0:T(8,128)(2,1)}) custom-call(s32[1,4]{1,0:T(1,128)} %pick_blk.5, s32[4,4]{1,0:T(4,128)} %pick_sub.5, bf16[1024,1024]{1,0:T(8,128)(2,1)} %embeds.5), custom_call_target="tpu_custom_call" | custom-call | tf_op jit(solution)/shard_map/pallas_call | solution.py:78
  3.0 0.1 collective-permute-start.6
  3.1 0.4 collective-permute-start.5
  3.5 0.0 copy-done
  3.5 0.0 copy-done.2
  3.5 0.0 copy-done.1
  3.5 1.1 %shard_map.55 = (bf16[256,1024]{1,0:T(8,128)(2,1)S(1)}, bf16[240,1024]{1,0:T(8,128)(2,1)S(1)}, bf16[16,1024]{1,0:T(8,128)(2,1)S(1)}, bf16[256,1024]{1,0:T(8,128)(2,1)S(1)}, bf16[256,1024]{1,0:T(8,128)(2,1)S(1)}) custom-call(s32[1,4]{1,0:T(1,128)S(1)} %copy-done.2, s32[4,4]{1,0:T(4,128)S(1)} %copy-done.1, bf16[1024,1024]{1,0:T(8,128)(2,1)S(1)} %copy-done), custom_call_target="tpu_custom_call" | custom-call | tf_op jit(solution)/shard_map/pallas_call | solution.py:115
  4.6 0.3 collective-permute-start.4
  4.9 1.9 %collective-permute-start.1 = (bf16[256,1024]{1,0:T(8,128)(2,1)S(1)}, bf16[256,1024]{1,0:T(8,128)(2,1)S(1)}, u32[]{:S(2)}, u32[]{:S(2)}) collective-permute-start(bf16[256,1024]{1,0:T(8,128)(2,1)S(1)} %get-tuple-element.33), channel_id=1, source_target_pairs={{0,1},{1,0},{2,3},{3,2},{4,5},{5,4},{6,7},{7,6},{8,9},{9,8},{10,11... | collective-permute-start | bytes 1572872 | tf_op jit(solution)/shard_map/ppermute | solution.py:224
  6.8 1.6 %collective-permute-start = (bf16[256,1024]{1,0:T(8,128)(2,1)S(1)}, bf16[256,1024]{1,0:T(8,128)(2,1)S(1)}, u32[]{:S(2)}, u32[]{:S(2)}) collective-permute-start(bf16[256,1024]{1,0:T(8,128)(2,1)S(1)} %get-tuple-element.29), channel_id=1, source_target_pairs={{0,3},{1,2},{2,1},{3,0},{4,7},{5,6},{6,5},{7,4},{8,11},{9,10},{10,... | collective-permute-start | bytes 1572872 | tf_op jit(solution)/shard_map/ppermute | solution.py:224
  8.4 0.0 collective-permute-done.6.arrived
  8.4 0.4 collective-permute-start.3
  8.8 18.5 %collective-permute-done.5.arrived = bf16[256,1024]{1,0:T(8,128)(2,1)S(1)} collective-permute-done((bf16[256,1024]{1,0:T(8,128)(2,1)}, bf16[256,1024]{1,0:T(8,128)(2,1)S(1)}, u32[]{:S(2)}, u32[]{:S(2)}) %collective-permute-start.5) | collective-permute-done | bytes 524320 | tf_op jit(solution)/shard_map/ppermute | solution.py:224
  27.3 0.0 collective-permute-start.2
  27.3 0.0 copy-done.3
  27.3 0.0 copy-done.4
  27.3 1.2 %shard_map.56 = (bf16[1024,1024]{1,0:T(8,128)(2,1)S(1)}, f32[7,4,128]{2,1,0:T(4,128)S(1)}, f32[7,8,128]{2,1,0:T(8,128)S(1)}) custom-call(s32[1,4]{1,0:T(1,128)S(1)} %copy-done.2, s32[4,4]{1,0:T(4,128)S(1)} %copy-done.1, s32[1,16]{1,0:T(1,128)S(1)} %copy-done.3, s32[1,16]{1,0:T(1,128)S(1)} %copy-done.4, bf16[1024,1024]{1,0:T(8,128)(2,1)S(1)} %copy-done), custom_call_target="tpu_custom_call" | custom-call | tf_op jit(solution)/shard_map/pallas_call | solution.py:147
  28.6 1.0 %shard_map.58 = (f32[8,128]{1,0:T(8,128)S(1)}, f32[8,128]{1,0:T(8,128)S(1)}) custom-call(bf16[256,1024]{1,0:T(8,128)(2,1)S(1)} %collective-permute-done.6.arrived, bf16[1024,1024]{1,0:T(8,128)(2,1)S(1)} %get-tuple-element.30.units, f32[7,4,128]{2,1,0:T(4,128)S(1)} %get-tuple-element.31.live, f32[7,8,128]{2,1,0:T(8,128)S(1)} %get-tuple-element.32.mine, ...), custom_call_target="tpu_custom_call" | custom-call | tf_op jit(solution)/shard_map/pallas_call | solution.py:191
  29.6 0.0 collective-permute-done.4.arrived
  29.6 0.5 collective-permute-start.7
  30.1 1.0 %shard_map.59 = (f32[8,128]{1,0:T(8,128)S(1)}, f32[8,128]{1,0:T(8,128)S(1)}) custom-call(bf16[256,1024]{1,0:T(8,128)(2,1)S(1)} %collective-permute-done.5.arrived, bf16[1024,1024]{1,0:T(8,128)(2,1)S(1)} %get-tuple-element.30.units, f32[7,4,128]{2,1,0:T(4,128)S(1)} %get-tuple-element.31.live, f32[7,8,128]{2,1,0:T(8,128)S(1)} %get-tuple-element.32.mine, ...), custom_call_target="tpu_custom_call" | custom-call | tf_op jit(solution)/shard_map/pallas_call | solution.py:191
  31.1 0.0 collective-permute-done.7.rest_0_
  31.1 1.0 %shard_map.60 = (f32[8,128]{1,0:T(8,128)S(1)}, f32[8,128]{1,0:T(8,128)S(1)}) custom-call(bf16[256,1024]{1,0:T(8,128)(2,1)S(1)} %collective-permute-done.4.arrived, bf16[1024,1024]{1,0:T(8,128)(2,1)S(1)} %get-tuple-element.30.units, f32[7,4,128]{2,1,0:T(4,128)S(1)} %get-tuple-element.31.live, f32[7,8,128]{2,1,0:T(8,128)S(1)} %get-tuple-element.32.mine, ...), custom_call_target="tpu_custom_call" | custom-call | tf_op jit(solution)/shard_map/pallas_call | solution.py:191
  32.1 1.8 %collective-permute-start.8 = (f32[8,128]{1,0:T(8,128)S(1)}, f32[8,128]{1,0:T(8,128)S(1)}, u32[]{:S(2)}, u32[]{:S(2)}) collective-permute-start(f32[8,128]{1,0:T(8,128)S(1)} %get-tuple-element.44), channel_id=1, source_target_pairs={{0,8},{4,12},{8,0},{12,4},{1,9},{5,13},{9,1},{13,5},{2,10},{6,14},... | collective-permute-start | bytes 12296 | tf_op jit(solution)/shard_map/ppermute | solution.py:224
  33.9 0.0 collective-permute-done.3.arrived
  33.9 1.0 %shard_map.61 = (f32[8,128]{1,0:T(8,128)S(1)}, f32[8,128]{1,0:T(8,128)S(1)}) custom-call(bf16[240,1024]{1,0:T(8,128)(2,1)S(1)} %collective-permute-done.3.arrived, bf16[1024,1024]{1,0:T(8,128)(2,1)S(1)} %get-tuple-element.30.units, f32[7,4,128]{2,1,0:T(4,128)S(1)} %get-tuple-element.31.live, f32[7,8,128]{2,1,0:T(8,128)S(1)} %get-tuple-element.32.mine, ...), custom_call_target="tpu_custom_call" | custom-call | tf_op jit(solution)/shard_map/pallas_call | solution.py:191
  34.9 0.0 collective-permute-done.2.arrived
  34.9 0.8 %collective-permute-done.8.rest_0_ = f32[8,128]{1,0:T(8,128)S(1)} collective-permute-done((f32[8,128]{1,0:T(8,128)S(1)}, f32[8,128]{1,0:T(8,128)S(1)}, u32[]{:S(2)}, u32[]{:S(2)}) %collective-permute-start.8) | collective-permute-done | bytes 4128 | tf_op jit(solution)/shard_map/ppermute | solution.py:224
  35.8 0.8 %shard_map.62 = (f32[8,128]{1,0:T(8,128)S(1)}, f32[8,128]{1,0:T(8,128)S(1)}) custom-call(bf16[16,1024]{1,0:T(8,128)(2,1)S(1)} %collective-permute-done.2.arrived, bf16[1024,1024]{1,0:T(8,128)(2,1)S(1)} %get-tuple-element.30.units, f32[7,4,128]{2,1,0:T(4,128)S(1)} %get-tuple-element.31.live, f32[7,8,128]{2,1,0:T(8,128)S(1)} %get-tuple-element.32.mine, ...), custom_call_target="tpu_custom_call" | custom-call | tf_op jit(solution)/shard_map/pallas_call | solution.py:191
  36.6 0.7 %collective-permute-start.9 = (f32[8,128]{1,0:T(8,128)S(1)}, f32[8,128]{1,0:T(8,128)S(1)}, u32[]{:S(2)}, u32[]{:S(2)}) collective-permute-start(f32[8,128]{1,0:T(8,128)S(1)} %get-tuple-element.48), channel_id=1, source_target_pairs={{0,12},{4,8},{8,4},{12,0},{1,13},{5,9},{9,5},{13,1},{2,14},{6,10},... | collective-permute-start | bytes 12296 | tf_op jit(solution)/shard_map/ppermute | solution.py:224
  37.3 3.3 %collective-permute-start.10 = (f32[8,128]{1,0:T(8,128)S(1)}, f32[8,128]{1,0:T(8,128)S(1)}, u32[]{:S(2)}, u32[]{:S(2)}) collective-permute-start(f32[8,128]{1,0:T(8,128)S(1)} %get-tuple-element.50), channel_id=1, source_target_pairs={{0,2},{1,3},{2,0},{3,1},{4,6},{5,7},{6,4},{7,5},{8,10},{9,11},{10,... | collective-permute-start | bytes 12296 | tf_op jit(solution)/shard_map/ppermute | solution.py:224
  40.5 0.0 collective-permute-done.1.arrived
  40.5 1.0 %shard_map.63 = (f32[8,128]{1,0:T(8,128)S(1)}, f32[8,128]{1,0:T(8,128)S(1)}) custom-call(bf16[256,1024]{1,0:T(8,128)(2,1)S(1)} %collective-permute-done.1.arrived, bf16[1024,1024]{1,0:T(8,128)(2,1)S(1)} %get-tuple-element.30.units, f32[7,4,128]{2,1,0:T(4,128)S(1)} %get-tuple-element.31.live, f32[7,8,128]{2,1,0:T(8,128)S(1)} %get-tuple-element.32.mine, ...), custom_call_target="tpu_custom_call" | custom-call | tf_op jit(solution)/shard_map/pallas_call | solution.py:191
  41.6 2.5 %collective-permute-start.11 = (f32[8,128]{1,0:T(8,128)S(1)}, f32[8,128]{1,0:T(8,128)S(1)}, u32[]{:S(2)}, u32[]{:S(2)}) collective-permute-start(f32[8,128]{1,0:T(8,128)S(1)} %get-tuple-element.51), channel_id=1, source_target_pairs={{0,1},{1,0},{2,3},{3,2},{4,5},{5,4},{6,7},{7,6},{8,9},{9,8},{10,11... | collective-permute-start | bytes 12296 | tf_op jit(solution)/shard_map/ppermute | solution.py:224
  44.0 8.5 %collective-permute-done.arrived = bf16[256,1024]{1,0:T(8,128)(2,1)S(1)} collective-permute-done((bf16[256,1024]{1,0:T(8,128)(2,1)S(1)}, bf16[256,1024]{1,0:T(8,128)(2,1)S(1)}, u32[]{:S(2)}, u32[]{:S(2)}) %collective-permute-start) | collective-permute-done | bytes 524320 | tf_op jit(solution)/shard_map/ppermute | solution.py:224
  52.5 0.0 collective-permute-done.9.rest_0_
  52.5 1.0 %shard_map.64 = (f32[8,128]{1,0:T(8,128)S(1)}, f32[8,128]{1,0:T(8,128)S(1)}) custom-call(bf16[256,1024]{1,0:T(8,128)(2,1)S(1)} %collective-permute-done.arrived, bf16[1024,1024]{1,0:T(8,128)(2,1)S(1)} %get-tuple-element.30.units, f32[7,4,128]{2,1,0:T(4,128)S(1)} %get-tuple-element.31.live, f32[7,8,128]{2,1,0:T(8,128)S(1)} %get-tuple-element.32.mine, ...), custom_call_target="tpu_custom_call" | custom-call | tf_op jit(solution)/shard_map/pallas_call | solution.py:191
  53.5 0.1 collective-permute-start.12
  53.6 0.0 collective-permute-done.10
  53.6 0.0 collective-permute-done.11
  53.6 3.6 %collective-permute-done.12 = f32[8,128]{1,0:T(8,128)S(1)} collective-permute-done((f32[8,128]{1,0:T(8,128)S(1)}, f32[8,128]{1,0:T(8,128)S(1)}, u32[]{:S(2)}, u32[]{:S(2)}) %collective-permute-start.12) | collective-permute-done | bytes 4128 | tf_op jit(solution)/shard_map/ppermute | solution.py:224
  57.2 0.6 %fusion.2 = f32[1024]{0:T(1024)} fusion(f32[8,128]{1,0:T(8,128)S(1)} %collective-permute-done.12, f32[8,128]{1,0:T(8,128)S(1)} %collective-permute-done.11, f32[8,128]{1,0:T(8,128)S(1)} %get-tuple-element.49, f32[8,128]{1,0:T(8,128)S(1)} %collective-permute-done.10, f32[7,8,128]{2,1,0:T(8,128)S(1)} %get-tuple-element.32.mine), kind=kLoop, calls=%fused_computation.3 | loop fusion | flops 7168 | bytes 32768 | tf_op jit(solution)/shard_map/reshape | solution.py:247
  (1 shorter events, 0.0 us)
Async XLA Ops:
  0.0 3.5 %copy-start = (bf16[1024,1024]{1,0:T(8,128)(2,1)S(1)}, bf16[1024,1024]{1,0:T(8,128)(2,1)}, u32[]{:S(2)}) copy-start(bf16[1024,1024]{1,0:T(8,128)(2,1)} %embeds.5) | copy-start | bytes 6291460
  0.0 3.5 %copy-start.2 = (s32[1,4]{1,0:T(1,128)S(1)}, s32[1,4]{1,0:T(1,128)}, u32[]{:S(2)}) copy-start(s32[1,4]{1,0:T(1,128)} %pick_blk.5) | copy-start | bytes 52
  0.0 3.5 %copy-start.1 = (s32[4,4]{1,0:T(4,128)S(1)}, s32[4,4]{1,0:T(4,128)}, u32[]{:S(2)}) copy-start(s32[4,4]{1,0:T(4,128)} %pick_sub.5) | copy-start | bytes 196
  0.0 27.3 %copy-start.3 = (s32[1,16]{1,0:T(1,128)S(1)}, s32[1,16]{1,0:T(1,128)}, u32[]{:S(2)}) copy-start(s32[1,16]{1,0:T(1,128)} %mask_blk.1) | copy-start | bytes 196
  0.0 27.3 %copy-start.4 = (s32[1,16]{1,0:T(1,128)S(1)}, s32[1,16]{1,0:T(1,128)}, u32[]{:S(2)}) copy-start(s32[1,16]{1,0:T(1,128)} %mask_sub.1) | copy-start | bytes 196
  3.0 5.4 %collective-permute-start.6 = (bf16[256,1024]{1,0:T(8,128)(2,1)}, bf16[256,1024]{1,0:T(8,128)(2,1)S(1)}, u32[]{:S(2)}, u32[]{:S(2)}) collective-permute-start(bf16[256,1024]{1,0:T(8,128)(2,1)} %get-tuple-element.38), channel_id=1, source_target_pairs={{0,4},{4,0},{8,12},{12,8},{1,5},{5,1},{9,13},{13,9},{2,6},{6,2},{1... | collective-permute-start | bytes 1572872 | tf_op jit(solution)/shard_map/ppermute | solution.py:224
  3.1 24.2 %collective-permute-start.5 = (bf16[256,1024]{1,0:T(8,128)(2,1)}, bf16[256,1024]{1,0:T(8,128)(2,1)S(1)}, u32[]{:S(2)}, u32[]{:S(2)}) collective-permute-start(bf16[256,1024]{1,0:T(8,128)(2,1)} %get-tuple-element.37), channel_id=1, source_target_pairs={{0,2},{1,3},{2,0},{3,1},{4,6},{5,7},{6,4},{7,5},{8,10},{9,11},{10,... | collective-permute-start | bytes 1572872 | tf_op jit(solution)/shard_map/ppermute | solution.py:224
  4.6 25.0 %collective-permute-start.4 = (bf16[256,1024]{1,0:T(8,128)(2,1)S(1)}, bf16[256,1024]{1,0:T(8,128)(2,1)S(1)}, u32[]{:S(2)}, u32[]{:S(2)}) collective-permute-start(bf16[256,1024]{1,0:T(8,128)(2,1)S(1)} %get-tuple-element.36), channel_id=1, source_target_pairs={{0,8},{4,12},{8,0},{12,4},{1,9},{5,13},{9,1},{13,5},{2,10},{6,14},... | collective-permute-start | bytes 1572872 | tf_op jit(solution)/shard_map/ppermute | solution.py:224
  4.9 35.6 %collective-permute-start.1 = (bf16[256,1024]{1,0:T(8,128)(2,1)S(1)}, bf16[256,1024]{1,0:T(8,128)(2,1)S(1)}, u32[]{:S(2)}, u32[]{:S(2)}) collective-permute-start(bf16[256,1024]{1,0:T(8,128)(2,1)S(1)} %get-tuple-element.33), channel_id=1, source_target_pairs={{0,1},{1,0},{2,3},{3,2},{4,5},{5,4},{6,7},{7,6},{8,9},{9,8},{10,11... | collective-permute-start | bytes 1572872 | tf_op jit(solution)/shard_map/ppermute | solution.py:224
  6.8 45.7 %collective-permute-start = (bf16[256,1024]{1,0:T(8,128)(2,1)S(1)}, bf16[256,1024]{1,0:T(8,128)(2,1)S(1)}, u32[]{:S(2)}, u32[]{:S(2)}) collective-permute-start(bf16[256,1024]{1,0:T(8,128)(2,1)S(1)} %get-tuple-element.29), channel_id=1, source_target_pairs={{0,3},{1,2},{2,1},{3,0},{4,7},{5,6},{6,5},{7,4},{8,11},{9,10},{10,... | collective-permute-start | bytes 1572872 | tf_op jit(solution)/shard_map/ppermute | solution.py:224
  8.4 25.5 %collective-permute-start.3 = (bf16[240,1024]{1,0:T(8,128)(2,1)S(1)}, bf16[240,1024]{1,0:T(8,128)(2,1)S(1)}, u32[]{:S(2)}, u32[]{:S(2)}) collective-permute-start(bf16[240,1024]{1,0:T(8,128)(2,1)S(1)} %get-tuple-element.35), channel_id=1, source_target_pairs={{0,12},{4,8},{8,4},{12,0},{1,13},{5,9},{9,5},{13,1},{2,14},{6,10},... | collective-permute-start | bytes 1474568 | tf_op jit(solution)/shard_map/ppermute | solution.py:224
  27.3 7.6 %collective-permute-start.2 = (bf16[16,1024]{1,0:T(8,128)(2,1)S(1)}, bf16[16,1024]{1,0:T(8,128)(2,1)S(1)}, u32[]{:S(2)}, u32[]{:S(2)}) collective-permute-start(bf16[16,1024]{1,0:T(8,128)(2,1)S(1)} %get-tuple-element.34), channel_id=1, source_target_pairs={{0,12},{4,8},{8,4},{12,0},{1,13},{5,9},{9,5},{13,1},{2,14},{6,10},... | collective-permute-start | bytes 98312 | tf_op jit(solution)/shard_map/ppermute | solution.py:224
  29.6 1.5 %collective-permute-start.7 = (f32[8,128]{1,0:T(8,128)S(1)}, f32[8,128]{1,0:T(8,128)S(1)}, u32[]{:S(2)}, u32[]{:S(2)}) collective-permute-start(f32[8,128]{1,0:T(8,128)S(1)} %get-tuple-element.41), channel_id=1, source_target_pairs={{0,4},{4,0},{8,12},{12,8},{1,5},{5,1},{9,13},{13,9},{2,6},{6,2},{1... | collective-permute-start | bytes 12296 | tf_op jit(solution)/shard_map/ppermute | solution.py:224
  32.1 3.7 %collective-permute-start.8 = (f32[8,128]{1,0:T(8,128)S(1)}, f32[8,128]{1,0:T(8,128)S(1)}, u32[]{:S(2)}, u32[]{:S(2)}) collective-permute-start(f32[8,128]{1,0:T(8,128)S(1)} %get-tuple-element.44), channel_id=1, source_target_pairs={{0,8},{4,12},{8,0},{12,4},{1,9},{5,13},{9,1},{13,5},{2,10},{6,14},... | collective-permute-start | bytes 12296 | tf_op jit(solution)/shard_map/ppermute | solution.py:224
  36.6 16.0 %collective-permute-start.9 = (f32[8,128]{1,0:T(8,128)S(1)}, f32[8,128]{1,0:T(8,128)S(1)}, u32[]{:S(2)}, u32[]{:S(2)}) collective-permute-start(f32[8,128]{1,0:T(8,128)S(1)} %get-tuple-element.48), channel_id=1, source_target_pairs={{0,12},{4,8},{8,4},{12,0},{1,13},{5,9},{9,5},{13,1},{2,14},{6,10},... | collective-permute-start | bytes 12296 | tf_op jit(solution)/shard_map/ppermute | solution.py:224
  37.3 16.3 %collective-permute-start.10 = (f32[8,128]{1,0:T(8,128)S(1)}, f32[8,128]{1,0:T(8,128)S(1)}, u32[]{:S(2)}, u32[]{:S(2)}) collective-permute-start(f32[8,128]{1,0:T(8,128)S(1)} %get-tuple-element.50), channel_id=1, source_target_pairs={{0,2},{1,3},{2,0},{3,1},{4,6},{5,7},{6,4},{7,5},{8,10},{9,11},{10,... | collective-permute-start | bytes 12296 | tf_op jit(solution)/shard_map/ppermute | solution.py:224
  41.6 12.1 %collective-permute-start.11 = (f32[8,128]{1,0:T(8,128)S(1)}, f32[8,128]{1,0:T(8,128)S(1)}, u32[]{:S(2)}, u32[]{:S(2)}) collective-permute-start(f32[8,128]{1,0:T(8,128)S(1)} %get-tuple-element.51), channel_id=1, source_target_pairs={{0,1},{1,0},{2,3},{3,2},{4,5},{5,4},{6,7},{7,6},{8,9},{9,8},{10,11... | collective-permute-start | bytes 12296 | tf_op jit(solution)/shard_map/ppermute | solution.py:224
  53.5 3.7 %collective-permute-start.12 = (f32[8,128]{1,0:T(8,128)S(1)}, f32[8,128]{1,0:T(8,128)S(1)}, u32[]{:S(2)}, u32[]{:S(2)}) collective-permute-start(f32[8,128]{1,0:T(8,128)S(1)} %get-tuple-element.52), channel_id=1, source_target_pairs={{0,3},{1,2},{2,1},{3,0},{4,7},{5,6},{6,5},{7,4},{8,11},{9,10},{10,... | collective-permute-start | bytes 12296 | tf_op jit(solution)/shard_map/ppermute | solution.py:224

commit v12 on v11

--- a/solution.py
+++ b/solution.py
@@ -202,14 +202,15 @@
 HALF = BLOCK // 2
 
 
-FIRST_CUT = 240
+FIRST_CUT = 128
 
 
 def plan_slots(sizes):
-    slots = [("blk", 1, 0, BLOCK), ("sub", 2, 0, BLOCK), ("blk", 2, 0, BLOCK)]
-    for k in range(3, sizes["blk"]):
-        slots += [("blk", k, 0, FIRST_CUT), ("blk", k, FIRST_CUT, BLOCK - FIRST_CUT)]
-    return slots + [("sub", k, 0, BLOCK) for k in (1, *range(3, sizes["sub"]))]
+    slots = [("blk", 1, 0, BLOCK), ("sub", 2, 0, BLOCK), ("sub", 1, 0, BLOCK)]
+    slots += [("blk", k, 0, BLOCK) for k in range(2, sizes["blk"])]
+    for k in range(3, sizes["sub"]):
+        slots += [("sub", k, 0, FIRST_CUT), ("sub", k, FIRST_CUT, BLOCK - FIRST_CUT)]
+    return slots
 
 
 AT_ONCE = 2

time: 58 us -> 57.8 us (level)
  the two profiles are of different devices: /device:TPU:18 before, /device:TPU:0 now
where the time goes in v12:
time: 57.8 us; the launch traced here: 57 us
  waiting for transfers between devices  22.3 us (39%)
  starting transfers between devices  21.9 us (38%)
  Pallas kernels  12 us (21%)
  other arithmetic  0.6 us (1%)
    ppermute x13, waiting for transfers between devices, send(): return lax.ppermute(array, slot[0], pairs(slot[1], sizes[slot[0]]))  22.3 us
    ppermute x13, starting transfers between devices, send(): return lax.ppermute(array, slot[0], pairs(slot[1], sizes[slot[0]]))  21.9 us
    pallas_call x7, Pallas kernels, work(): pl.pallas_call(functools.partial(slot_kernel, place, *slot[2:], [one for...  7.01 us
    pallas_call x1, Pallas kernels, first_rows(): pl.pallas_call(functools.partial(first_kernel, slots), out_shape=[jax.Sha...  2.97 us
    pallas_call x1, Pallas kernels, prepare(): pl.pallas_call(functools.partial(prepare_kernel, slots), out_shape=[jax.S...  1.23 us
  transfers between devices with their start and end apart: 13, of which 3 were waited for; matrix products, arithmetic and copies ran while one was open for 0% of the time, Pallas kernels for 16%

profile of v12, /device:TPU:0, one launch (start us, length us, event | category | flops | bytes accessed | tf_op | source)
XLA Modules:
  0.0 57.0 jit_solution(7359385305758769330)
XLA Ops:
  0.0 0.0 copy-start
  0.0 0.0 copy-start.2
  0.0 0.0 copy-start.1
  0.0 0.0 copy-start.3
  0.0 0.0 copy-start.4
  0.0 3.0 %shard_map.57 = (bf16[256,1024]{1,0:T(8,128)(2,1)}, bf16[256,1024]{1,0:T(8,128)(2,1)}) custom-call(s32[1,4]{1,0:T(1,128)} %pick_blk.5, s32[4,4]{1,0:T(4,128)} %pick_sub.5, bf16[1024,1024]{1,0:T(8,128)(2,1)} %embeds.5), custom_call_target="tpu_custom_call" | custom-call | tf_op jit(solution)/shard_map/pallas_call | solution.py:78
  3.0 0.5 collective-permute-start.6
  3.5 3.7 %collective-permute-start.5 = (bf16[256,1024]{1,0:T(8,128)(2,1)}, bf16[256,1024]{1,0:T(8,128)(2,1)S(1)}, u32[]{:S(2)}, u32[]{:S(2)}) collective-permute-start(bf16[256,1024]{1,0:T(8,128)(2,1)} %get-tuple-element.37), channel_id=1, source_target_pairs={{0,2},{1,3},{2,0},{3,1},{4,6},{5,7},{6,4},{7,5},{8,10},{9,11},{10,... | collective-permute-start | bytes 1572872 | tf_op jit(solution)/shard_map/ppermute | solution.py:225
  7.2 0.0 copy-done
  7.2 0.0 copy-done.2
  7.2 0.0 copy-done.1
  7.2 0.8 %shard_map.55 = (bf16[256,1024]{1,0:T(8,128)(2,1)S(1)}, bf16[256,1024]{1,0:T(8,128)(2,1)S(1)}, bf16[256,1024]{1,0:T(8,128)(2,1)S(1)}, bf16[128,1024]{1,0:T(8,128)(2,1)S(1)}, bf16[128,1024]{1,0:T(8,128)(2,1)S(1)}) custom-call(s32[1,4]{1,0:T(1,128)S(1)} %copy-done.2, s32[4,4]{1,0:T(4,128)S(1)} %copy-done.1, bf16[1024,1024]{1,0:T(8,128)(2,1)S(1)} %copy-done), custom_call_target="tpu_custom_call" | custom-call | tf_op jit(solution)/shard_map/pallas_call | solution.py:115
  8.0 1.6 %collective-permute-start.4 = (bf16[256,1024]{1,0:T(8,128)(2,1)S(1)}, bf16[256,1024]{1,0:T(8,128)(2,1)S(1)}, u32[]{:S(2)}, u32[]{:S(2)}) collective-permute-start(bf16[256,1024]{1,0:T(8,128)(2,1)S(1)} %get-tuple-element.36), channel_id=1, source_target_pairs={{0,1},{1,0},{2,3},{3,2},{4,5},{5,4},{6,7},{7,6},{8,9},{9,8},{10,11... | collective-permute-start | bytes 1572872 | tf_op jit(solution)/shard_map/ppermute | solution.py:225
  9.7 1.5 %collective-permute-start.3 = (bf16[256,1024]{1,0:T(8,128)(2,1)S(1)}, bf16[256,1024]{1,0:T(8,128)(2,1)S(1)}, u32[]{:S(2)}, u32[]{:S(2)}) collective-permute-start(bf16[256,1024]{1,0:T(8,128)(2,1)S(1)} %get-tuple-element.35), channel_id=1, source_target_pairs={{0,8},{4,12},{8,0},{12,4},{1,9},{5,13},{9,1},{13,5},{2,10},{6,14},... | collective-permute-start | bytes 1572872 | tf_op jit(solution)/shard_map/ppermute | solution.py:225
  11.2 0.0 collective-permute-start.2
  11.2 0.0 collective-permute-done.6.arrived
  11.2 0.2 collective-permute-start.1
  11.4 20.1 %collective-permute-done.5.arrived = bf16[256,1024]{1,0:T(8,128)(2,1)S(1)} collective-permute-done((bf16[256,1024]{1,0:T(8,128)(2,1)}, bf16[256,1024]{1,0:T(8,128)(2,1)S(1)}, u32[]{:S(2)}, u32[]{:S(2)}) %collective-permute-start.5) | collective-permute-done | bytes 524320 | tf_op jit(solution)/shard_map/ppermute | solution.py:225
  31.5 3.7 %collective-permute-start = (bf16[128,1024]{1,0:T(8,128)(2,1)S(1)}, bf16[128,1024]{1,0:T(8,128)(2,1)S(1)}, u32[]{:S(2)}, u32[]{:S(2)}) collective-permute-start(bf16[128,1024]{1,0:T(8,128)(2,1)S(1)} %get-tuple-element.29), channel_id=1, source_target_pairs={{0,3},{1,2},{2,1},{3,0},{4,7},{5,6},{6,5},{7,4},{8,11},{9,10},{10,... | collective-permute-start | bytes 786440 | tf_op jit(solution)/shard_map/ppermute | solution.py:225
  35.2 0.0 copy-done.3
  35.2 0.0 copy-done.4
  35.2 1.2 %shard_map.56 = (bf16[1024,1024]{1,0:T(8,128)(2,1)S(1)}, f32[7,4,128]{2,1,0:T(4,128)S(1)}, f32[7,8,128]{2,1,0:T(8,128)S(1)}) custom-call(s32[1,4]{1,0:T(1,128)S(1)} %copy-done.2, s32[4,4]{1,0:T(4,128)S(1)} %copy-done.1, s32[1,16]{1,0:T(1,128)S(1)} %copy-done.3, s32[1,16]{1,0:T(1,128)S(1)} %copy-done.4, bf16[1024,1024]{1,0:T(8,128)(2,1)S(1)} %copy-done), custom_call_target="tpu_custom_call" | custom-call | tf_op jit(solution)/shard_map/pallas_call | solution.py:147
  36.5 1.0 %shard_map.58 = (f32[8,128]{1,0:T(8,128)S(1)}, f32[8,128]{1,0:T(8,128)S(1)}) custom-call(bf16[256,1024]{1,0:T(8,128)(2,1)S(1)} %collective-permute-done.6.arrived, bf16[1024,1024]{1,0:T(8,128)(2,1)S(1)} %get-tuple-element.30.units, f32[7,4,128]{2,1,0:T(4,128)S(1)} %get-tuple-element.31.live, f32[7,8,128]{2,1,0:T(8,128)S(1)} %get-tuple-element.32.mine, ...), custom_call_target="tpu_custom_call" | custom-call | tf_op jit(solution)/shard_map/pallas_call | solution.py:191
  37.5 0.0 collective-permute-done.4.arrived
  37.5 0.1 collective-permute-start.7
  37.6 1.0 %shard_map.59 = (f32[8,128]{1,0:T(8,128)S(1)}, f32[8,128]{1,0:T(8,128)S(1)}) custom-call(bf16[256,1024]{1,0:T(8,128)(2,1)S(1)} %collective-permute-done.5.arrived, bf16[1024,1024]{1,0:T(8,128)(2,1)S(1)} %get-tuple-element.30.units, f32[7,4,128]{2,1,0:T(4,128)S(1)} %get-tuple-element.31.live, f32[7,8,128]{2,1,0:T(8,128)S(1)} %get-tuple-element.32.mine, ...), custom_call_target="tpu_custom_call" | custom-call | tf_op jit(solution)/shard_map/pallas_call | solution.py:191
  38.6 0.1 collective-permute-done.7.rest_0_
  38.7 1.0 %shard_map.60 = (f32[8,128]{1,0:T(8,128)S(1)}, f32[8,128]{1,0:T(8,128)S(1)}) custom-call(bf16[256,1024]{1,0:T(8,128)(2,1)S(1)} %collective-permute-done.4.arrived, bf16[1024,1024]{1,0:T(8,128)(2,1)S(1)} %get-tuple-element.30.units, f32[7,4,128]{2,1,0:T(4,128)S(1)} %get-tuple-element.31.live, f32[7,8,128]{2,1,0:T(8,128)S(1)} %get-tuple-element.32.mine, ...), custom_call_target="tpu_custom_call" | custom-call | tf_op jit(solution)/shard_map/pallas_call | solution.py:191
  39.7 0.0 collective-permute-done.3.arrived
  39.7 1.0 %shard_map.61 = (f32[8,128]{1,0:T(8,128)S(1)}, f32[8,128]{1,0:T(8,128)S(1)}) custom-call(bf16[256,1024]{1,0:T(8,128)(2,1)S(1)} %collective-permute-done.3.arrived, bf16[1024,1024]{1,0:T(8,128)(2,1)S(1)} %get-tuple-element.30.units, f32[7,4,128]{2,1,0:T(4,128)S(1)} %get-tuple-element.31.live, f32[7,8,128]{2,1,0:T(8,128)S(1)} %get-tuple-element.32.mine, ...), custom_call_target="tpu_custom_call" | custom-call | tf_op jit(solution)/shard_map/pallas_call | solution.py:191
  40.7 1.6 %collective-permute-start.8 = (f32[8,128]{1,0:T(8,128)S(1)}, f32[8,128]{1,0:T(8,128)S(1)}, u32[]{:S(2)}, u32[]{:S(2)}) collective-permute-start(f32[8,128]{1,0:T(8,128)S(1)} %get-tuple-element.45), channel_id=1, source_target_pairs={{0,8},{4,12},{8,0},{12,4},{1,9},{5,13},{9,1},{13,5},{2,10},{6,14},... | collective-permute-start | bytes 12296 | tf_op jit(solution)/shard_map/ppermute | solution.py:225
  42.3 0.0 collective-permute-done.2.arrived
  42.3 1.0 %shard_map.62 = (f32[8,128]{1,0:T(8,128)S(1)}, f32[8,128]{1,0:T(8,128)S(1)}) custom-call(bf16[256,1024]{1,0:T(8,128)(2,1)S(1)} %collective-permute-done.2.arrived, bf16[1024,1024]{1,0:T(8,128)(2,1)S(1)} %get-tuple-element.30.units, f32[7,4,128]{2,1,0:T(4,128)S(1)} %get-tuple-element.31.live, f32[7,8,128]{2,1,0:T(8,128)S(1)} %get-tuple-element.32.mine, ...), custom_call_target="tpu_custom_call" | custom-call | tf_op jit(solution)/shard_map/pallas_call | solution.py:191
  43.3 0.3 collective-permute-start.9
  43.6 0.0 collective-permute-start.10
  43.6 0.0 collective-permute-done.1.arrived
  43.6 5.3 %collective-permute-start.11 = (f32[8,128]{1,0:T(8,128)S(1)}, f32[8,128]{1,0:T(8,128)S(1)}, u32[]{:S(2)}, u32[]{:S(2)}) collective-permute-start(f32[8,128]{1,0:T(8,128)S(1)} %get-tuple-element.51), channel_id=1, source_target_pairs={{0,1},{1,0},{2,3},{3,2},{4,5},{5,4},{6,7},{7,6},{8,9},{9,8},{10,11... | collective-permute-start | bytes 12296 | tf_op jit(solution)/shard_map/ppermute | solution.py:225
  49.0 0.0 collective-permute-done.8.rest_0_
  49.0 1.0 %shard_map.63 = (f32[8,128]{1,0:T(8,128)S(1)}, f32[8,128]{1,0:T(8,128)S(1)}) custom-call(bf16[128,1024]{1,0:T(8,128)(2,1)S(1)} %collective-permute-done.1.arrived, bf16[1024,1024]{1,0:T(8,128)(2,1)S(1)} %get-tuple-element.30.units, f32[7,4,128]{2,1,0:T(4,128)S(1)} %get-tuple-element.31.live, f32[7,8,128]{2,1,0:T(8,128)S(1)} %get-tuple-element.32.mine, ...), custom_call_target="tpu_custom_call" | custom-call | tf_op jit(solution)/shard_map/pallas_call | solution.py:191
  49.9 0.0 collective-permute-done.arrived
  50.0 0.0 collective-permute-done.9.rest_0_
  50.0 1.0 %shard_map.64 = (f32[8,128]{1,0:T(8,128)S(1)}, f32[8,128]{1,0:T(8,128)S(1)}) custom-call(bf16[128,1024]{1,0:T(8,128)(2,1)S(1)} %collective-permute-done.arrived, bf16[1024,1024]{1,0:T(8,128)(2,1)S(1)} %get-tuple-element.30.units, f32[7,4,128]{2,1,0:T(4,128)S(1)} %get-tuple-element.31.live, f32[7,8,128]{2,1,0:T(8,128)S(1)} %get-tuple-element.32.mine, ...), custom_call_target="tpu_custom_call" | custom-call | tf_op jit(solution)/shard_map/pallas_call | solution.py:191
  50.9 3.4 %collective-permute-start.12 = (f32[8,128]{1,0:T(8,128)S(1)}, f32[8,128]{1,0:T(8,128)S(1)}, u32[]{:S(2)}, u32[]{:S(2)}) collective-permute-start(f32[8,128]{1,0:T(8,128)S(1)} %get-tuple-element.52), channel_id=1, source_target_pairs={{0,3},{1,2},{2,1},{3,0},{4,7},{5,6},{6,5},{7,4},{8,11},{9,10},{10,... | collective-permute-start | bytes 12296 | tf_op jit(solution)/shard_map/ppermute | solution.py:225
  54.3 0.0 collective-permute-done.10
  54.3 0.0 collective-permute-done.11
  54.3 2.1 %collective-permute-done.12 = f32[8,128]{1,0:T(8,128)S(1)} collective-permute-done((f32[8,128]{1,0:T(8,128)S(1)}, f32[8,128]{1,0:T(8,128)S(1)}, u32[]{:S(2)}, u32[]{:S(2)}) %collective-permute-start.12) | collective-permute-done | bytes 4128 | tf_op jit(solution)/shard_map/ppermute | solution.py:225
  56.4 0.6 %fusion.2 = f32[1024]{0:T(1024)} fusion(f32[8,128]{1,0:T(8,128)S(1)} %collective-permute-done.12, f32[8,128]{1,0:T(8,128)S(1)} %collective-permute-done.11, f32[8,128]{1,0:T(8,128)S(1)} %get-tuple-element.49, f32[8,128]{1,0:T(8,128)S(1)} %collective-permute-done.10, f32[7,8,128]{2,1,0:T(8,128)S(1)} %get-tuple-element.32.mine), kind=kLoop, calls=%fused_computation.3 | loop fusion | flops 7168 | bytes 32768 | tf_op jit(solution)/shard_map/reshape | solution.py:248
  (1 shorter events, 0.0 us)
Async XLA Ops:
  0.0 7.2 %copy-start = (bf16[1024,1024]{1,0:T(8,128)(2,1)S(1)}, bf16[1024,1024]{1,0:T(8,128)(2,1)}, u32[]{:S(2)}) copy-start(bf16[1024,1024]{1,0:T(8,128)(2,1)} %embeds.5) | copy-start | bytes 6291460
  0.0 7.2 %copy-start.2 = (s32[1,4]{1,0:T(1,128)S(1)}, s32[1,4]{1,0:T(1,128)}, u32[]{:S(2)}) copy-start(s32[1,4]{1,0:T(1,128)} %pick_blk.5) | copy-start | bytes 52
  0.0 7.2 %copy-start.1 = (s32[4,4]{1,0:T(4,128)S(1)}, s32[4,4]{1,0:T(4,128)}, u32[]{:S(2)}) copy-start(s32[4,4]{1,0:T(4,128)} %pick_sub.5) | copy-start | bytes 196
  0.0 35.2 %copy-start.3 = (s32[1,16]{1,0:T(1,128)S(1)}, s32[1,16]{1,0:T(1,128)}, u32[]{:S(2)}) copy-start(s32[1,16]{1,0:T(1,128)} %mask_blk.1) | copy-start | bytes 196
  0.0 35.2 %copy-start.4 = (s32[1,16]{1,0:T(1,128)S(1)}, s32[1,16]{1,0:T(1,128)}, u32[]{:S(2)}) copy-start(s32[1,16]{1,0:T(1,128)} %mask_sub.1) | copy-start | bytes 196
  3.0 8.2 %collective-permute-start.6 = (bf16[256,1024]{1,0:T(8,128)(2,1)}, bf16[256,1024]{1,0:T(8,128)(2,1)S(1)}, u32[]{:S(2)}, u32[]{:S(2)}) collective-permute-start(bf16[256,1024]{1,0:T(8,128)(2,1)} %get-tuple-element.38), channel_id=1, source_target_pairs={{0,4},{4,0},{8,12},{12,8},{1,5},{5,1},{9,13},{13,9},{2,6},{6,2},{1... | collective-permute-start | bytes 1572872 | tf_op jit(solution)/shard_map/ppermute | solution.py:225
  3.5 27.9 %collective-permute-start.5 = (bf16[256,1024]{1,0:T(8,128)(2,1)}, bf16[256,1024]{1,0:T(8,128)(2,1)S(1)}, u32[]{:S(2)}, u32[]{:S(2)}) collective-permute-start(bf16[256,1024]{1,0:T(8,128)(2,1)} %get-tuple-element.37), channel_id=1, source_target_pairs={{0,2},{1,3},{2,0},{3,1},{4,6},{5,7},{6,4},{7,5},{8,10},{9,11},{10,... | collective-permute-start | bytes 1572872 | tf_op jit(solution)/shard_map/ppermute | solution.py:225
  8.0 29.4 %collective-permute-start.4 = (bf16[256,1024]{1,0:T(8,128)(2,1)S(1)}, bf16[256,1024]{1,0:T(8,128)(2,1)S(1)}, u32[]{:S(2)}, u32[]{:S(2)}) collective-permute-start(bf16[256,1024]{1,0:T(8,128)(2,1)S(1)} %get-tuple-element.36), channel_id=1, source_target_pairs={{0,1},{1,0},{2,3},{3,2},{4,5},{5,4},{6,7},{7,6},{8,9},{9,8},{10,11... | collective-permute-start | bytes 1572872 | tf_op jit(solution)/shard_map/ppermute | solution.py:225
  9.7 30.1 %collective-permute-start.3 = (bf16[256,1024]{1,0:T(8,128)(2,1)S(1)}, bf16[256,1024]{1,0:T(8,128)(2,1)S(1)}, u32[]{:S(2)}, u32[]{:S(2)}) collective-permute-start(bf16[256,1024]{1,0:T(8,128)(2,1)S(1)} %get-tuple-element.35), channel_id=1, source_target_pairs={{0,8},{4,12},{8,0},{12,4},{1,9},{5,13},{9,1},{13,5},{2,10},{6,14},... | collective-permute-start | bytes 1572872 | tf_op jit(solution)/shard_map/ppermute | solution.py:225
  11.2 31.2 %collective-permute-start.2 = (bf16[256,1024]{1,0:T(8,128)(2,1)S(1)}, bf16[256,1024]{1,0:T(8,128)(2,1)S(1)}, u32[]{:S(2)}, u32[]{:S(2)}) collective-permute-start(bf16[256,1024]{1,0:T(8,128)(2,1)S(1)} %get-tuple-element.34), channel_id=1, source_target_pairs={{0,12},{4,8},{8,4},{12,0},{1,13},{5,9},{9,5},{13,1},{2,14},{6,10},... | collective-permute-start | bytes 1572872 | tf_op jit(solution)/shard_map/ppermute | solution.py:225
  11.2 32.4 %collective-permute-start.1 = (bf16[128,1024]{1,0:T(8,128)(2,1)S(1)}, bf16[128,1024]{1,0:T(8,128)(2,1)S(1)}, u32[]{:S(2)}, u32[]{:S(2)}) collective-permute-start(bf16[128,1024]{1,0:T(8,128)(2,1)S(1)} %get-tuple-element.33), channel_id=1, source_target_pairs={{0,3},{1,2},{2,1},{3,0},{4,7},{5,6},{6,5},{7,4},{8,11},{9,10},{10,... | collective-permute-start | bytes 786440 | tf_op jit(solution)/shard_map/ppermute | solution.py:225
  31.5 18.5 %collective-permute-start = (bf16[128,1024]{1,0:T(8,128)(2,1)S(1)}, bf16[128,1024]{1,0:T(8,128)(2,1)S(1)}, u32[]{:S(2)}, u32[]{:S(2)}) collective-permute-start(bf16[128,1024]{1,0:T(8,128)(2,1)S(1)} %get-tuple-element.29), channel_id=1, source_target_pairs={{0,3},{1,2},{2,1},{3,0},{4,7},{5,6},{6,5},{7,4},{8,11},{9,10},{10,... | collective-permute-start | bytes 786440 | tf_op jit(solution)/shard_map/ppermute | solution.py:225
  37.5 1.2 %collective-permute-start.7 = (f32[8,128]{1,0:T(8,128)S(1)}, f32[8,128]{1,0:T(8,128)S(1)}, u32[]{:S(2)}, u32[]{:S(2)}) collective-permute-start(f32[8,128]{1,0:T(8,128)S(1)} %get-tuple-element.41), channel_id=1, source_target_pairs={{0,4},{4,0},{8,12},{12,8},{1,5},{5,1},{9,13},{13,9},{2,6},{6,2},{1... | collective-permute-start | bytes 12296 | tf_op jit(solution)/shard_map/ppermute | solution.py:225
  40.7 8.2 %collective-permute-start.8 = (f32[8,128]{1,0:T(8,128)S(1)}, f32[8,128]{1,0:T(8,128)S(1)}, u32[]{:S(2)}, u32[]{:S(2)}) collective-permute-start(f32[8,128]{1,0:T(8,128)S(1)} %get-tuple-element.45), channel_id=1, source_target_pairs={{0,8},{4,12},{8,0},{12,4},{1,9},{5,13},{9,1},{13,5},{2,10},{6,14},... | collective-permute-start | bytes 12296 | tf_op jit(solution)/shard_map/ppermute | solution.py:225
  43.3 6.6 %collective-permute-start.9 = (f32[8,128]{1,0:T(8,128)S(1)}, f32[8,128]{1,0:T(8,128)S(1)}, u32[]{:S(2)}, u32[]{:S(2)}) collective-permute-start(f32[8,128]{1,0:T(8,128)S(1)} %get-tuple-element.47), channel_id=1, source_target_pairs={{0,12},{4,8},{8,4},{12,0},{1,13},{5,9},{9,5},{13,1},{2,14},{6,10},... | collective-permute-start | bytes 12296 | tf_op jit(solution)/shard_map/ppermute | solution.py:225
  43.6 10.7 %collective-permute-start.10 = (f32[8,128]{1,0:T(8,128)S(1)}, f32[8,128]{1,0:T(8,128)S(1)}, u32[]{:S(2)}, u32[]{:S(2)}) collective-permute-start(f32[8,128]{1,0:T(8,128)S(1)} %get-tuple-element.50), channel_id=1, source_target_pairs={{0,2},{1,3},{2,0},{3,1},{4,6},{5,7},{6,4},{7,5},{8,10},{9,11},{10,... | collective-permute-start | bytes 12296 | tf_op jit(solution)/shard_map/ppermute | solution.py:225
  43.6 10.7 %collective-permute-start.11 = (f32[8,128]{1,0:T(8,128)S(1)}, f32[8,128]{1,0:T(8,128)S(1)}, u32[]{:S(2)}, u32[]{:S(2)}) collective-permute-start(f32[8,128]{1,0:T(8,128)S(1)} %get-tuple-element.51), channel_id=1, source_target_pairs={{0,1},{1,0},{2,3},{3,2},{4,5},{5,4},{6,7},{7,6},{8,9},{9,8},{10,11... | collective-permute-start | bytes 12296 | tf_op jit(solution)/shard_map/ppermute | solution.py:225
  50.9 5.5 %collective-permute-start.12 = (f32[8,128]{1,0:T(8,128)S(1)}, f32[8,128]{1,0:T(8,128)S(1)}, u32[]{:S(2)}, u32[]{:S(2)}) collective-permute-start(f32[8,128]{1,0:T(8,128)S(1)} %get-tuple-element.52), channel_id=1, source_target_pairs={{0,3},{1,2},{2,1},{3,0},{4,7},{5,6},{6,5},{7,4},{8,11},{9,10},{10,... | collective-permute-start | bytes 12296 | tf_op jit(solution)/shard_map/ppermute | solution.py:225

commit v13 on v11

--- a/solution.py
+++ b/solution.py
@@ -129,7 +129,7 @@
 
 def prepare_kernel(slots, pick_blk, pick_sub, mask_blk, mask_sub, embeds, units, live, mine):
     for start in range(0, embeds.shape[0], BLOCK):
-        units[start : start + BLOCK] = rounded_units(embeds[start : start + BLOCK])
+        units[:, start : start + BLOCK] = rounded_units(embeds[start : start + BLOCK]).T
     count = live.shape[1]
     block_of = lax.broadcasted_iota(jnp.int32, mine.shape[1:], 0) // ROWS
     for place, (axis, step, _, _) in enumerate(slots):
@@ -147,7 +147,7 @@
     return pl.pallas_call(
         functools.partial(prepare_kernel, slots),
         out_shape=[
-            jax.ShapeDtypeStruct(embeds.shape, embeds.dtype),
+            jax.ShapeDtypeStruct(embeds.shape[::-1], embeds.dtype),
             jax.ShapeDtypeStruct((len(slots), count, LANES), jnp.float32),
             jax.ShapeDtypeStruct((len(slots), count * ROWS, LANES), jnp.float32),
         ],
@@ -167,8 +167,7 @@
     x = rounded_units(arrived[...])
     along_rows = jnp.zeros((rows, LANES), jnp.float32)
     for i in range(count):
-        y = units[i * BLOCK : (i + 1) * BLOCK]
-        cosines = lax.dot_general(x, y, (((1,), (1,)), ((), ())), preferred_element_type=jnp.float32)
+        cosines = jnp.dot(x, units[:, i * BLOCK : (i + 1) * BLOCK], preferred_element_type=jnp.float32)
         weights = soft_weights(cosines)
         alive = live[place, i : i + 1]
         parts = [weights[:, part * LANES : (part + 1) * LANES] for part in range(ROWS)]
@@ -206,13 +205,13 @@
 
 
 def plan_slots(sizes):
-    slots = [("blk", 1, 0, BLOCK), ("sub", 2, 0, BLOCK), ("blk", 2, 0, BLOCK)]
+    slots = [("sub", 2, 0, BLOCK), ("blk", 1, 0, BLOCK), ("blk", 2, 0, BLOCK)]
     for k in range(3, sizes["blk"]):
         slots += [("blk", k, 0, FIRST_CUT), ("blk", k, FIRST_CUT, BLOCK - FIRST_CUT)]
-    return slots + [("sub", k, 0, BLOCK) for k in (1, *range(3, sizes["sub"]))]
-
-
-AT_ONCE = 2
+    return slots + [("sub", k, 0, BLOCK) for k in (*range(3, sizes["sub"]), 1)]
+
+
+AT_ONCE = 1
 
 
 def body(embeds, pick_blk, mask_blk, pick_sub, mask_sub):

time: 58 us -> 69.5 us (1.20)
  the two profiles are of different devices: /device:TPU:18 before, /device:TPU:0 now
where the time goes in v13:
time: 69.5 us; the launch traced here: 69.3 us
  waiting for transfers between devices  41.9 us (60%)
  starting transfers between devices  14.6 us (21%)
  Pallas kernels  12.1 us (17%)
    ppermute x13, waiting for transfers between devices, send(): return lax.ppermute(array, slot[0], pairs(slot[1], sizes[slot[0]]))  41.9 us
    ppermute x13, starting transfers between devices, send(): return lax.ppermute(array, slot[0], pairs(slot[1], sizes[slot[0]]))  14.6 us
    pallas_call x7, Pallas kernels, work(): pl.pallas_call(functools.partial(slot_kernel, place, *slot[2:], [one for...  6.47 us
    pallas_call x1, Pallas kernels, first_rows(): pl.pallas_call(functools.partial(first_kernel, slots), out_shape=[jax.Sha...  2.67 us
    pallas_call x1, Pallas kernels, prepare(): pl.pallas_call(functools.partial(prepare_kernel, slots), out_shape=[jax.S...  1.77 us
  transfers between devices with their start and end apart: 13, of which 5 were waited for; matrix products, arithmetic and copies ran while one was open for 0% of the time, Pallas kernels for 14%

profile of v13, /device:TPU:0, one launch (start us, length us, event | category | flops | bytes accessed | tf_op | source)
XLA Modules:
  0.0 69.3 jit_solution(9365211708951785637)
XLA Ops:
  0.0 0.0 copy-start.1
  0.0 0.0 copy-start.2
  0.0 0.0 copy-start
  0.0 0.0 copy-start.4
  0.0 0.0 copy-start.3
  0.0 2.7 %shard_map.57 = bf16[256,1024]{1,0:T(8,128)(2,1)} custom-call(s32[1,4]{1,0:T(1,128)} %pick_blk.5, s32[4,4]{1,0:T(4,128)} %pick_sub.5, bf16[1024,1024]{1,0:T(8,128)(2,1)} %embeds.5), custom_call_target="tpu_custom_call" | custom-call | tf_op jit(solution)/shard_map/pallas_call | solution.py:78
  2.7 4.1 %collective-permute-start.6 = (bf16[256,1024]{1,0:T(8,128)(2,1)}, bf16[256,1024]{1,0:T(8,128)(2,1)S(1)}, u32[]{:S(2)}, u32[]{:S(2)}) collective-permute-start(bf16[256,1024]{1,0:T(8,128)(2,1)} %shard_map.57), channel_id=1, source_target_pairs={{0,2},{1,3},{2,0},{3,1},{4,6},{5,7},{6,4},{7,5},{8,10},{9,11},{10,... | collective-permute-start | bytes 1572872 | tf_op jit(solution)/shard_map/ppermute | solution.py:223
  6.8 0.0 copy-done.1
  6.8 0.0 copy-done.2
  6.8 0.0 copy-done
  6.8 1.2 %shard_map.55 = (bf16[256,1024]{1,0:T(8,128)(2,1)S(1)}, bf16[256,1024]{1,0:T(8,128)(2,1)S(1)}, bf16[240,1024]{1,0:T(8,128)(2,1)S(1)}, bf16[16,1024]{1,0:T(8,128)...) custom-call(s32[1,4]{1,0:T(1,128)S(1)} %copy-done.2, s32[4,4]{1,0:T(4,128)S(1)} %copy-done.1, ...), custom_call_target="tpu_custom_call" | custom-call | tf_op jit(solution)/shard_map/pallas_call | solution.py:115
  8.0 0.1 collective-permute-start.5
  8.1 1.6 %collective-permute-start.4 = (bf16[256,1024]{1,0:T(8,128)(2,1)S(1)}, bf16[256,1024]{1,0:T(8,128)(2,1)S(1)}, u32[]{:S(2)}, u32[]{:S(2)}) collective-permute-start(bf16[256,1024]{1,0:T(8,128)(2,1)S(1)} %get-tuple-element.35), channel_id=1, source_target_pairs={{0,8},{4,12},{8,0},{12,4},{1,9},{5,13},{9,1},{13,5},{2,10},{6,14},... | collective-permute-start | bytes 1572872 | tf_op jit(solution)/shard_map/ppermute | solution.py:223
  9.7 1.3 %collective-permute-start.1 = (bf16[256,1024]{1,0:T(8,128)(2,1)S(1)}, bf16[256,1024]{1,0:T(8,128)(2,1)S(1)}, u32[]{:S(2)}, u32[]{:S(2)}) collective-permute-start(bf16[256,1024]{1,0:T(8,128)(2,1)S(1)} %get-tuple-element.32), channel_id=1, source_target_pairs={{0,3},{1,2},{2,1},{3,0},{4,7},{5,6},{6,5},{7,4},{8,11},{9,10},{10,... | collective-permute-start | bytes 1572872 | tf_op jit(solution)/shard_map/ppermute | solution.py:223
  11.0 0.2 collective-permute-start
  11.2 31.1 %collective-permute-done.6.arrived = bf16[256,1024]{1,0:T(8,128)(2,1)S(1)} collective-permute-done((bf16[256,1024]{1,0:T(8,128)(2,1)}, bf16[256,1024]{1,0:T(8,128)(2,1)S(1)}, u32[]{:S(2)}, u32[]{:S(2)}) %collective-permute-start.6) | collective-permute-done | bytes 524320 | tf_op jit(solution)/shard_map/ppermute | solution.py:223
  42.3 0.0 collective-permute-start.3
  42.3 0.0 collective-permute-done.5.arrived
  42.3 1.7 %collective-permute-start.2 = (bf16[16,1024]{1,0:T(8,128)(2,1)S(1)}, bf16[16,1024]{1,0:T(8,128)(2,1)S(1)}, u32[]{:S(2)}, u32[]{:S(2)}) collective-permute-start(bf16[16,1024]{1,0:T(8,128)(2,1)S(1)} %get-tuple-element.33), channel_id=1, source_target_pairs={{0,12},{4,8},{8,4},{12,0},{1,13},{5,9},{9,5},{13,1},{2,14},{6,10},... | collective-permute-start | bytes 98312 | tf_op jit(solution)/shard_map/ppermute | solution.py:223
  44.0 0.0 copy-done.4
  44.0 0.0 copy-done.3
  44.0 1.8 %shard_map.56 = (bf16[1024,1024]{1,0:T(8,128)(2,1)S(1)}, f32[7,4,128]{2,1,0:T(4,128)S(1)}, f32[7,8,128]{2,1,0:T(8,128)S(1)}) custom-call(s32[1,4]{1,0:T(1,128)S(1)} %copy-done.2, s32[4,4]{1,0:T(4,128)S(1)} %copy-done.1, s32[1,16]{1,0:T(1,128)S(1)} %copy-done.3, s32[1,16]{1,0:T(1,128)S(1)} %copy-done.4, bf16[1024,1024]{1,0:T(8,128)(2,1)S(1)} %copy-done), custom_call_target="tpu_custom_call" | custom-call | tf_op jit(solution)/shard_map/pallas_call | solution.py:147
  45.8 1.0 %shard_map.58 = (f32[8,128]{1,0:T(8,128)S(1)}, f32[8,128]{1,0:T(8,128)S(1)}) custom-call(bf16[256,1024]{1,0:T(8,128)(2,1)S(1)} %collective-permute-done.6.arrived, bf16[1024,1024]{1,0:T(8,128)(2,1)S(1)} %get-tuple-element.29.units, f32[7,4,128]{2,1,0:T(4,128)S(1)} %get-tuple-element.30.live, f32[7,8,128]{2,1,0:T(8,128)S(1)} %get-tuple-element.31.mine, ...), custom_call_target="tpu_custom_call" | custom-call | tf_op jit(solution)/shard_map/pallas_call | solution.py:190
  46.8 1.0 %shard_map.59 = (f32[8,128]{1,0:T(8,128)S(1)}, f32[8,128]{1,0:T(8,128)S(1)}) custom-call(bf16[256,1024]{1,0:T(8,128)(2,1)S(1)} %collective-permute-done.5.arrived, bf16[1024,1024]{1,0:T(8,128)(2,1)S(1)} %get-tuple-element.29.units, f32[7,4,128]{2,1,0:T(4,128)S(1)} %get-tuple-element.30.live, f32[7,8,128]{2,1,0:T(8,128)S(1)} %get-tuple-element.31.mine, ...), custom_call_target="tpu_custom_call" | custom-call | tf_op jit(solution)/shard_map/pallas_call | solution.py:190
  47.8 0.0 collective-permute-done.4.arrived
  47.8 0.3 collective-permute-start.7
  48.1 1.0 %shard_map.60 = (f32[8,128]{1,0:T(8,128)S(1)}, f32[8,128]{1,0:T(8,128)S(1)}) custom-call(bf16[256,1024]{1,0:T(8,128)(2,1)S(1)} %collective-permute-done.4.arrived, bf16[1024,1024]{1,0:T(8,128)(2,1)S(1)} %get-tuple-element.29.units, f32[7,4,128]{2,1,0:T(4,128)S(1)} %get-tuple-element.30.live, f32[7,8,128]{2,1,0:T(8,128)S(1)} %get-tuple-element.31.mine, ...), custom_call_target="tpu_custom_call" | custom-call | tf_op jit(solution)/shard_map/pallas_call | solution.py:190
  49.1 6.4 %collective-permute-done.3.arrived = bf16[240,1024]{1,0:T(8,128)(2,1)S(1)} collective-permute-done((bf16[240,1024]{1,0:T(8,128)(2,1)S(1)}, bf16[240,1024]{1,0:T(8,128)(2,1)S(1)}, u32[]{:S(2)}, u32[]{:S(2)}) %collective-permute-start.3) | collective-permute-done | bytes 491552 | tf_op jit(solution)/shard_map/ppermute | solution.py:223
  55.5 1.2 %collective-permute-start.8 = (f32[8,128]{1,0:T(8,128)S(1)}, f32[8,128]{1,0:T(8,128)S(1)}, u32[]{:S(2)}, u32[]{:S(2)}) collective-permute-start(f32[8,128]{1,0:T(8,128)S(1)} %get-tuple-element.42), channel_id=1, source_target_pairs={{0,8},{4,12},{8,0},{12,4},{1,9},{5,13},{9,1},{13,5},{2,10},{6,14},... | collective-permute-start | bytes 12296 | tf_op jit(solution)/shard_map/ppermute | solution.py:223
  56.7 0.0 collective-permute-done.7.rest_0_
  56.7 0.9 %shard_map.61 = (f32[8,128]{1,0:T(8,128)S(1)}, f32[8,128]{1,0:T(8,128)S(1)}) custom-call(bf16[240,1024]{1,0:T(8,128)(2,1)S(1)} %collective-permute-done.3.arrived, bf16[1024,1024]{1,0:T(8,128)(2,1)S(1)} %get-tuple-element.29.units, f32[7,4,128]{2,1,0:T(4,128)S(1)} %get-tuple-element.30.live, f32[7,8,128]{2,1,0:T(8,128)S(1)} %get-tuple-element.31.mine, ...), custom_call_target="tpu_custom_call" | custom-call | tf_op jit(solution)/shard_map/pallas_call | solution.py:190
  57.7 0.0 collective-permute-done.2.arrived
  57.7 1.4 %collective-permute-done.8.rest_0_ = f32[8,128]{1,0:T(8,128)S(1)} collective-permute-done((f32[8,128]{1,0:T(8,128)S(1)}, f32[8,128]{1,0:T(8,128)S(1)}, u32[]{:S(2)}, u32[]{:S(2)}) %collective-permute-start.8) | collective-permute-done | bytes 4128 | tf_op jit(solution)/shard_map/ppermute | solution.py:223
  59.1 0.5 shard_map.62
  59.7 0.1 collective-permute-start.9
  59.7 0.1 collective-permute-start.10
  59.8 0.0 collective-permute-done.1.arrived
  59.8 1.0 %shard_map.63 = (f32[8,128]{1,0:T(8,128)S(1)}, f32[8,128]{1,0:T(8,128)S(1)}) custom-call(bf16[256,1024]{1,0:T(8,128)(2,1)S(1)} %collective-permute-done.1.arrived, bf16[1024,1024]{1,0:T(8,128)(2,1)S(1)} %get-tuple-element.29.units, f32[7,4,128]{2,1,0:T(4,128)S(1)} %get-tuple-element.30.live, f32[7,8,128]{2,1,0:T(8,128)S(1)} %get-tuple-element.31.mine, ...), custom_call_target="tpu_custom_call" | custom-call | tf_op jit(solution)/shard_map/pallas_call | solution.py:190
  60.8 3.2 %collective-permute-start.11 = (f32[8,128]{1,0:T(8,128)S(1)}, f32[8,128]{1,0:T(8,128)S(1)}, u32[]{:S(2)}, u32[]{:S(2)}) collective-permute-start(f32[8,128]{1,0:T(8,128)S(1)} %get-tuple-element.49), channel_id=1, source_target_pairs={{0,3},{1,2},{2,1},{3,0},{4,7},{5,6},{6,5},{7,4},{8,11},{9,10},{10,... | collective-permute-start | bytes 12296 | tf_op jit(solution)/shard_map/ppermute | solution.py:223
  64.1 0.0 collective-permute-done.arrived
  64.1 0.0 collective-permute-done.9.rest_0_
  64.1 1.0 %shard_map.64 = (f32[8,128]{1,0:T(8,128)S(1)}, f32[8,128]{1,0:T(8,128)S(1)}) custom-call(bf16[256,1024]{1,0:T(8,128)(2,1)S(1)} %collective-permute-done.arrived, bf16[1024,1024]{1,0:T(8,128)(2,1)S(1)} %get-tuple-element.29.units, f32[7,4,128]{2,1,0:T(4,128)S(1)} %get-tuple-element.30.live, f32[7,8,128]{2,1,0:T(8,128)S(1)} %get-tuple-element.31.mine, ...), custom_call_target="tpu_custom_call" | custom-call | tf_op jit(solution)/shard_map/pallas_call | solution.py:190
  65.1 0.7 collective-permute-start.12
  65.7 0.0 collective-permute-done.10
  65.7 0.6 collective-permute-done.11
  66.3 2.4 %collective-permute-done.12 = f32[8,128]{1,0:T(8,128)S(1)} collective-permute-done((f32[8,128]{1,0:T(8,128)S(1)}, f32[8,128]{1,0:T(8,128)S(1)}, u32[]{:S(2)}, u32[]{:S(2)}) %collective-permute-start.12) | collective-permute-done | bytes 4128 | tf_op jit(solution)/shard_map/ppermute | solution.py:223
  68.7 0.6 fusion.2
  (1 shorter events, 0.0 us)
Async XLA Ops:
  0.0 6.8 %copy-start.1 = (s32[4,4]{1,0:T(4,128)S(1)}, s32[4,4]{1,0:T(4,128)}, u32[]{:S(2)}) copy-start(s32[4,4]{1,0:T(4,128)} %pick_sub.5) | copy-start | bytes 196
  0.0 6.8 %copy-start.2 = (s32[1,4]{1,0:T(1,128)S(1)}, s32[1,4]{1,0:T(1,128)}, u32[]{:S(2)}) copy-start(s32[1,4]{1,0:T(1,128)} %pick_blk.5) | copy-start | bytes 52
  0.0 6.8 %copy-start = (bf16[1024,1024]{1,0:T(8,128)(2,1)S(1)}, bf16[1024,1024]{1,0:T(8,128)(2,1)}, u32[]{:S(2)}) copy-start(bf16[1024,1024]{1,0:T(8,128)(2,1)} %embeds.5) | copy-start | bytes 6291460
  0.0 44.0 %copy-start.4 = (s32[1,16]{1,0:T(1,128)S(1)}, s32[1,16]{1,0:T(1,128)}, u32[]{:S(2)}) copy-start(s32[1,16]{1,0:T(1,128)} %mask_sub.1) | copy-start | bytes 196
  0.0 44.0 %copy-start.3 = (s32[1,16]{1,0:T(1,128)S(1)}, s32[1,16]{1,0:T(1,128)}, u32[]{:S(2)}) copy-start(s32[1,16]{1,0:T(1,128)} %mask_blk.1) | copy-start | bytes 196
  2.7 39.6 %collective-permute-start.6 = (bf16[256,1024]{1,0:T(8,128)(2,1)}, bf16[256,1024]{1,0:T(8,128)(2,1)S(1)}, u32[]{:S(2)}, u32[]{:S(2)}) collective-permute-start(bf16[256,1024]{1,0:T(8,128)(2,1)} %shard_map.57), channel_id=1, source_target_pairs={{0,2},{1,3},{2,0},{3,1},{4,6},{5,7},{6,4},{7,5},{8,10},{9,11},{10,... | collective-permute-start | bytes 1572872 | tf_op jit(solution)/shard_map/ppermute | solution.py:223
  8.0 34.3 %collective-permute-start.5 = (bf16[256,1024]{1,0:T(8,128)(2,1)S(1)}, bf16[256,1024]{1,0:T(8,128)(2,1)S(1)}, u32[]{:S(2)}, u32[]{:S(2)}) collective-permute-start(bf16[256,1024]{1,0:T(8,128)(2,1)S(1)} %get-tuple-element.36), channel_id=1, source_target_pairs={{0,4},{4,0},{8,12},{12,8},{1,5},{5,1},{9,13},{13,9},{2,6},{6,2},{1... | collective-permute-start | bytes 1572872 | tf_op jit(solution)/shard_map/ppermute | solution.py:223
  8.1 39.7 %collective-permute-start.4 = (bf16[256,1024]{1,0:T(8,128)(2,1)S(1)}, bf16[256,1024]{1,0:T(8,128)(2,1)S(1)}, u32[]{:S(2)}, u32[]{:S(2)}) collective-permute-start(bf16[256,1024]{1,0:T(8,128)(2,1)S(1)} %get-tuple-element.35), channel_id=1, source_target_pairs={{0,8},{4,12},{8,0},{12,4},{1,9},{5,13},{9,1},{13,5},{2,10},{6,14},... | collective-permute-start | bytes 1572872 | tf_op jit(solution)/shard_map/ppermute | solution.py:223
  9.7 50.2 %collective-permute-start.1 = (bf16[256,1024]{1,0:T(8,128)(2,1)S(1)}, bf16[256,1024]{1,0:T(8,128)(2,1)S(1)}, u32[]{:S(2)}, u32[]{:S(2)}) collective-permute-start(bf16[256,1024]{1,0:T(8,128)(2,1)S(1)} %get-tuple-element.32), channel_id=1, source_target_pairs={{0,3},{1,2},{2,1},{3,0},{4,7},{5,6},{6,5},{7,4},{8,11},{9,10},{10,... | collective-permute-start | bytes 1572872 | tf_op jit(solution)/shard_map/ppermute | solution.py:223
  11.0 53.1 %collective-permute-start = (bf16[256,1024]{1,0:T(8,128)(2,1)S(1)}, bf16[256,1024]{1,0:T(8,128)(2,1)S(1)}, u32[]{:S(2)}, u32[]{:S(2)}) collective-permute-start(bf16[256,1024]{1,0:T(8,128)(2,1)S(1)} %get-tuple-element.28), channel_id=1, source_target_pairs={{0,1},{1,0},{2,3},{3,2},{4,5},{5,4},{6,7},{7,6},{8,9},{9,8},{10,11... | collective-permute-start | bytes 1572872 | tf_op jit(solution)/shard_map/ppermute | solution.py:223
  42.3 13.2 %collective-permute-start.3 = (bf16[240,1024]{1,0:T(8,128)(2,1)S(1)}, bf16[240,1024]{1,0:T(8,128)(2,1)S(1)}, u32[]{:S(2)}, u32[]{:S(2)}) collective-permute-start(bf16[240,1024]{1,0:T(8,128)(2,1)S(1)} %get-tuple-element.34), channel_id=1, source_target_pairs={{0,12},{4,8},{8,4},{12,0},{1,13},{5,9},{9,5},{13,1},{2,14},{6,10},... | collective-permute-start | bytes 1474568 | tf_op jit(solution)/shard_map/ppermute | solution.py:223
  42.3 15.4 %collective-permute-start.2 = (bf16[16,1024]{1,0:T(8,128)(2,1)S(1)}, bf16[16,1024]{1,0:T(8,128)(2,1)S(1)}, u32[]{:S(2)}, u32[]{:S(2)}) collective-permute-start(bf16[16,1024]{1,0:T(8,128)(2,1)S(1)} %get-tuple-element.33), channel_id=1, source_target_pairs={{0,12},{4,8},{8,4},{12,0},{1,13},{5,9},{9,5},{13,1},{2,14},{6,10},... | collective-permute-start | bytes 98312 | tf_op jit(solution)/shard_map/ppermute | solution.py:223
  47.8 8.9 %collective-permute-start.7 = (f32[8,128]{1,0:T(8,128)S(1)}, f32[8,128]{1,0:T(8,128)S(1)}, u32[]{:S(2)}, u32[]{:S(2)}) collective-permute-start(f32[8,128]{1,0:T(8,128)S(1)} %get-tuple-element.40), channel_id=1, source_target_pairs={{0,4},{4,0},{8,12},{12,8},{1,5},{5,1},{9,13},{13,9},{2,6},{6,2},{1... | collective-permute-start | bytes 12296 | tf_op jit(solution)/shard_map/ppermute | solution.py:223
  55.5 3.6 %collective-permute-start.8 = (f32[8,128]{1,0:T(8,128)S(1)}, f32[8,128]{1,0:T(8,128)S(1)}, u32[]{:S(2)}, u32[]{:S(2)}) collective-permute-start(f32[8,128]{1,0:T(8,128)S(1)} %get-tuple-element.42), channel_id=1, source_target_pairs={{0,8},{4,12},{8,0},{12,4},{1,9},{5,13},{9,1},{13,5},{2,10},{6,14},... | collective-permute-start | bytes 12296 | tf_op jit(solution)/shard_map/ppermute | solution.py:223
  59.7 4.4 %collective-permute-start.9 = (f32[8,128]{1,0:T(8,128)S(1)}, f32[8,128]{1,0:T(8,128)S(1)}, u32[]{:S(2)}, u32[]{:S(2)}) collective-permute-start(f32[8,128]{1,0:T(8,128)S(1)} %get-tuple-element.46), channel_id=1, source_target_pairs={{0,12},{4,8},{8,4},{12,0},{1,13},{5,9},{9,5},{13,1},{2,14},{6,10},... | collective-permute-start | bytes 12296 | tf_op jit(solution)/shard_map/ppermute | solution.py:223
  59.7 6.0 %collective-permute-start.10 = (f32[8,128]{1,0:T(8,128)S(1)}, f32[8,128]{1,0:T(8,128)S(1)}, u32[]{:S(2)}, u32[]{:S(2)}) collective-permute-start(f32[8,128]{1,0:T(8,128)S(1)} %get-tuple-element.48), channel_id=1, source_target_pairs={{0,2},{1,3},{2,0},{3,1},{4,6},{5,7},{6,4},{7,5},{8,10},{9,11},{10,... | collective-permute-start | bytes 12296 | tf_op jit(solution)/shard_map/ppermute | solution.py:223
  60.8 5.5 %collective-permute-start.11 = (f32[8,128]{1,0:T(8,128)S(1)}, f32[8,128]{1,0:T(8,128)S(1)}, u32[]{:S(2)}, u32[]{:S(2)}) collective-permute-start(f32[8,128]{1,0:T(8,128)S(1)} %get-tuple-element.49), channel_id=1, source_target_pairs={{0,3},{1,2},{2,1},{3,0},{4,7},{5,6},{6,5},{7,4},{8,11},{9,10},{10,... | collective-permute-start | bytes 12296 | tf_op jit(solution)/shard_map/ppermute | solution.py:223
  65.1 3.7 %collective-permute-start.12 = (f32[8,128]{1,0:T(8,128)S(1)}, f32[8,128]{1,0:T(8,128)S(1)}, u32[]{:S(2)}, u32[]{:S(2)}) collective-permute-start(f32[8,128]{1,0:T(8,128)S(1)} %get-tuple-element.50), channel_id=1, source_target_pairs={{0,1},{1,0},{2,3},{3,2},{4,5},{5,4},{6,7},{7,6},{8,9},{9,8},{10,11... | collective-permute-start | bytes 12296 | tf_op jit(solution)/shard_map/ppermute | solution.py:223

commit v14 on v13

--- a/solution.py
+++ b/solution.py
@@ -50,43 +50,46 @@
     ]
     for copy in scalars:
         copy.start()
-    for copy in scalars:
-        copy.wait()
-    entering, leaving = [], []
-    for place, (axis, step, first, rows) in enumerate(slots):
-        pick = take_pick(axis, step, blk_scalars, sub_scalars)
-        for start in range(0, rows, PART):
-            source = pl.multiple_of(pick * BLOCK + (first + start), PART)
-            here = staged.at[place, pl.ds(start, PART)]
-            number = len(entering)
-            entering.append(pltpu.make_async_copy(embeds.at[pl.ds(source, PART)], here, in_sems.at[number]))
-            leaving.append(pltpu.make_async_copy(here, outs[place].at[pl.ds(start, PART)], out_sems.at[number]))
+    starts = range(0, BLOCK, PART)
+    entering = []
+    for start in starts:
+        for top in range(start, embeds.shape[0], BLOCK):
+            rows = pl.ds(top, PART)
+            entering.append(pltpu.make_async_copy(embeds.at[rows], staged.at[rows], in_sems.at[len(entering)]))
             entering[-1].start()
-    for copy, onward in zip(entering, leaving):
-        copy.wait()
-        onward.start()
-    for onward in leaving:
-        onward.wait()
+    for copy in scalars:
+        copy.wait()
+    picks = [take_pick(axis, step, blk_scalars, sub_scalars) for axis, step, _, _ in slots]
+    count = embeds.shape[0] // BLOCK
+    leaving = []
+    for turn, start in enumerate(starts):
+        for copy in entering[turn * count : (turn + 1) * count]:
+            copy.wait()
+        for pick, out in zip(picks, outs):
+            here = staged.at[pl.ds(pl.multiple_of(pick * BLOCK + start, PART), PART)]
+            leaving.append(pltpu.make_async_copy(here, out.at[pl.ds(start, PART)], out_sems.at[len(leaving)]))
+            leaving[-1].start()
+    for copy in leaving:
+        copy.wait()
 
 
 PART = 64
 
 
 def first_rows(slots, pick_blk, pick_sub, embeds):
-    shape = (BLOCK, embeds.shape[1])
-    parts = len(slots) * (BLOCK // PART)
+    parts = BLOCK // PART
     return pl.pallas_call(
         functools.partial(first_kernel, slots),
-        out_shape=[jax.ShapeDtypeStruct(shape, embeds.dtype)] * len(slots),
+        out_shape=[jax.ShapeDtypeStruct((BLOCK, embeds.shape[1]), embeds.dtype)] * len(slots),
         in_specs=[ANY] * 3,
         out_specs=[ANY] * len(slots),
         scratch_shapes=[
             pltpu.SMEM(pick_blk.shape, jnp.int32),
             pltpu.SMEM(pick_sub.shape, jnp.int32),
-            pltpu.VMEM((len(slots), *shape), embeds.dtype),
+            pltpu.VMEM(embeds.shape, embeds.dtype),
             pltpu.SemaphoreType.DMA((2,)),
-            pltpu.SemaphoreType.DMA((parts,)),
-            pltpu.SemaphoreType.DMA((parts,)),
+            pltpu.SemaphoreType.DMA((embeds.shape[0] // PART,)),
+            pltpu.SemaphoreType.DMA((len(slots) * parts,)),
         ],
     )(pick_blk, pick_sub, embeds)
 
@@ -204,14 +207,18 @@
 FIRST_CUT = 240
 
 
+FIRST_CUT = 240
+
+
 def plan_slots(sizes):
-    slots = [("sub", 2, 0, BLOCK), ("blk", 1, 0, BLOCK), ("blk", 2, 0, BLOCK)]
-    for k in range(3, sizes["blk"]):
-        slots += [("blk", k, 0, FIRST_CUT), ("blk", k, FIRST_CUT, BLOCK - FIRST_CUT)]
-    return slots + [("sub", k, 0, BLOCK) for k in (*range(3, sizes["sub"]), 1)]
-
-
-AT_ONCE = 1
+    slots = [("blk", 1, 0, BLOCK), ("sub", 2, 0, BLOCK)]
+    slots += [("blk", k, 0, BLOCK) for k in range(2, sizes["blk"])]
+    for k in (1, *range(3, sizes["sub"])):
+        slots += [("sub", k, 0, FIRST_CUT), ("sub", k, FIRST_CUT, BLOCK - FIRST_CUT)]
+    return slots
+
+
+AT_ONCE = 2
 
 
 def body(embeds, pick_blk, mask_blk, pick_sub, mask_sub):
@@ -229,18 +236,23 @@
     units, live, mine = prepare(slots, pick_blk, pick_sub, mask_blk, mask_sub, embeds)
     totals = jnp.zeros((count * ROWS, LANES), jnp.float32)
     carried = {}
-    soon, late = [], []
+    waiting, late = [], []
     for place, slot in enumerate(slots):
         axis, step, first, rows = slot
-        done = len(soon) if place == len(slots) - 1 else sum(sent <= place - BEHIND for sent, _ in soon)
-        ready, soon = soon[:done], soon[done:]
+        last = place == len(slots) - 1
+        ready = [one for one in waiting if last or one[0] <= place]
+        waiting = [one for one in waiting if not last and one[0] > place]
         totals, back = work(
-            place, slot, arrived[place], units, live, mine, totals, ready, carried.pop((axis, step), None)
+            place, slot, arrived[place], units, live, mine, totals, [one[1:] for one in ready], carried.pop(slot[:2], None)
         )
         if first + rows < BLOCK:
             carried[axis, step] = back
+        elif axis == "blk":
+            waiting.append((place + BEHIND, place, send(back, slot)))
+        elif step == 1 and not last:
+            waiting.append((len(slots), place, send(back, slot)))
         else:
-            (soon if axis == "blk" else late).append((place, send(back, slot)))
+            late.append((place, send(back, slot)))
     for place, sums in late:
         totals = totals + mine[place] * sums
     return (totals * (1.0 / BLOCK)).reshape(-1)

time: 69.5 us -> 64.8 us (0.932)
  waiting for transfers between devices: 41.9 us -> 24.8 us
  starting transfers between devices: 14.6 us -> 26.3 us
  Pallas kernels: 12.1 us -> 12.8 us
    ppermute x13 -> x14, waiting for transfers between devices: 41.9 us -> 24.8 us  [send(): return lax.ppermute(array, slot[0], pairs(slot[1], sizes[slot[0]]))]
    ppermute x13 -> x14, starting transfers between devices: 14.6 us -> 26.3 us  [send(): return lax.ppermute(array, slot[0], pairs(slot[1], sizes[slot[0]]))]
    pallas_call x7 -> x8, Pallas kernels: 6.47 us -> 6.89 us  [work(): pl.pallas_call(functools.partial(slot_kernel, place, *slot[2:], [one for...]
  transfers between devices with their start and end apart: 13 -> 14, of which waited for: 5 -> 6; matrix products, arithmetic and copies ran while one was open for 0% -> 0% of each run, Pallas kernels for 14% -> 16%
where the time goes in v14:
time: 64.8 us; the launch traced here: 64.7 us
  starting transfers between devices  26.3 us (41%)
  waiting for transfers between devices  24.8 us (38%)
  Pallas kernels  12.8 us (20%)
    ppermute x14, starting transfers between devices, send(): return lax.ppermute(array, slot[0], pairs(slot[1], sizes[slot[0]]))  26.3 us
    ppermute x14, waiting for transfers between devices, send(): return lax.ppermute(array, slot[0], pairs(slot[1], sizes[slot[0]]))  24.8 us
    pallas_call x8, Pallas kernels, work(): pl.pallas_call(functools.partial(slot_kernel, place, *slot[2:], [one for...  6.89 us
    pallas_call x1, Pallas kernels, first_rows(): pl.pallas_call(functools.partial(first_kernel, slots), out_shape=[jax.Sha...  2.69 us
    pallas_call x1, Pallas kernels, prepare(): pl.pallas_call(functools.partial(prepare_kernel, slots), out_shape=[jax.S...  1.77 us
    pallas_call x1, Pallas kernels, pick_rows(): pl.pallas_call(functools.partial(pick_kernel, slots), out_shape=[jax.Shap...  1.47 us
  transfers between devices with their start and end apart: 14, of which 6 were waited for; matrix products, arithmetic and copies ran while one was open for 0% of the time, Pallas kernels for 16%

profile of v14, /device:TPU:0, one launch (start us, length us, event | category | flops | bytes accessed | tf_op | source)
XLA Modules:
  0.0 64.7 jit_solution(654134427319601600)
XLA Ops:
  0.0 0.0 copy-start
  0.0 0.0 copy-start.2
  0.0 0.0 copy-start.3
  0.0 2.7 %shard_map.57 = (bf16[256,1024]{1,0:T(8,128)(2,1)}, bf16[256,1024]{1,0:T(8,128)(2,1)}) custom-call(s32[1,4]{1,0:T(1,128)} %pick_blk.5, s32[4,4]{1,0:T(4,128)} %pick_sub.5, bf16[1024,1024]{1,0:T(8,128)(2,1)} %embeds.5), custom_call_target="tpu_custom_call" | custom-call | tf_op jit(solution)/shard_map/pallas_call | solution.py:81
  2.7 0.5 collective-permute-start.7
  3.2 3.7 %collective-permute-start.6 = (bf16[256,1024]{1,0:T(8,128)(2,1)}, bf16[256,1024]{1,0:T(8,128)(2,1)S(1)}, u32[]{:S(2)}, u32[]{:S(2)}) collective-permute-start(bf16[256,1024]{1,0:T(8,128)(2,1)} %get-tuple-element.41), channel_id=1, source_target_pairs={{0,2},{1,3},{2,0},{3,1},{4,6},{5,7},{6,4},{7,5},{8,10},{9,11},{10,... | collective-permute-start | bytes 1572872 | tf_op jit(solution)/shard_map/ppermute | solution.py:230
  6.9 0.0 copy-done
  6.9 0.0 copy-done.2
  6.9 0.0 copy-done.1
  6.9 1.5 %shard_map.55 = (bf16[256,1024]{1,0:T(8,128)(2,1)S(1)}, bf16[256,1024]{1,0:T(8,128)(2,1)S(1)}, bf16[240,1024]{1,0:T(8,128)(2,1)S(1)}, bf16[16,1024]{1,0:T(8,128)...) custom-call(s32[1,4]{1,0:T(1,128)S(1)} %copy-done.2, s32[4,4]{1,0:T(4,128)S(1)} %copy-done.1, ...), custom_call_target="tpu_custom_call" | custom-call | tf_op jit(solution)/shard_map/pallas_call | solution.py:118
  8.4 1.6 %collective-permute-start.5 = (bf16[256,1024]{1,0:T(8,128)(2,1)S(1)}, bf16[256,1024]{1,0:T(8,128)(2,1)S(1)}, u32[]{:S(2)}, u32[]{:S(2)}) collective-permute-start(bf16[256,1024]{1,0:T(8,128)(2,1)S(1)} %get-tuple-element.40), channel_id=1, source_target_pairs={{0,8},{4,12},{8,0},{12,4},{1,9},{5,13},{9,1},{13,5},{2,10},{6,14},... | collective-permute-start | bytes 1572872 | tf_op jit(solution)/shard_map/ppermute | solution.py:230
  10.0 0.0 collective-permute-start.4
  10.0 1.6 %collective-permute-start.3 = (bf16[240,1024]{1,0:T(8,128)(2,1)S(1)}, bf16[240,1024]{1,0:T(8,128)(2,1)S(1)}, u32[]{:S(2)}, u32[]{:S(2)}) collective-permute-start(bf16[240,1024]{1,0:T(8,128)(2,1)S(1)} %get-tuple-element.38), channel_id=1, source_target_pairs={{0,1},{1,0},{2,3},{3,2},{4,5},{5,4},{6,7},{7,6},{8,9},{9,8},{10,11... | collective-permute-start | bytes 1474568 | tf_op jit(solution)/shard_map/ppermute | solution.py:230
  11.6 0.0 collective-permute-done.7.arrived
  11.6 0.2 collective-permute-start.1
  11.8 0.0 copy-done.3
  11.8 0.0 copy-done.4
  11.8 1.8 %shard_map.56 = (bf16[1024,1024]{1,0:T(8,128)(2,1)S(1)}, f32[8,4,128]{2,1,0:T(4,128)S(1)}, f32[8,8,128]{2,1,0:T(8,128)S(1)}) custom-call(s32[1,4]{1,0:T(1,128)S(1)} %copy-done.2, s32[4,4]{1,0:T(4,128)S(1)} %copy-done.1, s32[1,16]{1,0:T(1,128)S(1)} %copy-done.3, s32[1,16]{1,0:T(1,128)S(1)} %copy-done.4, bf16[1024,1024]{1,0:T(8,128)(2,1)S(1)} %copy-done), custom_call_target="tpu_custom_call" | custom-call | tf_op jit(solution)/shard_map/pallas_call | solution.py:150
  13.6 1.0 %shard_map.58 = (f32[8,128]{1,0:T(8,128)S(1)}, f32[8,128]{1,0:T(8,128)S(1)}) custom-call(bf16[256,1024]{1,0:T(8,128)(2,1)S(1)} %collective-permute-done.7.arrived, bf16[1024,1024]{1,0:T(8,128)(2,1)S(1)} %get-tuple-element.33.units, f32[8,4,128]{2,1,0:T(4,128)S(1)} %get-tuple-element.34.live, f32[8,8,128]{2,1,0:T(8,128)S(1)} %get-tuple-element.35.mine, ...), custom_call_target="tpu_custom_call" | custom-call | tf_op jit(solution)/shard_map/pallas_call | solution.py:193
  14.6 16.9 %collective-permute-done.6.arrived = bf16[256,1024]{1,0:T(8,128)(2,1)S(1)} collective-permute-done((bf16[256,1024]{1,0:T(8,128)(2,1)}, bf16[256,1024]{1,0:T(8,128)(2,1)S(1)}, u32[]{:S(2)}, u32[]{:S(2)}) %collective-permute-start.6) | collective-permute-done | bytes 524320 | tf_op jit(solution)/shard_map/ppermute | solution.py:230
  31.5 10.8 %collective-permute-start.2 = (bf16[16,1024]{1,0:T(8,128)(2,1)S(1)}, bf16[16,1024]{1,0:T(8,128)(2,1)S(1)}, u32[]{:S(2)}, u32[]{:S(2)}) collective-permute-start(bf16[16,1024]{1,0:T(8,128)(2,1)S(1)} %get-tuple-element.37), channel_id=1, source_target_pairs={{0,1},{1,0},{2,3},{3,2},{4,5},{5,4},{6,7},{7,6},{8,9},{9,8},{10,11... | collective-permute-start | bytes 98312 | tf_op jit(solution)/shard_map/ppermute | solution.py:230
  42.3 0.0 collective-permute-done.5.arrived
  42.3 0.0 collective-permute-start.8
  42.3 1.2 %collective-permute-done.8.rest_0_ = f32[8,128]{1,0:T(8,128)S(1)} collective-permute-done((f32[8,128]{1,0:T(8,128)S(1)}, f32[8,128]{1,0:T(8,128)S(1)}, u32[]{:S(2)}, u32[]{:S(2)}) %collective-permute-start.8) | collective-permute-done | bytes 4128 | tf_op jit(solution)/shard_map/ppermute | solution.py:230
  43.5 2.7 %collective-permute-start = (bf16[16,1024]{1,0:T(8,128)(2,1)S(1)}, bf16[16,1024]{1,0:T(8,128)(2,1)S(1)}, u32[]{:S(2)}, u32[]{:S(2)}) collective-permute-start(bf16[16,1024]{1,0:T(8,128)(2,1)S(1)} %get-tuple-element.32), channel_id=1, source_target_pairs={{0,3},{1,2},{2,1},{3,0},{4,7},{5,6},{6,5},{7,4},{8,11},{9,10},{10,... | collective-permute-start | bytes 98312 | tf_op jit(solution)/shard_map/ppermute | solution.py:230
  46.2 1.0 %shard_map.59 = (f32[8,128]{1,0:T(8,128)S(1)}, f32[8,128]{1,0:T(8,128)S(1)}) custom-call(bf16[256,1024]{1,0:T(8,128)(2,1)S(1)} %collective-permute-done.6.arrived, bf16[1024,1024]{1,0:T(8,128)(2,1)S(1)} %get-tuple-element.33.units, f32[8,4,128]{2,1,0:T(4,128)S(1)} %get-tuple-element.34.live, f32[8,8,128]{2,1,0:T(8,128)S(1)} %get-tuple-element.35.mine, ...), custom_call_target="tpu_custom_call" | custom-call | tf_op jit(solution)/shard_map/pallas_call | solution.py:193
  47.2 1.0 %shard_map.60 = (f32[8,128]{1,0:T(8,128)S(1)}, f32[8,128]{1,0:T(8,128)S(1)}) custom-call(bf16[256,1024]{1,0:T(8,128)(2,1)S(1)} %collective-permute-done.5.arrived, bf16[1024,1024]{1,0:T(8,128)(2,1)S(1)} %get-tuple-element.33.units, f32[8,4,128]{2,1,0:T(4,128)S(1)} %get-tuple-element.34.live, f32[8,8,128]{2,1,0:T(8,128)S(1)} %get-tuple-element.35.mine, ...), custom_call_target="tpu_custom_call" | custom-call | tf_op jit(solution)/shard_map/pallas_call | solution.py:193
  48.2 0.0 collective-permute-done.4.arrived
  48.2 1.6 %collective-permute-start.9 = (f32[8,128]{1,0:T(8,128)S(1)}, f32[8,128]{1,0:T(8,128)S(1)}, u32[]{:S(2)}, u32[]{:S(2)}) collective-permute-start(f32[8,128]{1,0:T(8,128)S(1)} %get-tuple-element.48), channel_id=1, source_target_pairs={{0,8},{4,12},{8,0},{12,4},{1,9},{5,13},{9,1},{13,5},{2,10},{6,14},... | collective-permute-start | bytes 12296 | tf_op jit(solution)/shard_map/ppermute | solution.py:230
  49.8 1.0 %shard_map.61 = (f32[8,128]{1,0:T(8,128)S(1)}, f32[8,128]{1,0:T(8,128)S(1)}) custom-call(bf16[256,1024]{1,0:T(8,128)(2,1)S(1)} %collective-permute-done.4.arrived, bf16[1024,1024]{1,0:T(8,128)(2,1)S(1)} %get-tuple-element.33.units, f32[8,4,128]{2,1,0:T(4,128)S(1)} %get-tuple-element.34.live, f32[8,8,128]{2,1,0:T(8,128)S(1)} %get-tuple-element.35.mine, ...), custom_call_target="tpu_custom_call" | custom-call | tf_op jit(solution)/shard_map/pallas_call | solution.py:193
  50.8 0.0 collective-permute-done.3.arrived
  50.8 0.1 collective-permute-start.10
  50.8 1.0 %collective-permute-done.9.rest_0_ = f32[8,128]{1,0:T(8,128)S(1)} collective-permute-done((f32[8,128]{1,0:T(8,128)S(1)}, f32[8,128]{1,0:T(8,128)S(1)}, u32[]{:S(2)}, u32[]{:S(2)}) %collective-permute-start.9) | collective-permute-done | bytes 4128 | tf_op jit(solution)/shard_map/ppermute | solution.py:230
  51.9 1.0 %shard_map.62 = (f32[8,128]{1,0:T(8,128)S(1)}, f32[8,128]{1,0:T(8,128)S(1)}) custom-call(bf16[240,1024]{1,0:T(8,128)(2,1)S(1)} %collective-permute-done.3.arrived, bf16[1024,1024]{1,0:T(8,128)(2,1)S(1)} %get-tuple-element.33.units, f32[8,4,128]{2,1,0:T(4,128)S(1)} %get-tuple-element.34.live, f32[8,8,128]{2,1,0:T(8,128)S(1)} %get-tuple-element.35.mine, ...), custom_call_target="tpu_custom_call" | custom-call | tf_op jit(solution)/shard_map/pallas_call | solution.py:193
  52.8 0.0 collective-permute-done.2.arrived
  52.8 1.0 %collective-permute-done.10.rest_0_ = f32[8,128]{1,0:T(8,128)S(1)} collective-permute-done((f32[8,128]{1,0:T(8,128)S(1)}, f32[8,128]{1,0:T(8,128)S(1)}, u32[]{:S(2)}, u32[]{:S(2)}) %collective-permute-start.10) | collective-permute-done | bytes 4128 | tf_op jit(solution)/shard_map/ppermute | solution.py:230
  53.9 0.5 shard_map.63
  54.4 1.2 %collective-permute-start.11 = (f32[8,128]{1,0:T(8,128)S(1)}, f32[8,128]{1,0:T(8,128)S(1)}, u32[]{:S(2)}, u32[]{:S(2)}) collective-permute-start(f32[8,128]{1,0:T(8,128)S(1)} %get-tuple-element.54), channel_id=1, source_target_pairs={{0,1},{1,0},{2,3},{3,2},{4,5},{5,4},{6,7},{7,6},{8,9},{9,8},{10,11... | collective-permute-start | bytes 12296 | tf_op jit(solution)/shard_map/ppermute | solution.py:230
  55.6 0.5 collective-permute-start.12
  56.1 0.0 collective-permute-done.1.arrived
  56.1 0.9 %shard_map.64 = (f32[8,128]{1,0:T(8,128)S(1)}, f32[8,128]{1,0:T(8,128)S(1)}) custom-call(bf16[240,1024]{1,0:T(8,128)(2,1)S(1)} %collective-permute-done.1.arrived, bf16[1024,1024]{1,0:T(8,128)(2,1)S(1)} %get-tuple-element.33.units, f32[8,4,128]{2,1,0:T(4,128)S(1)} %get-tuple-element.34.live, f32[8,8,128]{2,1,0:T(8,128)S(1)} %get-tuple-element.35.mine, ...), custom_call_target="tpu_custom_call" | custom-call | tf_op jit(solution)/shard_map/pallas_call | solution.py:193
  57.1 0.0 collective-permute-done.arrived
  57.1 1.0 %collective-permute-done.11.rest_0_ = f32[8,128]{1,0:T(8,128)S(1)} collective-permute-done((f32[8,128]{1,0:T(8,128)S(1)}, f32[8,128]{1,0:T(8,128)S(1)}, u32[]{:S(2)}, u32[]{:S(2)}) %collective-permute-start.11) | collective-permute-done | bytes 4128 | tf_op jit(solution)/shard_map/ppermute | solution.py:230
  58.1 0.5 shard_map.65
  58.6 1.8 %collective-permute-start.13 = (f32[8,128]{1,0:T(8,128)S(1)}, f32[8,128]{1,0:T(8,128)S(1)}, u32[]{:S(2)}, u32[]{:S(2)}) collective-permute-start(f32[8,128]{1,0:T(8,128)S(1)} %get-tuple-element.58), channel_id=1, source_target_pairs={{0,3},{1,2},{2,1},{3,0},{4,7},{5,6},{6,5},{7,4},{8,11},{9,10},{10,... | collective-permute-start | bytes 12296 | tf_op jit(solution)/shard_map/ppermute | solution.py:230
  60.4 0.0 collective-permute-done.12
  60.4 3.6 %collective-permute-done.13 = f32[8,128]{1,0:T(8,128)S(1)} collective-permute-done((f32[8,128]{1,0:T(8,128)S(1)}, f32[8,128]{1,0:T(8,128)S(1)}, u32[]{:S(2)}, u32[]{:S(2)}) %collective-permute-start.13) | collective-permute-done | bytes 4128 | tf_op jit(solution)/shard_map/ppermute | solution.py:230
  64.1 0.6 fusion.2
  (3 shorter events, 0.0 us)
Async XLA Ops:
  0.0 6.9 %copy-start = (bf16[1024,1024]{1,0:T(8,128)(2,1)S(1)}, bf16[1024,1024]{1,0:T(8,128)(2,1)}, u32[]{:S(2)}) copy-start(bf16[1024,1024]{1,0:T(8,128)(2,1)} %embeds.5) | copy-start | bytes 6291460
  0.0 6.9 %copy-start.2 = (s32[1,4]{1,0:T(1,128)S(1)}, s32[1,4]{1,0:T(1,128)}, u32[]{:S(2)}) copy-start(s32[1,4]{1,0:T(1,128)} %pick_blk.5) | copy-start | bytes 52
  0.0 6.9 %copy-start.1 = (s32[4,4]{1,0:T(4,128)S(1)}, s32[4,4]{1,0:T(4,128)}, u32[]{:S(2)}) copy-start(s32[4,4]{1,0:T(4,128)} %pick_sub.5) | copy-start | bytes 196
  0.0 11.8 %copy-start.3 = (s32[1,16]{1,0:T(1,128)S(1)}, s32[1,16]{1,0:T(1,128)}, u32[]{:S(2)}) copy-start(s32[1,16]{1,0:T(1,128)} %mask_blk.1) | copy-start | bytes 196
  0.0 11.8 %copy-start.4 = (s32[1,16]{1,0:T(1,128)S(1)}, s32[1,16]{1,0:T(1,128)}, u32[]{:S(2)}) copy-start(s32[1,16]{1,0:T(1,128)} %mask_sub.1) | copy-start | bytes 196
  2.7 8.9 %collective-permute-start.7 = (bf16[256,1024]{1,0:T(8,128)(2,1)}, bf16[256,1024]{1,0:T(8,128)(2,1)S(1)}, u32[]{:S(2)}, u32[]{:S(2)}) collective-permute-start(bf16[256,1024]{1,0:T(8,128)(2,1)} %get-tuple-element.42), channel_id=1, source_target_pairs={{0,4},{4,0},{8,12},{12,8},{1,5},{5,1},{9,13},{13,9},{2,6},{6,2},{1... | collective-permute-start | bytes 1572872 | tf_op jit(solution)/shard_map/ppermute | solution.py:230
  3.2 28.3 %collective-permute-start.6 = (bf16[256,1024]{1,0:T(8,128)(2,1)}, bf16[256,1024]{1,0:T(8,128)(2,1)S(1)}, u32[]{:S(2)}, u32[]{:S(2)}) collective-permute-start(bf16[256,1024]{1,0:T(8,128)(2,1)} %get-tuple-element.41), channel_id=1, source_target_pairs={{0,2},{1,3},{2,0},{3,1},{4,6},{5,7},{6,4},{7,5},{8,10},{9,11},{10,... | collective-permute-start | bytes 1572872 | tf_op jit(solution)/shard_map/ppermute | solution.py:230
  8.4 33.9 %collective-permute-start.5 = (bf16[256,1024]{1,0:T(8,128)(2,1)S(1)}, bf16[256,1024]{1,0:T(8,128)(2,1)S(1)}, u32[]{:S(2)}, u32[]{:S(2)}) collective-permute-start(bf16[256,1024]{1,0:T(8,128)(2,1)S(1)} %get-tuple-element.40), channel_id=1, source_target_pairs={{0,8},{4,12},{8,0},{12,4},{1,9},{5,13},{9,1},{13,5},{2,10},{6,14},... | collective-permute-start | bytes 1572872 | tf_op jit(solution)/shard_map/ppermute | solution.py:230
  10.0 38.2 %collective-permute-start.4 = (bf16[256,1024]{1,0:T(8,128)(2,1)S(1)}, bf16[256,1024]{1,0:T(8,128)(2,1)S(1)}, u32[]{:S(2)}, u32[]{:S(2)}) collective-permute-start(bf16[256,1024]{1,0:T(8,128)(2,1)S(1)} %get-tuple-element.39), channel_id=1, source_target_pairs={{0,12},{4,8},{8,4},{12,0},{1,13},{5,9},{9,5},{13,1},{2,14},{6,10},... | collective-permute-start | bytes 1572872 | tf_op jit(solution)/shard_map/ppermute | solution.py:230
  10.0 40.8 %collective-permute-start.3 = (bf16[240,1024]{1,0:T(8,128)(2,1)S(1)}, bf16[240,1024]{1,0:T(8,128)(2,1)S(1)}, u32[]{:S(2)}, u32[]{:S(2)}) collective-permute-start(bf16[240,1024]{1,0:T(8,128)(2,1)S(1)} %get-tuple-element.38), channel_id=1, source_target_pairs={{0,1},{1,0},{2,3},{3,2},{4,5},{5,4},{6,7},{7,6},{8,9},{9,8},{10,11... | collective-permute-start | bytes 1474568 | tf_op jit(solution)/shard_map/ppermute | solution.py:230
  11.6 44.5 %collective-permute-start.1 = (bf16[240,1024]{1,0:T(8,128)(2,1)S(1)}, bf16[240,1024]{1,0:T(8,128)(2,1)S(1)}, u32[]{:S(2)}, u32[]{:S(2)}) collective-permute-start(bf16[240,1024]{1,0:T(8,128)(2,1)S(1)} %get-tuple-element.36), channel_id=1, source_target_pairs={{0,3},{1,2},{2,1},{3,0},{4,7},{5,6},{6,5},{7,4},{8,11},{9,10},{10,... | collective-permute-start | bytes 1474568 | tf_op jit(solution)/shard_map/ppermute | solution.py:230
  31.5 21.3 %collective-permute-start.2 = (bf16[16,1024]{1,0:T(8,128)(2,1)S(1)}, bf16[16,1024]{1,0:T(8,128)(2,1)S(1)}, u32[]{:S(2)}, u32[]{:S(2)}) collective-permute-start(bf16[16,1024]{1,0:T(8,128)(2,1)S(1)} %get-tuple-element.37), channel_id=1, source_target_pairs={{0,1},{1,0},{2,3},{3,2},{4,5},{5,4},{6,7},{7,6},{8,9},{9,8},{10,11... | collective-permute-start | bytes 98312 | tf_op jit(solution)/shard_map/ppermute | solution.py:230
  42.3 1.2 %collective-permute-start.8 = (f32[8,128]{1,0:T(8,128)S(1)}, f32[8,128]{1,0:T(8,128)S(1)}, u32[]{:S(2)}, u32[]{:S(2)}) collective-permute-start(f32[8,128]{1,0:T(8,128)S(1)} %get-tuple-element.45), channel_id=1, source_target_pairs={{0,4},{4,0},{8,12},{12,8},{1,5},{5,1},{9,13},{13,9},{2,6},{6,2},{1... | collective-permute-start | bytes 12296 | tf_op jit(solution)/shard_map/ppermute | solution.py:230
  43.5 13.6 %collective-permute-start = (bf16[16,1024]{1,0:T(8,128)(2,1)S(1)}, bf16[16,1024]{1,0:T(8,128)(2,1)S(1)}, u32[]{:S(2)}, u32[]{:S(2)}) collective-permute-start(bf16[16,1024]{1,0:T(8,128)(2,1)S(1)} %get-tuple-element.32), channel_id=1, source_target_pairs={{0,3},{1,2},{2,1},{3,0},{4,7},{5,6},{6,5},{7,4},{8,11},{9,10},{10,... | collective-permute-start | bytes 98312 | tf_op jit(solution)/shard_map/ppermute | solution.py:230
  48.2 3.7 %collective-permute-start.9 = (f32[8,128]{1,0:T(8,128)S(1)}, f32[8,128]{1,0:T(8,128)S(1)}, u32[]{:S(2)}, u32[]{:S(2)}) collective-permute-start(f32[8,128]{1,0:T(8,128)S(1)} %get-tuple-element.48), channel_id=1, source_target_pairs={{0,8},{4,12},{8,0},{12,4},{1,9},{5,13},{9,1},{13,5},{2,10},{6,14},... | collective-permute-start | bytes 12296 | tf_op jit(solution)/shard_map/ppermute | solution.py:230
  50.8 3.1 %collective-permute-start.10 = (f32[8,128]{1,0:T(8,128)S(1)}, f32[8,128]{1,0:T(8,128)S(1)}, u32[]{:S(2)}, u32[]{:S(2)}) collective-permute-start(f32[8,128]{1,0:T(8,128)S(1)} %get-tuple-element.50), channel_id=1, source_target_pairs={{0,12},{4,8},{8,4},{12,0},{1,13},{5,9},{9,5},{13,1},{2,14},{6,10},... | collective-permute-start | bytes 12296 | tf_op jit(solution)/shard_map/ppermute | solution.py:230
  54.4 3.7 %collective-permute-start.11 = (f32[8,128]{1,0:T(8,128)S(1)}, f32[8,128]{1,0:T(8,128)S(1)}, u32[]{:S(2)}, u32[]{:S(2)}) collective-permute-start(f32[8,128]{1,0:T(8,128)S(1)} %get-tuple-element.54), channel_id=1, source_target_pairs={{0,1},{1,0},{2,3},{3,2},{4,5},{5,4},{6,7},{7,6},{8,9},{9,8},{10,11... | collective-permute-start | bytes 12296 | tf_op jit(solution)/shard_map/ppermute | solution.py:230
  55.6 4.9 %collective-permute-start.12 = (f32[8,128]{1,0:T(8,128)S(1)}, f32[8,128]{1,0:T(8,128)S(1)}, u32[]{:S(2)}, u32[]{:S(2)}) collective-permute-start(f32[8,128]{1,0:T(8,128)S(1)} %get-tuple-element.57), channel_id=1, source_target_pairs={{0,2},{1,3},{2,0},{3,1},{4,6},{5,7},{6,4},{7,5},{8,10},{9,11},{10,... | collective-permute-start | bytes 12296 | tf_op jit(solution)/shard_map/ppermute | solution.py:230
  58.6 5.5 %collective-permute-start.13 = (f32[8,128]{1,0:T(8,128)S(1)}, f32[8,128]{1,0:T(8,128)S(1)}, u32[]{:S(2)}, u32[]{:S(2)}) collective-permute-start(f32[8,128]{1,0:T(8,128)S(1)} %get-tuple-element.58), channel_id=1, source_target_pairs={{0,3},{1,2},{2,1},{3,0},{4,7},{5,6},{6,5},{7,4},{8,11},{9,10},{10,... | collective-permute-start | bytes 12296 | tf_op jit(solution)/shard_map/ppermute | solution.py:230

commit v15 on v14

--- a/solution.py
+++ b/solution.py
@@ -50,9 +50,9 @@
     ]
     for copy in scalars:
         copy.start()
-    starts = range(0, BLOCK, PART)
+    half = BLOCK // 2
     entering = []
-    for start in starts:
+    for start in range(0, half, PART):
         for top in range(start, embeds.shape[0], BLOCK):
             rows = pl.ds(top, PART)
             entering.append(pltpu.make_async_copy(embeds.at[rows], staged.at[rows], in_sems.at[len(entering)]))
@@ -60,15 +60,29 @@
     for copy in scalars:
         copy.wait()
     picks = [take_pick(axis, step, blk_scalars, sub_scalars) for axis, step, _, _ in slots]
-    count = embeds.shape[0] // BLOCK
+    lower = []
+    for start in range(half, BLOCK, PART):
+        for place, pick in enumerate(picks):
+            source = embeds.at[pl.ds(pl.multiple_of(pick * BLOCK + start, PART), PART)]
+            here = staged.at[pl.ds(embeds.shape[0] + place * half + start - half, PART)]
+            lower.append(pltpu.make_async_copy(source, here, in_sems.at[len(entering) + len(lower)]))
+            lower[-1].start()
+    for copy in entering:
+        copy.wait()
     leaving = []
-    for turn, start in enumerate(starts):
-        for copy in entering[turn * count : (turn + 1) * count]:
-            copy.wait()
-        for pick, out in zip(picks, outs):
-            here = staged.at[pl.ds(pl.multiple_of(pick * BLOCK + start, PART), PART)]
-            leaving.append(pltpu.make_async_copy(here, out.at[pl.ds(start, PART)], out_sems.at[len(leaving)]))
-            leaving[-1].start()
+
+    def leave(place, here, start):
+        target = outs[place].at[pl.ds(start, PART)]
+        leaving.append(pltpu.make_async_copy(here, target, out_sems.at[len(leaving)]))
+        leaving[-1].start()
+
+    for start in range(0, half, PART):
+        for place, pick in enumerate(picks):
+            leave(place, staged.at[pl.ds(pl.multiple_of(pick * BLOCK + start, PART), PART)], start)
+    for turn, copy in enumerate(lower):
+        copy.wait()
+        start, place = divmod(turn, len(slots))
+        leave(place, staged.at[pl.ds(embeds.shape[0] + place * half + start * PART, PART)], half + start * PART)
     for copy in leaving:
         copy.wait()
 
@@ -78,6 +92,7 @@
 
 def first_rows(slots, pick_blk, pick_sub, embeds):
     parts = BLOCK // PART
+    lower_rows = len(slots) * (BLOCK // 2)
     return pl.pallas_call(
         functools.partial(first_kernel, slots),
         out_shape=[jax.ShapeDtypeStruct((BLOCK, embeds.shape[1]), embeds.dtype)] * len(slots),
@@ -86,9 +101,9 @@
         scratch_shapes=[
             pltpu.SMEM(pick_blk.shape, jnp.int32),
             pltpu.SMEM(pick_sub.shape, jnp.int32),
-            pltpu.VMEM(embeds.shape, embeds.dtype),
+            pltpu.VMEM((embeds.shape[0] + lower_rows, embeds.shape[1]), embeds.dtype),
             pltpu.SemaphoreType.DMA((2,)),
-            pltpu.SemaphoreType.DMA((embeds.shape[0] // PART,)),
+            pltpu.SemaphoreType.DMA((embeds.shape[0] // 2 // PART + lower_rows // PART,)),
             pltpu.SemaphoreType.DMA((len(slots) * parts,)),
         ],
     )(pick_blk, pick_sub, embeds)
@@ -204,16 +219,16 @@
 HALF = BLOCK // 2
 
 
-FIRST_CUT = 240
-
-
-FIRST_CUT = 240
+FIRST_CUT = 192
+
+
+FIRST_CUT = 192
 
 
 def plan_slots(sizes):
-    slots = [("blk", 1, 0, BLOCK), ("sub", 2, 0, BLOCK)]
+    slots = [("blk", 1, 0, BLOCK), ("sub", 2, 0, BLOCK), ("sub", 1, 0, BLOCK)]
     slots += [("blk", k, 0, BLOCK) for k in range(2, sizes["blk"])]
-    for k in (1, *range(3, sizes["sub"])):
+    for k in range(3, sizes["sub"]):
         slots += [("sub", k, 0, FIRST_CUT), ("sub", k, FIRST_CUT, BLOCK - FIRST_CUT)]
     return slots
 
@@ -249,8 +264,6 @@
             carried[axis, step] = back
         elif axis == "blk":
             waiting.append((place + BEHIND, place, send(back, slot)))
-        elif step == 1 and not last:
-            waiting.append((len(slots), place, send(back, slot)))
         else:
             late.append((place, send(back, slot)))
     for place, sums in late:

time: 64.8 us -> 60.6 us (0.935)
  starting transfers between devices: 26.3 us -> 18.6 us
  waiting for transfers between devices: 24.8 us -> 28.7 us
    ppermute x14 -> x13, starting transfers between devices: 26.3 us -> 18.6 us  [send(): return lax.ppermute(array, slot[0], pairs(slot[1], sizes[slot[0]]))]
    ppermute x14 -> x13, waiting for transfers between devices: 24.8 us -> 28.7 us  [send(): return lax.ppermute(array, slot[0], pairs(slot[1], sizes[slot[0]]))]
    pallas_call x8 -> x7, Pallas kernels: 6.89 us -> 6.46 us  [work(): pl.pallas_call(functools.partial(slot_kernel, place, *slot[2:], [one for...]
  transfers between devices with their start and end apart: 14 -> 13, of which waited for: 6 -> 4; matrix products, arithmetic and copies ran while one was open for 0% -> 0% of each run, Pallas kernels for 16% -> 15%
where the time goes in v15:
time: 60.6 us; the launch traced here: 60.5 us
  waiting for transfers between devices  28.7 us (47%)
  starting transfers between devices  18.6 us (31%)
  Pallas kernels  12.5 us (21%)
    ppermute x13, waiting for transfers between devices, send(): return lax.ppermute(array, slot[0], pairs(slot[1], sizes[slot[0]]))  28.7 us
    ppermute x13, starting transfers between devices, send(): return lax.ppermute(array, slot[0], pairs(slot[1], sizes[slot[0]]))  18.6 us
    pallas_call x7, Pallas kernels, work(): pl.pallas_call(functools.partial(slot_kernel, place, *slot[2:], [one for...  6.46 us
    pallas_call x1, Pallas kernels, first_rows(): pl.pallas_call(functools.partial(first_kernel, slots), out_shape=[jax.Sha...  3.11 us
    pallas_call x1, Pallas kernels, prepare(): pl.pallas_call(functools.partial(prepare_kernel, slots), out_shape=[jax.S...  1.77 us
  transfers between devices with their start and end apart: 13, of which 4 were waited for; matrix products, arithmetic and copies ran while one was open for 0% of the time, Pallas kernels for 15%

profile of v15, /device:TPU:0, one launch (start us, length us, event | category | flops | bytes accessed | tf_op | source)
XLA Modules:
  0.0 60.5 jit_solution(4235409236202600708)
XLA Ops:
  0.0 0.0 copy-start
  0.0 0.0 copy-start.2
  0.0 0.0 copy-start.1
  0.0 0.0 copy-start.3
  0.0 0.0 copy-start.4
  0.0 3.1 %shard_map.57 = (bf16[256,1024]{1,0:T(8,128)(2,1)}, bf16[256,1024]{1,0:T(8,128)(2,1)}) custom-call(s32[1,4]{1,0:T(1,128)} %pick_blk.5, s32[4,4]{1,0:T(4,128)} %pick_sub.5, bf16[1024,1024]{1,0:T(8,128)(2,1)} %embeds.5), custom_call_target="tpu_custom_call" | custom-call | tf_op jit(solution)/shard_map/pallas_call | solution.py:96
  3.1 0.5 collective-permute-start.6
  3.7 3.7 %collective-permute-start.5 = (bf16[256,1024]{1,0:T(8,128)(2,1)}, bf16[256,1024]{1,0:T(8,128)(2,1)S(1)}, u32[]{:S(2)}, u32[]{:S(2)}) collective-permute-start(bf16[256,1024]{1,0:T(8,128)(2,1)} %get-tuple-element.37), channel_id=1, source_target_pairs={{0,2},{1,3},{2,0},{3,1},{4,6},{5,7},{6,4},{7,5},{8,10},{9,11},{10,... | collective-permute-start | bytes 1572872 | tf_op jit(solution)/shard_map/ppermute | solution.py:245
  7.3 0.0 copy-done
  7.3 0.0 copy-done.2
  7.3 0.0 copy-done.1
  7.3 1.1 %shard_map.55 = (bf16[256,1024]{1,0:T(8,128)(2,1)S(1)}, bf16[256,1024]{1,0:T(8,128)(2,1)S(1)}, bf16[256,1024]{1,0:T(8,128)(2,1)S(1)}, bf16[192,1024]{1,0:T(8,128)(2,1)S(1)}, bf16[64,1024]{1,0:T(8,128)(2,1)S(1)}) custom-call(s32[1,4]{1,0:T(1,128)S(1)} %copy-done.2, s32[4,4]{1,0:T(4,128)S(1)} %copy-done.1, bf16[1024,1024]{1,0:T(8,128)(2,1)S(1)} %copy-done), custom_call_target="tpu_custom_call" | custom-call | tf_op jit(solution)/shard_map/pallas_call | solution.py:133
  8.5 1.6 %collective-permute-start.4 = (bf16[256,1024]{1,0:T(8,128)(2,1)S(1)}, bf16[256,1024]{1,0:T(8,128)(2,1)S(1)}, u32[]{:S(2)}, u32[]{:S(2)}) collective-permute-start(bf16[256,1024]{1,0:T(8,128)(2,1)S(1)} %get-tuple-element.36), channel_id=1, source_target_pairs={{0,1},{1,0},{2,3},{3,2},{4,5},{5,4},{6,7},{7,6},{8,9},{9,8},{10,11... | collective-permute-start | bytes 1572872 | tf_op jit(solution)/shard_map/ppermute | solution.py:245
  10.1 1.5 %collective-permute-start.3 = (bf16[256,1024]{1,0:T(8,128)(2,1)S(1)}, bf16[256,1024]{1,0:T(8,128)(2,1)S(1)}, u32[]{:S(2)}, u32[]{:S(2)}) collective-permute-start(bf16[256,1024]{1,0:T(8,128)(2,1)S(1)} %get-tuple-element.35), channel_id=1, source_target_pairs={{0,8},{4,12},{8,0},{12,4},{1,9},{5,13},{9,1},{13,5},{2,10},{6,14},... | collective-permute-start | bytes 1572872 | tf_op jit(solution)/shard_map/ppermute | solution.py:245
  11.6 0.0 collective-permute-start.2
  11.6 0.0 collective-permute-done.6.arrived
  11.6 0.2 collective-permute-start.1
  11.8 19.7 %collective-permute-done.5.arrived = bf16[256,1024]{1,0:T(8,128)(2,1)S(1)} collective-permute-done((bf16[256,1024]{1,0:T(8,128)(2,1)}, bf16[256,1024]{1,0:T(8,128)(2,1)S(1)}, u32[]{:S(2)}, u32[]{:S(2)}) %collective-permute-start.5) | collective-permute-done | bytes 524320 | tf_op jit(solution)/shard_map/ppermute | solution.py:245
  31.6 3.8 %collective-permute-start = (bf16[64,1024]{1,0:T(8,128)(2,1)S(1)}, bf16[64,1024]{1,0:T(8,128)(2,1)S(1)}, u32[]{:S(2)}, u32[]{:S(2)}) collective-permute-start(bf16[64,1024]{1,0:T(8,128)(2,1)S(1)} %get-tuple-element.29), channel_id=1, source_target_pairs={{0,3},{1,2},{2,1},{3,0},{4,7},{5,6},{6,5},{7,4},{8,11},{9,10},{10,... | collective-permute-start | bytes 393224 | tf_op jit(solution)/shard_map/ppermute | solution.py:245
  35.4 0.0 copy-done.3
  35.4 0.0 copy-done.4
  35.4 1.8 %shard_map.56 = (bf16[1024,1024]{1,0:T(8,128)(2,1)S(1)}, f32[7,4,128]{2,1,0:T(4,128)S(1)}, f32[7,8,128]{2,1,0:T(8,128)S(1)}) custom-call(s32[1,4]{1,0:T(1,128)S(1)} %copy-done.2, s32[4,4]{1,0:T(4,128)S(1)} %copy-done.1, s32[1,16]{1,0:T(1,128)S(1)} %copy-done.3, s32[1,16]{1,0:T(1,128)S(1)} %copy-done.4, bf16[1024,1024]{1,0:T(8,128)(2,1)S(1)} %copy-done), custom_call_target="tpu_custom_call" | custom-call | tf_op jit(solution)/shard_map/pallas_call | solution.py:165
  37.2 1.0 %shard_map.58 = (f32[8,128]{1,0:T(8,128)S(1)}, f32[8,128]{1,0:T(8,128)S(1)}) custom-call(bf16[256,1024]{1,0:T(8,128)(2,1)S(1)} %collective-permute-done.6.arrived, bf16[1024,1024]{1,0:T(8,128)(2,1)S(1)} %get-tuple-element.30.units, f32[7,4,128]{2,1,0:T(4,128)S(1)} %get-tuple-element.31.live, f32[7,8,128]{2,1,0:T(8,128)S(1)} %get-tuple-element.32.mine, ...), custom_call_target="tpu_custom_call" | custom-call | tf_op jit(solution)/shard_map/pallas_call | solution.py:208
  38.2 5.6 %collective-permute-done.4.arrived = bf16[256,1024]{1,0:T(8,128)(2,1)S(1)} collective-permute-done((bf16[256,1024]{1,0:T(8,128)(2,1)S(1)}, bf16[256,1024]{1,0:T(8,128)(2,1)S(1)}, u32[]{:S(2)}, u32[]{:S(2)}) %collective-permute-start.4) | collective-permute-done | bytes 524320 | tf_op jit(solution)/shard_map/ppermute | solution.py:245
  43.8 0.0 collective-permute-start.7
  43.8 1.0 %shard_map.59 = (f32[8,128]{1,0:T(8,128)S(1)}, f32[8,128]{1,0:T(8,128)S(1)}) custom-call(bf16[256,1024]{1,0:T(8,128)(2,1)S(1)} %collective-permute-done.5.arrived, bf16[1024,1024]{1,0:T(8,128)(2,1)S(1)} %get-tuple-element.30.units, f32[7,4,128]{2,1,0:T(4,128)S(1)} %get-tuple-element.31.live, f32[7,8,128]{2,1,0:T(8,128)S(1)} %get-tuple-element.32.mine, ...), custom_call_target="tpu_custom_call" | custom-call | tf_op jit(solution)/shard_map/pallas_call | solution.py:208
  44.8 0.2 collective-permute-done.7.rest_0_
  45.0 1.0 %shard_map.60 = (f32[8,128]{1,0:T(8,128)S(1)}, f32[8,128]{1,0:T(8,128)S(1)}) custom-call(bf16[256,1024]{1,0:T(8,128)(2,1)S(1)} %collective-permute-done.4.arrived, bf16[1024,1024]{1,0:T(8,128)(2,1)S(1)} %get-tuple-element.30.units, f32[7,4,128]{2,1,0:T(4,128)S(1)} %get-tuple-element.31.live, f32[7,8,128]{2,1,0:T(8,128)S(1)} %get-tuple-element.32.mine, ...), custom_call_target="tpu_custom_call" | custom-call | tf_op jit(solution)/shard_map/pallas_call | solution.py:208
  46.0 0.0 collective-permute-done.3.arrived
  46.0 1.0 %shard_map.61 = (f32[8,128]{1,0:T(8,128)S(1)}, f32[8,128]{1,0:T(8,128)S(1)}) custom-call(bf16[256,1024]{1,0:T(8,128)(2,1)S(1)} %collective-permute-done.3.arrived, bf16[1024,1024]{1,0:T(8,128)(2,1)S(1)} %get-tuple-element.30.units, f32[7,4,128]{2,1,0:T(4,128)S(1)} %get-tuple-element.31.live, f32[7,8,128]{2,1,0:T(8,128)S(1)} %get-tuple-element.32.mine, ...), custom_call_target="tpu_custom_call" | custom-call | tf_op jit(solution)/shard_map/pallas_call | solution.py:208
  47.0 1.6 %collective-permute-start.8 = (f32[8,128]{1,0:T(8,128)S(1)}, f32[8,128]{1,0:T(8,128)S(1)}, u32[]{:S(2)}, u32[]{:S(2)}) collective-permute-start(f32[8,128]{1,0:T(8,128)S(1)} %get-tuple-element.45), channel_id=1, source_target_pairs={{0,8},{4,12},{8,0},{12,4},{1,9},{5,13},{9,1},{13,5},{2,10},{6,14},... | collective-permute-start | bytes 12296 | tf_op jit(solution)/shard_map/ppermute | solution.py:245
  48.6 0.0 collective-permute-done.2.arrived
  48.6 1.0 %shard_map.62 = (f32[8,128]{1,0:T(8,128)S(1)}, f32[8,128]{1,0:T(8,128)S(1)}) custom-call(bf16[256,1024]{1,0:T(8,128)(2,1)S(1)} %collective-permute-done.2.arrived, bf16[1024,1024]{1,0:T(8,128)(2,1)S(1)} %get-tuple-element.30.units, f32[7,4,128]{2,1,0:T(4,128)S(1)} %get-tuple-element.31.live, f32[7,8,128]{2,1,0:T(8,128)S(1)} %get-tuple-element.32.mine, ...), custom_call_target="tpu_custom_call" | custom-call | tf_op jit(solution)/shard_map/pallas_call | solution.py:208
  49.6 0.2 collective-permute-start.9
  49.8 0.0 collective-permute-start.10
  49.8 0.0 collective-permute-done.1.arrived
  49.8 3.1 %collective-permute-start.11 = (f32[8,128]{1,0:T(8,128)S(1)}, f32[8,128]{1,0:T(8,128)S(1)}, u32[]{:S(2)}, u32[]{:S(2)}) collective-permute-start(f32[8,128]{1,0:T(8,128)S(1)} %get-tuple-element.51), channel_id=1, source_target_pairs={{0,1},{1,0},{2,3},{3,2},{4,5},{5,4},{6,7},{7,6},{8,9},{9,8},{10,11... | collective-permute-start | bytes 12296 | tf_op jit(solution)/shard_map/ppermute | solution.py:245
  52.9 0.0 collective-permute-done.8.rest_0_
  52.9 0.8 %shard_map.63 = (f32[8,128]{1,0:T(8,128)S(1)}, f32[8,128]{1,0:T(8,128)S(1)}) custom-call(bf16[192,1024]{1,0:T(8,128)(2,1)S(1)} %collective-permute-done.1.arrived, bf16[1024,1024]{1,0:T(8,128)(2,1)S(1)} %get-tuple-element.30.units, f32[7,4,128]{2,1,0:T(4,128)S(1)} %get-tuple-element.31.live, f32[7,8,128]{2,1,0:T(8,128)S(1)} %get-tuple-element.32.mine, ...), custom_call_target="tpu_custom_call" | custom-call | tf_op jit(solution)/shard_map/pallas_call | solution.py:208
  53.7 0.0 collective-permute-done.arrived
  53.8 0.0 collective-permute-done.9.rest_0_
  53.8 0.7 %shard_map.64 = (f32[8,128]{1,0:T(8,128)S(1)}, f32[8,128]{1,0:T(8,128)S(1)}) custom-call(bf16[64,1024]{1,0:T(8,128)(2,1)S(1)} %collective-permute-done.arrived, bf16[1024,1024]{1,0:T(8,128)(2,1)S(1)} %get-tuple-element.30.units, f32[7,4,128]{2,1,0:T(4,128)S(1)} %get-tuple-element.31.live, f32[7,8,128]{2,1,0:T(8,128)S(1)} %get-tuple-element.32.mine, ...), custom_call_target="tpu_custom_call" | custom-call | tf_op jit(solution)/shard_map/pallas_call | solution.py:208
  54.4 2.3 %collective-permute-start.12 = (f32[8,128]{1,0:T(8,128)S(1)}, f32[8,128]{1,0:T(8,128)S(1)}, u32[]{:S(2)}, u32[]{:S(2)}) collective-permute-start(f32[8,128]{1,0:T(8,128)S(1)} %get-tuple-element.52), channel_id=1, source_target_pairs={{0,3},{1,2},{2,1},{3,0},{4,7},{5,6},{6,5},{7,4},{8,11},{9,10},{10,... | collective-permute-start | bytes 12296 | tf_op jit(solution)/shard_map/ppermute | solution.py:245
  56.7 0.0 collective-permute-done.10
  56.7 0.0 collective-permute-done.11
  56.7 3.2 %collective-permute-done.12 = f32[8,128]{1,0:T(8,128)S(1)} collective-permute-done((f32[8,128]{1,0:T(8,128)S(1)}, f32[8,128]{1,0:T(8,128)S(1)}, u32[]{:S(2)}, u32[]{:S(2)}) %collective-permute-start.12) | collective-permute-done | bytes 4128 | tf_op jit(solution)/shard_map/ppermute | solution.py:245
  59.9 0.6 fusion.2
  (1 shorter events, 0.0 us)
Async XLA Ops:
  0.0 7.3 %copy-start = (bf16[1024,1024]{1,0:T(8,128)(2,1)S(1)}, bf16[1024,1024]{1,0:T(8,128)(2,1)}, u32[]{:S(2)}) copy-start(bf16[1024,1024]{1,0:T(8,128)(2,1)} %embeds.5) | copy-start | bytes 6291460
  0.0 7.3 %copy-start.2 = (s32[1,4]{1,0:T(1,128)S(1)}, s32[1,4]{1,0:T(1,128)}, u32[]{:S(2)}) copy-start(s32[1,4]{1,0:T(1,128)} %pick_blk.5) | copy-start | bytes 52
  0.0 7.3 %copy-start.1 = (s32[4,4]{1,0:T(4,128)S(1)}, s32[4,4]{1,0:T(4,128)}, u32[]{:S(2)}) copy-start(s32[4,4]{1,0:T(4,128)} %pick_sub.5) | copy-start | bytes 196
  0.0 35.4 %copy-start.3 = (s32[1,16]{1,0:T(1,128)S(1)}, s32[1,16]{1,0:T(1,128)}, u32[]{:S(2)}) copy-start(s32[1,16]{1,0:T(1,128)} %mask_blk.1) | copy-start | bytes 196
  0.0 35.4 %copy-start.4 = (s32[1,16]{1,0:T(1,128)S(1)}, s32[1,16]{1,0:T(1,128)}, u32[]{:S(2)}) copy-start(s32[1,16]{1,0:T(1,128)} %mask_sub.1) | copy-start | bytes 196
  3.1 8.5 %collective-permute-start.6 = (bf16[256,1024]{1,0:T(8,128)(2,1)}, bf16[256,1024]{1,0:T(8,128)(2,1)S(1)}, u32[]{:S(2)}, u32[]{:S(2)}) collective-permute-start(bf16[256,1024]{1,0:T(8,128)(2,1)} %get-tuple-element.38), channel_id=1, source_target_pairs={{0,4},{4,0},{8,12},{12,8},{1,5},{5,1},{9,13},{13,9},{2,6},{6,2},{1... | collective-permute-start | bytes 1572872 | tf_op jit(solution)/shard_map/ppermute | solution.py:245
  3.7 27.9 %collective-permute-start.5 = (bf16[256,1024]{1,0:T(8,128)(2,1)}, bf16[256,1024]{1,0:T(8,128)(2,1)S(1)}, u32[]{:S(2)}, u32[]{:S(2)}) collective-permute-start(bf16[256,1024]{1,0:T(8,128)(2,1)} %get-tuple-element.37), channel_id=1, source_target_pairs={{0,2},{1,3},{2,0},{3,1},{4,6},{5,7},{6,4},{7,5},{8,10},{9,11},{10,... | collective-permute-start | bytes 1572872 | tf_op jit(solution)/shard_map/ppermute | solution.py:245
  8.5 35.4 %collective-permute-start.4 = (bf16[256,1024]{1,0:T(8,128)(2,1)S(1)}, bf16[256,1024]{1,0:T(8,128)(2,1)S(1)}, u32[]{:S(2)}, u32[]{:S(2)}) collective-permute-start(bf16[256,1024]{1,0:T(8,128)(2,1)S(1)} %get-tuple-element.36), channel_id=1, source_target_pairs={{0,1},{1,0},{2,3},{3,2},{4,5},{5,4},{6,7},{7,6},{8,9},{9,8},{10,11... | collective-permute-start | bytes 1572872 | tf_op jit(solution)/shard_map/ppermute | solution.py:245
  10.1 35.9 %collective-permute-start.3 = (bf16[256,1024]{1,0:T(8,128)(2,1)S(1)}, bf16[256,1024]{1,0:T(8,128)(2,1)S(1)}, u32[]{:S(2)}, u32[]{:S(2)}) collective-permute-start(bf16[256,1024]{1,0:T(8,128)(2,1)S(1)} %get-tuple-element.35), channel_id=1, source_target_pairs={{0,8},{4,12},{8,0},{12,4},{1,9},{5,13},{9,1},{13,5},{2,10},{6,14},... | collective-permute-start | bytes 1572872 | tf_op jit(solution)/shard_map/ppermute | solution.py:245
  11.6 37.0 %collective-permute-start.2 = (bf16[256,1024]{1,0:T(8,128)(2,1)S(1)}, bf16[256,1024]{1,0:T(8,128)(2,1)S(1)}, u32[]{:S(2)}, u32[]{:S(2)}) collective-permute-start(bf16[256,1024]{1,0:T(8,128)(2,1)S(1)} %get-tuple-element.34), channel_id=1, source_target_pairs={{0,12},{4,8},{8,4},{12,0},{1,13},{5,9},{9,5},{13,1},{2,14},{6,10},... | collective-permute-start | bytes 1572872 | tf_op jit(solution)/shard_map/ppermute | solution.py:245
  11.6 38.2 %collective-permute-start.1 = (bf16[192,1024]{1,0:T(8,128)(2,1)S(1)}, bf16[192,1024]{1,0:T(8,128)(2,1)S(1)}, u32[]{:S(2)}, u32[]{:S(2)}) collective-permute-start(bf16[192,1024]{1,0:T(8,128)(2,1)S(1)} %get-tuple-element.33), channel_id=1, source_target_pairs={{0,3},{1,2},{2,1},{3,0},{4,7},{5,6},{6,5},{7,4},{8,11},{9,10},{10,... | collective-permute-start | bytes 1179656 | tf_op jit(solution)/shard_map/ppermute | solution.py:245
  31.6 22.2 %collective-permute-start = (bf16[64,1024]{1,0:T(8,128)(2,1)S(1)}, bf16[64,1024]{1,0:T(8,128)(2,1)S(1)}, u32[]{:S(2)}, u32[]{:S(2)}) collective-permute-start(bf16[64,1024]{1,0:T(8,128)(2,1)S(1)} %get-tuple-element.29), channel_id=1, source_target_pairs={{0,3},{1,2},{2,1},{3,0},{4,7},{5,6},{6,5},{7,4},{8,11},{9,10},{10,... | collective-permute-start | bytes 393224 | tf_op jit(solution)/shard_map/ppermute | solution.py:245
  43.8 1.2 %collective-permute-start.7 = (f32[8,128]{1,0:T(8,128)S(1)}, f32[8,128]{1,0:T(8,128)S(1)}, u32[]{:S(2)}, u32[]{:S(2)}) collective-permute-start(f32[8,128]{1,0:T(8,128)S(1)} %get-tuple-element.41), channel_id=1, source_target_pairs={{0,4},{4,0},{8,12},{12,8},{1,5},{5,1},{9,13},{13,9},{2,6},{6,2},{1... | collective-permute-start | bytes 12296 | tf_op jit(solution)/shard_map/ppermute | solution.py:245
  47.0 5.9 %collective-permute-start.8 = (f32[8,128]{1,0:T(8,128)S(1)}, f32[8,128]{1,0:T(8,128)S(1)}, u32[]{:S(2)}, u32[]{:S(2)}) collective-permute-start(f32[8,128]{1,0:T(8,128)S(1)} %get-tuple-element.45), channel_id=1, source_target_pairs={{0,8},{4,12},{8,0},{12,4},{1,9},{5,13},{9,1},{13,5},{2,10},{6,14},... | collective-permute-start | bytes 12296 | tf_op jit(solution)/shard_map/ppermute | solution.py:245
  49.6 4.1 %collective-permute-start.9 = (f32[8,128]{1,0:T(8,128)S(1)}, f32[8,128]{1,0:T(8,128)S(1)}, u32[]{:S(2)}, u32[]{:S(2)}) collective-permute-start(f32[8,128]{1,0:T(8,128)S(1)} %get-tuple-element.47), channel_id=1, source_target_pairs={{0,12},{4,8},{8,4},{12,0},{1,13},{5,9},{9,5},{13,1},{2,14},{6,10},... | collective-permute-start | bytes 12296 | tf_op jit(solution)/shard_map/ppermute | solution.py:245
  49.8 6.9 %collective-permute-start.10 = (f32[8,128]{1,0:T(8,128)S(1)}, f32[8,128]{1,0:T(8,128)S(1)}, u32[]{:S(2)}, u32[]{:S(2)}) collective-permute-start(f32[8,128]{1,0:T(8,128)S(1)} %get-tuple-element.50), channel_id=1, source_target_pairs={{0,2},{1,3},{2,0},{3,1},{4,6},{5,7},{6,4},{7,5},{8,10},{9,11},{10,... | collective-permute-start | bytes 12296 | tf_op jit(solution)/shard_map/ppermute | solution.py:245
  49.8 6.9 %collective-permute-start.11 = (f32[8,128]{1,0:T(8,128)S(1)}, f32[8,128]{1,0:T(8,128)S(1)}, u32[]{:S(2)}, u32[]{:S(2)}) collective-permute-start(f32[8,128]{1,0:T(8,128)S(1)} %get-tuple-element.51), channel_id=1, source_target_pairs={{0,1},{1,0},{2,3},{3,2},{4,5},{5,4},{6,7},{7,6},{8,9},{9,8},{10,11... | collective-permute-start | bytes 12296 | tf_op jit(solution)/shard_map/ppermute | solution.py:245
  54.4 5.5 %collective-permute-start.12 = (f32[8,128]{1,0:T(8,128)S(1)}, f32[8,128]{1,0:T(8,128)S(1)}, u32[]{:S(2)}, u32[]{:S(2)}) collective-permute-start(f32[8,128]{1,0:T(8,128)S(1)} %get-tuple-element.52), channel_id=1, source_target_pairs={{0,3},{1,2},{2,1},{3,0},{4,7},{5,6},{6,5},{7,4},{8,11},{9,10},{10,... | collective-permute-start | bytes 12296 | tf_op jit(solution)/shard_map/ppermute | solution.py:245

commit v16 on v14

--- a/solution.py
+++ b/solution.py
@@ -204,16 +204,13 @@
 HALF = BLOCK // 2
 
 
-FIRST_CUT = 240
-
-
-FIRST_CUT = 240
+FIRST_CUT = 128
 
 
 def plan_slots(sizes):
-    slots = [("blk", 1, 0, BLOCK), ("sub", 2, 0, BLOCK)]
+    slots = [("blk", 1, 0, BLOCK), ("sub", 2, 0, BLOCK), ("sub", 1, 0, BLOCK)]
     slots += [("blk", k, 0, BLOCK) for k in range(2, sizes["blk"])]
-    for k in (1, *range(3, sizes["sub"])):
+    for k in range(3, sizes["sub"]):
         slots += [("sub", k, 0, FIRST_CUT), ("sub", k, FIRST_CUT, BLOCK - FIRST_CUT)]
     return slots
 
@@ -249,8 +246,6 @@
             carried[axis, step] = back
         elif axis == "blk":
             waiting.append((place + BEHIND, place, send(back, slot)))
-        elif step == 1 and not last:
-            waiting.append((len(slots), place, send(back, slot)))
         else:
             late.append((place, send(back, slot)))
     for place, sums in late:

time: 64.8 us -> 57.2 us (0.88); the launches traced: 64.7 us -> 56.1 us
  starting transfers between devices: 26.3 us -> 21.4 us
  waiting for transfers between devices: 24.8 us -> 22.4 us
  Pallas kernels: 12.8 us -> 11.6 us
    ppermute x14 -> x13, starting transfers between devices: 26.3 us -> 21.4 us  [send(): return lax.ppermute(array, slot[0], pairs(slot[1], sizes[slot[0]]))]
    ppermute x14 -> x13, waiting for transfers between devices: 24.8 us -> 22.4 us  [send(): return lax.ppermute(array, slot[0], pairs(slot[1], sizes[slot[0]]))]
    pallas_call x1, Pallas kernels: 1.47 us -> 0.82 us  [pick_rows(): pl.pallas_call(functools.partial(pick_kernel, slots), out_shape=[jax.Shap...]
    pallas_call x8 -> x7, Pallas kernels: 6.89 us -> 6.29 us  [work(): pl.pallas_call(functools.partial(slot_kernel, place, *slot[2:], [one for...]
  transfers between devices with their start and end apart: 14 -> 13, of which waited for: 6 -> 4; matrix products, arithmetic and copies ran while one was open for 0% -> 0% of each run, Pallas kernels for 16% -> 16%
where the time goes in v16:
time: 57.2 us; the launch traced here: 56.1 us
  waiting for transfers between devices  22.4 us (39%)
  starting transfers between devices  21.4 us (37%)
  Pallas kernels  11.6 us (20%)
  other arithmetic  0.6 us (1%)
    ppermute x13, waiting for transfers between devices, send(): return lax.ppermute(array, slot[0], pairs(slot[1], sizes[slot[0]]))  22.4 us
    ppermute x13, starting transfers between devices, send(): return lax.ppermute(array, slot[0], pairs(slot[1], sizes[slot[0]]))  21.4 us
    pallas_call x7, Pallas kernels, work(): pl.pallas_call(functools.partial(slot_kernel, place, *slot[2:], [one for...  6.29 us
    pallas_call x1, Pallas kernels, first_rows(): pl.pallas_call(functools.partial(first_kernel, slots), out_shape=[jax.Sha...  2.68 us
    pallas_call x1, Pallas kernels, prepare(): pl.pallas_call(functools.partial(prepare_kernel, slots), out_shape=[jax.S...  1.77 us
  transfers between devices with their start and end apart: 13, of which 4 were waited for; matrix products, arithmetic and copies ran while one was open for 0% of the time, Pallas kernels for 16%

profile of v16, /device:TPU:0, one launch (start us, length us, event | category | flops | bytes accessed | tf_op | source)
XLA Modules:
  0.0 56.1 jit_solution(7506230449509999074)
XLA Ops:
  0.0 0.0 copy-start
  0.0 0.0 copy-start.2
  0.0 0.0 copy-start.1
  0.0 0.0 copy-start.3
  0.0 0.0 copy-start.4
  0.0 2.7 %shard_map.57 = (bf16[256,1024]{1,0:T(8,128)(2,1)}, bf16[256,1024]{1,0:T(8,128)(2,1)}) custom-call(s32[1,4]{1,0:T(1,128)} %pick_blk.5, s32[4,4]{1,0:T(4,128)} %pick_sub.5, bf16[1024,1024]{1,0:T(8,128)(2,1)} %embeds.5), custom_call_target="tpu_custom_call" | custom-call | tf_op jit(solution)/shard_map/pallas_call | solution.py:81
  2.7 0.5 collective-permute-start.6
  3.2 3.7 %collective-permute-start.5 = (bf16[256,1024]{1,0:T(8,128)(2,1)}, bf16[256,1024]{1,0:T(8,128)(2,1)S(1)}, u32[]{:S(2)}, u32[]{:S(2)}) collective-permute-start(bf16[256,1024]{1,0:T(8,128)(2,1)} %get-tuple-element.37), channel_id=1, source_target_pairs={{0,2},{1,3},{2,0},{3,1},{4,6},{5,7},{6,4},{7,5},{8,10},{9,11},{10,... | collective-permute-start | bytes 1572872 | tf_op jit(solution)/shard_map/ppermute | solution.py:227
  6.9 0.0 copy-done
  6.9 0.0 copy-done.2
  6.9 0.0 copy-done.1
  6.9 0.8 %shard_map.55 = (bf16[256,1024]{1,0:T(8,128)(2,1)S(1)}, bf16[256,1024]{1,0:T(8,128)(2,1)S(1)}, bf16[256,1024]{1,0:T(8,128)(2,1)S(1)}, bf16[128,1024]{1,0:T(8,128)(2,1)S(1)}, bf16[128,1024]{1,0:T(8,128)(2,1)S(1)}) custom-call(s32[1,4]{1,0:T(1,128)S(1)} %copy-done.2, s32[4,4]{1,0:T(4,128)S(1)} %copy-done.1, bf16[1024,1024]{1,0:T(8,128)(2,1)S(1)} %copy-done), custom_call_target="tpu_custom_call" | custom-call | tf_op jit(solution)/shard_map/pallas_call | solution.py:118
  7.7 1.6 %collective-permute-start.4 = (bf16[256,1024]{1,0:T(8,128)(2,1)S(1)}, bf16[256,1024]{1,0:T(8,128)(2,1)S(1)}, u32[]{:S(2)}, u32[]{:S(2)}) collective-permute-start(bf16[256,1024]{1,0:T(8,128)(2,1)S(1)} %get-tuple-element.36), channel_id=1, source_target_pairs={{0,1},{1,0},{2,3},{3,2},{4,5},{5,4},{6,7},{7,6},{8,9},{9,8},{10,11... | collective-permute-start | bytes 1572872 | tf_op jit(solution)/shard_map/ppermute | solution.py:227
  9.4 1.5 %collective-permute-start.3 = (bf16[256,1024]{1,0:T(8,128)(2,1)S(1)}, bf16[256,1024]{1,0:T(8,128)(2,1)S(1)}, u32[]{:S(2)}, u32[]{:S(2)}) collective-permute-start(bf16[256,1024]{1,0:T(8,128)(2,1)S(1)} %get-tuple-element.35), channel_id=1, source_target_pairs={{0,8},{4,12},{8,0},{12,4},{1,9},{5,13},{9,1},{13,5},{2,10},{6,14},... | collective-permute-start | bytes 1572872 | tf_op jit(solution)/shard_map/ppermute | solution.py:227
  10.9 0.0 collective-permute-start.2
  10.9 0.0 collective-permute-done.6.arrived
  10.9 0.2 collective-permute-start.1
  11.1 20.1 %collective-permute-done.5.arrived = bf16[256,1024]{1,0:T(8,128)(2,1)S(1)} collective-permute-done((bf16[256,1024]{1,0:T(8,128)(2,1)}, bf16[256,1024]{1,0:T(8,128)(2,1)S(1)}, u32[]{:S(2)}, u32[]{:S(2)}) %collective-permute-start.5) | collective-permute-done | bytes 524320 | tf_op jit(solution)/shard_map/ppermute | solution.py:227
  31.2 3.7 %collective-permute-start = (bf16[128,1024]{1,0:T(8,128)(2,1)S(1)}, bf16[128,1024]{1,0:T(8,128)(2,1)S(1)}, u32[]{:S(2)}, u32[]{:S(2)}) collective-permute-start(bf16[128,1024]{1,0:T(8,128)(2,1)S(1)} %get-tuple-element.29), channel_id=1, source_target_pairs={{0,3},{1,2},{2,1},{3,0},{4,7},{5,6},{6,5},{7,4},{8,11},{9,10},{10,... | collective-permute-start | bytes 786440 | tf_op jit(solution)/shard_map/ppermute | solution.py:227
  34.9 0.0 copy-done.3
  34.9 0.0 copy-done.4
  34.9 1.8 %shard_map.56 = (bf16[1024,1024]{1,0:T(8,128)(2,1)S(1)}, f32[7,4,128]{2,1,0:T(4,128)S(1)}, f32[7,8,128]{2,1,0:T(8,128)S(1)}) custom-call(s32[1,4]{1,0:T(1,128)S(1)} %copy-done.2, s32[4,4]{1,0:T(4,128)S(1)} %copy-done.1, s32[1,16]{1,0:T(1,128)S(1)} %copy-done.3, s32[1,16]{1,0:T(1,128)S(1)} %copy-done.4, bf16[1024,1024]{1,0:T(8,128)(2,1)S(1)} %copy-done), custom_call_target="tpu_custom_call" | custom-call | tf_op jit(solution)/shard_map/pallas_call | solution.py:150
  36.7 1.0 %shard_map.58 = (f32[8,128]{1,0:T(8,128)S(1)}, f32[8,128]{1,0:T(8,128)S(1)}) custom-call(bf16[256,1024]{1,0:T(8,128)(2,1)S(1)} %collective-permute-done.6.arrived, bf16[1024,1024]{1,0:T(8,128)(2,1)S(1)} %get-tuple-element.30.units, f32[7,4,128]{2,1,0:T(4,128)S(1)} %get-tuple-element.31.live, f32[7,8,128]{2,1,0:T(8,128)S(1)} %get-tuple-element.32.mine, ...), custom_call_target="tpu_custom_call" | custom-call | tf_op jit(solution)/shard_map/pallas_call | solution.py:193
  37.7 0.0 collective-permute-done.4.arrived
  37.7 0.1 collective-permute-start.7
  37.8 1.0 %shard_map.59 = (f32[8,128]{1,0:T(8,128)S(1)}, f32[8,128]{1,0:T(8,128)S(1)}) custom-call(bf16[256,1024]{1,0:T(8,128)(2,1)S(1)} %collective-permute-done.5.arrived, bf16[1024,1024]{1,0:T(8,128)(2,1)S(1)} %get-tuple-element.30.units, f32[7,4,128]{2,1,0:T(4,128)S(1)} %get-tuple-element.31.live, f32[7,8,128]{2,1,0:T(8,128)S(1)} %get-tuple-element.32.mine, ...), custom_call_target="tpu_custom_call" | custom-call | tf_op jit(solution)/shard_map/pallas_call | solution.py:193
  38.8 0.2 collective-permute-done.7.rest_0_
  38.9 1.0 %shard_map.60 = (f32[8,128]{1,0:T(8,128)S(1)}, f32[8,128]{1,0:T(8,128)S(1)}) custom-call(bf16[256,1024]{1,0:T(8,128)(2,1)S(1)} %collective-permute-done.4.arrived, bf16[1024,1024]{1,0:T(8,128)(2,1)S(1)} %get-tuple-element.30.units, f32[7,4,128]{2,1,0:T(4,128)S(1)} %get-tuple-element.31.live, f32[7,8,128]{2,1,0:T(8,128)S(1)} %get-tuple-element.32.mine, ...), custom_call_target="tpu_custom_call" | custom-call | tf_op jit(solution)/shard_map/pallas_call | solution.py:193
  39.9 0.0 collective-permute-done.3.arrived
  39.9 1.0 %shard_map.61 = (f32[8,128]{1,0:T(8,128)S(1)}, f32[8,128]{1,0:T(8,128)S(1)}) custom-call(bf16[256,1024]{1,0:T(8,128)(2,1)S(1)} %collective-permute-done.3.arrived, bf16[1024,1024]{1,0:T(8,128)(2,1)S(1)} %get-tuple-element.30.units, f32[7,4,128]{2,1,0:T(4,128)S(1)} %get-tuple-element.31.live, f32[7,8,128]{2,1,0:T(8,128)S(1)} %get-tuple-element.32.mine, ...), custom_call_target="tpu_custom_call" | custom-call | tf_op jit(solution)/shard_map/pallas_call | solution.py:193
  40.9 1.6 %collective-permute-start.8 = (f32[8,128]{1,0:T(8,128)S(1)}, f32[8,128]{1,0:T(8,128)S(1)}, u32[]{:S(2)}, u32[]{:S(2)}) collective-permute-start(f32[8,128]{1,0:T(8,128)S(1)} %get-tuple-element.45), channel_id=1, source_target_pairs={{0,8},{4,12},{8,0},{12,4},{1,9},{5,13},{9,1},{13,5},{2,10},{6,14},... | collective-permute-start | bytes 12296 | tf_op jit(solution)/shard_map/ppermute | solution.py:227
  42.5 0.0 collective-permute-done.2.arrived
  42.5 1.0 %shard_map.62 = (f32[8,128]{1,0:T(8,128)S(1)}, f32[8,128]{1,0:T(8,128)S(1)}) custom-call(bf16[256,1024]{1,0:T(8,128)(2,1)S(1)} %collective-permute-done.2.arrived, bf16[1024,1024]{1,0:T(8,128)(2,1)S(1)} %get-tuple-element.30.units, f32[7,4,128]{2,1,0:T(4,128)S(1)} %get-tuple-element.31.live, f32[7,8,128]{2,1,0:T(8,128)S(1)} %get-tuple-element.32.mine, ...), custom_call_target="tpu_custom_call" | custom-call | tf_op jit(solution)/shard_map/pallas_call | solution.py:193
  43.5 0.3 collective-permute-start.9
  43.8 0.0 collective-permute-start.10
  43.8 0.0 collective-permute-done.1.arrived
  43.8 4.9 %collective-permute-start.11 = (f32[8,128]{1,0:T(8,128)S(1)}, f32[8,128]{1,0:T(8,128)S(1)}, u32[]{:S(2)}, u32[]{:S(2)}) collective-permute-start(f32[8,128]{1,0:T(8,128)S(1)} %get-tuple-element.51), channel_id=1, source_target_pairs={{0,1},{1,0},{2,3},{3,2},{4,5},{5,4},{6,7},{7,6},{8,9},{9,8},{10,11... | collective-permute-start | bytes 12296 | tf_op jit(solution)/shard_map/ppermute | solution.py:227
  48.7 0.0 collective-permute-done.8.rest_0_
  48.7 0.7 %shard_map.63 = (f32[8,128]{1,0:T(8,128)S(1)}, f32[8,128]{1,0:T(8,128)S(1)}) custom-call(bf16[128,1024]{1,0:T(8,128)(2,1)S(1)} %collective-permute-done.1.arrived, bf16[1024,1024]{1,0:T(8,128)(2,1)S(1)} %get-tuple-element.30.units, f32[7,4,128]{2,1,0:T(4,128)S(1)} %get-tuple-element.31.live, f32[7,8,128]{2,1,0:T(8,128)S(1)} %get-tuple-element.32.mine, ...), custom_call_target="tpu_custom_call" | custom-call | tf_op jit(solution)/shard_map/pallas_call | solution.py:193
  49.3 0.0 collective-permute-done.arrived
  49.3 0.0 collective-permute-done.9.rest_0_
  49.3 0.7 %shard_map.64 = (f32[8,128]{1,0:T(8,128)S(1)}, f32[8,128]{1,0:T(8,128)S(1)}) custom-call(bf16[128,1024]{1,0:T(8,128)(2,1)S(1)} %collective-permute-done.arrived, bf16[1024,1024]{1,0:T(8,128)(2,1)S(1)} %get-tuple-element.30.units, f32[7,4,128]{2,1,0:T(4,128)S(1)} %get-tuple-element.31.live, f32[7,8,128]{2,1,0:T(8,128)S(1)} %get-tuple-element.32.mine, ...), custom_call_target="tpu_custom_call" | custom-call | tf_op jit(solution)/shard_map/pallas_call | solution.py:193
  50.0 3.4 %collective-permute-start.12 = (f32[8,128]{1,0:T(8,128)S(1)}, f32[8,128]{1,0:T(8,128)S(1)}, u32[]{:S(2)}, u32[]{:S(2)}) collective-permute-start(f32[8,128]{1,0:T(8,128)S(1)} %get-tuple-element.52), channel_id=1, source_target_pairs={{0,3},{1,2},{2,1},{3,0},{4,7},{5,6},{6,5},{7,4},{8,11},{9,10},{10,... | collective-permute-start | bytes 12296 | tf_op jit(solution)/shard_map/ppermute | solution.py:227
  53.4 0.2 collective-permute-done.10
  53.6 0.0 collective-permute-done.11
  53.6 1.9 %collective-permute-done.12 = f32[8,128]{1,0:T(8,128)S(1)} collective-permute-done((f32[8,128]{1,0:T(8,128)S(1)}, f32[8,128]{1,0:T(8,128)S(1)}, u32[]{:S(2)}, u32[]{:S(2)}) %collective-permute-start.12) | collective-permute-done | bytes 4128 | tf_op jit(solution)/shard_map/ppermute | solution.py:227
  55.5 0.6 %fusion.2 = f32[1024]{0:T(1024)} fusion(f32[8,128]{1,0:T(8,128)S(1)} %collective-permute-done.12, f32[8,128]{1,0:T(8,128)S(1)} %collective-permute-done.11, f32[8,128]{1,0:T(8,128)S(1)} %get-tuple-element.49, f32[8,128]{1,0:T(8,128)S(1)} %collective-permute-done.10, f32[7,8,128]{2,1,0:T(8,128)S(1)} %get-tuple-element.32.mine), kind=kLoop, calls=%fused_computation.3 | loop fusion | flops 7168 | bytes 32768 | tf_op jit(solution)/shard_map/reshape | solution.py:253
  (1 shorter events, 0.0 us)
Async XLA Ops:
  0.0 6.9 %copy-start = (bf16[1024,1024]{1,0:T(8,128)(2,1)S(1)}, bf16[1024,1024]{1,0:T(8,128)(2,1)}, u32[]{:S(2)}) copy-start(bf16[1024,1024]{1,0:T(8,128)(2,1)} %embeds.5) | copy-start | bytes 6291460
  0.0 6.9 %copy-start.2 = (s32[1,4]{1,0:T(1,128)S(1)}, s32[1,4]{1,0:T(1,128)}, u32[]{:S(2)}) copy-start(s32[1,4]{1,0:T(1,128)} %pick_blk.5) | copy-start | bytes 52
  0.0 6.9 %copy-start.1 = (s32[4,4]{1,0:T(4,128)S(1)}, s32[4,4]{1,0:T(4,128)}, u32[]{:S(2)}) copy-start(s32[4,4]{1,0:T(4,128)} %pick_sub.5) | copy-start | bytes 196
  0.0 34.9 %copy-start.3 = (s32[1,16]{1,0:T(1,128)S(1)}, s32[1,16]{1,0:T(1,128)}, u32[]{:S(2)}) copy-start(s32[1,16]{1,0:T(1,128)} %mask_blk.1) | copy-start | bytes 196
  0.0 34.9 %copy-start.4 = (s32[1,16]{1,0:T(1,128)S(1)}, s32[1,16]{1,0:T(1,128)}, u32[]{:S(2)}) copy-start(s32[1,16]{1,0:T(1,128)} %mask_sub.1) | copy-start | bytes 196
  2.7 8.2 %collective-permute-start.6 = (bf16[256,1024]{1,0:T(8,128)(2,1)}, bf16[256,1024]{1,0:T(8,128)(2,1)S(1)}, u32[]{:S(2)}, u32[]{:S(2)}) collective-permute-start(bf16[256,1024]{1,0:T(8,128)(2,1)} %get-tuple-element.38), channel_id=1, source_target_pairs={{0,4},{4,0},{8,12},{12,8},{1,5},{5,1},{9,13},{13,9},{2,6},{6,2},{1... | collective-permute-start | bytes 1572872 | tf_op jit(solution)/shard_map/ppermute | solution.py:227
  3.2 27.9 %collective-permute-start.5 = (bf16[256,1024]{1,0:T(8,128)(2,1)}, bf16[256,1024]{1,0:T(8,128)(2,1)S(1)}, u32[]{:S(2)}, u32[]{:S(2)}) collective-permute-start(bf16[256,1024]{1,0:T(8,128)(2,1)} %get-tuple-element.37), channel_id=1, source_target_pairs={{0,2},{1,3},{2,0},{3,1},{4,6},{5,7},{6,4},{7,5},{8,10},{9,11},{10,... | collective-permute-start | bytes 1572872 | tf_op jit(solution)/shard_map/ppermute | solution.py:227
  7.7 30.0 %collective-permute-start.4 = (bf16[256,1024]{1,0:T(8,128)(2,1)S(1)}, bf16[256,1024]{1,0:T(8,128)(2,1)S(1)}, u32[]{:S(2)}, u32[]{:S(2)}) collective-permute-start(bf16[256,1024]{1,0:T(8,128)(2,1)S(1)} %get-tuple-element.36), channel_id=1, source_target_pairs={{0,1},{1,0},{2,3},{3,2},{4,5},{5,4},{6,7},{7,6},{8,9},{9,8},{10,11... | collective-permute-start | bytes 1572872 | tf_op jit(solution)/shard_map/ppermute | solution.py:227
  9.4 30.6 %collective-permute-start.3 = (bf16[256,1024]{1,0:T(8,128)(2,1)S(1)}, bf16[256,1024]{1,0:T(8,128)(2,1)S(1)}, u32[]{:S(2)}, u32[]{:S(2)}) collective-permute-start(bf16[256,1024]{1,0:T(8,128)(2,1)S(1)} %get-tuple-element.35), channel_id=1, source_target_pairs={{0,8},{4,12},{8,0},{12,4},{1,9},{5,13},{9,1},{13,5},{2,10},{6,14},... | collective-permute-start | bytes 1572872 | tf_op jit(solution)/shard_map/ppermute | solution.py:227
  10.9 31.6 %collective-permute-start.2 = (bf16[256,1024]{1,0:T(8,128)(2,1)S(1)}, bf16[256,1024]{1,0:T(8,128)(2,1)S(1)}, u32[]{:S(2)}, u32[]{:S(2)}) collective-permute-start(bf16[256,1024]{1,0:T(8,128)(2,1)S(1)} %get-tuple-element.34), channel_id=1, source_target_pairs={{0,12},{4,8},{8,4},{12,0},{1,13},{5,9},{9,5},{13,1},{2,14},{6,10},... | collective-permute-start | bytes 1572872 | tf_op jit(solution)/shard_map/ppermute | solution.py:227
  10.9 32.9 %collective-permute-start.1 = (bf16[128,1024]{1,0:T(8,128)(2,1)S(1)}, bf16[128,1024]{1,0:T(8,128)(2,1)S(1)}, u32[]{:S(2)}, u32[]{:S(2)}) collective-permute-start(bf16[128,1024]{1,0:T(8,128)(2,1)S(1)} %get-tuple-element.33), channel_id=1, source_target_pairs={{0,3},{1,2},{2,1},{3,0},{4,7},{5,6},{6,5},{7,4},{8,11},{9,10},{10,... | collective-permute-start | bytes 786440 | tf_op jit(solution)/shard_map/ppermute | solution.py:227
  31.2 18.2 %collective-permute-start = (bf16[128,1024]{1,0:T(8,128)(2,1)S(1)}, bf16[128,1024]{1,0:T(8,128)(2,1)S(1)}, u32[]{:S(2)}, u32[]{:S(2)}) collective-permute-start(bf16[128,1024]{1,0:T(8,128)(2,1)S(1)} %get-tuple-element.29), channel_id=1, source_target_pairs={{0,3},{1,2},{2,1},{3,0},{4,7},{5,6},{6,5},{7,4},{8,11},{9,10},{10,... | collective-permute-start | bytes 786440 | tf_op jit(solution)/shard_map/ppermute | solution.py:227
  37.7 1.2 %collective-permute-start.7 = (f32[8,128]{1,0:T(8,128)S(1)}, f32[8,128]{1,0:T(8,128)S(1)}, u32[]{:S(2)}, u32[]{:S(2)}) collective-permute-start(f32[8,128]{1,0:T(8,128)S(1)} %get-tuple-element.41), channel_id=1, source_target_pairs={{0,4},{4,0},{8,12},{12,8},{1,5},{5,1},{9,13},{13,9},{2,6},{6,2},{1... | collective-permute-start | bytes 12296 | tf_op jit(solution)/shard_map/ppermute | solution.py:227
  40.9 7.7 %collective-permute-start.8 = (f32[8,128]{1,0:T(8,128)S(1)}, f32[8,128]{1,0:T(8,128)S(1)}, u32[]{:S(2)}, u32[]{:S(2)}) collective-permute-start(f32[8,128]{1,0:T(8,128)S(1)} %get-tuple-element.45), channel_id=1, source_target_pairs={{0,8},{4,12},{8,0},{12,4},{1,9},{5,13},{9,1},{13,5},{2,10},{6,14},... | collective-permute-start | bytes 12296 | tf_op jit(solution)/shard_map/ppermute | solution.py:227
  43.5 5.8 %collective-permute-start.9 = (f32[8,128]{1,0:T(8,128)S(1)}, f32[8,128]{1,0:T(8,128)S(1)}, u32[]{:S(2)}, u32[]{:S(2)}) collective-permute-start(f32[8,128]{1,0:T(8,128)S(1)} %get-tuple-element.47), channel_id=1, source_target_pairs={{0,12},{4,8},{8,4},{12,0},{1,13},{5,9},{9,5},{13,1},{2,14},{6,10},... | collective-permute-start | bytes 12296 | tf_op jit(solution)/shard_map/ppermute | solution.py:227
  43.8 9.8 %collective-permute-start.10 = (f32[8,128]{1,0:T(8,128)S(1)}, f32[8,128]{1,0:T(8,128)S(1)}, u32[]{:S(2)}, u32[]{:S(2)}) collective-permute-start(f32[8,128]{1,0:T(8,128)S(1)} %get-tuple-element.50), channel_id=1, source_target_pairs={{0,2},{1,3},{2,0},{3,1},{4,6},{5,7},{6,4},{7,5},{8,10},{9,11},{10,... | collective-permute-start | bytes 12296 | tf_op jit(solution)/shard_map/ppermute | solution.py:227
  43.8 9.8 %collective-permute-start.11 = (f32[8,128]{1,0:T(8,128)S(1)}, f32[8,128]{1,0:T(8,128)S(1)}, u32[]{:S(2)}, u32[]{:S(2)}) collective-permute-start(f32[8,128]{1,0:T(8,128)S(1)} %get-tuple-element.51), channel_id=1, source_target_pairs={{0,1},{1,0},{2,3},{3,2},{4,5},{5,4},{6,7},{7,6},{8,9},{9,8},{10,11... | collective-permute-start | bytes 12296 | tf_op jit(solution)/shard_map/ppermute | solution.py:227
  50.0 5.5 %collective-permute-start.12 = (f32[8,128]{1,0:T(8,128)S(1)}, f32[8,128]{1,0:T(8,128)S(1)}, u32[]{:S(2)}, u32[]{:S(2)}) collective-permute-start(f32[8,128]{1,0:T(8,128)S(1)} %get-tuple-element.52), channel_id=1, source_target_pairs={{0,3},{1,2},{2,1},{3,0},{4,7},{5,6},{6,5},{7,4},{8,11},{9,10},{10,... | collective-permute-start | bytes 12296 | tf_op jit(solution)/shard_map/ppermute | solution.py:227

commit v17 on v16

--- a/solution.py
+++ b/solution.py
@@ -17,7 +17,6 @@
 
 SMEM = pl.BlockSpec(memory_space=pltpu.SMEM)
 VMEM = pl.BlockSpec(memory_space=pltpu.VMEM)
-HBM = pl.BlockSpec(memory_space=pltpu.HBM)
 ANY = pl.BlockSpec(memory_space=pl.ANY)
 PARAMS = pltpu.CompilerParams(vmem_limit_bytes=32 * 2**20)
 
@@ -42,7 +41,7 @@
     return pick_blk[0, target] if axis == "blk" else pick_sub[lax.axis_index("sub"), target]
 
 
-def first_kernel(slots, pick_blk, pick_sub, embeds, *rest):
+def pick_kernel(slots, pick_blk, pick_sub, embeds, *rest):
     outs, (blk_scalars, sub_scalars, staged, scalar_sems, in_sems, out_sems) = rest[: len(slots)], rest[len(slots) :]
     scalars = [
         pltpu.make_async_copy(pick_blk, blk_scalars, scalar_sems.at[0]),
@@ -73,13 +72,13 @@
         copy.wait()
 
 
-PART = 64
-
-
-def first_rows(slots, pick_blk, pick_sub, embeds):
+PART = 128
+
+
+def pick_rows(slots, pick_blk, pick_sub, embeds):
     parts = BLOCK // PART
     return pl.pallas_call(
-        functools.partial(first_kernel, slots),
+        functools.partial(pick_kernel, slots),
         out_shape=[jax.ShapeDtypeStruct((BLOCK, embeds.shape[1]), embeds.dtype)] * len(slots),
         in_specs=[ANY] * 3,
         out_specs=[ANY] * len(slots),
@@ -91,42 +90,6 @@
             pltpu.SemaphoreType.DMA((embeds.shape[0] // PART,)),
             pltpu.SemaphoreType.DMA((len(slots) * parts,)),
         ],
-    )(pick_blk, pick_sub, embeds)
-
-
-def pick_kernel(slots, pick_blk, pick_sub, embeds, *rest):
-    outs, (blk_scalars, sub_scalars, scalar_sems, row_sems) = rest[: len(slots)], rest[len(slots) :]
-    scalars = [
-        pltpu.make_async_copy(pick_blk, blk_scalars, scalar_sems.at[0]),
-        pltpu.make_async_copy(pick_sub, sub_scalars, scalar_sems.at[1]),
-    ]
-    for copy in scalars:
-        copy.start()
-    for copy in scalars:
-        copy.wait()
-    copies = []
-    for place, (axis, step, first, rows) in enumerate(slots):
-        pick = take_pick(axis, step, blk_scalars, sub_scalars)
-        start = pl.multiple_of(pick * BLOCK + first, math.gcd(BLOCK, first))
-        copies.append(pltpu.make_async_copy(embeds.at[pl.ds(start, rows)], outs[place], row_sems.at[place]))
-        copies[-1].start()
-    for copy in copies:
-        copy.wait()
-
-
-def pick_rows(slots, pick_blk, pick_sub, embeds):
-    return pl.pallas_call(
-        functools.partial(pick_kernel, slots),
-        out_shape=[jax.ShapeDtypeStruct((rows, embeds.shape[1]), embeds.dtype) for _, _, _, rows in slots],
-        in_specs=[HBM] * 3,
-        out_specs=[VMEM] * len(slots),
-        scratch_shapes=[
-            pltpu.SMEM(pick_blk.shape, jnp.int32),
-            pltpu.SMEM(pick_sub.shape, jnp.int32),
-            pltpu.SemaphoreType.DMA((2,)),
-            pltpu.SemaphoreType.DMA((len(slots),)),
-        ],
-        compiler_params=PARAMS,
     )(pick_blk, pick_sub, embeds)
 
 
@@ -160,14 +123,18 @@
     )(pick_blk, pick_sub, mask_blk, mask_sub, embeds)
 
 
-def slot_kernel(place, first, rows, back_places, carries, arrived, units, live, mine, totals, *rest):
+def slot_kernel(place, axis, step, first, rows, back_places, carries, arrived, units, live, mine, totals, *rest):
     new_totals, back = rest[-2:]
     count = live.shape[1]
     before = totals[...]
     for back_place, sums in zip(back_places, rest):
         before = before + mine[back_place] * sums[...]
     new_totals[...] = before
-    x = rounded_units(arrived[...])
+    top = 0
+    if arrived.shape[0] != rows:
+        own = lax.axis_index(axis)
+        top = pl.multiple_of(jnp.where((own ^ step) > own, rows, 0), rows)
+    x = rounded_units(arrived[pl.ds(top, rows)])
     along_rows = jnp.zeros((rows, LANES), jnp.float32)
     for i in range(count):
         cosines = jnp.dot(x, units[:, i * BLOCK : (i + 1) * BLOCK], preferred_element_type=jnp.float32)
@@ -191,7 +158,7 @@
     operands = [arrived, units, live, mine, totals] + [sums for _, sums in returned]
     operands += [] if carried is None else [carried]
     return pl.pallas_call(
-        functools.partial(slot_kernel, place, *slot[2:], [one for one, _ in returned], carried is not None),
+        functools.partial(slot_kernel, place, *slot, [one for one, _ in returned], carried is not None),
         out_shape=[jax.ShapeDtypeStruct(totals.shape, jnp.float32)] * 2,
         in_specs=[VMEM] * len(operands),
         out_specs=[VMEM] * 2,
@@ -200,22 +167,10 @@
 
 
 BEHIND = 2
-EARLY_ROWS = 192
-HALF = BLOCK // 2
-
-
-FIRST_CUT = 128
-
-
 def plan_slots(sizes):
-    slots = [("blk", 1, 0, BLOCK), ("sub", 2, 0, BLOCK), ("sub", 1, 0, BLOCK)]
+    slots = [("sub", 2, 0, BLOCK), ("blk", 1, 0, BLOCK)]
     slots += [("blk", k, 0, BLOCK) for k in range(2, sizes["blk"])]
-    for k in range(3, sizes["sub"]):
-        slots += [("sub", k, 0, FIRST_CUT), ("sub", k, FIRST_CUT, BLOCK - FIRST_CUT)]
-    return slots
-
-
-AT_ONCE = 2
+    return slots + [("sub", k, 0, BLOCK) for k in (1, *range(3, sizes["sub"]))]
 
 
 def body(embeds, pick_blk, mask_blk, pick_sub, mask_sub):
@@ -226,9 +181,14 @@
     def send(array, slot):
         return lax.ppermute(array, slot[0], pairs(slot[1], sizes[slot[0]]))
 
-    outgoing = first_rows(slots[:AT_ONCE], pick_blk, pick_sub, embeds)
-    outgoing += pick_rows(slots[AT_ONCE:], pick_blk, pick_sub, embeds)
-    arrived = [send(rows, slot) for rows, slot in zip(outgoing, slots)]
+    def exchange(array, slot):
+        if slot[0] == "sub":
+            return send(array, slot)
+        groups = [[a, b] for a, b in pairs(slot[1], sizes["blk"]) if a < b]
+        return lax.all_gather(array, "blk", axis_index_groups=groups, axis=0, tiled=True)
+
+    outgoing = pick_rows(slots, pick_blk, pick_sub, embeds)
+    arrived = [exchange(rows, slot) for rows, slot in zip(outgoing, slots)]
 
     units, live, mine = prepare(slots, pick_blk, pick_sub, mask_blk, mask_sub, embeds)
     totals = jnp.zeros((count * ROWS, LANES), jnp.float32)

time: 57.2 us -> 89.6 us (1.57)
  waiting for transfers between devices: 22.4 us -> 37.8 us
  between operations: 0.1 us -> 13.2 us
  local copies, waits for them, and re-layouts: 0.02 us -> 5.31 us
  Pallas kernels: 11.6 us -> 10.7 us
    all_gather x0 -> x3, waiting for transfers between devices: none -> 12.1 us  [exchange(): lax.all_gather(array, 'blk', axis_index_groups=groups, axis=0, tiled=True)]
    unnamed x10 -> x16, local copies, waits for them, and re-layouts: 0.02 us -> 5.3 us
    pallas_call x8 -> x6, Pallas kernels: 8.97 us -> 5.88 us  [work(): pl.pallas_call(functools.partial(slot_kernel, place, *slot, [one for one,...]
    pallas_call x1, Pallas kernels: 0.82 us -> 3.02 us  [pick_rows(): pl.pallas_call(functools.partial(pick_kernel, slots), out_shape=[jax.Shap...]
    ppermute x13 -> x9, waiting for transfers between devices: 22.4 us -> 24.4 us  [send(): return lax.ppermute(array, slot[0], pairs(slot[1], sizes[slot[0]]))]
    unnamed x0 -> x3, waiting for transfers between devices: none -> 1.39 us
    ppermute x13 -> x9, starting transfers between devices: 21.4 us -> 21.6 us  [send(): return lax.ppermute(array, slot[0], pairs(slot[1], sizes[slot[0]]))]
  transfers between devices with their start and end apart: 13 -> 12, of which waited for: 4 -> 4; matrix products, arithmetic and copies ran while one was open for 0% -> 0% of each run, Pallas kernels for 16% -> 9%
where the time goes in v17:
time: 89.6 us; the launch traced here: 89.3 us
  waiting for transfers between devices  37.8 us (42%)
  starting transfers between devices  21.7 us (24%)
  between operations  13.2 us (15%)
  Pallas kernels  10.7 us (12%)
  local copies, waits for them, and re-layouts  5.31 us (6%)
    ppermute x9, waiting for transfers between devices, send(): return lax.ppermute(array, slot[0], pairs(slot[1], sizes[slot[0]]))  24.4 us
    ppermute x9, starting transfers between devices, send(): return lax.ppermute(array, slot[0], pairs(slot[1], sizes[slot[0]]))  21.6 us
    all_gather x3, waiting for transfers between devices, exchange(): lax.all_gather(array, 'blk', axis_index_groups=groups, axis=0, tiled=True)  12.1 us
    pallas_call x6, Pallas kernels, work(): pl.pallas_call(functools.partial(slot_kernel, place, *slot, [one for one,...  5.88 us
    unnamed x16, local copies, waits for them, and re-layouts  5.3 us
    pallas_call x1, Pallas kernels, pick_rows(): pl.pallas_call(functools.partial(pick_kernel, slots), out_shape=[jax.Shap...  3.02 us
  transfers between devices with their start and end apart: 12, of which 4 were waited for; matrix products, arithmetic and copies ran while one was open for 0% of the time, Pallas kernels for 9%

profile of v17, /device:TPU:0, one launch (start us, length us, event | category | flops | bytes accessed | tf_op | source)
XLA Modules:
  0.0 89.3 jit_solution(17274032710084383188)
XLA Ops:
  6.5 0.0 copy-start.5
  6.5 0.0 copy-start.4
  6.5 0.0 all-gather.8.cloned.1.call-start
  6.6 3.0 %shard_map.55 = (bf16[256,1024]{1,0:T(8,128)(2,1)}, bf16[256,1024]{1,0:T(8,128)(2,1)}, bf16[256,1024]{1,0:T(8,128)(2,1)}, bf16[256,1024]{1,0:T(8,128)(2,1)}, bf1...) custom-call(s32[1,4]{1,0:T(1,128)} %pick_blk.3, s32[4,4]{1,0:T(4,128)} %pick_sub.3, bf16[1024,1024]{1,0:T(8,128)(2,1)} %embeds.3), custom_call_target="tpu_custom_call" | custom-call | tf_op jit(solution)/shard_map/pallas_call | solution.py:80
  9.6 0.0 all-gather.8.cloned.1.call-update
  9.6 0.0 all-gather.6.cloned.1.call-start
  9.7 0.7 all-gather.6.cloned.1.call-update
  10.4 0.0 all-gather.4.cloned.1.call-start
  10.4 0.7 all-gather.4.cloned.1.call-update
  11.1 4.1 %collective-permute-start.2 = (bf16[256,1024]{1,0:T(8,128)(2,1)}, bf16[256,1024]{1,0:T(8,128)(2,1)S(1)}, u32[]{:S(2)}, u32[]{:S(2)}) collective-permute-start(bf16[256,1024]{1,0:T(8,128)(2,1)} %get-tuple-element.34), channel_id=1, source_target_pairs={{0,2},{1,3},{2,0},{3,1},{4,6},{5,7},{6,4},{7,5},{8,10},{9,11},{10,... | collective-permute-start | bytes 1572872 | tf_op jit(solution)/shard_map/ppermute | solution.py:182
  15.2 1.6 %collective-permute-start.1 = (bf16[256,1024]{1,0:T(8,128)(2,1)}, bf16[256,1024]{1,0:T(8,128)(2,1)S(1)}, u32[]{:S(2)}, u32[]{:S(2)}) collective-permute-start(bf16[256,1024]{1,0:T(8,128)(2,1)} %get-tuple-element.30), channel_id=1, source_target_pairs={{0,1},{1,0},{2,3},{3,2},{4,5},{5,4},{6,7},{7,6},{8,9},{9,8},{10,11... | collective-permute-start | bytes 1572872 | tf_op jit(solution)/shard_map/ppermute | solution.py:182
  16.8 0.0 collective-permute-start
  16.8 0.0 copy-done.5
  16.8 0.0 copy-done.4
  16.8 0.0 copy-done.6
  16.8 0.0 copy-done.7
  16.8 0.0 copy-start
  16.8 1.6 %copy-done = bf16[1024,1024]{1,0:T(8,128)(2,1)S(1)} copy-done((bf16[1024,1024]{1,0:T(8,128)(2,1)S(1)}, bf16[1024,1024]{1,0:T(8,128)(2,1)}, u32[]{:S(2)}) %copy-start) | copy-done | bytes 2097176
  18.5 1.8 %shard_map.56 = (bf16[1024,1024]{1,0:T(8,128)(2,1)S(1)}, f32[6,4,128]{2,1,0:T(4,128)S(1)}, f32[6,8,128]{2,1,0:T(8,128)S(1)}) custom-call(s32[1,4]{1,0:T(1,128)S(1)} %copy-done.5, s32[4,4]{1,0:T(4,128)S(1)} %copy-done.4, s32[1,16]{1,0:T(1,128)S(1)} %copy-done.6, s32[1,16]{1,0:T(1,128)S(1)} %copy-done.7, bf16[1024,1024]{1,0:T(8,128)(2,1)S(1)} %copy-done), custom_call_target="tpu_custom_call" | custom-call | tf_op jit(solution)/shard_map/pallas_call | solution.py:113
  20.2 20.1 %collective-permute-done.2.arrived = bf16[256,1024]{1,0:T(8,128)(2,1)S(1)} collective-permute-done((bf16[256,1024]{1,0:T(8,128)(2,1)}, bf16[256,1024]{1,0:T(8,128)(2,1)S(1)}, u32[]{:S(2)}, u32[]{:S(2)}) %collective-permute-start.2) | collective-permute-done | bytes 524320 | tf_op jit(solution)/shard_map/ppermute | solution.py:182
  40.3 1.0 %shard_map.57 = (f32[8,128]{1,0:T(8,128)S(1)}, f32[8,128]{1,0:T(8,128)S(1)}) custom-call(bf16[256,1024]{1,0:T(8,128)(2,1)S(1)} %collective-permute-done.2.arrived, bf16[1024,1024]{1,0:T(8,128)(2,1)S(1)} %get-tuple-element.27.units, f32[6,4,128]{2,1,0:T(4,128)S(1)} %get-tuple-element.28.live, f32[6,8,128]{2,1,0:T(8,128)S(1)} %get-tuple-element.29.mine, ...), custom_call_target="tpu_custom_call" | custom-call | tf_op jit(solution)/shard_map/pallas_call | solution.py:160
  41.3 0.0 all-gather.8.cloned.1.call-done.arrived
  41.3 0.0 copy-start.2
  41.4 1.2 %copy-done.2 = bf16[512,1024]{1,0:T(8,128)(2,1)S(1)} copy-done((bf16[512,1024]{1,0:T(8,128)(2,1)S(1)}, bf16[512,1024]{1,0:T(8,128)(2,1)}, u32[]{:S(2)}) %copy-start.2) | copy-done | bytes 1048600
  42.6 1.0 %shard_map.58 = (f32[8,128]{1,0:T(8,128)S(1)}, f32[8,128]{1,0:T(8,128)S(1)}) custom-call(bf16[512,1024]{1,0:T(8,128)(2,1)S(1)} %copy-done.2, bf16[1024,1024]{1,0:T(8,128)(2,1)S(1)} %get-tuple-element.27.units, f32[6,4,128]{2,1,0:T(4,128)S(1)} %get-tuple-element.28.live, f32[6,8,128]{2,1,0:T(8,128)S(1)} %get-tuple-element.29.mine, ...), custom_call_target="tpu_custom_call" | custom-call | tf_op jit(solution)/shard_map/pallas_call | solution.py:160
  43.6 0.1 collective-permute-start.3
  43.6 1.9 %all-gather.6.cloned.1.call-done.arrived = bf16[512,1024]{1,0:T(8,128)(2,1)} async-done(((bf16[256,1024]{1,0:T(8,128)(2,1)}), bf16[512,1024]{1,0:T(8,128)(2,1)}) %all-gather.6.cloned.1.call-update) | async-done | bytes 1048592 | tf_op jit(solution)/shard_map/all_gather | solution.py:188
  45.6 1.2 %copy-done.1 = bf16[512,1024]{1,0:T(8,128)(2,1)S(1)} copy-done((bf16[512,1024]{1,0:T(8,128)(2,1)S(1)}, bf16[512,1024]{1,0:T(8,128)(2,1)}, u32[]{:S(2)}) %copy-start.1) | copy-done | bytes 1048600
  46.8 1.0 %shard_map.59 = (f32[8,128]{1,0:T(8,128)S(1)}, f32[8,128]{1,0:T(8,128)S(1)}) custom-call(bf16[512,1024]{1,0:T(8,128)(2,1)S(1)} %copy-done.1, bf16[1024,1024]{1,0:T(8,128)(2,1)S(1)} %get-tuple-element.27.units, f32[6,4,128]{2,1,0:T(4,128)S(1)} %get-tuple-element.28.live, f32[6,8,128]{2,1,0:T(8,128)S(1)} %get-tuple-element.29.mine, ...), custom_call_target="tpu_custom_call" | custom-call | tf_op jit(solution)/shard_map/pallas_call | solution.py:160
  47.8 10.4 %collective-permute-start.4 = (f32[8,128]{1,0:T(8,128)S(1)}, f32[8,128]{1,0:T(8,128)S(1)}, u32[]{:S(2)}, u32[]{:S(2)}) collective-permute-start(f32[8,128]{1,0:T(8,128)S(1)} %get-tuple-element.40), channel_id=1, source_target_pairs={{0,8},{4,12},{8,0},{12,4},{1,9},{5,13},{9,1},{13,5},{2,10},{6,14},... | collective-permute-start | bytes 12296 | tf_op jit(solution)/shard_map/ppermute | solution.py:182
  58.2 10.1 %all-gather.4.cloned.1.call-done.arrived = bf16[512,1024]{1,0:T(8,128)(2,1)} async-done(((bf16[256,1024]{1,0:T(8,128)(2,1)}), bf16[512,1024]{1,0:T(8,128)(2,1)}) %all-gather.4.cloned.1.call-update) | async-done | bytes 1048592 | tf_op jit(solution)/shard_map/all_gather | solution.py:188
  68.3 0.0 collective-permute-done.3.rest_0_
  68.3 1.2 %copy-done.3 = bf16[512,1024]{1,0:T(8,128)(2,1)S(1)} copy-done((bf16[512,1024]{1,0:T(8,128)(2,1)S(1)}, bf16[512,1024]{1,0:T(8,128)(2,1)}, u32[]{:S(2)}) %copy-start.3) | copy-done | bytes 1048600
  69.5 1.0 %shard_map.60 = (f32[8,128]{1,0:T(8,128)S(1)}, f32[8,128]{1,0:T(8,128)S(1)}) custom-call(bf16[512,1024]{1,0:T(8,128)(2,1)S(1)} %copy-done.3, bf16[1024,1024]{1,0:T(8,128)(2,1)S(1)} %get-tuple-element.27.units, f32[6,4,128]{2,1,0:T(4,128)S(1)} %get-tuple-element.28.live, f32[6,8,128]{2,1,0:T(8,128)S(1)} %get-tuple-element.29.mine, ...), custom_call_target="tpu_custom_call" | custom-call | tf_op jit(solution)/shard_map/pallas_call | solution.py:160
  70.5 0.3 collective-permute-start.5
  70.7 2.4 %collective-permute-start.6 = (f32[8,128]{1,0:T(8,128)S(1)}, f32[8,128]{1,0:T(8,128)S(1)}, u32[]{:S(2)}, u32[]{:S(2)}) collective-permute-start(f32[8,128]{1,0:T(8,128)S(1)} %get-tuple-element.44), channel_id=1, source_target_pairs={{0,2},{1,3},{2,0},{3,1},{4,6},{5,7},{6,4},{7,5},{8,10},{9,11},{10,... | collective-permute-start | bytes 12296 | tf_op jit(solution)/shard_map/ppermute | solution.py:182
  73.1 0.0 collective-permute-done.1.arrived
  73.1 0.0 collective-permute-done.4.rest_0_
  73.2 1.0 %shard_map.61 = (f32[8,128]{1,0:T(8,128)S(1)}, f32[8,128]{1,0:T(8,128)S(1)}) custom-call(bf16[256,1024]{1,0:T(8,128)(2,1)S(1)} %collective-permute-done.1.arrived, bf16[1024,1024]{1,0:T(8,128)(2,1)S(1)} %get-tuple-element.27.units, f32[6,4,128]{2,1,0:T(4,128)S(1)} %get-tuple-element.28.live, f32[6,8,128]{2,1,0:T(8,128)S(1)} %get-tuple-element.29.mine, ...), custom_call_target="tpu_custom_call" | custom-call | tf_op jit(solution)/shard_map/pallas_call | solution.py:160
  74.1 1.6 %collective-permute-start.7 = (f32[8,128]{1,0:T(8,128)S(1)}, f32[8,128]{1,0:T(8,128)S(1)}, u32[]{:S(2)}, u32[]{:S(2)}) collective-permute-start(f32[8,128]{1,0:T(8,128)S(1)} %get-tuple-element.45), channel_id=1, source_target_pairs={{0,1},{1,0},{2,3},{3,2},{4,5},{5,4},{6,7},{7,6},{8,9},{9,8},{10,11... | collective-permute-start | bytes 12296 | tf_op jit(solution)/shard_map/ppermute | solution.py:182
  75.7 0.0 collective-permute-done.arrived
  75.7 0.0 collective-permute-done.5.rest_0_
  75.7 1.0 %shard_map.62 = (f32[8,128]{1,0:T(8,128)S(1)}, f32[8,128]{1,0:T(8,128)S(1)}) custom-call(bf16[256,1024]{1,0:T(8,128)(2,1)S(1)} %collective-permute-done.arrived, bf16[1024,1024]{1,0:T(8,128)(2,1)S(1)} %get-tuple-element.27.units, f32[6,4,128]{2,1,0:T(4,128)S(1)} %get-tuple-element.28.live, f32[6,8,128]{2,1,0:T(8,128)S(1)} %get-tuple-element.29.mine, ...), custom_call_target="tpu_custom_call" | custom-call | tf_op jit(solution)/shard_map/pallas_call | solution.py:160
  76.7 1.2 %collective-permute-start.8 = (f32[8,128]{1,0:T(8,128)S(1)}, f32[8,128]{1,0:T(8,128)S(1)}, u32[]{:S(2)}, u32[]{:S(2)}) collective-permute-start(f32[8,128]{1,0:T(8,128)S(1)} %get-tuple-element.46), channel_id=1, source_target_pairs={{0,3},{1,2},{2,1},{3,0},{4,7},{5,6},{6,5},{7,4},{8,11},{9,10},{10,... | collective-permute-start | bytes 12296 | tf_op jit(solution)/shard_map/ppermute | solution.py:182
  77.9 0.0 collective-permute-done.6
  77.9 0.0 collective-permute-done.7
  77.9 4.3 %collective-permute-done.8 = f32[8,128]{1,0:T(8,128)S(1)} collective-permute-done((f32[8,128]{1,0:T(8,128)S(1)}, f32[8,128]{1,0:T(8,128)S(1)}, u32[]{:S(2)}, u32[]{:S(2)}) %collective-permute-start.8) | collective-permute-done | bytes 4128 | tf_op jit(solution)/shard_map/ppermute | solution.py:182
  82.1 0.6 fusion.2
  (5 shorter events, 0.0 us)
Async XLA Ops:
  6.5 10.3 %copy-start.5 = (s32[1,4]{1,0:T(1,128)S(1)}, s32[1,4]{1,0:T(1,128)}, u32[]{:S(2)}) copy-start(s32[1,4]{1,0:T(1,128)} %pick_blk.3) | copy-start | bytes 52
  6.5 10.3 %copy-start.4 = (s32[4,4]{1,0:T(4,128)S(1)}, s32[4,4]{1,0:T(4,128)}, u32[]{:S(2)}) copy-start(s32[4,4]{1,0:T(4,128)} %pick_sub.3) | copy-start | bytes 196
  6.5 10.3 %copy-start.6 = (s32[1,16]{1,0:T(1,128)S(1)}, s32[1,16]{1,0:T(1,128)}, u32[]{:S(2)}) copy-start(s32[1,16]{1,0:T(1,128)} %mask_blk.1) | copy-start | bytes 196
  6.5 10.3 %copy-start.7 = (s32[1,16]{1,0:T(1,128)S(1)}, s32[1,16]{1,0:T(1,128)}, u32[]{:S(2)}) copy-start(s32[1,16]{1,0:T(1,128)} %mask_sub.1) | copy-start | bytes 196
  6.5 34.8 %all-gather.8.cloned.1.call-start = ((), (), s32[]{:S(2)}) async-start(), calls=%async_computation.2 | async-start | bytes 1572864 | tf_op jit(solution)/shard_map/all_gather | solution.py:188
  9.6 35.9 %all-gather.6.cloned.1.call-start = ((), (), s32[]{:S(2)}) async-start(), calls=%async_computation.1 | async-start | bytes 1572864 | tf_op jit(solution)/shard_map/all_gather | solution.py:188
  10.4 57.9 %all-gather.4.cloned.1.call-start = ((), (), s32[]{:S(2)}) async-start(), calls=%async_computation | async-start | bytes 1572864 | tf_op jit(solution)/shard_map/all_gather | solution.py:188
  11.1 29.2 %collective-permute-start.2 = (bf16[256,1024]{1,0:T(8,128)(2,1)}, bf16[256,1024]{1,0:T(8,128)(2,1)S(1)}, u32[]{:S(2)}, u32[]{:S(2)}) collective-permute-start(bf16[256,1024]{1,0:T(8,128)(2,1)} %get-tuple-element.34), channel_id=1, source_target_pairs={{0,2},{1,3},{2,0},{3,1},{4,6},{5,7},{6,4},{7,5},{8,10},{9,11},{10,... | collective-permute-start | bytes 1572872 | tf_op jit(solution)/shard_map/ppermute | solution.py:182
  15.2 57.9 %collective-permute-start.1 = (bf16[256,1024]{1,0:T(8,128)(2,1)}, bf16[256,1024]{1,0:T(8,128)(2,1)S(1)}, u32[]{:S(2)}, u32[]{:S(2)}) collective-permute-start(bf16[256,1024]{1,0:T(8,128)(2,1)} %get-tuple-element.30), channel_id=1, source_target_pairs={{0,1},{1,0},{2,3},{3,2},{4,5},{5,4},{6,7},{7,6},{8,9},{9,8},{10,11... | collective-permute-start | bytes 1572872 | tf_op jit(solution)/shard_map/ppermute | solution.py:182
  16.8 58.9 %collective-permute-start = (bf16[256,1024]{1,0:T(8,128)(2,1)}, bf16[256,1024]{1,0:T(8,128)(2,1)S(1)}, u32[]{:S(2)}, u32[]{:S(2)}) collective-permute-start(bf16[256,1024]{1,0:T(8,128)(2,1)} %get-tuple-element.26), channel_id=1, source_target_pairs={{0,3},{1,2},{2,1},{3,0},{4,7},{5,6},{6,5},{7,4},{8,11},{9,10},{10,... | collective-permute-start | bytes 1572872 | tf_op jit(solution)/shard_map/ppermute | solution.py:182
  16.8 1.6 %copy-start = (bf16[1024,1024]{1,0:T(8,128)(2,1)S(1)}, bf16[1024,1024]{1,0:T(8,128)(2,1)}, u32[]{:S(2)}) copy-start(bf16[1024,1024]{1,0:T(8,128)(2,1)} %embeds.3) | copy-start | bytes 6291460
  41.3 1.2 %copy-start.2 = (bf16[512,1024]{1,0:T(8,128)(2,1)S(1)}, bf16[512,1024]{1,0:T(8,128)(2,1)}, u32[]{:S(2)}) copy-start(bf16[512,1024]{1,0:T(8,128)(2,1)} %all-gather.8.cloned.1.call-done.arrived) | copy-start | bytes 3145732
  43.6 24.7 %collective-permute-start.3 = (f32[8,128]{1,0:T(8,128)S(1)}, f32[8,128]{1,0:T(8,128)S(1)}, u32[]{:S(2)}, u32[]{:S(2)}) collective-permute-start(f32[8,128]{1,0:T(8,128)S(1)} %get-tuple-element.38), channel_id=1, source_target_pairs={{0,4},{4,0},{8,12},{12,8},{1,5},{5,1},{9,13},{13,9},{2,6},{6,2},{1... | collective-permute-start | bytes 12296 | tf_op jit(solution)/shard_map/ppermute | solution.py:182
  45.6 1.2 %copy-start.1 = (bf16[512,1024]{1,0:T(8,128)(2,1)S(1)}, bf16[512,1024]{1,0:T(8,128)(2,1)}, u32[]{:S(2)}) copy-start(bf16[512,1024]{1,0:T(8,128)(2,1)} %all-gather.6.cloned.1.call-done.arrived) | copy-start | bytes 3145732
  47.8 25.4 %collective-permute-start.4 = (f32[8,128]{1,0:T(8,128)S(1)}, f32[8,128]{1,0:T(8,128)S(1)}, u32[]{:S(2)}, u32[]{:S(2)}) collective-permute-start(f32[8,128]{1,0:T(8,128)S(1)} %get-tuple-element.40), channel_id=1, source_target_pairs={{0,8},{4,12},{8,0},{12,4},{1,9},{5,13},{9,1},{13,5},{2,10},{6,14},... | collective-permute-start | bytes 12296 | tf_op jit(solution)/shard_map/ppermute | solution.py:182
  68.3 1.2 %copy-start.3 = (bf16[512,1024]{1,0:T(8,128)(2,1)S(1)}, bf16[512,1024]{1,0:T(8,128)(2,1)}, u32[]{:S(2)}) copy-start(bf16[512,1024]{1,0:T(8,128)(2,1)} %all-gather.4.cloned.1.call-done.arrived) | copy-start | bytes 3145732
  70.5 5.2 %collective-permute-start.5 = (f32[8,128]{1,0:T(8,128)S(1)}, f32[8,128]{1,0:T(8,128)S(1)}, u32[]{:S(2)}, u32[]{:S(2)}) collective-permute-start(f32[8,128]{1,0:T(8,128)S(1)} %get-tuple-element.42), channel_id=1, source_target_pairs={{0,12},{4,8},{8,4},{12,0},{1,13},{5,9},{9,5},{13,1},{2,14},{6,10},... | collective-permute-start | bytes 12296 | tf_op jit(solution)/shard_map/ppermute | solution.py:182
  70.7 7.1 %collective-permute-start.6 = (f32[8,128]{1,0:T(8,128)S(1)}, f32[8,128]{1,0:T(8,128)S(1)}, u32[]{:S(2)}, u32[]{:S(2)}) collective-permute-start(f32[8,128]{1,0:T(8,128)S(1)} %get-tuple-element.44), channel_id=1, source_target_pairs={{0,2},{1,3},{2,0},{3,1},{4,6},{5,7},{6,4},{7,5},{8,10},{9,11},{10,... | collective-permute-start | bytes 12296 | tf_op jit(solution)/shard_map/ppermute | solution.py:182
  74.1 3.7 %collective-permute-start.7 = (f32[8,128]{1,0:T(8,128)S(1)}, f32[8,128]{1,0:T(8,128)S(1)}, u32[]{:S(2)}, u32[]{:S(2)}) collective-permute-start(f32[8,128]{1,0:T(8,128)S(1)} %get-tuple-element.45), channel_id=1, source_target_pairs={{0,1},{1,0},{2,3},{3,2},{4,5},{5,4},{6,7},{7,6},{8,9},{9,8},{10,11... | collective-permute-start | bytes 12296 | tf_op jit(solution)/shard_map/ppermute | solution.py:182
  76.7 5.5 %collective-permute-start.8 = (f32[8,128]{1,0:T(8,128)S(1)}, f32[8,128]{1,0:T(8,128)S(1)}, u32[]{:S(2)}, u32[]{:S(2)}) collective-permute-start(f32[8,128]{1,0:T(8,128)S(1)} %get-tuple-element.46), channel_id=1, source_target_pairs={{0,3},{1,2},{2,1},{3,0},{4,7},{5,6},{6,5},{7,4},{8,11},{9,10},{10,... | collective-permute-start | bytes 12296 | tf_op jit(solution)/shard_map/ppermute | solution.py:182
Sparse Core Ops, SparseCore 0:
  9.8 11.7 all-gather.7
  23.1 22.4 all-gather.5
  47.1 21.1 all-gather.3

commit v18 on v14

--- a/solution.py
+++ b/solution.py
@@ -200,22 +200,15 @@
 
 
 BEHIND = 2
-EARLY_ROWS = 192
-HALF = BLOCK // 2
-
-
-FIRST_CUT = 240
-
-
-FIRST_CUT = 240
+NEAR_CUT = 128
+FAR_CUT = 160
 
 
 def plan_slots(sizes):
-    slots = [("blk", 1, 0, BLOCK), ("sub", 2, 0, BLOCK)]
+    slots = [("blk", 1, 0, BLOCK), ("sub", 2, 0, BLOCK), ("sub", 1, 0, NEAR_CUT)]
     slots += [("blk", k, 0, BLOCK) for k in range(2, sizes["blk"])]
-    for k in (1, *range(3, sizes["sub"])):
-        slots += [("sub", k, 0, FIRST_CUT), ("sub", k, FIRST_CUT, BLOCK - FIRST_CUT)]
-    return slots
+    slots += [("sub", k, 0, FAR_CUT) for k in range(3, sizes["sub"])] + [("sub", 1, NEAR_CUT, BLOCK - NEAR_CUT)]
+    return slots + [("sub", k, FAR_CUT, BLOCK - FAR_CUT) for k in range(3, sizes["sub"])]
 
 
 AT_ONCE = 2

time: 64.8 us -> 62.2 us (0.960)
  starting transfers between devices: 26.3 us -> 18.2 us
  waiting for transfers between devices: 24.8 us -> 30.8 us
    ppermute x14, starting transfers between devices: 26.3 us -> 18.2 us  [send(): return lax.ppermute(array, slot[0], pairs(slot[1], sizes[slot[0]]))]
    ppermute x14, waiting for transfers between devices: 24.8 us -> 30.8 us  [send(): return lax.ppermute(array, slot[0], pairs(slot[1], sizes[slot[0]]))]
  transfers between devices with their start and end apart: 14 -> 14, of which waited for: 6 -> 7; matrix products, arithmetic and copies ran while one was open for 0% -> 0% of each run, Pallas kernels for 16% -> 15%
where the time goes in v18:
time: 62.2 us; the launch traced here: 62.1 us
  waiting for transfers between devices  30.8 us (50%)
  starting transfers between devices  18.2 us (29%)
  Pallas kernels  12.3 us (20%)
    ppermute x14, waiting for transfers between devices, send(): return lax.ppermute(array, slot[0], pairs(slot[1], sizes[slot[0]]))  30.8 us
    ppermute x14, starting transfers between devices, send(): return lax.ppermute(array, slot[0], pairs(slot[1], sizes[slot[0]]))  18.2 us
    pallas_call x8, Pallas kernels, work(): pl.pallas_call(functools.partial(slot_kernel, place, *slot[2:], [one for...  6.65 us
    pallas_call x1, Pallas kernels, first_rows(): pl.pallas_call(functools.partial(first_kernel, slots), out_shape=[jax.Sha...  2.69 us
    pallas_call x1, Pallas kernels, prepare(): pl.pallas_call(functools.partial(prepare_kernel, slots), out_shape=[jax.S...  1.77 us
  transfers between devices with their start and end apart: 14, of which 7 were waited for; matrix products, arithmetic and copies ran while one was open for 0% of the time, Pallas kernels for 15%

profile of v18, /device:TPU:0, one launch (start us, length us, event | category | flops | bytes accessed | tf_op | source)
XLA Modules:
  0.0 62.1 jit_solution(7801527687479634273)
XLA Ops:
  0.0 0.0 copy-start
  0.0 0.0 copy-start.2
  0.0 0.0 copy-start.1
  0.0 2.7 %shard_map.57 = (bf16[256,1024]{1,0:T(8,128)(2,1)}, bf16[256,1024]{1,0:T(8,128)(2,1)}) custom-call(s32[1,4]{1,0:T(1,128)} %pick_blk.5, s32[4,4]{1,0:T(4,128)} %pick_sub.5, bf16[1024,1024]{1,0:T(8,128)(2,1)} %embeds.5), custom_call_target="tpu_custom_call" | custom-call | tf_op jit(solution)/shard_map/pallas_call | solution.py:81
  2.7 0.5 collective-permute-start.7
  3.2 3.7 %collective-permute-start.6 = (bf16[256,1024]{1,0:T(8,128)(2,1)}, bf16[256,1024]{1,0:T(8,128)(2,1)S(1)}, u32[]{:S(2)}, u32[]{:S(2)}) collective-permute-start(bf16[256,1024]{1,0:T(8,128)(2,1)} %get-tuple-element.41), channel_id=1, source_target_pairs={{0,2},{1,3},{2,0},{3,1},{4,6},{5,7},{6,4},{7,5},{8,10},{9,11},{10,... | collective-permute-start | bytes 1572872 | tf_op jit(solution)/shard_map/ppermute | solution.py:223
  6.9 0.0 copy-done
  6.9 0.0 copy-done.2
  6.9 0.0 copy-done.1
  6.9 1.2 %shard_map.55 = (bf16[128,1024]{1,0:T(8,128)(2,1)S(1)}, bf16[256,1024]{1,0:T(8,128)(2,1)S(1)}, bf16[256,1024]{1,0:T(8,128)(2,1)S(1)}, bf16[160,1024]{1,0:T(8,128...) custom-call(s32[1,4]{1,0:T(1,128)S(1)} %copy-done.2, s32[4,4]{1,0:T(4,128)S(1)} %copy-done.1, ...), custom_call_target="tpu_custom_call" | custom-call | tf_op jit(solution)/shard_map/pallas_call | solution.py:118
  8.1 1.6 %collective-permute-start.5 = (bf16[128,1024]{1,0:T(8,128)(2,1)S(1)}, bf16[128,1024]{1,0:T(8,128)(2,1)S(1)}, u32[]{:S(2)}, u32[]{:S(2)}) collective-permute-start(bf16[128,1024]{1,0:T(8,128)(2,1)S(1)} %get-tuple-element.40), channel_id=1, source_target_pairs={{0,1},{1,0},{2,3},{3,2},{4,5},{5,4},{6,7},{7,6},{8,9},{9,8},{10,11... | collective-permute-start | bytes 786440 | tf_op jit(solution)/shard_map/ppermute | solution.py:223
  9.7 1.5 %collective-permute-start.4 = (bf16[256,1024]{1,0:T(8,128)(2,1)S(1)}, bf16[256,1024]{1,0:T(8,128)(2,1)S(1)}, u32[]{:S(2)}, u32[]{:S(2)}) collective-permute-start(bf16[256,1024]{1,0:T(8,128)(2,1)S(1)} %get-tuple-element.39), channel_id=1, source_target_pairs={{0,8},{4,12},{8,0},{12,4},{1,9},{5,13},{9,1},{13,5},{2,10},{6,14},... | collective-permute-start | bytes 1572872 | tf_op jit(solution)/shard_map/ppermute | solution.py:223
  11.2 0.0 collective-permute-start.3
  11.2 13.4 %collective-permute-done.5.arrived = bf16[128,1024]{1,0:T(8,128)(2,1)S(1)} collective-permute-done((bf16[128,1024]{1,0:T(8,128)(2,1)S(1)}, bf16[128,1024]{1,0:T(8,128)(2,1)S(1)}, u32[]{:S(2)}, u32[]{:S(2)}) %collective-permute-start.5) | collective-permute-done | bytes 262176 | tf_op jit(solution)/shard_map/ppermute | solution.py:223
  24.6 1.3 %collective-permute-start.2 = (bf16[160,1024]{1,0:T(8,128)(2,1)S(1)}, bf16[160,1024]{1,0:T(8,128)(2,1)S(1)}, u32[]{:S(2)}, u32[]{:S(2)}) collective-permute-start(bf16[160,1024]{1,0:T(8,128)(2,1)S(1)} %get-tuple-element.37), channel_id=1, source_target_pairs={{0,3},{1,2},{2,1},{3,0},{4,7},{5,6},{6,5},{7,4},{8,11},{9,10},{10,... | collective-permute-start | bytes 983048 | tf_op jit(solution)/shard_map/ppermute | solution.py:223
  25.9 0.0 collective-permute-done.7.arrived
  25.9 1.6 %collective-permute-start.1 = (bf16[128,1024]{1,0:T(8,128)(2,1)S(1)}, bf16[128,1024]{1,0:T(8,128)(2,1)S(1)}, u32[]{:S(2)}, u32[]{:S(2)}) collective-permute-start(bf16[128,1024]{1,0:T(8,128)(2,1)S(1)} %get-tuple-element.36), channel_id=1, source_target_pairs={{0,1},{1,0},{2,3},{3,2},{4,5},{5,4},{6,7},{7,6},{8,9},{9,8},{10,11... | collective-permute-start | bytes 786440 | tf_op jit(solution)/shard_map/ppermute | solution.py:223
  27.5 0.0 copy-done.3
  27.5 0.0 copy-done.4
  27.5 1.8 %shard_map.56 = (bf16[1024,1024]{1,0:T(8,128)(2,1)S(1)}, f32[8,4,128]{2,1,0:T(4,128)S(1)}, f32[8,8,128]{2,1,0:T(8,128)S(1)}) custom-call(s32[1,4]{1,0:T(1,128)S(1)} %copy-done.2, s32[4,4]{1,0:T(4,128)S(1)} %copy-done.1, s32[1,16]{1,0:T(1,128)S(1)} %copy-done.3, s32[1,16]{1,0:T(1,128)S(1)} %copy-done.4, bf16[1024,1024]{1,0:T(8,128)(2,1)S(1)} %copy-done), custom_call_target="tpu_custom_call" | custom-call | tf_op jit(solution)/shard_map/pallas_call | solution.py:150
  29.3 1.0 %shard_map.58 = (f32[8,128]{1,0:T(8,128)S(1)}, f32[8,128]{1,0:T(8,128)S(1)}) custom-call(bf16[256,1024]{1,0:T(8,128)(2,1)S(1)} %collective-permute-done.7.arrived, bf16[1024,1024]{1,0:T(8,128)(2,1)S(1)} %get-tuple-element.33.units, f32[8,4,128]{2,1,0:T(4,128)S(1)} %get-tuple-element.34.live, f32[8,8,128]{2,1,0:T(8,128)S(1)} %get-tuple-element.35.mine, ...), custom_call_target="tpu_custom_call" | custom-call | tf_op jit(solution)/shard_map/pallas_call | solution.py:193
  30.3 7.9 %collective-permute-done.6.arrived = bf16[256,1024]{1,0:T(8,128)(2,1)S(1)} collective-permute-done((bf16[256,1024]{1,0:T(8,128)(2,1)}, bf16[256,1024]{1,0:T(8,128)(2,1)S(1)}, u32[]{:S(2)}, u32[]{:S(2)}) %collective-permute-start.6) | collective-permute-done | bytes 524320 | tf_op jit(solution)/shard_map/ppermute | solution.py:223
  38.2 0.0 collective-permute-start.8
  38.2 1.2 %collective-permute-done.8.rest_0_ = f32[8,128]{1,0:T(8,128)S(1)} collective-permute-done((f32[8,128]{1,0:T(8,128)S(1)}, f32[8,128]{1,0:T(8,128)S(1)}, u32[]{:S(2)}, u32[]{:S(2)}) %collective-permute-start.8) | collective-permute-done | bytes 4128 | tf_op jit(solution)/shard_map/ppermute | solution.py:223
  39.4 3.4 %collective-permute-start = (bf16[96,1024]{1,0:T(8,128)(2,1)S(1)}, bf16[96,1024]{1,0:T(8,128)(2,1)S(1)}, u32[]{:S(2)}, u32[]{:S(2)}) collective-permute-start(bf16[96,1024]{1,0:T(8,128)(2,1)S(1)} %get-tuple-element.32), channel_id=1, source_target_pairs={{0,3},{1,2},{2,1},{3,0},{4,7},{5,6},{6,5},{7,4},{8,11},{9,10},{10,... | collective-permute-start | bytes 589832 | tf_op jit(solution)/shard_map/ppermute | solution.py:223
  42.7 1.0 %shard_map.59 = (f32[8,128]{1,0:T(8,128)S(1)}, f32[8,128]{1,0:T(8,128)S(1)}) custom-call(bf16[256,1024]{1,0:T(8,128)(2,1)S(1)} %collective-permute-done.6.arrived, bf16[1024,1024]{1,0:T(8,128)(2,1)S(1)} %get-tuple-element.33.units, f32[8,4,128]{2,1,0:T(4,128)S(1)} %get-tuple-element.34.live, f32[8,8,128]{2,1,0:T(8,128)S(1)} %get-tuple-element.35.mine, ...), custom_call_target="tpu_custom_call" | custom-call | tf_op jit(solution)/shard_map/pallas_call | solution.py:193
  43.7 0.7 %shard_map.60 = (f32[8,128]{1,0:T(8,128)S(1)}, f32[8,128]{1,0:T(8,128)S(1)}) custom-call(bf16[128,1024]{1,0:T(8,128)(2,1)S(1)} %collective-permute-done.5.arrived, bf16[1024,1024]{1,0:T(8,128)(2,1)S(1)} %get-tuple-element.33.units, f32[8,4,128]{2,1,0:T(4,128)S(1)} %get-tuple-element.34.live, f32[8,8,128]{2,1,0:T(8,128)S(1)} %get-tuple-element.35.mine, ...), custom_call_target="tpu_custom_call" | custom-call | tf_op jit(solution)/shard_map/pallas_call | solution.py:193
  44.4 0.0 collective-permute-done.4.arrived
  44.4 1.0 %shard_map.61 = (f32[8,128]{1,0:T(8,128)S(1)}, f32[8,128]{1,0:T(8,128)S(1)}) custom-call(bf16[256,1024]{1,0:T(8,128)(2,1)S(1)} %collective-permute-done.4.arrived, bf16[1024,1024]{1,0:T(8,128)(2,1)S(1)} %get-tuple-element.33.units, f32[8,4,128]{2,1,0:T(4,128)S(1)} %get-tuple-element.34.live, f32[8,8,128]{2,1,0:T(8,128)S(1)} %get-tuple-element.35.mine, ...), custom_call_target="tpu_custom_call" | custom-call | tf_op jit(solution)/shard_map/pallas_call | solution.py:193
  45.3 1.6 %collective-permute-start.9 = (f32[8,128]{1,0:T(8,128)S(1)}, f32[8,128]{1,0:T(8,128)S(1)}, u32[]{:S(2)}, u32[]{:S(2)}) collective-permute-start(f32[8,128]{1,0:T(8,128)S(1)} %get-tuple-element.49), channel_id=1, source_target_pairs={{0,8},{4,12},{8,0},{12,4},{1,9},{5,13},{9,1},{13,5},{2,10},{6,14},... | collective-permute-start | bytes 12296 | tf_op jit(solution)/shard_map/ppermute | solution.py:223
  46.9 0.0 collective-permute-done.3.arrived
  46.9 1.0 %shard_map.62 = (f32[8,128]{1,0:T(8,128)S(1)}, f32[8,128]{1,0:T(8,128)S(1)}) custom-call(bf16[256,1024]{1,0:T(8,128)(2,1)S(1)} %collective-permute-done.3.arrived, bf16[1024,1024]{1,0:T(8,128)(2,1)S(1)} %get-tuple-element.33.units, f32[8,4,128]{2,1,0:T(4,128)S(1)} %get-tuple-element.34.live, f32[8,8,128]{2,1,0:T(8,128)S(1)} %get-tuple-element.35.mine, ...), custom_call_target="tpu_custom_call" | custom-call | tf_op jit(solution)/shard_map/pallas_call | solution.py:193
  47.9 0.1 collective-permute-start.10
  48.0 0.0 collective-permute-done.2.arrived
  48.0 1.0 %collective-permute-done.9.rest_0_ = f32[8,128]{1,0:T(8,128)S(1)} collective-permute-done((f32[8,128]{1,0:T(8,128)S(1)}, f32[8,128]{1,0:T(8,128)S(1)}, u32[]{:S(2)}, u32[]{:S(2)}) %collective-permute-start.9) | collective-permute-done | bytes 4128 | tf_op jit(solution)/shard_map/ppermute | solution.py:223
  49.0 0.8 %shard_map.63 = (f32[8,128]{1,0:T(8,128)S(1)}, f32[8,128]{1,0:T(8,128)S(1)}) custom-call(bf16[160,1024]{1,0:T(8,128)(2,1)S(1)} %collective-permute-done.2.arrived, bf16[1024,1024]{1,0:T(8,128)(2,1)S(1)} %get-tuple-element.33.units, f32[8,4,128]{2,1,0:T(4,128)S(1)} %get-tuple-element.34.live, f32[8,8,128]{2,1,0:T(8,128)S(1)} %get-tuple-element.35.mine, ...), custom_call_target="tpu_custom_call" | custom-call | tf_op jit(solution)/shard_map/pallas_call | solution.py:193
  49.8 0.0 collective-permute-done.1.arrived
  49.8 1.2 %collective-permute-done.10.rest_0_ = f32[8,128]{1,0:T(8,128)S(1)} collective-permute-done((f32[8,128]{1,0:T(8,128)S(1)}, f32[8,128]{1,0:T(8,128)S(1)}, u32[]{:S(2)}, u32[]{:S(2)}) %collective-permute-start.10) | collective-permute-done | bytes 4128 | tf_op jit(solution)/shard_map/ppermute | solution.py:223
  51.0 0.7 %shard_map.64 = (f32[8,128]{1,0:T(8,128)S(1)}, f32[8,128]{1,0:T(8,128)S(1)}) custom-call(bf16[128,1024]{1,0:T(8,128)(2,1)S(1)} %collective-permute-done.1.arrived, bf16[1024,1024]{1,0:T(8,128)(2,1)S(1)} %get-tuple-element.33.units, f32[8,4,128]{2,1,0:T(4,128)S(1)} %get-tuple-element.34.live, f32[8,8,128]{2,1,0:T(8,128)S(1)} %get-tuple-element.35.mine, ...), custom_call_target="tpu_custom_call" | custom-call | tf_op jit(solution)/shard_map/pallas_call | solution.py:193
  51.7 0.1 collective-permute-start.11
  51.7 1.7 %collective-permute-start.12 = (f32[8,128]{1,0:T(8,128)S(1)}, f32[8,128]{1,0:T(8,128)S(1)}, u32[]{:S(2)}, u32[]{:S(2)}) collective-permute-start(f32[8,128]{1,0:T(8,128)S(1)} %get-tuple-element.57), channel_id=1, source_target_pairs={{0,2},{1,3},{2,0},{3,1},{4,6},{5,7},{6,4},{7,5},{8,10},{9,11},{10,... | collective-permute-start | bytes 12296 | tf_op jit(solution)/shard_map/ppermute | solution.py:223
  53.5 0.0 collective-permute-done.arrived
  53.5 1.9 %collective-permute-done.11.rest_0_ = f32[8,128]{1,0:T(8,128)S(1)} collective-permute-done((f32[8,128]{1,0:T(8,128)S(1)}, f32[8,128]{1,0:T(8,128)S(1)}, u32[]{:S(2)}, u32[]{:S(2)}) %collective-permute-start.11) | collective-permute-done | bytes 4128 | tf_op jit(solution)/shard_map/ppermute | solution.py:223
  55.3 0.7 %shard_map.65 = (f32[8,128]{1,0:T(8,128)S(1)}, f32[8,128]{1,0:T(8,128)S(1)}) custom-call(bf16[96,1024]{1,0:T(8,128)(2,1)S(1)} %collective-permute-done.arrived, bf16[1024,1024]{1,0:T(8,128)(2,1)S(1)} %get-tuple-element.33.units, f32[8,4,128]{2,1,0:T(4,128)S(1)} %get-tuple-element.34.live, f32[8,8,128]{2,1,0:T(8,128)S(1)} %get-tuple-element.35.mine, ...), custom_call_target="tpu_custom_call" | custom-call | tf_op jit(solution)/shard_map/pallas_call | solution.py:193
  56.0 1.2 %collective-permute-start.13 = (f32[8,128]{1,0:T(8,128)S(1)}, f32[8,128]{1,0:T(8,128)S(1)}, u32[]{:S(2)}, u32[]{:S(2)}) collective-permute-start(f32[8,128]{1,0:T(8,128)S(1)} %get-tuple-element.58), channel_id=1, source_target_pairs={{0,3},{1,2},{2,1},{3,0},{4,7},{5,6},{6,5},{7,4},{8,11},{9,10},{10,... | collective-permute-start | bytes 12296 | tf_op jit(solution)/shard_map/ppermute | solution.py:223
  57.2 0.0 collective-permute-done.12
  57.2 4.3 %collective-permute-done.13 = f32[8,128]{1,0:T(8,128)S(1)} collective-permute-done((f32[8,128]{1,0:T(8,128)S(1)}, f32[8,128]{1,0:T(8,128)S(1)}, u32[]{:S(2)}, u32[]{:S(2)}) %collective-permute-start.13) | collective-permute-done | bytes 4128 | tf_op jit(solution)/shard_map/ppermute | solution.py:223
  61.5 0.6 fusion.2
  (3 shorter events, 0.0 us)
Async XLA Ops:
  0.0 6.9 %copy-start = (bf16[1024,1024]{1,0:T(8,128)(2,1)S(1)}, bf16[1024,1024]{1,0:T(8,128)(2,1)}, u32[]{:S(2)}) copy-start(bf16[1024,1024]{1,0:T(8,128)(2,1)} %embeds.5) | copy-start | bytes 6291460
  0.0 6.9 %copy-start.2 = (s32[1,4]{1,0:T(1,128)S(1)}, s32[1,4]{1,0:T(1,128)}, u32[]{:S(2)}) copy-start(s32[1,4]{1,0:T(1,128)} %pick_blk.5) | copy-start | bytes 52
  0.0 6.9 %copy-start.1 = (s32[4,4]{1,0:T(4,128)S(1)}, s32[4,4]{1,0:T(4,128)}, u32[]{:S(2)}) copy-start(s32[4,4]{1,0:T(4,128)} %pick_sub.5) | copy-start | bytes 196
  0.0 27.5 %copy-start.3 = (s32[1,16]{1,0:T(1,128)S(1)}, s32[1,16]{1,0:T(1,128)}, u32[]{:S(2)}) copy-start(s32[1,16]{1,0:T(1,128)} %mask_blk.1) | copy-start | bytes 196
  0.0 27.5 %copy-start.4 = (s32[1,16]{1,0:T(1,128)S(1)}, s32[1,16]{1,0:T(1,128)}, u32[]{:S(2)}) copy-start(s32[1,16]{1,0:T(1,128)} %mask_sub.1) | copy-start | bytes 196
  2.7 23.2 %collective-permute-start.7 = (bf16[256,1024]{1,0:T(8,128)(2,1)}, bf16[256,1024]{1,0:T(8,128)(2,1)S(1)}, u32[]{:S(2)}, u32[]{:S(2)}) collective-permute-start(bf16[256,1024]{1,0:T(8,128)(2,1)} %get-tuple-element.42), channel_id=1, source_target_pairs={{0,4},{4,0},{8,12},{12,8},{1,5},{5,1},{9,13},{13,9},{2,6},{6,2},{1... | collective-permute-start | bytes 1572872 | tf_op jit(solution)/shard_map/ppermute | solution.py:223
  3.2 34.9 %collective-permute-start.6 = (bf16[256,1024]{1,0:T(8,128)(2,1)}, bf16[256,1024]{1,0:T(8,128)(2,1)S(1)}, u32[]{:S(2)}, u32[]{:S(2)}) collective-permute-start(bf16[256,1024]{1,0:T(8,128)(2,1)} %get-tuple-element.41), channel_id=1, source_target_pairs={{0,2},{1,3},{2,0},{3,1},{4,6},{5,7},{6,4},{7,5},{8,10},{9,11},{10,... | collective-permute-start | bytes 1572872 | tf_op jit(solution)/shard_map/ppermute | solution.py:223
  8.1 16.5 %collective-permute-start.5 = (bf16[128,1024]{1,0:T(8,128)(2,1)S(1)}, bf16[128,1024]{1,0:T(8,128)(2,1)S(1)}, u32[]{:S(2)}, u32[]{:S(2)}) collective-permute-start(bf16[128,1024]{1,0:T(8,128)(2,1)S(1)} %get-tuple-element.40), channel_id=1, source_target_pairs={{0,1},{1,0},{2,3},{3,2},{4,5},{5,4},{6,7},{7,6},{8,9},{9,8},{10,11... | collective-permute-start | bytes 786440 | tf_op jit(solution)/shard_map/ppermute | solution.py:223
  9.7 34.6 %collective-permute-start.4 = (bf16[256,1024]{1,0:T(8,128)(2,1)S(1)}, bf16[256,1024]{1,0:T(8,128)(2,1)S(1)}, u32[]{:S(2)}, u32[]{:S(2)}) collective-permute-start(bf16[256,1024]{1,0:T(8,128)(2,1)S(1)} %get-tuple-element.39), channel_id=1, source_target_pairs={{0,8},{4,12},{8,0},{12,4},{1,9},{5,13},{9,1},{13,5},{2,10},{6,14},... | collective-permute-start | bytes 1572872 | tf_op jit(solution)/shard_map/ppermute | solution.py:223
  11.2 35.7 %collective-permute-start.3 = (bf16[256,1024]{1,0:T(8,128)(2,1)S(1)}, bf16[256,1024]{1,0:T(8,128)(2,1)S(1)}, u32[]{:S(2)}, u32[]{:S(2)}) collective-permute-start(bf16[256,1024]{1,0:T(8,128)(2,1)S(1)} %get-tuple-element.38), channel_id=1, source_target_pairs={{0,12},{4,8},{8,4},{12,0},{1,13},{5,9},{9,5},{13,1},{2,14},{6,10},... | collective-permute-start | bytes 1572872 | tf_op jit(solution)/shard_map/ppermute | solution.py:223
  24.6 23.4 %collective-permute-start.2 = (bf16[160,1024]{1,0:T(8,128)(2,1)S(1)}, bf16[160,1024]{1,0:T(8,128)(2,1)S(1)}, u32[]{:S(2)}, u32[]{:S(2)}) collective-permute-start(bf16[160,1024]{1,0:T(8,128)(2,1)S(1)} %get-tuple-element.37), channel_id=1, source_target_pairs={{0,3},{1,2},{2,1},{3,0},{4,7},{5,6},{6,5},{7,4},{8,11},{9,10},{10,... | collective-permute-start | bytes 983048 | tf_op jit(solution)/shard_map/ppermute | solution.py:223
  25.9 23.9 %collective-permute-start.1 = (bf16[128,1024]{1,0:T(8,128)(2,1)S(1)}, bf16[128,1024]{1,0:T(8,128)(2,1)S(1)}, u32[]{:S(2)}, u32[]{:S(2)}) collective-permute-start(bf16[128,1024]{1,0:T(8,128)(2,1)S(1)} %get-tuple-element.36), channel_id=1, source_target_pairs={{0,1},{1,0},{2,3},{3,2},{4,5},{5,4},{6,7},{7,6},{8,9},{9,8},{10,11... | collective-permute-start | bytes 786440 | tf_op jit(solution)/shard_map/ppermute | solution.py:223
  38.2 1.2 %collective-permute-start.8 = (f32[8,128]{1,0:T(8,128)S(1)}, f32[8,128]{1,0:T(8,128)S(1)}, u32[]{:S(2)}, u32[]{:S(2)}) collective-permute-start(f32[8,128]{1,0:T(8,128)S(1)} %get-tuple-element.45), channel_id=1, source_target_pairs={{0,4},{4,0},{8,12},{12,8},{1,5},{5,1},{9,13},{13,9},{2,6},{6,2},{1... | collective-permute-start | bytes 12296 | tf_op jit(solution)/shard_map/ppermute | solution.py:223
  39.4 14.1 %collective-permute-start = (bf16[96,1024]{1,0:T(8,128)(2,1)S(1)}, bf16[96,1024]{1,0:T(8,128)(2,1)S(1)}, u32[]{:S(2)}, u32[]{:S(2)}) collective-permute-start(bf16[96,1024]{1,0:T(8,128)(2,1)S(1)} %get-tuple-element.32), channel_id=1, source_target_pairs={{0,3},{1,2},{2,1},{3,0},{4,7},{5,6},{6,5},{7,4},{8,11},{9,10},{10,... | collective-permute-start | bytes 589832 | tf_op jit(solution)/shard_map/ppermute | solution.py:223
  45.3 3.7 %collective-permute-start.9 = (f32[8,128]{1,0:T(8,128)S(1)}, f32[8,128]{1,0:T(8,128)S(1)}, u32[]{:S(2)}, u32[]{:S(2)}) collective-permute-start(f32[8,128]{1,0:T(8,128)S(1)} %get-tuple-element.49), channel_id=1, source_target_pairs={{0,8},{4,12},{8,0},{12,4},{1,9},{5,13},{9,1},{13,5},{2,10},{6,14},... | collective-permute-start | bytes 12296 | tf_op jit(solution)/shard_map/ppermute | solution.py:223
  47.9 3.1 %collective-permute-start.10 = (f32[8,128]{1,0:T(8,128)S(1)}, f32[8,128]{1,0:T(8,128)S(1)}, u32[]{:S(2)}, u32[]{:S(2)}) collective-permute-start(f32[8,128]{1,0:T(8,128)S(1)} %get-tuple-element.51), channel_id=1, source_target_pairs={{0,12},{4,8},{8,4},{12,0},{1,13},{5,9},{9,5},{13,1},{2,14},{6,10},... | collective-permute-start | bytes 12296 | tf_op jit(solution)/shard_map/ppermute | solution.py:223
  51.7 3.7 %collective-permute-start.11 = (f32[8,128]{1,0:T(8,128)S(1)}, f32[8,128]{1,0:T(8,128)S(1)}, u32[]{:S(2)}, u32[]{:S(2)}) collective-permute-start(f32[8,128]{1,0:T(8,128)S(1)} %get-tuple-element.54), channel_id=1, source_target_pairs={{0,1},{1,0},{2,3},{3,2},{4,5},{5,4},{6,7},{7,6},{8,9},{9,8},{10,11... | collective-permute-start | bytes 12296 | tf_op jit(solution)/shard_map/ppermute | solution.py:223
  51.7 5.4 %collective-permute-start.12 = (f32[8,128]{1,0:T(8,128)S(1)}, f32[8,128]{1,0:T(8,128)S(1)}, u32[]{:S(2)}, u32[]{:S(2)}) collective-permute-start(f32[8,128]{1,0:T(8,128)S(1)} %get-tuple-element.57), channel_id=1, source_target_pairs={{0,2},{1,3},{2,0},{3,1},{4,6},{5,7},{6,4},{7,5},{8,10},{9,11},{10,... | collective-permute-start | bytes 12296 | tf_op jit(solution)/shard_map/ppermute | solution.py:223
  56.0 5.5 %collective-permute-start.13 = (f32[8,128]{1,0:T(8,128)S(1)}, f32[8,128]{1,0:T(8,128)S(1)}, u32[]{:S(2)}, u32[]{:S(2)}) collective-permute-start(f32[8,128]{1,0:T(8,128)S(1)} %get-tuple-element.58), channel_id=1, source_target_pairs={{0,3},{1,2},{2,1},{3,0},{4,7},{5,6},{6,5},{7,4},{8,11},{9,10},{10,... | collective-permute-start | bytes 12296 | tf_op jit(solution)/shard_map/ppermute | solution.py:223

commit v19 on v16

--- a/solution.py
+++ b/solution.py
@@ -73,7 +73,7 @@
         copy.wait()
 
 
-PART = 64
+PART = 128
 
 
 def first_rows(slots, pick_blk, pick_sub, embeds):
@@ -200,10 +200,6 @@
 
 
 BEHIND = 2
-EARLY_ROWS = 192
-HALF = BLOCK // 2
-
-
 FIRST_CUT = 128
 
 

time: 57.2 us -> 57.1 us (level)
  no operation moved by 1% of the time
where the time goes in v19:
time: 57.1 us; the launch traced here: 56 us
  waiting for transfers between devices  22.4 us (39%)
  starting transfers between devices  21.4 us (37%)
  Pallas kernels  11.5 us (20%)
  other arithmetic  0.6 us (1%)
    ppermute x13, waiting for transfers between devices, send(): return lax.ppermute(array, slot[0], pairs(slot[1], sizes[slot[0]]))  22.4 us
    ppermute x13, starting transfers between devices, send(): return lax.ppermute(array, slot[0], pairs(slot[1], sizes[slot[0]]))  21.4 us
    pallas_call x7, Pallas kernels, work(): pl.pallas_call(functools.partial(slot_kernel, place, *slot[2:], [one for...  6.29 us
    pallas_call x1, Pallas kernels, first_rows(): pl.pallas_call(functools.partial(first_kernel, slots), out_shape=[jax.Sha...  2.6 us
    pallas_call x1, Pallas kernels, prepare(): pl.pallas_call(functools.partial(prepare_kernel, slots), out_shape=[jax.S...  1.77 us
  transfers between devices with their start and end apart: 13, of which 4 were waited for; matrix products, arithmetic and copies ran while one was open for 0% of the time, Pallas kernels for 16%

profile of v19, /device:TPU:0, one launch (start us, length us, event | category | flops | bytes accessed | tf_op | source)
XLA Modules:
  0.0 56.0 jit_solution(10900560649334699507)
XLA Ops:
  0.0 0.0 copy-start
  0.0 0.0 copy-start.2
  0.0 0.0 copy-start.1
  0.0 0.0 copy-start.3
  0.0 0.0 copy-start.4
  0.0 2.6 %shard_map.57 = (bf16[256,1024]{1,0:T(8,128)(2,1)}, bf16[256,1024]{1,0:T(8,128)(2,1)}) custom-call(s32[1,4]{1,0:T(1,128)} %pick_blk.5, s32[4,4]{1,0:T(4,128)} %pick_sub.5, bf16[1024,1024]{1,0:T(8,128)(2,1)} %embeds.5), custom_call_target="tpu_custom_call" | custom-call | tf_op jit(solution)/shard_map/pallas_call | solution.py:81
  2.6 0.5 collective-permute-start.6
  3.2 3.7 %collective-permute-start.5 = (bf16[256,1024]{1,0:T(8,128)(2,1)}, bf16[256,1024]{1,0:T(8,128)(2,1)S(1)}, u32[]{:S(2)}, u32[]{:S(2)}) collective-permute-start(bf16[256,1024]{1,0:T(8,128)(2,1)} %get-tuple-element.37), channel_id=1, source_target_pairs={{0,2},{1,3},{2,0},{3,1},{4,6},{5,7},{6,4},{7,5},{8,10},{9,11},{10,... | collective-permute-start | bytes 1572872 | tf_op jit(solution)/shard_map/ppermute | solution.py:223
  6.8 0.0 copy-done
  6.8 0.0 copy-done.2
  6.8 0.0 copy-done.1
  6.8 0.8 %shard_map.55 = (bf16[256,1024]{1,0:T(8,128)(2,1)S(1)}, bf16[256,1024]{1,0:T(8,128)(2,1)S(1)}, bf16[256,1024]{1,0:T(8,128)(2,1)S(1)}, bf16[128,1024]{1,0:T(8,128)(2,1)S(1)}, bf16[128,1024]{1,0:T(8,128)(2,1)S(1)}) custom-call(s32[1,4]{1,0:T(1,128)S(1)} %copy-done.2, s32[4,4]{1,0:T(4,128)S(1)} %copy-done.1, bf16[1024,1024]{1,0:T(8,128)(2,1)S(1)} %copy-done), custom_call_target="tpu_custom_call" | custom-call | tf_op jit(solution)/shard_map/pallas_call | solution.py:118
  7.7 1.6 %collective-permute-start.4 = (bf16[256,1024]{1,0:T(8,128)(2,1)S(1)}, bf16[256,1024]{1,0:T(8,128)(2,1)S(1)}, u32[]{:S(2)}, u32[]{:S(2)}) collective-permute-start(bf16[256,1024]{1,0:T(8,128)(2,1)S(1)} %get-tuple-element.36), channel_id=1, source_target_pairs={{0,1},{1,0},{2,3},{3,2},{4,5},{5,4},{6,7},{7,6},{8,9},{9,8},{10,11... | collective-permute-start | bytes 1572872 | tf_op jit(solution)/shard_map/ppermute | solution.py:223
  9.3 1.5 %collective-permute-start.3 = (bf16[256,1024]{1,0:T(8,128)(2,1)S(1)}, bf16[256,1024]{1,0:T(8,128)(2,1)S(1)}, u32[]{:S(2)}, u32[]{:S(2)}) collective-permute-start(bf16[256,1024]{1,0:T(8,128)(2,1)S(1)} %get-tuple-element.35), channel_id=1, source_target_pairs={{0,8},{4,12},{8,0},{12,4},{1,9},{5,13},{9,1},{13,5},{2,10},{6,14},... | collective-permute-start | bytes 1572872 | tf_op jit(solution)/shard_map/ppermute | solution.py:223
  10.8 0.0 collective-permute-start.2
  10.8 0.0 collective-permute-done.6.arrived
  10.8 0.2 collective-permute-start.1
  11.0 20.1 %collective-permute-done.5.arrived = bf16[256,1024]{1,0:T(8,128)(2,1)S(1)} collective-permute-done((bf16[256,1024]{1,0:T(8,128)(2,1)}, bf16[256,1024]{1,0:T(8,128)(2,1)S(1)}, u32[]{:S(2)}, u32[]{:S(2)}) %collective-permute-start.5) | collective-permute-done | bytes 524320 | tf_op jit(solution)/shard_map/ppermute | solution.py:223
  31.1 3.7 %collective-permute-start = (bf16[128,1024]{1,0:T(8,128)(2,1)S(1)}, bf16[128,1024]{1,0:T(8,128)(2,1)S(1)}, u32[]{:S(2)}, u32[]{:S(2)}) collective-permute-start(bf16[128,1024]{1,0:T(8,128)(2,1)S(1)} %get-tuple-element.29), channel_id=1, source_target_pairs={{0,3},{1,2},{2,1},{3,0},{4,7},{5,6},{6,5},{7,4},{8,11},{9,10},{10,... | collective-permute-start | bytes 786440 | tf_op jit(solution)/shard_map/ppermute | solution.py:223
  34.8 0.0 copy-done.3
  34.8 0.0 copy-done.4
  34.8 1.8 %shard_map.56 = (bf16[1024,1024]{1,0:T(8,128)(2,1)S(1)}, f32[7,4,128]{2,1,0:T(4,128)S(1)}, f32[7,8,128]{2,1,0:T(8,128)S(1)}) custom-call(s32[1,4]{1,0:T(1,128)S(1)} %copy-done.2, s32[4,4]{1,0:T(4,128)S(1)} %copy-done.1, s32[1,16]{1,0:T(1,128)S(1)} %copy-done.3, s32[1,16]{1,0:T(1,128)S(1)} %copy-done.4, bf16[1024,1024]{1,0:T(8,128)(2,1)S(1)} %copy-done), custom_call_target="tpu_custom_call" | custom-call | tf_op jit(solution)/shard_map/pallas_call | solution.py:150
  36.6 1.0 %shard_map.58 = (f32[8,128]{1,0:T(8,128)S(1)}, f32[8,128]{1,0:T(8,128)S(1)}) custom-call(bf16[256,1024]{1,0:T(8,128)(2,1)S(1)} %collective-permute-done.6.arrived, bf16[1024,1024]{1,0:T(8,128)(2,1)S(1)} %get-tuple-element.30.units, f32[7,4,128]{2,1,0:T(4,128)S(1)} %get-tuple-element.31.live, f32[7,8,128]{2,1,0:T(8,128)S(1)} %get-tuple-element.32.mine, ...), custom_call_target="tpu_custom_call" | custom-call | tf_op jit(solution)/shard_map/pallas_call | solution.py:193
  37.6 0.0 collective-permute-done.4.arrived
  37.6 0.1 collective-permute-start.7
  37.7 1.0 %shard_map.59 = (f32[8,128]{1,0:T(8,128)S(1)}, f32[8,128]{1,0:T(8,128)S(1)}) custom-call(bf16[256,1024]{1,0:T(8,128)(2,1)S(1)} %collective-permute-done.5.arrived, bf16[1024,1024]{1,0:T(8,128)(2,1)S(1)} %get-tuple-element.30.units, f32[7,4,128]{2,1,0:T(4,128)S(1)} %get-tuple-element.31.live, f32[7,8,128]{2,1,0:T(8,128)S(1)} %get-tuple-element.32.mine, ...), custom_call_target="tpu_custom_call" | custom-call | tf_op jit(solution)/shard_map/pallas_call | solution.py:193
  38.7 0.2 collective-permute-done.7.rest_0_
  38.9 1.0 %shard_map.60 = (f32[8,128]{1,0:T(8,128)S(1)}, f32[8,128]{1,0:T(8,128)S(1)}) custom-call(bf16[256,1024]{1,0:T(8,128)(2,1)S(1)} %collective-permute-done.4.arrived, bf16[1024,1024]{1,0:T(8,128)(2,1)S(1)} %get-tuple-element.30.units, f32[7,4,128]{2,1,0:T(4,128)S(1)} %get-tuple-element.31.live, f32[7,8,128]{2,1,0:T(8,128)S(1)} %get-tuple-element.32.mine, ...), custom_call_target="tpu_custom_call" | custom-call | tf_op jit(solution)/shard_map/pallas_call | solution.py:193
  39.9 0.0 collective-permute-done.3.arrived
  39.9 1.0 %shard_map.61 = (f32[8,128]{1,0:T(8,128)S(1)}, f32[8,128]{1,0:T(8,128)S(1)}) custom-call(bf16[256,1024]{1,0:T(8,128)(2,1)S(1)} %collective-permute-done.3.arrived, bf16[1024,1024]{1,0:T(8,128)(2,1)S(1)} %get-tuple-element.30.units, f32[7,4,128]{2,1,0:T(4,128)S(1)} %get-tuple-element.31.live, f32[7,8,128]{2,1,0:T(8,128)S(1)} %get-tuple-element.32.mine, ...), custom_call_target="tpu_custom_call" | custom-call | tf_op jit(solution)/shard_map/pallas_call | solution.py:193
  40.9 1.6 %collective-permute-start.8 = (f32[8,128]{1,0:T(8,128)S(1)}, f32[8,128]{1,0:T(8,128)S(1)}, u32[]{:S(2)}, u32[]{:S(2)}) collective-permute-start(f32[8,128]{1,0:T(8,128)S(1)} %get-tuple-element.45), channel_id=1, source_target_pairs={{0,8},{4,12},{8,0},{12,4},{1,9},{5,13},{9,1},{13,5},{2,10},{6,14},... | collective-permute-start | bytes 12296 | tf_op jit(solution)/shard_map/ppermute | solution.py:223
  42.4 0.0 collective-permute-done.2.arrived
  42.4 1.0 %shard_map.62 = (f32[8,128]{1,0:T(8,128)S(1)}, f32[8,128]{1,0:T(8,128)S(1)}) custom-call(bf16[256,1024]{1,0:T(8,128)(2,1)S(1)} %collective-permute-done.2.arrived, bf16[1024,1024]{1,0:T(8,128)(2,1)S(1)} %get-tuple-element.30.units, f32[7,4,128]{2,1,0:T(4,128)S(1)} %get-tuple-element.31.live, f32[7,8,128]{2,1,0:T(8,128)S(1)} %get-tuple-element.32.mine, ...), custom_call_target="tpu_custom_call" | custom-call | tf_op jit(solution)/shard_map/pallas_call | solution.py:193
  43.4 0.3 collective-permute-start.9
  43.7 0.0 collective-permute-start.10
  43.7 0.0 collective-permute-done.1.arrived
  43.7 4.9 %collective-permute-start.11 = (f32[8,128]{1,0:T(8,128)S(1)}, f32[8,128]{1,0:T(8,128)S(1)}, u32[]{:S(2)}, u32[]{:S(2)}) collective-permute-start(f32[8,128]{1,0:T(8,128)S(1)} %get-tuple-element.51), channel_id=1, source_target_pairs={{0,1},{1,0},{2,3},{3,2},{4,5},{5,4},{6,7},{7,6},{8,9},{9,8},{10,11... | collective-permute-start | bytes 12296 | tf_op jit(solution)/shard_map/ppermute | solution.py:223
  48.6 0.0 collective-permute-done.8.rest_0_
  48.6 0.7 %shard_map.63 = (f32[8,128]{1,0:T(8,128)S(1)}, f32[8,128]{1,0:T(8,128)S(1)}) custom-call(bf16[128,1024]{1,0:T(8,128)(2,1)S(1)} %collective-permute-done.1.arrived, bf16[1024,1024]{1,0:T(8,128)(2,1)S(1)} %get-tuple-element.30.units, f32[7,4,128]{2,1,0:T(4,128)S(1)} %get-tuple-element.31.live, f32[7,8,128]{2,1,0:T(8,128)S(1)} %get-tuple-element.32.mine, ...), custom_call_target="tpu_custom_call" | custom-call | tf_op jit(solution)/shard_map/pallas_call | solution.py:193
  49.2 0.0 collective-permute-done.arrived
  49.3 0.0 collective-permute-done.9.rest_0_
  49.3 0.7 %shard_map.64 = (f32[8,128]{1,0:T(8,128)S(1)}, f32[8,128]{1,0:T(8,128)S(1)}) custom-call(bf16[128,1024]{1,0:T(8,128)(2,1)S(1)} %collective-permute-done.arrived, bf16[1024,1024]{1,0:T(8,128)(2,1)S(1)} %get-tuple-element.30.units, f32[7,4,128]{2,1,0:T(4,128)S(1)} %get-tuple-element.31.live, f32[7,8,128]{2,1,0:T(8,128)S(1)} %get-tuple-element.32.mine, ...), custom_call_target="tpu_custom_call" | custom-call | tf_op jit(solution)/shard_map/pallas_call | solution.py:193
  49.9 3.4 %collective-permute-start.12 = (f32[8,128]{1,0:T(8,128)S(1)}, f32[8,128]{1,0:T(8,128)S(1)}, u32[]{:S(2)}, u32[]{:S(2)}) collective-permute-start(f32[8,128]{1,0:T(8,128)S(1)} %get-tuple-element.52), channel_id=1, source_target_pairs={{0,3},{1,2},{2,1},{3,0},{4,7},{5,6},{6,5},{7,4},{8,11},{9,10},{10,... | collective-permute-start | bytes 12296 | tf_op jit(solution)/shard_map/ppermute | solution.py:223
  53.3 0.2 collective-permute-done.10
  53.5 0.0 collective-permute-done.11
  53.5 1.9 %collective-permute-done.12 = f32[8,128]{1,0:T(8,128)S(1)} collective-permute-done((f32[8,128]{1,0:T(8,128)S(1)}, f32[8,128]{1,0:T(8,128)S(1)}, u32[]{:S(2)}, u32[]{:S(2)}) %collective-permute-start.12) | collective-permute-done | bytes 4128 | tf_op jit(solution)/shard_map/ppermute | solution.py:223
  55.4 0.6 %fusion.2 = f32[1024]{0:T(1024)} fusion(f32[8,128]{1,0:T(8,128)S(1)} %collective-permute-done.12, f32[8,128]{1,0:T(8,128)S(1)} %collective-permute-done.11, f32[8,128]{1,0:T(8,128)S(1)} %get-tuple-element.49, f32[8,128]{1,0:T(8,128)S(1)} %collective-permute-done.10, f32[7,8,128]{2,1,0:T(8,128)S(1)} %get-tuple-element.32.mine), kind=kLoop, calls=%fused_computation.3 | loop fusion | flops 7168 | bytes 32768 | tf_op jit(solution)/shard_map/reshape | solution.py:249
  (1 shorter events, 0.0 us)
Async XLA Ops:
  0.0 6.8 %copy-start = (bf16[1024,1024]{1,0:T(8,128)(2,1)S(1)}, bf16[1024,1024]{1,0:T(8,128)(2,1)}, u32[]{:S(2)}) copy-start(bf16[1024,1024]{1,0:T(8,128)(2,1)} %embeds.5) | copy-start | bytes 6291460
  0.0 6.8 %copy-start.2 = (s32[1,4]{1,0:T(1,128)S(1)}, s32[1,4]{1,0:T(1,128)}, u32[]{:S(2)}) copy-start(s32[1,4]{1,0:T(1,128)} %pick_blk.5) | copy-start | bytes 52
  0.0 6.8 %copy-start.1 = (s32[4,4]{1,0:T(4,128)S(1)}, s32[4,4]{1,0:T(4,128)}, u32[]{:S(2)}) copy-start(s32[4,4]{1,0:T(4,128)} %pick_sub.5) | copy-start | bytes 196
  0.0 34.8 %copy-start.3 = (s32[1,16]{1,0:T(1,128)S(1)}, s32[1,16]{1,0:T(1,128)}, u32[]{:S(2)}) copy-start(s32[1,16]{1,0:T(1,128)} %mask_blk.1) | copy-start | bytes 196
  0.0 34.8 %copy-start.4 = (s32[1,16]{1,0:T(1,128)S(1)}, s32[1,16]{1,0:T(1,128)}, u32[]{:S(2)}) copy-start(s32[1,16]{1,0:T(1,128)} %mask_sub.1) | copy-start | bytes 196
  2.6 8.2 %collective-permute-start.6 = (bf16[256,1024]{1,0:T(8,128)(2,1)}, bf16[256,1024]{1,0:T(8,128)(2,1)S(1)}, u32[]{:S(2)}, u32[]{:S(2)}) collective-permute-start(bf16[256,1024]{1,0:T(8,128)(2,1)} %get-tuple-element.38), channel_id=1, source_target_pairs={{0,4},{4,0},{8,12},{12,8},{1,5},{5,1},{9,13},{13,9},{2,6},{6,2},{1... | collective-permute-start | bytes 1572872 | tf_op jit(solution)/shard_map/ppermute | solution.py:223
  3.2 27.9 %collective-permute-start.5 = (bf16[256,1024]{1,0:T(8,128)(2,1)}, bf16[256,1024]{1,0:T(8,128)(2,1)S(1)}, u32[]{:S(2)}, u32[]{:S(2)}) collective-permute-start(bf16[256,1024]{1,0:T(8,128)(2,1)} %get-tuple-element.37), channel_id=1, source_target_pairs={{0,2},{1,3},{2,0},{3,1},{4,6},{5,7},{6,4},{7,5},{8,10},{9,11},{10,... | collective-permute-start | bytes 1572872 | tf_op jit(solution)/shard_map/ppermute | solution.py:223
  7.7 30.0 %collective-permute-start.4 = (bf16[256,1024]{1,0:T(8,128)(2,1)S(1)}, bf16[256,1024]{1,0:T(8,128)(2,1)S(1)}, u32[]{:S(2)}, u32[]{:S(2)}) collective-permute-start(bf16[256,1024]{1,0:T(8,128)(2,1)S(1)} %get-tuple-element.36), channel_id=1, source_target_pairs={{0,1},{1,0},{2,3},{3,2},{4,5},{5,4},{6,7},{7,6},{8,9},{9,8},{10,11... | collective-permute-start | bytes 1572872 | tf_op jit(solution)/shard_map/ppermute | solution.py:223
  9.3 30.6 %collective-permute-start.3 = (bf16[256,1024]{1,0:T(8,128)(2,1)S(1)}, bf16[256,1024]{1,0:T(8,128)(2,1)S(1)}, u32[]{:S(2)}, u32[]{:S(2)}) collective-permute-start(bf16[256,1024]{1,0:T(8,128)(2,1)S(1)} %get-tuple-element.35), channel_id=1, source_target_pairs={{0,8},{4,12},{8,0},{12,4},{1,9},{5,13},{9,1},{13,5},{2,10},{6,14},... | collective-permute-start | bytes 1572872 | tf_op jit(solution)/shard_map/ppermute | solution.py:223
  10.8 31.6 %collective-permute-start.2 = (bf16[256,1024]{1,0:T(8,128)(2,1)S(1)}, bf16[256,1024]{1,0:T(8,128)(2,1)S(1)}, u32[]{:S(2)}, u32[]{:S(2)}) collective-permute-start(bf16[256,1024]{1,0:T(8,128)(2,1)S(1)} %get-tuple-element.34), channel_id=1, source_target_pairs={{0,12},{4,8},{8,4},{12,0},{1,13},{5,9},{9,5},{13,1},{2,14},{6,10},... | collective-permute-start | bytes 1572872 | tf_op jit(solution)/shard_map/ppermute | solution.py:223
  10.8 32.9 %collective-permute-start.1 = (bf16[128,1024]{1,0:T(8,128)(2,1)S(1)}, bf16[128,1024]{1,0:T(8,128)(2,1)S(1)}, u32[]{:S(2)}, u32[]{:S(2)}) collective-permute-start(bf16[128,1024]{1,0:T(8,128)(2,1)S(1)} %get-tuple-element.33), channel_id=1, source_target_pairs={{0,3},{1,2},{2,1},{3,0},{4,7},{5,6},{6,5},{7,4},{8,11},{9,10},{10,... | collective-permute-start | bytes 786440 | tf_op jit(solution)/shard_map/ppermute | solution.py:223
  31.1 18.2 %collective-permute-start = (bf16[128,1024]{1,0:T(8,128)(2,1)S(1)}, bf16[128,1024]{1,0:T(8,128)(2,1)S(1)}, u32[]{:S(2)}, u32[]{:S(2)}) collective-permute-start(bf16[128,1024]{1,0:T(8,128)(2,1)S(1)} %get-tuple-element.29), channel_id=1, source_target_pairs={{0,3},{1,2},{2,1},{3,0},{4,7},{5,6},{6,5},{7,4},{8,11},{9,10},{10,... | collective-permute-start | bytes 786440 | tf_op jit(solution)/shard_map/ppermute | solution.py:223
  37.6 1.2 %collective-permute-start.7 = (f32[8,128]{1,0:T(8,128)S(1)}, f32[8,128]{1,0:T(8,128)S(1)}, u32[]{:S(2)}, u32[]{:S(2)}) collective-permute-start(f32[8,128]{1,0:T(8,128)S(1)} %get-tuple-element.41), channel_id=1, source_target_pairs={{0,4},{4,0},{8,12},{12,8},{1,5},{5,1},{9,13},{13,9},{2,6},{6,2},{1... | collective-permute-start | bytes 12296 | tf_op jit(solution)/shard_map/ppermute | solution.py:223
  40.9 7.7 %collective-permute-start.8 = (f32[8,128]{1,0:T(8,128)S(1)}, f32[8,128]{1,0:T(8,128)S(1)}, u32[]{:S(2)}, u32[]{:S(2)}) collective-permute-start(f32[8,128]{1,0:T(8,128)S(1)} %get-tuple-element.45), channel_id=1, source_target_pairs={{0,8},{4,12},{8,0},{12,4},{1,9},{5,13},{9,1},{13,5},{2,10},{6,14},... | collective-permute-start | bytes 12296 | tf_op jit(solution)/shard_map/ppermute | solution.py:223
  43.4 5.8 %collective-permute-start.9 = (f32[8,128]{1,0:T(8,128)S(1)}, f32[8,128]{1,0:T(8,128)S(1)}, u32[]{:S(2)}, u32[]{:S(2)}) collective-permute-start(f32[8,128]{1,0:T(8,128)S(1)} %get-tuple-element.47), channel_id=1, source_target_pairs={{0,12},{4,8},{8,4},{12,0},{1,13},{5,9},{9,5},{13,1},{2,14},{6,10},... | collective-permute-start | bytes 12296 | tf_op jit(solution)/shard_map/ppermute | solution.py:223
  43.7 9.8 %collective-permute-start.10 = (f32[8,128]{1,0:T(8,128)S(1)}, f32[8,128]{1,0:T(8,128)S(1)}, u32[]{:S(2)}, u32[]{:S(2)}) collective-permute-start(f32[8,128]{1,0:T(8,128)S(1)} %get-tuple-element.50), channel_id=1, source_target_pairs={{0,2},{1,3},{2,0},{3,1},{4,6},{5,7},{6,4},{7,5},{8,10},{9,11},{10,... | collective-permute-start | bytes 12296 | tf_op jit(solution)/shard_map/ppermute | solution.py:223
  43.7 9.8 %collective-permute-start.11 = (f32[8,128]{1,0:T(8,128)S(1)}, f32[8,128]{1,0:T(8,128)S(1)}, u32[]{:S(2)}, u32[]{:S(2)}) collective-permute-start(f32[8,128]{1,0:T(8,128)S(1)} %get-tuple-element.51), channel_id=1, source_target_pairs={{0,1},{1,0},{2,3},{3,2},{4,5},{5,4},{6,7},{7,6},{8,9},{9,8},{10,11... | collective-permute-start | bytes 12296 | tf_op jit(solution)/shard_map/ppermute | solution.py:223
  49.9 5.5 %collective-permute-start.12 = (f32[8,128]{1,0:T(8,128)S(1)}, f32[8,128]{1,0:T(8,128)S(1)}, u32[]{:S(2)}, u32[]{:S(2)}) collective-permute-start(f32[8,128]{1,0:T(8,128)S(1)} %get-tuple-element.52), channel_id=1, source_target_pairs={{0,3},{1,2},{2,1},{3,0},{4,7},{5,6},{6,5},{7,4},{8,11},{9,10},{10,... | collective-permute-start | bytes 12296 | tf_op jit(solution)/shard_map/ppermute | solution.py:223

commit v20 on v19

--- a/solution.py
+++ b/solution.py
@@ -22,8 +22,15 @@
 PARAMS = pltpu.CompilerParams(vmem_limit_bytes=32 * 2**20)
 
 
-def pairs(step, size):
-    return [(i, i ^ step) for i in range(size)]
+def pairs(axis, step, size):
+    return [(i, i ^ step if axis == "blk" else (i + step) % size) for i in range(size)]
+
+
+def target_and_source(axis, step, size):
+    own = lax.axis_index(axis)
+    if axis == "blk":
+        return own ^ step, own ^ step
+    return lax.rem(own + step, size), lax.rem(own + size - step, size)
 
 
 def rounded_units(rows):
@@ -38,7 +45,7 @@
 
 
 def take_pick(axis, step, pick_blk, pick_sub):
-    target = lax.axis_index(axis) ^ step
+    target, _ = target_and_source(axis, step, pick_sub.shape[1])
     return pick_blk[0, target] if axis == "blk" else pick_sub[lax.axis_index("sub"), target]
 
 
@@ -136,8 +143,8 @@
     count = live.shape[1]
     block_of = lax.broadcasted_iota(jnp.int32, mine.shape[1:], 0) // ROWS
     for place, (axis, step, _, _) in enumerate(slots):
-        source = lax.axis_index(axis) ^ step
         mask = mask_blk if axis == "blk" else mask_sub
+        _, source = target_and_source(axis, step, mask.shape[1] // count)
         for i in range(count):
             value = mask[0, source * count + i].astype(jnp.float32)
             live[place, i : i + 1] = jnp.full((1, LANES), value, jnp.float32)
@@ -204,9 +211,9 @@
 
 
 def plan_slots(sizes):
-    slots = [("blk", 1, 0, BLOCK), ("sub", 2, 0, BLOCK), ("sub", 1, 0, BLOCK)]
+    slots = [("blk", 1, 0, BLOCK), ("sub", 2, 0, BLOCK), ("sub", sizes["sub"] - 1, 0, BLOCK)]
     slots += [("blk", k, 0, BLOCK) for k in range(2, sizes["blk"])]
-    for k in range(3, sizes["sub"]):
+    for k in (1, *range(3, sizes["sub"] - 1)):
         slots += [("sub", k, 0, FIRST_CUT), ("sub", k, FIRST_CUT, BLOCK - FIRST_CUT)]
     return slots
 
@@ -219,8 +226,10 @@
     sizes = {"sub": lax.axis_size("sub"), "blk": lax.axis_size("blk")}
     slots = plan_slots(sizes)
 
-    def send(array, slot):
-        return lax.ppermute(array, slot[0], pairs(slot[1], sizes[slot[0]]))
+    def send(array, slot, back=False):
+        axis, step, _, _ = slot
+        there = pairs(axis, step, sizes[axis])
+        return lax.ppermute(array, axis, [(b, a) for a, b in there] if back else there)
 
     outgoing = first_rows(slots[:AT_ONCE], pick_blk, pick_sub, embeds)
     outgoing += pick_rows(slots[AT_ONCE:], pick_blk, pick_sub, embeds)
@@ -241,9 +250,9 @@
         if first + rows < BLOCK:
             carried[axis, step] = back
         elif axis == "blk":
-            waiting.append((place + BEHIND, place, send(back, slot)))
+            waiting.append((place + BEHIND, place, send(back, slot, back=True)))
         else:
-            late.append((place, send(back, slot)))
+            late.append((place, send(back, slot, back=True)))
     for place, sums in late:
         totals = totals + mine[place] * sums
     return (totals * (1.0 / BLOCK)).reshape(-1)

time: 57.1 us -> 66.1 us (1.16); the launches traced: 56 us -> 66 us
  starting transfers between devices: 21.4 us -> 32.4 us
  waiting for transfers between devices: 22.4 us -> 21.3 us
    ppermute x13, starting transfers between devices: 21.4 us -> 32.4 us  [send(): lax.ppermute(array, axis, [(b, a) for a, b in there] if back else there)]
    ppermute x13, waiting for transfers between devices: 22.4 us -> 21.3 us  [send(): lax.ppermute(array, axis, [(b, a) for a, b in there] if back else there)]
  transfers between devices with their start and end apart: 13 -> 13, of which waited for: 4 -> 4; matrix products, arithmetic and copies ran while one was open for 0% -> 0% of each run, Pallas kernels for 16% -> 13%
where the time goes in v20:
time: 66.1 us; the launch traced here: 66 us
  starting transfers between devices  32.4 us (49%)
  waiting for transfers between devices  21.3 us (32%)
  Pallas kernels  11.5 us (17%)
    ppermute x13, starting transfers between devices, send(): lax.ppermute(array, axis, [(b, a) for a, b in there] if back else there)  32.4 us
    ppermute x13, waiting for transfers between devices, send(): lax.ppermute(array, axis, [(b, a) for a, b in there] if back else there)  21.3 us
    pallas_call x7, Pallas kernels, work(): pl.pallas_call(functools.partial(slot_kernel, place, *slot[2:], [one for...  6.29 us
    pallas_call x1, Pallas kernels, first_rows(): pl.pallas_call(functools.partial(first_kernel, slots), out_shape=[jax.Sha...  2.6 us
    pallas_call x1, Pallas kernels, prepare(): pl.pallas_call(functools.partial(prepare_kernel, slots), out_shape=[jax.S...  1.77 us
  transfers between devices with their start and end apart: 13, of which 4 were waited for; matrix products, arithmetic and copies ran while one was open for 0% of the time, Pallas kernels for 13%

profile of v20, /device:TPU:0, one launch (start us, length us, event | category | flops | bytes accessed | tf_op | source)
XLA Modules:
  0.0 66.0 jit_solution(6988283270311961254)
XLA Ops:
  0.0 0.0 copy-start
  0.0 0.0 copy-start.2
  0.0 0.0 copy-start.1
  0.0 0.0 copy-start.3
  0.0 0.0 copy-start.4
  0.0 2.6 %shard_map.57 = (bf16[256,1024]{1,0:T(8,128)(2,1)}, bf16[256,1024]{1,0:T(8,128)(2,1)}) custom-call(s32[1,4]{1,0:T(1,128)} %pick_blk.5, s32[4,4]{1,0:T(4,128)} %pick_sub.5, bf16[1024,1024]{1,0:T(8,128)(2,1)} %embeds.5), custom_call_target="tpu_custom_call" | custom-call | tf_op jit(solution)/shard_map/pallas_call | solution.py:88
  2.6 0.5 collective-permute-start.6
  3.2 3.7 %collective-permute-start.5 = (bf16[256,1024]{1,0:T(8,128)(2,1)}, bf16[256,1024]{1,0:T(8,128)(2,1)S(1)}, u32[]{:S(2)}, u32[]{:S(2)}) collective-permute-start(bf16[256,1024]{1,0:T(8,128)(2,1)} %get-tuple-element.37), channel_id=1, source_target_pairs={{0,2},{1,3},{2,0},{3,1},{4,6},{5,7},{6,4},{7,5},{8,10},{9,11},{10,... | collective-permute-start | bytes 1572872 | tf_op jit(solution)/shard_map/ppermute | solution.py:232
  6.8 0.0 copy-done
  6.8 0.0 copy-done.2
  6.8 0.0 copy-done.1
  6.8 0.8 %shard_map.55 = (bf16[256,1024]{1,0:T(8,128)(2,1)S(1)}, bf16[256,1024]{1,0:T(8,128)(2,1)S(1)}, bf16[256,1024]{1,0:T(8,128)(2,1)S(1)}, bf16[128,1024]{1,0:T(8,128)(2,1)S(1)}, bf16[128,1024]{1,0:T(8,128)(2,1)S(1)}) custom-call(s32[1,4]{1,0:T(1,128)S(1)} %copy-done.2, s32[4,4]{1,0:T(4,128)S(1)} %copy-done.1, bf16[1024,1024]{1,0:T(8,128)(2,1)S(1)} %copy-done), custom_call_target="tpu_custom_call" | custom-call | tf_op jit(solution)/shard_map/pallas_call | solution.py:125
  7.7 1.4 %collective-permute-start.4 = (bf16[256,1024]{1,0:T(8,128)(2,1)S(1)}, bf16[256,1024]{1,0:T(8,128)(2,1)S(1)}, u32[]{:S(2)}, u32[]{:S(2)}) collective-permute-start(bf16[256,1024]{1,0:T(8,128)(2,1)S(1)} %get-tuple-element.36), channel_id=1, source_target_pairs={{0,3},{1,0},{2,1},{3,2},{4,7},{5,4},{6,5},{7,6},{8,11},{9,8},{10,9... | collective-permute-start | bytes 1572872 | tf_op jit(solution)/shard_map/ppermute | solution.py:232
  9.1 1.5 %collective-permute-start.3 = (bf16[256,1024]{1,0:T(8,128)(2,1)S(1)}, bf16[256,1024]{1,0:T(8,128)(2,1)S(1)}, u32[]{:S(2)}, u32[]{:S(2)}) collective-permute-start(bf16[256,1024]{1,0:T(8,128)(2,1)S(1)} %get-tuple-element.35), channel_id=1, source_target_pairs={{0,8},{4,12},{8,0},{12,4},{1,9},{5,13},{9,1},{13,5},{2,10},{6,14},... | collective-permute-start | bytes 1572872 | tf_op jit(solution)/shard_map/ppermute | solution.py:232
  10.6 0.0 collective-permute-start.2
  10.6 0.0 collective-permute-done.6.arrived
  10.6 0.7 %collective-permute-start.1 = (bf16[128,1024]{1,0:T(8,128)(2,1)S(1)}, bf16[128,1024]{1,0:T(8,128)(2,1)S(1)}, u32[]{:S(2)}, u32[]{:S(2)}) collective-permute-start(bf16[128,1024]{1,0:T(8,128)(2,1)S(1)} %get-tuple-element.33), channel_id=1, source_target_pairs={{0,1},{1,2},{2,3},{3,0},{4,5},{5,6},{6,7},{7,4},{8,9},{9,10},{10,1... | collective-permute-start | bytes 786440 | tf_op jit(solution)/shard_map/ppermute | solution.py:232
  11.2 19.8 %collective-permute-done.5.arrived = bf16[256,1024]{1,0:T(8,128)(2,1)S(1)} collective-permute-done((bf16[256,1024]{1,0:T(8,128)(2,1)}, bf16[256,1024]{1,0:T(8,128)(2,1)S(1)}, u32[]{:S(2)}, u32[]{:S(2)}) %collective-permute-start.5) | collective-permute-done | bytes 524320 | tf_op jit(solution)/shard_map/ppermute | solution.py:232
  31.1 11.8 %collective-permute-start = (bf16[128,1024]{1,0:T(8,128)(2,1)S(1)}, bf16[128,1024]{1,0:T(8,128)(2,1)S(1)}, u32[]{:S(2)}, u32[]{:S(2)}) collective-permute-start(bf16[128,1024]{1,0:T(8,128)(2,1)S(1)} %get-tuple-element.29), channel_id=1, source_target_pairs={{0,1},{1,2},{2,3},{3,0},{4,5},{5,6},{6,7},{7,4},{8,9},{9,10},{10,1... | collective-permute-start | bytes 786440 | tf_op jit(solution)/shard_map/ppermute | solution.py:232
  42.9 0.0 copy-done.3
  42.9 0.0 copy-done.4
  42.9 1.8 %shard_map.56 = (bf16[1024,1024]{1,0:T(8,128)(2,1)S(1)}, f32[7,4,128]{2,1,0:T(4,128)S(1)}, f32[7,8,128]{2,1,0:T(8,128)S(1)}) custom-call(s32[1,4]{1,0:T(1,128)S(1)} %copy-done.2, s32[4,4]{1,0:T(4,128)S(1)} %copy-done.1, s32[1,16]{1,0:T(1,128)S(1)} %copy-done.3, s32[1,16]{1,0:T(1,128)S(1)} %copy-done.4, bf16[1024,1024]{1,0:T(8,128)(2,1)S(1)} %copy-done), custom_call_target="tpu_custom_call" | custom-call | tf_op jit(solution)/shard_map/pallas_call | solution.py:157
  44.7 1.0 %shard_map.58 = (f32[8,128]{1,0:T(8,128)S(1)}, f32[8,128]{1,0:T(8,128)S(1)}) custom-call(bf16[256,1024]{1,0:T(8,128)(2,1)S(1)} %collective-permute-done.6.arrived, bf16[1024,1024]{1,0:T(8,128)(2,1)S(1)} %get-tuple-element.30.units, f32[7,4,128]{2,1,0:T(4,128)S(1)} %get-tuple-element.31.live, f32[7,8,128]{2,1,0:T(8,128)S(1)} %get-tuple-element.32.mine, ...), custom_call_target="tpu_custom_call" | custom-call | tf_op jit(solution)/shard_map/pallas_call | solution.py:200
  45.7 0.0 collective-permute-done.4.arrived
  45.7 0.1 collective-permute-start.7
  45.8 1.0 %shard_map.59 = (f32[8,128]{1,0:T(8,128)S(1)}, f32[8,128]{1,0:T(8,128)S(1)}) custom-call(bf16[256,1024]{1,0:T(8,128)(2,1)S(1)} %collective-permute-done.5.arrived, bf16[1024,1024]{1,0:T(8,128)(2,1)S(1)} %get-tuple-element.30.units, f32[7,4,128]{2,1,0:T(4,128)S(1)} %get-tuple-element.31.live, f32[7,8,128]{2,1,0:T(8,128)S(1)} %get-tuple-element.32.mine, ...), custom_call_target="tpu_custom_call" | custom-call | tf_op jit(solution)/shard_map/pallas_call | solution.py:200
  46.8 0.2 collective-permute-done.7.rest_0_
  46.9 1.0 %shard_map.60 = (f32[8,128]{1,0:T(8,128)S(1)}, f32[8,128]{1,0:T(8,128)S(1)}) custom-call(bf16[256,1024]{1,0:T(8,128)(2,1)S(1)} %collective-permute-done.4.arrived, bf16[1024,1024]{1,0:T(8,128)(2,1)S(1)} %get-tuple-element.30.units, f32[7,4,128]{2,1,0:T(4,128)S(1)} %get-tuple-element.31.live, f32[7,8,128]{2,1,0:T(8,128)S(1)} %get-tuple-element.32.mine, ...), custom_call_target="tpu_custom_call" | custom-call | tf_op jit(solution)/shard_map/pallas_call | solution.py:200
  47.9 0.0 collective-permute-done.3.arrived
  47.9 1.0 %shard_map.61 = (f32[8,128]{1,0:T(8,128)S(1)}, f32[8,128]{1,0:T(8,128)S(1)}) custom-call(bf16[256,1024]{1,0:T(8,128)(2,1)S(1)} %collective-permute-done.3.arrived, bf16[1024,1024]{1,0:T(8,128)(2,1)S(1)} %get-tuple-element.30.units, f32[7,4,128]{2,1,0:T(4,128)S(1)} %get-tuple-element.31.live, f32[7,8,128]{2,1,0:T(8,128)S(1)} %get-tuple-element.32.mine, ...), custom_call_target="tpu_custom_call" | custom-call | tf_op jit(solution)/shard_map/pallas_call | solution.py:200
  48.9 1.6 %collective-permute-start.8 = (f32[8,128]{1,0:T(8,128)S(1)}, f32[8,128]{1,0:T(8,128)S(1)}, u32[]{:S(2)}, u32[]{:S(2)}) collective-permute-start(f32[8,128]{1,0:T(8,128)S(1)} %get-tuple-element.45), channel_id=1, source_target_pairs={{8,0},{12,4},{0,8},{4,12},{9,1},{13,5},{1,9},{5,13},{10,2},{14,6},... | collective-permute-start | bytes 12296 | tf_op jit(solution)/shard_map/ppermute | solution.py:232
  50.5 0.0 collective-permute-done.2.arrived
  50.5 1.0 %shard_map.62 = (f32[8,128]{1,0:T(8,128)S(1)}, f32[8,128]{1,0:T(8,128)S(1)}) custom-call(bf16[256,1024]{1,0:T(8,128)(2,1)S(1)} %collective-permute-done.2.arrived, bf16[1024,1024]{1,0:T(8,128)(2,1)S(1)} %get-tuple-element.30.units, f32[7,4,128]{2,1,0:T(4,128)S(1)} %get-tuple-element.31.live, f32[7,8,128]{2,1,0:T(8,128)S(1)} %get-tuple-element.32.mine, ...), custom_call_target="tpu_custom_call" | custom-call | tf_op jit(solution)/shard_map/pallas_call | solution.py:200
  51.5 0.3 collective-permute-start.9
  51.8 7.1 %collective-permute-start.10 = (f32[8,128]{1,0:T(8,128)S(1)}, f32[8,128]{1,0:T(8,128)S(1)}, u32[]{:S(2)}, u32[]{:S(2)}) collective-permute-start(f32[8,128]{1,0:T(8,128)S(1)} %get-tuple-element.50), channel_id=1, source_target_pairs={{2,0},{3,1},{0,2},{1,3},{6,4},{7,5},{4,6},{5,7},{10,8},{11,9},{8,1... | collective-permute-start | bytes 12296 | tf_op jit(solution)/shard_map/ppermute | solution.py:232
  58.8 0.0 collective-permute-done.1.arrived
  58.8 1.0 %collective-permute-start.11 = (f32[8,128]{1,0:T(8,128)S(1)}, f32[8,128]{1,0:T(8,128)S(1)}, u32[]{:S(2)}, u32[]{:S(2)}) collective-permute-start(f32[8,128]{1,0:T(8,128)S(1)} %get-tuple-element.51), channel_id=1, source_target_pairs={{3,0},{0,1},{1,2},{2,3},{7,4},{4,5},{5,6},{6,7},{11,8},{8,9},{9,10... | collective-permute-start | bytes 12296 | tf_op jit(solution)/shard_map/ppermute | solution.py:232
  59.9 0.0 collective-permute-done.8.rest_0_
  59.9 0.7 shard_map.63
  60.5 0.0 collective-permute-done.arrived
  60.5 0.0 collective-permute-done.9.rest_0_
  60.6 0.7 shard_map.64
  61.2 2.8 %collective-permute-start.12 = (f32[8,128]{1,0:T(8,128)S(1)}, f32[8,128]{1,0:T(8,128)S(1)}, u32[]{:S(2)}, u32[]{:S(2)}) collective-permute-start(f32[8,128]{1,0:T(8,128)S(1)} %get-tuple-element.52), channel_id=1, source_target_pairs={{1,0},{2,1},{3,2},{0,3},{5,4},{6,5},{7,6},{4,7},{9,8},{10,9},{11,1... | collective-permute-start | bytes 12296 | tf_op jit(solution)/shard_map/ppermute | solution.py:232
  64.1 0.0 collective-permute-done.10
  64.1 0.2 collective-permute-done.11
  64.2 1.1 %collective-permute-done.12 = f32[8,128]{1,0:T(8,128)S(1)} collective-permute-done((f32[8,128]{1,0:T(8,128)S(1)}, f32[8,128]{1,0:T(8,128)S(1)}, u32[]{:S(2)}, u32[]{:S(2)}) %collective-permute-start.12) | collective-permute-done | bytes 4128 | tf_op jit(solution)/shard_map/ppermute | solution.py:232
  65.4 0.6 fusion.2
  (1 shorter events, 0.0 us)
Async XLA Ops:
  0.0 6.8 %copy-start = (bf16[1024,1024]{1,0:T(8,128)(2,1)S(1)}, bf16[1024,1024]{1,0:T(8,128)(2,1)}, u32[]{:S(2)}) copy-start(bf16[1024,1024]{1,0:T(8,128)(2,1)} %embeds.5) | copy-start | bytes 6291460
  0.0 6.8 %copy-start.2 = (s32[1,4]{1,0:T(1,128)S(1)}, s32[1,4]{1,0:T(1,128)}, u32[]{:S(2)}) copy-start(s32[1,4]{1,0:T(1,128)} %pick_blk.5) | copy-start | bytes 52
  0.0 6.8 %copy-start.1 = (s32[4,4]{1,0:T(4,128)S(1)}, s32[4,4]{1,0:T(4,128)}, u32[]{:S(2)}) copy-start(s32[4,4]{1,0:T(4,128)} %pick_sub.5) | copy-start | bytes 196
  0.0 42.9 %copy-start.3 = (s32[1,16]{1,0:T(1,128)S(1)}, s32[1,16]{1,0:T(1,128)}, u32[]{:S(2)}) copy-start(s32[1,16]{1,0:T(1,128)} %mask_blk.1) | copy-start | bytes 196
  0.0 42.9 %copy-start.4 = (s32[1,16]{1,0:T(1,128)S(1)}, s32[1,16]{1,0:T(1,128)}, u32[]{:S(2)}) copy-start(s32[1,16]{1,0:T(1,128)} %mask_sub.1) | copy-start | bytes 196
  2.6 7.9 %collective-permute-start.6 = (bf16[256,1024]{1,0:T(8,128)(2,1)}, bf16[256,1024]{1,0:T(8,128)(2,1)S(1)}, u32[]{:S(2)}, u32[]{:S(2)}) collective-permute-start(bf16[256,1024]{1,0:T(8,128)(2,1)} %get-tuple-element.38), channel_id=1, source_target_pairs={{0,4},{4,0},{8,12},{12,8},{1,5},{5,1},{9,13},{13,9},{2,6},{6,2},{1... | collective-permute-start | bytes 1572872 | tf_op jit(solution)/shard_map/ppermute | solution.py:232
  3.2 27.9 %collective-permute-start.5 = (bf16[256,1024]{1,0:T(8,128)(2,1)}, bf16[256,1024]{1,0:T(8,128)(2,1)S(1)}, u32[]{:S(2)}, u32[]{:S(2)}) collective-permute-start(bf16[256,1024]{1,0:T(8,128)(2,1)} %get-tuple-element.37), channel_id=1, source_target_pairs={{0,2},{1,3},{2,0},{3,1},{4,6},{5,7},{6,4},{7,5},{8,10},{9,11},{10,... | collective-permute-start | bytes 1572872 | tf_op jit(solution)/shard_map/ppermute | solution.py:232
  7.7 38.0 %collective-permute-start.4 = (bf16[256,1024]{1,0:T(8,128)(2,1)S(1)}, bf16[256,1024]{1,0:T(8,128)(2,1)S(1)}, u32[]{:S(2)}, u32[]{:S(2)}) collective-permute-start(bf16[256,1024]{1,0:T(8,128)(2,1)S(1)} %get-tuple-element.36), channel_id=1, source_target_pairs={{0,3},{1,0},{2,1},{3,2},{4,7},{5,4},{6,5},{7,6},{8,11},{9,8},{10,9... | collective-permute-start | bytes 1572872 | tf_op jit(solution)/shard_map/ppermute | solution.py:232
  9.1 38.9 %collective-permute-start.3 = (bf16[256,1024]{1,0:T(8,128)(2,1)S(1)}, bf16[256,1024]{1,0:T(8,128)(2,1)S(1)}, u32[]{:S(2)}, u32[]{:S(2)}) collective-permute-start(bf16[256,1024]{1,0:T(8,128)(2,1)S(1)} %get-tuple-element.35), channel_id=1, source_target_pairs={{0,8},{4,12},{8,0},{12,4},{1,9},{5,13},{9,1},{13,5},{2,10},{6,14},... | collective-permute-start | bytes 1572872 | tf_op jit(solution)/shard_map/ppermute | solution.py:232
  10.6 39.9 %collective-permute-start.2 = (bf16[256,1024]{1,0:T(8,128)(2,1)S(1)}, bf16[256,1024]{1,0:T(8,128)(2,1)S(1)}, u32[]{:S(2)}, u32[]{:S(2)}) collective-permute-start(bf16[256,1024]{1,0:T(8,128)(2,1)S(1)} %get-tuple-element.34), channel_id=1, source_target_pairs={{0,12},{4,8},{8,4},{12,0},{1,13},{5,9},{9,5},{13,1},{2,14},{6,10},... | collective-permute-start | bytes 1572872 | tf_op jit(solution)/shard_map/ppermute | solution.py:232
  10.6 48.3 %collective-permute-start.1 = (bf16[128,1024]{1,0:T(8,128)(2,1)S(1)}, bf16[128,1024]{1,0:T(8,128)(2,1)S(1)}, u32[]{:S(2)}, u32[]{:S(2)}) collective-permute-start(bf16[128,1024]{1,0:T(8,128)(2,1)S(1)} %get-tuple-element.33), channel_id=1, source_target_pairs={{0,1},{1,2},{2,3},{3,0},{4,5},{5,6},{6,7},{7,4},{8,9},{9,10},{10,1... | collective-permute-start | bytes 786440 | tf_op jit(solution)/shard_map/ppermute | solution.py:232
  31.1 29.5 %collective-permute-start = (bf16[128,1024]{1,0:T(8,128)(2,1)S(1)}, bf16[128,1024]{1,0:T(8,128)(2,1)S(1)}, u32[]{:S(2)}, u32[]{:S(2)}) collective-permute-start(bf16[128,1024]{1,0:T(8,128)(2,1)S(1)} %get-tuple-element.29), channel_id=1, source_target_pairs={{0,1},{1,2},{2,3},{3,0},{4,5},{5,6},{6,7},{7,4},{8,9},{9,10},{10,1... | collective-permute-start | bytes 786440 | tf_op jit(solution)/shard_map/ppermute | solution.py:232
  45.7 1.2 %collective-permute-start.7 = (f32[8,128]{1,0:T(8,128)S(1)}, f32[8,128]{1,0:T(8,128)S(1)}, u32[]{:S(2)}, u32[]{:S(2)}) collective-permute-start(f32[8,128]{1,0:T(8,128)S(1)} %get-tuple-element.41), channel_id=1, source_target_pairs={{4,0},{0,4},{12,8},{8,12},{5,1},{1,5},{13,9},{9,13},{6,2},{2,6},{1... | collective-permute-start | bytes 12296 | tf_op jit(solution)/shard_map/ppermute | solution.py:232
  48.9 10.9 %collective-permute-start.8 = (f32[8,128]{1,0:T(8,128)S(1)}, f32[8,128]{1,0:T(8,128)S(1)}, u32[]{:S(2)}, u32[]{:S(2)}) collective-permute-start(f32[8,128]{1,0:T(8,128)S(1)} %get-tuple-element.45), channel_id=1, source_target_pairs={{8,0},{12,4},{0,8},{4,12},{9,1},{13,5},{1,9},{5,13},{10,2},{14,6},... | collective-permute-start | bytes 12296 | tf_op jit(solution)/shard_map/ppermute | solution.py:232
  51.5 9.1 %collective-permute-start.9 = (f32[8,128]{1,0:T(8,128)S(1)}, f32[8,128]{1,0:T(8,128)S(1)}, u32[]{:S(2)}, u32[]{:S(2)}) collective-permute-start(f32[8,128]{1,0:T(8,128)S(1)} %get-tuple-element.47), channel_id=1, source_target_pairs={{12,0},{8,4},{4,8},{0,12},{13,1},{9,5},{5,9},{1,13},{14,2},{10,6},... | collective-permute-start | bytes 12296 | tf_op jit(solution)/shard_map/ppermute | solution.py:232
  51.8 12.3 %collective-permute-start.10 = (f32[8,128]{1,0:T(8,128)S(1)}, f32[8,128]{1,0:T(8,128)S(1)}, u32[]{:S(2)}, u32[]{:S(2)}) collective-permute-start(f32[8,128]{1,0:T(8,128)S(1)} %get-tuple-element.50), channel_id=1, source_target_pairs={{2,0},{3,1},{0,2},{1,3},{6,4},{7,5},{4,6},{5,7},{10,8},{11,9},{8,1... | collective-permute-start | bytes 12296 | tf_op jit(solution)/shard_map/ppermute | solution.py:232
  58.8 5.4 %collective-permute-start.11 = (f32[8,128]{1,0:T(8,128)S(1)}, f32[8,128]{1,0:T(8,128)S(1)}, u32[]{:S(2)}, u32[]{:S(2)}) collective-permute-start(f32[8,128]{1,0:T(8,128)S(1)} %get-tuple-element.51), channel_id=1, source_target_pairs={{3,0},{0,1},{1,2},{2,3},{7,4},{4,5},{5,6},{6,7},{11,8},{8,9},{9,10... | collective-permute-start | bytes 12296 | tf_op jit(solution)/shard_map/ppermute | solution.py:232
  61.2 4.2 %collective-permute-start.12 = (f32[8,128]{1,0:T(8,128)S(1)}, f32[8,128]{1,0:T(8,128)S(1)}, u32[]{:S(2)}, u32[]{:S(2)}) collective-permute-start(f32[8,128]{1,0:T(8,128)S(1)} %get-tuple-element.52), channel_id=1, source_target_pairs={{1,0},{2,1},{3,2},{0,3},{5,4},{6,5},{7,6},{4,7},{9,8},{10,9},{11,1... | collective-permute-start | bytes 12296 | tf_op jit(solution)/shard_map/ppermute | solution.py:232

commit v21 on v19

--- a/solution.py
+++ b/solution.py
@@ -200,18 +200,17 @@
 
 
 BEHIND = 2
-FIRST_CUT = 128
+FIRST_CUT = 240
 
 
 def plan_slots(sizes):
-    slots = [("blk", 1, 0, BLOCK), ("sub", 2, 0, BLOCK), ("sub", 1, 0, BLOCK)]
-    slots += [("blk", k, 0, BLOCK) for k in range(2, sizes["blk"])]
-    for k in range(3, sizes["sub"]):
-        slots += [("sub", k, 0, FIRST_CUT), ("sub", k, FIRST_CUT, BLOCK - FIRST_CUT)]
-    return slots
-
-
-AT_ONCE = 2
+    slots = [("sub", 2, 0, BLOCK), ("sub", 1, 0, BLOCK), ("blk", 1, 0, BLOCK), ("blk", 2, 0, BLOCK)]
+    for k in range(3, sizes["blk"]):
+        slots += [("blk", k, 0, FIRST_CUT), ("blk", k, FIRST_CUT, BLOCK - FIRST_CUT)]
+    return slots + [("sub", k, 0, BLOCK) for k in range(3, sizes["sub"])]
+
+
+AT_ONCE = 1
 
 
 def body(embeds, pick_blk, mask_blk, pick_sub, mask_sub):

time: 57.1 us -> 66.3 us (1.16)
  the two profiles are of different devices: /device:TPU:0 before, /device:TPU:4 now
where the time goes in v21:
time: 66.3 us; the launch traced here: 66.2 us
  waiting for transfers between devices  42.5 us (64%)
  Pallas kernels  11.9 us (18%)
  starting transfers between devices  11 us (17%)
    ppermute x13, waiting for transfers between devices, send(): return lax.ppermute(array, slot[0], pairs(slot[1], sizes[slot[0]]))  42.5 us
    ppermute x13, starting transfers between devices, send(): return lax.ppermute(array, slot[0], pairs(slot[1], sizes[slot[0]]))  11 us
    pallas_call x7, Pallas kernels, work(): pl.pallas_call(functools.partial(slot_kernel, place, *slot[2:], [one for...  6.47 us
    pallas_call x1, Pallas kernels, first_rows(): pl.pallas_call(functools.partial(first_kernel, slots), out_shape=[jax.Sha...  2.45 us
    pallas_call x1, Pallas kernels, prepare(): pl.pallas_call(functools.partial(prepare_kernel, slots), out_shape=[jax.S...  1.77 us
  transfers between devices with their start and end apart: 13, of which 5 were waited for; matrix products, arithmetic and copies ran while one was open for 0% of the time, Pallas kernels for 14%

profile of v21, /device:TPU:4, one launch (start us, length us, event | category | flops | bytes accessed | tf_op | source)
XLA Modules:
  0.0 66.2 jit_solution(9261330456091835988)
XLA Ops:
  0.0 0.0 copy-start.1
  0.0 0.0 copy-start.2
  0.0 0.0 copy-start
  0.0 0.0 copy-start.4
  0.0 0.0 copy-start.3
  0.0 2.4 %shard_map.57 = bf16[256,1024]{1,0:T(8,128)(2,1)} custom-call(s32[1,4]{1,0:T(1,128)} %pick_blk.5, s32[4,4]{1,0:T(4,128)} %pick_sub.5, bf16[1024,1024]{1,0:T(8,128)(2,1)} %embeds.5), custom_call_target="tpu_custom_call" | custom-call | tf_op jit(solution)/shard_map/pallas_call | solution.py:81
  2.5 2.7 %collective-permute-start.6 = (bf16[256,1024]{1,0:T(8,128)(2,1)}, bf16[256,1024]{1,0:T(8,128)(2,1)S(1)}, u32[]{:S(2)}, u32[]{:S(2)}) collective-permute-start(bf16[256,1024]{1,0:T(8,128)(2,1)} %shard_map.57), channel_id=1, source_target_pairs={{0,2},{1,3},{2,0},{3,1},{4,6},{5,7},{6,4},{7,5},{8,10},{9,11},{10,... | collective-permute-start | bytes 1572872 | tf_op jit(solution)/shard_map/ppermute | solution.py:222
  5.1 0.0 copy-done.1
  5.1 0.0 copy-done.2
  5.1 0.0 copy-done
  5.1 1.2 %shard_map.55 = (bf16[256,1024]{1,0:T(8,128)(2,1)S(1)}, bf16[256,1024]{1,0:T(8,128)(2,1)S(1)}, bf16[256,1024]{1,0:T(8,128)(2,1)S(1)}, bf16[240,1024]{1,0:T(8,128...) custom-call(s32[1,4]{1,0:T(1,128)S(1)} %copy-done.2, s32[4,4]{1,0:T(4,128)S(1)} %copy-done.1, ...), custom_call_target="tpu_custom_call" | custom-call | tf_op jit(solution)/shard_map/pallas_call | solution.py:118
  6.3 1.6 %collective-permute-start.5 = (bf16[256,1024]{1,0:T(8,128)(2,1)S(1)}, bf16[256,1024]{1,0:T(8,128)(2,1)S(1)}, u32[]{:S(2)}, u32[]{:S(2)}) collective-permute-start(bf16[256,1024]{1,0:T(8,128)(2,1)S(1)} %get-tuple-element.36), channel_id=1, source_target_pairs={{0,1},{1,0},{2,3},{3,2},{4,5},{5,4},{6,7},{7,6},{8,9},{9,8},{10,11... | collective-permute-start | bytes 1572872 | tf_op jit(solution)/shard_map/ppermute | solution.py:222
  8.0 0.0 collective-permute-start.4
  8.0 1.5 %collective-permute-start.3 = (bf16[256,1024]{1,0:T(8,128)(2,1)S(1)}, bf16[256,1024]{1,0:T(8,128)(2,1)S(1)}, u32[]{:S(2)}, u32[]{:S(2)}) collective-permute-start(bf16[256,1024]{1,0:T(8,128)(2,1)S(1)} %get-tuple-element.34), channel_id=1, source_target_pairs={{0,8},{4,12},{8,0},{12,4},{1,9},{5,13},{9,1},{13,5},{2,10},{6,14},... | collective-permute-start | bytes 1572872 | tf_op jit(solution)/shard_map/ppermute | solution.py:222
  9.5 0.2 collective-permute-start
  9.7 31.3 %collective-permute-done.6.arrived = bf16[256,1024]{1,0:T(8,128)(2,1)S(1)} collective-permute-done((bf16[256,1024]{1,0:T(8,128)(2,1)}, bf16[256,1024]{1,0:T(8,128)(2,1)S(1)}, u32[]{:S(2)}, u32[]{:S(2)}) %collective-permute-start.6) | collective-permute-done | bytes 524320 | tf_op jit(solution)/shard_map/ppermute | solution.py:222
  41.0 0.0 collective-permute-start.2
  41.0 0.1 collective-permute-done.5.arrived
  41.2 1.6 %collective-permute-start.1 = (bf16[16,1024]{1,0:T(8,128)(2,1)S(1)}, bf16[16,1024]{1,0:T(8,128)(2,1)S(1)}, u32[]{:S(2)}, u32[]{:S(2)}) collective-permute-start(bf16[16,1024]{1,0:T(8,128)(2,1)S(1)} %get-tuple-element.32), channel_id=1, source_target_pairs={{0,12},{4,8},{8,4},{12,0},{1,13},{5,9},{9,5},{13,1},{2,14},{6,10},... | collective-permute-start | bytes 98312 | tf_op jit(solution)/shard_map/ppermute | solution.py:222
  42.8 0.0 copy-done.4
  42.8 0.0 copy-done.3
  42.8 1.8 %shard_map.56 = (bf16[1024,1024]{1,0:T(8,128)(2,1)S(1)}, f32[7,4,128]{2,1,0:T(4,128)S(1)}, f32[7,8,128]{2,1,0:T(8,128)S(1)}) custom-call(s32[1,4]{1,0:T(1,128)S(1)} %copy-done.2, s32[4,4]{1,0:T(4,128)S(1)} %copy-done.1, s32[1,16]{1,0:T(1,128)S(1)} %copy-done.3, s32[1,16]{1,0:T(1,128)S(1)} %copy-done.4, bf16[1024,1024]{1,0:T(8,128)(2,1)S(1)} %copy-done), custom_call_target="tpu_custom_call" | custom-call | tf_op jit(solution)/shard_map/pallas_call | solution.py:150
  44.6 1.0 %shard_map.58 = (f32[8,128]{1,0:T(8,128)S(1)}, f32[8,128]{1,0:T(8,128)S(1)}) custom-call(bf16[256,1024]{1,0:T(8,128)(2,1)S(1)} %collective-permute-done.6.arrived, bf16[1024,1024]{1,0:T(8,128)(2,1)S(1)} %get-tuple-element.29.units, f32[7,4,128]{2,1,0:T(4,128)S(1)} %get-tuple-element.30.live, f32[7,8,128]{2,1,0:T(8,128)S(1)} %get-tuple-element.31.mine, ...), custom_call_target="tpu_custom_call" | custom-call | tf_op jit(solution)/shard_map/pallas_call | solution.py:193
  45.6 1.0 %shard_map.59 = (f32[8,128]{1,0:T(8,128)S(1)}, f32[8,128]{1,0:T(8,128)S(1)}) custom-call(bf16[256,1024]{1,0:T(8,128)(2,1)S(1)} %collective-permute-done.5.arrived, bf16[1024,1024]{1,0:T(8,128)(2,1)S(1)} %get-tuple-element.29.units, f32[7,4,128]{2,1,0:T(4,128)S(1)} %get-tuple-element.30.live, f32[7,8,128]{2,1,0:T(8,128)S(1)} %get-tuple-element.31.mine, ...), custom_call_target="tpu_custom_call" | custom-call | tf_op jit(solution)/shard_map/pallas_call | solution.py:193
  46.6 0.0 collective-permute-done.4.arrived
  46.6 1.0 %shard_map.60 = (f32[8,128]{1,0:T(8,128)S(1)}, f32[8,128]{1,0:T(8,128)S(1)}) custom-call(bf16[256,1024]{1,0:T(8,128)(2,1)S(1)} %collective-permute-done.4.arrived, bf16[1024,1024]{1,0:T(8,128)(2,1)S(1)} %get-tuple-element.29.units, f32[7,4,128]{2,1,0:T(4,128)S(1)} %get-tuple-element.30.live, f32[7,8,128]{2,1,0:T(8,128)S(1)} %get-tuple-element.31.mine, ...), custom_call_target="tpu_custom_call" | custom-call | tf_op jit(solution)/shard_map/pallas_call | solution.py:193
  47.6 0.1 collective-permute-start.7
  47.6 0.0 collective-permute-done.3.arrived
  47.7 1.0 %shard_map.61 = (f32[8,128]{1,0:T(8,128)S(1)}, f32[8,128]{1,0:T(8,128)S(1)}) custom-call(bf16[256,1024]{1,0:T(8,128)(2,1)S(1)} %collective-permute-done.3.arrived, bf16[1024,1024]{1,0:T(8,128)(2,1)S(1)} %get-tuple-element.29.units, f32[7,4,128]{2,1,0:T(4,128)S(1)} %get-tuple-element.30.live, f32[7,8,128]{2,1,0:T(8,128)S(1)} %get-tuple-element.31.mine, ...), custom_call_target="tpu_custom_call" | custom-call | tf_op jit(solution)/shard_map/pallas_call | solution.py:193
  48.7 1.6 %collective-permute-start.8 = (f32[8,128]{1,0:T(8,128)S(1)}, f32[8,128]{1,0:T(8,128)S(1)}, u32[]{:S(2)}, u32[]{:S(2)}) collective-permute-start(f32[8,128]{1,0:T(8,128)S(1)} %get-tuple-element.43), channel_id=1, source_target_pairs={{0,8},{4,12},{8,0},{12,4},{1,9},{5,13},{9,1},{13,5},{2,10},{6,14},... | collective-permute-start | bytes 12296 | tf_op jit(solution)/shard_map/ppermute | solution.py:222
  50.2 4.3 %collective-permute-done.2.arrived = bf16[240,1024]{1,0:T(8,128)(2,1)S(1)} collective-permute-done((bf16[240,1024]{1,0:T(8,128)(2,1)S(1)}, bf16[240,1024]{1,0:T(8,128)(2,1)S(1)}, u32[]{:S(2)}, u32[]{:S(2)}) %collective-permute-start.2) | collective-permute-done | bytes 491552 | tf_op jit(solution)/shard_map/ppermute | solution.py:222
  54.5 0.0 collective-permute-done.7.rest_0_
  54.5 0.9 %shard_map.62 = (f32[8,128]{1,0:T(8,128)S(1)}, f32[8,128]{1,0:T(8,128)S(1)}) custom-call(bf16[240,1024]{1,0:T(8,128)(2,1)S(1)} %collective-permute-done.2.arrived, bf16[1024,1024]{1,0:T(8,128)(2,1)S(1)} %get-tuple-element.29.units, f32[7,4,128]{2,1,0:T(4,128)S(1)} %get-tuple-element.30.live, f32[7,8,128]{2,1,0:T(8,128)S(1)} %get-tuple-element.31.mine, ...), custom_call_target="tpu_custom_call" | custom-call | tf_op jit(solution)/shard_map/pallas_call | solution.py:193
  55.4 0.0 collective-permute-done.1.arrived
  55.5 0.0 collective-permute-done.8.rest_0_
  55.5 0.5 shard_map.63
  56.0 0.2 collective-permute-start.9
  56.2 0.0 collective-permute-start.10
  56.2 0.0 collective-permute-start.11
  56.2 0.0 collective-permute-done.arrived
  56.3 2.9 %collective-permute-done.9.rest_0_ = f32[8,128]{1,0:T(8,128)S(1)} collective-permute-done((f32[8,128]{1,0:T(8,128)S(1)}, f32[8,128]{1,0:T(8,128)S(1)}, u32[]{:S(2)}, u32[]{:S(2)}) %collective-permute-start.9) | collective-permute-done | bytes 4128 | tf_op jit(solution)/shard_map/ppermute | solution.py:222
  59.1 1.0 %shard_map.64 = (f32[8,128]{1,0:T(8,128)S(1)}, f32[8,128]{1,0:T(8,128)S(1)}) custom-call(bf16[256,1024]{1,0:T(8,128)(2,1)S(1)} %collective-permute-done.arrived, bf16[1024,1024]{1,0:T(8,128)(2,1)S(1)} %get-tuple-element.29.units, f32[7,4,128]{2,1,0:T(4,128)S(1)} %get-tuple-element.30.live, f32[7,8,128]{2,1,0:T(8,128)S(1)} %get-tuple-element.31.mine, ...), custom_call_target="tpu_custom_call" | custom-call | tf_op jit(solution)/shard_map/pallas_call | solution.py:193
  60.1 1.5 %collective-permute-start.12 = (f32[8,128]{1,0:T(8,128)S(1)}, f32[8,128]{1,0:T(8,128)S(1)}, u32[]{:S(2)}, u32[]{:S(2)}) collective-permute-start(f32[8,128]{1,0:T(8,128)S(1)} %get-tuple-element.50), channel_id=1, source_target_pairs={{0,3},{1,2},{2,1},{3,0},{4,7},{5,6},{6,5},{7,4},{8,11},{9,10},{10,... | collective-permute-start | bytes 12296 | tf_op jit(solution)/shard_map/ppermute | solution.py:222
  61.6 0.0 collective-permute-done.10
  61.6 0.0 collective-permute-done.11
  61.7 3.9 %collective-permute-done.12 = f32[8,128]{1,0:T(8,128)S(1)} collective-permute-done((f32[8,128]{1,0:T(8,128)S(1)}, f32[8,128]{1,0:T(8,128)S(1)}, u32[]{:S(2)}, u32[]{:S(2)}) %collective-permute-start.12) | collective-permute-done | bytes 4128 | tf_op jit(solution)/shard_map/ppermute | solution.py:222
  65.6 0.6 fusion.2
  (1 shorter events, 0.0 us)
Async XLA Ops:
  0.0 5.1 %copy-start.1 = (s32[4,4]{1,0:T(4,128)S(1)}, s32[4,4]{1,0:T(4,128)}, u32[]{:S(2)}) copy-start(s32[4,4]{1,0:T(4,128)} %pick_sub.5) | copy-start | bytes 196
  0.0 5.1 %copy-start.2 = (s32[1,4]{1,0:T(1,128)S(1)}, s32[1,4]{1,0:T(1,128)}, u32[]{:S(2)}) copy-start(s32[1,4]{1,0:T(1,128)} %pick_blk.5) | copy-start | bytes 52
  0.0 5.1 %copy-start = (bf16[1024,1024]{1,0:T(8,128)(2,1)S(1)}, bf16[1024,1024]{1,0:T(8,128)(2,1)}, u32[]{:S(2)}) copy-start(bf16[1024,1024]{1,0:T(8,128)(2,1)} %embeds.5) | copy-start | bytes 6291460
  0.0 42.8 %copy-start.4 = (s32[1,16]{1,0:T(1,128)S(1)}, s32[1,16]{1,0:T(1,128)}, u32[]{:S(2)}) copy-start(s32[1,16]{1,0:T(1,128)} %mask_sub.1) | copy-start | bytes 196
  0.0 42.8 %copy-start.3 = (s32[1,16]{1,0:T(1,128)S(1)}, s32[1,16]{1,0:T(1,128)}, u32[]{:S(2)}) copy-start(s32[1,16]{1,0:T(1,128)} %mask_blk.1) | copy-start | bytes 196
  2.5 38.5 %collective-permute-start.6 = (bf16[256,1024]{1,0:T(8,128)(2,1)}, bf16[256,1024]{1,0:T(8,128)(2,1)S(1)}, u32[]{:S(2)}, u32[]{:S(2)}) collective-permute-start(bf16[256,1024]{1,0:T(8,128)(2,1)} %shard_map.57), channel_id=1, source_target_pairs={{0,2},{1,3},{2,0},{3,1},{4,6},{5,7},{6,4},{7,5},{8,10},{9,11},{10,... | collective-permute-start | bytes 1572872 | tf_op jit(solution)/shard_map/ppermute | solution.py:222
  6.3 34.8 %collective-permute-start.5 = (bf16[256,1024]{1,0:T(8,128)(2,1)S(1)}, bf16[256,1024]{1,0:T(8,128)(2,1)S(1)}, u32[]{:S(2)}, u32[]{:S(2)}) collective-permute-start(bf16[256,1024]{1,0:T(8,128)(2,1)S(1)} %get-tuple-element.36), channel_id=1, source_target_pairs={{0,1},{1,0},{2,3},{3,2},{4,5},{5,4},{6,7},{7,6},{8,9},{9,8},{10,11... | collective-permute-start | bytes 1572872 | tf_op jit(solution)/shard_map/ppermute | solution.py:222
  8.0 38.6 %collective-permute-start.4 = (bf16[256,1024]{1,0:T(8,128)(2,1)S(1)}, bf16[256,1024]{1,0:T(8,128)(2,1)S(1)}, u32[]{:S(2)}, u32[]{:S(2)}) collective-permute-start(bf16[256,1024]{1,0:T(8,128)(2,1)S(1)} %get-tuple-element.35), channel_id=1, source_target_pairs={{0,4},{4,0},{8,12},{12,8},{1,5},{5,1},{9,13},{13,9},{2,6},{6,2},{1... | collective-permute-start | bytes 1572872 | tf_op jit(solution)/shard_map/ppermute | solution.py:222
  8.0 39.7 %collective-permute-start.3 = (bf16[256,1024]{1,0:T(8,128)(2,1)S(1)}, bf16[256,1024]{1,0:T(8,128)(2,1)S(1)}, u32[]{:S(2)}, u32[]{:S(2)}) collective-permute-start(bf16[256,1024]{1,0:T(8,128)(2,1)S(1)} %get-tuple-element.34), channel_id=1, source_target_pairs={{0,8},{4,12},{8,0},{12,4},{1,9},{5,13},{9,1},{13,5},{2,10},{6,14},... | collective-permute-start | bytes 1572872 | tf_op jit(solution)/shard_map/ppermute | solution.py:222
  9.5 46.8 %collective-permute-start = (bf16[256,1024]{1,0:T(8,128)(2,1)S(1)}, bf16[256,1024]{1,0:T(8,128)(2,1)S(1)}, u32[]{:S(2)}, u32[]{:S(2)}) collective-permute-start(bf16[256,1024]{1,0:T(8,128)(2,1)S(1)} %get-tuple-element.28), channel_id=1, source_target_pairs={{0,3},{1,2},{2,1},{3,0},{4,7},{5,6},{6,5},{7,4},{8,11},{9,10},{10,... | collective-permute-start | bytes 1572872 | tf_op jit(solution)/shard_map/ppermute | solution.py:222
  41.0 13.5 %collective-permute-start.2 = (bf16[240,1024]{1,0:T(8,128)(2,1)S(1)}, bf16[240,1024]{1,0:T(8,128)(2,1)S(1)}, u32[]{:S(2)}, u32[]{:S(2)}) collective-permute-start(bf16[240,1024]{1,0:T(8,128)(2,1)S(1)} %get-tuple-element.33), channel_id=1, source_target_pairs={{0,12},{4,8},{8,4},{12,0},{1,13},{5,9},{9,5},{13,1},{2,14},{6,10},... | collective-permute-start | bytes 1474568 | tf_op jit(solution)/shard_map/ppermute | solution.py:222
  41.2 14.3 %collective-permute-start.1 = (bf16[16,1024]{1,0:T(8,128)(2,1)S(1)}, bf16[16,1024]{1,0:T(8,128)(2,1)S(1)}, u32[]{:S(2)}, u32[]{:S(2)}) collective-permute-start(bf16[16,1024]{1,0:T(8,128)(2,1)S(1)} %get-tuple-element.32), channel_id=1, source_target_pairs={{0,12},{4,8},{8,4},{12,0},{1,13},{5,9},{9,5},{13,1},{2,14},{6,10},... | collective-permute-start | bytes 98312 | tf_op jit(solution)/shard_map/ppermute | solution.py:222
  47.6 6.9 %collective-permute-start.7 = (f32[8,128]{1,0:T(8,128)S(1)}, f32[8,128]{1,0:T(8,128)S(1)}, u32[]{:S(2)}, u32[]{:S(2)}) collective-permute-start(f32[8,128]{1,0:T(8,128)S(1)} %get-tuple-element.41), channel_id=1, source_target_pairs={{0,4},{4,0},{8,12},{12,8},{1,5},{5,1},{9,13},{13,9},{2,6},{6,2},{1... | collective-permute-start | bytes 12296 | tf_op jit(solution)/shard_map/ppermute | solution.py:222
  48.7 6.8 %collective-permute-start.8 = (f32[8,128]{1,0:T(8,128)S(1)}, f32[8,128]{1,0:T(8,128)S(1)}, u32[]{:S(2)}, u32[]{:S(2)}) collective-permute-start(f32[8,128]{1,0:T(8,128)S(1)} %get-tuple-element.43), channel_id=1, source_target_pairs={{0,8},{4,12},{8,0},{12,4},{1,9},{5,13},{9,1},{13,5},{2,10},{6,14},... | collective-permute-start | bytes 12296 | tf_op jit(solution)/shard_map/ppermute | solution.py:222
  56.0 3.1 %collective-permute-start.9 = (f32[8,128]{1,0:T(8,128)S(1)}, f32[8,128]{1,0:T(8,128)S(1)}, u32[]{:S(2)}, u32[]{:S(2)}) collective-permute-start(f32[8,128]{1,0:T(8,128)S(1)} %get-tuple-element.46), channel_id=1, source_target_pairs={{0,12},{4,8},{8,4},{12,0},{1,13},{5,9},{9,5},{13,1},{2,14},{6,10},... | collective-permute-start | bytes 12296 | tf_op jit(solution)/shard_map/ppermute | solution.py:222
  56.2 5.5 %collective-permute-start.10 = (f32[8,128]{1,0:T(8,128)S(1)}, f32[8,128]{1,0:T(8,128)S(1)}, u32[]{:S(2)}, u32[]{:S(2)}) collective-permute-start(f32[8,128]{1,0:T(8,128)S(1)} %get-tuple-element.48), channel_id=1, source_target_pairs={{0,2},{1,3},{2,0},{3,1},{4,6},{5,7},{6,4},{7,5},{8,10},{9,11},{10,... | collective-permute-start | bytes 12296 | tf_op jit(solution)/shard_map/ppermute | solution.py:222
  56.2 5.5 %collective-permute-start.11 = (f32[8,128]{1,0:T(8,128)S(1)}, f32[8,128]{1,0:T(8,128)S(1)}, u32[]{:S(2)}, u32[]{:S(2)}) collective-permute-start(f32[8,128]{1,0:T(8,128)S(1)} %get-tuple-element.49), channel_id=1, source_target_pairs={{0,1},{1,0},{2,3},{3,2},{4,5},{5,4},{6,7},{7,6},{8,9},{9,8},{10,11... | collective-permute-start | bytes 12296 | tf_op jit(solution)/shard_map/ppermute | solution.py:222
  60.1 5.5 %collective-permute-start.12 = (f32[8,128]{1,0:T(8,128)S(1)}, f32[8,128]{1,0:T(8,128)S(1)}, u32[]{:S(2)}, u32[]{:S(2)}) collective-permute-start(f32[8,128]{1,0:T(8,128)S(1)} %get-tuple-element.50), channel_id=1, source_target_pairs={{0,3},{1,2},{2,1},{3,0},{4,7},{5,6},{6,5},{7,4},{8,11},{9,10},{10,... | collective-permute-start | bytes 12296 | tf_op jit(solution)/shard_map/ppermute | solution.py:222

commit v22 on v19

--- a/solution.py
+++ b/solution.py
@@ -200,14 +200,14 @@
 
 
 BEHIND = 2
-FIRST_CUT = 128
+LAST_CUTS = ((0, 128), (128, 112), (240, 16))
 
 
 def plan_slots(sizes):
     slots = [("blk", 1, 0, BLOCK), ("sub", 2, 0, BLOCK), ("sub", 1, 0, BLOCK)]
     slots += [("blk", k, 0, BLOCK) for k in range(2, sizes["blk"])]
     for k in range(3, sizes["sub"]):
-        slots += [("sub", k, 0, FIRST_CUT), ("sub", k, FIRST_CUT, BLOCK - FIRST_CUT)]
+        slots += [("sub", k, first, rows) for first, rows in LAST_CUTS]
     return slots
 
 

time: 57.1 us -> 62.3 us (1.091); the launches traced: 56 us -> 62.2 us
  waiting for transfers between devices: 22.4 us -> 30.4 us
  starting transfers between devices: 21.4 us -> 18.7 us
  Pallas kernels: 11.5 us -> 12.3 us
    ppermute x13 -> x14, waiting for transfers between devices: 22.4 us -> 30.4 us  [send(): return lax.ppermute(array, slot[0], pairs(slot[1], sizes[slot[0]]))]
    ppermute x13 -> x14, starting transfers between devices: 21.4 us -> 18.7 us  [send(): return lax.ppermute(array, slot[0], pairs(slot[1], sizes[slot[0]]))]
    pallas_call x7 -> x8, Pallas kernels: 6.29 us -> 6.75 us  [work(): pl.pallas_call(functools.partial(slot_kernel, place, *slot[2:], [one for...]
  transfers between devices with their start and end apart: 13 -> 14, of which waited for: 4 -> 6; matrix products, arithmetic and copies ran while one was open for 0% -> 0% of each run, Pallas kernels for 16% -> 16%
where the time goes in v22:
time: 62.3 us; the launch traced here: 62.2 us
  waiting for transfers between devices  30.4 us (49%)
  starting transfers between devices  18.7 us (30%)
  Pallas kernels  12.3 us (20%)
    ppermute x14, waiting for transfers between devices, send(): return lax.ppermute(array, slot[0], pairs(slot[1], sizes[slot[0]]))  30.4 us
    ppermute x14, starting transfers between devices, send(): return lax.ppermute(array, slot[0], pairs(slot[1], sizes[slot[0]]))  18.7 us
    pallas_call x8, Pallas kernels, work(): pl.pallas_call(functools.partial(slot_kernel, place, *slot[2:], [one for...  6.75 us
    pallas_call x1, Pallas kernels, first_rows(): pl.pallas_call(functools.partial(first_kernel, slots), out_shape=[jax.Sha...  2.58 us
    pallas_call x1, Pallas kernels, prepare(): pl.pallas_call(functools.partial(prepare_kernel, slots), out_shape=[jax.S...  1.77 us
  transfers between devices with their start and end apart: 14, of which 6 were waited for; matrix products, arithmetic and copies ran while one was open for 0% of the time, Pallas kernels for 16%

profile of v22, /device:TPU:0, one launch (start us, length us, event | category | flops | bytes accessed | tf_op | source)
XLA Modules:
  0.0 62.2 jit_solution(619084077670955567)
XLA Ops:
  0.0 0.0 copy-start
  0.0 0.0 copy-start.2
  0.0 0.0 copy-start.3
  0.0 2.6 %shard_map.57 = (bf16[256,1024]{1,0:T(8,128)(2,1)}, bf16[256,1024]{1,0:T(8,128)(2,1)}) custom-call(s32[1,4]{1,0:T(1,128)} %pick_blk.5, s32[4,4]{1,0:T(4,128)} %pick_sub.5, bf16[1024,1024]{1,0:T(8,128)(2,1)} %embeds.5), custom_call_target="tpu_custom_call" | custom-call | tf_op jit(solution)/shard_map/pallas_call | solution.py:81
  2.6 0.5 collective-permute-start.7
  3.1 3.7 %collective-permute-start.6 = (bf16[256,1024]{1,0:T(8,128)(2,1)}, bf16[256,1024]{1,0:T(8,128)(2,1)S(1)}, u32[]{:S(2)}, u32[]{:S(2)}) collective-permute-start(bf16[256,1024]{1,0:T(8,128)(2,1)} %get-tuple-element.41), channel_id=1, source_target_pairs={{0,2},{1,3},{2,0},{3,1},{4,6},{5,7},{6,4},{7,5},{8,10},{9,11},{10,... | collective-permute-start | bytes 1572872 | tf_op jit(solution)/shard_map/ppermute | solution.py:223
  6.8 0.0 copy-done
  6.8 0.0 copy-done.2
  6.8 0.0 copy-done.1
  6.8 1.2 %shard_map.55 = (bf16[256,1024]{1,0:T(8,128)(2,1)S(1)}, bf16[256,1024]{1,0:T(8,128)(2,1)S(1)}, bf16[256,1024]{1,0:T(8,128)(2,1)S(1)}, bf16[128,1024]{1,0:T(8,128...) custom-call(s32[1,4]{1,0:T(1,128)S(1)} %copy-done.2, s32[4,4]{1,0:T(4,128)S(1)} %copy-done.1, ...), custom_call_target="tpu_custom_call" | custom-call | tf_op jit(solution)/shard_map/pallas_call | solution.py:118
  8.0 1.6 %collective-permute-start.5 = (bf16[256,1024]{1,0:T(8,128)(2,1)S(1)}, bf16[256,1024]{1,0:T(8,128)(2,1)S(1)}, u32[]{:S(2)}, u32[]{:S(2)}) collective-permute-start(bf16[256,1024]{1,0:T(8,128)(2,1)S(1)} %get-tuple-element.40), channel_id=1, source_target_pairs={{0,1},{1,0},{2,3},{3,2},{4,5},{5,4},{6,7},{7,6},{8,9},{9,8},{10,11... | collective-permute-start | bytes 1572872 | tf_op jit(solution)/shard_map/ppermute | solution.py:223
  9.6 1.5 %collective-permute-start.4 = (bf16[256,1024]{1,0:T(8,128)(2,1)S(1)}, bf16[256,1024]{1,0:T(8,128)(2,1)S(1)}, u32[]{:S(2)}, u32[]{:S(2)}) collective-permute-start(bf16[256,1024]{1,0:T(8,128)(2,1)S(1)} %get-tuple-element.39), channel_id=1, source_target_pairs={{0,8},{4,12},{8,0},{12,4},{1,9},{5,13},{9,1},{13,5},{2,10},{6,14},... | collective-permute-start | bytes 1572872 | tf_op jit(solution)/shard_map/ppermute | solution.py:223
  11.1 0.0 collective-permute-start.3
  11.1 0.0 collective-permute-done.7.arrived
  11.1 0.2 collective-permute-start.2
  11.3 19.7 %collective-permute-done.6.arrived = bf16[256,1024]{1,0:T(8,128)(2,1)S(1)} collective-permute-done((bf16[256,1024]{1,0:T(8,128)(2,1)}, bf16[256,1024]{1,0:T(8,128)(2,1)S(1)}, u32[]{:S(2)}, u32[]{:S(2)}) %collective-permute-start.6) | collective-permute-done | bytes 524320 | tf_op jit(solution)/shard_map/ppermute | solution.py:223
  31.1 3.8 %collective-permute-start.1 = (bf16[112,1024]{1,0:T(8,128)(2,1)S(1)}, bf16[112,1024]{1,0:T(8,128)(2,1)S(1)}, u32[]{:S(2)}, u32[]{:S(2)}) collective-permute-start(bf16[112,1024]{1,0:T(8,128)(2,1)S(1)} %get-tuple-element.36), channel_id=1, source_target_pairs={{0,3},{1,2},{2,1},{3,0},{4,7},{5,6},{6,5},{7,4},{8,11},{9,10},{10,... | collective-permute-start | bytes 688136 | tf_op jit(solution)/shard_map/ppermute | solution.py:223
  34.9 0.0 copy-done.3
  34.9 0.0 copy-done.4
  34.9 1.8 %shard_map.56 = (bf16[1024,1024]{1,0:T(8,128)(2,1)S(1)}, f32[8,4,128]{2,1,0:T(4,128)S(1)}, f32[8,8,128]{2,1,0:T(8,128)S(1)}) custom-call(s32[1,4]{1,0:T(1,128)S(1)} %copy-done.2, s32[4,4]{1,0:T(4,128)S(1)} %copy-done.1, s32[1,16]{1,0:T(1,128)S(1)} %copy-done.3, s32[1,16]{1,0:T(1,128)S(1)} %copy-done.4, bf16[1024,1024]{1,0:T(8,128)(2,1)S(1)} %copy-done), custom_call_target="tpu_custom_call" | custom-call | tf_op jit(solution)/shard_map/pallas_call | solution.py:150
  36.7 1.0 %shard_map.58 = (f32[8,128]{1,0:T(8,128)S(1)}, f32[8,128]{1,0:T(8,128)S(1)}) custom-call(bf16[256,1024]{1,0:T(8,128)(2,1)S(1)} %collective-permute-done.7.arrived, bf16[1024,1024]{1,0:T(8,128)(2,1)S(1)} %get-tuple-element.33.units, f32[8,4,128]{2,1,0:T(4,128)S(1)} %get-tuple-element.34.live, f32[8,8,128]{2,1,0:T(8,128)S(1)} %get-tuple-element.35.mine, ...), custom_call_target="tpu_custom_call" | custom-call | tf_op jit(solution)/shard_map/pallas_call | solution.py:193
  37.7 5.0 %collective-permute-done.5.arrived = bf16[256,1024]{1,0:T(8,128)(2,1)S(1)} collective-permute-done((bf16[256,1024]{1,0:T(8,128)(2,1)S(1)}, bf16[256,1024]{1,0:T(8,128)(2,1)S(1)}, u32[]{:S(2)}, u32[]{:S(2)}) %collective-permute-start.5) | collective-permute-done | bytes 524320 | tf_op jit(solution)/shard_map/ppermute | solution.py:223
  42.6 0.0 collective-permute-start.8
  42.6 1.2 %collective-permute-done.8.rest_0_ = f32[8,128]{1,0:T(8,128)S(1)} collective-permute-done((f32[8,128]{1,0:T(8,128)S(1)}, f32[8,128]{1,0:T(8,128)S(1)}, u32[]{:S(2)}, u32[]{:S(2)}) %collective-permute-start.8) | collective-permute-done | bytes 4128 | tf_op jit(solution)/shard_map/ppermute | solution.py:223
  43.8 2.5 %collective-permute-start = (bf16[16,1024]{1,0:T(8,128)(2,1)S(1)}, bf16[16,1024]{1,0:T(8,128)(2,1)S(1)}, u32[]{:S(2)}, u32[]{:S(2)}) collective-permute-start(bf16[16,1024]{1,0:T(8,128)(2,1)S(1)} %get-tuple-element.32), channel_id=1, source_target_pairs={{0,3},{1,2},{2,1},{3,0},{4,7},{5,6},{6,5},{7,4},{8,11},{9,10},{10,... | collective-permute-start | bytes 98312 | tf_op jit(solution)/shard_map/ppermute | solution.py:223
  46.3 1.0 %shard_map.59 = (f32[8,128]{1,0:T(8,128)S(1)}, f32[8,128]{1,0:T(8,128)S(1)}) custom-call(bf16[256,1024]{1,0:T(8,128)(2,1)S(1)} %collective-permute-done.6.arrived, bf16[1024,1024]{1,0:T(8,128)(2,1)S(1)} %get-tuple-element.33.units, f32[8,4,128]{2,1,0:T(4,128)S(1)} %get-tuple-element.34.live, f32[8,8,128]{2,1,0:T(8,128)S(1)} %get-tuple-element.35.mine, ...), custom_call_target="tpu_custom_call" | custom-call | tf_op jit(solution)/shard_map/pallas_call | solution.py:193
  47.3 1.0 %shard_map.60 = (f32[8,128]{1,0:T(8,128)S(1)}, f32[8,128]{1,0:T(8,128)S(1)}) custom-call(bf16[256,1024]{1,0:T(8,128)(2,1)S(1)} %collective-permute-done.5.arrived, bf16[1024,1024]{1,0:T(8,128)(2,1)S(1)} %get-tuple-element.33.units, f32[8,4,128]{2,1,0:T(4,128)S(1)} %get-tuple-element.34.live, f32[8,8,128]{2,1,0:T(8,128)S(1)} %get-tuple-element.35.mine, ...), custom_call_target="tpu_custom_call" | custom-call | tf_op jit(solution)/shard_map/pallas_call | solution.py:193
  48.3 0.0 collective-permute-done.4.arrived
  48.3 1.0 %shard_map.61 = (f32[8,128]{1,0:T(8,128)S(1)}, f32[8,128]{1,0:T(8,128)S(1)}) custom-call(bf16[256,1024]{1,0:T(8,128)(2,1)S(1)} %collective-permute-done.4.arrived, bf16[1024,1024]{1,0:T(8,128)(2,1)S(1)} %get-tuple-element.33.units, f32[8,4,128]{2,1,0:T(4,128)S(1)} %get-tuple-element.34.live, f32[8,8,128]{2,1,0:T(8,128)S(1)} %get-tuple-element.35.mine, ...), custom_call_target="tpu_custom_call" | custom-call | tf_op jit(solution)/shard_map/pallas_call | solution.py:193
  49.3 1.6 %collective-permute-start.9 = (f32[8,128]{1,0:T(8,128)S(1)}, f32[8,128]{1,0:T(8,128)S(1)}, u32[]{:S(2)}, u32[]{:S(2)}) collective-permute-start(f32[8,128]{1,0:T(8,128)S(1)} %get-tuple-element.49), channel_id=1, source_target_pairs={{0,8},{4,12},{8,0},{12,4},{1,9},{5,13},{9,1},{13,5},{2,10},{6,14},... | collective-permute-start | bytes 12296 | tf_op jit(solution)/shard_map/ppermute | solution.py:223
  50.8 0.0 collective-permute-done.3.arrived
  50.8 1.0 %shard_map.62 = (f32[8,128]{1,0:T(8,128)S(1)}, f32[8,128]{1,0:T(8,128)S(1)}) custom-call(bf16[256,1024]{1,0:T(8,128)(2,1)S(1)} %collective-permute-done.3.arrived, bf16[1024,1024]{1,0:T(8,128)(2,1)S(1)} %get-tuple-element.33.units, f32[8,4,128]{2,1,0:T(4,128)S(1)} %get-tuple-element.34.live, f32[8,8,128]{2,1,0:T(8,128)S(1)} %get-tuple-element.35.mine, ...), custom_call_target="tpu_custom_call" | custom-call | tf_op jit(solution)/shard_map/pallas_call | solution.py:193
  51.8 0.1 collective-permute-start.10
  51.9 0.0 collective-permute-done.2.arrived
  51.9 0.1 collective-permute-start.11
  52.0 1.0 %collective-permute-done.9.rest_0_ = f32[8,128]{1,0:T(8,128)S(1)} collective-permute-done((f32[8,128]{1,0:T(8,128)S(1)}, f32[8,128]{1,0:T(8,128)S(1)}, u32[]{:S(2)}, u32[]{:S(2)}) %collective-permute-start.9) | collective-permute-done | bytes 4128 | tf_op jit(solution)/shard_map/ppermute | solution.py:223
  52.9 1.0 %collective-permute-start.12 = (f32[8,128]{1,0:T(8,128)S(1)}, f32[8,128]{1,0:T(8,128)S(1)}, u32[]{:S(2)}, u32[]{:S(2)}) collective-permute-start(f32[8,128]{1,0:T(8,128)S(1)} %get-tuple-element.57), channel_id=1, source_target_pairs={{0,1},{1,0},{2,3},{3,2},{4,5},{5,4},{6,7},{7,6},{8,9},{9,8},{10,11... | collective-permute-start | bytes 12296 | tf_op jit(solution)/shard_map/ppermute | solution.py:223
  53.9 0.7 %shard_map.63 = (f32[8,128]{1,0:T(8,128)S(1)}, f32[8,128]{1,0:T(8,128)S(1)}) custom-call(bf16[128,1024]{1,0:T(8,128)(2,1)S(1)} %collective-permute-done.2.arrived, bf16[1024,1024]{1,0:T(8,128)(2,1)S(1)} %get-tuple-element.33.units, f32[8,4,128]{2,1,0:T(4,128)S(1)} %get-tuple-element.34.live, f32[8,8,128]{2,1,0:T(8,128)S(1)} %get-tuple-element.35.mine, ...), custom_call_target="tpu_custom_call" | custom-call | tf_op jit(solution)/shard_map/pallas_call | solution.py:193
  54.5 0.0 collective-permute-done.1.arrived
  54.6 0.3 collective-permute-done.10.rest_0_
  54.9 0.7 %shard_map.64 = (f32[8,128]{1,0:T(8,128)S(1)}, f32[8,128]{1,0:T(8,128)S(1)}) custom-call(bf16[112,1024]{1,0:T(8,128)(2,1)S(1)} %collective-permute-done.1.arrived, bf16[1024,1024]{1,0:T(8,128)(2,1)S(1)} %get-tuple-element.33.units, f32[8,4,128]{2,1,0:T(4,128)S(1)} %get-tuple-element.34.live, f32[8,8,128]{2,1,0:T(8,128)S(1)} %get-tuple-element.35.mine, ...), custom_call_target="tpu_custom_call" | custom-call | tf_op jit(solution)/shard_map/pallas_call | solution.py:193
  55.5 0.0 collective-permute-done.arrived
  55.6 0.5 shard_map.65
  56.1 2.2 %collective-permute-start.13 = (f32[8,128]{1,0:T(8,128)S(1)}, f32[8,128]{1,0:T(8,128)S(1)}, u32[]{:S(2)}, u32[]{:S(2)}) collective-permute-start(f32[8,128]{1,0:T(8,128)S(1)} %get-tuple-element.58), channel_id=1, source_target_pairs={{0,3},{1,2},{2,1},{3,0},{4,7},{5,6},{6,5},{7,4},{8,11},{9,10},{10,... | collective-permute-start | bytes 12296 | tf_op jit(solution)/shard_map/ppermute | solution.py:223
  58.3 0.0 collective-permute-done.11
  58.3 0.0 collective-permute-done.12
  58.3 3.3 %collective-permute-done.13 = f32[8,128]{1,0:T(8,128)S(1)} collective-permute-done((f32[8,128]{1,0:T(8,128)S(1)}, f32[8,128]{1,0:T(8,128)S(1)}, u32[]{:S(2)}, u32[]{:S(2)}) %collective-permute-start.13) | collective-permute-done | bytes 4128 | tf_op jit(solution)/shard_map/ppermute | solution.py:223
  61.6 0.6 fusion.2
  (3 shorter events, 0.0 us)
Async XLA Ops:
  0.0 6.8 %copy-start = (bf16[1024,1024]{1,0:T(8,128)(2,1)S(1)}, bf16[1024,1024]{1,0:T(8,128)(2,1)}, u32[]{:S(2)}) copy-start(bf16[1024,1024]{1,0:T(8,128)(2,1)} %embeds.5) | copy-start | bytes 6291460
  0.0 6.8 %copy-start.2 = (s32[1,4]{1,0:T(1,128)S(1)}, s32[1,4]{1,0:T(1,128)}, u32[]{:S(2)}) copy-start(s32[1,4]{1,0:T(1,128)} %pick_blk.5) | copy-start | bytes 52
  0.0 6.8 %copy-start.1 = (s32[4,4]{1,0:T(4,128)S(1)}, s32[4,4]{1,0:T(4,128)}, u32[]{:S(2)}) copy-start(s32[4,4]{1,0:T(4,128)} %pick_sub.5) | copy-start | bytes 196
  0.0 34.9 %copy-start.3 = (s32[1,16]{1,0:T(1,128)S(1)}, s32[1,16]{1,0:T(1,128)}, u32[]{:S(2)}) copy-start(s32[1,16]{1,0:T(1,128)} %mask_blk.1) | copy-start | bytes 196
  0.0 34.9 %copy-start.4 = (s32[1,16]{1,0:T(1,128)S(1)}, s32[1,16]{1,0:T(1,128)}, u32[]{:S(2)}) copy-start(s32[1,16]{1,0:T(1,128)} %mask_sub.1) | copy-start | bytes 196
  2.6 8.5 %collective-permute-start.7 = (bf16[256,1024]{1,0:T(8,128)(2,1)}, bf16[256,1024]{1,0:T(8,128)(2,1)S(1)}, u32[]{:S(2)}, u32[]{:S(2)}) collective-permute-start(bf16[256,1024]{1,0:T(8,128)(2,1)} %get-tuple-element.42), channel_id=1, source_target_pairs={{0,4},{4,0},{8,12},{12,8},{1,5},{5,1},{9,13},{13,9},{2,6},{6,2},{1... | collective-permute-start | bytes 1572872 | tf_op jit(solution)/shard_map/ppermute | solution.py:223
  3.1 27.9 %collective-permute-start.6 = (bf16[256,1024]{1,0:T(8,128)(2,1)}, bf16[256,1024]{1,0:T(8,128)(2,1)S(1)}, u32[]{:S(2)}, u32[]{:S(2)}) collective-permute-start(bf16[256,1024]{1,0:T(8,128)(2,1)} %get-tuple-element.41), channel_id=1, source_target_pairs={{0,2},{1,3},{2,0},{3,1},{4,6},{5,7},{6,4},{7,5},{8,10},{9,11},{10,... | collective-permute-start | bytes 1572872 | tf_op jit(solution)/shard_map/ppermute | solution.py:223
  8.0 34.6 %collective-permute-start.5 = (bf16[256,1024]{1,0:T(8,128)(2,1)S(1)}, bf16[256,1024]{1,0:T(8,128)(2,1)S(1)}, u32[]{:S(2)}, u32[]{:S(2)}) collective-permute-start(bf16[256,1024]{1,0:T(8,128)(2,1)S(1)} %get-tuple-element.40), channel_id=1, source_target_pairs={{0,1},{1,0},{2,3},{3,2},{4,5},{5,4},{6,7},{7,6},{8,9},{9,8},{10,11... | collective-permute-start | bytes 1572872 | tf_op jit(solution)/shard_map/ppermute | solution.py:223
  9.6 38.7 %collective-permute-start.4 = (bf16[256,1024]{1,0:T(8,128)(2,1)S(1)}, bf16[256,1024]{1,0:T(8,128)(2,1)S(1)}, u32[]{:S(2)}, u32[]{:S(2)}) collective-permute-start(bf16[256,1024]{1,0:T(8,128)(2,1)S(1)} %get-tuple-element.39), channel_id=1, source_target_pairs={{0,8},{4,12},{8,0},{12,4},{1,9},{5,13},{9,1},{13,5},{2,10},{6,14},... | collective-permute-start | bytes 1572872 | tf_op jit(solution)/shard_map/ppermute | solution.py:223
  11.1 39.7 %collective-permute-start.3 = (bf16[256,1024]{1,0:T(8,128)(2,1)S(1)}, bf16[256,1024]{1,0:T(8,128)(2,1)S(1)}, u32[]{:S(2)}, u32[]{:S(2)}) collective-permute-start(bf16[256,1024]{1,0:T(8,128)(2,1)S(1)} %get-tuple-element.38), channel_id=1, source_target_pairs={{0,12},{4,8},{8,4},{12,0},{1,13},{5,9},{9,5},{13,1},{2,14},{6,10},... | collective-permute-start | bytes 1572872 | tf_op jit(solution)/shard_map/ppermute | solution.py:223
  11.1 40.8 %collective-permute-start.2 = (bf16[128,1024]{1,0:T(8,128)(2,1)S(1)}, bf16[128,1024]{1,0:T(8,128)(2,1)S(1)}, u32[]{:S(2)}, u32[]{:S(2)}) collective-permute-start(bf16[128,1024]{1,0:T(8,128)(2,1)S(1)} %get-tuple-element.37), channel_id=1, source_target_pairs={{0,3},{1,2},{2,1},{3,0},{4,7},{5,6},{6,5},{7,4},{8,11},{9,10},{10,... | collective-permute-start | bytes 786440 | tf_op jit(solution)/shard_map/ppermute | solution.py:223
  31.1 23.5 %collective-permute-start.1 = (bf16[112,1024]{1,0:T(8,128)(2,1)S(1)}, bf16[112,1024]{1,0:T(8,128)(2,1)S(1)}, u32[]{:S(2)}, u32[]{:S(2)}) collective-permute-start(bf16[112,1024]{1,0:T(8,128)(2,1)S(1)} %get-tuple-element.36), channel_id=1, source_target_pairs={{0,3},{1,2},{2,1},{3,0},{4,7},{5,6},{6,5},{7,4},{8,11},{9,10},{10,... | collective-permute-start | bytes 688136 | tf_op jit(solution)/shard_map/ppermute | solution.py:223
  42.6 1.2 %collective-permute-start.8 = (f32[8,128]{1,0:T(8,128)S(1)}, f32[8,128]{1,0:T(8,128)S(1)}, u32[]{:S(2)}, u32[]{:S(2)}) collective-permute-start(f32[8,128]{1,0:T(8,128)S(1)} %get-tuple-element.45), channel_id=1, source_target_pairs={{0,4},{4,0},{8,12},{12,8},{1,5},{5,1},{9,13},{13,9},{2,6},{6,2},{1... | collective-permute-start | bytes 12296 | tf_op jit(solution)/shard_map/ppermute | solution.py:223
  43.8 11.8 %collective-permute-start = (bf16[16,1024]{1,0:T(8,128)(2,1)S(1)}, bf16[16,1024]{1,0:T(8,128)(2,1)S(1)}, u32[]{:S(2)}, u32[]{:S(2)}) collective-permute-start(bf16[16,1024]{1,0:T(8,128)(2,1)S(1)} %get-tuple-element.32), channel_id=1, source_target_pairs={{0,3},{1,2},{2,1},{3,0},{4,7},{5,6},{6,5},{7,4},{8,11},{9,10},{10,... | collective-permute-start | bytes 98312 | tf_op jit(solution)/shard_map/ppermute | solution.py:223
  49.3 3.7 %collective-permute-start.9 = (f32[8,128]{1,0:T(8,128)S(1)}, f32[8,128]{1,0:T(8,128)S(1)}, u32[]{:S(2)}, u32[]{:S(2)}) collective-permute-start(f32[8,128]{1,0:T(8,128)S(1)} %get-tuple-element.49), channel_id=1, source_target_pairs={{0,8},{4,12},{8,0},{12,4},{1,9},{5,13},{9,1},{13,5},{2,10},{6,14},... | collective-permute-start | bytes 12296 | tf_op jit(solution)/shard_map/ppermute | solution.py:223
  51.8 3.1 %collective-permute-start.10 = (f32[8,128]{1,0:T(8,128)S(1)}, f32[8,128]{1,0:T(8,128)S(1)}, u32[]{:S(2)}, u32[]{:S(2)}) collective-permute-start(f32[8,128]{1,0:T(8,128)S(1)} %get-tuple-element.51), channel_id=1, source_target_pairs={{0,12},{4,8},{8,4},{12,0},{1,13},{5,9},{9,5},{13,1},{2,14},{6,10},... | collective-permute-start | bytes 12296 | tf_op jit(solution)/shard_map/ppermute | solution.py:223
  51.9 6.4 %collective-permute-start.11 = (f32[8,128]{1,0:T(8,128)S(1)}, f32[8,128]{1,0:T(8,128)S(1)}, u32[]{:S(2)}, u32[]{:S(2)}) collective-permute-start(f32[8,128]{1,0:T(8,128)S(1)} %get-tuple-element.56), channel_id=1, source_target_pairs={{0,2},{1,3},{2,0},{3,1},{4,6},{5,7},{6,4},{7,5},{8,10},{9,11},{10,... | collective-permute-start | bytes 12296 | tf_op jit(solution)/shard_map/ppermute | solution.py:223
  52.9 5.4 %collective-permute-start.12 = (f32[8,128]{1,0:T(8,128)S(1)}, f32[8,128]{1,0:T(8,128)S(1)}, u32[]{:S(2)}, u32[]{:S(2)}) collective-permute-start(f32[8,128]{1,0:T(8,128)S(1)} %get-tuple-element.57), channel_id=1, source_target_pairs={{0,1},{1,0},{2,3},{3,2},{4,5},{5,4},{6,7},{7,6},{8,9},{9,8},{10,11... | collective-permute-start | bytes 12296 | tf_op jit(solution)/shard_map/ppermute | solution.py:223
  56.1 5.5 %collective-permute-start.13 = (f32[8,128]{1,0:T(8,128)S(1)}, f32[8,128]{1,0:T(8,128)S(1)}, u32[]{:S(2)}, u32[]{:S(2)}) collective-permute-start(f32[8,128]{1,0:T(8,128)S(1)} %get-tuple-element.58), channel_id=1, source_target_pairs={{0,3},{1,2},{2,1},{3,0},{4,7},{5,6},{6,5},{7,4},{8,11},{9,10},{10,... | collective-permute-start | bytes 12296 | tf_op jit(solution)/shard_map/ppermute | solution.py:223

commit v23 on v19

--- a/solution.py
+++ b/solution.py
@@ -204,8 +204,8 @@
 
 
 def plan_slots(sizes):
-    slots = [("blk", 1, 0, BLOCK), ("sub", 2, 0, BLOCK), ("sub", 1, 0, BLOCK)]
-    slots += [("blk", k, 0, BLOCK) for k in range(2, sizes["blk"])]
+    slots = [("blk", 1, 0, BLOCK), ("sub", 2, 0, BLOCK), ("blk", 2, 0, BLOCK), ("sub", 1, 0, BLOCK)]
+    slots += [("blk", k, 0, BLOCK) for k in range(3, sizes["blk"])]
     for k in range(3, sizes["sub"]):
         slots += [("sub", k, 0, FIRST_CUT), ("sub", k, FIRST_CUT, BLOCK - FIRST_CUT)]
     return slots

time: 57.1 us -> 57.2 us (level); the launches traced: 56 us -> 56.8 us
  waiting for transfers between devices: 22.4 us -> 26.7 us
  starting transfers between devices: 21.4 us -> 17.9 us
    ppermute x13, waiting for transfers between devices: 22.4 us -> 26.7 us  [send(): return lax.ppermute(array, slot[0], pairs(slot[1], sizes[slot[0]]))]
    ppermute x13, starting transfers between devices: 21.4 us -> 17.9 us  [send(): return lax.ppermute(array, slot[0], pairs(slot[1], sizes[slot[0]]))]
  transfers between devices with their start and end apart: 13 -> 13, of which waited for: 4 -> 5; matrix products, arithmetic and copies ran while one was open for 0% -> 0% of each run, Pallas kernels for 16% -> 16%
where the time goes in v23:
time: 57.2 us; the launch traced here: 56.8 us
  waiting for transfers between devices  26.7 us (47%)
  starting transfers between devices  17.9 us (31%)
  Pallas kernels  11.5 us (20%)
  other arithmetic  0.6 us (1%)
    ppermute x13, waiting for transfers between devices, send(): return lax.ppermute(array, slot[0], pairs(slot[1], sizes[slot[0]]))  26.7 us
    ppermute x13, starting transfers between devices, send(): return lax.ppermute(array, slot[0], pairs(slot[1], sizes[slot[0]]))  17.9 us
    pallas_call x7, Pallas kernels, work(): pl.pallas_call(functools.partial(slot_kernel, place, *slot[2:], [one for...  6.29 us
    pallas_call x1, Pallas kernels, first_rows(): pl.pallas_call(functools.partial(first_kernel, slots), out_shape=[jax.Sha...  2.6 us
    pallas_call x1, Pallas kernels, prepare(): pl.pallas_call(functools.partial(prepare_kernel, slots), out_shape=[jax.S...  1.77 us
  transfers between devices with their start and end apart: 13, of which 5 were waited for; matrix products, arithmetic and copies ran while one was open for 0% of the time, Pallas kernels for 16%

profile of v23, /device:TPU:0, one launch (start us, length us, event | category | flops | bytes accessed | tf_op | source)
XLA Modules:
  0.0 56.8 jit_solution(14854058688051237697)
XLA Ops:
  0.0 0.0 copy-start
  0.0 0.0 copy-start.2
  0.0 0.0 copy-start.1
  0.0 0.0 copy-start.3
  0.0 0.0 copy-start.4
  0.0 2.6 %shard_map.57 = (bf16[256,1024]{1,0:T(8,128)(2,1)}, bf16[256,1024]{1,0:T(8,128)(2,1)}) custom-call(s32[1,4]{1,0:T(1,128)} %pick_blk.5, s32[4,4]{1,0:T(4,128)} %pick_sub.5, bf16[1024,1024]{1,0:T(8,128)(2,1)} %embeds.5), custom_call_target="tpu_custom_call" | custom-call | tf_op jit(solution)/shard_map/pallas_call | solution.py:81
  2.6 0.5 collective-permute-start.6
  3.2 3.7 %collective-permute-start.5 = (bf16[256,1024]{1,0:T(8,128)(2,1)}, bf16[256,1024]{1,0:T(8,128)(2,1)S(1)}, u32[]{:S(2)}, u32[]{:S(2)}) collective-permute-start(bf16[256,1024]{1,0:T(8,128)(2,1)} %get-tuple-element.37), channel_id=1, source_target_pairs={{0,2},{1,3},{2,0},{3,1},{4,6},{5,7},{6,4},{7,5},{8,10},{9,11},{10,... | collective-permute-start | bytes 1572872 | tf_op jit(solution)/shard_map/ppermute | solution.py:223
  6.8 0.0 copy-done
  6.8 0.0 copy-done.2
  6.8 0.0 copy-done.1
  6.8 0.8 %shard_map.55 = (bf16[256,1024]{1,0:T(8,128)(2,1)S(1)}, bf16[256,1024]{1,0:T(8,128)(2,1)S(1)}, bf16[256,1024]{1,0:T(8,128)(2,1)S(1)}, bf16[128,1024]{1,0:T(8,128)(2,1)S(1)}, bf16[128,1024]{1,0:T(8,128)(2,1)S(1)}) custom-call(s32[1,4]{1,0:T(1,128)S(1)} %copy-done.2, s32[4,4]{1,0:T(4,128)S(1)} %copy-done.1, bf16[1024,1024]{1,0:T(8,128)(2,1)S(1)} %copy-done), custom_call_target="tpu_custom_call" | custom-call | tf_op jit(solution)/shard_map/pallas_call | solution.py:118
  7.7 1.6 %collective-permute-start.4 = (bf16[256,1024]{1,0:T(8,128)(2,1)S(1)}, bf16[256,1024]{1,0:T(8,128)(2,1)S(1)}, u32[]{:S(2)}, u32[]{:S(2)}) collective-permute-start(bf16[256,1024]{1,0:T(8,128)(2,1)S(1)} %get-tuple-element.36), channel_id=1, source_target_pairs={{0,8},{4,12},{8,0},{12,4},{1,9},{5,13},{9,1},{13,5},{2,10},{6,14},... | collective-permute-start | bytes 1572872 | tf_op jit(solution)/shard_map/ppermute | solution.py:223
  9.2 1.6 %collective-permute-start.3 = (bf16[256,1024]{1,0:T(8,128)(2,1)S(1)}, bf16[256,1024]{1,0:T(8,128)(2,1)S(1)}, u32[]{:S(2)}, u32[]{:S(2)}) collective-permute-start(bf16[256,1024]{1,0:T(8,128)(2,1)S(1)} %get-tuple-element.35), channel_id=1, source_target_pairs={{0,1},{1,0},{2,3},{3,2},{4,5},{5,4},{6,7},{7,6},{8,9},{9,8},{10,11... | collective-permute-start | bytes 1572872 | tf_op jit(solution)/shard_map/ppermute | solution.py:223
  10.8 0.0 collective-permute-start.2
  10.8 0.0 collective-permute-done.6.arrived
  10.8 0.2 collective-permute-start.1
  11.0 20.1 %collective-permute-done.5.arrived = bf16[256,1024]{1,0:T(8,128)(2,1)S(1)} collective-permute-done((bf16[256,1024]{1,0:T(8,128)(2,1)}, bf16[256,1024]{1,0:T(8,128)(2,1)S(1)}, u32[]{:S(2)}, u32[]{:S(2)}) %collective-permute-start.5) | collective-permute-done | bytes 524320 | tf_op jit(solution)/shard_map/ppermute | solution.py:223
  31.1 3.8 %collective-permute-start = (bf16[128,1024]{1,0:T(8,128)(2,1)S(1)}, bf16[128,1024]{1,0:T(8,128)(2,1)S(1)}, u32[]{:S(2)}, u32[]{:S(2)}) collective-permute-start(bf16[128,1024]{1,0:T(8,128)(2,1)S(1)} %get-tuple-element.29), channel_id=1, source_target_pairs={{0,3},{1,2},{2,1},{3,0},{4,7},{5,6},{6,5},{7,4},{8,11},{9,10},{10,... | collective-permute-start | bytes 786440 | tf_op jit(solution)/shard_map/ppermute | solution.py:223
  34.9 0.0 copy-done.3
  34.9 0.0 copy-done.4
  34.9 1.8 %shard_map.56 = (bf16[1024,1024]{1,0:T(8,128)(2,1)S(1)}, f32[7,4,128]{2,1,0:T(4,128)S(1)}, f32[7,8,128]{2,1,0:T(8,128)S(1)}) custom-call(s32[1,4]{1,0:T(1,128)S(1)} %copy-done.2, s32[4,4]{1,0:T(4,128)S(1)} %copy-done.1, s32[1,16]{1,0:T(1,128)S(1)} %copy-done.3, s32[1,16]{1,0:T(1,128)S(1)} %copy-done.4, bf16[1024,1024]{1,0:T(8,128)(2,1)S(1)} %copy-done), custom_call_target="tpu_custom_call" | custom-call | tf_op jit(solution)/shard_map/pallas_call | solution.py:150
  36.7 1.0 %shard_map.58 = (f32[8,128]{1,0:T(8,128)S(1)}, f32[8,128]{1,0:T(8,128)S(1)}) custom-call(bf16[256,1024]{1,0:T(8,128)(2,1)S(1)} %collective-permute-done.6.arrived, bf16[1024,1024]{1,0:T(8,128)(2,1)S(1)} %get-tuple-element.30.units, f32[7,4,128]{2,1,0:T(4,128)S(1)} %get-tuple-element.31.live, f32[7,8,128]{2,1,0:T(8,128)S(1)} %get-tuple-element.32.mine, ...), custom_call_target="tpu_custom_call" | custom-call | tf_op jit(solution)/shard_map/pallas_call | solution.py:193
  37.7 0.0 collective-permute-done.4.arrived
  37.7 0.1 collective-permute-start.7
  37.8 1.0 %shard_map.59 = (f32[8,128]{1,0:T(8,128)S(1)}, f32[8,128]{1,0:T(8,128)S(1)}) custom-call(bf16[256,1024]{1,0:T(8,128)(2,1)S(1)} %collective-permute-done.5.arrived, bf16[1024,1024]{1,0:T(8,128)(2,1)S(1)} %get-tuple-element.30.units, f32[7,4,128]{2,1,0:T(4,128)S(1)} %get-tuple-element.31.live, f32[7,8,128]{2,1,0:T(8,128)S(1)} %get-tuple-element.32.mine, ...), custom_call_target="tpu_custom_call" | custom-call | tf_op jit(solution)/shard_map/pallas_call | solution.py:193
  38.8 0.2 collective-permute-done.7.rest_0_
  38.9 1.0 %shard_map.60 = (f32[8,128]{1,0:T(8,128)S(1)}, f32[8,128]{1,0:T(8,128)S(1)}) custom-call(bf16[256,1024]{1,0:T(8,128)(2,1)S(1)} %collective-permute-done.4.arrived, bf16[1024,1024]{1,0:T(8,128)(2,1)S(1)} %get-tuple-element.30.units, f32[7,4,128]{2,1,0:T(4,128)S(1)} %get-tuple-element.31.live, f32[7,8,128]{2,1,0:T(8,128)S(1)} %get-tuple-element.32.mine, ...), custom_call_target="tpu_custom_call" | custom-call | tf_op jit(solution)/shard_map/pallas_call | solution.py:193
  39.9 1.6 %collective-permute-start.8 = (f32[8,128]{1,0:T(8,128)S(1)}, f32[8,128]{1,0:T(8,128)S(1)}, u32[]{:S(2)}, u32[]{:S(2)}) collective-permute-start(f32[8,128]{1,0:T(8,128)S(1)} %get-tuple-element.44), channel_id=1, source_target_pairs={{0,8},{4,12},{8,0},{12,4},{1,9},{5,13},{9,1},{13,5},{2,10},{6,14},... | collective-permute-start | bytes 12296 | tf_op jit(solution)/shard_map/ppermute | solution.py:223
  41.5 2.7 %collective-permute-done.3.arrived = bf16[256,1024]{1,0:T(8,128)(2,1)S(1)} collective-permute-done((bf16[256,1024]{1,0:T(8,128)(2,1)S(1)}, bf16[256,1024]{1,0:T(8,128)(2,1)S(1)}, u32[]{:S(2)}, u32[]{:S(2)}) %collective-permute-start.3) | collective-permute-done | bytes 524320 | tf_op jit(solution)/shard_map/ppermute | solution.py:223
  44.2 1.0 %shard_map.61 = (f32[8,128]{1,0:T(8,128)S(1)}, f32[8,128]{1,0:T(8,128)S(1)}) custom-call(bf16[256,1024]{1,0:T(8,128)(2,1)S(1)} %collective-permute-done.3.arrived, bf16[1024,1024]{1,0:T(8,128)(2,1)S(1)} %get-tuple-element.30.units, f32[7,4,128]{2,1,0:T(4,128)S(1)} %get-tuple-element.31.live, f32[7,8,128]{2,1,0:T(8,128)S(1)} %get-tuple-element.32.mine, ...), custom_call_target="tpu_custom_call" | custom-call | tf_op jit(solution)/shard_map/pallas_call | solution.py:193
  45.2 0.0 collective-permute-done.2.arrived
  45.2 0.0 collective-permute-done.8.rest_0_
  45.2 1.0 %shard_map.62 = (f32[8,128]{1,0:T(8,128)S(1)}, f32[8,128]{1,0:T(8,128)S(1)}) custom-call(bf16[256,1024]{1,0:T(8,128)(2,1)S(1)} %collective-permute-done.2.arrived, bf16[1024,1024]{1,0:T(8,128)(2,1)S(1)} %get-tuple-element.30.units, f32[7,4,128]{2,1,0:T(4,128)S(1)} %get-tuple-element.31.live, f32[7,8,128]{2,1,0:T(8,128)S(1)} %get-tuple-element.32.mine, ...), custom_call_target="tpu_custom_call" | custom-call | tf_op jit(solution)/shard_map/pallas_call | solution.py:193
  46.2 0.1 collective-permute-start.9
  46.3 0.6 %collective-permute-start.10 = (f32[8,128]{1,0:T(8,128)S(1)}, f32[8,128]{1,0:T(8,128)S(1)}, u32[]{:S(2)}, u32[]{:S(2)}) collective-permute-start(f32[8,128]{1,0:T(8,128)S(1)} %get-tuple-element.50), channel_id=1, source_target_pairs={{0,2},{1,3},{2,0},{3,1},{4,6},{5,7},{6,4},{7,5},{8,10},{9,11},{10,... | collective-permute-start | bytes 12296 | tf_op jit(solution)/shard_map/ppermute | solution.py:223
  46.9 2.5 %collective-permute-start.11 = (f32[8,128]{1,0:T(8,128)S(1)}, f32[8,128]{1,0:T(8,128)S(1)}, u32[]{:S(2)}, u32[]{:S(2)}) collective-permute-start(f32[8,128]{1,0:T(8,128)S(1)} %get-tuple-element.51), channel_id=1, source_target_pairs={{0,1},{1,0},{2,3},{3,2},{4,5},{5,4},{6,7},{7,6},{8,9},{9,8},{10,11... | collective-permute-start | bytes 12296 | tf_op jit(solution)/shard_map/ppermute | solution.py:223
  49.4 0.0 collective-permute-done.1.arrived
  49.4 0.7 %shard_map.63 = (f32[8,128]{1,0:T(8,128)S(1)}, f32[8,128]{1,0:T(8,128)S(1)}) custom-call(bf16[128,1024]{1,0:T(8,128)(2,1)S(1)} %collective-permute-done.1.arrived, bf16[1024,1024]{1,0:T(8,128)(2,1)S(1)} %get-tuple-element.30.units, f32[7,4,128]{2,1,0:T(4,128)S(1)} %get-tuple-element.31.live, f32[7,8,128]{2,1,0:T(8,128)S(1)} %get-tuple-element.32.mine, ...), custom_call_target="tpu_custom_call" | custom-call | tf_op jit(solution)/shard_map/pallas_call | solution.py:193
  50.1 0.0 collective-permute-done.arrived
  50.1 0.0 collective-permute-done.9.rest_0_
  50.1 0.7 %shard_map.64 = (f32[8,128]{1,0:T(8,128)S(1)}, f32[8,128]{1,0:T(8,128)S(1)}) custom-call(bf16[128,1024]{1,0:T(8,128)(2,1)S(1)} %collective-permute-done.arrived, bf16[1024,1024]{1,0:T(8,128)(2,1)S(1)} %get-tuple-element.30.units, f32[7,4,128]{2,1,0:T(4,128)S(1)} %get-tuple-element.31.live, f32[7,8,128]{2,1,0:T(8,128)S(1)} %get-tuple-element.32.mine, ...), custom_call_target="tpu_custom_call" | custom-call | tf_op jit(solution)/shard_map/pallas_call | solution.py:193
  50.7 1.7 %collective-permute-start.12 = (f32[8,128]{1,0:T(8,128)S(1)}, f32[8,128]{1,0:T(8,128)S(1)}, u32[]{:S(2)}, u32[]{:S(2)}) collective-permute-start(f32[8,128]{1,0:T(8,128)S(1)} %get-tuple-element.52), channel_id=1, source_target_pairs={{0,3},{1,2},{2,1},{3,0},{4,7},{5,6},{6,5},{7,4},{8,11},{9,10},{10,... | collective-permute-start | bytes 12296 | tf_op jit(solution)/shard_map/ppermute | solution.py:223
  52.5 1.0 %collective-permute-done.10 = f32[8,128]{1,0:T(8,128)S(1)} collective-permute-done((f32[8,128]{1,0:T(8,128)S(1)}, f32[8,128]{1,0:T(8,128)S(1)}, u32[]{:S(2)}, u32[]{:S(2)}) %collective-permute-start.10) | collective-permute-done | bytes 4128 | tf_op jit(solution)/shard_map/ppermute | solution.py:223
  53.5 0.0 collective-permute-done.11
  53.5 2.7 %collective-permute-done.12 = f32[8,128]{1,0:T(8,128)S(1)} collective-permute-done((f32[8,128]{1,0:T(8,128)S(1)}, f32[8,128]{1,0:T(8,128)S(1)}, u32[]{:S(2)}, u32[]{:S(2)}) %collective-permute-start.12) | collective-permute-done | bytes 4128 | tf_op jit(solution)/shard_map/ppermute | solution.py:223
  56.2 0.6 %fusion.2 = f32[1024]{0:T(1024)} fusion(f32[8,128]{1,0:T(8,128)S(1)} %collective-permute-done.12, f32[8,128]{1,0:T(8,128)S(1)} %collective-permute-done.11, f32[8,128]{1,0:T(8,128)S(1)} %get-tuple-element.49, f32[8,128]{1,0:T(8,128)S(1)} %collective-permute-done.10, f32[7,8,128]{2,1,0:T(8,128)S(1)} %get-tuple-element.32.mine), kind=kLoop, calls=%fused_computation.3 | loop fusion | flops 7168 | bytes 32768 | tf_op jit(solution)/shard_map/reshape | solution.py:249
  (1 shorter events, 0.0 us)
Async XLA Ops:
  0.0 6.8 %copy-start = (bf16[1024,1024]{1,0:T(8,128)(2,1)S(1)}, bf16[1024,1024]{1,0:T(8,128)(2,1)}, u32[]{:S(2)}) copy-start(bf16[1024,1024]{1,0:T(8,128)(2,1)} %embeds.5) | copy-start | bytes 6291460
  0.0 6.8 %copy-start.2 = (s32[1,4]{1,0:T(1,128)S(1)}, s32[1,4]{1,0:T(1,128)}, u32[]{:S(2)}) copy-start(s32[1,4]{1,0:T(1,128)} %pick_blk.5) | copy-start | bytes 52
  0.0 6.8 %copy-start.1 = (s32[4,4]{1,0:T(4,128)S(1)}, s32[4,4]{1,0:T(4,128)}, u32[]{:S(2)}) copy-start(s32[4,4]{1,0:T(4,128)} %pick_sub.5) | copy-start | bytes 196
  0.0 34.9 %copy-start.3 = (s32[1,16]{1,0:T(1,128)S(1)}, s32[1,16]{1,0:T(1,128)}, u32[]{:S(2)}) copy-start(s32[1,16]{1,0:T(1,128)} %mask_blk.1) | copy-start | bytes 196
  0.0 34.9 %copy-start.4 = (s32[1,16]{1,0:T(1,128)S(1)}, s32[1,16]{1,0:T(1,128)}, u32[]{:S(2)}) copy-start(s32[1,16]{1,0:T(1,128)} %mask_sub.1) | copy-start | bytes 196
  2.6 8.2 %collective-permute-start.6 = (bf16[256,1024]{1,0:T(8,128)(2,1)}, bf16[256,1024]{1,0:T(8,128)(2,1)S(1)}, u32[]{:S(2)}, u32[]{:S(2)}) collective-permute-start(bf16[256,1024]{1,0:T(8,128)(2,1)} %get-tuple-element.38), channel_id=1, source_target_pairs={{0,4},{4,0},{8,12},{12,8},{1,5},{5,1},{9,13},{13,9},{2,6},{6,2},{1... | collective-permute-start | bytes 1572872 | tf_op jit(solution)/shard_map/ppermute | solution.py:223
  3.2 27.9 %collective-permute-start.5 = (bf16[256,1024]{1,0:T(8,128)(2,1)}, bf16[256,1024]{1,0:T(8,128)(2,1)S(1)}, u32[]{:S(2)}, u32[]{:S(2)}) collective-permute-start(bf16[256,1024]{1,0:T(8,128)(2,1)} %get-tuple-element.37), channel_id=1, source_target_pairs={{0,2},{1,3},{2,0},{3,1},{4,6},{5,7},{6,4},{7,5},{8,10},{9,11},{10,... | collective-permute-start | bytes 1572872 | tf_op jit(solution)/shard_map/ppermute | solution.py:223
  7.7 30.0 %collective-permute-start.4 = (bf16[256,1024]{1,0:T(8,128)(2,1)S(1)}, bf16[256,1024]{1,0:T(8,128)(2,1)S(1)}, u32[]{:S(2)}, u32[]{:S(2)}) collective-permute-start(bf16[256,1024]{1,0:T(8,128)(2,1)S(1)} %get-tuple-element.36), channel_id=1, source_target_pairs={{0,8},{4,12},{8,0},{12,4},{1,9},{5,13},{9,1},{13,5},{2,10},{6,14},... | collective-permute-start | bytes 1572872 | tf_op jit(solution)/shard_map/ppermute | solution.py:223
  9.2 35.0 %collective-permute-start.3 = (bf16[256,1024]{1,0:T(8,128)(2,1)S(1)}, bf16[256,1024]{1,0:T(8,128)(2,1)S(1)}, u32[]{:S(2)}, u32[]{:S(2)}) collective-permute-start(bf16[256,1024]{1,0:T(8,128)(2,1)S(1)} %get-tuple-element.35), channel_id=1, source_target_pairs={{0,1},{1,0},{2,3},{3,2},{4,5},{5,4},{6,7},{7,6},{8,9},{9,8},{10,11... | collective-permute-start | bytes 1572872 | tf_op jit(solution)/shard_map/ppermute | solution.py:223
  10.8 34.4 %collective-permute-start.2 = (bf16[256,1024]{1,0:T(8,128)(2,1)S(1)}, bf16[256,1024]{1,0:T(8,128)(2,1)S(1)}, u32[]{:S(2)}, u32[]{:S(2)}) collective-permute-start(bf16[256,1024]{1,0:T(8,128)(2,1)S(1)} %get-tuple-element.34), channel_id=1, source_target_pairs={{0,12},{4,8},{8,4},{12,0},{1,13},{5,9},{9,5},{13,1},{2,14},{6,10},... | collective-permute-start | bytes 1572872 | tf_op jit(solution)/shard_map/ppermute | solution.py:223
  10.8 38.6 %collective-permute-start.1 = (bf16[128,1024]{1,0:T(8,128)(2,1)S(1)}, bf16[128,1024]{1,0:T(8,128)(2,1)S(1)}, u32[]{:S(2)}, u32[]{:S(2)}) collective-permute-start(bf16[128,1024]{1,0:T(8,128)(2,1)S(1)} %get-tuple-element.33), channel_id=1, source_target_pairs={{0,3},{1,2},{2,1},{3,0},{4,7},{5,6},{6,5},{7,4},{8,11},{9,10},{10,... | collective-permute-start | bytes 786440 | tf_op jit(solution)/shard_map/ppermute | solution.py:223
  31.1 19.0 %collective-permute-start = (bf16[128,1024]{1,0:T(8,128)(2,1)S(1)}, bf16[128,1024]{1,0:T(8,128)(2,1)S(1)}, u32[]{:S(2)}, u32[]{:S(2)}) collective-permute-start(bf16[128,1024]{1,0:T(8,128)(2,1)S(1)} %get-tuple-element.29), channel_id=1, source_target_pairs={{0,3},{1,2},{2,1},{3,0},{4,7},{5,6},{6,5},{7,4},{8,11},{9,10},{10,... | collective-permute-start | bytes 786440 | tf_op jit(solution)/shard_map/ppermute | solution.py:223
  37.7 1.2 %collective-permute-start.7 = (f32[8,128]{1,0:T(8,128)S(1)}, f32[8,128]{1,0:T(8,128)S(1)}, u32[]{:S(2)}, u32[]{:S(2)}) collective-permute-start(f32[8,128]{1,0:T(8,128)S(1)} %get-tuple-element.41), channel_id=1, source_target_pairs={{0,4},{4,0},{8,12},{12,8},{1,5},{5,1},{9,13},{13,9},{2,6},{6,2},{1... | collective-permute-start | bytes 12296 | tf_op jit(solution)/shard_map/ppermute | solution.py:223
  39.9 5.3 %collective-permute-start.8 = (f32[8,128]{1,0:T(8,128)S(1)}, f32[8,128]{1,0:T(8,128)S(1)}, u32[]{:S(2)}, u32[]{:S(2)}) collective-permute-start(f32[8,128]{1,0:T(8,128)S(1)} %get-tuple-element.44), channel_id=1, source_target_pairs={{0,8},{4,12},{8,0},{12,4},{1,9},{5,13},{9,1},{13,5},{2,10},{6,14},... | collective-permute-start | bytes 12296 | tf_op jit(solution)/shard_map/ppermute | solution.py:223
  46.2 3.8 %collective-permute-start.9 = (f32[8,128]{1,0:T(8,128)S(1)}, f32[8,128]{1,0:T(8,128)S(1)}, u32[]{:S(2)}, u32[]{:S(2)}) collective-permute-start(f32[8,128]{1,0:T(8,128)S(1)} %get-tuple-element.47), channel_id=1, source_target_pairs={{0,12},{4,8},{8,4},{12,0},{1,13},{5,9},{9,5},{13,1},{2,14},{6,10},... | collective-permute-start | bytes 12296 | tf_op jit(solution)/shard_map/ppermute | solution.py:223
  46.3 7.2 %collective-permute-start.10 = (f32[8,128]{1,0:T(8,128)S(1)}, f32[8,128]{1,0:T(8,128)S(1)}, u32[]{:S(2)}, u32[]{:S(2)}) collective-permute-start(f32[8,128]{1,0:T(8,128)S(1)} %get-tuple-element.50), channel_id=1, source_target_pairs={{0,2},{1,3},{2,0},{3,1},{4,6},{5,7},{6,4},{7,5},{8,10},{9,11},{10,... | collective-permute-start | bytes 12296 | tf_op jit(solution)/shard_map/ppermute | solution.py:223
  46.9 6.6 %collective-permute-start.11 = (f32[8,128]{1,0:T(8,128)S(1)}, f32[8,128]{1,0:T(8,128)S(1)}, u32[]{:S(2)}, u32[]{:S(2)}) collective-permute-start(f32[8,128]{1,0:T(8,128)S(1)} %get-tuple-element.51), channel_id=1, source_target_pairs={{0,1},{1,0},{2,3},{3,2},{4,5},{5,4},{6,7},{7,6},{8,9},{9,8},{10,11... | collective-permute-start | bytes 12296 | tf_op jit(solution)/shard_map/ppermute | solution.py:223
  50.7 5.5 %collective-permute-start.12 = (f32[8,128]{1,0:T(8,128)S(1)}, f32[8,128]{1,0:T(8,128)S(1)}, u32[]{:S(2)}, u32[]{:S(2)}) collective-permute-start(f32[8,128]{1,0:T(8,128)S(1)} %get-tuple-element.52), channel_id=1, source_target_pairs={{0,3},{1,2},{2,1},{3,0},{4,7},{5,6},{6,5},{7,4},{8,11},{9,10},{10,... | collective-permute-start | bytes 12296 | tf_op jit(solution)/shard_map/ppermute | solution.py:223

commit v24 on v23

--- a/solution.py
+++ b/solution.py
@@ -200,15 +200,10 @@
 
 
 BEHIND = 2
-FIRST_CUT = 128
-
-
 def plan_slots(sizes):
     slots = [("blk", 1, 0, BLOCK), ("sub", 2, 0, BLOCK), ("blk", 2, 0, BLOCK), ("sub", 1, 0, BLOCK)]
     slots += [("blk", k, 0, BLOCK) for k in range(3, sizes["blk"])]
-    for k in range(3, sizes["sub"]):
-        slots += [("sub", k, 0, FIRST_CUT), ("sub", k, FIRST_CUT, BLOCK - FIRST_CUT)]
-    return slots
+    return slots + [("sub", k, 0, BLOCK) for k in range(3, sizes["sub"])]
 
 
 AT_ONCE = 2

time: 57.2 us -> 57.5 us (level); the launches traced: 56.8 us -> 56.4 us
  waiting for transfers between devices: 26.7 us -> 29.6 us
  starting transfers between devices: 17.9 us -> 15 us
    ppermute x13 -> x12, starting transfers between devices: 17.9 us -> 15 us  [send(): return lax.ppermute(array, slot[0], pairs(slot[1], sizes[slot[0]]))]
    ppermute x13 -> x12, waiting for transfers between devices: 26.7 us -> 29.6 us  [send(): return lax.ppermute(array, slot[0], pairs(slot[1], sizes[slot[0]]))]
    pallas_call x7 -> x6, Pallas kernels: 6.29 us -> 5.98 us  [work(): pl.pallas_call(functools.partial(slot_kernel, place, *slot[2:], [one for...]
  transfers between devices with their start and end apart: 13 -> 12, of which waited for: 5 -> 5; matrix products, arithmetic and copies ran while one was open for 0% -> 0% of each run, Pallas kernels for 16% -> 15%
where the time goes in v24:
time: 57.5 us; the launch traced here: 56.4 us
  waiting for transfers between devices  29.6 us (51%)
  starting transfers between devices  15 us (26%)
  Pallas kernels  11.1 us (19%)
  other arithmetic  0.6 us (1%)
    ppermute x12, waiting for transfers between devices, send(): return lax.ppermute(array, slot[0], pairs(slot[1], sizes[slot[0]]))  29.6 us
    ppermute x12, starting transfers between devices, send(): return lax.ppermute(array, slot[0], pairs(slot[1], sizes[slot[0]]))  15 us
    pallas_call x6, Pallas kernels, work(): pl.pallas_call(functools.partial(slot_kernel, place, *slot[2:], [one for...  5.98 us
    pallas_call x1, Pallas kernels, first_rows(): pl.pallas_call(functools.partial(first_kernel, slots), out_shape=[jax.Sha...  2.59 us
    pallas_call x1, Pallas kernels, prepare(): pl.pallas_call(functools.partial(prepare_kernel, slots), out_shape=[jax.S...  1.77 us
  transfers between devices with their start and end apart: 12, of which 5 were waited for; matrix products, arithmetic and copies ran while one was open for 0% of the time, Pallas kernels for 15%

profile of v24, /device:TPU:0, one launch (start us, length us, event | category | flops | bytes accessed | tf_op | source)
XLA Modules:
  0.0 56.4 jit_solution(13559696039235552621)
XLA Ops:
  0.0 0.0 copy-start
  0.0 0.0 copy-start.2
  0.0 0.0 copy-start.1
  0.0 0.0 copy-start.3
  0.0 0.0 copy-start.4
  0.0 2.6 %shard_map.57 = (bf16[256,1024]{1,0:T(8,128)(2,1)}, bf16[256,1024]{1,0:T(8,128)(2,1)}) custom-call(s32[1,4]{1,0:T(1,128)} %pick_blk.5, s32[4,4]{1,0:T(4,128)} %pick_sub.5, bf16[1024,1024]{1,0:T(8,128)(2,1)} %embeds.5), custom_call_target="tpu_custom_call" | custom-call | tf_op jit(solution)/shard_map/pallas_call | solution.py:81
  2.6 0.5 collective-permute-start.5
  3.1 3.7 %collective-permute-start.4 = (bf16[256,1024]{1,0:T(8,128)(2,1)}, bf16[256,1024]{1,0:T(8,128)(2,1)S(1)}, u32[]{:S(2)}, u32[]{:S(2)}) collective-permute-start(bf16[256,1024]{1,0:T(8,128)(2,1)} %get-tuple-element.33), channel_id=1, source_target_pairs={{0,2},{1,3},{2,0},{3,1},{4,6},{5,7},{6,4},{7,5},{8,10},{9,11},{10,... | collective-permute-start | bytes 1572872 | tf_op jit(solution)/shard_map/ppermute | solution.py:218
  6.8 0.0 copy-done
  6.8 0.0 copy-done.2
  6.8 0.0 copy-done.1
  6.8 0.8 %shard_map.55 = (bf16[256,1024]{1,0:T(8,128)(2,1)S(1)}, bf16[256,1024]{1,0:T(8,128)(2,1)S(1)}, bf16[256,1024]{1,0:T(8,128)(2,1)S(1)}, bf16[256,1024]{1,0:T(8,128)(2,1)S(1)}) custom-call(s32[1,4]{1,0:T(1,128)S(1)} %copy-done.2, s32[4,4]{1,0:T(4,128)S(1)} %copy-done.1, bf16[1024,1024]{1,0:T(8,128)(2,1)S(1)} %copy-done), custom_call_target="tpu_custom_call" | custom-call | tf_op jit(solution)/shard_map/pallas_call | solution.py:118
  7.6 1.6 %collective-permute-start.3 = (bf16[256,1024]{1,0:T(8,128)(2,1)S(1)}, bf16[256,1024]{1,0:T(8,128)(2,1)S(1)}, u32[]{:S(2)}, u32[]{:S(2)}) collective-permute-start(bf16[256,1024]{1,0:T(8,128)(2,1)S(1)} %get-tuple-element.32), channel_id=1, source_target_pairs={{0,8},{4,12},{8,0},{12,4},{1,9},{5,13},{9,1},{13,5},{2,10},{6,14},... | collective-permute-start | bytes 1572872 | tf_op jit(solution)/shard_map/ppermute | solution.py:218
  9.2 1.6 %collective-permute-start.2 = (bf16[256,1024]{1,0:T(8,128)(2,1)S(1)}, bf16[256,1024]{1,0:T(8,128)(2,1)S(1)}, u32[]{:S(2)}, u32[]{:S(2)}) collective-permute-start(bf16[256,1024]{1,0:T(8,128)(2,1)S(1)} %get-tuple-element.31), channel_id=1, source_target_pairs={{0,1},{1,0},{2,3},{3,2},{4,5},{5,4},{6,7},{7,6},{8,9},{9,8},{10,11... | collective-permute-start | bytes 1572872 | tf_op jit(solution)/shard_map/ppermute | solution.py:218
  10.8 0.0 collective-permute-start.1
  10.8 0.0 collective-permute-done.5.arrived
  10.8 0.2 collective-permute-start
  11.0 0.0 copy-done.3
  11.0 0.0 copy-done.4
  11.0 1.8 %shard_map.56 = (bf16[1024,1024]{1,0:T(8,128)(2,1)S(1)}, f32[6,4,128]{2,1,0:T(4,128)S(1)}, f32[6,8,128]{2,1,0:T(8,128)S(1)}) custom-call(s32[1,4]{1,0:T(1,128)S(1)} %copy-done.2, s32[4,4]{1,0:T(4,128)S(1)} %copy-done.1, s32[1,16]{1,0:T(1,128)S(1)} %copy-done.3, s32[1,16]{1,0:T(1,128)S(1)} %copy-done.4, bf16[1024,1024]{1,0:T(8,128)(2,1)S(1)} %copy-done), custom_call_target="tpu_custom_call" | custom-call | tf_op jit(solution)/shard_map/pallas_call | solution.py:150
  12.8 1.0 %shard_map.58 = (f32[8,128]{1,0:T(8,128)S(1)}, f32[8,128]{1,0:T(8,128)S(1)}) custom-call(bf16[256,1024]{1,0:T(8,128)(2,1)S(1)} %collective-permute-done.5.arrived, bf16[1024,1024]{1,0:T(8,128)(2,1)S(1)} %get-tuple-element.27.units, f32[6,4,128]{2,1,0:T(4,128)S(1)} %get-tuple-element.28.live, f32[6,8,128]{2,1,0:T(8,128)S(1)} %get-tuple-element.29.mine, ...), custom_call_target="tpu_custom_call" | custom-call | tf_op jit(solution)/shard_map/pallas_call | solution.py:193
  13.8 17.3 %collective-permute-done.4.arrived = bf16[256,1024]{1,0:T(8,128)(2,1)S(1)} collective-permute-done((bf16[256,1024]{1,0:T(8,128)(2,1)}, bf16[256,1024]{1,0:T(8,128)(2,1)S(1)}, u32[]{:S(2)}, u32[]{:S(2)}) %collective-permute-start.4) | collective-permute-done | bytes 524320 | tf_op jit(solution)/shard_map/ppermute | solution.py:218
  31.1 0.0 collective-permute-start.6
  31.1 1.0 %shard_map.59 = (f32[8,128]{1,0:T(8,128)S(1)}, f32[8,128]{1,0:T(8,128)S(1)}) custom-call(bf16[256,1024]{1,0:T(8,128)(2,1)S(1)} %collective-permute-done.4.arrived, bf16[1024,1024]{1,0:T(8,128)(2,1)S(1)} %get-tuple-element.27.units, f32[6,4,128]{2,1,0:T(4,128)S(1)} %get-tuple-element.28.live, f32[6,8,128]{2,1,0:T(8,128)S(1)} %get-tuple-element.29.mine, ...), custom_call_target="tpu_custom_call" | custom-call | tf_op jit(solution)/shard_map/pallas_call | solution.py:193
  32.1 0.0 collective-permute-done.3.arrived
  32.1 0.2 collective-permute-done.6.rest_0_
  32.2 1.0 %shard_map.60 = (f32[8,128]{1,0:T(8,128)S(1)}, f32[8,128]{1,0:T(8,128)S(1)}) custom-call(bf16[256,1024]{1,0:T(8,128)(2,1)S(1)} %collective-permute-done.3.arrived, bf16[1024,1024]{1,0:T(8,128)(2,1)S(1)} %get-tuple-element.27.units, f32[6,4,128]{2,1,0:T(4,128)S(1)} %get-tuple-element.28.live, f32[6,8,128]{2,1,0:T(8,128)S(1)} %get-tuple-element.29.mine, ...), custom_call_target="tpu_custom_call" | custom-call | tf_op jit(solution)/shard_map/pallas_call | solution.py:193
  33.2 1.8 %collective-permute-start.7 = (f32[8,128]{1,0:T(8,128)S(1)}, f32[8,128]{1,0:T(8,128)S(1)}, u32[]{:S(2)}, u32[]{:S(2)}) collective-permute-start(f32[8,128]{1,0:T(8,128)S(1)} %get-tuple-element.40), channel_id=1, source_target_pairs={{0,8},{4,12},{8,0},{12,4},{1,9},{5,13},{9,1},{13,5},{2,10},{6,14},... | collective-permute-start | bytes 12296 | tf_op jit(solution)/shard_map/ppermute | solution.py:218
  35.1 9.1 %collective-permute-done.2.arrived = bf16[256,1024]{1,0:T(8,128)(2,1)S(1)} collective-permute-done((bf16[256,1024]{1,0:T(8,128)(2,1)S(1)}, bf16[256,1024]{1,0:T(8,128)(2,1)S(1)}, u32[]{:S(2)}, u32[]{:S(2)}) %collective-permute-start.2) | collective-permute-done | bytes 524320 | tf_op jit(solution)/shard_map/ppermute | solution.py:218
  44.2 1.0 %shard_map.61 = (f32[8,128]{1,0:T(8,128)S(1)}, f32[8,128]{1,0:T(8,128)S(1)}) custom-call(bf16[256,1024]{1,0:T(8,128)(2,1)S(1)} %collective-permute-done.2.arrived, bf16[1024,1024]{1,0:T(8,128)(2,1)S(1)} %get-tuple-element.27.units, f32[6,4,128]{2,1,0:T(4,128)S(1)} %get-tuple-element.28.live, f32[6,8,128]{2,1,0:T(8,128)S(1)} %get-tuple-element.29.mine, ...), custom_call_target="tpu_custom_call" | custom-call | tf_op jit(solution)/shard_map/pallas_call | solution.py:193
  45.2 0.0 collective-permute-done.1.arrived
  45.2 0.0 collective-permute-done.7.rest_0_
  45.2 1.0 %shard_map.62 = (f32[8,128]{1,0:T(8,128)S(1)}, f32[8,128]{1,0:T(8,128)S(1)}) custom-call(bf16[256,1024]{1,0:T(8,128)(2,1)S(1)} %collective-permute-done.1.arrived, bf16[1024,1024]{1,0:T(8,128)(2,1)S(1)} %get-tuple-element.27.units, f32[6,4,128]{2,1,0:T(4,128)S(1)} %get-tuple-element.28.live, f32[6,8,128]{2,1,0:T(8,128)S(1)} %get-tuple-element.29.mine, ...), custom_call_target="tpu_custom_call" | custom-call | tf_op jit(solution)/shard_map/pallas_call | solution.py:193
  46.2 0.1 collective-permute-start.8
  46.3 0.6 %collective-permute-start.9 = (f32[8,128]{1,0:T(8,128)S(1)}, f32[8,128]{1,0:T(8,128)S(1)}, u32[]{:S(2)}, u32[]{:S(2)}) collective-permute-start(f32[8,128]{1,0:T(8,128)S(1)} %get-tuple-element.44), channel_id=1, source_target_pairs={{0,2},{1,3},{2,0},{3,1},{4,6},{5,7},{6,4},{7,5},{8,10},{9,11},{10,... | collective-permute-start | bytes 12296 | tf_op jit(solution)/shard_map/ppermute | solution.py:218
  46.9 2.5 %collective-permute-start.10 = (f32[8,128]{1,0:T(8,128)S(1)}, f32[8,128]{1,0:T(8,128)S(1)}, u32[]{:S(2)}, u32[]{:S(2)}) collective-permute-start(f32[8,128]{1,0:T(8,128)S(1)} %get-tuple-element.45), channel_id=1, source_target_pairs={{0,1},{1,0},{2,3},{3,2},{4,5},{5,4},{6,7},{7,6},{8,9},{9,8},{10,11... | collective-permute-start | bytes 12296 | tf_op jit(solution)/shard_map/ppermute | solution.py:218
  49.4 0.0 collective-permute-done.arrived
  49.4 0.0 collective-permute-done.8.rest_0_
  49.4 1.0 %shard_map.63 = (f32[8,128]{1,0:T(8,128)S(1)}, f32[8,128]{1,0:T(8,128)S(1)}) custom-call(bf16[256,1024]{1,0:T(8,128)(2,1)S(1)} %collective-permute-done.arrived, bf16[1024,1024]{1,0:T(8,128)(2,1)S(1)} %get-tuple-element.27.units, f32[6,4,128]{2,1,0:T(4,128)S(1)} %get-tuple-element.28.live, f32[6,8,128]{2,1,0:T(8,128)S(1)} %get-tuple-element.29.mine, ...), custom_call_target="tpu_custom_call" | custom-call | tf_op jit(solution)/shard_map/pallas_call | solution.py:193
  50.4 2.4 %collective-permute-start.11 = (f32[8,128]{1,0:T(8,128)S(1)}, f32[8,128]{1,0:T(8,128)S(1)}, u32[]{:S(2)}, u32[]{:S(2)}) collective-permute-start(f32[8,128]{1,0:T(8,128)S(1)} %get-tuple-element.46), channel_id=1, source_target_pairs={{0,3},{1,2},{2,1},{3,0},{4,7},{5,6},{6,5},{7,4},{8,11},{9,10},{10,... | collective-permute-start | bytes 12296 | tf_op jit(solution)/shard_map/ppermute | solution.py:218
  52.8 0.7 %collective-permute-done.9 = f32[8,128]{1,0:T(8,128)S(1)} collective-permute-done((f32[8,128]{1,0:T(8,128)S(1)}, f32[8,128]{1,0:T(8,128)S(1)}, u32[]{:S(2)}, u32[]{:S(2)}) %collective-permute-start.9) | collective-permute-done | bytes 4128 | tf_op jit(solution)/shard_map/ppermute | solution.py:218
  53.5 0.0 collective-permute-done.10
  53.5 2.4 %collective-permute-done.11 = f32[8,128]{1,0:T(8,128)S(1)} collective-permute-done((f32[8,128]{1,0:T(8,128)S(1)}, f32[8,128]{1,0:T(8,128)S(1)}, u32[]{:S(2)}, u32[]{:S(2)}) %collective-permute-start.11) | collective-permute-done | bytes 4128 | tf_op jit(solution)/shard_map/ppermute | solution.py:218
  55.8 0.6 %fusion.2 = f32[1024]{0:T(1024)} fusion(f32[8,128]{1,0:T(8,128)S(1)} %collective-permute-done.11, f32[8,128]{1,0:T(8,128)S(1)} %collective-permute-done.10, f32[8,128]{1,0:T(8,128)S(1)} %get-tuple-element.43, f32[8,128]{1,0:T(8,128)S(1)} %collective-permute-done.9, f32[6,8,128]{2,1,0:T(8,128)S(1)} %get-tuple-element.29.mine), kind=kLoop, calls=%fused_computation.3 | loop fusion | flops 7168 | bytes 32768 | tf_op jit(solution)/shard_map/reshape | solution.py:244
  (1 shorter events, 0.0 us)
Async XLA Ops:
  0.0 6.8 %copy-start = (bf16[1024,1024]{1,0:T(8,128)(2,1)S(1)}, bf16[1024,1024]{1,0:T(8,128)(2,1)}, u32[]{:S(2)}) copy-start(bf16[1024,1024]{1,0:T(8,128)(2,1)} %embeds.5) | copy-start | bytes 6291460
  0.0 6.8 %copy-start.2 = (s32[1,4]{1,0:T(1,128)S(1)}, s32[1,4]{1,0:T(1,128)}, u32[]{:S(2)}) copy-start(s32[1,4]{1,0:T(1,128)} %pick_blk.5) | copy-start | bytes 52
  0.0 6.8 %copy-start.1 = (s32[4,4]{1,0:T(4,128)S(1)}, s32[4,4]{1,0:T(4,128)}, u32[]{:S(2)}) copy-start(s32[4,4]{1,0:T(4,128)} %pick_sub.5) | copy-start | bytes 196
  0.0 11.0 %copy-start.3 = (s32[1,16]{1,0:T(1,128)S(1)}, s32[1,16]{1,0:T(1,128)}, u32[]{:S(2)}) copy-start(s32[1,16]{1,0:T(1,128)} %mask_blk.1) | copy-start | bytes 196
  0.0 11.0 %copy-start.4 = (s32[1,16]{1,0:T(1,128)S(1)}, s32[1,16]{1,0:T(1,128)}, u32[]{:S(2)}) copy-start(s32[1,16]{1,0:T(1,128)} %mask_sub.1) | copy-start | bytes 196
  2.6 8.2 %collective-permute-start.5 = (bf16[256,1024]{1,0:T(8,128)(2,1)}, bf16[256,1024]{1,0:T(8,128)(2,1)S(1)}, u32[]{:S(2)}, u32[]{:S(2)}) collective-permute-start(bf16[256,1024]{1,0:T(8,128)(2,1)} %get-tuple-element.34), channel_id=1, source_target_pairs={{0,4},{4,0},{8,12},{12,8},{1,5},{5,1},{9,13},{13,9},{2,6},{6,2},{1... | collective-permute-start | bytes 1572872 | tf_op jit(solution)/shard_map/ppermute | solution.py:218
  3.1 27.9 %collective-permute-start.4 = (bf16[256,1024]{1,0:T(8,128)(2,1)}, bf16[256,1024]{1,0:T(8,128)(2,1)S(1)}, u32[]{:S(2)}, u32[]{:S(2)}) collective-permute-start(bf16[256,1024]{1,0:T(8,128)(2,1)} %get-tuple-element.33), channel_id=1, source_target_pairs={{0,2},{1,3},{2,0},{3,1},{4,6},{5,7},{6,4},{7,5},{8,10},{9,11},{10,... | collective-permute-start | bytes 1572872 | tf_op jit(solution)/shard_map/ppermute | solution.py:218
  7.6 24.4 %collective-permute-start.3 = (bf16[256,1024]{1,0:T(8,128)(2,1)S(1)}, bf16[256,1024]{1,0:T(8,128)(2,1)S(1)}, u32[]{:S(2)}, u32[]{:S(2)}) collective-permute-start(bf16[256,1024]{1,0:T(8,128)(2,1)S(1)} %get-tuple-element.32), channel_id=1, source_target_pairs={{0,8},{4,12},{8,0},{12,4},{1,9},{5,13},{9,1},{13,5},{2,10},{6,14},... | collective-permute-start | bytes 1572872 | tf_op jit(solution)/shard_map/ppermute | solution.py:218
  9.2 35.0 %collective-permute-start.2 = (bf16[256,1024]{1,0:T(8,128)(2,1)S(1)}, bf16[256,1024]{1,0:T(8,128)(2,1)S(1)}, u32[]{:S(2)}, u32[]{:S(2)}) collective-permute-start(bf16[256,1024]{1,0:T(8,128)(2,1)S(1)} %get-tuple-element.31), channel_id=1, source_target_pairs={{0,1},{1,0},{2,3},{3,2},{4,5},{5,4},{6,7},{7,6},{8,9},{9,8},{10,11... | collective-permute-start | bytes 1572872 | tf_op jit(solution)/shard_map/ppermute | solution.py:218
  10.8 34.4 %collective-permute-start.1 = (bf16[256,1024]{1,0:T(8,128)(2,1)S(1)}, bf16[256,1024]{1,0:T(8,128)(2,1)S(1)}, u32[]{:S(2)}, u32[]{:S(2)}) collective-permute-start(bf16[256,1024]{1,0:T(8,128)(2,1)S(1)} %get-tuple-element.30), channel_id=1, source_target_pairs={{0,12},{4,8},{8,4},{12,0},{1,13},{5,9},{9,5},{13,1},{2,14},{6,10},... | collective-permute-start | bytes 1572872 | tf_op jit(solution)/shard_map/ppermute | solution.py:218
  10.8 38.6 %collective-permute-start = (bf16[256,1024]{1,0:T(8,128)(2,1)S(1)}, bf16[256,1024]{1,0:T(8,128)(2,1)S(1)}, u32[]{:S(2)}, u32[]{:S(2)}) collective-permute-start(bf16[256,1024]{1,0:T(8,128)(2,1)S(1)} %get-tuple-element.26), channel_id=1, source_target_pairs={{0,3},{1,2},{2,1},{3,0},{4,7},{5,6},{6,5},{7,4},{8,11},{9,10},{10,... | collective-permute-start | bytes 1572872 | tf_op jit(solution)/shard_map/ppermute | solution.py:218
  31.1 1.2 %collective-permute-start.6 = (f32[8,128]{1,0:T(8,128)S(1)}, f32[8,128]{1,0:T(8,128)S(1)}, u32[]{:S(2)}, u32[]{:S(2)}) collective-permute-start(f32[8,128]{1,0:T(8,128)S(1)} %get-tuple-element.37), channel_id=1, source_target_pairs={{0,4},{4,0},{8,12},{12,8},{1,5},{5,1},{9,13},{13,9},{2,6},{6,2},{1... | collective-permute-start | bytes 12296 | tf_op jit(solution)/shard_map/ppermute | solution.py:218
  33.2 12.0 %collective-permute-start.7 = (f32[8,128]{1,0:T(8,128)S(1)}, f32[8,128]{1,0:T(8,128)S(1)}, u32[]{:S(2)}, u32[]{:S(2)}) collective-permute-start(f32[8,128]{1,0:T(8,128)S(1)} %get-tuple-element.40), channel_id=1, source_target_pairs={{0,8},{4,12},{8,0},{12,4},{1,9},{5,13},{9,1},{13,5},{2,10},{6,14},... | collective-permute-start | bytes 12296 | tf_op jit(solution)/shard_map/ppermute | solution.py:218
  46.2 3.2 %collective-permute-start.8 = (f32[8,128]{1,0:T(8,128)S(1)}, f32[8,128]{1,0:T(8,128)S(1)}, u32[]{:S(2)}, u32[]{:S(2)}) collective-permute-start(f32[8,128]{1,0:T(8,128)S(1)} %get-tuple-element.42), channel_id=1, source_target_pairs={{0,12},{4,8},{8,4},{12,0},{1,13},{5,9},{9,5},{13,1},{2,14},{6,10},... | collective-permute-start | bytes 12296 | tf_op jit(solution)/shard_map/ppermute | solution.py:218
  46.3 7.2 %collective-permute-start.9 = (f32[8,128]{1,0:T(8,128)S(1)}, f32[8,128]{1,0:T(8,128)S(1)}, u32[]{:S(2)}, u32[]{:S(2)}) collective-permute-start(f32[8,128]{1,0:T(8,128)S(1)} %get-tuple-element.44), channel_id=1, source_target_pairs={{0,2},{1,3},{2,0},{3,1},{4,6},{5,7},{6,4},{7,5},{8,10},{9,11},{10,... | collective-permute-start | bytes 12296 | tf_op jit(solution)/shard_map/ppermute | solution.py:218
  46.9 6.6 %collective-permute-start.10 = (f32[8,128]{1,0:T(8,128)S(1)}, f32[8,128]{1,0:T(8,128)S(1)}, u32[]{:S(2)}, u32[]{:S(2)}) collective-permute-start(f32[8,128]{1,0:T(8,128)S(1)} %get-tuple-element.45), channel_id=1, source_target_pairs={{0,1},{1,0},{2,3},{3,2},{4,5},{5,4},{6,7},{7,6},{8,9},{9,8},{10,11... | collective-permute-start | bytes 12296 | tf_op jit(solution)/shard_map/ppermute | solution.py:218
  50.4 5.5 %collective-permute-start.11 = (f32[8,128]{1,0:T(8,128)S(1)}, f32[8,128]{1,0:T(8,128)S(1)}, u32[]{:S(2)}, u32[]{:S(2)}) collective-permute-start(f32[8,128]{1,0:T(8,128)S(1)} %get-tuple-element.46), channel_id=1, source_target_pairs={{0,3},{1,2},{2,1},{3,0},{4,7},{5,6},{6,5},{7,4},{8,11},{9,10},{10,... | collective-permute-start | bytes 12296 | tf_op jit(solution)/shard_map/ppermute | solution.py:218

commit v25 on v23

--- a/solution.py
+++ b/solution.py
@@ -200,7 +200,7 @@
 
 
 BEHIND = 2
-FIRST_CUT = 128
+FIRST_CUT = 192
 
 
 def plan_slots(sizes):

time: 57.2 us -> 57.4 us (level)
  no operation moved by 1% of the time
where the time goes in v25:
time: 57.4 us; the launch traced here: 57.3 us
  waiting for transfers between devices  26.8 us (47%)
  starting transfers between devices  17.7 us (31%)
  Pallas kernels  12 us (21%)
  other arithmetic  0.6 us (1%)
    ppermute x13, waiting for transfers between devices, send(): return lax.ppermute(array, slot[0], pairs(slot[1], sizes[slot[0]]))  26.8 us
    ppermute x13, starting transfers between devices, send(): return lax.ppermute(array, slot[0], pairs(slot[1], sizes[slot[0]]))  17.7 us
    pallas_call x7, Pallas kernels, work(): pl.pallas_call(functools.partial(slot_kernel, place, *slot[2:], [one for...  6.46 us
    pallas_call x1, Pallas kernels, first_rows(): pl.pallas_call(functools.partial(first_kernel, slots), out_shape=[jax.Sha...  2.6 us
    pallas_call x1, Pallas kernels, prepare(): pl.pallas_call(functools.partial(prepare_kernel, slots), out_shape=[jax.S...  1.77 us
  transfers between devices with their start and end apart: 13, of which 5 were waited for; matrix products, arithmetic and copies ran while one was open for 0% of the time, Pallas kernels for 16%

profile of v25, /device:TPU:0, one launch (start us, length us, event | category | flops | bytes accessed | tf_op | source)
XLA Modules:
  0.0 57.3 jit_solution(6029899643026233279)
XLA Ops:
  0.0 0.0 copy-start
  0.0 0.0 copy-start.2
  0.0 0.0 copy-start.1
  0.0 0.0 copy-start.3
  0.0 0.0 copy-start.4
  0.0 2.6 %shard_map.57 = (bf16[256,1024]{1,0:T(8,128)(2,1)}, bf16[256,1024]{1,0:T(8,128)(2,1)}) custom-call(s32[1,4]{1,0:T(1,128)} %pick_blk.5, s32[4,4]{1,0:T(4,128)} %pick_sub.5, bf16[1024,1024]{1,0:T(8,128)(2,1)} %embeds.5), custom_call_target="tpu_custom_call" | custom-call | tf_op jit(solution)/shard_map/pallas_call | solution.py:81
  2.6 0.5 collective-permute-start.6
  3.2 3.7 %collective-permute-start.5 = (bf16[256,1024]{1,0:T(8,128)(2,1)}, bf16[256,1024]{1,0:T(8,128)(2,1)S(1)}, u32[]{:S(2)}, u32[]{:S(2)}) collective-permute-start(bf16[256,1024]{1,0:T(8,128)(2,1)} %get-tuple-element.37), channel_id=1, source_target_pairs={{0,2},{1,3},{2,0},{3,1},{4,6},{5,7},{6,4},{7,5},{8,10},{9,11},{10,... | collective-permute-start | bytes 1572872 | tf_op jit(solution)/shard_map/ppermute | solution.py:223
  6.8 0.0 copy-done
  6.8 0.0 copy-done.2
  6.8 0.0 copy-done.1
  6.8 1.1 %shard_map.55 = (bf16[256,1024]{1,0:T(8,128)(2,1)S(1)}, bf16[256,1024]{1,0:T(8,128)(2,1)S(1)}, bf16[256,1024]{1,0:T(8,128)(2,1)S(1)}, bf16[192,1024]{1,0:T(8,128)(2,1)S(1)}, bf16[64,1024]{1,0:T(8,128)(2,1)S(1)}) custom-call(s32[1,4]{1,0:T(1,128)S(1)} %copy-done.2, s32[4,4]{1,0:T(4,128)S(1)} %copy-done.1, bf16[1024,1024]{1,0:T(8,128)(2,1)S(1)} %copy-done), custom_call_target="tpu_custom_call" | custom-call | tf_op jit(solution)/shard_map/pallas_call | solution.py:118
  8.0 1.6 %collective-permute-start.4 = (bf16[256,1024]{1,0:T(8,128)(2,1)S(1)}, bf16[256,1024]{1,0:T(8,128)(2,1)S(1)}, u32[]{:S(2)}, u32[]{:S(2)}) collective-permute-start(bf16[256,1024]{1,0:T(8,128)(2,1)S(1)} %get-tuple-element.36), channel_id=1, source_target_pairs={{0,8},{4,12},{8,0},{12,4},{1,9},{5,13},{9,1},{13,5},{2,10},{6,14},... | collective-permute-start | bytes 1572872 | tf_op jit(solution)/shard_map/ppermute | solution.py:223
  9.5 1.6 %collective-permute-start.3 = (bf16[256,1024]{1,0:T(8,128)(2,1)S(1)}, bf16[256,1024]{1,0:T(8,128)(2,1)S(1)}, u32[]{:S(2)}, u32[]{:S(2)}) collective-permute-start(bf16[256,1024]{1,0:T(8,128)(2,1)S(1)} %get-tuple-element.35), channel_id=1, source_target_pairs={{0,1},{1,0},{2,3},{3,2},{4,5},{5,4},{6,7},{7,6},{8,9},{9,8},{10,11... | collective-permute-start | bytes 1572872 | tf_op jit(solution)/shard_map/ppermute | solution.py:223
  11.1 0.0 collective-permute-start.2
  11.1 0.0 collective-permute-done.6.arrived
  11.1 0.2 collective-permute-start.1
  11.3 19.7 %collective-permute-done.5.arrived = bf16[256,1024]{1,0:T(8,128)(2,1)S(1)} collective-permute-done((bf16[256,1024]{1,0:T(8,128)(2,1)}, bf16[256,1024]{1,0:T(8,128)(2,1)S(1)}, u32[]{:S(2)}, u32[]{:S(2)}) %collective-permute-start.5) | collective-permute-done | bytes 524320 | tf_op jit(solution)/shard_map/ppermute | solution.py:223
  31.1 3.8 %collective-permute-start = (bf16[64,1024]{1,0:T(8,128)(2,1)S(1)}, bf16[64,1024]{1,0:T(8,128)(2,1)S(1)}, u32[]{:S(2)}, u32[]{:S(2)}) collective-permute-start(bf16[64,1024]{1,0:T(8,128)(2,1)S(1)} %get-tuple-element.29), channel_id=1, source_target_pairs={{0,3},{1,2},{2,1},{3,0},{4,7},{5,6},{6,5},{7,4},{8,11},{9,10},{10,... | collective-permute-start | bytes 393224 | tf_op jit(solution)/shard_map/ppermute | solution.py:223
  34.9 0.0 copy-done.3
  34.9 0.0 copy-done.4
  34.9 1.8 %shard_map.56 = (bf16[1024,1024]{1,0:T(8,128)(2,1)S(1)}, f32[7,4,128]{2,1,0:T(4,128)S(1)}, f32[7,8,128]{2,1,0:T(8,128)S(1)}) custom-call(s32[1,4]{1,0:T(1,128)S(1)} %copy-done.2, s32[4,4]{1,0:T(4,128)S(1)} %copy-done.1, s32[1,16]{1,0:T(1,128)S(1)} %copy-done.3, s32[1,16]{1,0:T(1,128)S(1)} %copy-done.4, bf16[1024,1024]{1,0:T(8,128)(2,1)S(1)} %copy-done), custom_call_target="tpu_custom_call" | custom-call | tf_op jit(solution)/shard_map/pallas_call | solution.py:150
  36.7 1.0 %shard_map.58 = (f32[8,128]{1,0:T(8,128)S(1)}, f32[8,128]{1,0:T(8,128)S(1)}) custom-call(bf16[256,1024]{1,0:T(8,128)(2,1)S(1)} %collective-permute-done.6.arrived, bf16[1024,1024]{1,0:T(8,128)(2,1)S(1)} %get-tuple-element.30.units, f32[7,4,128]{2,1,0:T(4,128)S(1)} %get-tuple-element.31.live, f32[7,8,128]{2,1,0:T(8,128)S(1)} %get-tuple-element.32.mine, ...), custom_call_target="tpu_custom_call" | custom-call | tf_op jit(solution)/shard_map/pallas_call | solution.py:193
  37.7 0.0 collective-permute-done.4.arrived
  37.7 0.1 collective-permute-start.7
  37.8 1.0 %shard_map.59 = (f32[8,128]{1,0:T(8,128)S(1)}, f32[8,128]{1,0:T(8,128)S(1)}) custom-call(bf16[256,1024]{1,0:T(8,128)(2,1)S(1)} %collective-permute-done.5.arrived, bf16[1024,1024]{1,0:T(8,128)(2,1)S(1)} %get-tuple-element.30.units, f32[7,4,128]{2,1,0:T(4,128)S(1)} %get-tuple-element.31.live, f32[7,8,128]{2,1,0:T(8,128)S(1)} %get-tuple-element.32.mine, ...), custom_call_target="tpu_custom_call" | custom-call | tf_op jit(solution)/shard_map/pallas_call | solution.py:193
  38.8 0.2 collective-permute-done.7.rest_0_
  38.9 1.0 %shard_map.60 = (f32[8,128]{1,0:T(8,128)S(1)}, f32[8,128]{1,0:T(8,128)S(1)}) custom-call(bf16[256,1024]{1,0:T(8,128)(2,1)S(1)} %collective-permute-done.4.arrived, bf16[1024,1024]{1,0:T(8,128)(2,1)S(1)} %get-tuple-element.30.units, f32[7,4,128]{2,1,0:T(4,128)S(1)} %get-tuple-element.31.live, f32[7,8,128]{2,1,0:T(8,128)S(1)} %get-tuple-element.32.mine, ...), custom_call_target="tpu_custom_call" | custom-call | tf_op jit(solution)/shard_map/pallas_call | solution.py:193
  39.9 1.6 %collective-permute-start.8 = (f32[8,128]{1,0:T(8,128)S(1)}, f32[8,128]{1,0:T(8,128)S(1)}, u32[]{:S(2)}, u32[]{:S(2)}) collective-permute-start(f32[8,128]{1,0:T(8,128)S(1)} %get-tuple-element.44), channel_id=1, source_target_pairs={{0,8},{4,12},{8,0},{12,4},{1,9},{5,13},{9,1},{13,5},{2,10},{6,14},... | collective-permute-start | bytes 12296 | tf_op jit(solution)/shard_map/ppermute | solution.py:223
  41.5 3.0 %collective-permute-done.3.arrived = bf16[256,1024]{1,0:T(8,128)(2,1)S(1)} collective-permute-done((bf16[256,1024]{1,0:T(8,128)(2,1)S(1)}, bf16[256,1024]{1,0:T(8,128)(2,1)S(1)}, u32[]{:S(2)}, u32[]{:S(2)}) %collective-permute-start.3) | collective-permute-done | bytes 524320 | tf_op jit(solution)/shard_map/ppermute | solution.py:223
  44.5 1.0 %shard_map.61 = (f32[8,128]{1,0:T(8,128)S(1)}, f32[8,128]{1,0:T(8,128)S(1)}) custom-call(bf16[256,1024]{1,0:T(8,128)(2,1)S(1)} %collective-permute-done.3.arrived, bf16[1024,1024]{1,0:T(8,128)(2,1)S(1)} %get-tuple-element.30.units, f32[7,4,128]{2,1,0:T(4,128)S(1)} %get-tuple-element.31.live, f32[7,8,128]{2,1,0:T(8,128)S(1)} %get-tuple-element.32.mine, ...), custom_call_target="tpu_custom_call" | custom-call | tf_op jit(solution)/shard_map/pallas_call | solution.py:193
  45.5 0.0 collective-permute-done.2.arrived
  45.5 0.0 collective-permute-done.8.rest_0_
  45.6 1.0 %shard_map.62 = (f32[8,128]{1,0:T(8,128)S(1)}, f32[8,128]{1,0:T(8,128)S(1)}) custom-call(bf16[256,1024]{1,0:T(8,128)(2,1)S(1)} %collective-permute-done.2.arrived, bf16[1024,1024]{1,0:T(8,128)(2,1)S(1)} %get-tuple-element.30.units, f32[7,4,128]{2,1,0:T(4,128)S(1)} %get-tuple-element.31.live, f32[7,8,128]{2,1,0:T(8,128)S(1)} %get-tuple-element.32.mine, ...), custom_call_target="tpu_custom_call" | custom-call | tf_op jit(solution)/shard_map/pallas_call | solution.py:193
  46.5 0.1 collective-permute-start.9
  46.6 0.6 %collective-permute-start.10 = (f32[8,128]{1,0:T(8,128)S(1)}, f32[8,128]{1,0:T(8,128)S(1)}, u32[]{:S(2)}, u32[]{:S(2)}) collective-permute-start(f32[8,128]{1,0:T(8,128)S(1)} %get-tuple-element.50), channel_id=1, source_target_pairs={{0,2},{1,3},{2,0},{3,1},{4,6},{5,7},{6,4},{7,5},{8,10},{9,11},{10,... | collective-permute-start | bytes 12296 | tf_op jit(solution)/shard_map/ppermute | solution.py:223
  47.2 2.5 %collective-permute-start.11 = (f32[8,128]{1,0:T(8,128)S(1)}, f32[8,128]{1,0:T(8,128)S(1)}, u32[]{:S(2)}, u32[]{:S(2)}) collective-permute-start(f32[8,128]{1,0:T(8,128)S(1)} %get-tuple-element.51), channel_id=1, source_target_pairs={{0,1},{1,0},{2,3},{3,2},{4,5},{5,4},{6,7},{7,6},{8,9},{9,8},{10,11... | collective-permute-start | bytes 12296 | tf_op jit(solution)/shard_map/ppermute | solution.py:223
  49.7 0.0 collective-permute-done.1.arrived
  49.7 0.8 %shard_map.63 = (f32[8,128]{1,0:T(8,128)S(1)}, f32[8,128]{1,0:T(8,128)S(1)}) custom-call(bf16[192,1024]{1,0:T(8,128)(2,1)S(1)} %collective-permute-done.1.arrived, bf16[1024,1024]{1,0:T(8,128)(2,1)S(1)} %get-tuple-element.30.units, f32[7,4,128]{2,1,0:T(4,128)S(1)} %get-tuple-element.31.live, f32[7,8,128]{2,1,0:T(8,128)S(1)} %get-tuple-element.32.mine, ...), custom_call_target="tpu_custom_call" | custom-call | tf_op jit(solution)/shard_map/pallas_call | solution.py:193
  50.5 0.0 collective-permute-done.arrived
  50.5 0.0 collective-permute-done.9.rest_0_
  50.5 0.7 %shard_map.64 = (f32[8,128]{1,0:T(8,128)S(1)}, f32[8,128]{1,0:T(8,128)S(1)}) custom-call(bf16[64,1024]{1,0:T(8,128)(2,1)S(1)} %collective-permute-done.arrived, bf16[1024,1024]{1,0:T(8,128)(2,1)S(1)} %get-tuple-element.30.units, f32[7,4,128]{2,1,0:T(4,128)S(1)} %get-tuple-element.31.live, f32[7,8,128]{2,1,0:T(8,128)S(1)} %get-tuple-element.32.mine, ...), custom_call_target="tpu_custom_call" | custom-call | tf_op jit(solution)/shard_map/pallas_call | solution.py:193
  51.2 1.6 %collective-permute-start.12 = (f32[8,128]{1,0:T(8,128)S(1)}, f32[8,128]{1,0:T(8,128)S(1)}, u32[]{:S(2)}, u32[]{:S(2)}) collective-permute-start(f32[8,128]{1,0:T(8,128)S(1)} %get-tuple-element.52), channel_id=1, source_target_pairs={{0,3},{1,2},{2,1},{3,0},{4,7},{5,6},{6,5},{7,4},{8,11},{9,10},{10,... | collective-permute-start | bytes 12296 | tf_op jit(solution)/shard_map/ppermute | solution.py:223
  52.8 0.7 %collective-permute-done.10 = f32[8,128]{1,0:T(8,128)S(1)} collective-permute-done((f32[8,128]{1,0:T(8,128)S(1)}, f32[8,128]{1,0:T(8,128)S(1)}, u32[]{:S(2)}, u32[]{:S(2)}) %collective-permute-start.10) | collective-permute-done | bytes 4128 | tf_op jit(solution)/shard_map/ppermute | solution.py:223
  53.5 0.0 collective-permute-done.11
  53.5 3.2 %collective-permute-done.12 = f32[8,128]{1,0:T(8,128)S(1)} collective-permute-done((f32[8,128]{1,0:T(8,128)S(1)}, f32[8,128]{1,0:T(8,128)S(1)}, u32[]{:S(2)}, u32[]{:S(2)}) %collective-permute-start.12) | collective-permute-done | bytes 4128 | tf_op jit(solution)/shard_map/ppermute | solution.py:223
  56.7 0.6 %fusion.2 = f32[1024]{0:T(1024)} fusion(f32[8,128]{1,0:T(8,128)S(1)} %collective-permute-done.12, f32[8,128]{1,0:T(8,128)S(1)} %collective-permute-done.11, f32[8,128]{1,0:T(8,128)S(1)} %get-tuple-element.49, f32[8,128]{1,0:T(8,128)S(1)} %collective-permute-done.10, f32[7,8,128]{2,1,0:T(8,128)S(1)} %get-tuple-element.32.mine), kind=kLoop, calls=%fused_computation.3 | loop fusion | flops 7168 | bytes 32768 | tf_op jit(solution)/shard_map/reshape | solution.py:249
  (1 shorter events, 0.0 us)
Async XLA Ops:
  0.0 6.8 %copy-start = (bf16[1024,1024]{1,0:T(8,128)(2,1)S(1)}, bf16[1024,1024]{1,0:T(8,128)(2,1)}, u32[]{:S(2)}) copy-start(bf16[1024,1024]{1,0:T(8,128)(2,1)} %embeds.5) | copy-start | bytes 6291460
  0.0 6.8 %copy-start.2 = (s32[1,4]{1,0:T(1,128)S(1)}, s32[1,4]{1,0:T(1,128)}, u32[]{:S(2)}) copy-start(s32[1,4]{1,0:T(1,128)} %pick_blk.5) | copy-start | bytes 52
  0.0 6.8 %copy-start.1 = (s32[4,4]{1,0:T(4,128)S(1)}, s32[4,4]{1,0:T(4,128)}, u32[]{:S(2)}) copy-start(s32[4,4]{1,0:T(4,128)} %pick_sub.5) | copy-start | bytes 196
  0.0 34.9 %copy-start.3 = (s32[1,16]{1,0:T(1,128)S(1)}, s32[1,16]{1,0:T(1,128)}, u32[]{:S(2)}) copy-start(s32[1,16]{1,0:T(1,128)} %mask_blk.1) | copy-start | bytes 196
  0.0 34.9 %copy-start.4 = (s32[1,16]{1,0:T(1,128)S(1)}, s32[1,16]{1,0:T(1,128)}, u32[]{:S(2)}) copy-start(s32[1,16]{1,0:T(1,128)} %mask_sub.1) | copy-start | bytes 196
  2.6 8.5 %collective-permute-start.6 = (bf16[256,1024]{1,0:T(8,128)(2,1)}, bf16[256,1024]{1,0:T(8,128)(2,1)S(1)}, u32[]{:S(2)}, u32[]{:S(2)}) collective-permute-start(bf16[256,1024]{1,0:T(8,128)(2,1)} %get-tuple-element.38), channel_id=1, source_target_pairs={{0,4},{4,0},{8,12},{12,8},{1,5},{5,1},{9,13},{13,9},{2,6},{6,2},{1... | collective-permute-start | bytes 1572872 | tf_op jit(solution)/shard_map/ppermute | solution.py:223
  3.2 27.9 %collective-permute-start.5 = (bf16[256,1024]{1,0:T(8,128)(2,1)}, bf16[256,1024]{1,0:T(8,128)(2,1)S(1)}, u32[]{:S(2)}, u32[]{:S(2)}) collective-permute-start(bf16[256,1024]{1,0:T(8,128)(2,1)} %get-tuple-element.37), channel_id=1, source_target_pairs={{0,2},{1,3},{2,0},{3,1},{4,6},{5,7},{6,4},{7,5},{8,10},{9,11},{10,... | collective-permute-start | bytes 1572872 | tf_op jit(solution)/shard_map/ppermute | solution.py:223
  8.0 29.7 %collective-permute-start.4 = (bf16[256,1024]{1,0:T(8,128)(2,1)S(1)}, bf16[256,1024]{1,0:T(8,128)(2,1)S(1)}, u32[]{:S(2)}, u32[]{:S(2)}) collective-permute-start(bf16[256,1024]{1,0:T(8,128)(2,1)S(1)} %get-tuple-element.36), channel_id=1, source_target_pairs={{0,8},{4,12},{8,0},{12,4},{1,9},{5,13},{9,1},{13,5},{2,10},{6,14},... | collective-permute-start | bytes 1572872 | tf_op jit(solution)/shard_map/ppermute | solution.py:223
  9.5 35.0 %collective-permute-start.3 = (bf16[256,1024]{1,0:T(8,128)(2,1)S(1)}, bf16[256,1024]{1,0:T(8,128)(2,1)S(1)}, u32[]{:S(2)}, u32[]{:S(2)}) collective-permute-start(bf16[256,1024]{1,0:T(8,128)(2,1)S(1)} %get-tuple-element.35), channel_id=1, source_target_pairs={{0,1},{1,0},{2,3},{3,2},{4,5},{5,4},{6,7},{7,6},{8,9},{9,8},{10,11... | collective-permute-start | bytes 1572872 | tf_op jit(solution)/shard_map/ppermute | solution.py:223
  11.1 34.4 %collective-permute-start.2 = (bf16[256,1024]{1,0:T(8,128)(2,1)S(1)}, bf16[256,1024]{1,0:T(8,128)(2,1)S(1)}, u32[]{:S(2)}, u32[]{:S(2)}) collective-permute-start(bf16[256,1024]{1,0:T(8,128)(2,1)S(1)} %get-tuple-element.34), channel_id=1, source_target_pairs={{0,12},{4,8},{8,4},{12,0},{1,13},{5,9},{9,5},{13,1},{2,14},{6,10},... | collective-permute-start | bytes 1572872 | tf_op jit(solution)/shard_map/ppermute | solution.py:223
  11.1 38.6 %collective-permute-start.1 = (bf16[192,1024]{1,0:T(8,128)(2,1)S(1)}, bf16[192,1024]{1,0:T(8,128)(2,1)S(1)}, u32[]{:S(2)}, u32[]{:S(2)}) collective-permute-start(bf16[192,1024]{1,0:T(8,128)(2,1)S(1)} %get-tuple-element.33), channel_id=1, source_target_pairs={{0,3},{1,2},{2,1},{3,0},{4,7},{5,6},{6,5},{7,4},{8,11},{9,10},{10,... | collective-permute-start | bytes 1179656 | tf_op jit(solution)/shard_map/ppermute | solution.py:223
  31.1 19.4 %collective-permute-start = (bf16[64,1024]{1,0:T(8,128)(2,1)S(1)}, bf16[64,1024]{1,0:T(8,128)(2,1)S(1)}, u32[]{:S(2)}, u32[]{:S(2)}) collective-permute-start(bf16[64,1024]{1,0:T(8,128)(2,1)S(1)} %get-tuple-element.29), channel_id=1, source_target_pairs={{0,3},{1,2},{2,1},{3,0},{4,7},{5,6},{6,5},{7,4},{8,11},{9,10},{10,... | collective-permute-start | bytes 393224 | tf_op jit(solution)/shard_map/ppermute | solution.py:223
  37.7 1.2 %collective-permute-start.7 = (f32[8,128]{1,0:T(8,128)S(1)}, f32[8,128]{1,0:T(8,128)S(1)}, u32[]{:S(2)}, u32[]{:S(2)}) collective-permute-start(f32[8,128]{1,0:T(8,128)S(1)} %get-tuple-element.41), channel_id=1, source_target_pairs={{0,4},{4,0},{8,12},{12,8},{1,5},{5,1},{9,13},{13,9},{2,6},{6,2},{1... | collective-permute-start | bytes 12296 | tf_op jit(solution)/shard_map/ppermute | solution.py:223
  39.9 5.6 %collective-permute-start.8 = (f32[8,128]{1,0:T(8,128)S(1)}, f32[8,128]{1,0:T(8,128)S(1)}, u32[]{:S(2)}, u32[]{:S(2)}) collective-permute-start(f32[8,128]{1,0:T(8,128)S(1)} %get-tuple-element.44), channel_id=1, source_target_pairs={{0,8},{4,12},{8,0},{12,4},{1,9},{5,13},{9,1},{13,5},{2,10},{6,14},... | collective-permute-start | bytes 12296 | tf_op jit(solution)/shard_map/ppermute | solution.py:223
  46.5 4.0 %collective-permute-start.9 = (f32[8,128]{1,0:T(8,128)S(1)}, f32[8,128]{1,0:T(8,128)S(1)}, u32[]{:S(2)}, u32[]{:S(2)}) collective-permute-start(f32[8,128]{1,0:T(8,128)S(1)} %get-tuple-element.47), channel_id=1, source_target_pairs={{0,12},{4,8},{8,4},{12,0},{1,13},{5,9},{9,5},{13,1},{2,14},{6,10},... | collective-permute-start | bytes 12296 | tf_op jit(solution)/shard_map/ppermute | solution.py:223
  46.6 6.8 %collective-permute-start.10 = (f32[8,128]{1,0:T(8,128)S(1)}, f32[8,128]{1,0:T(8,128)S(1)}, u32[]{:S(2)}, u32[]{:S(2)}) collective-permute-start(f32[8,128]{1,0:T(8,128)S(1)} %get-tuple-element.50), channel_id=1, source_target_pairs={{0,2},{1,3},{2,0},{3,1},{4,6},{5,7},{6,4},{7,5},{8,10},{9,11},{10,... | collective-permute-start | bytes 12296 | tf_op jit(solution)/shard_map/ppermute | solution.py:223
  47.2 6.3 %collective-permute-start.11 = (f32[8,128]{1,0:T(8,128)S(1)}, f32[8,128]{1,0:T(8,128)S(1)}, u32[]{:S(2)}, u32[]{:S(2)}) collective-permute-start(f32[8,128]{1,0:T(8,128)S(1)} %get-tuple-element.51), channel_id=1, source_target_pairs={{0,1},{1,0},{2,3},{3,2},{4,5},{5,4},{6,7},{7,6},{8,9},{9,8},{10,11... | collective-permute-start | bytes 12296 | tf_op jit(solution)/shard_map/ppermute | solution.py:223
  51.2 5.5 %collective-permute-start.12 = (f32[8,128]{1,0:T(8,128)S(1)}, f32[8,128]{1,0:T(8,128)S(1)}, u32[]{:S(2)}, u32[]{:S(2)}) collective-permute-start(f32[8,128]{1,0:T(8,128)S(1)} %get-tuple-element.52), channel_id=1, source_target_pairs={{0,3},{1,2},{2,1},{3,0},{4,7},{5,6},{6,5},{7,4},{8,11},{9,10},{10,... | collective-permute-start | bytes 12296 | tf_op jit(solution)/shard_map/ppermute | solution.py:223

commit v26 on v23

--- a/solution.py
+++ b/solution.py
@@ -199,7 +199,7 @@
     )(*operands)
 
 
-BEHIND = 2
+BEHIND = 3
 FIRST_CUT = 128
 
 

time: 57.2 us -> 57.5 us (level)
  waiting for transfers between devices: 26.7 us -> 28.1 us
  starting transfers between devices: 17.9 us -> 17.1 us
    ppermute x13, waiting for transfers between devices: 26.7 us -> 28.1 us  [send(): return lax.ppermute(array, slot[0], pairs(slot[1], sizes[slot[0]]))]
    ppermute x13, starting transfers between devices: 17.9 us -> 17.1 us  [send(): return lax.ppermute(array, slot[0], pairs(slot[1], sizes[slot[0]]))]
  transfers between devices with their start and end apart: 13 -> 13, of which waited for: 5 -> 4; matrix products, arithmetic and copies ran while one was open for 0% -> 0% of each run, Pallas kernels for 16% -> 15%
where the time goes in v26:
time: 57.5 us; the launch traced here: 57.4 us
  waiting for transfers between devices  28.1 us (49%)
  starting transfers between devices  17.1 us (30%)
  Pallas kernels  11.5 us (20%)
  other arithmetic  0.6 us (1%)
    ppermute x13, waiting for transfers between devices, send(): return lax.ppermute(array, slot[0], pairs(slot[1], sizes[slot[0]]))  28.1 us
    ppermute x13, starting transfers between devices, send(): return lax.ppermute(array, slot[0], pairs(slot[1], sizes[slot[0]]))  17.1 us
    pallas_call x7, Pallas kernels, work(): pl.pallas_call(functools.partial(slot_kernel, place, *slot[2:], [one for...  6.3 us
    pallas_call x1, Pallas kernels, first_rows(): pl.pallas_call(functools.partial(first_kernel, slots), out_shape=[jax.Sha...  2.6 us
    pallas_call x1, Pallas kernels, prepare(): pl.pallas_call(functools.partial(prepare_kernel, slots), out_shape=[jax.S...  1.77 us
  transfers between devices with their start and end apart: 13, of which 4 were waited for; matrix products, arithmetic and copies ran while one was open for 0% of the time, Pallas kernels for 15%

profile of v26, /device:TPU:0, one launch (start us, length us, event | category | flops | bytes accessed | tf_op | source)
XLA Modules:
  0.0 57.4 jit_solution(14797288806988425178)
XLA Ops:
  0.0 0.0 copy-start
  0.0 0.0 copy-start.2
  0.0 0.0 copy-start.1
  0.0 0.0 copy-start.3
  0.0 0.0 copy-start.4
  0.0 2.6 %shard_map.57 = (bf16[256,1024]{1,0:T(8,128)(2,1)}, bf16[256,1024]{1,0:T(8,128)(2,1)}) custom-call(s32[1,4]{1,0:T(1,128)} %pick_blk.5, s32[4,4]{1,0:T(4,128)} %pick_sub.5, bf16[1024,1024]{1,0:T(8,128)(2,1)} %embeds.5), custom_call_target="tpu_custom_call" | custom-call | tf_op jit(solution)/shard_map/pallas_call | solution.py:81
  2.6 0.5 collective-permute-start.6
  3.2 3.7 %collective-permute-start.5 = (bf16[256,1024]{1,0:T(8,128)(2,1)}, bf16[256,1024]{1,0:T(8,128)(2,1)S(1)}, u32[]{:S(2)}, u32[]{:S(2)}) collective-permute-start(bf16[256,1024]{1,0:T(8,128)(2,1)} %get-tuple-element.37), channel_id=1, source_target_pairs={{0,2},{1,3},{2,0},{3,1},{4,6},{5,7},{6,4},{7,5},{8,10},{9,11},{10,... | collective-permute-start | bytes 1572872 | tf_op jit(solution)/shard_map/ppermute | solution.py:223
  6.8 0.0 copy-done
  6.8 0.0 copy-done.2
  6.8 0.0 copy-done.1
  6.8 0.8 %shard_map.55 = (bf16[256,1024]{1,0:T(8,128)(2,1)S(1)}, bf16[256,1024]{1,0:T(8,128)(2,1)S(1)}, bf16[256,1024]{1,0:T(8,128)(2,1)S(1)}, bf16[128,1024]{1,0:T(8,128)(2,1)S(1)}, bf16[128,1024]{1,0:T(8,128)(2,1)S(1)}) custom-call(s32[1,4]{1,0:T(1,128)S(1)} %copy-done.2, s32[4,4]{1,0:T(4,128)S(1)} %copy-done.1, bf16[1024,1024]{1,0:T(8,128)(2,1)S(1)} %copy-done), custom_call_target="tpu_custom_call" | custom-call | tf_op jit(solution)/shard_map/pallas_call | solution.py:118
  7.7 1.6 %collective-permute-start.4 = (bf16[256,1024]{1,0:T(8,128)(2,1)S(1)}, bf16[256,1024]{1,0:T(8,128)(2,1)S(1)}, u32[]{:S(2)}, u32[]{:S(2)}) collective-permute-start(bf16[256,1024]{1,0:T(8,128)(2,1)S(1)} %get-tuple-element.36), channel_id=1, source_target_pairs={{0,8},{4,12},{8,0},{12,4},{1,9},{5,13},{9,1},{13,5},{2,10},{6,14},... | collective-permute-start | bytes 1572872 | tf_op jit(solution)/shard_map/ppermute | solution.py:223
  9.2 1.6 %collective-permute-start.3 = (bf16[256,1024]{1,0:T(8,128)(2,1)S(1)}, bf16[256,1024]{1,0:T(8,128)(2,1)S(1)}, u32[]{:S(2)}, u32[]{:S(2)}) collective-permute-start(bf16[256,1024]{1,0:T(8,128)(2,1)S(1)} %get-tuple-element.35), channel_id=1, source_target_pairs={{0,1},{1,0},{2,3},{3,2},{4,5},{5,4},{6,7},{7,6},{8,9},{9,8},{10,11... | collective-permute-start | bytes 1572872 | tf_op jit(solution)/shard_map/ppermute | solution.py:223
  10.8 0.0 collective-permute-start.2
  10.8 0.0 collective-permute-done.6.arrived
  10.8 0.2 collective-permute-start.1
  11.0 20.1 %collective-permute-done.5.arrived = bf16[256,1024]{1,0:T(8,128)(2,1)S(1)} collective-permute-done((bf16[256,1024]{1,0:T(8,128)(2,1)}, bf16[256,1024]{1,0:T(8,128)(2,1)S(1)}, u32[]{:S(2)}, u32[]{:S(2)}) %collective-permute-start.5) | collective-permute-done | bytes 524320 | tf_op jit(solution)/shard_map/ppermute | solution.py:223
  31.1 3.8 %collective-permute-start = (bf16[128,1024]{1,0:T(8,128)(2,1)S(1)}, bf16[128,1024]{1,0:T(8,128)(2,1)S(1)}, u32[]{:S(2)}, u32[]{:S(2)}) collective-permute-start(bf16[128,1024]{1,0:T(8,128)(2,1)S(1)} %get-tuple-element.29), channel_id=1, source_target_pairs={{0,3},{1,2},{2,1},{3,0},{4,7},{5,6},{6,5},{7,4},{8,11},{9,10},{10,... | collective-permute-start | bytes 786440 | tf_op jit(solution)/shard_map/ppermute | solution.py:223
  34.9 0.0 copy-done.3
  34.9 0.0 copy-done.4
  34.9 1.8 %shard_map.56 = (bf16[1024,1024]{1,0:T(8,128)(2,1)S(1)}, f32[7,4,128]{2,1,0:T(4,128)S(1)}, f32[7,8,128]{2,1,0:T(8,128)S(1)}) custom-call(s32[1,4]{1,0:T(1,128)S(1)} %copy-done.2, s32[4,4]{1,0:T(4,128)S(1)} %copy-done.1, s32[1,16]{1,0:T(1,128)S(1)} %copy-done.3, s32[1,16]{1,0:T(1,128)S(1)} %copy-done.4, bf16[1024,1024]{1,0:T(8,128)(2,1)S(1)} %copy-done), custom_call_target="tpu_custom_call" | custom-call | tf_op jit(solution)/shard_map/pallas_call | solution.py:150
  36.7 1.0 %shard_map.58 = (f32[8,128]{1,0:T(8,128)S(1)}, f32[8,128]{1,0:T(8,128)S(1)}) custom-call(bf16[256,1024]{1,0:T(8,128)(2,1)S(1)} %collective-permute-done.6.arrived, bf16[1024,1024]{1,0:T(8,128)(2,1)S(1)} %get-tuple-element.30.units, f32[7,4,128]{2,1,0:T(4,128)S(1)} %get-tuple-element.31.live, f32[7,8,128]{2,1,0:T(8,128)S(1)} %get-tuple-element.32.mine, ...), custom_call_target="tpu_custom_call" | custom-call | tf_op jit(solution)/shard_map/pallas_call | solution.py:193
  37.7 0.0 collective-permute-done.4.arrived
  37.7 0.1 collective-permute-start.7
  37.8 1.0 %shard_map.59 = (f32[8,128]{1,0:T(8,128)S(1)}, f32[8,128]{1,0:T(8,128)S(1)}) custom-call(bf16[256,1024]{1,0:T(8,128)(2,1)S(1)} %collective-permute-done.5.arrived, bf16[1024,1024]{1,0:T(8,128)(2,1)S(1)} %get-tuple-element.30.units, f32[7,4,128]{2,1,0:T(4,128)S(1)} %get-tuple-element.31.live, f32[7,8,128]{2,1,0:T(8,128)S(1)} %get-tuple-element.32.mine, ...), custom_call_target="tpu_custom_call" | custom-call | tf_op jit(solution)/shard_map/pallas_call | solution.py:193
  38.8 1.0 %shard_map.60 = (f32[8,128]{1,0:T(8,128)S(1)}, f32[8,128]{1,0:T(8,128)S(1)}) custom-call(bf16[256,1024]{1,0:T(8,128)(2,1)S(1)} %collective-permute-done.4.arrived, bf16[1024,1024]{1,0:T(8,128)(2,1)S(1)} %get-tuple-element.30.units, f32[7,4,128]{2,1,0:T(4,128)S(1)} %get-tuple-element.31.live, f32[7,8,128]{2,1,0:T(8,128)S(1)} %get-tuple-element.32.mine, ...), custom_call_target="tpu_custom_call" | custom-call | tf_op jit(solution)/shard_map/pallas_call | solution.py:193
  39.8 4.4 %collective-permute-done.3.arrived = bf16[256,1024]{1,0:T(8,128)(2,1)S(1)} collective-permute-done((bf16[256,1024]{1,0:T(8,128)(2,1)S(1)}, bf16[256,1024]{1,0:T(8,128)(2,1)S(1)}, u32[]{:S(2)}, u32[]{:S(2)}) %collective-permute-start.3) | collective-permute-done | bytes 524320 | tf_op jit(solution)/shard_map/ppermute | solution.py:223
  44.2 0.6 %collective-permute-start.8 = (f32[8,128]{1,0:T(8,128)S(1)}, f32[8,128]{1,0:T(8,128)S(1)}, u32[]{:S(2)}, u32[]{:S(2)}) collective-permute-start(f32[8,128]{1,0:T(8,128)S(1)} %get-tuple-element.45), channel_id=1, source_target_pairs={{0,8},{4,12},{8,0},{12,4},{1,9},{5,13},{9,1},{13,5},{2,10},{6,14},... | collective-permute-start | bytes 12296 | tf_op jit(solution)/shard_map/ppermute | solution.py:223
  44.8 0.0 collective-permute-done.7.rest_0_
  44.8 1.0 %shard_map.61 = (f32[8,128]{1,0:T(8,128)S(1)}, f32[8,128]{1,0:T(8,128)S(1)}) custom-call(bf16[256,1024]{1,0:T(8,128)(2,1)S(1)} %collective-permute-done.3.arrived, bf16[1024,1024]{1,0:T(8,128)(2,1)S(1)} %get-tuple-element.30.units, f32[7,4,128]{2,1,0:T(4,128)S(1)} %get-tuple-element.31.live, f32[7,8,128]{2,1,0:T(8,128)S(1)} %get-tuple-element.32.mine, ...), custom_call_target="tpu_custom_call" | custom-call | tf_op jit(solution)/shard_map/pallas_call | solution.py:193
  45.8 0.0 collective-permute-done.2.arrived
  45.8 1.0 %shard_map.62 = (f32[8,128]{1,0:T(8,128)S(1)}, f32[8,128]{1,0:T(8,128)S(1)}) custom-call(bf16[256,1024]{1,0:T(8,128)(2,1)S(1)} %collective-permute-done.2.arrived, bf16[1024,1024]{1,0:T(8,128)(2,1)S(1)} %get-tuple-element.30.units, f32[7,4,128]{2,1,0:T(4,128)S(1)} %get-tuple-element.31.live, f32[7,8,128]{2,1,0:T(8,128)S(1)} %get-tuple-element.32.mine, ...), custom_call_target="tpu_custom_call" | custom-call | tf_op jit(solution)/shard_map/pallas_call | solution.py:193
  46.8 0.1 collective-permute-start.9
  46.9 0.1 collective-permute-start.10
  47.0 0.0 collective-permute-done.1.arrived
  47.0 3.0 %collective-permute-start.11 = (f32[8,128]{1,0:T(8,128)S(1)}, f32[8,128]{1,0:T(8,128)S(1)}, u32[]{:S(2)}, u32[]{:S(2)}) collective-permute-start(f32[8,128]{1,0:T(8,128)S(1)} %get-tuple-element.51), channel_id=1, source_target_pairs={{0,1},{1,0},{2,3},{3,2},{4,5},{5,4},{6,7},{7,6},{8,9},{9,8},{10,11... | collective-permute-start | bytes 12296 | tf_op jit(solution)/shard_map/ppermute | solution.py:223
  50.0 0.0 collective-permute-done.8.rest_0_
  50.0 0.7 %shard_map.63 = (f32[8,128]{1,0:T(8,128)S(1)}, f32[8,128]{1,0:T(8,128)S(1)}) custom-call(bf16[128,1024]{1,0:T(8,128)(2,1)S(1)} %collective-permute-done.1.arrived, bf16[1024,1024]{1,0:T(8,128)(2,1)S(1)} %get-tuple-element.30.units, f32[7,4,128]{2,1,0:T(4,128)S(1)} %get-tuple-element.31.live, f32[7,8,128]{2,1,0:T(8,128)S(1)} %get-tuple-element.32.mine, ...), custom_call_target="tpu_custom_call" | custom-call | tf_op jit(solution)/shard_map/pallas_call | solution.py:193
  50.7 0.0 collective-permute-done.arrived
  50.7 0.0 collective-permute-done.9.rest_0_
  50.7 0.7 %shard_map.64 = (f32[8,128]{1,0:T(8,128)S(1)}, f32[8,128]{1,0:T(8,128)S(1)}) custom-call(bf16[128,1024]{1,0:T(8,128)(2,1)S(1)} %collective-permute-done.arrived, bf16[1024,1024]{1,0:T(8,128)(2,1)S(1)} %get-tuple-element.30.units, f32[7,4,128]{2,1,0:T(4,128)S(1)} %get-tuple-element.31.live, f32[7,8,128]{2,1,0:T(8,128)S(1)} %get-tuple-element.32.mine, ...), custom_call_target="tpu_custom_call" | custom-call | tf_op jit(solution)/shard_map/pallas_call | solution.py:193
  51.3 1.9 %collective-permute-start.12 = (f32[8,128]{1,0:T(8,128)S(1)}, f32[8,128]{1,0:T(8,128)S(1)}, u32[]{:S(2)}, u32[]{:S(2)}) collective-permute-start(f32[8,128]{1,0:T(8,128)S(1)} %get-tuple-element.52), channel_id=1, source_target_pairs={{0,3},{1,2},{2,1},{3,0},{4,7},{5,6},{6,5},{7,4},{8,11},{9,10},{10,... | collective-permute-start | bytes 12296 | tf_op jit(solution)/shard_map/ppermute | solution.py:223
  53.2 0.2 collective-permute-done.10
  53.5 0.0 collective-permute-done.11
  53.5 3.3 %collective-permute-done.12 = f32[8,128]{1,0:T(8,128)S(1)} collective-permute-done((f32[8,128]{1,0:T(8,128)S(1)}, f32[8,128]{1,0:T(8,128)S(1)}, u32[]{:S(2)}, u32[]{:S(2)}) %collective-permute-start.12) | collective-permute-done | bytes 4128 | tf_op jit(solution)/shard_map/ppermute | solution.py:223
  56.8 0.6 %fusion.2 = f32[1024]{0:T(1024)} fusion(f32[8,128]{1,0:T(8,128)S(1)} %collective-permute-done.12, f32[8,128]{1,0:T(8,128)S(1)} %collective-permute-done.11, f32[8,128]{1,0:T(8,128)S(1)} %get-tuple-element.49, f32[8,128]{1,0:T(8,128)S(1)} %collective-permute-done.10, f32[7,8,128]{2,1,0:T(8,128)S(1)} %get-tuple-element.32.mine), kind=kLoop, calls=%fused_computation.3 | loop fusion | flops 7168 | bytes 32768 | tf_op jit(solution)/shard_map/reshape | solution.py:249
  (1 shorter events, 0.0 us)
Async XLA Ops:
  0.0 6.8 %copy-start = (bf16[1024,1024]{1,0:T(8,128)(2,1)S(1)}, bf16[1024,1024]{1,0:T(8,128)(2,1)}, u32[]{:S(2)}) copy-start(bf16[1024,1024]{1,0:T(8,128)(2,1)} %embeds.5) | copy-start | bytes 6291460
  0.0 6.8 %copy-start.2 = (s32[1,4]{1,0:T(1,128)S(1)}, s32[1,4]{1,0:T(1,128)}, u32[]{:S(2)}) copy-start(s32[1,4]{1,0:T(1,128)} %pick_blk.5) | copy-start | bytes 52
  0.0 6.8 %copy-start.1 = (s32[4,4]{1,0:T(4,128)S(1)}, s32[4,4]{1,0:T(4,128)}, u32[]{:S(2)}) copy-start(s32[4,4]{1,0:T(4,128)} %pick_sub.5) | copy-start | bytes 196
  0.0 34.9 %copy-start.3 = (s32[1,16]{1,0:T(1,128)S(1)}, s32[1,16]{1,0:T(1,128)}, u32[]{:S(2)}) copy-start(s32[1,16]{1,0:T(1,128)} %mask_blk.1) | copy-start | bytes 196
  0.0 34.9 %copy-start.4 = (s32[1,16]{1,0:T(1,128)S(1)}, s32[1,16]{1,0:T(1,128)}, u32[]{:S(2)}) copy-start(s32[1,16]{1,0:T(1,128)} %mask_sub.1) | copy-start | bytes 196
  2.6 8.2 %collective-permute-start.6 = (bf16[256,1024]{1,0:T(8,128)(2,1)}, bf16[256,1024]{1,0:T(8,128)(2,1)S(1)}, u32[]{:S(2)}, u32[]{:S(2)}) collective-permute-start(bf16[256,1024]{1,0:T(8,128)(2,1)} %get-tuple-element.38), channel_id=1, source_target_pairs={{0,4},{4,0},{8,12},{12,8},{1,5},{5,1},{9,13},{13,9},{2,6},{6,2},{1... | collective-permute-start | bytes 1572872 | tf_op jit(solution)/shard_map/ppermute | solution.py:223
  3.2 27.9 %collective-permute-start.5 = (bf16[256,1024]{1,0:T(8,128)(2,1)}, bf16[256,1024]{1,0:T(8,128)(2,1)S(1)}, u32[]{:S(2)}, u32[]{:S(2)}) collective-permute-start(bf16[256,1024]{1,0:T(8,128)(2,1)} %get-tuple-element.37), channel_id=1, source_target_pairs={{0,2},{1,3},{2,0},{3,1},{4,6},{5,7},{6,4},{7,5},{8,10},{9,11},{10,... | collective-permute-start | bytes 1572872 | tf_op jit(solution)/shard_map/ppermute | solution.py:223
  7.7 30.0 %collective-permute-start.4 = (bf16[256,1024]{1,0:T(8,128)(2,1)S(1)}, bf16[256,1024]{1,0:T(8,128)(2,1)S(1)}, u32[]{:S(2)}, u32[]{:S(2)}) collective-permute-start(bf16[256,1024]{1,0:T(8,128)(2,1)S(1)} %get-tuple-element.36), channel_id=1, source_target_pairs={{0,8},{4,12},{8,0},{12,4},{1,9},{5,13},{9,1},{13,5},{2,10},{6,14},... | collective-permute-start | bytes 1572872 | tf_op jit(solution)/shard_map/ppermute | solution.py:223
  9.2 35.0 %collective-permute-start.3 = (bf16[256,1024]{1,0:T(8,128)(2,1)S(1)}, bf16[256,1024]{1,0:T(8,128)(2,1)S(1)}, u32[]{:S(2)}, u32[]{:S(2)}) collective-permute-start(bf16[256,1024]{1,0:T(8,128)(2,1)S(1)} %get-tuple-element.35), channel_id=1, source_target_pairs={{0,1},{1,0},{2,3},{3,2},{4,5},{5,4},{6,7},{7,6},{8,9},{9,8},{10,11... | collective-permute-start | bytes 1572872 | tf_op jit(solution)/shard_map/ppermute | solution.py:223
  10.8 35.0 %collective-permute-start.2 = (bf16[256,1024]{1,0:T(8,128)(2,1)S(1)}, bf16[256,1024]{1,0:T(8,128)(2,1)S(1)}, u32[]{:S(2)}, u32[]{:S(2)}) collective-permute-start(bf16[256,1024]{1,0:T(8,128)(2,1)S(1)} %get-tuple-element.34), channel_id=1, source_target_pairs={{0,12},{4,8},{8,4},{12,0},{1,13},{5,9},{9,5},{13,1},{2,14},{6,10},... | collective-permute-start | bytes 1572872 | tf_op jit(solution)/shard_map/ppermute | solution.py:223
  10.8 36.2 %collective-permute-start.1 = (bf16[128,1024]{1,0:T(8,128)(2,1)S(1)}, bf16[128,1024]{1,0:T(8,128)(2,1)S(1)}, u32[]{:S(2)}, u32[]{:S(2)}) collective-permute-start(bf16[128,1024]{1,0:T(8,128)(2,1)S(1)} %get-tuple-element.33), channel_id=1, source_target_pairs={{0,3},{1,2},{2,1},{3,0},{4,7},{5,6},{6,5},{7,4},{8,11},{9,10},{10,... | collective-permute-start | bytes 786440 | tf_op jit(solution)/shard_map/ppermute | solution.py:223
  31.1 19.6 %collective-permute-start = (bf16[128,1024]{1,0:T(8,128)(2,1)S(1)}, bf16[128,1024]{1,0:T(8,128)(2,1)S(1)}, u32[]{:S(2)}, u32[]{:S(2)}) collective-permute-start(bf16[128,1024]{1,0:T(8,128)(2,1)S(1)} %get-tuple-element.29), channel_id=1, source_target_pairs={{0,3},{1,2},{2,1},{3,0},{4,7},{5,6},{6,5},{7,4},{8,11},{9,10},{10,... | collective-permute-start | bytes 786440 | tf_op jit(solution)/shard_map/ppermute | solution.py:223
  37.7 7.1 %collective-permute-start.7 = (f32[8,128]{1,0:T(8,128)S(1)}, f32[8,128]{1,0:T(8,128)S(1)}, u32[]{:S(2)}, u32[]{:S(2)}) collective-permute-start(f32[8,128]{1,0:T(8,128)S(1)} %get-tuple-element.42), channel_id=1, source_target_pairs={{0,4},{4,0},{8,12},{12,8},{1,5},{5,1},{9,13},{13,9},{2,6},{6,2},{1... | collective-permute-start | bytes 12296 | tf_op jit(solution)/shard_map/ppermute | solution.py:223
  44.2 5.8 %collective-permute-start.8 = (f32[8,128]{1,0:T(8,128)S(1)}, f32[8,128]{1,0:T(8,128)S(1)}, u32[]{:S(2)}, u32[]{:S(2)}) collective-permute-start(f32[8,128]{1,0:T(8,128)S(1)} %get-tuple-element.45), channel_id=1, source_target_pairs={{0,8},{4,12},{8,0},{12,4},{1,9},{5,13},{9,1},{13,5},{2,10},{6,14},... | collective-permute-start | bytes 12296 | tf_op jit(solution)/shard_map/ppermute | solution.py:223
  46.8 3.8 %collective-permute-start.9 = (f32[8,128]{1,0:T(8,128)S(1)}, f32[8,128]{1,0:T(8,128)S(1)}, u32[]{:S(2)}, u32[]{:S(2)}) collective-permute-start(f32[8,128]{1,0:T(8,128)S(1)} %get-tuple-element.47), channel_id=1, source_target_pairs={{0,12},{4,8},{8,4},{12,0},{1,13},{5,9},{9,5},{13,1},{2,14},{6,10},... | collective-permute-start | bytes 12296 | tf_op jit(solution)/shard_map/ppermute | solution.py:223
  46.9 6.6 %collective-permute-start.10 = (f32[8,128]{1,0:T(8,128)S(1)}, f32[8,128]{1,0:T(8,128)S(1)}, u32[]{:S(2)}, u32[]{:S(2)}) collective-permute-start(f32[8,128]{1,0:T(8,128)S(1)} %get-tuple-element.50), channel_id=1, source_target_pairs={{0,2},{1,3},{2,0},{3,1},{4,6},{5,7},{6,4},{7,5},{8,10},{9,11},{10,... | collective-permute-start | bytes 12296 | tf_op jit(solution)/shard_map/ppermute | solution.py:223
  47.0 6.5 %collective-permute-start.11 = (f32[8,128]{1,0:T(8,128)S(1)}, f32[8,128]{1,0:T(8,128)S(1)}, u32[]{:S(2)}, u32[]{:S(2)}) collective-permute-start(f32[8,128]{1,0:T(8,128)S(1)} %get-tuple-element.51), channel_id=1, source_target_pairs={{0,1},{1,0},{2,3},{3,2},{4,5},{5,4},{6,7},{7,6},{8,9},{9,8},{10,11... | collective-permute-start | bytes 12296 | tf_op jit(solution)/shard_map/ppermute | solution.py:223
  51.3 5.5 %collective-permute-start.12 = (f32[8,128]{1,0:T(8,128)S(1)}, f32[8,128]{1,0:T(8,128)S(1)}, u32[]{:S(2)}, u32[]{:S(2)}) collective-permute-start(f32[8,128]{1,0:T(8,128)S(1)} %get-tuple-element.52), channel_id=1, source_target_pairs={{0,3},{1,2},{2,1},{3,0},{4,7},{5,6},{6,5},{7,4},{8,11},{9,10},{10,... | collective-permute-start | bytes 12296 | tf_op jit(solution)/shard_map/ppermute | solution.py:223

commit v27 on v19

--- a/solution.py
+++ b/solution.py
@@ -73,7 +73,7 @@
         copy.wait()
 
 
-PART = 128
+PART = 256
 
 
 def first_rows(slots, pick_blk, pick_sub, embeds):

time: 57.1 us -> 57.2 us (level)
  no operation moved by 1% of the time
where the time goes in v27:
time: 57.2 us; the launch traced here: 56.1 us
  waiting for transfers between devices  22.4 us (39%)
  starting transfers between devices  21.4 us (37%)
  Pallas kernels  11.6 us (20%)
  other arithmetic  0.6 us (1%)
    ppermute x13, waiting for transfers between devices, send(): return lax.ppermute(array, slot[0], pairs(slot[1], sizes[slot[0]]))  22.4 us
    ppermute x13, starting transfers between devices, send(): return lax.ppermute(array, slot[0], pairs(slot[1], sizes[slot[0]]))  21.4 us
    pallas_call x7, Pallas kernels, work(): pl.pallas_call(functools.partial(slot_kernel, place, *slot[2:], [one for...  6.29 us
    pallas_call x1, Pallas kernels, first_rows(): pl.pallas_call(functools.partial(first_kernel, slots), out_shape=[jax.Sha...  2.74 us
    pallas_call x1, Pallas kernels, prepare(): pl.pallas_call(functools.partial(prepare_kernel, slots), out_shape=[jax.S...  1.77 us
  transfers between devices with their start and end apart: 13, of which 4 were waited for; matrix products, arithmetic and copies ran while one was open for 0% of the time, Pallas kernels for 16%

profile of v27, /device:TPU:0, one launch (start us, length us, event | category | flops | bytes accessed | tf_op | source)
XLA Modules:
  0.0 56.1 jit_solution(13016740306339007976)
XLA Ops:
  0.0 0.0 copy-start
  0.0 0.0 copy-start.2
  0.0 0.0 copy-start.1
  0.0 0.0 copy-start.3
  0.0 0.0 copy-start.4
  0.0 2.7 %shard_map.57 = (bf16[256,1024]{1,0:T(8,128)(2,1)}, bf16[256,1024]{1,0:T(8,128)(2,1)}) custom-call(s32[1,4]{1,0:T(1,128)} %pick_blk.5, s32[4,4]{1,0:T(4,128)} %pick_sub.5, bf16[1024,1024]{1,0:T(8,128)(2,1)} %embeds.5), custom_call_target="tpu_custom_call" | custom-call | tf_op jit(solution)/shard_map/pallas_call | solution.py:81
  2.8 0.5 collective-permute-start.6
  3.3 3.7 %collective-permute-start.5 = (bf16[256,1024]{1,0:T(8,128)(2,1)}, bf16[256,1024]{1,0:T(8,128)(2,1)S(1)}, u32[]{:S(2)}, u32[]{:S(2)}) collective-permute-start(bf16[256,1024]{1,0:T(8,128)(2,1)} %get-tuple-element.37), channel_id=1, source_target_pairs={{0,2},{1,3},{2,0},{3,1},{4,6},{5,7},{6,4},{7,5},{8,10},{9,11},{10,... | collective-permute-start | bytes 1572872 | tf_op jit(solution)/shard_map/ppermute | solution.py:223
  7.0 0.0 copy-done
  7.0 0.0 copy-done.2
  7.0 0.0 copy-done.1
  7.0 0.8 %shard_map.55 = (bf16[256,1024]{1,0:T(8,128)(2,1)S(1)}, bf16[256,1024]{1,0:T(8,128)(2,1)S(1)}, bf16[256,1024]{1,0:T(8,128)(2,1)S(1)}, bf16[128,1024]{1,0:T(8,128)(2,1)S(1)}, bf16[128,1024]{1,0:T(8,128)(2,1)S(1)}) custom-call(s32[1,4]{1,0:T(1,128)S(1)} %copy-done.2, s32[4,4]{1,0:T(4,128)S(1)} %copy-done.1, bf16[1024,1024]{1,0:T(8,128)(2,1)S(1)} %copy-done), custom_call_target="tpu_custom_call" | custom-call | tf_op jit(solution)/shard_map/pallas_call | solution.py:118
  7.8 1.6 %collective-permute-start.4 = (bf16[256,1024]{1,0:T(8,128)(2,1)S(1)}, bf16[256,1024]{1,0:T(8,128)(2,1)S(1)}, u32[]{:S(2)}, u32[]{:S(2)}) collective-permute-start(bf16[256,1024]{1,0:T(8,128)(2,1)S(1)} %get-tuple-element.36), channel_id=1, source_target_pairs={{0,1},{1,0},{2,3},{3,2},{4,5},{5,4},{6,7},{7,6},{8,9},{9,8},{10,11... | collective-permute-start | bytes 1572872 | tf_op jit(solution)/shard_map/ppermute | solution.py:223
  9.4 1.5 %collective-permute-start.3 = (bf16[256,1024]{1,0:T(8,128)(2,1)S(1)}, bf16[256,1024]{1,0:T(8,128)(2,1)S(1)}, u32[]{:S(2)}, u32[]{:S(2)}) collective-permute-start(bf16[256,1024]{1,0:T(8,128)(2,1)S(1)} %get-tuple-element.35), channel_id=1, source_target_pairs={{0,8},{4,12},{8,0},{12,4},{1,9},{5,13},{9,1},{13,5},{2,10},{6,14},... | collective-permute-start | bytes 1572872 | tf_op jit(solution)/shard_map/ppermute | solution.py:223
  10.9 0.0 collective-permute-start.2
  10.9 0.0 collective-permute-done.6.arrived
  10.9 0.2 collective-permute-start.1
  11.2 20.1 %collective-permute-done.5.arrived = bf16[256,1024]{1,0:T(8,128)(2,1)S(1)} collective-permute-done((bf16[256,1024]{1,0:T(8,128)(2,1)}, bf16[256,1024]{1,0:T(8,128)(2,1)S(1)}, u32[]{:S(2)}, u32[]{:S(2)}) %collective-permute-start.5) | collective-permute-done | bytes 524320 | tf_op jit(solution)/shard_map/ppermute | solution.py:223
  31.2 3.7 %collective-permute-start = (bf16[128,1024]{1,0:T(8,128)(2,1)S(1)}, bf16[128,1024]{1,0:T(8,128)(2,1)S(1)}, u32[]{:S(2)}, u32[]{:S(2)}) collective-permute-start(bf16[128,1024]{1,0:T(8,128)(2,1)S(1)} %get-tuple-element.29), channel_id=1, source_target_pairs={{0,3},{1,2},{2,1},{3,0},{4,7},{5,6},{6,5},{7,4},{8,11},{9,10},{10,... | collective-permute-start | bytes 786440 | tf_op jit(solution)/shard_map/ppermute | solution.py:223
  35.0 0.0 copy-done.3
  35.0 0.0 copy-done.4
  35.0 1.8 %shard_map.56 = (bf16[1024,1024]{1,0:T(8,128)(2,1)S(1)}, f32[7,4,128]{2,1,0:T(4,128)S(1)}, f32[7,8,128]{2,1,0:T(8,128)S(1)}) custom-call(s32[1,4]{1,0:T(1,128)S(1)} %copy-done.2, s32[4,4]{1,0:T(4,128)S(1)} %copy-done.1, s32[1,16]{1,0:T(1,128)S(1)} %copy-done.3, s32[1,16]{1,0:T(1,128)S(1)} %copy-done.4, bf16[1024,1024]{1,0:T(8,128)(2,1)S(1)} %copy-done), custom_call_target="tpu_custom_call" | custom-call | tf_op jit(solution)/shard_map/pallas_call | solution.py:150
  36.8 1.0 %shard_map.58 = (f32[8,128]{1,0:T(8,128)S(1)}, f32[8,128]{1,0:T(8,128)S(1)}) custom-call(bf16[256,1024]{1,0:T(8,128)(2,1)S(1)} %collective-permute-done.6.arrived, bf16[1024,1024]{1,0:T(8,128)(2,1)S(1)} %get-tuple-element.30.units, f32[7,4,128]{2,1,0:T(4,128)S(1)} %get-tuple-element.31.live, f32[7,8,128]{2,1,0:T(8,128)S(1)} %get-tuple-element.32.mine, ...), custom_call_target="tpu_custom_call" | custom-call | tf_op jit(solution)/shard_map/pallas_call | solution.py:193
  37.8 0.0 collective-permute-done.4.arrived
  37.8 0.1 collective-permute-start.7
  37.9 1.0 %shard_map.59 = (f32[8,128]{1,0:T(8,128)S(1)}, f32[8,128]{1,0:T(8,128)S(1)}) custom-call(bf16[256,1024]{1,0:T(8,128)(2,1)S(1)} %collective-permute-done.5.arrived, bf16[1024,1024]{1,0:T(8,128)(2,1)S(1)} %get-tuple-element.30.units, f32[7,4,128]{2,1,0:T(4,128)S(1)} %get-tuple-element.31.live, f32[7,8,128]{2,1,0:T(8,128)S(1)} %get-tuple-element.32.mine, ...), custom_call_target="tpu_custom_call" | custom-call | tf_op jit(solution)/shard_map/pallas_call | solution.py:193
  38.8 0.2 collective-permute-done.7.rest_0_
  39.0 1.0 %shard_map.60 = (f32[8,128]{1,0:T(8,128)S(1)}, f32[8,128]{1,0:T(8,128)S(1)}) custom-call(bf16[256,1024]{1,0:T(8,128)(2,1)S(1)} %collective-permute-done.4.arrived, bf16[1024,1024]{1,0:T(8,128)(2,1)S(1)} %get-tuple-element.30.units, f32[7,4,128]{2,1,0:T(4,128)S(1)} %get-tuple-element.31.live, f32[7,8,128]{2,1,0:T(8,128)S(1)} %get-tuple-element.32.mine, ...), custom_call_target="tpu_custom_call" | custom-call | tf_op jit(solution)/shard_map/pallas_call | solution.py:193
  40.0 0.0 collective-permute-done.3.arrived
  40.0 1.0 %shard_map.61 = (f32[8,128]{1,0:T(8,128)S(1)}, f32[8,128]{1,0:T(8,128)S(1)}) custom-call(bf16[256,1024]{1,0:T(8,128)(2,1)S(1)} %collective-permute-done.3.arrived, bf16[1024,1024]{1,0:T(8,128)(2,1)S(1)} %get-tuple-element.30.units, f32[7,4,128]{2,1,0:T(4,128)S(1)} %get-tuple-element.31.live, f32[7,8,128]{2,1,0:T(8,128)S(1)} %get-tuple-element.32.mine, ...), custom_call_target="tpu_custom_call" | custom-call | tf_op jit(solution)/shard_map/pallas_call | solution.py:193
  41.0 1.6 %collective-permute-start.8 = (f32[8,128]{1,0:T(8,128)S(1)}, f32[8,128]{1,0:T(8,128)S(1)}, u32[]{:S(2)}, u32[]{:S(2)}) collective-permute-start(f32[8,128]{1,0:T(8,128)S(1)} %get-tuple-element.45), channel_id=1, source_target_pairs={{0,8},{4,12},{8,0},{12,4},{1,9},{5,13},{9,1},{13,5},{2,10},{6,14},... | collective-permute-start | bytes 12296 | tf_op jit(solution)/shard_map/ppermute | solution.py:223
  42.6 0.0 collective-permute-done.2.arrived
  42.6 1.0 %shard_map.62 = (f32[8,128]{1,0:T(8,128)S(1)}, f32[8,128]{1,0:T(8,128)S(1)}) custom-call(bf16[256,1024]{1,0:T(8,128)(2,1)S(1)} %collective-permute-done.2.arrived, bf16[1024,1024]{1,0:T(8,128)(2,1)S(1)} %get-tuple-element.30.units, f32[7,4,128]{2,1,0:T(4,128)S(1)} %get-tuple-element.31.live, f32[7,8,128]{2,1,0:T(8,128)S(1)} %get-tuple-element.32.mine, ...), custom_call_target="tpu_custom_call" | custom-call | tf_op jit(solution)/shard_map/pallas_call | solution.py:193
  43.6 0.3 collective-permute-start.9
  43.8 0.0 collective-permute-start.10
  43.8 0.0 collective-permute-done.1.arrived
  43.8 4.9 %collective-permute-start.11 = (f32[8,128]{1,0:T(8,128)S(1)}, f32[8,128]{1,0:T(8,128)S(1)}, u32[]{:S(2)}, u32[]{:S(2)}) collective-permute-start(f32[8,128]{1,0:T(8,128)S(1)} %get-tuple-element.51), channel_id=1, source_target_pairs={{0,1},{1,0},{2,3},{3,2},{4,5},{5,4},{6,7},{7,6},{8,9},{9,8},{10,11... | collective-permute-start | bytes 12296 | tf_op jit(solution)/shard_map/ppermute | solution.py:223
  48.7 0.0 collective-permute-done.8.rest_0_
  48.7 0.7 %shard_map.63 = (f32[8,128]{1,0:T(8,128)S(1)}, f32[8,128]{1,0:T(8,128)S(1)}) custom-call(bf16[128,1024]{1,0:T(8,128)(2,1)S(1)} %collective-permute-done.1.arrived, bf16[1024,1024]{1,0:T(8,128)(2,1)S(1)} %get-tuple-element.30.units, f32[7,4,128]{2,1,0:T(4,128)S(1)} %get-tuple-element.31.live, f32[7,8,128]{2,1,0:T(8,128)S(1)} %get-tuple-element.32.mine, ...), custom_call_target="tpu_custom_call" | custom-call | tf_op jit(solution)/shard_map/pallas_call | solution.py:193
  49.4 0.0 collective-permute-done.arrived
  49.4 0.0 collective-permute-done.9.rest_0_
  49.4 0.7 %shard_map.64 = (f32[8,128]{1,0:T(8,128)S(1)}, f32[8,128]{1,0:T(8,128)S(1)}) custom-call(bf16[128,1024]{1,0:T(8,128)(2,1)S(1)} %collective-permute-done.arrived, bf16[1024,1024]{1,0:T(8,128)(2,1)S(1)} %get-tuple-element.30.units, f32[7,4,128]{2,1,0:T(4,128)S(1)} %get-tuple-element.31.live, f32[7,8,128]{2,1,0:T(8,128)S(1)} %get-tuple-element.32.mine, ...), custom_call_target="tpu_custom_call" | custom-call | tf_op jit(solution)/shard_map/pallas_call | solution.py:193
  50.1 3.4 %collective-permute-start.12 = (f32[8,128]{1,0:T(8,128)S(1)}, f32[8,128]{1,0:T(8,128)S(1)}, u32[]{:S(2)}, u32[]{:S(2)}) collective-permute-start(f32[8,128]{1,0:T(8,128)S(1)} %get-tuple-element.52), channel_id=1, source_target_pairs={{0,3},{1,2},{2,1},{3,0},{4,7},{5,6},{6,5},{7,4},{8,11},{9,10},{10,... | collective-permute-start | bytes 12296 | tf_op jit(solution)/shard_map/ppermute | solution.py:223
  53.4 0.2 collective-permute-done.10
  53.6 0.0 collective-permute-done.11
  53.6 1.9 %collective-permute-done.12 = f32[8,128]{1,0:T(8,128)S(1)} collective-permute-done((f32[8,128]{1,0:T(8,128)S(1)}, f32[8,128]{1,0:T(8,128)S(1)}, u32[]{:S(2)}, u32[]{:S(2)}) %collective-permute-start.12) | collective-permute-done | bytes 4128 | tf_op jit(solution)/shard_map/ppermute | solution.py:223
  55.5 0.6 %fusion.2 = f32[1024]{0:T(1024)} fusion(f32[8,128]{1,0:T(8,128)S(1)} %collective-permute-done.12, f32[8,128]{1,0:T(8,128)S(1)} %collective-permute-done.11, f32[8,128]{1,0:T(8,128)S(1)} %get-tuple-element.49, f32[8,128]{1,0:T(8,128)S(1)} %collective-permute-done.10, f32[7,8,128]{2,1,0:T(8,128)S(1)} %get-tuple-element.32.mine), kind=kLoop, calls=%fused_computation.3 | loop fusion | flops 7168 | bytes 32768 | tf_op jit(solution)/shard_map/reshape | solution.py:249
  (1 shorter events, 0.0 us)
Async XLA Ops:
  0.0 7.0 %copy-start = (bf16[1024,1024]{1,0:T(8,128)(2,1)S(1)}, bf16[1024,1024]{1,0:T(8,128)(2,1)}, u32[]{:S(2)}) copy-start(bf16[1024,1024]{1,0:T(8,128)(2,1)} %embeds.5) | copy-start | bytes 6291460
  0.0 7.0 %copy-start.2 = (s32[1,4]{1,0:T(1,128)S(1)}, s32[1,4]{1,0:T(1,128)}, u32[]{:S(2)}) copy-start(s32[1,4]{1,0:T(1,128)} %pick_blk.5) | copy-start | bytes 52
  0.0 7.0 %copy-start.1 = (s32[4,4]{1,0:T(4,128)S(1)}, s32[4,4]{1,0:T(4,128)}, u32[]{:S(2)}) copy-start(s32[4,4]{1,0:T(4,128)} %pick_sub.5) | copy-start | bytes 196
  0.0 35.0 %copy-start.3 = (s32[1,16]{1,0:T(1,128)S(1)}, s32[1,16]{1,0:T(1,128)}, u32[]{:S(2)}) copy-start(s32[1,16]{1,0:T(1,128)} %mask_blk.1) | copy-start | bytes 196
  0.0 35.0 %copy-start.4 = (s32[1,16]{1,0:T(1,128)S(1)}, s32[1,16]{1,0:T(1,128)}, u32[]{:S(2)}) copy-start(s32[1,16]{1,0:T(1,128)} %mask_sub.1) | copy-start | bytes 196
  2.8 8.2 %collective-permute-start.6 = (bf16[256,1024]{1,0:T(8,128)(2,1)}, bf16[256,1024]{1,0:T(8,128)(2,1)S(1)}, u32[]{:S(2)}, u32[]{:S(2)}) collective-permute-start(bf16[256,1024]{1,0:T(8,128)(2,1)} %get-tuple-element.38), channel_id=1, source_target_pairs={{0,4},{4,0},{8,12},{12,8},{1,5},{5,1},{9,13},{13,9},{2,6},{6,2},{1... | collective-permute-start | bytes 1572872 | tf_op jit(solution)/shard_map/ppermute | solution.py:223
  3.3 27.9 %collective-permute-start.5 = (bf16[256,1024]{1,0:T(8,128)(2,1)}, bf16[256,1024]{1,0:T(8,128)(2,1)S(1)}, u32[]{:S(2)}, u32[]{:S(2)}) collective-permute-start(bf16[256,1024]{1,0:T(8,128)(2,1)} %get-tuple-element.37), channel_id=1, source_target_pairs={{0,2},{1,3},{2,0},{3,1},{4,6},{5,7},{6,4},{7,5},{8,10},{9,11},{10,... | collective-permute-start | bytes 1572872 | tf_op jit(solution)/shard_map/ppermute | solution.py:223
  7.8 30.0 %collective-permute-start.4 = (bf16[256,1024]{1,0:T(8,128)(2,1)S(1)}, bf16[256,1024]{1,0:T(8,128)(2,1)S(1)}, u32[]{:S(2)}, u32[]{:S(2)}) collective-permute-start(bf16[256,1024]{1,0:T(8,128)(2,1)S(1)} %get-tuple-element.36), channel_id=1, source_target_pairs={{0,1},{1,0},{2,3},{3,2},{4,5},{5,4},{6,7},{7,6},{8,9},{9,8},{10,11... | collective-permute-start | bytes 1572872 | tf_op jit(solution)/shard_map/ppermute | solution.py:223
  9.4 30.6 %collective-permute-start.3 = (bf16[256,1024]{1,0:T(8,128)(2,1)S(1)}, bf16[256,1024]{1,0:T(8,128)(2,1)S(1)}, u32[]{:S(2)}, u32[]{:S(2)}) collective-permute-start(bf16[256,1024]{1,0:T(8,128)(2,1)S(1)} %get-tuple-element.35), channel_id=1, source_target_pairs={{0,8},{4,12},{8,0},{12,4},{1,9},{5,13},{9,1},{13,5},{2,10},{6,14},... | collective-permute-start | bytes 1572872 | tf_op jit(solution)/shard_map/ppermute | solution.py:223
  10.9 31.6 %collective-permute-start.2 = (bf16[256,1024]{1,0:T(8,128)(2,1)S(1)}, bf16[256,1024]{1,0:T(8,128)(2,1)S(1)}, u32[]{:S(2)}, u32[]{:S(2)}) collective-permute-start(bf16[256,1024]{1,0:T(8,128)(2,1)S(1)} %get-tuple-element.34), channel_id=1, source_target_pairs={{0,12},{4,8},{8,4},{12,0},{1,13},{5,9},{9,5},{13,1},{2,14},{6,10},... | collective-permute-start | bytes 1572872 | tf_op jit(solution)/shard_map/ppermute | solution.py:223
  10.9 32.9 %collective-permute-start.1 = (bf16[128,1024]{1,0:T(8,128)(2,1)S(1)}, bf16[128,1024]{1,0:T(8,128)(2,1)S(1)}, u32[]{:S(2)}, u32[]{:S(2)}) collective-permute-start(bf16[128,1024]{1,0:T(8,128)(2,1)S(1)} %get-tuple-element.33), channel_id=1, source_target_pairs={{0,3},{1,2},{2,1},{3,0},{4,7},{5,6},{6,5},{7,4},{8,11},{9,10},{10,... | collective-permute-start | bytes 786440 | tf_op jit(solution)/shard_map/ppermute | solution.py:223
  31.2 18.2 %collective-permute-start = (bf16[128,1024]{1,0:T(8,128)(2,1)S(1)}, bf16[128,1024]{1,0:T(8,128)(2,1)S(1)}, u32[]{:S(2)}, u32[]{:S(2)}) collective-permute-start(bf16[128,1024]{1,0:T(8,128)(2,1)S(1)} %get-tuple-element.29), channel_id=1, source_target_pairs={{0,3},{1,2},{2,1},{3,0},{4,7},{5,6},{6,5},{7,4},{8,11},{9,10},{10,... | collective-permute-start | bytes 786440 | tf_op jit(solution)/shard_map/ppermute | solution.py:223
  37.8 1.2 %collective-permute-start.7 = (f32[8,128]{1,0:T(8,128)S(1)}, f32[8,128]{1,0:T(8,128)S(1)}, u32[]{:S(2)}, u32[]{:S(2)}) collective-permute-start(f32[8,128]{1,0:T(8,128)S(1)} %get-tuple-element.41), channel_id=1, source_target_pairs={{0,4},{4,0},{8,12},{12,8},{1,5},{5,1},{9,13},{13,9},{2,6},{6,2},{1... | collective-permute-start | bytes 12296 | tf_op jit(solution)/shard_map/ppermute | solution.py:223
  41.0 7.7 %collective-permute-start.8 = (f32[8,128]{1,0:T(8,128)S(1)}, f32[8,128]{1,0:T(8,128)S(1)}, u32[]{:S(2)}, u32[]{:S(2)}) collective-permute-start(f32[8,128]{1,0:T(8,128)S(1)} %get-tuple-element.45), channel_id=1, source_target_pairs={{0,8},{4,12},{8,0},{12,4},{1,9},{5,13},{9,1},{13,5},{2,10},{6,14},... | collective-permute-start | bytes 12296 | tf_op jit(solution)/shard_map/ppermute | solution.py:223
  43.6 5.8 %collective-permute-start.9 = (f32[8,128]{1,0:T(8,128)S(1)}, f32[8,128]{1,0:T(8,128)S(1)}, u32[]{:S(2)}, u32[]{:S(2)}) collective-permute-start(f32[8,128]{1,0:T(8,128)S(1)} %get-tuple-element.47), channel_id=1, source_target_pairs={{0,12},{4,8},{8,4},{12,0},{1,13},{5,9},{9,5},{13,1},{2,14},{6,10},... | collective-permute-start | bytes 12296 | tf_op jit(solution)/shard_map/ppermute | solution.py:223
  43.8 9.8 %collective-permute-start.10 = (f32[8,128]{1,0:T(8,128)S(1)}, f32[8,128]{1,0:T(8,128)S(1)}, u32[]{:S(2)}, u32[]{:S(2)}) collective-permute-start(f32[8,128]{1,0:T(8,128)S(1)} %get-tuple-element.50), channel_id=1, source_target_pairs={{0,2},{1,3},{2,0},{3,1},{4,6},{5,7},{6,4},{7,5},{8,10},{9,11},{10,... | collective-permute-start | bytes 12296 | tf_op jit(solution)/shard_map/ppermute | solution.py:223
  43.8 9.8 %collective-permute-start.11 = (f32[8,128]{1,0:T(8,128)S(1)}, f32[8,128]{1,0:T(8,128)S(1)}, u32[]{:S(2)}, u32[]{:S(2)}) collective-permute-start(f32[8,128]{1,0:T(8,128)S(1)} %get-tuple-element.51), channel_id=1, source_target_pairs={{0,1},{1,0},{2,3},{3,2},{4,5},{5,4},{6,7},{7,6},{8,9},{9,8},{10,11... | collective-permute-start | bytes 12296 | tf_op jit(solution)/shard_map/ppermute | solution.py:223
  50.1 5.5 %collective-permute-start.12 = (f32[8,128]{1,0:T(8,128)S(1)}, f32[8,128]{1,0:T(8,128)S(1)}, u32[]{:S(2)}, u32[]{:S(2)}) collective-permute-start(f32[8,128]{1,0:T(8,128)S(1)} %get-tuple-element.52), channel_id=1, source_target_pairs={{0,3},{1,2},{2,1},{3,0},{4,7},{5,6},{6,5},{7,4},{8,11},{9,10},{10,... | collective-permute-start | bytes 12296 | tf_op jit(solution)/shard_map/ppermute | solution.py:223
